TPU v7x, 256 devices: a whole 4x4x8 slice. The times are simulated.
256 devices in a mesh: wide: 64 (over x, z, core), narrow: 4 (over y).
Axes of the slice: x: 4, y: 4, z: 8, core: 2. Of those that a mesh axis runs over, the one named last changes fastest.
Arguments:
- source: float32 [256, 256, 256], P('wide', 'narrow'), may hold values from -6 to 6
- coef_first: float32 [256, 256, 256], P('wide', 'narrow'), may hold values from 0.25 to 4
- coef_second: float32 [256, 256, 256], P('wide', 'narrow'), may hold values from 0.25 to 4
- coef_third: float32 [256, 256, 256], P('wide', 'narrow'), may hold values from 0.25 to 4
Outputs:
- correction: float32 [256, 256, 256], P('wide', 'narrow')
All inputs are finite; a program needn't handle non-finite values.
Results may differ from a plain program's by a relative error of at most 0.00002.
Values sent between devices are 32-bit elements; how exact they have to be, the bound alone decides.
No kernel may reach another device: no remote copies, remote signals or barrier semaphores. Data moves between devices by JAX's collectives and lax.ppermute only.
A program may use at most 128 MiB of HBM per device.

v0:
```python
import functools

import jax
import jax.numpy as jnp
from jax import lax
from jax.experimental import pallas as pl
from jax.experimental.pallas import tpu as pltpu
from jax.sharding import PartitionSpec as P

THETA = 1.125
DELTA = 0.875
RATIO = THETA / DELTA
SIG = [0.0002 * 4.0**level for level in range(5)]
F32 = jnp.float32
HIGHEST = lax.Precision.HIGHEST


def factors(degree):
    rho, out = 1.0 / RATIO, []
    for _ in range(degree - 1):
        new = 1.0 / (2.0 * RATIO - rho)
        out.append((new * rho, 2.0 * new / DELTA))
        rho = new
    return out


(KEEP, GAIN), = factors(2)


def roll(x, by, axis):
    return pltpu.roll(x, by % x.shape[axis], axis)


def gather_sum(below, here, above, c1, h1, c2, c3):
    first = c1 * below + h1 * above
    second = c2 * roll(here, 1, 0) + roll(c2 * here, -1, 0)
    third = c3 * roll(here, 1, 1) + roll(c3 * here, -1, 1)
    return first + second + third


def diagonal(sig, c1, h1, c2, c3):
    return sig + c1 + h1 + c2 + roll(c2, -1, 0) + c3 + roll(c3, -1, 1)


def iota(shape, dim):
    return lax.broadcasted_iota(jnp.int32, shape, dim)


def pairs_of_lanes(lanes, period, even=False):
    row, col = iota((lanes, 128), 0), iota((lanes, 128), 1) % period
    hit = row == 2 * col if even else row // 2 == col
    return hit.astype(F32)


def copies_of_lanes(lanes_in, lanes_out):
    row, col = iota((lanes_in, lanes_out), 0), iota((lanes_in, lanes_out), 1)
    return (row == col // 2).astype(F32)


def mul(a, b):
    return jnp.dot(a, b, precision=HIGHEST, preferred_element_type=F32)


def pair_rows(x, scratch, start=0, count=None, even=False):
    rows = x.shape[0]
    count = rows // 2 if count is None else count
    scratch[0:rows, :] = x
    first = scratch[pl.ds(start, count, stride=2), :]
    if even:
        return first
    return first + scratch[pl.ds(start + 1, count, stride=2), :]


def twice_rows(x, scratch):
    rows = x.shape[0]
    scratch[pl.ds(0, rows, stride=2), :] = x
    scratch[pl.ds(1, rows, stride=2), :] = x
    return scratch[0 : 2 * rows, :]


def coarse_coefs(planes, scratch, lanes, period, start=0, count=None):
    both = pairs_of_lanes(lanes, period)
    alone = pairs_of_lanes(lanes, period, even=True)
    return (
        0.25 * pair_rows(mul(planes[0], both), scratch, start, count),
        0.25 * pair_rows(mul(planes[1], both), scratch, start, count, even=True),
        0.25 * pair_rows(mul(planes[2], alone), scratch, start, count),
    )


def spread_block(x, block, width):
    lane = iota(x.shape, 1)
    x = jnp.where(lane // width == block, x, 0.0)
    while width < 128:
        x = x + pltpu.roll(x, width, 1)
        width *= 2
    return x


def smooth_two(u1, below, above, f, g, c1, h1, c2, c3):
    near = gather_sum(below, u1, above, c1, h1, c2, c3)
    return (1.0 + KEEP) * u1 + GAIN * (g * (f + near) - u1)


def first_post(v, below, above, f, g, c1, h1, c2, c3):
    near = gather_sum(below, v, above, c1, h1, c2, c3)
    return v + (1.0 / THETA) * (g * (f + near) - v)


def second_post(u, v, below, above, f, g, c1, h1, c2, c3):
    near = gather_sum(below, u, above, c1, h1, c2, c3)
    return u + KEEP * (u - v) + GAIN * (g * (f + near) - u)


def call(kernel, outs, scratch=(), smem=0):
    def run(*args):
        in_specs = [pl.BlockSpec(memory_space=pltpu.SMEM if i < smem else pltpu.VMEM) for i in range(len(args))]
        return pl.pallas_call(
            kernel,
            out_shape=[jax.ShapeDtypeStruct(s, F32) for s in outs],
            in_specs=in_specs,
            out_specs=[pl.BlockSpec(memory_space=pltpu.VMEM)] * len(outs),
            scratch_shapes=[pltpu.VMEM(s, F32) for s in scratch],
            compiler_params=pltpu.CompilerParams(vmem_limit_bytes=40 * 2**20),
        )(*args)

    return run


def start_kernel(f, c1, c2, c3, up, down, coef3, scr):
    for a, ref in enumerate((f, c1, c2, c3)):
        up[4 * a : 4 * a + 4] = ref[:, 56:64, :]
        down[4 * a : 4 * a + 4] = ref[:, 0:8, :]
    k1 = jnp.concatenate([c1[0], c1[2]], axis=0)
    k2 = jnp.concatenate([c2[0] + c2[1], c2[2] + c2[3]], axis=0)
    k3 = jnp.concatenate([c3[0] + c3[1], c3[2] + c3[3]], axis=0)
    k1, k2, k3 = coarse_coefs((k1, k2, k3), scr, 256, 128)
    k1, k2, k3 = k1[:32], k2[:32] + k2[32:], k3[:32] + k3[32:]
    k1, k2, k3 = coarse_coefs((k1, k2, k3), scr, 128, 64)
    k1, k2, k3 = coarse_coefs((k1, k2, k3), scr, 128, 32)
    lane = iota(k1.shape, 1)
    coef3[...] = jnp.where(lane < 32, k1, jnp.where(lane < 64, k2, k3))


def pad_kernel(f, c1, c2, c3, low, high, own, coef1, up, down, scr):
    for a, ref in enumerate((f, c1, c2, c3)):
        for p in range(4):
            own[4 * a + p, 0:8] = low[4 * a + p]
            own[4 * a + p, 8:72] = ref[p]
            own[4 * a + p, 72:80] = high[4 * a + p]
    for p, out, slot in ((1, down, 5), (2, up, 4)):
        diag = diagonal(SIG[0], own[4 + p], own[5 + p], own[8 + p], own[12 + p])
        out[slot] = own[p] / diag / THETA
    for a in range(4):
        up[a] = own[4 * a + 3]
        down[a] = own[4 * a]
    down[4] = own[5]
    k1 = jnp.concatenate([own[4], own[6]], axis=0)
    k2 = jnp.concatenate([own[8] + own[9], own[10] + own[11]], axis=0)
    k3 = jnp.concatenate([own[12] + own[13], own[14] + own[15]], axis=0)
    coarse = coarse_coefs((k1, k2, k3), scr, 256, 128)
    for a in range(3):
        for p in range(2):
            coef1[2 * a + p] = coarse[a][40 * p : 40 * p + 40]
    for out, at in ((up, 5), (down, 6)):
        out[at, 0:40, 0:128] = coef1[0]
        out[at, 0:40, 128:256] = coef1[1]
        out[at, 40:80, 0:128] = coef1[2]
        out[at, 40:80, 128:256] = coef1[3]
        out[at + 1, 0:40, 0:128] = coef1[4]
        out[at + 1, 0:40, 128:256] = coef1[5]
        out[at + 1, 40:80, :] = jnp.zeros((40, 256), F32)


def unpack(ref, at, index):
    plane, slot = at + index // 4, index % 4
    row, lane = 40 * (slot // 2), 128 * (slot % 2)
    return ref[plane, row : row + 40, lane : lane + 128]


CHUNK = 16


def chunked(rows, body):
    for r0 in range(0, rows, CHUNK):
        body(r0, rows)


def near_chunk(u, p, c1, c2, c3, q, r0, rows):
    here = pl.ds(r0, CHUNK)
    x = u[p, here, :]
    if r0 > 0:
        lower = u[p, pl.ds(r0 - 1, CHUNK), :]
    else:
        lower = roll(x, 1, 0)
    if r0 + CHUNK < rows:
        after = pl.ds(r0 + 1, CHUNK)
        upper = c2[q, after, :] * u[p, after, :]
    else:
        upper = roll(c2[q, here, :] * x, -1, 0)
    k3 = c3[q, here, :]
    first = c1[q, here, :] * u[p - 1, here, :] + c1[q + 1, here, :] * u[p + 1, here, :]
    second = c2[q, here, :] * lower + upper
    third = k3 * roll(x, 1, 1) + roll(k3 * x, -1, 1)
    return x, first + second + third


def diag_chunk(c1, c2, c3, q, r0, rows):
    here = pl.ds(r0, CHUNK)
    k2, k3 = c2[q, here, :], c3[q, here, :]
    if r0 + CHUNK < rows:
        h2 = c2[q, pl.ds(r0 + 1, CHUNK), :]
    else:
        h2 = roll(k2, -1, 0)
    return SIG[0] + c1[q, here, :] + c1[q + 1, here, :] + k2 + h2 + k3 + roll(k3, -1, 1)


def fine_pre_kernel(own, coef1, low, high, f, c1, c2, c3, g, u2, w1, g1, msg_up, msg_down, f1, coef2, u1, res, scr):
    for a, ref in enumerate((f, c1, c2, c3)):
        ref[0] = low[a]
        ref[1:5] = own[4 * a : 4 * a + 4]
        ref[5] = high[a]
    c1[6] = high[4]
    u1[0] = low[4]
    u1[7] = high[5]

    def smooth_first(q, carry):
        def rows(r0, n):
            here = pl.ds(r0, CHUNK)
            inverse = 1.0 / diag_chunk(c1, c2, c3, q, r0, n)
            g[q, here, :] = inverse
            u1[q + 1, here, :] = f[q, here, :] * inverse * (1.0 / THETA)

        chunked(80, rows)
        return carry

    lax.fori_loop(0, 6, smooth_first, 0)

    def smooth_second(q, carry):
        def rows(r0, n):
            here = pl.ds(r0, CHUNK)
            x, near = near_chunk(u1, q + 1, c1, c2, c3, q, r0, n)
            u2[q + 1, here, :] = (1.0 + KEEP) * x + GAIN * (g[q, here, :] * (f[q, here, :] + near) - x)

        chunked(80, rows)
        return carry

    lax.fori_loop(0, 6, smooth_second, 0)

    def residual(q, carry):
        def rows(r0, n):
            here = pl.ds(r0, CHUNK)
            x, near = near_chunk(u2, q + 1, c1, c2, c3, q, r0, n)
            res[q - 1, here, :] = f[q, here, :] + near - diag_chunk(c1, c2, c3, q, r0, n) * x

        chunked(80, rows)
        return carry

    lax.fori_loop(1, 5, residual, 0)

    both = pairs_of_lanes(256, 128)
    sums = jnp.concatenate([res[0] + res[1], res[2] + res[3]], axis=0)
    coarse = 0.5 * pair_rows(mul(sums, both), scr)
    f1[0] = coarse[:40]
    f1[1] = coarse[40:]
    for a in range(3):
        for p in range(2):
            w1[6 * a + p] = unpack(low, 5, 2 * a + p)
            w1[6 * a + 2 + p] = coef1[2 * a + p]
            w1[6 * a + 4 + p] = unpack(high, 6, 2 * a + p)
    for k in range(4):
        p = k + 1
        g1[k] = 1.0 / diagonal(SIG[1], w1[p], w1[p + 1], w1[6 + p], w1[12 + p])
    for p in range(2):
        start = f1[p] * g1[1 + p] * (1.0 / THETA)
        for out in (msg_up, msg_down):
            out[p] = f1[p]
            out[2 + p] = start
    for out, plane in ((msg_up, 4), (msg_down, 3)):
        out[4] = u2[plane, 0:40, 0:128]
        out[5] = u2[plane, 0:40, 128:256]
        out[6] = u2[plane, 40:80, 0:128]
        out[7] = u2[plane, 40:80, 128:256]
    k1 = jnp.concatenate([w1[0], w1[2], w1[4]], axis=0)
    k2 = jnp.concatenate([w1[6 + 2 * k] + w1[7 + 2 * k] for k in range(3)], axis=0)
    k3 = jnp.concatenate([w1[12 + 2 * k] + w1[13 + 2 * k] for k in range(3)], axis=0)
    coarse = coarse_coefs((k1, k2, k3), scr, 128, 64)
    for a in range(3):
        for k in range(3):
            coef2[3 * a + k] = coarse[a][20 * k + 2 : 20 * k + 18]


def middle_pre_kernel(own, low, high, w1, g1, f, u2, f2, up, down, u1, scr):
    f[0] = low[1]
    f[1:3] = own[0:2]
    f[3] = high[0]
    u1[0:2] = low[2:4]
    u1[2:4] = own[2:4]
    u1[4:6] = high[2:4]
    u2[0] = jnp.zeros((40, 128), F32)
    u2[5] = jnp.zeros((40, 128), F32)
    for p in range(1, 5):
        u2[p] = smooth_two(u1[p], u1[p - 1], u1[p + 1], f[p - 1], g1[p - 1], w1[p], w1[p + 1], w1[6 + p], w1[12 + p])
    total = 0.0
    for p in (2, 3):
        k1, h1, k2, k3 = w1[p], w1[p + 1], w1[6 + p], w1[12 + p]
        near = gather_sum(u2[p - 1], u2[p], u2[p + 1], k1, h1, k2, k3)
        total = total + (f[p - 1] + near - diagonal(SIG[1], k1, h1, k2, k3) * u2[p])
    coarse = 0.5 * pair_rows(mul(total, pairs_of_lanes(128, 64)), scr, 4, 16)
    f2[...] = coarse
    up[0:16] = coarse
    down[0:16] = coarse
    for p in range(2):
        up[16 + 8 * p : 24 + 8 * p] = u2[2 + p, 28:36]
        down[16 + 8 * p : 24 + 8 * p] = u2[2 + p, 4:12]


def coarse_start_kernel(place, f2, low, high, far, coef2, u2fine, c2w, own, msg, far_msg):
    n = place[1]
    for piece, by in ((f2, 0), (high, 1), (far, 2), (low, 3)):
        at = pl.multiple_of(16 * lax.rem(n + by, 4), 16)
        own[0, pl.ds(at, 16), :] = piece[0:16, :]
    for k in range(9):
        for m in range(4):
            c2w[k, 16 * m : 16 * m + 16] = coef2[9 * m + k]
    g = 1.0 / diagonal(SIG[2], c2w[1], c2w[2], c2w[4], c2w[7])
    own[1] = g
    start = own[0] * g * (1.0 / THETA)
    own[2] = start
    far_msg[...] = start
    msg[0:64] = own[0]
    msg[64:128] = g
    msg[128:192] = c2w[2]
    for p in range(2):
        at = 192 + 40 * p
        msg[at : at + 40] = u2fine[2 + p]
        msg[at : at + 4] = low[20 + 8 * p : 24 + 8 * p]
        msg[at + 36 : at + 40] = high[16 + 8 * p : 20 + 8 * p]


def coarse_pre_kernel(own, c2w, low, high, low2, high2, u2, mine, send, scr):
    f = (low[0:64], own[0], high[0:64])
    g = (low[64:128], own[1], high[64:128])
    u1 = [low2[...], f[0] * g[0] * (1.0 / THETA), own[2], f[2] * g[2] * (1.0 / THETA), high2[...]]
    h1 = (c2w[1], c2w[2], high[128:192])
    for k in range(3):
        u2[k] = smooth_two(u1[k + 1], u1[k], u1[k + 2], f[k], g[k], c2w[k], h1[k], c2w[3 + k], c2w[6 + k])
    mine[...] = u2[1]
    k1, k2, k3 = c2w[1], c2w[4], c2w[7]
    near = gather_sum(u2[0], u2[1], u2[2], k1, h1[1], k2, k3)
    res = f[1] + near - diagonal(SIG[2], k1, h1[1], k2, k3) * u2[1]
    part = 0.5 * pair_rows(mul(res, pairs_of_lanes(128, 32)), scr)
    block = iota((8, 128), 1) // 32
    packed = part[0:8]
    for q in range(1, 4):
        packed = jnp.where(block == q, part[8 * q : 8 * q + 8], packed)
    for w in range(send.shape[0]):
        send[w] = packed


def rows_loop(count, body):
    def step(j, carry):
        body(j)
        return carry

    lax.fori_loop(0, count, step, 0)


def coarse_coef_kernel(coef3, c1, c2, c3, g3, d1, d2, d3, g4, scr):
    n3, n4 = c1.shape[0] - 1, d1.shape[0] - 1

    def unpack_plane(j):
        for m in range(4):
            even, odd = coef3[m, 2 * j], coef3[m, 2 * j + 1]
            rows = pl.ds(8 * m, 8)
            c1[j, rows, :] = spread_block(even, 0, 32)
            c2[j, rows, :] = spread_block(even + odd, 1, 32)
            c3[j, rows, :] = spread_block(even + odd, 2, 32)

    rows_loop(n3, unpack_plane)
    c1[n3] = c1[0]

    def inverse3(j):
        g3[j] = 1.0 / diagonal(SIG[3], c1[j], c1[j + 1], c2[j], c3[j])

    rows_loop(n3, inverse3)
    k1 = jnp.concatenate([c1[2 * j] for j in range(n4)], axis=0)
    k2 = jnp.concatenate([c2[2 * j] + c2[2 * j + 1] for j in range(n4)], axis=0)
    k3 = jnp.concatenate([c3[2 * j] + c3[2 * j + 1] for j in range(n4)], axis=0)
    coarse = coarse_coefs((k1, k2, k3), scr, 128, 16)
    for a, ref in enumerate((d1, d2, d3)):
        for j in range(n4):
            ref[j] = coarse[a][16 * j : 16 * j + 16]
    d1[n4] = d1[0]

    def inverse4(j):
        g4[j] = 1.0 / diagonal(SIG[4], d1[j], d1[j + 1], d2[j], d3[j])

    rows_loop(n4, inverse4)


def around(j, n):
    return lax.rem(j + n, n)


def bottom_kernel(place, parts, c1, c2, c3, g3, d1, d2, d3, g4, own, c2w, low, high, u2w, u2low, u2high, out,
                  f3, u1, u2, res, f4, ua, ub, st, v3, w3, scr):
    n3, n4 = f3.shape[0], f4.shape[0]

    def unpack_plane(j):
        both = parts[2 * j] + parts[2 * j + 1]
        for q in range(4):
            f3[j, 8 * q : 8 * q + 8] = spread_block(both, q, 32)
        u1[j] = f3[j] * g3[j] * (1.0 / THETA)

    rows_loop(n3, unpack_plane)

    def pre(j):
        u2[j] = smooth_two(u1[j], u1[around(j - 1, n3)], u1[around(j + 1, n3)], f3[j], g3[j], c1[j], c1[j + 1], c2[j], c3[j])

    rows_loop(n3, pre)

    def residual(k):
        total = 0.0
        for half in range(2):
            j = 2 * k + half
            near = gather_sum(u2[around(j - 1, n3)], u2[j], u2[around(j + 1, n3)], c1[j], c1[j + 1], c2[j], c3[j])
            total = total + (f3[j] + near - diagonal(SIG[3], c1[j], c1[j + 1], c2[j], c3[j]) * u2[j])
        res[pl.ds(pl.multiple_of(32 * k, 32), 32), :] = total

    rows_loop(n4, residual)
    coarse = 0.5 * pair_rows(mul(res[0 : 32 * n4, :], pairs_of_lanes(128, 16)), scr)
    for k in range(n4):
        f4[k] = coarse[16 * k : 16 * k + 16]

    def first4(k):
        x = f4[k] * g4[k] * (1.0 / THETA)
        ua[k] = x
        st[k] = x

    rows_loop(n4, first4)
    src, dst = ua, ub
    for keep, gain in factors(4):
        def sweep(k, src=src, dst=dst, keep=keep, gain=gain):
            x = src[k]
            near = gather_sum(src[around(k - 1, n4)], x, src[around(k + 1, n4)], d1[k], d1[k + 1], d2[k], d3[k])
            step = keep * st[k] + gain * (g4[k] * (f4[k] + near) - x)
            st[k] = step
            dst[k] = x + step

        rows_loop(n4, sweep)
        src, dst = dst, src

    j0 = around(place[0] - 2, 2 * n3) // 2
    for k in range(5):
        scr[16 * k : 16 * k + 16] = src[around(around(j0 - 2, n3) // 2 + k, n4)]
    e4 = mul(scr[0:80, :], fold_copies(16))
    fine = twice_rows(e4, scr)
    odd = lax.rem(around(j0 - 2, n3), 2)
    for k in range(5):
        res[32 * k : 32 * k + 32] = fine[32 * k : 32 * k + 32]

    def add(k):
        j = around(j0 - 2 + k, n3)
        at = pl.multiple_of(32 * ((odd + k) // 2), 32)
        v3[k] = u2[j] + res[pl.ds(at, 32), :]

    rows_loop(7, add)

    def post1(k):
        j = around(j0 - 2 + k, n3)
        w3[k] = first_post(v3[k], v3[k - 1], v3[k + 1], f3[j], g3[j], c1[j], c1[j + 1], c2[j], c3[j])

    lax.fori_loop(1, 6, lambda k, c: (post1(k), c)[1], 0)
    for k in range(2, 5):
        j = around(j0 - 2 + k, n3)
        x = second_post(w3[k], v3[k], w3[k - 1], w3[k + 1], f3[j], g3[j], c1[j], c1[j + 1], c2[j], c3[j])
        res[32 * (k - 2) : 32 * (k - 2) + 32] = x
    e3 = mul(res[0:96, :], fold_copies(32))
    fine = twice_rows(e3, scr)
    for k in range(3):
        res[64 * k : 64 * k + 64] = fine[64 * k : 64 * k + 64]

    odd = lax.rem(around(place[0] - 2, 2 * n3), 2)
    base = (u2low[...], u2w[0], u2w[1], u2w[2], u2high[...])
    v = [base[k] + res[pl.ds(pl.multiple_of(64 * ((odd + k) // 2), 64), 64), :] for k in range(5)]
    f = (low[0:64], own[0], high[0:64])
    g = (low[64:128], own[1], high[64:128])
    h1 = (c2w[1], c2w[2], high[128:192])
    w = [first_post(v[k + 1], v[k], v[k + 2], f[k], g[k], c2w[k], h1[k], c2w[3 + k], c2w[6 + k]) for k in range(3)]
    out[...] = second_post(w[1], v[2], w[0], w[2], f[1], g[1], c2w[1], h1[1], c2w[4], c2w[7])


def fold_copies(period):
    row, col = iota((128, 128), 0), iota((128, 128), 1) % (2 * period)
    return (row == col // 2).astype(F32)


def middle_post_kernel(place, e2low, e2, e2high, msg, low, high, u2, f, g1, w1, out, up, down, v, w):
    n = place[1]
    row, col = iota((40, 64), 0), iota((40, 64), 1)
    pick = (col == lax.rem(16 * n + (row + 4) // 2 + 60, 64)).astype(F32)
    lanes = copies_of_lanes(128, 128)
    fine = [mul(mul(pick, e[...]), lanes) for e in (e2low, e2, e2high)]
    for p in range(6):
        if p < 2:
            base = low[192 + 40 * p : 232 + 40 * p]
        elif p < 4:
            base = msg[192 + 40 * (p - 2) : 232 + 40 * (p - 2)]
        else:
            base = high[192 + 40 * (p - 4) : 232 + 40 * (p - 4)]
        v[p] = base + fine[p // 2]
    for p in range(1, 5):
        w[p] = first_post(v[p], v[p - 1], v[p + 1], f[p - 1], g1[p - 1], w1[p], w1[p + 1], w1[6 + p], w1[12 + p])
    for p in (2, 3):
        out[p - 2] = second_post(w[p], v[p], w[p - 1], w[p + 1], f[p - 1], g1[p - 1], w1[p], w1[p + 1], w1[6 + p], w1[12 + p])
    up[...] = out[1]
    down[...] = out[0]


def fine_post_kernel(e1, e1low, e1high, low, high, f, c1, c2, c3, g, u2, out, v, w, scr):
    lanes = copies_of_lanes(128, 256)
    rows = twice_rows(jnp.concatenate([e1low[...], e1[0], e1[1], e1high[...]], axis=0), scr)
    fine = mul(rows, lanes)
    for k, ref in ((0, low), (7, high)):
        part = fine[80 * (k // 2) : 80 * (k // 2) + 80]
        v[k, 0:40, 0:128] = ref[4] + part[0:40, 0:128]
        v[k, 0:40, 128:256] = ref[5] + part[0:40, 128:256]
        v[k, 40:80, 0:128] = ref[6] + part[40:80, 0:128]
        v[k, 40:80, 128:256] = ref[7] + part[40:80, 128:256]
    for k in range(1, 7):
        v[k] = u2[k] + fine[80 * (k // 2) : 80 * (k // 2) + 80]

    def post1(q, carry):
        def chunk(r0, n):
            here = pl.ds(r0, CHUNK)
            x, near = near_chunk(v, q + 1, c1, c2, c3, q, r0, n)
            w[q + 1, here, :] = x + (1.0 / THETA) * (g[q, here, :] * (f[q, here, :] + near) - x)

        chunked(80, chunk)
        return carry

    lax.fori_loop(0, 6, post1, 0)

    def post2(q, carry):
        for r0 in range(8, 72, CHUNK):
            here = pl.ds(r0, CHUNK)
            x, near = near_chunk(w, q + 1, c1, c2, c3, q, r0, 80)
            step = KEEP * (x - v[q + 1, here, :]) + GAIN * (g[q, here, :] * (f[q, here, :] + near) - x)
            out[q - 1, pl.ds(r0 - 8, CHUNK), :] = x + step
        return carry

    lax.fori_loop(1, 5, post2, 0)


def shift(x, axis, by):
    count = lax.axis_size(axis)
    return lax.ppermute(x, axis, [(i, (i + by) % count) for i in range(count)])


def body(source, coef_first, coef_second, coef_third):
    wide = lax.axis_size("wide")
    n3, n4 = wide // 2, wide // 4
    place = jnp.stack([lax.axis_index("wide"), lax.axis_index("narrow")]).astype(jnp.int32)
    inputs = (source, coef_first, coef_second, coef_third)
    big = (80, 256)

    up, down, part3 = call(start_kernel, [(16, 8, 256), (16, 8, 256), (8, 128)], [(128, 128)])(*inputs)
    low, high = shift(up, "narrow", 1), shift(down, "narrow", -1)
    coef3 = lax.all_gather(part3, "wide", tiled=True)
    coef3 = lax.all_gather(coef3, "narrow", tiled=True).reshape(4, wide, 8, 128)

    own, coef1, up, down = call(
        pad_kernel, [(16,) + big, (6, 40, 128), (7,) + big, (8,) + big], [(160, 128)]
    )(*inputs, low, high)
    low, high = shift(up, "wide", 1), shift(down, "wide", -1)

    f, c1, c2, c3, g, u2, w1, g1, up, down, f1, coef2 = call(
        fine_pre_kernel,
        [(6,) + big, (7,) + big, (6,) + big, (6,) + big, (6,) + big, (8,) + big]
        + [(18, 40, 128), (4, 40, 128), (8, 40, 128), (8, 40, 128), (2, 40, 128), (9, 16, 128)],
        [(8,) + big, (4,) + big, (160, 128)],
    )(own, coef1, low, high)
    coef2 = lax.all_gather(coef2, "narrow", tiled=True)
    low1, high1 = shift(up, "wide", 1), shift(down, "wide", -1)

    f1w, u2m, f2, up, down = call(
        middle_pre_kernel,
        [(4, 40, 128), (6, 40, 128), (16, 128), (32, 128), (32, 128)],
        [(6, 40, 128), (40, 128)],
    )(up, low1, high1, w1, g1)
    low, high, far = shift(up, "narrow", 1), shift(down, "narrow", -1), shift(f2, "narrow", 2)

    c2w, own2, msg, far_msg = call(
        coarse_start_kernel, [(9, 64, 128), (3, 64, 128), (272, 128), (64, 128)], smem=1
    )(place, f2, low, high, far, coef2, u2m)
    low2, high2 = shift(msg, "wide", 1), shift(msg, "wide", -1)
    low2f, high2f = shift(far_msg, "wide", 2), shift(far_msg, "wide", -2)

    u2w, mine, send = call(
        coarse_pre_kernel, [(3, 64, 128), (64, 128), (wide, 8, 128)], [(64, 128)]
    )(own2, c2w, low2, high2, low2f, high2f)
    u2low, u2high = shift(mine, "wide", 2), shift(mine, "wide", -2)
    parts = lax.all_to_all(send, "wide", split_axis=0, concat_axis=0, tiled=True)

    three, four = (n3, 32, 128), (n4, 16, 128)
    coefs = call(
        coarse_coef_kernel,
        [(n3 + 1, 32, 128), three, three, three, (n4 + 1, 16, 128), four, four, four],
        [(n4 * 32, 128)],
    )(coef3)
    (e2,) = call(
        bottom_kernel,
        [(64, 128)],
        [three, three, three, (max(n4 * 32, 192), 128), four, four, four, four, (7, 32, 128), (7, 32, 128)]
        + [(max(n4 * 32, 192), 128)],
        smem=1,
    )(place, parts, *coefs, own2, c2w, low2, high2, u2w, u2low, u2high)
    e2low, e2high = shift(e2, "wide", 1), shift(e2, "wide", -1)

    e1, up, down = call(
        middle_post_kernel,
        [(2, 40, 128), (40, 128), (40, 128)],
        [(6, 40, 128), (6, 40, 128)],
        smem=1,
    )(place, e2low, e2, e2high, msg, low2, high2, u2m, f1w, g1, w1)
    e1low, e1high = shift(up, "wide", 1), shift(down, "wide", -1)

    (out,) = call(
        fine_post_kernel, [(4, 64, 256)], [(8,) + big, (8,) + big, (320, 128)]
    )(e1, e1low, e1high, low1, high1, f, c1, c2, c3, g, u2)
    return out


def solution(mesh):
    spec = P("wide", "narrow", None)
    return jax.shard_map(body, mesh=mesh, in_specs=(spec,) * 4, out_specs=spec, check_vma=False)
```

profile of v0, /device:TPU:1, one launch (start us, length us, event | category | flops | bytes accessed | tf_op | source)
XLA Modules:
  0.0 205.3 jit_solution(6829984882041054979)
XLA Ops:
  6.5 0.9 copy-done.1
  7.5 0.9 copy-done.2
  9.4 0.9 copy-done.4
  10.3 1.0 shard_map.46
  11.3 2.1 %collective-permute-start = (f32[16,8,256]{2,1,0:T(8,128)S(1)}, f32[16,8,256]{2,1,0:T(8,128)S(1)}, u32[]{:S(2)}, u32[]{:S(2)}) collective-permute-start(f32[16,8,256]{2,1,0:T(8,128)S(1)} %get-tuple-element.46), channel_id=1, source_target_pairs={{0,1},{1,2},{2,3},{3,0},{4,5},{5,6},{6,7},{7,4},{8,9},{9,10},{10,1... | collective-permute-start | bytes 393224 | tf_op jit(solution)/shard_map/ppermute | solution.py:558
  13.5 1.5 collective-permute-start.1
  15.0 2.3 %collective-permute-done.low = f32[16,8,256]{2,1,0:T(8,128)S(1)} collective-permute-done((f32[16,8,256]{2,1,0:T(8,128)S(1)}, f32[16,8,256]{2,1,0:T(8,128)S(1)}, u32[]{:S(2)}, u32[]{:S(2)}) %collective-permute-start) | collective-permute-done | bytes 131104 | tf_op jit(solution)/shard_map/ppermute | solution.py:558
  18.8 3.5 %collective-permute-start.3 = (f32[8,80,256]{2,1,0:T(8,128)S(1)}, f32[8,80,256]{2,1,0:T(8,128)S(1)}, u32[]{:S(2)}, u32[]{:S(2)}) collective-permute-start(f32[8,80,256]{2,1,0:T(8,128)S(1)} %get-tuple-element.51), channel_id=1, source_target_pairs={{0,252},{4,0},{8,4},{12,8},{16,12},{20,16},{24,20},{28,24},{32,28}... | collective-permute-start | bytes 1966088 | tf_op jit(solution)/shard_map/ppermute | solution.py:558
  22.3 53.6 %all_gather.10 = f32[512,128]{1,0:T(8,128)} all-gather(f32[8,128]{1,0:T(8,128)S(1)} %get-tuple-element.66), channel_id=1, replica_groups=mesh['wide'=64,'narrow'=4] {'wide'}, dimensions={0}, use_global_device_ids=true | all-gather | bytes 266240 | tf_op jit(solution)/shard_map/all_gather | solution.py:570
  76.0 7.0 %collective-permute-done.2.low = f32[7,80,256]{2,1,0:T(8,128)S(1)} collective-permute-done((f32[7,80,256]{2,1,0:T(8,128)}, f32[7,80,256]{2,1,0:T(8,128)S(1)}, u32[]{:S(2)}, u32[]{:S(2)}) %collective-permute-start.2) | collective-permute-done | bytes 573472 | tf_op jit(solution)/shard_map/ppermute | solution.py:558
  83.0 3.4 %shard_map.48 = (f32[6,80,256]{2,1,0:T(8,128)S(1)}, f32[7,80,256]{2,1,0:T(8,128)S(1)}, f32[6,80,256]{2,1,0:T(8,128)S(1)}, f32[6,80,256]{2,1,0:T(8,128)S(1)}, f32...) custom-call(f32[16,80,256]{2,1,0:T(8,128)S(1)} %get-tuple-element.48, ...), custom_call_target="tpu_custom_call" | custom-call | tf_op jit(solution)/shard_map/pallas_call | solution.py:118
  90.4 2.4 %collective-permute-start.4 = (f32[8,40,128]{2,1,0:T(8,128)S(1)}, f32[8,40,128]{2,1,0:T(8,128)S(1)}, u32[]{:S(2)}, u32[]{:S(2)}) collective-permute-start(f32[8,40,128]{2,1,0:T(8,128)S(1)} %get-tuple-element.52.own), channel_id=1, source_target_pairs={{0,4},{4,8},{8,12},{12,16},{16,20},{20,24},{24,28},{28,32},{32,36}... | collective-permute-start | bytes 491528 | tf_op jit(solution)/shard_map/ppermute | solution.py:558
  92.7 3.5 %collective-permute-start.5 = (f32[8,40,128]{2,1,0:T(8,128)}, f32[8,40,128]{2,1,0:T(8,128)S(1)}, u32[]{:S(2)}, u32[]{:S(2)}) collective-permute-start(f32[8,40,128]{2,1,0:T(8,128)} %get-tuple-element.53), channel_id=1, source_target_pairs={{0,252},{4,0},{8,4},{12,8},{16,12},{20,16},{24,20},{28,24},{32,28}... | collective-permute-start | bytes 491528 | tf_op jit(solution)/shard_map/ppermute | solution.py:558
  99.1 2.0 collective-permute-start.7
  101.9 9.4 %all_gather.9.coef2 = f32[36,16,128]{2,1,0:T(8,128)S(1)} all-gather(f32[9,16,128]{2,1,0:T(8,128)S(1)} %get-tuple-element.59), channel_id=1, replica_groups=mesh['wide'=64,'narrow'=4] {'narrow'}, dimensions={0}, use_global_device_ids=true | all-gather | bytes 368640 | tf_op jit(solution)/shard_map/all_gather | solution.py:584
  112.0 3.9 %collective-permute-start.9 = (f32[272,128]{1,0:T(8,128)S(1)}, f32[272,128]{1,0:T(8,128)S(1)}, u32[]{:S(2)}, u32[]{:S(2)}) collective-permute-start(f32[272,128]{1,0:T(8,128)S(1)} %get-tuple-element.63.msg), channel_id=1, source_target_pairs={{0,4},{4,8},{8,12},{12,16},{16,20},{20,24},{24,28},{28,32},{32,36}... | collective-permute-start | bytes 417800 | tf_op jit(solution)/shard_map/ppermute | solution.py:558
  115.9 6.9 %collective-permute-start.10 = (f32[272,128]{1,0:T(8,128)S(1)}, f32[272,128]{1,0:T(8,128)S(1)}, u32[]{:S(2)}, u32[]{:S(2)}) collective-permute-start(f32[272,128]{1,0:T(8,128)S(1)} %get-tuple-element.63.msg), channel_id=1, source_target_pairs={{0,252},{4,0},{8,4},{12,8},{16,12},{20,16},{24,20},{28,24},{32,28}... | collective-permute-start | bytes 417800 | tf_op jit(solution)/shard_map/ppermute | solution.py:558
  122.8 4.8 %collective-permute-start.12 = (f32[64,128]{1,0:T(8,128)S(1)}, f32[64,128]{1,0:T(8,128)S(1)}, u32[]{:S(2)}, u32[]{:S(2)}) collective-permute-start(f32[64,128]{1,0:T(8,128)S(1)} %get-tuple-element.64), channel_id=1, source_target_pairs={{0,248},{4,252},{8,0},{12,4},{16,8},{20,12},{24,16},{28,20},{32,24... | collective-permute-start | bytes 98312 | tf_op jit(solution)/shard_map/ppermute | solution.py:558
  127.6 2.6 %collective-permute-done.11.low2 = f32[64,128]{1,0:T(8,128)S(1)} collective-permute-done((f32[64,128]{1,0:T(8,128)S(1)}, f32[64,128]{1,0:T(8,128)S(1)}, u32[]{:S(2)}, u32[]{:S(2)}) %collective-permute-start.11) | collective-permute-done | bytes 32800 | tf_op jit(solution)/shard_map/ppermute | solution.py:558
  130.2 1.1 shard_map.51
  131.9 12.0 %all-to-all-start = ((f32[64,8,128]{2,1,0:T(8,128)}), f32[64,8,128]{2,1,0:T(8,128)S(1)}, u32[]{:S(2)}, u32[]{:S(2)}) async-start(f32[64,8,128]{2,1,0:T(8,128)} %get-tuple-element.65), calls=%async_computation | async-start | bytes 524288 | tf_op jit(solution)/shard_map/all_to_all | solution.py:604
  144.0 1.5 collective-permute-start.13
  145.4 3.7 %collective-permute-start.14 = (f32[64,128]{1,0:T(8,128)}, f32[64,128]{1,0:T(8,128)S(1)}, u32[]{:S(2)}, u32[]{:S(2)}) collective-permute-start(f32[64,128]{1,0:T(8,128)} %get-tuple-element.76), channel_id=1, source_target_pairs={{0,248},{4,252},{8,0},{12,4},{16,8},{20,12},{24,16},{28,20},{32,24... | collective-permute-start | bytes 98312 | tf_op jit(solution)/shard_map/ppermute | solution.py:558
  149.1 1.2 copy-done
  150.4 9.6 %shard_map.52 = (f32[33,32,128]{2,1,0:T(8,128)S(1)}, f32[32,32,128]{2,1,0:T(8,128)S(1)}, f32[32,32,128]{2,1,0:T(8,128)S(1)}, f32[32,32,128]{2,1,0:T(8,128)S(1)},...) custom-call(f32[4,64,8,128]{3,2,1,0:T(8,128)S(1)} %bitcast.3), custom_call_target="tpu_custom_call" | custom-call | tf_op jit(solution)/shard_map/pallas_call | solution.py:118
  164.2 1.0 copy-done.8
  165.3 1.0 copy-done.10
  170.8 15.4 %shard_map.53.e2 = f32[64,128]{1,0:T(8,128)S(1)} custom-call(s32[2]{0:T(128)S(1)} %pad_add_fusion.place, f32[64,8,128]{2,1,0:T(8,128)S(1)} %all-to-all-done.parts, f32[33,32,128]{2,1,0:T(8,128)S(1)} %get-tuple-element.67.c1, f32[32,32,128]{2,1,0:T(8,128)S(1)} %get-tuple-element.68.c2, f32[32,32,128]{2,1,0:T(8,128)S(1)} %copy-done.8, ...), custom_call_target="tpu_custom_call" | custom-call | tf_op jit(solution)/shard_map/pallas_call | solution.py:118
  187.8 2.0 collective-permute-done.16.e2high
  189.8 1.2 shard_map.54
  191.1 4.0 %collective-permute-start.18 = (f32[40,128]{1,0:T(8,128)S(1)}, f32[40,128]{1,0:T(8,128)S(1)}, u32[]{:S(2)}, u32[]{:S(2)}) collective-permute-start(f32[40,128]{1,0:T(8,128)S(1)} %get-tuple-element.80), channel_id=1, source_target_pairs={{0,252},{4,0},{8,4},{12,8},{16,12},{20,16},{24,20},{28,24},{32,28}... | collective-permute-start | bytes 61448 | tf_op jit(solution)/shard_map/ppermute | solution.py:558
  196.0 2.5 %shard_map.55 = f32[4,64,256]{2,1,0:T(8,128)} custom-call(f32[2,40,128]{2,1,0:T(8,128)S(1)} %get-tuple-element.78.e1, f32[40,128]{1,0:T(8,128)S(1)} %collective-permute-done.17.e1low, f32[40,128]{1,0:T(8,128)S(1)} %collective-permute-done.18.e1high, f32[8,40,128]{2,1,0:T(8,128)S(1)} %collective-permute-done.4.low, ...), custom_call_target="tpu_custom_call" | custom-call | tf_op jit(solution)/shard_map/pallas_call | solution.py:118
  (96 shorter events, 22.7 us)
Async XLA Ops:
  6.5 142.6 %all-gather.2.cloned.1.call-start = ((), (), s32[]{:S(2)}) async-start(), calls=%async_computation.1 | async-start | bytes 1310720 | tf_op jit(solution)/shard_map/all_gather | solution.py:571
  11.3 5.9 %collective-permute-start = (f32[16,8,256]{2,1,0:T(8,128)S(1)}, f32[16,8,256]{2,1,0:T(8,128)S(1)}, u32[]{:S(2)}, u32[]{:S(2)}) collective-permute-start(f32[16,8,256]{2,1,0:T(8,128)S(1)} %get-tuple-element.46), channel_id=1, source_target_pairs={{0,1},{1,2},{2,3},{3,0},{4,5},{5,6},{6,7},{7,4},{8,9},{9,10},{10,1... | collective-permute-start | bytes 393224 | tf_op jit(solution)/shard_map/ppermute | solution.py:558
  13.5 3.8 %collective-permute-start.1 = (f32[16,8,256]{2,1,0:T(8,128)S(1)}, f32[16,8,256]{2,1,0:T(8,128)S(1)}, u32[]{:S(2)}, u32[]{:S(2)}) collective-permute-start(f32[16,8,256]{2,1,0:T(8,128)S(1)} %get-tuple-element.47), channel_id=1, source_target_pairs={{0,3},{1,0},{2,1},{3,2},{4,7},{5,4},{6,5},{7,6},{8,11},{9,8},{10,9... | collective-permute-start | bytes 393224 | tf_op jit(solution)/shard_map/ppermute | solution.py:558
  18.8 64.2 %collective-permute-start.3 = (f32[8,80,256]{2,1,0:T(8,128)S(1)}, f32[8,80,256]{2,1,0:T(8,128)S(1)}, u32[]{:S(2)}, u32[]{:S(2)}) collective-permute-start(f32[8,80,256]{2,1,0:T(8,128)S(1)} %get-tuple-element.51), channel_id=1, source_target_pairs={{0,252},{4,0},{8,4},{12,8},{16,12},{20,16},{24,20},{28,24},{32,28}... | collective-permute-start | bytes 1966088 | tf_op jit(solution)/shard_map/ppermute | solution.py:558
  76.0 7.1 %collective-permute-start.2 = (f32[7,80,256]{2,1,0:T(8,128)}, f32[7,80,256]{2,1,0:T(8,128)S(1)}, u32[]{:S(2)}, u32[]{:S(2)}) collective-permute-start(f32[7,80,256]{2,1,0:T(8,128)} %copy-done.35), channel_id=1, source_target_pairs={{0,4},{4,8},{8,12},{12,16},{16,20},{20,24},{24,28},{28,32},{32,36}... | collective-permute-start | bytes 1720328 | tf_op jit(solution)/shard_map/ppermute | solution.py:558
  90.4 41.6 %copy-start.19 = (f32[4,40,128]{2,1,0:T(8,128)}, f32[4,40,128]{2,1,0:T(8,128)S(1)}, u32[]{:S(2)}) copy-start(f32[4,40,128]{2,1,0:T(8,128)S(1)} %get-tuple-element.55.g1) | copy-start | bytes 245764
  90.4 6.8 %collective-permute-start.4 = (f32[8,40,128]{2,1,0:T(8,128)S(1)}, f32[8,40,128]{2,1,0:T(8,128)S(1)}, u32[]{:S(2)}, u32[]{:S(2)}) collective-permute-start(f32[8,40,128]{2,1,0:T(8,128)S(1)} %get-tuple-element.52.own), channel_id=1, source_target_pairs={{0,4},{4,8},{8,12},{12,16},{16,20},{20,24},{24,28},{28,32},{32,36}... | collective-permute-start | bytes 491528 | tf_op jit(solution)/shard_map/ppermute | solution.py:558
  92.7 5.3 %collective-permute-start.5 = (f32[8,40,128]{2,1,0:T(8,128)}, f32[8,40,128]{2,1,0:T(8,128)S(1)}, u32[]{:S(2)}, u32[]{:S(2)}) collective-permute-start(f32[8,40,128]{2,1,0:T(8,128)} %get-tuple-element.53), channel_id=1, source_target_pairs={{0,252},{4,0},{8,4},{12,8},{16,12},{20,16},{24,20},{28,24},{32,28}... | collective-permute-start | bytes 491528 | tf_op jit(solution)/shard_map/ppermute | solution.py:558
  98.4 13.0 %copy-start.33 = (f32[4,40,128]{2,1,0:T(8,128)}, f32[4,40,128]{2,1,0:T(8,128)S(1)}, u32[]{:S(2)}) copy-start(f32[4,40,128]{2,1,0:T(8,128)S(1)} %get-tuple-element.77.f) | copy-start | bytes 245764
  98.4 13.0 %collective-permute-start.6 = (f32[32,128]{1,0:T(8,128)S(1)}, f32[32,128]{1,0:T(8,128)S(1)}, u32[]{:S(2)}, u32[]{:S(2)}) collective-permute-start(f32[32,128]{1,0:T(8,128)S(1)} %get-tuple-element.57), channel_id=1, source_target_pairs={{0,1},{1,2},{2,3},{3,0},{4,5},{5,6},{6,7},{7,4},{8,9},{9,10},{10,1... | collective-permute-start | bytes 49160 | tf_op jit(solution)/shard_map/ppermute | solution.py:558
  99.1 12.2 %collective-permute-start.7 = (f32[32,128]{1,0:T(8,128)S(1)}, f32[32,128]{1,0:T(8,128)S(1)}, u32[]{:S(2)}, u32[]{:S(2)}) collective-permute-start(f32[32,128]{1,0:T(8,128)S(1)} %get-tuple-element.58), channel_id=1, source_target_pairs={{0,3},{1,0},{2,1},{3,2},{4,7},{5,4},{6,5},{7,6},{8,11},{9,8},{10,9... | collective-permute-start | bytes 49160 | tf_op jit(solution)/shard_map/ppermute | solution.py:558
  101.1 10.2 %collective-permute-start.8 = (f32[16,128]{1,0:T(8,128)S(1)}, f32[16,128]{1,0:T(8,128)S(1)}, u32[]{:S(2)}, u32[]{:S(2)}) collective-permute-start(f32[16,128]{1,0:T(8,128)S(1)} %get-tuple-element.56.f2), channel_id=1, source_target_pairs={{0,2},{1,3},{2,0},{3,1},{4,6},{5,7},{6,4},{7,5},{8,10},{9,11},{10,... | collective-permute-start | bytes 24584 | tf_op jit(solution)/shard_map/ppermute | solution.py:558
  112.0 20.0 %copy-start.23 = (f32[272,128]{1,0:T(8,128)}, f32[272,128]{1,0:T(8,128)S(1)}, u32[]{:S(2)}) copy-start(f32[272,128]{1,0:T(8,128)S(1)} %get-tuple-element.63.msg) | copy-start | bytes 417796
  112.0 18.2 %collective-permute-start.9 = (f32[272,128]{1,0:T(8,128)S(1)}, f32[272,128]{1,0:T(8,128)S(1)}, u32[]{:S(2)}, u32[]{:S(2)}) collective-permute-start(f32[272,128]{1,0:T(8,128)S(1)} %get-tuple-element.63.msg), channel_id=1, source_target_pairs={{0,4},{4,8},{8,12},{12,16},{16,20},{20,24},{24,28},{28,32},{32,36}... | collective-permute-start | bytes 417800 | tf_op jit(solution)/shard_map/ppermute | solution.py:558
  115.9 14.3 %collective-permute-start.10 = (f32[272,128]{1,0:T(8,128)S(1)}, f32[272,128]{1,0:T(8,128)S(1)}, u32[]{:S(2)}, u32[]{:S(2)}) collective-permute-start(f32[272,128]{1,0:T(8,128)S(1)} %get-tuple-element.63.msg), channel_id=1, source_target_pairs={{0,252},{4,0},{8,4},{12,8},{16,12},{20,16},{24,20},{28,24},{32,28}... | collective-permute-start | bytes 417800 | tf_op jit(solution)/shard_map/ppermute | solution.py:558
  122.8 7.4 %collective-permute-start.11 = (f32[64,128]{1,0:T(8,128)S(1)}, f32[64,128]{1,0:T(8,128)S(1)}, u32[]{:S(2)}, u32[]{:S(2)}) collective-permute-start(f32[64,128]{1,0:T(8,128)S(1)} %get-tuple-element.64), channel_id=1, source_target_pairs={{0,8},{4,12},{8,16},{12,20},{16,24},{20,28},{24,32},{28,36},{32,40... | collective-permute-start | bytes 98312 | tf_op jit(solution)/shard_map/ppermute | solution.py:558
  122.8 7.4 %collective-permute-start.12 = (f32[64,128]{1,0:T(8,128)S(1)}, f32[64,128]{1,0:T(8,128)S(1)}, u32[]{:S(2)}, u32[]{:S(2)}) collective-permute-start(f32[64,128]{1,0:T(8,128)S(1)} %get-tuple-element.64), channel_id=1, source_target_pairs={{0,248},{4,252},{8,0},{12,4},{16,8},{20,12},{24,16},{28,20},{32,24... | collective-permute-start | bytes 98312 | tf_op jit(solution)/shard_map/ppermute | solution.py:558
  131.9 32.3 %all-to-all-start = ((f32[64,8,128]{2,1,0:T(8,128)}), f32[64,8,128]{2,1,0:T(8,128)S(1)}, u32[]{:S(2)}, u32[]{:S(2)}) async-start(f32[64,8,128]{2,1,0:T(8,128)} %get-tuple-element.65), calls=%async_computation | async-start | bytes 524288 | tf_op jit(solution)/shard_map/all_to_all | solution.py:604
  144.0 20.2 %collective-permute-start.13 = (f32[64,128]{1,0:T(8,128)}, f32[64,128]{1,0:T(8,128)S(1)}, u32[]{:S(2)}, u32[]{:S(2)}) collective-permute-start(f32[64,128]{1,0:T(8,128)} %get-tuple-element.76), channel_id=1, source_target_pairs={{0,8},{4,12},{8,16},{12,20},{16,24},{20,28},{24,32},{28,36},{32,40... | collective-permute-start | bytes 98312 | tf_op jit(solution)/shard_map/ppermute | solution.py:558
  145.4 18.8 %collective-permute-start.14 = (f32[64,128]{1,0:T(8,128)}, f32[64,128]{1,0:T(8,128)S(1)}, u32[]{:S(2)}, u32[]{:S(2)}) collective-permute-start(f32[64,128]{1,0:T(8,128)} %get-tuple-element.76), channel_id=1, source_target_pairs={{0,248},{4,252},{8,0},{12,4},{16,8},{20,12},{24,16},{28,20},{32,24... | collective-permute-start | bytes 98312 | tf_op jit(solution)/shard_map/ppermute | solution.py:558
  170.8 19.0 %copy-start.20 = (f32[4,40,128]{2,1,0:T(8,128)S(1)}, f32[4,40,128]{2,1,0:T(8,128)}, u32[]{:S(2)}) copy-start(f32[4,40,128]{2,1,0:T(8,128)} %copy-done.19) | copy-start | bytes 245764
  170.8 19.0 %copy-start.24 = (f32[272,128]{1,0:T(8,128)S(1)}, f32[272,128]{1,0:T(8,128)}, u32[]{:S(2)}) copy-start(f32[272,128]{1,0:T(8,128)} %copy-done.23) | copy-start | bytes 417796
  170.8 19.0 %copy-start.34 = (f32[4,40,128]{2,1,0:T(8,128)S(1)}, f32[4,40,128]{2,1,0:T(8,128)}, u32[]{:S(2)}) copy-start(f32[4,40,128]{2,1,0:T(8,128)} %copy-done.33) | copy-start | bytes 245764
  170.8 25.2 %copy-start.14 = (f32[6,80,256]{2,1,0:T(8,128)S(1)}, f32[6,80,256]{2,1,0:T(8,128)}, u32[]{:S(2)}) copy-start(f32[6,80,256]{2,1,0:T(8,128)} %copy-done.13) | copy-start | bytes 1474564
  170.8 25.2 %copy-start.16 = (f32[6,80,256]{2,1,0:T(8,128)S(1)}, f32[6,80,256]{2,1,0:T(8,128)}, u32[]{:S(2)}) copy-start(f32[6,80,256]{2,1,0:T(8,128)} %copy-done.15) | copy-start | bytes 1474564
  170.8 25.2 %copy-start.18 = (f32[6,80,256]{2,1,0:T(8,128)S(1)}, f32[6,80,256]{2,1,0:T(8,128)}, u32[]{:S(2)}) copy-start(f32[6,80,256]{2,1,0:T(8,128)} %copy-done.17) | copy-start | bytes 1474564
  186.3 9.7 %copy-start.6 = (f32[7,80,256]{2,1,0:T(8,128)S(1)}, f32[7,80,256]{2,1,0:T(8,128)}, u32[]{:S(2)}) copy-start(f32[7,80,256]{2,1,0:T(8,128)} %copy-done.5) | copy-start | bytes 1720324
  186.3 9.7 %copy-start.12 = (f32[6,80,256]{2,1,0:T(8,128)S(1)}, f32[6,80,256]{2,1,0:T(8,128)}, u32[]{:S(2)}) copy-start(f32[6,80,256]{2,1,0:T(8,128)} %copy-done.11) | copy-start | bytes 1474564
  186.3 1.5 collective-permute-start.15
  186.4 3.4 %collective-permute-start.16 = (f32[64,128]{1,0:T(8,128)S(1)}, f32[64,128]{1,0:T(8,128)S(1)}, u32[]{:S(2)}, u32[]{:S(2)}) collective-permute-start(f32[64,128]{1,0:T(8,128)S(1)} %shard_map.53.e2), channel_id=1, source_target_pairs={{0,252},{4,0},{8,4},{12,8},{16,12},{20,16},{24,20},{28,24},{32,28}... | collective-permute-start | bytes 98312 | tf_op jit(solution)/shard_map/ppermute | solution.py:558
  191.0 4.7 %collective-permute-start.17 = (f32[40,128]{1,0:T(8,128)S(1)}, f32[40,128]{1,0:T(8,128)S(1)}, u32[]{:S(2)}, u32[]{:S(2)}) collective-permute-start(f32[40,128]{1,0:T(8,128)S(1)} %get-tuple-element.79), channel_id=1, source_target_pairs={{0,4},{4,8},{8,12},{12,16},{16,20},{20,24},{24,28},{28,32},{32,36}... | collective-permute-start | bytes 61448 | tf_op jit(solution)/shard_map/ppermute | solution.py:558
  191.1 4.9 %collective-permute-start.18 = (f32[40,128]{1,0:T(8,128)S(1)}, f32[40,128]{1,0:T(8,128)S(1)}, u32[]{:S(2)}, u32[]{:S(2)}) collective-permute-start(f32[40,128]{1,0:T(8,128)S(1)} %get-tuple-element.80), channel_id=1, source_target_pairs={{0,252},{4,0},{8,4},{12,8},{16,12},{20,16},{24,20},{28,24},{32,28}... | collective-permute-start | bytes 61448 | tf_op jit(solution)/shard_map/ppermute | solution.py:558
  (25 other events, 21.3 us)
Sparse Core Ops, SparseCore 0:
  76.1 20.9 all-gather.1
where the time goes:
time: 209 us; the launch traced here: 205 us
  blocking collectives  63.1 us (30%)
  starting transfers between devices  54.4 us (26%)
  Pallas kernels  35.8 us (17%)
  local copies, waits for them, and re-layouts  21.3 us (10%)
  waiting for transfers between devices  17.1 us (8%)
  between operations  13.6 us (7%)
    all_gather x1, blocking collectives, body(): coef3 = lax.all_gather(part3, 'wide', tiled=True)  53.6 us
    ppermute x19, starting transfers between devices, shift(): return lax.ppermute(x, axis, [(i, (i + by) % count) for i in range(count)])  42.3 us
    pallas_call x10, Pallas kernels, run(): pl.pallas_call(kernel, out_shape=[jax.ShapeDtypeStruct(s, F32) for s in o...  35.8 us
    unnamed x72, local copies, waits for them, and re-layouts  21.3 us
    ppermute x19, waiting for transfers between devices, shift(): return lax.ppermute(x, axis, [(i, (i + by) % count) for i in range(count)])  17.1 us
    all_to_all x1, starting transfers between devices, body(): lax.all_to_all(send, 'wide', split_axis=0, concat_axis=0, tiled=True)  12 us
    all_gather x1, blocking collectives, body(): coef2 = lax.all_gather(coef2, 'narrow', tiled=True)  9.42 us
  transfers between devices with their start and end apart: 21, of which 9 were waited for; matrix products, arithmetic and copies ran while one was open for 0% of the time, Pallas kernels for 7%

commit v1 on v0

--- a/solution.py
+++ b/solution.py
@@ -112,49 +112,93 @@
     return u + KEEP * (u - v) + GAIN * (g * (f + near) - u)
 
 
-def call(kernel, outs, scratch=(), smem=0):
+def call(kernel, outs, scratch=(), places=(), limit=8, alias=None):
+    places = dict(places)
+
     def run(*args):
-        in_specs = [pl.BlockSpec(memory_space=pltpu.SMEM if i < smem else pltpu.VMEM) for i in range(len(args))]
+        in_specs = [pl.BlockSpec(memory_space=places.get(i, pltpu.VMEM)) for i in range(len(args))]
         return pl.pallas_call(
             kernel,
             out_shape=[jax.ShapeDtypeStruct(s, F32) for s in outs],
             in_specs=in_specs,
             out_specs=[pl.BlockSpec(memory_space=pltpu.VMEM)] * len(outs),
-            scratch_shapes=[pltpu.VMEM(s, F32) for s in scratch],
-            compiler_params=pltpu.CompilerParams(vmem_limit_bytes=40 * 2**20),
+            scratch_shapes=[pltpu.VMEM(s, F32) if isinstance(s, tuple) else s for s in scratch],
+            input_output_aliases=alias or {},
+            compiler_params=pltpu.CompilerParams(vmem_limit_bytes=limit * 2**20),
         )(*args)
 
     return run
 
 
-def start_kernel(f, c1, c2, c3, up, down, coef3, scr):
+SCALARS = {0: pltpu.SMEM}
+
+
+def two_blocks(x):
+    half = x.shape[0] // 2
+    return jnp.where(iota((half, 128), 1) < 64, x[:half], x[half:])
+
+
+def start_kernel(f, c1, c2, c3, own, up, down, far, scr, sems):
+    copies = []
     for a, ref in enumerate((f, c1, c2, c3)):
-        up[4 * a : 4 * a + 4] = ref[:, 56:64, :]
-        down[4 * a : 4 * a + 4] = ref[:, 0:8, :]
-    k1 = jnp.concatenate([c1[0], c1[2]], axis=0)
-    k2 = jnp.concatenate([c2[0] + c2[1], c2[2] + c2[3]], axis=0)
-    k3 = jnp.concatenate([c3[0] + c3[1], c3[2] + c3[3]], axis=0)
+        copy = pltpu.make_async_copy(ref, own.at[pl.ds(4 * a, 4), pl.ds(8, 64), :], sems.at[a])
+        copy.start()
+        copies.append(copy)
+    for copy in copies:
+        copy.wait()
+    inner = pl.ds(8, 64)
+    for a in range(16):
+        up[a] = own[a, 64:72, :]
+        down[a] = own[a, 8:16, :]
+    k1 = jnp.concatenate([own[4, inner], own[6, inner]], axis=0)
+    k2 = jnp.concatenate([own[8, inner] + own[9, inner], own[10, inner] + own[11, inner]], axis=0)
+    k3 = jnp.concatenate([own[12, inner] + own[13, inner], own[14, inner] + own[15, inner]], axis=0)
     k1, k2, k3 = coarse_coefs((k1, k2, k3), scr, 256, 128)
     k1, k2, k3 = k1[:32], k2[:32] + k2[32:], k3[:32] + k3[32:]
     k1, k2, k3 = coarse_coefs((k1, k2, k3), scr, 128, 64)
-    k1, k2, k3 = coarse_coefs((k1, k2, k3), scr, 128, 32)
-    lane = iota(k1.shape, 1)
-    coef3[...] = jnp.where(lane < 32, k1, jnp.where(lane < 64, k2, k3))
-
-
-def pad_kernel(f, c1, c2, c3, low, high, own, coef1, up, down, scr):
-    for a, ref in enumerate((f, c1, c2, c3)):
-        for p in range(4):
-            own[4 * a + p, 0:8] = low[4 * a + p]
-            own[4 * a + p, 8:72] = ref[p]
-            own[4 * a + p, 72:80] = high[4 * a + p]
+    far[0, :, 0:128] = two_blocks(k1)
+    far[0, :, 128:256] = two_blocks(k2)
+    far[1, :, 0:128] = two_blocks(k3)
+    far[1, :, 128:256] = jnp.zeros((8, 128), F32)
+    both, alone = pairs_of_lanes(128, 32), pairs_of_lanes(128, 32, even=True)
+    block = iota((2, 128), 1) // 32
+    for a, (k, lanes) in enumerate(((k1, both), (k2, both), (k3, alone))):
+        scr[0:16, :] = 0.25 * mul(k, lanes)
+        packed = 0.0
+        for q in range(4):
+            part = scr[pl.ds(2 * q, 2, stride=8), :]
+            if a != 1:
+                part = part + scr[pl.ds(2 * q + 1, 2, stride=8), :]
+            packed = jnp.where(block == q, part, packed)
+        far[1, 2 * a : 2 * a + 2, 128:256] = packed
+    up[16:18] = far[...]
+    down[16:18] = far[...]
+
+
+def pad_kernel(place, old, low, high, mine, far, own, coef1, coef2, coef3, up, down, scr):
+    n = place[1]
+    for a in range(16):
+        own[a, 0:8] = low[a]
+        own[a, 8:72] = old[a, 8:72]
+        own[a, 72:80] = high[a]
+    row = iota((8, 128), 0)
+    coef3[...] = jnp.zeros((32, 128), F32)
+    for ref, at, by in ((mine, 0, 0), (high, 16, 1), (far, 0, 2), (low, 16, 3)):
+        m = lax.rem(n + by, 4)
+        for a in range(3):
+            tile = ref[at + a // 2, :, 128 * (a % 2) : 128 * (a % 2) + 128]
+            here = pl.multiple_of(16 * m, 16)
+            coef2[a, pl.ds(here, 8), :] = spread_block(tile, 0, 64)
+            coef2[a, pl.ds(here + 8, 8), :] = spread_block(tile, 1, 64)
+            part = pltpu.roll(ref[at + 1, :, 128:256], lax.rem(2 * m + 8 - 2 * a, 8), 0)
+            coef3[8 * a : 8 * a + 8] = jnp.where(row // 2 == m, part, coef3[8 * a : 8 * a + 8])
     for p, out, slot in ((1, down, 5), (2, up, 4)):
         diag = diagonal(SIG[0], own[4 + p], own[5 + p], own[8 + p], own[12 + p])
-        out[slot] = own[p] / diag / THETA
+        out[80 * slot : 80 * slot + 80] = own[p] / diag / THETA
     for a in range(4):
-        up[a] = own[4 * a + 3]
-        down[a] = own[4 * a]
-    down[4] = own[5]
+        up[80 * a : 80 * a + 80] = own[4 * a + 3]
+        down[80 * a : 80 * a + 80] = own[4 * a]
+    down[320:400] = own[5]
     k1 = jnp.concatenate([own[4], own[6]], axis=0)
     k2 = jnp.concatenate([own[8] + own[9], own[10] + own[11]], axis=0)
     k3 = jnp.concatenate([own[12] + own[13], own[14] + own[15]], axis=0)
@@ -162,20 +206,20 @@
     for a in range(3):
         for p in range(2):
             coef1[2 * a + p] = coarse[a][40 * p : 40 * p + 40]
-    for out, at in ((up, 5), (down, 6)):
-        out[at, 0:40, 0:128] = coef1[0]
-        out[at, 0:40, 128:256] = coef1[1]
-        out[at, 40:80, 0:128] = coef1[2]
-        out[at, 40:80, 128:256] = coef1[3]
-        out[at + 1, 0:40, 0:128] = coef1[4]
-        out[at + 1, 0:40, 128:256] = coef1[5]
-        out[at + 1, 40:80, :] = jnp.zeros((40, 256), F32)
+    for out, at in ((up, 400), (down, 480)):
+        for k in range(6):
+            row, lane = at + 40 * (k // 2), 128 * (k % 2)
+            out[row : row + 40, lane : lane + 128] = coef1[k]
+        for a in range(3):
+            both = two_blocks(coef2[a])
+            row = at + 120 + 16 * a
+            out[row : row + 16, 0:128] = both[:16]
+            out[row : row + 16, 128:256] = both[16:]
 
 
 def unpack(ref, at, index):
-    plane, slot = at + index // 4, index % 4
-    row, lane = 40 * (slot // 2), 128 * (slot % 2)
-    return ref[plane, row : row + 40, lane : lane + 128]
+    row, lane = at + 40 * (index // 2), 128 * (index % 2)
+    return ref[row : row + 40, lane : lane + 128]
 
 
 CHUNK = 16
@@ -215,14 +259,14 @@
     return SIG[0] + c1[q, here, :] + c1[q + 1, here, :] + k2 + h2 + k3 + roll(k3, -1, 1)
 
 
-def fine_pre_kernel(own, coef1, low, high, f, c1, c2, c3, g, u2, w1, g1, msg_up, msg_down, f1, coef2, u1, res, scr):
+def fine_pre_kernel(own, coef1, coef2, low, high, f, c1, c2, c3, g, u2, w1, g1, msg_up, msg_down, c2w, f1, u1, res, scr):
     for a, ref in enumerate((f, c1, c2, c3)):
-        ref[0] = low[a]
+        ref[0] = low[80 * a : 80 * a + 80]
         ref[1:5] = own[4 * a : 4 * a + 4]
-        ref[5] = high[a]
-    c1[6] = high[4]
-    u1[0] = low[4]
-    u1[7] = high[5]
+        ref[5] = high[80 * a : 80 * a + 80]
+    c1[6] = high[320:400]
+    u1[0] = low[320:400]
+    u1[7] = high[400:480]
 
     def smooth_first(q, carry):
         def rows(r0, n):
@@ -265,9 +309,9 @@
     f1[1] = coarse[40:]
     for a in range(3):
         for p in range(2):
-            w1[6 * a + p] = unpack(low, 5, 2 * a + p)
+            w1[6 * a + p] = unpack(low, 400, 2 * a + p)
             w1[6 * a + 2 + p] = coef1[2 * a + p]
-            w1[6 * a + 4 + p] = unpack(high, 6, 2 * a + p)
+            w1[6 * a + 4 + p] = unpack(high, 480, 2 * a + p)
     for k in range(4):
         p = k + 1
         g1[k] = 1.0 / diagonal(SIG[1], w1[p], w1[p + 1], w1[6 + p], w1[12 + p])
@@ -281,13 +325,14 @@
         out[5] = u2[plane, 0:40, 128:256]
         out[6] = u2[plane, 40:80, 0:128]
         out[7] = u2[plane, 40:80, 128:256]
-    k1 = jnp.concatenate([w1[0], w1[2], w1[4]], axis=0)
-    k2 = jnp.concatenate([w1[6 + 2 * k] + w1[7 + 2 * k] for k in range(3)], axis=0)
-    k3 = jnp.concatenate([w1[12 + 2 * k] + w1[13 + 2 * k] for k in range(3)], axis=0)
-    coarse = coarse_coefs((k1, k2, k3), scr, 128, 64)
     for a in range(3):
-        for k in range(3):
-            coef2[3 * a + k] = coarse[a][20 * k + 2 : 20 * k + 18]
+        c2w[3 * a + 1] = coef2[a]
+        for k, ref, at in ((0, low, 520), (2, high, 600)):
+            row = at + 16 * a
+            for half in range(2):
+                part = ref[row : row + 16, 128 * half : 128 * half + 128]
+                c2w[3 * a + k, 16 * half : 16 * half + 16] = spread_block(part, 0, 64)
+                c2w[3 * a + k, 32 + 16 * half : 48 + 16 * half] = spread_block(part, 1, 64)
 
 
 def middle_pre_kernel(own, low, high, w1, g1, f, u2, f2, up, down, u1, scr):
@@ -315,14 +360,11 @@
         down[16 + 8 * p : 24 + 8 * p] = u2[2 + p, 4:12]
 
 
-def coarse_start_kernel(place, f2, low, high, far, coef2, u2fine, c2w, own, msg, far_msg):
+def coarse_start_kernel(place, f2, low, high, far, c2w, u2fine, own, msg, far_msg):
     n = place[1]
     for piece, by in ((f2, 0), (high, 1), (far, 2), (low, 3)):
         at = pl.multiple_of(16 * lax.rem(n + by, 4), 16)
         own[0, pl.ds(at, 16), :] = piece[0:16, :]
-    for k in range(9):
-        for m in range(4):
-            c2w[k, 16 * m : 16 * m + 16] = coef2[9 * m + k]
     g = 1.0 / diagonal(SIG[2], c2w[1], c2w[2], c2w[4], c2w[7])
     own[1] = g
     start = own[0] * g * (1.0 / THETA)
@@ -349,151 +391,185 @@
     k1, k2, k3 = c2w[1], c2w[4], c2w[7]
     near = gather_sum(u2[0], u2[1], u2[2], k1, h1[1], k2, k3)
     res = f[1] + near - diagonal(SIG[2], k1, h1[1], k2, k3) * u2[1]
-    part = 0.5 * pair_rows(mul(res, pairs_of_lanes(128, 32)), scr)
+    scr[...] = 0.5 * mul(res, pairs_of_lanes(128, 32))
     block = iota((8, 128), 1) // 32
-    packed = part[0:8]
-    for q in range(1, 4):
-        packed = jnp.where(block == q, part[8 * q : 8 * q + 8], packed)
+    packed = 0.0
+    for q in range(4):
+        part = scr[pl.ds(2 * q, 8, stride=8), :] + scr[pl.ds(2 * q + 1, 8, stride=8), :]
+        packed = jnp.where(block == q, part, packed)
     for w in range(send.shape[0]):
         send[w] = packed
 
 
-def rows_loop(count, body):
-    def step(j, carry):
-        body(j)
-        return carry
-
-    lax.fori_loop(0, count, step, 0)
-
-
-def coarse_coef_kernel(coef3, c1, c2, c3, g3, d1, d2, d3, g4, scr):
-    n3, n4 = c1.shape[0] - 1, d1.shape[0] - 1
-
-    def unpack_plane(j):
-        for m in range(4):
-            even, odd = coef3[m, 2 * j], coef3[m, 2 * j + 1]
-            rows = pl.ds(8 * m, 8)
-            c1[j, rows, :] = spread_block(even, 0, 32)
-            c2[j, rows, :] = spread_block(even + odd, 1, 32)
-            c3[j, rows, :] = spread_block(even + odd, 2, 32)
-
-    rows_loop(n3, unpack_plane)
-    c1[n3] = c1[0]
-
-    def inverse3(j):
-        g3[j] = 1.0 / diagonal(SIG[3], c1[j], c1[j + 1], c2[j], c3[j])
-
-    rows_loop(n3, inverse3)
-    k1 = jnp.concatenate([c1[2 * j] for j in range(n4)], axis=0)
-    k2 = jnp.concatenate([c2[2 * j] + c2[2 * j + 1] for j in range(n4)], axis=0)
-    k3 = jnp.concatenate([c3[2 * j] + c3[2 * j + 1] for j in range(n4)], axis=0)
-    coarse = coarse_coefs((k1, k2, k3), scr, 128, 16)
-    for a, ref in enumerate((d1, d2, d3)):
-        for j in range(n4):
-            ref[j] = coarse[a][16 * j : 16 * j + 16]
-    d1[n4] = d1[0]
-
-    def inverse4(j):
-        g4[j] = 1.0 / diagonal(SIG[4], d1[j], d1[j + 1], d2[j], d3[j])
-
-    rows_loop(n4, inverse4)
+def packed_sum(below, x, above, c1, h1, c2, c3, width, blocks):
+    lane = iota(x.shape, 2)
+    block, inner = lane // width % blocks, lane % width
+
+    def second_down(x):
+        x = pltpu.roll(x, width, 2)
+        return jnp.where(block == 0, pltpu.roll(x, 1, 1), x)
+
+    def second_up(x):
+        x = pltpu.roll(x, 128 - width, 2)
+        return jnp.where(block == blocks - 1, pltpu.roll(x, 7, 1), x)
+
+    def third_down(x):
+        return jnp.where(inner == 0, pltpu.roll(x, 129 - width, 2), pltpu.roll(x, 1, 2))
+
+    def third_up(x):
+        return jnp.where(inner == width - 1, pltpu.roll(x, width - 1, 2), pltpu.roll(x, 127, 2))
+
+    first = c1 * below + h1 * above
+    second = c2 * second_down(x) + second_up(c2 * x)
+    third = c3 * third_down(x) + third_up(c3 * x)
+    return first + second + third
+
+
+def packed_diagonal(sig, c1, h1, c2, c3, width, blocks):
+    lane = iota(c1.shape, 2)
+    block, inner = lane // width % blocks, lane % width
+    h2 = pltpu.roll(c2, 128 - width, 2)
+    h2 = jnp.where(block == blocks - 1, pltpu.roll(h2, 7, 1), h2)
+    h3 = jnp.where(inner == width - 1, pltpu.roll(c3, width - 1, 2), pltpu.roll(c3, 127, 2))
+    return sig + c1 + h1 + c2 + h2 + c3 + h3
+
+
+def fold_matrix(even2=False, even3=False):
+    k, j = iota((128, 128), 0), iota((128, 128), 1)
+    k2, k3, j2, j3 = k // 32, k % 32, j // 16 % 2, j % 16
+    hit2 = k2 == 2 * j2 if even2 else k2 // 2 == j2
+    hit3 = k3 == 2 * j3 if even3 else k3 // 2 == j3
+    return (hit2 & hit3).astype(F32)
+
+
+def wrap(ref, count):
+    ref[0] = ref[count]
+    ref[count + 1] = ref[1]
 
 
 def around(j, n):
     return lax.rem(j + n, n)
 
 
-def bottom_kernel(place, parts, c1, c2, c3, g3, d1, d2, d3, g4, own, c2w, low, high, u2w, u2low, u2high, out,
-                  f3, u1, u2, res, f4, ua, ub, st, v3, w3, scr):
+STEP = 8
+THREE, FOUR = (32, 4), (16, 2)
+
+
+def bottom_kernel(place, parts, coef3, own, c2w, low, high, u2w, u2low, u2high, out,
+                  f3, c1, c2, c3, d3, g3, u1, u2, res, f4, d1, d2, e3, g4, ua, ub, st, scr):
     n3, n4 = f3.shape[0], f4.shape[0]
 
-    def unpack_plane(j):
-        both = parts[2 * j] + parts[2 * j + 1]
-        for q in range(4):
-            f3[j, 8 * q : 8 * q + 8] = spread_block(both, q, 32)
-        u1[j] = f3[j] * g3[j] * (1.0 / THETA)
-
-    rows_loop(n3, unpack_plane)
+    def loop(body):
+        def step(c, carry):
+            body(pl.multiple_of(c * STEP, STEP))
+            return carry
+
+        lax.fori_loop(0, n3 // STEP, step, 0)
+
+    def load(j):
+        here = pl.ds(j, STEP)
+        f3[here] = parts[here, 0] + parts[here, 1]
+        c1[here] = coef3[here, 0, 0]
+        c2[here] = coef3[here, 0, 1] + coef3[here, 1, 1]
+        c3[here] = coef3[here, 0, 2] + coef3[here, 1, 2]
+
+    loop(load)
+    c1[n3] = c1[0]
+
+    def start(j):
+        here = pl.ds(j, STEP)
+        diag = packed_diagonal(SIG[3], c1[here], c1[pl.ds(j + 1, STEP)], c2[here], c3[here], *THREE)
+        inverse = 1.0 / diag
+        d3[here] = diag
+        g3[here] = inverse
+        u1[pl.ds(j + 1, STEP)] = f3[here] * inverse * (1.0 / THETA)
+
+    loop(start)
+    wrap(u1, n3)
+
+    def near3(u, j):
+        here = pl.ds(j, STEP)
+        x = u[pl.ds(j + 1, STEP)]
+        args = (c1[here], c1[pl.ds(j + 1, STEP)], c2[here], c3[here])
+        return here, x, packed_sum(u[here], x, u[pl.ds(j + 2, STEP)], *args, *THREE)
 
     def pre(j):
-        u2[j] = smooth_two(u1[j], u1[around(j - 1, n3)], u1[around(j + 1, n3)], f3[j], g3[j], c1[j], c1[j + 1], c2[j], c3[j])
-
-    rows_loop(n3, pre)
-
-    def residual(k):
-        total = 0.0
-        for half in range(2):
-            j = 2 * k + half
-            near = gather_sum(u2[around(j - 1, n3)], u2[j], u2[around(j + 1, n3)], c1[j], c1[j + 1], c2[j], c3[j])
-            total = total + (f3[j] + near - diagonal(SIG[3], c1[j], c1[j + 1], c2[j], c3[j]) * u2[j])
-        res[pl.ds(pl.multiple_of(32 * k, 32), 32), :] = total
-
-    rows_loop(n4, residual)
-    coarse = 0.5 * pair_rows(mul(res[0 : 32 * n4, :], pairs_of_lanes(128, 16)), scr)
-    for k in range(n4):
-        f4[k] = coarse[16 * k : 16 * k + 16]
-
-    def first4(k):
-        x = f4[k] * g4[k] * (1.0 / THETA)
-        ua[k] = x
-        st[k] = x
-
-    rows_loop(n4, first4)
+        here, x, near = near3(u1, j)
+        u2[pl.ds(j + 1, STEP)] = (1.0 + KEEP) * x + GAIN * (g3[here] * (f3[here] + near) - x)
+
+    loop(pre)
+    wrap(u2, n3)
+
+    def residual(j):
+        here, x, near = near3(u2, j)
+        left = (f3[here] + near - d3[here] * x).reshape(STEP // 2, 2, 8, 128)
+        res[pl.ds(j // 2, STEP // 2)] = left[:, 0] + left[:, 1]
+
+    loop(residual)
+
+    def fold(x, *even):
+        return mul(x.reshape(8 * n4, 128), fold_matrix(*even)).reshape(n4, 8, 128)
+
+    def halves(ref):
+        x = ref[0:n3].reshape(n4, 2, 8, 128)
+        return x[:, 0], x[:, 1]
+
+    f4[...] = 0.5 * fold(res[...])
+    d1[0:n4] = 0.25 * fold(halves(c1)[0])
+    d1[n4] = d1[0]
+    d2[...] = 0.25 * fold(sum(halves(c2)), True, False)
+    e3[...] = 0.25 * fold(sum(halves(c3)), False, True)
+    coefs4 = (d1[0:n4], d1[1 : n4 + 1], d2[...], e3[...])
+    g4[...] = 1.0 / packed_diagonal(SIG[4], *coefs4, *FOUR)
+    x = f4[...] * g4[...] * (1.0 / THETA)
+    ua[1 : n4 + 1] = x
+    wrap(ua, n4)
+    st[...] = x
     src, dst = ua, ub
     for keep, gain in factors(4):
-        def sweep(k, src=src, dst=dst, keep=keep, gain=gain):
-            x = src[k]
-            near = gather_sum(src[around(k - 1, n4)], x, src[around(k + 1, n4)], d1[k], d1[k + 1], d2[k], d3[k])
-            step = keep * st[k] + gain * (g4[k] * (f4[k] + near) - x)
-            st[k] = step
-            dst[k] = x + step
-
-        rows_loop(n4, sweep)
+        x = src[1 : n4 + 1]
+        near = packed_sum(src[0:n4], x, src[2 : n4 + 2], d1[0:n4], d1[1 : n4 + 1], d2[...], e3[...], *FOUR)
+        step = keep * st[...] + gain * (g4[...] * (f4[...] + near) - x)
+        st[...] = step
+        dst[1 : n4 + 1] = x + step
+        wrap(dst, n4)
         src, dst = dst, src
 
     j0 = around(place[0] - 2, 2 * n3) // 2
-    for k in range(5):
-        scr[16 * k : 16 * k + 16] = src[around(around(j0 - 2, n3) // 2 + k, n4)]
-    e4 = mul(scr[0:80, :], fold_copies(16))
-    fine = twice_rows(e4, scr)
+    k, j = iota((128, 128), 0), iota((128, 128), 1)
+    unfold = (k == 16 * (j // 64) + j % 32 // 2).astype(F32)
+    coarse = jnp.concatenate([src[1 + around(around(j0 - 2, n3) // 2 + m, n4)] for m in range(4)], axis=0)
+    scr[0:32] = mul(coarse, unfold)
     odd = lax.rem(around(j0 - 2, n3), 2)
-    for k in range(5):
-        res[32 * k : 32 * k + 32] = fine[32 * k : 32 * k + 32]
-
-    def add(k):
-        j = around(j0 - 2 + k, n3)
-        at = pl.multiple_of(32 * ((odd + k) // 2), 32)
-        v3[k] = u2[j] + res[pl.ds(at, 32), :]
-
-    rows_loop(7, add)
-
-    def post1(k):
-        j = around(j0 - 2 + k, n3)
-        w3[k] = first_post(v3[k], v3[k - 1], v3[k + 1], f3[j], g3[j], c1[j], c1[j + 1], c2[j], c3[j])
-
-    lax.fori_loop(1, 6, lambda k, c: (post1(k), c)[1], 0)
-    for k in range(2, 5):
-        j = around(j0 - 2 + k, n3)
-        x = second_post(w3[k], v3[k], w3[k - 1], w3[k + 1], f3[j], g3[j], c1[j], c1[j + 1], c2[j], c3[j])
-        res[32 * (k - 2) : 32 * (k - 2) + 32] = x
-    e3 = mul(res[0:96, :], fold_copies(32))
-    fine = twice_rows(e3, scr)
-    for k in range(3):
-        res[64 * k : 64 * k + 64] = fine[64 * k : 64 * k + 64]
+    js = [around(j0 - 2 + m, n3) for m in range(7)]
+    v = [u2[1 + js[m]] + scr[pl.ds(pl.multiple_of(8 * ((odd + m) // 2), 8), 8), :] for m in range(7)]
+    v = jnp.stack(v)
+
+    def window(ref, first, count, by=0):
+        return jnp.stack([ref[js[m] + by] for m in range(first, first + count)])
+
+    def args(first, count):
+        return window(c1, first, count), window(c1, first, count, 1), window(c2, first, count), window(c3, first, count)
+
+    f, g = window(f3, 1, 5), window(g3, 1, 5)
+    near = packed_sum(v[0:5], v[1:6], v[2:7], *args(1, 5), *THREE)
+    w = v[1:6] + (1.0 / THETA) * (g * (f + near) - v[1:6])
+    near = packed_sum(w[0:3], w[1:4], w[2:5], *args(2, 3), *THREE)
+    x = w[1:4] + KEEP * (w[1:4] - v[2:5]) + GAIN * (g[1:4] * (f[1:4] + near) - w[1:4])
+    x = x.reshape(24, 128)
+    for q in range(4):
+        fine = mul(x, (k == 32 * q + j % 64 // 2).astype(F32))
+        scr[pl.ds(2 * q, 24, stride=8), :] = fine
+        scr[pl.ds(2 * q + 1, 24, stride=8), :] = fine
 
     odd = lax.rem(around(place[0] - 2, 2 * n3), 2)
     base = (u2low[...], u2w[0], u2w[1], u2w[2], u2high[...])
-    v = [base[k] + res[pl.ds(pl.multiple_of(64 * ((odd + k) // 2), 64), 64), :] for k in range(5)]
+    v = [base[m] + scr[pl.ds(pl.multiple_of(64 * ((odd + m) // 2), 64), 64), :] for m in range(5)]
     f = (low[0:64], own[0], high[0:64])
     g = (low[64:128], own[1], high[64:128])
     h1 = (c2w[1], c2w[2], high[128:192])
-    w = [first_post(v[k + 1], v[k], v[k + 2], f[k], g[k], c2w[k], h1[k], c2w[3 + k], c2w[6 + k]) for k in range(3)]
+    w = [first_post(v[m + 1], v[m], v[m + 2], f[m], g[m], c2w[m], h1[m], c2w[3 + m], c2w[6 + m]) for m in range(3)]
     out[...] = second_post(w[1], v[2], w[0], w[2], f[1], g[1], c2w[1], h1[1], c2w[4], c2w[7])
-
-
-def fold_copies(period):
-    row, col = iota((128, 128), 0), iota((128, 128), 1) % (2 * period)
-    return (row == col // 2).astype(F32)
 
 
 def middle_post_kernel(place, e2low, e2, e2high, msg, low, high, u2, f, g1, w1, out, up, down, v, w):
@@ -562,26 +638,31 @@
     wide = lax.axis_size("wide")
     n3, n4 = wide // 2, wide // 4
     place = jnp.stack([lax.axis_index("wide"), lax.axis_index("narrow")]).astype(jnp.int32)
-    inputs = (source, coef_first, coef_second, coef_third)
     big = (80, 256)
 
-    up, down, part3 = call(start_kernel, [(16, 8, 256), (16, 8, 256), (8, 128)], [(128, 128)])(*inputs)
-    low, high = shift(up, "narrow", 1), shift(down, "narrow", -1)
-    coef3 = lax.all_gather(part3, "wide", tiled=True)
-    coef3 = lax.all_gather(coef3, "narrow", tiled=True).reshape(4, wide, 8, 128)
-
-    own, coef1, up, down = call(
-        pad_kernel, [(16,) + big, (6, 40, 128), (7,) + big, (8,) + big], [(160, 128)]
-    )(*inputs, low, high)
+    own, up, down, mine = call(
+        start_kernel,
+        [(16,) + big, (18, 8, 256), (18, 8, 256), (2, 8, 256)],
+        [(128, 128), pltpu.SemaphoreType.DMA((4,))],
+        {k: pl.ANY for k in range(4)},
+    )(source, coef_first, coef_second, coef_third)
+    low, high, far = shift(up, "narrow", 1), shift(down, "narrow", -1), shift(mine, "narrow", 2)
+
+    own, coef1, coef2, coef3, up, down = call(
+        pad_kernel,
+        [(16,) + big, (6, 40, 128), (3, 64, 128), (32, 128), (568, 256), (648, 256)],
+        [(160, 128)],
+        SCALARS,
+    )(place, own, low, high, mine, far)
     low, high = shift(up, "wide", 1), shift(down, "wide", -1)
-
-    f, c1, c2, c3, g, u2, w1, g1, up, down, f1, coef2 = call(
+    coef3 = lax.all_gather(coef3, "wide", tiled=True).reshape(n3, 2, 4, 8, 128)
+
+    f, c1, c2, c3, g, u2, w1, g1, up, down, c2w, f1 = call(
         fine_pre_kernel,
         [(6,) + big, (7,) + big, (6,) + big, (6,) + big, (6,) + big, (8,) + big]
-        + [(18, 40, 128), (4, 40, 128), (8, 40, 128), (8, 40, 128), (2, 40, 128), (9, 16, 128)],
+        + [(18, 40, 128), (4, 40, 128), (8, 40, 128), (8, 40, 128), (9, 64, 128), (2, 40, 128)],
         [(8,) + big, (4,) + big, (160, 128)],
-    )(own, coef1, low, high)
-    coef2 = lax.all_gather(coef2, "narrow", tiled=True)
+    )(own, coef1, coef2, low, high)
     low1, high1 = shift(up, "wide", 1), shift(down, "wide", -1)
 
     f1w, u2m, f2, up, down = call(
@@ -591,9 +672,9 @@
     )(up, low1, high1, w1, g1)
     low, high, far = shift(up, "narrow", 1), shift(down, "narrow", -1), shift(f2, "narrow", 2)
 
-    c2w, own2, msg, far_msg = call(
-        coarse_start_kernel, [(9, 64, 128), (3, 64, 128), (272, 128), (64, 128)], smem=1
-    )(place, f2, low, high, far, coef2, u2m)
+    own2, msg, far_msg = call(
+        coarse_start_kernel, [(3, 64, 128), (272, 128), (64, 128)], (), SCALARS
+    )(place, f2, low, high, far, c2w, u2m)
     low2, high2 = shift(msg, "wide", 1), shift(msg, "wide", -1)
     low2f, high2f = shift(far_msg, "wide", 2), shift(far_msg, "wide", -2)
 
@@ -601,28 +682,23 @@
         coarse_pre_kernel, [(3, 64, 128), (64, 128), (wide, 8, 128)], [(64, 128)]
     )(own2, c2w, low2, high2, low2f, high2f)
     u2low, u2high = shift(mine, "wide", 2), shift(mine, "wide", -2)
-    parts = lax.all_to_all(send, "wide", split_axis=0, concat_axis=0, tiled=True)
-
-    three, four = (n3, 32, 128), (n4, 16, 128)
-    coefs = call(
-        coarse_coef_kernel,
-        [(n3 + 1, 32, 128), three, three, three, (n4 + 1, 16, 128), four, four, four],
-        [(n4 * 32, 128)],
-    )(coef3)
+    parts = lax.all_to_all(send, "wide", split_axis=0, concat_axis=0, tiled=True).reshape(n3, 2, 8, 128)
+
+    three, four = (n3, 8, 128), (n4, 8, 128)
     (e2,) = call(
         bottom_kernel,
         [(64, 128)],
-        [three, three, three, (max(n4 * 32, 192), 128), four, four, four, four, (7, 32, 128), (7, 32, 128)]
-        + [(max(n4 * 32, 192), 128)],
-        smem=1,
-    )(place, parts, *coefs, own2, c2w, low2, high2, u2w, u2low, u2high)
+        [three, (n3 + 1, 8, 128), three, three, three, three, (n3 + 2, 8, 128), (n3 + 2, 8, 128), four, four]
+        + [(n4 + 1, 8, 128), four, four, four, (n4 + 2, 8, 128), (n4 + 2, 8, 128), four, (192, 128)],
+        SCALARS,
+    )(place, parts, coef3, own2, c2w, low2, high2, u2w, u2low, u2high)
     e2low, e2high = shift(e2, "wide", 1), shift(e2, "wide", -1)
 
     e1, up, down = call(
         middle_post_kernel,
         [(2, 40, 128), (40, 128), (40, 128)],
         [(6, 40, 128), (6, 40, 128)],
-        smem=1,
+        SCALARS,
     )(place, e2low, e2, e2high, msg, low2, high2, u2m, f1w, g1, w1)
     e1low, e1high = shift(up, "wide", 1), shift(down, "wide", -1)
 

time: 209 us -> 132 us (0.63)
  the two profiles are of different devices: /device:TPU:1 before, /device:TPU:16 now
where the time goes in v1:
time: 132 us
  starting transfers between devices  55.5 us (42%)
  waiting for transfers between devices  36.8 us (28%)
  Pallas kernels  15.4 us (12%)
  between operations  13.5 us (10%)
  local copies, waits for them, and re-layouts  10.6 us (8%)
    ppermute x20, starting transfers between devices, shift(): return lax.ppermute(x, axis, [(i, (i + by) % count) for i in range(count)])  47.9 us
    ppermute x20, waiting for transfers between devices, shift(): return lax.ppermute(x, axis, [(i, (i + by) % count) for i in range(count)])  31.8 us
    pallas_call x9, Pallas kernels, run(): pl.pallas_call(kernel, out_shape=[jax.ShapeDtypeStruct(s, F32) for s in o...  15.4 us
    unnamed x38, local copies, waits for them, and re-layouts  10.6 us
    all_to_all x1, starting transfers between devices, body(): lax.all_to_all(send, 'wide', split_axis=0, concat_axis=0, tiled=True)  7.62 us
    all_gather x1, waiting for transfers between devices, body(): coef3 = lax.all_gather(coef3, 'wide', tiled=True).reshape(n3, 2, 4, 8, 128)  3.97 us
  transfers between devices with their start and end apart: 22, of which 11 were waited for; matrix products, arithmetic and copies ran while one was open for 0% of the time, Pallas kernels for 4%

profile of v1, /device:TPU:16, one launch (start us, length us, event | category | flops | bytes accessed | tf_op | source)
XLA Modules:
  0.0 132.0 jit_solution(13888170497585564791)
XLA Ops:
  6.5 0.9 copy-done.11
  10.3 1.1 shard_map.46
  11.5 1.4 %collective-permute-start = (f32[18,8,256]{2,1,0:T(8,128)S(1)}, f32[18,8,256]{2,1,0:T(8,128)S(1)}, u32[]{:S(2)}, u32[]{:S(2)}) collective-permute-start(f32[18,8,256]{2,1,0:T(8,128)S(1)} %get-tuple-element.41), channel_id=1, source_target_pairs={{0,1},{1,2},{2,3},{3,0},{4,5},{5,6},{6,7},{7,4},{8,9},{9,10},{10,1... | collective-permute-start | bytes 442376 | tf_op jit(solution)/shard_map/ppermute | solution.py:634
  13.6 3.3 %collective-permute-start.2 = (f32[2,8,256]{2,1,0:T(8,128)S(1)}, f32[2,8,256]{2,1,0:T(8,128)S(1)}, u32[]{:S(2)}, u32[]{:S(2)}) collective-permute-start(f32[2,8,256]{2,1,0:T(8,128)S(1)} %get-tuple-element.43.mine), channel_id=1, source_target_pairs={{0,2},{1,3},{2,0},{3,1},{4,6},{5,7},{6,4},{7,5},{8,10},{9,11},{10,... | collective-permute-start | bytes 49160 | tf_op jit(solution)/shard_map/ppermute | solution.py:634
  16.9 1.9 %collective-permute-done.2.far = f32[2,8,256]{2,1,0:T(8,128)S(1)} collective-permute-done((f32[2,8,256]{2,1,0:T(8,128)S(1)}, f32[2,8,256]{2,1,0:T(8,128)S(1)}, u32[]{:S(2)}, u32[]{:S(2)}) %collective-permute-start.2) | collective-permute-done | bytes 16416 | tf_op jit(solution)/shard_map/ppermute | solution.py:634
  18.8 1.8 %shard_map.47 = (f32[16,80,256]{2,1,0:T(8,128)S(1)}, f32[6,40,128]{2,1,0:T(8,128)S(1)}, f32[3,64,128]{2,1,0:T(8,128)S(1)}, f32[32,128]{1,0:T(8,128)}, f32[568,256]{1,0:T(8,128)S(1)}, /*index=5*/f32[648,256]{1,0:T(8,128)S(1)}) custom-call(s32[2]{0:T(128)S(1)} %pad_add_fusion.place, f32[16,80,256]{2,1,0:T(8,128)S(1)} %get-tuple-element.40.old, ...), custom_call_target="tpu_custom_call" | custom-call | tf_op jit(solution)/shard_map/pallas_call | solution.py:120
  23.0 6.0 %collective-permute-start.4 = (f32[648,256]{1,0:T(8,128)}, f32[648,256]{1,0:T(8,128)S(1)}, u32[]{:S(2)}, u32[]{:S(2)}) collective-permute-start(f32[648,256]{1,0:T(8,128)} %copy-done.17), channel_id=1, source_target_pairs={{0,252},{4,0},{8,4},{12,8},{16,12},{20,16},{24,20},{28,24},{32,28}... | collective-permute-start | bytes 1990664 | tf_op jit(solution)/shard_map/ppermute | solution.py:634
  29.0 12.7 %collective-permute-done.3.low = f32[568,256]{1,0:T(8,128)S(1)} collective-permute-done((f32[568,256]{1,0:T(8,128)}, f32[568,256]{1,0:T(8,128)S(1)}, u32[]{:S(2)}, u32[]{:S(2)}) %collective-permute-start.3) | collective-permute-done | bytes 581664 | tf_op jit(solution)/shard_map/ppermute | solution.py:634
  42.6 3.1 %shard_map.48 = (f32[6,80,256]{2,1,0:T(8,128)S(1)}, f32[7,80,256]{2,1,0:T(8,128)S(1)}, f32[6,80,256]{2,1,0:T(8,128)S(1)}, f32[6,80,256]{2,1,0:T(8,128)S(1)}, f32...) custom-call(f32[16,80,256]{2,1,0:T(8,128)S(1)} %get-tuple-element.44, ...), custom_call_target="tpu_custom_call" | custom-call | tf_op jit(solution)/shard_map/pallas_call | solution.py:120
  48.1 5.1 %collective-permute-start.6 = (f32[8,40,128]{2,1,0:T(8,128)S(1)}, f32[8,40,128]{2,1,0:T(8,128)S(1)}, u32[]{:S(2)}, u32[]{:S(2)}) collective-permute-start(f32[8,40,128]{2,1,0:T(8,128)S(1)} %get-tuple-element.50), channel_id=1, source_target_pairs={{0,252},{4,0},{8,4},{12,8},{16,12},{20,16},{24,20},{28,24},{32,28}... | collective-permute-start | bytes 491528 | tf_op jit(solution)/shard_map/ppermute | solution.py:634
  53.2 3.1 %collective-permute-done.5.low = f32[8,40,128]{2,1,0:T(8,128)S(1)} collective-permute-done((f32[8,40,128]{2,1,0:T(8,128)S(1)}, f32[8,40,128]{2,1,0:T(8,128)S(1)}, u32[]{:S(2)}, u32[]{:S(2)}) %collective-permute-start.5) | collective-permute-done | bytes 163872 | tf_op jit(solution)/shard_map/ppermute | solution.py:634
  56.6 1.6 %collective-permute-start.7 = (f32[32,128]{1,0:T(8,128)S(1)}, f32[32,128]{1,0:T(8,128)S(1)}, u32[]{:S(2)}, u32[]{:S(2)}) collective-permute-start(f32[32,128]{1,0:T(8,128)S(1)} %get-tuple-element.54), channel_id=1, source_target_pairs={{0,1},{1,2},{2,3},{3,0},{4,5},{5,6},{6,7},{7,4},{8,9},{9,10},{10,1... | collective-permute-start | bytes 49160 | tf_op jit(solution)/shard_map/ppermute | solution.py:634
  58.7 3.0 %collective-permute-start.9 = (f32[16,128]{1,0:T(8,128)S(1)}, f32[16,128]{1,0:T(8,128)S(1)}, u32[]{:S(2)}, u32[]{:S(2)}) collective-permute-start(f32[16,128]{1,0:T(8,128)S(1)} %get-tuple-element.53.f2), channel_id=1, source_target_pairs={{0,2},{1,3},{2,0},{3,1},{4,6},{5,7},{6,4},{7,5},{8,10},{9,11},{10,... | collective-permute-start | bytes 24584 | tf_op jit(solution)/shard_map/ppermute | solution.py:634
  61.8 2.1 %collective-permute-done.9.far = f32[16,128]{1,0:T(8,128)S(1)} collective-permute-done((f32[16,128]{1,0:T(8,128)S(1)}, f32[16,128]{1,0:T(8,128)S(1)}, u32[]{:S(2)}, u32[]{:S(2)}) %collective-permute-start.9) | collective-permute-done | bytes 8224 | tf_op jit(solution)/shard_map/ppermute | solution.py:634
  64.6 5.1 %collective-permute-start.11 = (f32[272,128]{1,0:T(8,128)S(1)}, f32[272,128]{1,0:T(8,128)S(1)}, u32[]{:S(2)}, u32[]{:S(2)}) collective-permute-start(f32[272,128]{1,0:T(8,128)S(1)} %get-tuple-element.59.msg), channel_id=1, source_target_pairs={{0,252},{4,0},{8,4},{12,8},{16,12},{20,16},{24,20},{28,24},{32,28}... | collective-permute-start | bytes 417800 | tf_op jit(solution)/shard_map/ppermute | solution.py:634
  69.7 5.3 %collective-permute-start.13 = (f32[64,128]{1,0:T(8,128)S(1)}, f32[64,128]{1,0:T(8,128)S(1)}, u32[]{:S(2)}, u32[]{:S(2)}) collective-permute-start(f32[64,128]{1,0:T(8,128)S(1)} %get-tuple-element.60), channel_id=1, source_target_pairs={{0,248},{4,252},{8,0},{12,4},{16,8},{20,12},{24,16},{28,20},{32,24... | collective-permute-start | bytes 98312 | tf_op jit(solution)/shard_map/ppermute | solution.py:634
  75.0 1.9 %collective-permute-done.12.low2 = f32[64,128]{1,0:T(8,128)S(1)} collective-permute-done((f32[64,128]{1,0:T(8,128)S(1)}, f32[64,128]{1,0:T(8,128)S(1)}, u32[]{:S(2)}, u32[]{:S(2)}) %collective-permute-start.12) | collective-permute-done | bytes 32800 | tf_op jit(solution)/shard_map/ppermute | solution.py:634
  76.9 1.1 shard_map.51
  78.0 7.6 %all-to-all-start = ((f32[64,8,128]{2,1,0:T(8,128)}), f32[64,8,128]{2,1,0:T(8,128)S(1)}, u32[]{:S(2)}, u32[]{:S(2)}) async-start(f32[64,8,128]{2,1,0:T(8,128)} %get-tuple-element.61), calls=%async_computation | async-start | bytes 524288 | tf_op jit(solution)/shard_map/all_to_all | solution.py:685
  85.6 1.6 %collective-permute-start.14 = (f32[64,128]{1,0:T(8,128)S(1)}, f32[64,128]{1,0:T(8,128)S(1)}, u32[]{:S(2)}, u32[]{:S(2)}) collective-permute-start(f32[64,128]{1,0:T(8,128)S(1)} %get-tuple-element.64), channel_id=1, source_target_pairs={{0,8},{4,12},{8,16},{12,20},{16,24},{20,28},{24,32},{28,36},{32,40... | collective-permute-start | bytes 98312 | tf_op jit(solution)/shard_map/ppermute | solution.py:634
  87.3 3.8 %collective-permute-start.15 = (f32[64,128]{1,0:T(8,128)S(1)}, f32[64,128]{1,0:T(8,128)S(1)}, u32[]{:S(2)}, u32[]{:S(2)}) collective-permute-start(f32[64,128]{1,0:T(8,128)S(1)} %get-tuple-element.64), channel_id=1, source_target_pairs={{0,248},{4,252},{8,0},{12,4},{16,8},{20,12},{24,16},{28,20},{32,24... | collective-permute-start | bytes 98312 | tf_op jit(solution)/shard_map/ppermute | solution.py:634
  91.1 6.9 %collective-permute-done.14.u2low = f32[64,128]{1,0:T(8,128)S(1)} collective-permute-done((f32[64,128]{1,0:T(8,128)S(1)}, f32[64,128]{1,0:T(8,128)S(1)}, u32[]{:S(2)}, u32[]{:S(2)}) %collective-permute-start.14) | collective-permute-done | bytes 32800 | tf_op jit(solution)/shard_map/ppermute | solution.py:634
  98.0 1.1 all-to-all-done
  99.1 4.0 %all-gather.2.cloned.1.call-done = f32[2048,128]{1,0:T(8,128)} async-done(((f32[32,128]{1,0:T(8,128)}), f32[2048,128]{1,0:T(8,128)}) %all-gather.2.cloned.1.call-update) | async-done | bytes 1048592 | tf_op jit(solution)/shard_map/all_gather | solution.py:658
  103.0 1.2 copy-done
  104.3 3.8 %shard_map.52.e2 = f32[64,128]{1,0:T(8,128)S(1)} custom-call(s32[2]{0:T(128)S(1)} %pad_add_fusion.place, f32[32,2,8,128]{3,2,1,0:T(8,128)S(1)} %bitcast.5, f32[32,2,4,8,128]{4,3,2,1,0:T(8,128)S(1)} %bitcast.4, f32[3,64,128]{2,1,0:T(8,128)S(1)} %get-tuple-element.58.own, f32[9,64,128]{2,1,0:T(8,128)S(1)} %get-tuple-element.56.c2w, ...), custom_call_target="tpu_custom_call" | custom-call | tf_op jit(solution)/shard_map/pallas_call | solution.py:120
  108.5 4.8 %collective-permute-start.17 = (f32[64,128]{1,0:T(8,128)S(1)}, f32[64,128]{1,0:T(8,128)S(1)}, u32[]{:S(2)}, u32[]{:S(2)}) collective-permute-start(f32[64,128]{1,0:T(8,128)S(1)} %shard_map.52.e2), channel_id=1, source_target_pairs={{0,252},{4,0},{8,4},{12,8},{16,12},{20,16},{24,20},{28,24},{32,28}... | collective-permute-start | bytes 98312 | tf_op jit(solution)/shard_map/ppermute | solution.py:634
  113.3 1.6 %collective-permute-done.16.e2low = f32[64,128]{1,0:T(8,128)S(1)} collective-permute-done((f32[64,128]{1,0:T(8,128)S(1)}, f32[64,128]{1,0:T(8,128)S(1)}, u32[]{:S(2)}, u32[]{:S(2)}) %collective-permute-start.16) | collective-permute-done | bytes 32800 | tf_op jit(solution)/shard_map/ppermute | solution.py:634
  114.9 1.2 shard_map.53
  116.2 5.1 %collective-permute-start.19 = (f32[40,128]{1,0:T(8,128)S(1)}, f32[40,128]{1,0:T(8,128)S(1)}, u32[]{:S(2)}, u32[]{:S(2)}) collective-permute-start(f32[40,128]{1,0:T(8,128)S(1)} %get-tuple-element.68), channel_id=1, source_target_pairs={{0,252},{4,0},{8,4},{12,8},{16,12},{20,16},{24,20},{28,24},{32,28}... | collective-permute-start | bytes 61448 | tf_op jit(solution)/shard_map/ppermute | solution.py:634
  121.3 1.4 %collective-permute-done.18.e1low = f32[40,128]{1,0:T(8,128)S(1)} collective-permute-done((f32[40,128]{1,0:T(8,128)S(1)}, f32[40,128]{1,0:T(8,128)S(1)}, u32[]{:S(2)}, u32[]{:S(2)}) %collective-permute-start.18) | collective-permute-done | bytes 20512 | tf_op jit(solution)/shard_map/ppermute | solution.py:634
  122.8 2.3 %shard_map.54 = f32[4,64,256]{2,1,0:T(8,128)} custom-call(f32[2,40,128]{2,1,0:T(8,128)S(1)} %get-tuple-element.66.e1, f32[40,128]{1,0:T(8,128)S(1)} %collective-permute-done.18.e1low, f32[40,128]{1,0:T(8,128)S(1)} %collective-permute-done.19.e1high, f32[8,40,128]{2,1,0:T(8,128)S(1)} %collective-permute-done.5.low, ...), custom_call_target="tpu_custom_call" | custom-call | tf_op jit(solution)/shard_map/pallas_call | solution.py:120
  (61 shorter events, 11.4 us)
Async XLA Ops:
  6.5 96.5 %all-gather.2.cloned.1.call-start = ((), (), s32[]{:S(2)}) async-start(), calls=%async_computation.1 | async-start | bytes 1064960 | tf_op jit(solution)/shard_map/all_gather | solution.py:658
  6.5 0.9 copy-start.11
  7.5 0.9 copy-start.12
  11.5 7.4 %collective-permute-start = (f32[18,8,256]{2,1,0:T(8,128)S(1)}, f32[18,8,256]{2,1,0:T(8,128)S(1)}, u32[]{:S(2)}, u32[]{:S(2)}) collective-permute-start(f32[18,8,256]{2,1,0:T(8,128)S(1)} %get-tuple-element.41), channel_id=1, source_target_pairs={{0,1},{1,2},{2,3},{3,0},{4,5},{5,6},{6,7},{7,4},{8,9},{9,10},{10,1... | collective-permute-start | bytes 442376 | tf_op jit(solution)/shard_map/ppermute | solution.py:634
  12.8 6.0 %collective-permute-start.1 = (f32[18,8,256]{2,1,0:T(8,128)S(1)}, f32[18,8,256]{2,1,0:T(8,128)S(1)}, u32[]{:S(2)}, u32[]{:S(2)}) collective-permute-start(f32[18,8,256]{2,1,0:T(8,128)S(1)} %get-tuple-element.42), channel_id=1, source_target_pairs={{0,3},{1,0},{2,1},{3,2},{4,7},{5,4},{6,5},{7,6},{8,11},{9,8},{10,9... | collective-permute-start | bytes 442376 | tf_op jit(solution)/shard_map/ppermute | solution.py:634
  13.6 5.2 %collective-permute-start.2 = (f32[2,8,256]{2,1,0:T(8,128)S(1)}, f32[2,8,256]{2,1,0:T(8,128)S(1)}, u32[]{:S(2)}, u32[]{:S(2)}) collective-permute-start(f32[2,8,256]{2,1,0:T(8,128)S(1)} %get-tuple-element.43.mine), channel_id=1, source_target_pairs={{0,2},{1,3},{2,0},{3,1},{4,6},{5,7},{6,4},{7,5},{8,10},{9,11},{10,... | collective-permute-start | bytes 49160 | tf_op jit(solution)/shard_map/ppermute | solution.py:634
  23.0 18.8 %collective-permute-start.4 = (f32[648,256]{1,0:T(8,128)}, f32[648,256]{1,0:T(8,128)S(1)}, u32[]{:S(2)}, u32[]{:S(2)}) collective-permute-start(f32[648,256]{1,0:T(8,128)} %copy-done.17), channel_id=1, source_target_pairs={{0,252},{4,0},{8,4},{12,8},{16,12},{20,16},{24,20},{28,24},{32,28}... | collective-permute-start | bytes 1990664 | tf_op jit(solution)/shard_map/ppermute | solution.py:634
  29.0 12.8 %collective-permute-start.3 = (f32[568,256]{1,0:T(8,128)}, f32[568,256]{1,0:T(8,128)S(1)}, u32[]{:S(2)}, u32[]{:S(2)}) collective-permute-start(f32[568,256]{1,0:T(8,128)} %copy-done.18), channel_id=1, source_target_pairs={{0,4},{4,8},{8,12},{12,16},{16,20},{20,24},{24,28},{28,32},{32,36}... | collective-permute-start | bytes 1744904 | tf_op jit(solution)/shard_map/ppermute | solution.py:634
  48.1 16.4 %copy-start.3 = (f32[6,80,256]{2,1,0:T(8,128)}, f32[6,80,256]{2,1,0:T(8,128)S(1)}, u32[]{:S(2)}) copy-start(f32[6,80,256]{2,1,0:T(8,128)S(1)} %get-tuple-element.69.f) | copy-start | bytes 1474564
  48.1 28.8 %copy-start.1 = (f32[7,80,256]{2,1,0:T(8,128)}, f32[7,80,256]{2,1,0:T(8,128)S(1)}, u32[]{:S(2)}) copy-start(f32[7,80,256]{2,1,0:T(8,128)S(1)} %get-tuple-element.70.c1) | copy-start | bytes 1720324
  48.1 8.2 %collective-permute-start.5 = (f32[8,40,128]{2,1,0:T(8,128)S(1)}, f32[8,40,128]{2,1,0:T(8,128)S(1)}, u32[]{:S(2)}, u32[]{:S(2)}) collective-permute-start(f32[8,40,128]{2,1,0:T(8,128)S(1)} %get-tuple-element.49.own), channel_id=1, source_target_pairs={{0,4},{4,8},{8,12},{12,16},{16,20},{20,24},{24,28},{28,32},{32,36}... | collective-permute-start | bytes 491528 | tf_op jit(solution)/shard_map/ppermute | solution.py:634
  48.1 8.2 %collective-permute-start.6 = (f32[8,40,128]{2,1,0:T(8,128)S(1)}, f32[8,40,128]{2,1,0:T(8,128)S(1)}, u32[]{:S(2)}, u32[]{:S(2)}) collective-permute-start(f32[8,40,128]{2,1,0:T(8,128)S(1)} %get-tuple-element.50), channel_id=1, source_target_pairs={{0,252},{4,0},{8,4},{12,8},{16,12},{20,16},{24,20},{28,24},{32,28}... | collective-permute-start | bytes 491528 | tf_op jit(solution)/shard_map/ppermute | solution.py:634
  56.6 7.3 %collective-permute-start.7 = (f32[32,128]{1,0:T(8,128)S(1)}, f32[32,128]{1,0:T(8,128)S(1)}, u32[]{:S(2)}, u32[]{:S(2)}) collective-permute-start(f32[32,128]{1,0:T(8,128)S(1)} %get-tuple-element.54), channel_id=1, source_target_pairs={{0,1},{1,2},{2,3},{3,0},{4,5},{5,6},{6,7},{7,4},{8,9},{9,10},{10,1... | collective-permute-start | bytes 49160 | tf_op jit(solution)/shard_map/ppermute | solution.py:634
  58.3 5.6 %collective-permute-start.8 = (f32[32,128]{1,0:T(8,128)S(1)}, f32[32,128]{1,0:T(8,128)S(1)}, u32[]{:S(2)}, u32[]{:S(2)}) collective-permute-start(f32[32,128]{1,0:T(8,128)S(1)} %get-tuple-element.55), channel_id=1, source_target_pairs={{0,3},{1,0},{2,1},{3,2},{4,7},{5,4},{6,5},{7,6},{8,11},{9,8},{10,9... | collective-permute-start | bytes 49160 | tf_op jit(solution)/shard_map/ppermute | solution.py:634
  58.7 5.2 %collective-permute-start.9 = (f32[16,128]{1,0:T(8,128)S(1)}, f32[16,128]{1,0:T(8,128)S(1)}, u32[]{:S(2)}, u32[]{:S(2)}) collective-permute-start(f32[16,128]{1,0:T(8,128)S(1)} %get-tuple-element.53.f2), channel_id=1, source_target_pairs={{0,2},{1,3},{2,0},{3,1},{4,6},{5,7},{6,4},{7,5},{8,10},{9,11},{10,... | collective-permute-start | bytes 24584 | tf_op jit(solution)/shard_map/ppermute | solution.py:634
  64.5 12.4 %collective-permute-start.10 = (f32[272,128]{1,0:T(8,128)S(1)}, f32[272,128]{1,0:T(8,128)S(1)}, u32[]{:S(2)}, u32[]{:S(2)}) collective-permute-start(f32[272,128]{1,0:T(8,128)S(1)} %get-tuple-element.59.msg), channel_id=1, source_target_pairs={{0,4},{4,8},{8,12},{12,16},{16,20},{20,24},{24,28},{28,32},{32,36}... | collective-permute-start | bytes 417800 | tf_op jit(solution)/shard_map/ppermute | solution.py:634
  64.6 12.3 %collective-permute-start.11 = (f32[272,128]{1,0:T(8,128)S(1)}, f32[272,128]{1,0:T(8,128)S(1)}, u32[]{:S(2)}, u32[]{:S(2)}) collective-permute-start(f32[272,128]{1,0:T(8,128)S(1)} %get-tuple-element.59.msg), channel_id=1, source_target_pairs={{0,252},{4,0},{8,4},{12,8},{16,12},{20,16},{24,20},{28,24},{32,28}... | collective-permute-start | bytes 417800 | tf_op jit(solution)/shard_map/ppermute | solution.py:634
  69.7 7.2 %collective-permute-start.12 = (f32[64,128]{1,0:T(8,128)S(1)}, f32[64,128]{1,0:T(8,128)S(1)}, u32[]{:S(2)}, u32[]{:S(2)}) collective-permute-start(f32[64,128]{1,0:T(8,128)S(1)} %get-tuple-element.60), channel_id=1, source_target_pairs={{0,8},{4,12},{8,16},{12,20},{16,24},{20,28},{24,32},{28,36},{32,40... | collective-permute-start | bytes 98312 | tf_op jit(solution)/shard_map/ppermute | solution.py:634
  69.7 7.2 %collective-permute-start.13 = (f32[64,128]{1,0:T(8,128)S(1)}, f32[64,128]{1,0:T(8,128)S(1)}, u32[]{:S(2)}, u32[]{:S(2)}) collective-permute-start(f32[64,128]{1,0:T(8,128)S(1)} %get-tuple-element.60), channel_id=1, source_target_pairs={{0,248},{4,252},{8,0},{12,4},{16,8},{20,12},{24,16},{28,20},{32,24... | collective-permute-start | bytes 98312 | tf_op jit(solution)/shard_map/ppermute | solution.py:634
  78.0 21.1 %all-to-all-start = ((f32[64,8,128]{2,1,0:T(8,128)}), f32[64,8,128]{2,1,0:T(8,128)S(1)}, u32[]{:S(2)}, u32[]{:S(2)}) async-start(f32[64,8,128]{2,1,0:T(8,128)} %get-tuple-element.61), calls=%async_computation | async-start | bytes 524288 | tf_op jit(solution)/shard_map/all_to_all | solution.py:685
  85.6 12.4 %collective-permute-start.14 = (f32[64,128]{1,0:T(8,128)S(1)}, f32[64,128]{1,0:T(8,128)S(1)}, u32[]{:S(2)}, u32[]{:S(2)}) collective-permute-start(f32[64,128]{1,0:T(8,128)S(1)} %get-tuple-element.64), channel_id=1, source_target_pairs={{0,8},{4,12},{8,16},{12,20},{16,24},{20,28},{24,32},{28,36},{32,40... | collective-permute-start | bytes 98312 | tf_op jit(solution)/shard_map/ppermute | solution.py:634
  87.3 10.7 %collective-permute-start.15 = (f32[64,128]{1,0:T(8,128)S(1)}, f32[64,128]{1,0:T(8,128)S(1)}, u32[]{:S(2)}, u32[]{:S(2)}) collective-permute-start(f32[64,128]{1,0:T(8,128)S(1)} %get-tuple-element.64), channel_id=1, source_target_pairs={{0,248},{4,252},{8,0},{12,4},{16,8},{20,12},{24,16},{28,20},{32,24... | collective-permute-start | bytes 98312 | tf_op jit(solution)/shard_map/ppermute | solution.py:634
  103.0 1.2 copy-start
  104.3 18.5 %copy-start.2 = (f32[7,80,256]{2,1,0:T(8,128)S(1)}, f32[7,80,256]{2,1,0:T(8,128)}, u32[]{:S(2)}) copy-start(f32[7,80,256]{2,1,0:T(8,128)} %copy-done.1) | copy-start | bytes 1720324
  104.3 18.5 %copy-start.4 = (f32[6,80,256]{2,1,0:T(8,128)S(1)}, f32[6,80,256]{2,1,0:T(8,128)}, u32[]{:S(2)}) copy-start(f32[6,80,256]{2,1,0:T(8,128)} %copy-done.3) | copy-start | bytes 1474564
  104.3 18.5 %copy-start.6 = (f32[6,80,256]{2,1,0:T(8,128)S(1)}, f32[6,80,256]{2,1,0:T(8,128)}, u32[]{:S(2)}) copy-start(f32[6,80,256]{2,1,0:T(8,128)} %copy-done.5) | copy-start | bytes 1474564
  104.3 18.5 %copy-start.8 = (f32[6,80,256]{2,1,0:T(8,128)S(1)}, f32[6,80,256]{2,1,0:T(8,128)}, u32[]{:S(2)}) copy-start(f32[6,80,256]{2,1,0:T(8,128)} %copy-done.7) | copy-start | bytes 1474564
  104.3 18.5 %copy-start.10 = (f32[6,80,256]{2,1,0:T(8,128)S(1)}, f32[6,80,256]{2,1,0:T(8,128)}, u32[]{:S(2)}) copy-start(f32[6,80,256]{2,1,0:T(8,128)} %copy-done.9) | copy-start | bytes 1474564
  108.1 6.7 %collective-permute-start.16 = (f32[64,128]{1,0:T(8,128)S(1)}, f32[64,128]{1,0:T(8,128)S(1)}, u32[]{:S(2)}, u32[]{:S(2)}) collective-permute-start(f32[64,128]{1,0:T(8,128)S(1)} %shard_map.52.e2), channel_id=1, source_target_pairs={{0,4},{4,8},{8,12},{12,16},{16,20},{20,24},{24,28},{28,32},{32,36}... | collective-permute-start | bytes 98312 | tf_op jit(solution)/shard_map/ppermute | solution.py:634
  108.5 6.4 %collective-permute-start.17 = (f32[64,128]{1,0:T(8,128)S(1)}, f32[64,128]{1,0:T(8,128)S(1)}, u32[]{:S(2)}, u32[]{:S(2)}) collective-permute-start(f32[64,128]{1,0:T(8,128)S(1)} %shard_map.52.e2), channel_id=1, source_target_pairs={{0,252},{4,0},{8,4},{12,8},{16,12},{20,16},{24,20},{28,24},{32,28}... | collective-permute-start | bytes 98312 | tf_op jit(solution)/shard_map/ppermute | solution.py:634
  116.1 6.6 %collective-permute-start.18 = (f32[40,128]{1,0:T(8,128)S(1)}, f32[40,128]{1,0:T(8,128)S(1)}, u32[]{:S(2)}, u32[]{:S(2)}) collective-permute-start(f32[40,128]{1,0:T(8,128)S(1)} %get-tuple-element.67), channel_id=1, source_target_pairs={{0,4},{4,8},{8,12},{12,16},{16,20},{20,24},{24,28},{28,32},{32,36}... | collective-permute-start | bytes 61448 | tf_op jit(solution)/shard_map/ppermute | solution.py:634
  116.2 6.6 %collective-permute-start.19 = (f32[40,128]{1,0:T(8,128)S(1)}, f32[40,128]{1,0:T(8,128)S(1)}, u32[]{:S(2)}, u32[]{:S(2)}) collective-permute-start(f32[40,128]{1,0:T(8,128)S(1)} %get-tuple-element.68), channel_id=1, source_target_pairs={{0,252},{4,0},{8,4},{12,8},{16,12},{20,16},{24,20},{28,24},{32,28}... | collective-permute-start | bytes 61448 | tf_op jit(solution)/shard_map/ppermute | solution.py:634
  (9 other events, 7.5 us)
Sparse Core Ops, SparseCore 0:
  23.1 79.9 all-gather.1

commit v2 on v1

--- a/solution.py
+++ b/solution.py
@@ -112,8 +112,8 @@
     return u + KEEP * (u - v) + GAIN * (g * (f + near) - u)
 
 
-def call(kernel, outs, scratch=(), places=(), limit=8, alias=None):
-    places = dict(places)
+def call(kernel, outs, scratch=(), places=(), out_places=(), limit=8):
+    places, out_places = dict(places), dict(out_places)
 
     def run(*args):
         in_specs = [pl.BlockSpec(memory_space=places.get(i, pltpu.VMEM)) for i in range(len(args))]
@@ -121,9 +121,8 @@
             kernel,
             out_shape=[jax.ShapeDtypeStruct(s, F32) for s in outs],
             in_specs=in_specs,
-            out_specs=[pl.BlockSpec(memory_space=pltpu.VMEM)] * len(outs),
+            out_specs=[pl.BlockSpec(memory_space=out_places.get(i, pltpu.VMEM)) for i in range(len(outs))],
             scratch_shapes=[pltpu.VMEM(s, F32) if isinstance(s, tuple) else s for s in scratch],
-            input_output_aliases=alias or {},
             compiler_params=pltpu.CompilerParams(vmem_limit_bytes=limit * 2**20),
         )(*args)
 
@@ -160,29 +159,16 @@
     far[0, :, 128:256] = two_blocks(k2)
     far[1, :, 0:128] = two_blocks(k3)
     far[1, :, 128:256] = jnp.zeros((8, 128), F32)
-    both, alone = pairs_of_lanes(128, 32), pairs_of_lanes(128, 32, even=True)
-    block = iota((2, 128), 1) // 32
-    for a, (k, lanes) in enumerate(((k1, both), (k2, both), (k3, alone))):
-        scr[0:16, :] = 0.25 * mul(k, lanes)
-        packed = 0.0
-        for q in range(4):
-            part = scr[pl.ds(2 * q, 2, stride=8), :]
-            if a != 1:
-                part = part + scr[pl.ds(2 * q + 1, 2, stride=8), :]
-            packed = jnp.where(block == q, part, packed)
-        far[1, 2 * a : 2 * a + 2, 128:256] = packed
     up[16:18] = far[...]
     down[16:18] = far[...]
 
 
-def pad_kernel(place, old, low, high, mine, far, own, coef1, coef2, coef3, up, down, scr):
+def pad_kernel(place, old, low, high, mine, far, own, coef1, coef2, up, down, scr):
     n = place[1]
     for a in range(16):
         own[a, 0:8] = low[a]
         own[a, 8:72] = old[a, 8:72]
         own[a, 72:80] = high[a]
-    row = iota((8, 128), 0)
-    coef3[...] = jnp.zeros((32, 128), F32)
     for ref, at, by in ((mine, 0, 0), (high, 16, 1), (far, 0, 2), (low, 16, 3)):
         m = lax.rem(n + by, 4)
         for a in range(3):
@@ -190,8 +176,6 @@
             here = pl.multiple_of(16 * m, 16)
             coef2[a, pl.ds(here, 8), :] = spread_block(tile, 0, 64)
             coef2[a, pl.ds(here + 8, 8), :] = spread_block(tile, 1, 64)
-            part = pltpu.roll(ref[at + 1, :, 128:256], lax.rem(2 * m + 8 - 2 * a, 8), 0)
-            coef3[8 * a : 8 * a + 8] = jnp.where(row // 2 == m, part, coef3[8 * a : 8 * a + 8])
     for p, out, slot in ((1, down, 5), (2, up, 4)):
         diag = diagonal(SIG[0], own[4 + p], own[5 + p], own[8 + p], own[12 + p])
         out[80 * slot : 80 * slot + 80] = own[p] / diag / THETA
@@ -259,7 +243,8 @@
     return SIG[0] + c1[q, here, :] + c1[q + 1, here, :] + k2 + h2 + k3 + roll(k3, -1, 1)
 
 
-def fine_pre_kernel(own, coef1, coef2, low, high, f, c1, c2, c3, g, u2, w1, g1, msg_up, msg_down, c2w, f1, u1, res, scr):
+def fine_pre_kernel(own, coef1, coef2, low, high, f_out, c1_out, c2_out, c3_out, g_out, u2_out, w1, g1, msg_up, msg_down, c2w, f1,
+                    f, c1, c2, c3, g, u2, u1, res, scr, sems):
     for a, ref in enumerate((f, c1, c2, c3)):
         ref[0] = low[80 * a : 80 * a + 80]
         ref[1:5] = own[4 * a : 4 * a + 4]
@@ -267,6 +252,15 @@
     c1[6] = high[320:400]
     u1[0] = low[320:400]
     u1[7] = high[400:480]
+    copies = []
+
+    def leave(*pairs):
+        for src, dst in pairs:
+            copy = pltpu.make_async_copy(src, dst, sems.at[len(copies)])
+            copy.start()
+            copies.append(copy)
+
+    leave((f, f_out), (c1, c1_out), (c2, c2_out), (c3, c3_out))
 
     def smooth_first(q, carry):
         def rows(r0, n):
@@ -279,6 +273,7 @@
         return carry
 
     lax.fori_loop(0, 6, smooth_first, 0)
+    leave((g, g_out))
 
     def smooth_second(q, carry):
         def rows(r0, n):
@@ -289,7 +284,10 @@
         chunked(80, rows)
         return carry
 
+    u2[0] = u1[0]
+    u2[7] = u1[7]
     lax.fori_loop(0, 6, smooth_second, 0)
+    leave((u2, u2_out))
 
     def residual(q, carry):
         def rows(r0, n):
@@ -333,6 +331,8 @@
                 part = ref[row : row + 16, 128 * half : 128 * half + 128]
                 c2w[3 * a + k, 16 * half : 16 * half + 16] = spread_block(part, 0, 64)
                 c2w[3 * a + k, 32 + 16 * half : 48 + 16 * half] = spread_block(part, 1, 64)
+    for copy in copies:
+        copy.wait()
 
 
 def middle_pre_kernel(own, low, high, w1, g1, f, u2, f2, up, down, u1, scr):
@@ -360,45 +360,101 @@
         down[16 + 8 * p : 24 + 8 * p] = u2[2 + p, 4:12]
 
 
-def coarse_start_kernel(place, f2, low, high, far, c2w, u2fine, own, msg, far_msg):
+def both_halves(x):
+    return jnp.concatenate([spread_block(x, 0, 64), spread_block(x, 1, 64)], axis=0)
+
+
+def coarse_start_kernel(place, f2, low, high, far, c2w, u2fine, own, msg):
     n = place[1]
     for piece, by in ((f2, 0), (high, 1), (far, 2), (low, 3)):
         at = pl.multiple_of(16 * lax.rem(n + by, 4), 16)
         own[0, pl.ds(at, 16), :] = piece[0:16, :]
-    g = 1.0 / diagonal(SIG[2], c2w[1], c2w[2], c2w[4], c2w[7])
-    own[1] = g
-    start = own[0] * g * (1.0 / THETA)
-    own[2] = start
-    far_msg[...] = start
-    msg[0:64] = own[0]
-    msg[64:128] = g
-    msg[128:192] = c2w[2]
+    own[1] = 1.0 / diagonal(SIG[2], c2w[1], c2w[2], c2w[4], c2w[7])
+    msg[0:32] = two_blocks(own[0])
+    msg[32:64] = two_blocks(own[1])
     for p in range(2):
-        at = 192 + 40 * p
+        at = 64 + 40 * p
         msg[at : at + 40] = u2fine[2 + p]
         msg[at : at + 4] = low[20 + 8 * p : 24 + 8 * p]
         msg[at + 36 : at + 40] = high[16 + 8 * p : 20 + 8 * p]
 
 
-def coarse_pre_kernel(own, c2w, low, high, low2, high2, u2, mine, send, scr):
-    f = (low[0:64], own[0], high[0:64])
-    g = (low[64:128], own[1], high[64:128])
-    u1 = [low2[...], f[0] * g[0] * (1.0 / THETA), own[2], f[2] * g[2] * (1.0 / THETA), high2[...]]
-    h1 = (c2w[1], c2w[2], high[128:192])
-    for k in range(3):
-        u2[k] = smooth_two(u1[k + 1], u1[k], u1[k + 2], f[k], g[k], c2w[k], h1[k], c2w[3 + k], c2w[6 + k])
-    mine[...] = u2[1]
-    k1, k2, k3 = c2w[1], c2w[4], c2w[7]
-    near = gather_sum(u2[0], u2[1], u2[2], k1, h1[1], k2, k3)
-    res = f[1] + near - diagonal(SIG[2], k1, h1[1], k2, k3) * u2[1]
-    scr[...] = 0.5 * mul(res, pairs_of_lanes(128, 32))
+def coarse_tiles_kernel(place, c2w, tiles, scr):
+    par = lax.rem(place[0], 2)
+    for a in range(3):
+        x = c2w[3 * a + 1 - par]
+        if a > 0:
+            x = x + c2w[3 * a + 2 - par]
+        scr[...] = 0.25 * mul(x, pairs_of_lanes(128, 32, even=a == 2))
+        tiles[a] = tile_of(scr, a == 1)
+
+
+def tile_of(scr, even=False):
     block = iota((8, 128), 1) // 32
     packed = 0.0
     for q in range(4):
-        part = scr[pl.ds(2 * q, 8, stride=8), :] + scr[pl.ds(2 * q + 1, 8, stride=8), :]
+        part = scr[pl.ds(2 * q, 8, stride=8), :]
+        if not even:
+            part = part + scr[pl.ds(2 * q + 1, 8, stride=8), :]
         packed = jnp.where(block == q, part, packed)
-    for w in range(send.shape[0]):
-        send[w] = packed
+    return packed
+
+
+def coarse_swap_kernel(own, msg, sib, c2w, out):
+    out[0:64] = msg[0:64]
+    for a in range(3):
+        out[64 + 32 * a : 96 + 32 * a] = two_blocks(c2w[3 * a + 1])
+    out[160:192] = sib[0:32] * sib[32:64] * (1.0 / THETA)
+    out[192:224] = two_blocks(c2w[2])
+    out[224:304] = msg[64:144]
+
+
+def coarse_pre_kernel(place, own, c2w, sib, near, other, w, u2, late, u1):
+    par = lax.rem(place[0], 2)
+    odd = par == 1
+
+    def below(k):
+        here = slice(32 * k, 32 * k + 32)
+        return both_halves(jnp.where(odd, other[here], near[here]))
+
+    def above(k):
+        here = slice(32 * k, 32 * k + 32)
+        return both_halves(jnp.where(odd, near[here], other[here]))
+
+    for a in range(2):
+        mine, theirs = own[a], both_halves(sib[32 * a : 32 * a + 32])
+        w[4 * a] = below(a)
+        w[4 * a + 1] = jnp.where(odd, theirs, mine)
+        w[4 * a + 2] = jnp.where(odd, mine, theirs)
+        w[4 * a + 3] = above(a)
+    for a, base in ((0, 8), (1, 13), (2, 17)):
+        w[base] = below(2 + a)
+        w[base + 1] = c2w[3 * a + 1 - par]
+        w[base + 2] = c2w[3 * a + 2 - par]
+        w[base + 3] = above(2 + a)
+    w[12] = above(6)
+    u1[0] = below(5)
+    u1[5] = above(5)
+    for k in range(4):
+        u1[k + 1] = w[k] * w[4 + k] * (1.0 / THETA)
+    for k in range(4):
+        u2[k] = smooth_two(u1[k + 1], u1[k], u1[k + 2], w[k], w[4 + k], w[8 + k], w[9 + k], w[13 + k], w[17 + k])
+    late[...] = two_blocks(jnp.where(odd, u2[1], u2[2]))
+
+
+def coarse_send_kernel(place, w, u2, tiles, send, scr):
+    odd = lax.rem(place[0], 2) == 1
+    total = 0.0
+    for k in (1, 2):
+        args = (w[8 + k], w[9 + k], w[13 + k], w[17 + k])
+        near = gather_sum(u2[k - 1], u2[k], u2[k + 1], *args)
+        total = total + (w[k] + near - diagonal(SIG[2], *args) * u2[k])
+    scr[...] = 0.5 * mul(total, pairs_of_lanes(128, 32))
+    first = jnp.where(odd, tiles[1], tile_of(scr))
+    second = jnp.where(odd, tiles[2], tiles[0])
+    for k in range(send.shape[0]):
+        send[k, 0] = first
+        send[k, 1] = second
 
 
 def packed_sum(below, x, above, c1, h1, c2, c3, width, blocks):
@@ -455,7 +511,7 @@
 THREE, FOUR = (32, 4), (16, 2)
 
 
-def bottom_kernel(place, parts, coef3, own, c2w, low, high, u2w, u2low, u2high, out,
+def bottom_kernel(place, mine, theirs, win, u2w, late, late_other, out, msg,
                   f3, c1, c2, c3, d3, g3, u1, u2, res, f4, d1, d2, e3, g4, ua, ub, st, scr):
     n3, n4 = f3.shape[0], f4.shape[0]
 
@@ -466,12 +522,15 @@
 
         lax.fori_loop(0, n3 // STEP, step, 0)
 
+    odd = lax.rem(place[0], 2) == 1
+
     def load(j):
         here = pl.ds(j, STEP)
-        f3[here] = parts[here, 0] + parts[here, 1]
-        c1[here] = coef3[here, 0, 0]
-        c2[here] = coef3[here, 0, 1] + coef3[here, 1, 1]
-        c3[here] = coef3[here, 0, 2] + coef3[here, 1, 2]
+        a, b, c, d = mine[here, 0], mine[here, 1], theirs[here, 0], theirs[here, 1]
+        f3[here] = jnp.where(odd, c, a)
+        c1[here] = jnp.where(odd, d, b)
+        c2[here] = jnp.where(odd, a, c)
+        c3[here] = jnp.where(odd, b, d)
 
     loop(load)
     c1[n3] = c1[0]
@@ -535,14 +594,14 @@
         wrap(dst, n4)
         src, dst = dst, src
 
-    j0 = around(place[0] - 2, 2 * n3) // 2
+    j0 = around(place[0] // 2 - 1, n3)
     k, j = iota((128, 128), 0), iota((128, 128), 1)
     unfold = (k == 16 * (j // 64) + j % 32 // 2).astype(F32)
     coarse = jnp.concatenate([src[1 + around(around(j0 - 2, n3) // 2 + m, n4)] for m in range(4)], axis=0)
     scr[0:32] = mul(coarse, unfold)
-    odd = lax.rem(around(j0 - 2, n3), 2)
+    shifted = lax.rem(around(j0 - 2, n3), 2)
     js = [around(j0 - 2 + m, n3) for m in range(7)]
-    v = [u2[1 + js[m]] + scr[pl.ds(pl.multiple_of(8 * ((odd + m) // 2), 8), 8), :] for m in range(7)]
+    v = [u2[1 + js[m]] + scr[pl.ds(pl.multiple_of(8 * ((shifted + m) // 2), 8), 8), :] for m in range(7)]
     v = jnp.stack(v)
 
     def window(ref, first, count, by=0):
@@ -562,29 +621,36 @@
         scr[pl.ds(2 * q, 24, stride=8), :] = fine
         scr[pl.ds(2 * q + 1, 24, stride=8), :] = fine
 
-    odd = lax.rem(around(place[0] - 2, 2 * n3), 2)
-    base = (u2low[...], u2w[0], u2w[1], u2w[2], u2high[...])
-    v = [base[m] + scr[pl.ds(pl.multiple_of(64 * ((odd + m) // 2), 64), 64), :] for m in range(5)]
-    f = (low[0:64], own[0], high[0:64])
-    g = (low[64:128], own[1], high[64:128])
-    h1 = (c2w[1], c2w[2], high[128:192])
-    w = [first_post(v[m + 1], v[m], v[m + 2], f[m], g[m], c2w[m], h1[m], c2w[3 + m], c2w[6 + m]) for m in range(3)]
-    out[...] = second_post(w[1], v[2], w[0], w[2], f[1], g[1], c2w[1], h1[1], c2w[4], c2w[7])
-
-
-def middle_post_kernel(place, e2low, e2, e2high, msg, low, high, u2, f, g1, w1, out, up, down, v, w):
+    lower = both_halves(jnp.where(odd, late_other[...], late[...]))
+    upper = both_halves(jnp.where(odd, late[...], late_other[...]))
+    base = (lower, u2w[0], u2w[1], u2w[2], u2w[3], upper)
+    v = [base[m] + scr[64 * (m // 2) : 64 * (m // 2) + 64, :] for m in range(6)]
+
+    def args2(m):
+        return win[m], win[4 + m], win[8 + m], win[9 + m], win[13 + m], win[17 + m]
+
+    w = [first_post(v[m + 1], v[m], v[m + 2], *args2(m)) for m in range(4)]
+    for p in range(2):
+        out[p] = second_post(w[p + 1], v[p + 2], w[p], w[p + 2], *args2(p + 1))
+    msg[...] = jnp.where(odd, out[1], out[0])
+
+
+def middle_post_kernel(place, e2, far, msg, sib, near, f, g1, w1, out, up, down, v, w):
     n = place[1]
+    odd = lax.rem(place[0], 2) == 1
+    planes = (jnp.where(odd, e2[0], far[...]), jnp.where(odd, e2[1], e2[0]), jnp.where(odd, far[...], e2[1]))
     row, col = iota((40, 64), 0), iota((40, 64), 1)
     pick = (col == lax.rem(16 * n + (row + 4) // 2 + 60, 64)).astype(F32)
     lanes = copies_of_lanes(128, 128)
-    fine = [mul(mul(pick, e[...]), lanes) for e in (e2low, e2, e2high)]
+    fine = [mul(mul(pick, e), lanes) for e in planes]
     for p in range(6):
+        ours, next_chip = 64 + 40 * (p % 2), 224 + 40 * (p % 2)
         if p < 2:
-            base = low[192 + 40 * p : 232 + 40 * p]
+            base = jnp.where(odd, sib[ours : ours + 40], near[next_chip : next_chip + 40])
         elif p < 4:
-            base = msg[192 + 40 * (p - 2) : 232 + 40 * (p - 2)]
+            base = msg[ours : ours + 40]
         else:
-            base = high[192 + 40 * (p - 4) : 232 + 40 * (p - 4)]
+            base = jnp.where(odd, near[next_chip : next_chip + 40], sib[ours : ours + 40])
         v[p] = base + fine[p // 2]
     for p in range(1, 5):
         w[p] = first_post(v[p], v[p - 1], v[p + 1], f[p - 1], g1[p - 1], w1[p], w1[p + 1], w1[6 + p], w1[12 + p])
@@ -634,6 +700,15 @@
     return lax.ppermute(x, axis, [(i, (i + by) % count) for i in range(count)])
 
 
+def sibling(x):
+    return lax.ppermute(x, "wide", [(i, i ^ 1) for i in range(lax.axis_size("wide"))])
+
+
+def across(x):
+    count = lax.axis_size("wide")
+    return lax.ppermute(x, "wide", [(i, (i + 1 if i % 2 else i - 1) % count) for i in range(count)])
+
+
 def body(source, coef_first, coef_second, coef_third):
     wide = lax.axis_size("wide")
     n3, n4 = wide // 2, wide // 4
@@ -644,26 +719,27 @@
         start_kernel,
         [(16,) + big, (18, 8, 256), (18, 8, 256), (2, 8, 256)],
         [(128, 128), pltpu.SemaphoreType.DMA((4,))],
-        {k: pl.ANY for k in range(4)},
+        {k: pltpu.HBM for k in range(4)},
     )(source, coef_first, coef_second, coef_third)
     low, high, far = shift(up, "narrow", 1), shift(down, "narrow", -1), shift(mine, "narrow", 2)
 
-    own, coef1, coef2, coef3, up, down = call(
+    own, coef1, coef2, up, down = call(
         pad_kernel,
-        [(16,) + big, (6, 40, 128), (3, 64, 128), (32, 128), (568, 256), (648, 256)],
+        [(16,) + big, (6, 40, 128), (3, 64, 128), (568, 256), (648, 256)],
         [(160, 128)],
         SCALARS,
     )(place, own, low, high, mine, far)
     low, high = shift(up, "wide", 1), shift(down, "wide", -1)
-    coef3 = lax.all_gather(coef3, "wide", tiled=True).reshape(n3, 2, 4, 8, 128)
-
+
+    windows = [(6,) + big, (7,) + big, (6,) + big, (6,) + big, (6,) + big, (8,) + big]
     f, c1, c2, c3, g, u2, w1, g1, up, down, c2w, f1 = call(
         fine_pre_kernel,
-        [(6,) + big, (7,) + big, (6,) + big, (6,) + big, (6,) + big, (8,) + big]
-        + [(18, 40, 128), (4, 40, 128), (8, 40, 128), (8, 40, 128), (9, 64, 128), (2, 40, 128)],
-        [(8,) + big, (4,) + big, (160, 128)],
+        windows + [(18, 40, 128), (4, 40, 128), (8, 40, 128), (8, 40, 128), (9, 64, 128), (2, 40, 128)],
+        windows + [(8,) + big, (4,) + big, (160, 128), pltpu.SemaphoreType.DMA((6,))],
+        out_places={k: pltpu.HBM for k in range(6)},
     )(own, coef1, coef2, low, high)
     low1, high1 = shift(up, "wide", 1), shift(down, "wide", -1)
+    (tiles,) = call(coarse_tiles_kernel, [(3, 8, 128)], [(64, 128)], SCALARS)(place, c2w)
 
     f1w, u2m, f2, up, down = call(
         middle_pre_kernel,
@@ -672,34 +748,36 @@
     )(up, low1, high1, w1, g1)
     low, high, far = shift(up, "narrow", 1), shift(down, "narrow", -1), shift(f2, "narrow", 2)
 
-    own2, msg, far_msg = call(
-        coarse_start_kernel, [(3, 64, 128), (272, 128), (64, 128)], (), SCALARS
-    )(place, f2, low, high, far, c2w, u2m)
-    low2, high2 = shift(msg, "wide", 1), shift(msg, "wide", -1)
-    low2f, high2f = shift(far_msg, "wide", 2), shift(far_msg, "wide", -2)
-
-    u2w, mine, send = call(
-        coarse_pre_kernel, [(3, 64, 128), (64, 128), (wide, 8, 128)], [(64, 128)]
-    )(own2, c2w, low2, high2, low2f, high2f)
-    u2low, u2high = shift(mine, "wide", 2), shift(mine, "wide", -2)
-    parts = lax.all_to_all(send, "wide", split_axis=0, concat_axis=0, tiled=True).reshape(n3, 2, 8, 128)
+    own2, msg = call(coarse_start_kernel, [(2, 64, 128), (144, 128)], (), SCALARS)(place, f2, low, high, far, c2w, u2m)
+    sib = sibling(msg)
+    (swap,) = call(coarse_swap_kernel, [(304, 128)])(own2, msg, sib, c2w)
+    near = across(swap)
+    other = sibling(near)
+    w2, u2w, late = call(
+        coarse_pre_kernel, [(21, 64, 128), (4, 64, 128), (32, 128)], [(6, 64, 128)], SCALARS
+    )(place, own2, c2w, sib, near, other)
+    late = across(late)
+    (send,) = call(coarse_send_kernel, [(n3, 2, 8, 128)], [(64, 128)], SCALARS)(place, w2, u2w, tiles)
+    cores = [[k for k in range(wide) if k % 2 == c] for c in range(2)]
+    parts = lax.all_to_all(send, "wide", split_axis=0, concat_axis=0, tiled=True, axis_index_groups=cores)
+    theirs, late_other = sibling(parts), sibling(late)
 
     three, four = (n3, 8, 128), (n4, 8, 128)
-    (e2,) = call(
+    e2, msg2 = call(
         bottom_kernel,
-        [(64, 128)],
+        [(2, 64, 128), (64, 128)],
         [three, (n3 + 1, 8, 128), three, three, three, three, (n3 + 2, 8, 128), (n3 + 2, 8, 128), four, four]
         + [(n4 + 1, 8, 128), four, four, four, (n4 + 2, 8, 128), (n4 + 2, 8, 128), four, (192, 128)],
         SCALARS,
-    )(place, parts, coef3, own2, c2w, low2, high2, u2w, u2low, u2high)
-    e2low, e2high = shift(e2, "wide", 1), shift(e2, "wide", -1)
+    )(place, parts, theirs, w2, u2w, late, late_other)
+    far = across(msg2)
 
     e1, up, down = call(
         middle_post_kernel,
         [(2, 40, 128), (40, 128), (40, 128)],
         [(6, 40, 128), (6, 40, 128)],
         SCALARS,
-    )(place, e2low, e2, e2high, msg, low2, high2, u2m, f1w, g1, w1)
+    )(place, e2, far, msg, sib, near, f1w, g1, w1)
     e1low, e1high = shift(up, "wide", 1), shift(down, "wide", -1)
 
     (out,) = call(

time: 132 us -> 112 us (0.85)
  the two profiles are of different devices: /device:TPU:16 before, /device:TPU:0 now
where the time goes in v2:
time: 112 us; the launch traced here: 111 us
  waiting for transfers between devices  51.2 us (46%)
  starting transfers between devices  22.9 us (20%)
  Pallas kernels  17.6 us (16%)
  blocking collectives  15.6 us (14%)
  local copies, waits for them, and re-layouts  3.8 us (3%)
    ppermute x12, waiting for transfers between devices, shift(): return lax.ppermute(x, axis, [(i, (i + by) % count) for i in range(count)])  31.7 us
    ppermute x12, starting transfers between devices, shift(): return lax.ppermute(x, axis, [(i, (i + by) % count) for i in range(count)])  18 us
    pallas_call x12, Pallas kernels, run(): pl.pallas_call(kernel, out_shape=[jax.ShapeDtypeStruct(s, F32) for s in o...  17.6 us
    ppermute x3, waiting for transfers between devices, across(): lax.ppermute(x, 'wide', [(i, (i + 1 if i % 2 else i - 1) % count) for i i...  16.6 us
    all_to_all x1, blocking collectives, body(): lax.all_to_all(send, 'wide', split_axis=0, concat_axis=0, tiled=True, axi...  15.6 us
    ppermute x3, starting transfers between devices, across(): lax.ppermute(x, 'wide', [(i, (i + 1 if i % 2 else i - 1) % count) for i i...  4.74 us
    unnamed x8, local copies, waits for them, and re-layouts  3.8 us
    ppermute x4, waiting for transfers between devices, sibling(): lax.ppermute(x, 'wide', [(i, i ^ 1) for i in range(lax.axis_size('wide'))])  3.02 us
  transfers between devices with their start and end apart: 19, of which 12 were waited for; matrix products, arithmetic and copies ran while one was open for 0% of the time, Pallas kernels for 1%

profile of v2, /device:TPU:0, one launch (start us, length us, event | category | flops | bytes accessed | tf_op | source)
XLA Modules:
  0.0 111.3 jit_solution(17019669465441253884)
XLA Ops:
  0.0 0.9 copy-done
  1.0 0.9 copy-done.1
  1.9 0.9 copy-done.2
  2.9 0.9 copy-done.3
  3.8 0.9 shard_map.46
  4.8 3.2 %collective-permute-start.1 = (f32[18,8,256]{2,1,0:T(8,128)S(1)}, f32[18,8,256]{2,1,0:T(8,128)S(1)}, u32[]{:S(2)}, u32[]{:S(2)}) collective-permute-start(f32[18,8,256]{2,1,0:T(8,128)S(1)} %get-tuple-element.42), channel_id=1, source_target_pairs={{0,3},{1,0},{2,1},{3,2},{4,7},{5,4},{6,5},{7,6},{8,11},{9,8},{10,9... | collective-permute-start | bytes 442376 | tf_op jit(solution)/shard_map/ppermute | solution.py:700
  8.4 4.9 %collective-permute-done.2.far = f32[2,8,256]{2,1,0:T(8,128)S(1)} collective-permute-done((f32[2,8,256]{2,1,0:T(8,128)S(1)}, f32[2,8,256]{2,1,0:T(8,128)S(1)}, u32[]{:S(2)}, u32[]{:S(2)}) %collective-permute-start.2) | collective-permute-done | bytes 16416 | tf_op jit(solution)/shard_map/ppermute | solution.py:700
  13.3 1.2 %shard_map.47 = (f32[16,80,256]{2,1,0:T(8,128)S(1)}, f32[6,40,128]{2,1,0:T(8,128)S(1)}, f32[3,64,128]{2,1,0:T(8,128)S(1)}, f32[568,256]{1,0:T(8,128)S(1)}, f32[648,256]{1,0:T(8,128)S(1)}) custom-call(s32[2]{0:T(128)S(1)} %pad_add_fusion.place, f32[16,80,256]{2,1,0:T(8,128)S(1)} %get-tuple-element.40.old, f32[18,8,256]{2,1,0:T(8,128)S(1)} %collective-permute-done.low, ...), custom_call_target="tpu_custom_call" | custom-call | tf_op jit(solution)/shard_map/pallas_call | solution.py:120
  14.5 4.6 %collective-permute-start.4 = (f32[648,256]{1,0:T(8,128)S(1)}, f32[648,256]{1,0:T(8,128)S(1)}, u32[]{:S(2)}, u32[]{:S(2)}) collective-permute-start(f32[648,256]{1,0:T(8,128)S(1)} %get-tuple-element.48), channel_id=1, source_target_pairs={{0,252},{4,0},{8,4},{12,8},{16,12},{20,16},{24,20},{28,24},{32,28}... | collective-permute-start | bytes 1990664 | tf_op jit(solution)/shard_map/ppermute | solution.py:700
  19.1 12.5 %collective-permute-done.3.low = f32[568,256]{1,0:T(8,128)S(1)} collective-permute-done((f32[568,256]{1,0:T(8,128)S(1)}, f32[568,256]{1,0:T(8,128)S(1)}, u32[]{:S(2)}, u32[]{:S(2)}) %collective-permute-start.3) | collective-permute-done | bytes 581664 | tf_op jit(solution)/shard_map/ppermute | solution.py:700
  31.6 4.6 %shard_map.48 = (f32[6,80,256]{2,1,0:T(8,128)S(1)}, f32[7,80,256]{2,1,0:T(8,128)S(1)}, f32[6,80,256]{2,1,0:T(8,128)S(1)}, f32[6,80,256]{2,1,0:T(8,128)S(1)}, f32...) custom-call(f32[16,80,256]{2,1,0:T(8,128)S(1)} %get-tuple-element.44, ...), custom_call_target="tpu_custom_call" | custom-call | tf_op jit(solution)/shard_map/pallas_call | solution.py:120
  36.2 0.9 collective-permute-start.6
  37.2 2.8 %collective-permute-done.6.high = f32[8,40,128]{2,1,0:T(8,128)S(1)} collective-permute-done((f32[8,40,128]{2,1,0:T(8,128)S(1)}, f32[8,40,128]{2,1,0:T(8,128)S(1)}, u32[]{:S(2)}, u32[]{:S(2)}) %collective-permute-start.6) | collective-permute-done | bytes 163872 | tf_op jit(solution)/shard_map/ppermute | solution.py:700
  40.0 5.2 %collective-permute-done.5.low = f32[8,40,128]{2,1,0:T(8,128)S(1)} collective-permute-done((f32[8,40,128]{2,1,0:T(8,128)S(1)}, f32[8,40,128]{2,1,0:T(8,128)S(1)}, u32[]{:S(2)}, u32[]{:S(2)}) %collective-permute-start.5) | collective-permute-done | bytes 163872 | tf_op jit(solution)/shard_map/ppermute | solution.py:700
  45.6 0.9 collective-permute-start.7
  46.5 2.4 %collective-permute-start.8 = (f32[32,128]{1,0:T(8,128)S(1)}, f32[32,128]{1,0:T(8,128)S(1)}, u32[]{:S(2)}, u32[]{:S(2)}) collective-permute-start(f32[32,128]{1,0:T(8,128)S(1)} %get-tuple-element.55), channel_id=1, source_target_pairs={{0,3},{1,0},{2,1},{3,2},{4,7},{5,4},{6,5},{7,6},{8,11},{9,8},{10,9... | collective-permute-start | bytes 49160 | tf_op jit(solution)/shard_map/ppermute | solution.py:700
  49.4 4.6 %collective-permute-done.9.far = f32[16,128]{1,0:T(8,128)S(1)} collective-permute-done((f32[16,128]{1,0:T(8,128)S(1)}, f32[16,128]{1,0:T(8,128)S(1)}, u32[]{:S(2)}, u32[]{:S(2)}) %collective-permute-start.9) | collective-permute-done | bytes 8224 | tf_op jit(solution)/shard_map/ppermute | solution.py:700
  54.8 1.3 %collective-permute-done.10.sib = f32[144,128]{1,0:T(8,128)S(1)} collective-permute-done((f32[144,128]{1,0:T(8,128)S(1)}, f32[144,128]{1,0:T(8,128)S(1)}, u32[]{:S(2)}, u32[]{:S(2)}) %collective-permute-start.10) | collective-permute-done | bytes 73760 | tf_op jit(solution)/shard_map/ppermute | solution.py:704
  56.2 8.0 %collective-permute-done.11.near = f32[304,128]{1,0:T(8,128)S(1)} collective-permute-done((f32[304,128]{1,0:T(8,128)S(1)}, f32[304,128]{1,0:T(8,128)S(1)}, u32[]{:S(2)}, u32[]{:S(2)}) %collective-permute-start.11) | collective-permute-done | bytes 155680 | tf_op jit(solution)/shard_map/ppermute | solution.py:709
  65.5 0.9 shard_map.52
  66.4 0.8 shard_map.54
  67.2 15.6 %all_to_all.5.mine = f32[32,2,8,128]{3,2,1,0:T(8,128)S(1)} all-to-all(f32[32,2,8,128]{3,2,1,0:T(8,128)S(1)} %shard_map.54), channel_id=1, replica_groups={{0,8,16,24,32,40,48,56,64,72,80,88,96,104,112,120,128,136,144,152,160,1..., dimensions={0} | all-to-all | bytes 524288 | tf_op jit(solution)/shard_map/all_to_all | solution.py:762
  82.8 2.3 %collective-permute-start.14 = (f32[32,128]{1,0:T(8,128)S(1)}, f32[32,128]{1,0:T(8,128)S(1)}, u32[]{:S(2)}, u32[]{:S(2)}) collective-permute-start(f32[32,128]{1,0:T(8,128)S(1)} %get-tuple-element.62), channel_id=1, source_target_pairs={{0,252},{4,8},{8,4},{12,16},{16,12},{20,24},{24,20},{28,32},{32,28... | collective-permute-start | bytes 49160 | tf_op jit(solution)/shard_map/ppermute | solution.py:709
  85.1 4.2 %collective-permute-done.14.late = f32[32,128]{1,0:T(8,128)S(1)} collective-permute-done((f32[32,128]{1,0:T(8,128)S(1)}, f32[32,128]{1,0:T(8,128)S(1)}, u32[]{:S(2)}, u32[]{:S(2)}) %collective-permute-start.14) | collective-permute-done | bytes 16416 | tf_op jit(solution)/shard_map/ppermute | solution.py:709
  89.3 1.2 %collective-permute-done.15.late_other = f32[32,128]{1,0:T(8,128)S(1)} collective-permute-done((f32[32,128]{1,0:T(8,128)S(1)}, f32[32,128]{1,0:T(8,128)S(1)}, u32[]{:S(2)}, u32[]{:S(2)}) %collective-permute-start.15) | collective-permute-done | bytes 16416 | tf_op jit(solution)/shard_map/ppermute | solution.py:704
  90.5 3.9 %shard_map.55 = (f32[2,64,128]{2,1,0:T(8,128)S(1)}, f32[64,128]{1,0:T(8,128)S(1)}) custom-call(s32[2]{0:T(128)S(1)} %pad_add_fusion.place, f32[32,2,8,128]{3,2,1,0:T(8,128)S(1)} %all_to_all.5.mine, f32[32,2,8,128]{3,2,1,0:T(8,128)S(1)} %collective-permute-done.13.theirs, f32[21,64,128]{2,1,0:T(8,128)S(1)} %get-tuple-element.60.w.win, ...), custom_call_target="tpu_custom_call" | custom-call | tf_op jit(solution)/shard_map/pallas_call | solution.py:120
  94.4 2.4 %collective-permute-start.16 = (f32[64,128]{1,0:T(8,128)S(1)}, f32[64,128]{1,0:T(8,128)S(1)}, u32[]{:S(2)}, u32[]{:S(2)}) collective-permute-start(f32[64,128]{1,0:T(8,128)S(1)} %get-tuple-element.64), channel_id=1, source_target_pairs={{0,252},{4,8},{8,4},{12,16},{16,12},{20,24},{24,20},{28,32},{32,28... | collective-permute-start | bytes 98312 | tf_op jit(solution)/shard_map/ppermute | solution.py:709
  96.7 4.4 %collective-permute-done.16.far = f32[64,128]{1,0:T(8,128)S(1)} collective-permute-done((f32[64,128]{1,0:T(8,128)S(1)}, f32[64,128]{1,0:T(8,128)S(1)}, u32[]{:S(2)}, u32[]{:S(2)}) %collective-permute-start.16) | collective-permute-done | bytes 32800 | tf_op jit(solution)/shard_map/ppermute | solution.py:709
  101.1 1.2 %shard_map.56 = (f32[2,40,128]{2,1,0:T(8,128)S(1)}, f32[40,128]{1,0:T(8,128)S(1)}, f32[40,128]{1,0:T(8,128)S(1)}) custom-call(s32[2]{0:T(128)S(1)} %pad_add_fusion.place, f32[2,64,128]{2,1,0:T(8,128)S(1)} %get-tuple-element.63.e2, f32[64,128]{1,0:T(8,128)S(1)} %collective-permute-done.16.far, f32[144,128]{1,0:T(8,128)S(1)} %get-tuple-element.59.msg, ...), custom_call_target="tpu_custom_call" | custom-call | tf_op jit(solution)/shard_map/pallas_call | solution.py:120
  102.4 5.1 %collective-permute-start.18 = (f32[40,128]{1,0:T(8,128)S(1)}, f32[40,128]{1,0:T(8,128)S(1)}, u32[]{:S(2)}, u32[]{:S(2)}) collective-permute-start(f32[40,128]{1,0:T(8,128)S(1)} %get-tuple-element.68), channel_id=1, source_target_pairs={{0,252},{4,0},{8,4},{12,8},{16,12},{20,16},{24,20},{28,24},{32,28}... | collective-permute-start | bytes 61448 | tf_op jit(solution)/shard_map/ppermute | solution.py:700
  107.5 1.5 %collective-permute-done.17.e1low = f32[40,128]{1,0:T(8,128)S(1)} collective-permute-done((f32[40,128]{1,0:T(8,128)S(1)}, f32[40,128]{1,0:T(8,128)S(1)}, u32[]{:S(2)}, u32[]{:S(2)}) %collective-permute-start.17) | collective-permute-done | bytes 20512 | tf_op jit(solution)/shard_map/ppermute | solution.py:700
  108.9 2.4 %shard_map.57 = f32[4,64,256]{2,1,0:T(8,128)} custom-call(f32[2,40,128]{2,1,0:T(8,128)S(1)} %get-tuple-element.66.e1, f32[40,128]{1,0:T(8,128)S(1)} %collective-permute-done.17.e1low, f32[40,128]{1,0:T(8,128)S(1)} %collective-permute-done.18.e1high, f32[8,40,128]{2,1,0:T(8,128)S(1)} %collective-permute-done.5.low, ...), custom_call_target="tpu_custom_call" | custom-call | tf_op jit(solution)/shard_map/pallas_call | solution.py:120
  (28 shorter events, 3.6 us)
Async XLA Ops:
  0.0 0.9 copy-start
  1.0 0.9 copy-start.1
  1.9 0.9 copy-start.2
  2.9 0.9 copy-start.3
  4.7 8.6 %collective-permute-start = (f32[18,8,256]{2,1,0:T(8,128)S(1)}, f32[18,8,256]{2,1,0:T(8,128)S(1)}, u32[]{:S(2)}, u32[]{:S(2)}) collective-permute-start(f32[18,8,256]{2,1,0:T(8,128)S(1)} %get-tuple-element.41), channel_id=1, source_target_pairs={{0,1},{1,2},{2,3},{3,0},{4,5},{5,6},{6,7},{7,4},{8,9},{9,10},{10,1... | collective-permute-start | bytes 442376 | tf_op jit(solution)/shard_map/ppermute | solution.py:700
  4.8 8.5 %collective-permute-start.1 = (f32[18,8,256]{2,1,0:T(8,128)S(1)}, f32[18,8,256]{2,1,0:T(8,128)S(1)}, u32[]{:S(2)}, u32[]{:S(2)}) collective-permute-start(f32[18,8,256]{2,1,0:T(8,128)S(1)} %get-tuple-element.42), channel_id=1, source_target_pairs={{0,3},{1,0},{2,1},{3,2},{4,7},{5,4},{6,5},{7,6},{8,11},{9,8},{10,9... | collective-permute-start | bytes 442376 | tf_op jit(solution)/shard_map/ppermute | solution.py:700
  8.0 5.2 %collective-permute-start.2 = (f32[2,8,256]{2,1,0:T(8,128)S(1)}, f32[2,8,256]{2,1,0:T(8,128)S(1)}, u32[]{:S(2)}, u32[]{:S(2)}) collective-permute-start(f32[2,8,256]{2,1,0:T(8,128)S(1)} %get-tuple-element.43.mine), channel_id=1, source_target_pairs={{0,2},{1,3},{2,0},{3,1},{4,6},{5,7},{6,4},{7,5},{8,10},{9,11},{10,... | collective-permute-start | bytes 49160 | tf_op jit(solution)/shard_map/ppermute | solution.py:700
  14.5 17.1 %collective-permute-start.4 = (f32[648,256]{1,0:T(8,128)S(1)}, f32[648,256]{1,0:T(8,128)S(1)}, u32[]{:S(2)}, u32[]{:S(2)}) collective-permute-start(f32[648,256]{1,0:T(8,128)S(1)} %get-tuple-element.48), channel_id=1, source_target_pairs={{0,252},{4,0},{8,4},{12,8},{16,12},{20,16},{24,20},{28,24},{32,28}... | collective-permute-start | bytes 1990664 | tf_op jit(solution)/shard_map/ppermute | solution.py:700
  19.1 12.5 %collective-permute-start.3 = (f32[568,256]{1,0:T(8,128)S(1)}, f32[568,256]{1,0:T(8,128)S(1)}, u32[]{:S(2)}, u32[]{:S(2)}) collective-permute-start(f32[568,256]{1,0:T(8,128)S(1)} %get-tuple-element.47), channel_id=1, source_target_pairs={{0,4},{4,8},{8,12},{12,16},{16,20},{20,24},{24,28},{28,32},{32,36}... | collective-permute-start | bytes 1744904 | tf_op jit(solution)/shard_map/ppermute | solution.py:700
  36.2 3.8 %collective-permute-start.6 = (f32[8,40,128]{2,1,0:T(8,128)S(1)}, f32[8,40,128]{2,1,0:T(8,128)S(1)}, u32[]{:S(2)}, u32[]{:S(2)}) collective-permute-start(f32[8,40,128]{2,1,0:T(8,128)S(1)} %get-tuple-element.50), channel_id=1, source_target_pairs={{0,252},{4,0},{8,4},{12,8},{16,12},{20,16},{24,20},{28,24},{32,28}... | collective-permute-start | bytes 491528 | tf_op jit(solution)/shard_map/ppermute | solution.py:700
  37.2 8.1 %collective-permute-start.5 = (f32[8,40,128]{2,1,0:T(8,128)S(1)}, f32[8,40,128]{2,1,0:T(8,128)S(1)}, u32[]{:S(2)}, u32[]{:S(2)}) collective-permute-start(f32[8,40,128]{2,1,0:T(8,128)S(1)} %get-tuple-element.49.own), channel_id=1, source_target_pairs={{0,4},{4,8},{8,12},{12,16},{16,20},{20,24},{24,28},{28,32},{32,36}... | collective-permute-start | bytes 491528 | tf_op jit(solution)/shard_map/ppermute | solution.py:700
  45.6 8.5 %collective-permute-start.7 = (f32[32,128]{1,0:T(8,128)S(1)}, f32[32,128]{1,0:T(8,128)S(1)}, u32[]{:S(2)}, u32[]{:S(2)}) collective-permute-start(f32[32,128]{1,0:T(8,128)S(1)} %get-tuple-element.54), channel_id=1, source_target_pairs={{0,1},{1,2},{2,3},{3,0},{4,5},{5,6},{6,7},{7,4},{8,9},{9,10},{10,1... | collective-permute-start | bytes 49160 | tf_op jit(solution)/shard_map/ppermute | solution.py:700
  46.5 7.6 %collective-permute-start.8 = (f32[32,128]{1,0:T(8,128)S(1)}, f32[32,128]{1,0:T(8,128)S(1)}, u32[]{:S(2)}, u32[]{:S(2)}) collective-permute-start(f32[32,128]{1,0:T(8,128)S(1)} %get-tuple-element.55), channel_id=1, source_target_pairs={{0,3},{1,0},{2,1},{3,2},{4,7},{5,4},{6,5},{7,6},{8,11},{9,8},{10,9... | collective-permute-start | bytes 49160 | tf_op jit(solution)/shard_map/ppermute | solution.py:700
  48.9 5.2 %collective-permute-start.9 = (f32[16,128]{1,0:T(8,128)S(1)}, f32[16,128]{1,0:T(8,128)S(1)}, u32[]{:S(2)}, u32[]{:S(2)}) collective-permute-start(f32[16,128]{1,0:T(8,128)S(1)} %get-tuple-element.53.f2), channel_id=1, source_target_pairs={{0,2},{1,3},{2,0},{3,1},{4,6},{5,7},{6,4},{7,5},{8,10},{9,11},{10,... | collective-permute-start | bytes 24584 | tf_op jit(solution)/shard_map/ppermute | solution.py:700
  54.7 1.4 %collective-permute-start.10 = (f32[144,128]{1,0:T(8,128)S(1)}, f32[144,128]{1,0:T(8,128)S(1)}, u32[]{:S(2)}, u32[]{:S(2)}) collective-permute-start(f32[144,128]{1,0:T(8,128)S(1)} %get-tuple-element.59.msg), channel_id=1, source_target_pairs={{0,4},{4,0},{8,12},{12,8},{16,20},{20,16},{24,28},{28,24},{32,36},... | collective-permute-start | bytes 221192 | tf_op jit(solution)/shard_map/ppermute | solution.py:704
  56.1 8.1 %collective-permute-start.11 = (f32[304,128]{1,0:T(8,128)S(1)}, f32[304,128]{1,0:T(8,128)S(1)}, u32[]{:S(2)}, u32[]{:S(2)}) collective-permute-start(f32[304,128]{1,0:T(8,128)S(1)} %shard_map.51), channel_id=1, source_target_pairs={{0,252},{4,8},{8,4},{12,16},{16,12},{20,24},{24,20},{28,32},{32,28... | collective-permute-start | bytes 466952 | tf_op jit(solution)/shard_map/ppermute | solution.py:709
  64.1 1.4 %collective-permute-start.12 = (f32[304,128]{1,0:T(8,128)S(1)}, f32[304,128]{1,0:T(8,128)S(1)}, u32[]{:S(2)}, u32[]{:S(2)}) collective-permute-start(f32[304,128]{1,0:T(8,128)S(1)} %collective-permute-done.11.near), channel_id=1, source_target_pairs={{0,4},{4,0},{8,12},{12,8},{16,20},{20,16},{24,28},{28,24},{32,36},... | collective-permute-start | bytes 466952 | tf_op jit(solution)/shard_map/ppermute | solution.py:704
  82.8 7.7 %collective-permute-start.13 = (f32[32,2,8,128]{3,2,1,0:T(8,128)S(1)}, f32[32,2,8,128]{3,2,1,0:T(8,128)S(1)}, u32[]{:S(2)}, u32[]{:S(2)}) collective-permute-start(f32[32,2,8,128]{3,2,1,0:T(8,128)S(1)} %all_to_all.5.mine), channel_id=1, source_target_pairs={{0,4},{4,0},{8,12},{12,8},{16,20},{20,16},{24,28},{28,24},{32,36},... | collective-permute-start | bytes 786440 | tf_op jit(solution)/shard_map/ppermute | solution.py:704
  82.8 6.5 %collective-permute-start.14 = (f32[32,128]{1,0:T(8,128)S(1)}, f32[32,128]{1,0:T(8,128)S(1)}, u32[]{:S(2)}, u32[]{:S(2)}) collective-permute-start(f32[32,128]{1,0:T(8,128)S(1)} %get-tuple-element.62), channel_id=1, source_target_pairs={{0,252},{4,8},{8,4},{12,16},{16,12},{20,24},{24,20},{28,32},{32,28... | collective-permute-start | bytes 49160 | tf_op jit(solution)/shard_map/ppermute | solution.py:709
  89.3 1.2 %collective-permute-start.15 = (f32[32,128]{1,0:T(8,128)S(1)}, f32[32,128]{1,0:T(8,128)S(1)}, u32[]{:S(2)}, u32[]{:S(2)}) collective-permute-start(f32[32,128]{1,0:T(8,128)S(1)} %collective-permute-done.14.late), channel_id=1, source_target_pairs={{0,4},{4,0},{8,12},{12,8},{16,20},{20,16},{24,28},{28,24},{32,36},... | collective-permute-start | bytes 49160 | tf_op jit(solution)/shard_map/ppermute | solution.py:704
  94.4 6.7 %collective-permute-start.16 = (f32[64,128]{1,0:T(8,128)S(1)}, f32[64,128]{1,0:T(8,128)S(1)}, u32[]{:S(2)}, u32[]{:S(2)}) collective-permute-start(f32[64,128]{1,0:T(8,128)S(1)} %get-tuple-element.64), channel_id=1, source_target_pairs={{0,252},{4,8},{8,4},{12,16},{16,12},{20,24},{24,20},{28,32},{32,28... | collective-permute-start | bytes 98312 | tf_op jit(solution)/shard_map/ppermute | solution.py:709
  102.3 6.6 %collective-permute-start.17 = (f32[40,128]{1,0:T(8,128)S(1)}, f32[40,128]{1,0:T(8,128)S(1)}, u32[]{:S(2)}, u32[]{:S(2)}) collective-permute-start(f32[40,128]{1,0:T(8,128)S(1)} %get-tuple-element.67), channel_id=1, source_target_pairs={{0,4},{4,8},{8,12},{12,16},{16,20},{20,24},{24,28},{28,32},{32,36}... | collective-permute-start | bytes 61448 | tf_op jit(solution)/shard_map/ppermute | solution.py:700
  102.4 6.5 %collective-permute-start.18 = (f32[40,128]{1,0:T(8,128)S(1)}, f32[40,128]{1,0:T(8,128)S(1)}, u32[]{:S(2)}, u32[]{:S(2)}) collective-permute-start(f32[40,128]{1,0:T(8,128)S(1)} %get-tuple-element.68), channel_id=1, source_target_pairs={{0,252},{4,0},{8,4},{12,8},{16,12},{20,16},{24,20},{28,24},{32,28}... | collective-permute-start | bytes 61448 | tf_op jit(solution)/shard_map/ppermute | solution.py:700

commit v3 on v2

--- a/solution.py
+++ b/solution.py
@@ -12,7 +12,6 @@
 RATIO = THETA / DELTA
 SIG = [0.0002 * 4.0**level for level in range(5)]
 F32 = jnp.float32
-HIGHEST = lax.Precision.HIGHEST
 
 
 def factors(degree):
@@ -57,8 +56,25 @@
     return (row == col // 2).astype(F32)
 
 
-def mul(a, b):
-    return jnp.dot(a, b, precision=HIGHEST, preferred_element_type=F32)
+def pieces(x):
+    out = []
+    for _ in range(3):
+        part = x.astype(jnp.bfloat16)
+        out.append(part)
+        x = x - part.astype(F32)
+    return out
+
+
+def mul(x, ones):
+    ones = ones.astype(jnp.bfloat16)
+    high, mid, low = [jnp.dot(part, ones, preferred_element_type=F32) for part in pieces(x)]
+    return high + (mid + low)
+
+
+def mul_left(ones, x):
+    ones = ones.astype(jnp.bfloat16)
+    high, mid, low = [jnp.dot(ones, part, preferred_element_type=F32) for part in pieces(x)]
+    return high + (mid + low)
 
 
 def pair_rows(x, scratch, start=0, count=None, even=False):
@@ -137,45 +153,22 @@
     return jnp.where(iota((half, 128), 1) < 64, x[:half], x[half:])
 
 
-def start_kernel(f, c1, c2, c3, own, up, down, far, scr, sems):
+def start_kernel(f, c1, c2, c3, up, down, sems):
     copies = []
     for a, ref in enumerate((f, c1, c2, c3)):
-        copy = pltpu.make_async_copy(ref, own.at[pl.ds(4 * a, 4), pl.ds(8, 64), :], sems.at[a])
-        copy.start()
-        copies.append(copy)
+        for k, (out, row) in enumerate(((up, 56), (down, 0))):
+            copy = pltpu.make_async_copy(ref.at[:, pl.ds(row, 8), :], out.at[pl.ds(4 * a, 4)], sems.at[2 * a + k])
+            copy.start()
+            copies.append(copy)
     for copy in copies:
         copy.wait()
-    inner = pl.ds(8, 64)
-    for a in range(16):
-        up[a] = own[a, 64:72, :]
-        down[a] = own[a, 8:16, :]
-    k1 = jnp.concatenate([own[4, inner], own[6, inner]], axis=0)
-    k2 = jnp.concatenate([own[8, inner] + own[9, inner], own[10, inner] + own[11, inner]], axis=0)
-    k3 = jnp.concatenate([own[12, inner] + own[13, inner], own[14, inner] + own[15, inner]], axis=0)
-    k1, k2, k3 = coarse_coefs((k1, k2, k3), scr, 256, 128)
-    k1, k2, k3 = k1[:32], k2[:32] + k2[32:], k3[:32] + k3[32:]
-    k1, k2, k3 = coarse_coefs((k1, k2, k3), scr, 128, 64)
-    far[0, :, 0:128] = two_blocks(k1)
-    far[0, :, 128:256] = two_blocks(k2)
-    far[1, :, 0:128] = two_blocks(k3)
-    far[1, :, 128:256] = jnp.zeros((8, 128), F32)
-    up[16:18] = far[...]
-    down[16:18] = far[...]
-
-
-def pad_kernel(place, old, low, high, mine, far, own, coef1, coef2, up, down, scr):
-    n = place[1]
+
+
+def pad_kernel(inner, low, high, own, coef1, up, down, scr):
     for a in range(16):
         own[a, 0:8] = low[a]
-        own[a, 8:72] = old[a, 8:72]
+        own[a, 8:72] = inner[a]
         own[a, 72:80] = high[a]
-    for ref, at, by in ((mine, 0, 0), (high, 16, 1), (far, 0, 2), (low, 16, 3)):
-        m = lax.rem(n + by, 4)
-        for a in range(3):
-            tile = ref[at + a // 2, :, 128 * (a % 2) : 128 * (a % 2) + 128]
-            here = pl.multiple_of(16 * m, 16)
-            coef2[a, pl.ds(here, 8), :] = spread_block(tile, 0, 64)
-            coef2[a, pl.ds(here + 8, 8), :] = spread_block(tile, 1, 64)
     for p, out, slot in ((1, down, 5), (2, up, 4)):
         diag = diagonal(SIG[0], own[4 + p], own[5 + p], own[8 + p], own[12 + p])
         out[80 * slot : 80 * slot + 80] = own[p] / diag / THETA
@@ -194,11 +187,6 @@
         for k in range(6):
             row, lane = at + 40 * (k // 2), 128 * (k % 2)
             out[row : row + 40, lane : lane + 128] = coef1[k]
-        for a in range(3):
-            both = two_blocks(coef2[a])
-            row = at + 120 + 16 * a
-            out[row : row + 16, 0:128] = both[:16]
-            out[row : row + 16, 128:256] = both[16:]
 
 
 def unpack(ref, at, index):
@@ -243,8 +231,7 @@
     return SIG[0] + c1[q, here, :] + c1[q + 1, here, :] + k2 + h2 + k3 + roll(k3, -1, 1)
 
 
-def fine_pre_kernel(own, coef1, coef2, low, high, f_out, c1_out, c2_out, c3_out, g_out, u2_out, w1, g1, msg_up, msg_down, c2w, f1,
-                    f, c1, c2, c3, g, u2, u1, res, scr, sems):
+def fine_pre_kernel(own, coef1, low, high, f, c1, c2, c3, g, u2, w1, g1, msg_up, msg_down, f1, u1, res, scr):
     for a, ref in enumerate((f, c1, c2, c3)):
         ref[0] = low[80 * a : 80 * a + 80]
         ref[1:5] = own[4 * a : 4 * a + 4]
@@ -252,15 +239,6 @@
     c1[6] = high[320:400]
     u1[0] = low[320:400]
     u1[7] = high[400:480]
-    copies = []
-
-    def leave(*pairs):
-        for src, dst in pairs:
-            copy = pltpu.make_async_copy(src, dst, sems.at[len(copies)])
-            copy.start()
-            copies.append(copy)
-
-    leave((f, f_out), (c1, c1_out), (c2, c2_out), (c3, c3_out))
 
     def smooth_first(q, carry):
         def rows(r0, n):
@@ -273,7 +251,6 @@
         return carry
 
     lax.fori_loop(0, 6, smooth_first, 0)
-    leave((g, g_out))
 
     def smooth_second(q, carry):
         def rows(r0, n):
@@ -287,7 +264,6 @@
     u2[0] = u1[0]
     u2[7] = u1[7]
     lax.fori_loop(0, 6, smooth_second, 0)
-    leave((u2, u2_out))
 
     def residual(q, carry):
         def rows(r0, n):
@@ -323,19 +299,20 @@
         out[5] = u2[plane, 0:40, 128:256]
         out[6] = u2[plane, 40:80, 0:128]
         out[7] = u2[plane, 40:80, 128:256]
-    for a in range(3):
-        c2w[3 * a + 1] = coef2[a]
-        for k, ref, at in ((0, low, 520), (2, high, 600)):
-            row = at + 16 * a
-            for half in range(2):
-                part = ref[row : row + 16, 128 * half : 128 * half + 128]
-                c2w[3 * a + k, 16 * half : 16 * half + 16] = spread_block(part, 0, 64)
-                c2w[3 * a + k, 32 + 16 * half : 48 + 16 * half] = spread_block(part, 1, 64)
-    for copy in copies:
-        copy.wait()
-
-
-def middle_pre_kernel(own, low, high, w1, g1, f, u2, f2, up, down, u1, scr):
+
+
+def coarse_coef_kernel(w1, out, scr):
+    k1 = jnp.concatenate([w1[2], w1[4]], axis=0)
+    k2, k3 = w1[8] + w1[9], w1[14] + w1[15]
+    both, alone = pairs_of_lanes(128, 64), pairs_of_lanes(128, 64, even=True)
+    k1 = 0.25 * pair_rows(mul(k1, both), scr)
+    k2 = 0.25 * pair_rows(mul(k2, both), scr, even=True)
+    k3 = 0.25 * pair_rows(mul(k3, alone), scr)
+    for k, x in enumerate((k1[2:18], k1[22:38], k2[2:18], k3[2:18])):
+        out[8 * k : 8 * k + 8] = two_blocks(x)
+
+
+def middle_pre_kernel(own, low, high, w1, g1, coefs, f, u2, f2, up, down, u1, scr):
     f[0] = low[1]
     f[1:3] = own[0:2]
     f[3] = high[0]
@@ -352,40 +329,41 @@
         near = gather_sum(u2[p - 1], u2[p], u2[p + 1], k1, h1, k2, k3)
         total = total + (f[p - 1] + near - diagonal(SIG[1], k1, h1, k2, k3) * u2[p])
     coarse = 0.5 * pair_rows(mul(total, pairs_of_lanes(128, 64)), scr, 4, 16)
-    f2[...] = coarse
-    up[0:16] = coarse
-    down[0:16] = coarse
+    f2[0:8] = two_blocks(coarse)
+    f2[8:40] = coefs[...]
     for p in range(2):
-        up[16 + 8 * p : 24 + 8 * p] = u2[2 + p, 28:36]
-        down[16 + 8 * p : 24 + 8 * p] = u2[2 + p, 4:12]
+        up[40 + 8 * p : 48 + 8 * p] = u2[2 + p, 28:36]
+        down[40 + 8 * p : 48 + 8 * p] = u2[2 + p, 4:12]
+    up[0:40] = f2[...]
+    down[0:40] = f2[...]
 
 
 def both_halves(x):
     return jnp.concatenate([spread_block(x, 0, 64), spread_block(x, 1, 64)], axis=0)
 
 
-def coarse_start_kernel(place, f2, low, high, far, c2w, u2fine, own, msg):
+def coarse_start_kernel(place, f2, low, high, far, u2fine, own, msg):
     n = place[1]
     for piece, by in ((f2, 0), (high, 1), (far, 2), (low, 3)):
         at = pl.multiple_of(16 * lax.rem(n + by, 4), 16)
-        own[0, pl.ds(at, 16), :] = piece[0:16, :]
-    own[1] = 1.0 / diagonal(SIG[2], c2w[1], c2w[2], c2w[4], c2w[7])
-    msg[0:32] = two_blocks(own[0])
-    msg[32:64] = two_blocks(own[1])
+        for k in range(5):
+            own[k, pl.ds(at, 16), :] = both_halves(piece[8 * k : 8 * k + 8])
+    own[5] = 1.0 / diagonal(SIG[2], own[1], own[2], own[3], own[4])
+    for k, plane in enumerate((0, 5, 1, 3, 4)):
+        msg[32 * k : 32 * k + 32] = two_blocks(own[plane])
     for p in range(2):
-        at = 64 + 40 * p
+        at = 160 + 40 * p
         msg[at : at + 40] = u2fine[2 + p]
-        msg[at : at + 4] = low[20 + 8 * p : 24 + 8 * p]
-        msg[at + 36 : at + 40] = high[16 + 8 * p : 20 + 8 * p]
-
-
-def coarse_tiles_kernel(place, c2w, tiles, scr):
-    par = lax.rem(place[0], 2)
+        msg[at : at + 4] = low[44 + 8 * p : 48 + 8 * p]
+        msg[at + 36 : at + 40] = high[40 + 8 * p : 44 + 8 * p]
+
+
+def coarse_tiles_kernel(place, msg, sib, tiles, scr):
+    odd = lax.rem(place[0], 2) == 1
     for a in range(3):
-        x = c2w[3 * a + 1 - par]
-        if a > 0:
-            x = x + c2w[3 * a + 2 - par]
-        scr[...] = 0.25 * mul(x, pairs_of_lanes(128, 32, even=a == 2))
+        here = slice(64 + 32 * a, 96 + 32 * a)
+        x = jnp.where(odd, sib[here], msg[here]) if a == 0 else msg[here] + sib[here]
+        scr[...] = 0.25 * mul(both_halves(x), pairs_of_lanes(128, 32, even=a == 2))
         tiles[a] = tile_of(scr, a == 1)
 
 
@@ -400,18 +378,15 @@
     return packed
 
 
-def coarse_swap_kernel(own, msg, sib, c2w, out):
-    out[0:64] = msg[0:64]
-    for a in range(3):
-        out[64 + 32 * a : 96 + 32 * a] = two_blocks(c2w[3 * a + 1])
+def coarse_swap_kernel(own, msg, sib, out):
+    out[0:160] = msg[0:160]
     out[160:192] = sib[0:32] * sib[32:64] * (1.0 / THETA)
-    out[192:224] = two_blocks(c2w[2])
-    out[224:304] = msg[64:144]
-
-
-def coarse_pre_kernel(place, own, c2w, sib, near, other, w, u2, late, u1):
-    par = lax.rem(place[0], 2)
-    odd = par == 1
+    out[192:224] = two_blocks(own[2])
+    out[224:304] = msg[160:240]
+
+
+def coarse_pre_kernel(place, own, sib, near, other, w, u2, late, u1):
+    odd = lax.rem(place[0], 2) == 1
 
     def below(k):
         here = slice(32 * k, 32 * k + 32)
@@ -421,17 +396,12 @@
         here = slice(32 * k, 32 * k + 32)
         return both_halves(jnp.where(odd, near[here], other[here]))
 
-    for a in range(2):
-        mine, theirs = own[a], both_halves(sib[32 * a : 32 * a + 32])
-        w[4 * a] = below(a)
-        w[4 * a + 1] = jnp.where(odd, theirs, mine)
-        w[4 * a + 2] = jnp.where(odd, mine, theirs)
-        w[4 * a + 3] = above(a)
-    for a, base in ((0, 8), (1, 13), (2, 17)):
-        w[base] = below(2 + a)
-        w[base + 1] = c2w[3 * a + 1 - par]
-        w[base + 2] = c2w[3 * a + 2 - par]
-        w[base + 3] = above(2 + a)
+    for a, (base, plane) in enumerate(((0, 0), (4, 5), (8, 1), (13, 3), (17, 4))):
+        mine, theirs = own[plane], both_halves(sib[32 * a : 32 * a + 32])
+        w[base] = below(a)
+        w[base + 1] = jnp.where(odd, theirs, mine)
+        w[base + 2] = jnp.where(odd, mine, theirs)
+        w[base + 3] = above(a)
     w[12] = above(6)
     u1[0] = below(5)
     u1[5] = above(5)
@@ -511,7 +481,7 @@
 THREE, FOUR = (32, 4), (16, 2)
 
 
-def bottom_kernel(place, mine, theirs, win, u2w, late, late_other, out, msg,
+def bottom_kernel(place, mine, theirs, e2,
                   f3, c1, c2, c3, d3, g3, u1, u2, res, f4, d1, d2, e3, g4, ua, ub, st, scr):
     n3, n4 = f3.shape[0], f4.shape[0]
 
@@ -618,33 +588,35 @@
     x = x.reshape(24, 128)
     for q in range(4):
         fine = mul(x, (k == 32 * q + j % 64 // 2).astype(F32))
-        scr[pl.ds(2 * q, 24, stride=8), :] = fine
-        scr[pl.ds(2 * q + 1, 24, stride=8), :] = fine
-
-    lower = both_halves(jnp.where(odd, late_other[...], late[...]))
-    upper = both_halves(jnp.where(odd, late[...], late_other[...]))
-    base = (lower, u2w[0], u2w[1], u2w[2], u2w[3], upper)
-    v = [base[m] + scr[64 * (m // 2) : 64 * (m // 2) + 64, :] for m in range(6)]
-
-    def args2(m):
-        return win[m], win[4 + m], win[8 + m], win[9 + m], win[13 + m], win[17 + m]
-
-    w = [first_post(v[m + 1], v[m], v[m + 2], *args2(m)) for m in range(4)]
-    for p in range(2):
-        out[p] = second_post(w[p + 1], v[p + 2], w[p], w[p + 2], *args2(p + 1))
-    msg[...] = jnp.where(odd, out[1], out[0])
-
-
-def middle_post_kernel(place, e2, far, msg, sib, near, f, g1, w1, out, up, down, v, w):
+        e2[pl.ds(2 * q, 24, stride=8), :] = fine
+        e2[pl.ds(2 * q + 1, 24, stride=8), :] = fine
+
+
+def coarse_post_kernel(place, e2, win, u2, late, out):
+    par = lax.rem(place[0], 2)
+    odd = par == 1
+    late = both_halves(late[...])
+    v = [jnp.where(odd, u2[0], late), u2[par], u2[1 + par], u2[2 + par], jnp.where(odd, late, u2[3])]
+    v = [v[m] + e2[pl.ds(pl.multiple_of(64 * ((m + par) // 2), 64), 64), :] for m in range(5)]
+
+    def args(m):
+        k = m + par
+        return win[k], win[4 + k], win[8 + k], win[9 + k], win[13 + k], win[17 + k]
+
+    w = [first_post(v[m + 1], v[m], v[m + 2], *args(m)) for m in range(3)]
+    out[...] = second_post(w[1], v[2], w[0], w[2], *args(1))
+
+
+def middle_post_kernel(place, e2, e2sib, far, msg, sib, near, f, g1, w1, out, up, down, v, w):
     n = place[1]
     odd = lax.rem(place[0], 2) == 1
-    planes = (jnp.where(odd, e2[0], far[...]), jnp.where(odd, e2[1], e2[0]), jnp.where(odd, far[...], e2[1]))
+    planes = (jnp.where(odd, e2sib[...], far[...]), e2[...], jnp.where(odd, far[...], e2sib[...]))
     row, col = iota((40, 64), 0), iota((40, 64), 1)
     pick = (col == lax.rem(16 * n + (row + 4) // 2 + 60, 64)).astype(F32)
     lanes = copies_of_lanes(128, 128)
-    fine = [mul(mul(pick, e), lanes) for e in planes]
+    fine = [mul(mul_left(pick, e), lanes) for e in planes]
     for p in range(6):
-        ours, next_chip = 64 + 40 * (p % 2), 224 + 40 * (p % 2)
+        ours, next_chip = 160 + 40 * (p % 2), 224 + 40 * (p % 2)
         if p < 2:
             base = jnp.where(odd, sib[ours : ours + 40], near[next_chip : next_chip + 40])
         elif p < 4:
@@ -661,17 +633,20 @@
 
 
 def fine_post_kernel(e1, e1low, e1high, low, high, f, c1, c2, c3, g, u2, out, v, w, scr):
-    lanes = copies_of_lanes(128, 256)
-    rows = twice_rows(jnp.concatenate([e1low[...], e1[0], e1[1], e1high[...]], axis=0), scr)
-    fine = mul(rows, lanes)
-    for k, ref in ((0, low), (7, high)):
-        part = fine[80 * (k // 2) : 80 * (k // 2) + 80]
-        v[k, 0:40, 0:128] = ref[4] + part[0:40, 0:128]
-        v[k, 0:40, 128:256] = ref[5] + part[0:40, 128:256]
-        v[k, 40:80, 0:128] = ref[6] + part[40:80, 0:128]
-        v[k, 40:80, 128:256] = ref[7] + part[40:80, 128:256]
-    for k in range(1, 7):
-        v[k] = u2[k] + fine[80 * (k // 2) : 80 * (k // 2) + 80]
+    x = jnp.concatenate([e1low[...], e1[0], e1[1], e1high[...]], axis=0)
+    for half in range(2):
+        here = slice(128 * half, 128 * half + 128)
+        row, col = iota((128, 128), 0), iota((128, 128), 1)
+        fine = mul(x, (row == 64 * half + col // 2).astype(F32))
+        scr[pl.ds(0, 160, stride=2), :] = fine
+        scr[pl.ds(1, 160, stride=2), :] = fine
+        for k, ref in ((0, low), (7, high)):
+            at = 80 * (k // 2)
+            v[k, 0:40, here] = ref[4 + half] + scr[at : at + 40, :]
+            v[k, 40:80, here] = ref[6 + half] + scr[at + 40 : at + 80, :]
+        for k in range(1, 7):
+            at = 80 * (k // 2)
+            v[k, :, here] = u2[k, :, here] + scr[at : at + 80, :]
 
     def post1(q, carry):
         def chunk(r0, n):
@@ -714,70 +689,70 @@
     n3, n4 = wide // 2, wide // 4
     place = jnp.stack([lax.axis_index("wide"), lax.axis_index("narrow")]).astype(jnp.int32)
     big = (80, 256)
-
-    own, up, down, mine = call(
+    inputs = (source, coef_first, coef_second, coef_third)
+
+    up, down = call(
         start_kernel,
-        [(16,) + big, (18, 8, 256), (18, 8, 256), (2, 8, 256)],
-        [(128, 128), pltpu.SemaphoreType.DMA((4,))],
+        [(16, 8, 256), (16, 8, 256)],
+        [pltpu.SemaphoreType.DMA((8,))],
         {k: pltpu.HBM for k in range(4)},
-    )(source, coef_first, coef_second, coef_third)
-    low, high, far = shift(up, "narrow", 1), shift(down, "narrow", -1), shift(mine, "narrow", 2)
-
-    own, coef1, coef2, up, down = call(
-        pad_kernel,
-        [(16,) + big, (6, 40, 128), (3, 64, 128), (568, 256), (648, 256)],
-        [(160, 128)],
-        SCALARS,
-    )(place, own, low, high, mine, far)
+        {k: pltpu.HBM for k in range(2)},
+        limit=60,
+    )(*inputs)
+    low, high = shift(up, "narrow", 1), shift(down, "narrow", -1)
+
+    own, coef1, up, down = call(
+        pad_kernel, [(16,) + big, (6, 40, 128), (520, 256), (600, 256)], [(160, 128)]
+    )(jnp.concatenate(inputs, axis=0), low, high)
     low, high = shift(up, "wide", 1), shift(down, "wide", -1)
 
-    windows = [(6,) + big, (7,) + big, (6,) + big, (6,) + big, (6,) + big, (8,) + big]
-    f, c1, c2, c3, g, u2, w1, g1, up, down, c2w, f1 = call(
+    f, c1, c2, c3, g, u2, w1, g1, up, down, f1 = call(
         fine_pre_kernel,
-        windows + [(18, 40, 128), (4, 40, 128), (8, 40, 128), (8, 40, 128), (9, 64, 128), (2, 40, 128)],
-        windows + [(8,) + big, (4,) + big, (160, 128), pltpu.SemaphoreType.DMA((6,))],
-        out_places={k: pltpu.HBM for k in range(6)},
-    )(own, coef1, coef2, low, high)
+        [(6,) + big, (7,) + big, (6,) + big, (6,) + big, (6,) + big, (8,) + big]
+        + [(18, 40, 128), (4, 40, 128), (8, 40, 128), (8, 40, 128), (2, 40, 128)],
+        [(8,) + big, (4,) + big, (160, 128)],
+    )(own, coef1, low, high)
     low1, high1 = shift(up, "wide", 1), shift(down, "wide", -1)
-    (tiles,) = call(coarse_tiles_kernel, [(3, 8, 128)], [(64, 128)], SCALARS)(place, c2w)
+    (coefs,) = call(coarse_coef_kernel, [(32, 128)], [(80, 128)])(w1)
 
     f1w, u2m, f2, up, down = call(
         middle_pre_kernel,
-        [(4, 40, 128), (6, 40, 128), (16, 128), (32, 128), (32, 128)],
+        [(4, 40, 128), (6, 40, 128), (40, 128), (56, 128), (56, 128)],
         [(6, 40, 128), (40, 128)],
-    )(up, low1, high1, w1, g1)
+    )(up, low1, high1, w1, g1, coefs)
     low, high, far = shift(up, "narrow", 1), shift(down, "narrow", -1), shift(f2, "narrow", 2)
 
-    own2, msg = call(coarse_start_kernel, [(2, 64, 128), (144, 128)], (), SCALARS)(place, f2, low, high, far, c2w, u2m)
+    own2, msg = call(coarse_start_kernel, [(6, 64, 128), (240, 128)], (), SCALARS)(place, f2, low, high, far, u2m)
     sib = sibling(msg)
-    (swap,) = call(coarse_swap_kernel, [(304, 128)])(own2, msg, sib, c2w)
+    (swap,) = call(coarse_swap_kernel, [(304, 128)])(own2, msg, sib)
     near = across(swap)
+    (tiles,) = call(coarse_tiles_kernel, [(3, 8, 128)], [(64, 128)], SCALARS)(place, msg, sib)
     other = sibling(near)
     w2, u2w, late = call(
         coarse_pre_kernel, [(21, 64, 128), (4, 64, 128), (32, 128)], [(6, 64, 128)], SCALARS
-    )(place, own2, c2w, sib, near, other)
-    late = across(late)
+    )(place, own2, sib, near, other)
     (send,) = call(coarse_send_kernel, [(n3, 2, 8, 128)], [(64, 128)], SCALARS)(place, w2, u2w, tiles)
     cores = [[k for k in range(wide) if k % 2 == c] for c in range(2)]
     parts = lax.all_to_all(send, "wide", split_axis=0, concat_axis=0, tiled=True, axis_index_groups=cores)
-    theirs, late_other = sibling(parts), sibling(late)
+    theirs, late = sibling(parts), across(late)
 
     three, four = (n3, 8, 128), (n4, 8, 128)
-    e2, msg2 = call(
+    (fine2,) = call(
         bottom_kernel,
-        [(2, 64, 128), (64, 128)],
+        [(192, 128)],
         [three, (n3 + 1, 8, 128), three, three, three, three, (n3 + 2, 8, 128), (n3 + 2, 8, 128), four, four]
-        + [(n4 + 1, 8, 128), four, four, four, (n4 + 2, 8, 128), (n4 + 2, 8, 128), four, (192, 128)],
+        + [(n4 + 1, 8, 128), four, four, four, (n4 + 2, 8, 128), (n4 + 2, 8, 128), four, (32, 128)],
         SCALARS,
-    )(place, parts, theirs, w2, u2w, late, late_other)
-    far = across(msg2)
+    )(place, parts, theirs)
+    (e2,) = call(coarse_post_kernel, [(64, 128)], (), SCALARS)(place, fine2, w2, u2w, late)
+    e2sib, far = sibling(e2), across(e2)
 
     e1, up, down = call(
         middle_post_kernel,
         [(2, 40, 128), (40, 128), (40, 128)],
         [(6, 40, 128), (6, 40, 128)],
         SCALARS,
-    )(place, e2, far, msg, sib, near, f1w, g1, w1)
+    )(place, e2, e2sib, far, msg, sib, near, f1w, g1, w1)
     e1low, e1high = shift(up, "wide", 1), shift(down, "wide", -1)
 
     (out,) = call(

time: 112 us -> 111 us (level)
  the two profiles are of different devices: /device:TPU:0 before, /device:TPU:24 now
where the time goes in v3:
time: 111 us
  waiting for transfers between devices  37.7 us (34%)
  starting transfers between devices  28.4 us (26%)
  Pallas kernels  25 us (23%)
  blocking collectives  17.5 us (16%)
  other arithmetic  1.33 us (1%)
    ppermute x11, waiting for transfers between devices, shift(): return lax.ppermute(x, axis, [(i, (i + by) % count) for i in range(count)])  25.6 us
    pallas_call x14, Pallas kernels, run(): pl.pallas_call(kernel, out_shape=[jax.ShapeDtypeStruct(s, F32) for s in o...  25 us
    ppermute x11, starting transfers between devices, shift(): return lax.ppermute(x, axis, [(i, (i + by) % count) for i in range(count)])  20.5 us
    all_to_all x1, blocking collectives, body(): lax.all_to_all(send, 'wide', split_axis=0, concat_axis=0, tiled=True, axi...  17.5 us
    ppermute x3, waiting for transfers between devices, across(): lax.ppermute(x, 'wide', [(i, (i + 1 if i % 2 else i - 1) % count) for i i...  10.2 us
    ppermute x3, starting transfers between devices, across(): lax.ppermute(x, 'wide', [(i, (i + 1 if i % 2 else i - 1) % count) for i i...  7.76 us
  transfers between devices with their start and end apart: 18, of which 11 were waited for; matrix products, arithmetic and copies ran while one was open for 1% of the time, Pallas kernels for 4%

profile of v3, /device:TPU:24, one launch (start us, length us, event | category | flops | bytes accessed | tf_op | source)
XLA Modules:
  0.0 110.9 jit_solution(6437478310946068389)
XLA Ops:
  0.0 9.1 %shard_map.46 = (f32[16,8,256]{2,1,0:T(8,128)}, f32[16,8,256]{2,1,0:T(8,128)}) custom-call(f32[4,64,256]{2,1,0:T(8,128)} %f.1, f32[4,64,256]{2,1,0:T(8,128)} %c1.1, f32[4,64,256]{2,1,0:T(8,128)} %c2.1, f32[4,64,256]{2,1,0:T(8,128)} %c3.1), custom_call_target="tpu_custom_call" | custom-call | tf_op jit(solution)/shard_map/pallas_call | solution.py:136
  9.1 2.0 %collective-permute-start = (f32[16,8,256]{2,1,0:T(8,128)}, f32[16,8,256]{2,1,0:T(8,128)S(1)}, u32[]{:S(2)}, u32[]{:S(2)}) collective-permute-start(f32[16,8,256]{2,1,0:T(8,128)} %get-tuple-element.34), channel_id=1, source_target_pairs={{0,1},{1,2},{2,3},{3,0},{4,5},{5,6},{6,7},{7,4},{8,9},{9,10},{10,1... | collective-permute-start | bytes 393224 | tf_op jit(solution)/shard_map/ppermute | solution.py:675
  11.2 1.3 %pad_maximum_fusion.inner = f32[16,64,256]{2,1,0:T(8,128)S(1)} fusion(f32[4,64,256]{2,1,0:T(8,128)} %c3.1, f32[4,64,256]{2,1,0:T(8,128)} %c2.1, f32[4,64,256]{2,1,0:T(8,128)} %c1.1, f32[4,64,256]{2,1,0:T(8,128)} %f.1), kind=kLoop, calls=%fused_computation | loop fusion | flops 786432 | bytes 2097152 | tf_op jit(solution)/shard_map/concatenate | solution.py:706
  12.5 2.2 %collective-permute-done.low = f32[16,8,256]{2,1,0:T(8,128)S(1)} collective-permute-done((f32[16,8,256]{2,1,0:T(8,128)}, f32[16,8,256]{2,1,0:T(8,128)S(1)}, u32[]{:S(2)}, u32[]{:S(2)}) %collective-permute-start) | collective-permute-done | bytes 131104 | tf_op jit(solution)/shard_map/ppermute | solution.py:675
  14.6 2.9 %collective-permute-done.1.high = f32[16,8,256]{2,1,0:T(8,128)S(1)} collective-permute-done((f32[16,8,256]{2,1,0:T(8,128)}, f32[16,8,256]{2,1,0:T(8,128)S(1)}, u32[]{:S(2)}, u32[]{:S(2)}) %collective-permute-start.1) | collective-permute-done | bytes 131104 | tf_op jit(solution)/shard_map/ppermute | solution.py:675
  18.0 4.9 %collective-permute-start.3 = (f32[600,256]{1,0:T(8,128)S(1)}, f32[600,256]{1,0:T(8,128)S(1)}, u32[]{:S(2)}, u32[]{:S(2)}) collective-permute-start(f32[600,256]{1,0:T(8,128)S(1)} %get-tuple-element.39), channel_id=1, source_target_pairs={{0,252},{4,0},{8,4},{12,8},{16,12},{20,16},{24,20},{28,24},{32,28}... | collective-permute-start | bytes 1843208 | tf_op jit(solution)/shard_map/ppermute | solution.py:675
  23.0 12.0 %collective-permute-done.2.low = f32[520,256]{1,0:T(8,128)S(1)} collective-permute-done((f32[520,256]{1,0:T(8,128)S(1)}, f32[520,256]{1,0:T(8,128)S(1)}, u32[]{:S(2)}, u32[]{:S(2)}) %collective-permute-start.2) | collective-permute-done | bytes 532512 | tf_op jit(solution)/shard_map/ppermute | solution.py:675
  35.0 3.1 %shard_map.48 = (f32[6,80,256]{2,1,0:T(8,128)S(1)}, f32[7,80,256]{2,1,0:T(8,128)S(1)}, f32[6,80,256]{2,1,0:T(8,128)S(1)}, f32[6,80,256]{2,1,0:T(8,128)S(1)}, f32...) custom-call(f32[16,80,256]{2,1,0:T(8,128)S(1)} %get-tuple-element.36, ...), custom_call_target="tpu_custom_call" | custom-call | tf_op jit(solution)/shard_map/pallas_call | solution.py:136
  38.1 0.8 copy-done
  38.9 5.1 %collective-permute-start.5 = (f32[8,40,128]{2,1,0:T(8,128)}, f32[8,40,128]{2,1,0:T(8,128)S(1)}, u32[]{:S(2)}, u32[]{:S(2)}) collective-permute-start(f32[8,40,128]{2,1,0:T(8,128)} %get-tuple-element.41), channel_id=1, source_target_pairs={{0,252},{4,0},{8,4},{12,8},{16,12},{20,16},{24,20},{28,24},{32,28}... | collective-permute-start | bytes 491528 | tf_op jit(solution)/shard_map/ppermute | solution.py:675
  44.2 3.0 %collective-permute-done.4.low = f32[8,40,128]{2,1,0:T(8,128)S(1)} collective-permute-done((f32[8,40,128]{2,1,0:T(8,128)}, f32[8,40,128]{2,1,0:T(8,128)S(1)}, u32[]{:S(2)}, u32[]{:S(2)}) %collective-permute-start.4) | collective-permute-done | bytes 163872 | tf_op jit(solution)/shard_map/ppermute | solution.py:675
  47.2 1.2 %shard_map.50 = (f32[4,40,128]{2,1,0:T(8,128)S(1)}, f32[6,40,128]{2,1,0:T(8,128)S(1)}, f32[40,128]{1,0:T(8,128)S(1)}, f32[56,128]{1,0:T(8,128)S(1)}, f32[56,128]{1,0:T(8,128)S(1)}) custom-call(f32[8,40,128]{2,1,0:T(8,128)} %get-tuple-element.40.own, f32[8,40,128]{2,1,0:T(8,128)S(1)} %collective-permute-done.4.low, ...), custom_call_target="tpu_custom_call" | custom-call | tf_op jit(solution)/shard_map/pallas_call | solution.py:136
  48.9 1.6 %collective-permute-start.7 = (f32[56,128]{1,0:T(8,128)S(1)}, f32[56,128]{1,0:T(8,128)S(1)}, u32[]{:S(2)}, u32[]{:S(2)}) collective-permute-start(f32[56,128]{1,0:T(8,128)S(1)} %get-tuple-element.46), channel_id=1, source_target_pairs={{0,3},{1,0},{2,1},{3,2},{4,7},{5,4},{6,5},{7,6},{8,11},{9,8},{10,9... | collective-permute-start | bytes 86024 | tf_op jit(solution)/shard_map/ppermute | solution.py:675
  50.5 1.1 %collective-permute-start.8 = (f32[40,128]{1,0:T(8,128)S(1)}, f32[40,128]{1,0:T(8,128)S(1)}, u32[]{:S(2)}, u32[]{:S(2)}) collective-permute-start(f32[40,128]{1,0:T(8,128)S(1)} %get-tuple-element.44.f2), channel_id=1, source_target_pairs={{0,2},{1,3},{2,0},{3,1},{4,6},{5,7},{6,4},{7,5},{8,10},{9,11},{10,... | collective-permute-start | bytes 61448 | tf_op jit(solution)/shard_map/ppermute | solution.py:675
  51.7 4.1 %collective-permute-done.8.far = f32[40,128]{1,0:T(8,128)S(1)} collective-permute-done((f32[40,128]{1,0:T(8,128)S(1)}, f32[40,128]{1,0:T(8,128)S(1)}, u32[]{:S(2)}, u32[]{:S(2)}) %collective-permute-start.8) | collective-permute-done | bytes 20512 | tf_op jit(solution)/shard_map/ppermute | solution.py:675
  55.8 0.7 shard_map.51
  56.7 1.3 %collective-permute-done.9.sib = f32[240,128]{1,0:T(8,128)S(1)} collective-permute-done((f32[240,128]{1,0:T(8,128)S(1)}, f32[240,128]{1,0:T(8,128)S(1)}, u32[]{:S(2)}, u32[]{:S(2)}) %collective-permute-start.9) | collective-permute-done | bytes 122912 | tf_op jit(solution)/shard_map/ppermute | solution.py:679
  58.0 3.4 %collective-permute-start.10 = (f32[304,128]{1,0:T(8,128)S(1)}, f32[304,128]{1,0:T(8,128)S(1)}, u32[]{:S(2)}, u32[]{:S(2)}) collective-permute-start(f32[304,128]{1,0:T(8,128)S(1)} %shard_map.52), channel_id=1, source_target_pairs={{0,252},{4,8},{8,4},{12,16},{16,12},{20,24},{24,20},{28,32},{32,28... | collective-permute-start | bytes 466952 | tf_op jit(solution)/shard_map/ppermute | solution.py:684
  61.5 4.6 %collective-permute-done.10.near = f32[304,128]{1,0:T(8,128)S(1)} collective-permute-done((f32[304,128]{1,0:T(8,128)S(1)}, f32[304,128]{1,0:T(8,128)S(1)}, u32[]{:S(2)}, u32[]{:S(2)}) %collective-permute-start.10) | collective-permute-done | bytes 155680 | tf_op jit(solution)/shard_map/ppermute | solution.py:684
  66.1 0.8 shard_map.54.tiles
  67.5 0.9 shard_map.53
  68.4 0.8 shard_map.55
  69.2 17.5 %all_to_all.5.mine = f32[32,2,8,128]{3,2,1,0:T(8,128)S(1)} all-to-all(f32[32,2,8,128]{3,2,1,0:T(8,128)S(1)} %shard_map.55), channel_id=1, replica_groups={{0,8,16,24,32,40,48,56,64,72,80,88,96,104,112,120,128,136,144,152,160,1..., dimensions={0} | all-to-all | bytes 524288 | tf_op jit(solution)/shard_map/all_to_all | solution.py:736
  86.7 2.1 %collective-permute-start.13 = (f32[32,128]{1,0:T(8,128)S(1)}, f32[32,128]{1,0:T(8,128)S(1)}, u32[]{:S(2)}, u32[]{:S(2)}) collective-permute-start(f32[32,128]{1,0:T(8,128)S(1)} %get-tuple-element.52), channel_id=1, source_target_pairs={{0,252},{4,8},{8,4},{12,16},{16,12},{20,24},{24,20},{28,32},{32,28... | collective-permute-start | bytes 49160 | tf_op jit(solution)/shard_map/ppermute | solution.py:684
  88.9 3.3 %shard_map.56.e2 = f32[192,128]{1,0:T(8,128)S(1)} custom-call(s32[2]{0:T(128)S(1)} %pad_add_fusion.place, f32[32,2,8,128]{3,2,1,0:T(8,128)S(1)} %all_to_all.5.mine, f32[32,2,8,128]{3,2,1,0:T(8,128)S(1)} %collective-permute-done.12.theirs), custom_call_target="tpu_custom_call" | custom-call | tf_op jit(solution)/shard_map/pallas_call | solution.py:136
  92.2 1.0 collective-permute-done.13.late
  94.1 2.2 %collective-permute-start.15 = (f32[64,128]{1,0:T(8,128)S(1)}, f32[64,128]{1,0:T(8,128)S(1)}, u32[]{:S(2)}, u32[]{:S(2)}) collective-permute-start(f32[64,128]{1,0:T(8,128)S(1)} %shard_map.57.e2), channel_id=1, source_target_pairs={{0,252},{4,8},{8,4},{12,16},{16,12},{20,24},{24,20},{28,32},{32,28... | collective-permute-start | bytes 98312 | tf_op jit(solution)/shard_map/ppermute | solution.py:684
  96.3 4.5 %collective-permute-done.15.far = f32[64,128]{1,0:T(8,128)S(1)} collective-permute-done((f32[64,128]{1,0:T(8,128)S(1)}, f32[64,128]{1,0:T(8,128)S(1)}, u32[]{:S(2)}, u32[]{:S(2)}) %collective-permute-start.15) | collective-permute-done | bytes 32800 | tf_op jit(solution)/shard_map/ppermute | solution.py:684
  100.8 1.2 %shard_map.58 = (f32[2,40,128]{2,1,0:T(8,128)S(1)}, f32[40,128]{1,0:T(8,128)S(1)}, f32[40,128]{1,0:T(8,128)S(1)}) custom-call(s32[2]{0:T(128)S(1)} %pad_add_fusion.place, f32[64,128]{1,0:T(8,128)S(1)} %shard_map.57.e2, f32[64,128]{1,0:T(8,128)S(1)} %collective-permute-done.14.e2sib, f32[64,128]{1,0:T(8,128)S(1)} %collective-permute-done.15.far, ...), custom_call_target="tpu_custom_call" | custom-call | tf_op jit(solution)/shard_map/pallas_call | solution.py:136
  102.1 5.1 %collective-permute-start.17 = (f32[40,128]{1,0:T(8,128)S(1)}, f32[40,128]{1,0:T(8,128)S(1)}, u32[]{:S(2)}, u32[]{:S(2)}) collective-permute-start(f32[40,128]{1,0:T(8,128)S(1)} %get-tuple-element.56), channel_id=1, source_target_pairs={{0,252},{4,0},{8,4},{12,8},{16,12},{20,16},{24,20},{28,24},{32,28}... | collective-permute-start | bytes 61448 | tf_op jit(solution)/shard_map/ppermute | solution.py:675
  107.2 1.5 %collective-permute-done.16.e1low = f32[40,128]{1,0:T(8,128)S(1)} collective-permute-done((f32[40,128]{1,0:T(8,128)S(1)}, f32[40,128]{1,0:T(8,128)S(1)}, u32[]{:S(2)}, u32[]{:S(2)}) %collective-permute-start.16) | collective-permute-done | bytes 20512 | tf_op jit(solution)/shard_map/ppermute | solution.py:675
  108.7 2.3 %shard_map.59 = f32[4,64,256]{2,1,0:T(8,128)} custom-call(f32[2,40,128]{2,1,0:T(8,128)S(1)} %get-tuple-element.54.e1, f32[40,128]{1,0:T(8,128)S(1)} %collective-permute-done.16.e1low, f32[40,128]{1,0:T(8,128)S(1)} %collective-permute-done.17.e1high, f32[8,40,128]{2,1,0:T(8,128)S(1)} %collective-permute-done.4.low, ...), custom_call_target="tpu_custom_call" | custom-call | tf_op jit(solution)/shard_map/pallas_call | solution.py:136
  (25 shorter events, 3.0 us)
Async XLA Ops:
  9.1 5.5 %collective-permute-start = (f32[16,8,256]{2,1,0:T(8,128)}, f32[16,8,256]{2,1,0:T(8,128)S(1)}, u32[]{:S(2)}, u32[]{:S(2)}) collective-permute-start(f32[16,8,256]{2,1,0:T(8,128)} %get-tuple-element.34), channel_id=1, source_target_pairs={{0,1},{1,2},{2,3},{3,0},{4,5},{5,6},{6,7},{7,4},{8,9},{9,10},{10,1... | collective-permute-start | bytes 393224 | tf_op jit(solution)/shard_map/ppermute | solution.py:675
  11.2 6.4 %collective-permute-start.1 = (f32[16,8,256]{2,1,0:T(8,128)}, f32[16,8,256]{2,1,0:T(8,128)S(1)}, u32[]{:S(2)}, u32[]{:S(2)}) collective-permute-start(f32[16,8,256]{2,1,0:T(8,128)} %get-tuple-element.35), channel_id=1, source_target_pairs={{0,3},{1,0},{2,1},{3,2},{4,7},{5,4},{6,5},{7,6},{8,11},{9,8},{10,9... | collective-permute-start | bytes 393224 | tf_op jit(solution)/shard_map/ppermute | solution.py:675
  18.0 17.0 %collective-permute-start.3 = (f32[600,256]{1,0:T(8,128)S(1)}, f32[600,256]{1,0:T(8,128)S(1)}, u32[]{:S(2)}, u32[]{:S(2)}) collective-permute-start(f32[600,256]{1,0:T(8,128)S(1)} %get-tuple-element.39), channel_id=1, source_target_pairs={{0,252},{4,0},{8,4},{12,8},{16,12},{20,16},{24,20},{28,24},{32,28}... | collective-permute-start | bytes 1843208 | tf_op jit(solution)/shard_map/ppermute | solution.py:675
  23.0 12.0 %collective-permute-start.2 = (f32[520,256]{1,0:T(8,128)S(1)}, f32[520,256]{1,0:T(8,128)S(1)}, u32[]{:S(2)}, u32[]{:S(2)}) collective-permute-start(f32[520,256]{1,0:T(8,128)S(1)} %get-tuple-element.38), channel_id=1, source_target_pairs={{0,4},{4,8},{8,12},{12,16},{16,20},{20,24},{24,28},{28,32},{32,36}... | collective-permute-start | bytes 1597448 | tf_op jit(solution)/shard_map/ppermute | solution.py:675
  38.1 0.8 copy-start
  38.9 8.3 %collective-permute-start.4 = (f32[8,40,128]{2,1,0:T(8,128)}, f32[8,40,128]{2,1,0:T(8,128)S(1)}, u32[]{:S(2)}, u32[]{:S(2)}) collective-permute-start(f32[8,40,128]{2,1,0:T(8,128)} %get-tuple-element.40.own), channel_id=1, source_target_pairs={{0,4},{4,8},{8,12},{12,16},{16,20},{20,24},{24,28},{28,32},{32,36}... | collective-permute-start | bytes 491528 | tf_op jit(solution)/shard_map/ppermute | solution.py:675
  38.9 8.3 %collective-permute-start.5 = (f32[8,40,128]{2,1,0:T(8,128)}, f32[8,40,128]{2,1,0:T(8,128)S(1)}, u32[]{:S(2)}, u32[]{:S(2)}) collective-permute-start(f32[8,40,128]{2,1,0:T(8,128)} %get-tuple-element.41), channel_id=1, source_target_pairs={{0,252},{4,0},{8,4},{12,8},{16,12},{20,16},{24,20},{28,24},{32,28}... | collective-permute-start | bytes 491528 | tf_op jit(solution)/shard_map/ppermute | solution.py:675
  48.4 7.4 %collective-permute-start.6 = (f32[56,128]{1,0:T(8,128)S(1)}, f32[56,128]{1,0:T(8,128)S(1)}, u32[]{:S(2)}, u32[]{:S(2)}) collective-permute-start(f32[56,128]{1,0:T(8,128)S(1)} %get-tuple-element.45), channel_id=1, source_target_pairs={{0,1},{1,2},{2,3},{3,0},{4,5},{5,6},{6,7},{7,4},{8,9},{9,10},{10,1... | collective-permute-start | bytes 86024 | tf_op jit(solution)/shard_map/ppermute | solution.py:675
  48.9 6.9 %collective-permute-start.7 = (f32[56,128]{1,0:T(8,128)S(1)}, f32[56,128]{1,0:T(8,128)S(1)}, u32[]{:S(2)}, u32[]{:S(2)}) collective-permute-start(f32[56,128]{1,0:T(8,128)S(1)} %get-tuple-element.46), channel_id=1, source_target_pairs={{0,3},{1,0},{2,1},{3,2},{4,7},{5,4},{6,5},{7,6},{8,11},{9,8},{10,9... | collective-permute-start | bytes 86024 | tf_op jit(solution)/shard_map/ppermute | solution.py:675
  50.5 5.3 %collective-permute-start.8 = (f32[40,128]{1,0:T(8,128)S(1)}, f32[40,128]{1,0:T(8,128)S(1)}, u32[]{:S(2)}, u32[]{:S(2)}) collective-permute-start(f32[40,128]{1,0:T(8,128)S(1)} %get-tuple-element.44.f2), channel_id=1, source_target_pairs={{0,2},{1,3},{2,0},{3,1},{4,6},{5,7},{6,4},{7,5},{8,10},{9,11},{10,... | collective-permute-start | bytes 61448 | tf_op jit(solution)/shard_map/ppermute | solution.py:675
  56.6 1.4 %collective-permute-start.9 = (f32[240,128]{1,0:T(8,128)S(1)}, f32[240,128]{1,0:T(8,128)S(1)}, u32[]{:S(2)}, u32[]{:S(2)}) collective-permute-start(f32[240,128]{1,0:T(8,128)S(1)} %get-tuple-element.49.msg), channel_id=1, source_target_pairs={{0,4},{4,0},{8,12},{12,8},{16,20},{20,16},{24,28},{28,24},{32,36},... | collective-permute-start | bytes 368648 | tf_op jit(solution)/shard_map/ppermute | solution.py:679
  58.0 8.1 %collective-permute-start.10 = (f32[304,128]{1,0:T(8,128)S(1)}, f32[304,128]{1,0:T(8,128)S(1)}, u32[]{:S(2)}, u32[]{:S(2)}) collective-permute-start(f32[304,128]{1,0:T(8,128)S(1)} %shard_map.52), channel_id=1, source_target_pairs={{0,252},{4,8},{8,4},{12,16},{16,12},{20,24},{24,20},{28,32},{32,28... | collective-permute-start | bytes 466952 | tf_op jit(solution)/shard_map/ppermute | solution.py:684
  66.1 1.4 %collective-permute-start.11 = (f32[304,128]{1,0:T(8,128)S(1)}, f32[304,128]{1,0:T(8,128)S(1)}, u32[]{:S(2)}, u32[]{:S(2)}) collective-permute-start(f32[304,128]{1,0:T(8,128)S(1)} %collective-permute-done.10.near), channel_id=1, source_target_pairs={{0,4},{4,0},{8,12},{12,8},{16,20},{20,16},{24,28},{28,24},{32,36},... | collective-permute-start | bytes 466952 | tf_op jit(solution)/shard_map/ppermute | solution.py:679
  86.7 2.1 %collective-permute-start.12 = (f32[32,2,8,128]{3,2,1,0:T(8,128)S(1)}, f32[32,2,8,128]{3,2,1,0:T(8,128)S(1)}, u32[]{:S(2)}, u32[]{:S(2)}) collective-permute-start(f32[32,2,8,128]{3,2,1,0:T(8,128)S(1)} %all_to_all.5.mine), channel_id=1, source_target_pairs={{0,4},{4,0},{8,12},{12,8},{16,20},{20,16},{24,28},{28,24},{32,36},... | collective-permute-start | bytes 786440 | tf_op jit(solution)/shard_map/ppermute | solution.py:679
  86.7 21.9 %copy-start.1 = (f32[6,80,256]{2,1,0:T(8,128)S(1)}, f32[6,80,256]{2,1,0:T(8,128)}, u32[]{:S(2)}) copy-start(f32[6,80,256]{2,1,0:T(8,128)} %copy-done) | copy-start | bytes 1474564
  86.7 6.5 %collective-permute-start.13 = (f32[32,128]{1,0:T(8,128)S(1)}, f32[32,128]{1,0:T(8,128)S(1)}, u32[]{:S(2)}, u32[]{:S(2)}) collective-permute-start(f32[32,128]{1,0:T(8,128)S(1)} %get-tuple-element.52), channel_id=1, source_target_pairs={{0,252},{4,8},{8,4},{12,16},{16,12},{20,24},{24,20},{28,32},{32,28... | collective-permute-start | bytes 49160 | tf_op jit(solution)/shard_map/ppermute | solution.py:684
  94.0 2.3 %collective-permute-start.14 = (f32[64,128]{1,0:T(8,128)S(1)}, f32[64,128]{1,0:T(8,128)S(1)}, u32[]{:S(2)}, u32[]{:S(2)}) collective-permute-start(f32[64,128]{1,0:T(8,128)S(1)} %shard_map.57.e2), channel_id=1, source_target_pairs={{0,4},{4,0},{8,12},{12,8},{16,20},{20,16},{24,28},{28,24},{32,36},... | collective-permute-start | bytes 98312 | tf_op jit(solution)/shard_map/ppermute | solution.py:679
  94.1 6.7 %collective-permute-start.15 = (f32[64,128]{1,0:T(8,128)S(1)}, f32[64,128]{1,0:T(8,128)S(1)}, u32[]{:S(2)}, u32[]{:S(2)}) collective-permute-start(f32[64,128]{1,0:T(8,128)S(1)} %shard_map.57.e2), channel_id=1, source_target_pairs={{0,252},{4,8},{8,4},{12,16},{16,12},{20,24},{24,20},{28,32},{32,28... | collective-permute-start | bytes 98312 | tf_op jit(solution)/shard_map/ppermute | solution.py:684
  102.0 6.6 %collective-permute-start.16 = (f32[40,128]{1,0:T(8,128)S(1)}, f32[40,128]{1,0:T(8,128)S(1)}, u32[]{:S(2)}, u32[]{:S(2)}) collective-permute-start(f32[40,128]{1,0:T(8,128)S(1)} %get-tuple-element.55), channel_id=1, source_target_pairs={{0,4},{4,8},{8,12},{12,16},{16,20},{20,24},{24,28},{28,32},{32,36}... | collective-permute-start | bytes 61448 | tf_op jit(solution)/shard_map/ppermute | solution.py:675
  102.1 6.5 %collective-permute-start.17 = (f32[40,128]{1,0:T(8,128)S(1)}, f32[40,128]{1,0:T(8,128)S(1)}, u32[]{:S(2)}, u32[]{:S(2)}) collective-permute-start(f32[40,128]{1,0:T(8,128)S(1)} %get-tuple-element.56), channel_id=1, source_target_pairs={{0,252},{4,0},{8,4},{12,8},{16,12},{20,16},{24,20},{28,24},{32,28}... | collective-permute-start | bytes 61448 | tf_op jit(solution)/shard_map/ppermute | solution.py:675

commit v4 on v3

--- a/solution.py
+++ b/solution.py
@@ -128,7 +128,7 @@
     return u + KEEP * (u - v) + GAIN * (g * (f + near) - u)
 
 
-def call(kernel, outs, scratch=(), places=(), out_places=(), limit=8):
+def call(kernel, outs, scratch=(), places=(), out_places=(), limit=4):
     places, out_places = dict(places), dict(out_places)
 
     def run(*args):
@@ -231,7 +231,7 @@
     return SIG[0] + c1[q, here, :] + c1[q + 1, here, :] + k2 + h2 + k3 + roll(k3, -1, 1)
 
 
-def fine_pre_kernel(own, coef1, low, high, f, c1, c2, c3, g, u2, w1, g1, msg_up, msg_down, f1, u1, res, scr):
+def fine_pre_kernel(own, coef1, low, high, f, c1, c2, c3, g, u2, w1, msg_up, msg_down, f1, u1, res, scr):
     for a, ref in enumerate((f, c1, c2, c3)):
         ref[0] = low[80 * a : 80 * a + 80]
         ref[1:5] = own[4 * a : 4 * a + 4]
@@ -286,14 +286,12 @@
             w1[6 * a + p] = unpack(low, 400, 2 * a + p)
             w1[6 * a + 2 + p] = coef1[2 * a + p]
             w1[6 * a + 4 + p] = unpack(high, 480, 2 * a + p)
-    for k in range(4):
-        p = k + 1
-        g1[k] = 1.0 / diagonal(SIG[1], w1[p], w1[p + 1], w1[6 + p], w1[12 + p])
     for p in range(2):
-        start = f1[p] * g1[1 + p] * (1.0 / THETA)
+        k = p + 2
+        inverse = 1.0 / diagonal(SIG[1], w1[k], w1[k + 1], w1[6 + k], w1[12 + k])
         for out in (msg_up, msg_down):
             out[p] = f1[p]
-            out[2 + p] = start
+            out[2 + p] = inverse
     for out, plane in ((msg_up, 4), (msg_down, 3)):
         out[4] = u2[plane, 0:40, 0:128]
         out[5] = u2[plane, 0:40, 128:256]
@@ -312,22 +310,21 @@
         out[8 * k : 8 * k + 8] = two_blocks(x)
 
 
-def middle_pre_kernel(own, low, high, w1, g1, coefs, f, u2, f2, up, down, u1, scr):
-    f[0] = low[1]
-    f[1:3] = own[0:2]
-    f[3] = high[0]
-    u1[0:2] = low[2:4]
-    u1[2:4] = own[2:4]
-    u1[4:6] = high[2:4]
-    u2[0] = jnp.zeros((40, 128), F32)
-    u2[5] = jnp.zeros((40, 128), F32)
+def middle_pre_kernel(own, low, high, w1, coefs, f, g, u2, f2, up, down, u1, scr):
+    for k, ref in enumerate((low, own, high)):
+        f[2 * k : 2 * k + 2] = ref[0:2]
+        g[2 * k : 2 * k + 2] = ref[2:4]
+    for p in range(6):
+        u1[p] = f[p] * g[p] * (1.0 / THETA)
+    u2[0] = u1[0]
+    u2[5] = u1[5]
     for p in range(1, 5):
-        u2[p] = smooth_two(u1[p], u1[p - 1], u1[p + 1], f[p - 1], g1[p - 1], w1[p], w1[p + 1], w1[6 + p], w1[12 + p])
+        u2[p] = smooth_two(u1[p], u1[p - 1], u1[p + 1], f[p], g[p], w1[p], w1[p + 1], w1[6 + p], w1[12 + p])
     total = 0.0
     for p in (2, 3):
         k1, h1, k2, k3 = w1[p], w1[p + 1], w1[6 + p], w1[12 + p]
         near = gather_sum(u2[p - 1], u2[p], u2[p + 1], k1, h1, k2, k3)
-        total = total + (f[p - 1] + near - diagonal(SIG[1], k1, h1, k2, k3) * u2[p])
+        total = total + (f[p] + near - diagonal(SIG[1], k1, h1, k2, k3) * u2[p])
     coarse = 0.5 * pair_rows(mul(total, pairs_of_lanes(128, 64)), scr, 4, 16)
     f2[0:8] = two_blocks(coarse)
     f2[8:40] = coefs[...]
@@ -378,11 +375,14 @@
     return packed
 
 
-def coarse_swap_kernel(own, msg, sib, out):
+def coarse_swap_kernel(place, own, msg, sib, w1, out):
     out[0:160] = msg[0:160]
     out[160:192] = sib[0:32] * sib[32:64] * (1.0 / THETA)
     out[192:224] = two_blocks(own[2])
     out[224:304] = msg[160:240]
+    par = lax.rem(place[0], 2)
+    out[304:344] = sib[pl.ds(pl.multiple_of(160 + 40 * par, 8), 40), :]
+    out[344:384] = w1[4]
 
 
 def coarse_pre_kernel(place, own, sib, near, other, w, u2, late, u1):
@@ -607,33 +607,42 @@
     out[...] = second_post(w[1], v[2], w[0], w[2], *args(1))
 
 
-def middle_post_kernel(place, e2, e2sib, far, msg, sib, near, f, g1, w1, out, up, down, v, w):
-    n = place[1]
-    odd = lax.rem(place[0], 2) == 1
-    planes = (jnp.where(odd, e2sib[...], far[...]), e2[...], jnp.where(odd, far[...], e2sib[...]))
+def middle_post_kernel(place, e2, e2sib, near0, near1, msg, sib, near, f, g, w1, own, edge, send, fine, c1, v, w):
+    n, par = place[1], lax.rem(place[0], 2)
+    odd = par == 1
     row, col = iota((40, 64), 0), iota((40, 64), 1)
     pick = (col == lax.rem(16 * n + (row + 4) // 2 + 60, 64)).astype(F32)
     lanes = copies_of_lanes(128, 128)
-    fine = [mul(mul_left(pick, e), lanes) for e in planes]
-    for p in range(6):
-        ours, next_chip = 160 + 40 * (p % 2), 224 + 40 * (p % 2)
-        if p < 2:
-            base = jnp.where(odd, sib[ours : ours + 40], near[next_chip : next_chip + 40])
-        elif p < 4:
-            base = msg[ours : ours + 40]
-        else:
-            base = jnp.where(odd, near[next_chip : next_chip + 40], sib[ours : ours + 40])
-        v[p] = base + fine[p // 2]
-    for p in range(1, 5):
-        w[p] = first_post(v[p], v[p - 1], v[p + 1], f[p - 1], g1[p - 1], w1[p], w1[p + 1], w1[6 + p], w1[12 + p])
-    for p in (2, 3):
-        out[p - 2] = second_post(w[p], v[p], w[p - 1], w[p + 1], f[p - 1], g1[p - 1], w1[p], w1[p + 1], w1[6 + p], w1[12 + p])
-    up[...] = out[1]
-    down[...] = out[0]
-
-
-def fine_post_kernel(e1, e1low, e1high, low, high, f, c1, c2, c3, g, u2, out, v, w, scr):
-    x = jnp.concatenate([e1low[...], e1[0], e1[1], e1high[...]], axis=0)
+    e2, e2sib, near0, near1 = e2[...], e2sib[...], near0[...], near1[...]
+    for k, (upper, lower) in enumerate(((e2sib, near1), (e2, near0), (near0, e2), (near1, e2sib))):
+        fine[k] = mul(mul_left(pick, jnp.where(odd, upper, lower)), lanes)
+    c1[0:6] = w1[0:6]
+    c1[6] = near[344:384]
+    ours = [msg[160 + 40 * p : 200 + 40 * p] for p in range(2)]
+    sibs = [sib[160 + 40 * p : 200 + 40 * p] for p in range(2)]
+    next_chip = [near[224 + 40 * p : 264 + 40 * p] for p in range(3)]
+    upper = sibs + ours + next_chip
+    lower = [next_chip[2]] + next_chip[:2] + ours + sibs
+    for i in range(7):
+        v[i] = jnp.where(odd, upper[i], lower[i]) + fine[(i + 1 - par) // 2]
+
+    def args(i):
+        k = i - 1 + par
+        return f[k], g[k], c1[k], c1[k + 1], w1[6 + k], w1[12 + k]
+
+    for i in range(1, 6):
+        w[i] = first_post(v[i], v[i - 1], v[i + 1], *args(i))
+    out = [second_post(w[i], v[i], w[i - 1], w[i + 1], *args(i)) for i in (2, 3, 4)]
+    own[0] = jnp.where(odd, out[0], out[1])
+    own[1] = jnp.where(odd, out[1], out[2])
+    edge[...] = jnp.where(odd, out[2], out[0])
+    send[...] = jnp.where(odd, out[0], out[2])
+
+
+def fine_post_kernel(place, e1, edge, other, low, high, f, c1, c2, c3, g, u2, out, v, w, scr):
+    odd = lax.rem(place[0], 2) == 1
+    below, above = jnp.where(odd, other[...], edge[...]), jnp.where(odd, edge[...], other[...])
+    x = jnp.concatenate([below, e1[0], e1[1], above], axis=0)
     for half in range(2):
         here = slice(128 * half, 128 * half + 128)
         row, col = iota((128, 128), 0), iota((128, 128), 1)
@@ -696,7 +705,6 @@
         [(16, 8, 256), (16, 8, 256)],
         [pltpu.SemaphoreType.DMA((8,))],
         {k: pltpu.HBM for k in range(4)},
-        {k: pltpu.HBM for k in range(2)},
         limit=60,
     )(*inputs)
     low, high = shift(up, "narrow", 1), shift(down, "narrow", -1)
@@ -706,25 +714,24 @@
     )(jnp.concatenate(inputs, axis=0), low, high)
     low, high = shift(up, "wide", 1), shift(down, "wide", -1)
 
-    f, c1, c2, c3, g, u2, w1, g1, up, down, f1 = call(
+    f, c1, c2, c3, g, u2, w1, up, down, f1 = call(
         fine_pre_kernel,
         [(6,) + big, (7,) + big, (6,) + big, (6,) + big, (6,) + big, (8,) + big]
-        + [(18, 40, 128), (4, 40, 128), (8, 40, 128), (8, 40, 128), (2, 40, 128)],
+        + [(18, 40, 128), (8, 40, 128), (8, 40, 128), (2, 40, 128)],
         [(8,) + big, (4,) + big, (160, 128)],
     )(own, coef1, low, high)
     low1, high1 = shift(up, "wide", 1), shift(down, "wide", -1)
     (coefs,) = call(coarse_coef_kernel, [(32, 128)], [(80, 128)])(w1)
 
-    f1w, u2m, f2, up, down = call(
-        middle_pre_kernel,
-        [(4, 40, 128), (6, 40, 128), (40, 128), (56, 128), (56, 128)],
-        [(6, 40, 128), (40, 128)],
-    )(up, low1, high1, w1, g1, coefs)
+    six = (6, 40, 128)
+    f1w, g1w, u2m, f2, up, down = call(
+        middle_pre_kernel, [six, six, six, (40, 128), (56, 128), (56, 128)], [six, (40, 128)]
+    )(up, low1, high1, w1, coefs)
     low, high, far = shift(up, "narrow", 1), shift(down, "narrow", -1), shift(f2, "narrow", 2)
 
     own2, msg = call(coarse_start_kernel, [(6, 64, 128), (240, 128)], (), SCALARS)(place, f2, low, high, far, u2m)
     sib = sibling(msg)
-    (swap,) = call(coarse_swap_kernel, [(304, 128)])(own2, msg, sib)
+    (swap,) = call(coarse_swap_kernel, [(384, 128)], (), SCALARS)(place, own2, msg, sib, w1)
     near = across(swap)
     (tiles,) = call(coarse_tiles_kernel, [(3, 8, 128)], [(64, 128)], SCALARS)(place, msg, sib)
     other = sibling(near)
@@ -745,19 +752,20 @@
         SCALARS,
     )(place, parts, theirs)
     (e2,) = call(coarse_post_kernel, [(64, 128)], (), SCALARS)(place, fine2, w2, u2w, late)
-    e2sib, far = sibling(e2), across(e2)
-
-    e1, up, down = call(
+    near0, e2sib = across(e2), sibling(e2)
+    near1 = across(e2sib)
+
+    e1, edge, send = call(
         middle_post_kernel,
         [(2, 40, 128), (40, 128), (40, 128)],
-        [(6, 40, 128), (6, 40, 128)],
+        [(4, 40, 128), (7, 40, 128), (7, 40, 128), (7, 40, 128)],
         SCALARS,
-    )(place, e2, e2sib, far, msg, sib, near, f1w, g1, w1)
-    e1low, e1high = shift(up, "wide", 1), shift(down, "wide", -1)
+    )(place, e2, e2sib, near0, near1, msg, sib, near, f1w, g1w, w1)
+    other1 = sibling(send)
 
     (out,) = call(
-        fine_post_kernel, [(4, 64, 256)], [(8,) + big, (8,) + big, (320, 128)]
-    )(e1, e1low, e1high, low1, high1, f, c1, c2, c3, g, u2)
+        fine_post_kernel, [(4, 64, 256)], [(8,) + big, (8,) + big, (320, 128)], SCALARS
+    )(place, e1, edge, other1, low1, high1, f, c1, c2, c3, g, u2)
     return out
 
 

time: 111 us -> 105 us (0.946)
  the two profiles are of different devices: /device:TPU:24 before, /device:TPU:1 now
where the time goes in v4:
time: 105 us; the launch traced here: 104 us
  starting transfers between devices  45.3 us (43%)
  waiting for transfers between devices  23.3 us (22%)
  Pallas kernels  18.6 us (18%)
  blocking collectives  14.9 us (14%)
  other arithmetic  1.33 us (1%)
    ppermute x5, starting transfers between devices, sibling(): lax.ppermute(x, 'wide', [(i, i ^ 1) for i in range(lax.axis_size('wide'))])  22 us
    ppermute x9, starting transfers between devices, shift(): return lax.ppermute(x, axis, [(i, (i + by) % count) for i in range(count)])  20.7 us
    pallas_call x14, Pallas kernels, run(): pl.pallas_call(kernel, out_shape=[jax.ShapeDtypeStruct(s, F32) for s in o...  18.6 us
    all_to_all x1, blocking collectives, body(): lax.all_to_all(send, 'wide', split_axis=0, concat_axis=0, tiled=True, axi...  14.9 us
    ppermute x9, waiting for transfers between devices, shift(): return lax.ppermute(x, axis, [(i, (i + by) % count) for i in range(count)])  12.9 us
    ppermute x4, waiting for transfers between devices, across(): lax.ppermute(x, 'wide', [(i, (i + 1 if i % 2 else i - 1) % count) for i i...  7.53 us
    ppermute x5, waiting for transfers between devices, sibling(): lax.ppermute(x, 'wide', [(i, i ^ 1) for i in range(lax.axis_size('wide'))])  2.88 us
    ppermute x4, starting transfers between devices, across(): lax.ppermute(x, 'wide', [(i, (i + 1 if i % 2 else i - 1) % count) for i i...  2.56 us
  transfers between devices with their start and end apart: 18, of which 13 were waited for; matrix products, arithmetic and copies ran while one was open for 1% of the time, Pallas kernels for 4%

profile of v4, /device:TPU:1, one launch (start us, length us, event | category | flops | bytes accessed | tf_op | source)
XLA Modules:
  0.0 104.4 jit_solution(12702031602787891)
XLA Ops:
  0.0 1.6 %shard_map.46 = (f32[16,8,256]{2,1,0:T(8,128)}, f32[16,8,256]{2,1,0:T(8,128)}) custom-call(f32[4,64,256]{2,1,0:T(8,128)} %f.1, f32[4,64,256]{2,1,0:T(8,128)} %c1.1, f32[4,64,256]{2,1,0:T(8,128)} %c2.1, f32[4,64,256]{2,1,0:T(8,128)} %c3.1), custom_call_target="tpu_custom_call" | custom-call | tf_op jit(solution)/shard_map/pallas_call | solution.py:136
  1.6 2.2 %collective-permute-start = (f32[16,8,256]{2,1,0:T(8,128)}, f32[16,8,256]{2,1,0:T(8,128)S(1)}, u32[]{:S(2)}, u32[]{:S(2)}) collective-permute-start(f32[16,8,256]{2,1,0:T(8,128)} %get-tuple-element.34), channel_id=1, source_target_pairs={{0,1},{1,2},{2,3},{3,0},{4,5},{5,6},{6,7},{7,4},{8,9},{9,10},{10,1... | collective-permute-start | bytes 393224 | tf_op jit(solution)/shard_map/ppermute | solution.py:684
  3.8 1.5 %collective-permute-start.1 = (f32[16,8,256]{2,1,0:T(8,128)}, f32[16,8,256]{2,1,0:T(8,128)S(1)}, u32[]{:S(2)}, u32[]{:S(2)}) collective-permute-start(f32[16,8,256]{2,1,0:T(8,128)} %get-tuple-element.35), channel_id=1, source_target_pairs={{0,3},{1,0},{2,1},{3,2},{4,7},{5,4},{6,5},{7,6},{8,11},{9,8},{10,9... | collective-permute-start | bytes 393224 | tf_op jit(solution)/shard_map/ppermute | solution.py:684
  5.4 1.3 %pad_maximum_fusion.inner = f32[16,64,256]{2,1,0:T(8,128)S(1)} fusion(f32[4,64,256]{2,1,0:T(8,128)} %c3.1, f32[4,64,256]{2,1,0:T(8,128)} %c2.1, f32[4,64,256]{2,1,0:T(8,128)} %c1.1, f32[4,64,256]{2,1,0:T(8,128)} %f.1), kind=kLoop, calls=%fused_computation | loop fusion | flops 786432 | bytes 2097152 | tf_op jit(solution)/shard_map/concatenate | solution.py:714
  6.6 1.2 %collective-permute-done.low = f32[16,8,256]{2,1,0:T(8,128)S(1)} collective-permute-done((f32[16,8,256]{2,1,0:T(8,128)}, f32[16,8,256]{2,1,0:T(8,128)S(1)}, u32[]{:S(2)}, u32[]{:S(2)}) %collective-permute-start) | collective-permute-done | bytes 131104 | tf_op jit(solution)/shard_map/ppermute | solution.py:684
  8.4 3.6 %collective-permute-start.3 = (f32[600,256]{1,0:T(8,128)S(1)}, f32[600,256]{1,0:T(8,128)S(1)}, u32[]{:S(2)}, u32[]{:S(2)}) collective-permute-start(f32[600,256]{1,0:T(8,128)S(1)} %get-tuple-element.39), channel_id=1, source_target_pairs={{0,252},{4,0},{8,4},{12,8},{16,12},{20,16},{24,20},{28,24},{32,28}... | collective-permute-start | bytes 1843208 | tf_op jit(solution)/shard_map/ppermute | solution.py:684
  12.2 6.5 %collective-permute-done.2.low = f32[520,256]{1,0:T(8,128)S(1)} collective-permute-done((f32[520,256]{1,0:T(8,128)S(1)}, f32[520,256]{1,0:T(8,128)S(1)}, u32[]{:S(2)}, u32[]{:S(2)}) %collective-permute-start.2) | collective-permute-done | bytes 532512 | tf_op jit(solution)/shard_map/ppermute | solution.py:684
  18.6 1.3 %collective-permute-done.3.high = f32[600,256]{1,0:T(8,128)S(1)} collective-permute-done((f32[600,256]{1,0:T(8,128)S(1)}, f32[600,256]{1,0:T(8,128)S(1)}, u32[]{:S(2)}, u32[]{:S(2)}) %collective-permute-start.3) | collective-permute-done | bytes 614432 | tf_op jit(solution)/shard_map/ppermute | solution.py:684
  19.9 3.1 %shard_map.48 = (f32[6,80,256]{2,1,0:T(8,128)S(1)}, f32[7,80,256]{2,1,0:T(8,128)S(1)}, f32[6,80,256]{2,1,0:T(8,128)S(1)}, f32[6,80,256]{2,1,0:T(8,128)S(1)}, f32...) custom-call(f32[16,80,256]{2,1,0:T(8,128)S(1)} %get-tuple-element.36, ...), custom_call_target="tpu_custom_call" | custom-call | tf_op jit(solution)/shard_map/pallas_call | solution.py:136
  23.8 1.0 collective-permute-start.4
  24.8 8.4 %collective-permute-start.5 = (f32[8,40,128]{2,1,0:T(8,128)}, f32[8,40,128]{2,1,0:T(8,128)S(1)}, u32[]{:S(2)}, u32[]{:S(2)}) collective-permute-start(f32[8,40,128]{2,1,0:T(8,128)} %get-tuple-element.41), channel_id=1, source_target_pairs={{0,252},{4,0},{8,4},{12,8},{16,12},{20,16},{24,20},{28,24},{32,28}... | collective-permute-start | bytes 491528 | tf_op jit(solution)/shard_map/ppermute | solution.py:684
  34.4 1.3 %shard_map.50 = (f32[6,40,128]{2,1,0:T(8,128)S(1)}, f32[6,40,128]{2,1,0:T(8,128)S(1)}, f32[6,40,128]{2,1,0:T(8,128)S(1)}, f32[40,128]{1,0:T(8,128)S(1)}, f32[56,128]{1,0:T(8,128)S(1)}, /*index=5*/f32[56,128]{1,0:T(8,128)S(1)}) custom-call(f32[8,40,128]{2,1,0:T(8,128)} %get-tuple-element.40.own, f32[8,40,128]{2,1,0:T(8,128)S(1)} %collective-permute-done.4.low, ...), custom_call_target="tpu_custom_call" | custom-call | tf_op jit(solution)/shard_map/pallas_call | solution.py:136
  35.6 1.1 %collective-permute-start.6 = (f32[56,128]{1,0:T(8,128)S(1)}, f32[56,128]{1,0:T(8,128)S(1)}, u32[]{:S(2)}, u32[]{:S(2)}) collective-permute-start(f32[56,128]{1,0:T(8,128)S(1)} %get-tuple-element.44), channel_id=1, source_target_pairs={{0,1},{1,2},{2,3},{3,0},{4,5},{5,6},{6,7},{7,4},{8,9},{9,10},{10,1... | collective-permute-start | bytes 86024 | tf_op jit(solution)/shard_map/ppermute | solution.py:684
  36.7 1.7 %collective-permute-start.7 = (f32[56,128]{1,0:T(8,128)S(1)}, f32[56,128]{1,0:T(8,128)S(1)}, u32[]{:S(2)}, u32[]{:S(2)}) collective-permute-start(f32[56,128]{1,0:T(8,128)S(1)} %get-tuple-element.45), channel_id=1, source_target_pairs={{0,3},{1,0},{2,1},{3,2},{4,7},{5,4},{6,5},{7,6},{8,11},{9,8},{10,9... | collective-permute-start | bytes 86024 | tf_op jit(solution)/shard_map/ppermute | solution.py:684
  38.4 1.1 %collective-permute-start.8 = (f32[40,128]{1,0:T(8,128)S(1)}, f32[40,128]{1,0:T(8,128)S(1)}, u32[]{:S(2)}, u32[]{:S(2)}) collective-permute-start(f32[40,128]{1,0:T(8,128)S(1)} %get-tuple-element.43.f2), channel_id=1, source_target_pairs={{0,2},{1,3},{2,0},{3,1},{4,6},{5,7},{6,4},{7,5},{8,10},{9,11},{10,... | collective-permute-start | bytes 61448 | tf_op jit(solution)/shard_map/ppermute | solution.py:684
  39.6 3.0 %collective-permute-done.8.far = f32[40,128]{1,0:T(8,128)S(1)} collective-permute-done((f32[40,128]{1,0:T(8,128)S(1)}, f32[40,128]{1,0:T(8,128)S(1)}, u32[]{:S(2)}, u32[]{:S(2)}) %collective-permute-start.8) | collective-permute-done | bytes 20512 | tf_op jit(solution)/shard_map/ppermute | solution.py:684
  43.3 8.8 %collective-permute-start.9 = (f32[240,128]{1,0:T(8,128)S(1)}, f32[240,128]{1,0:T(8,128)S(1)}, u32[]{:S(2)}, u32[]{:S(2)}) collective-permute-start(f32[240,128]{1,0:T(8,128)S(1)} %get-tuple-element.48.msg), channel_id=1, source_target_pairs={{0,4},{4,0},{8,12},{12,8},{16,20},{20,16},{24,28},{28,24},{32,36},... | collective-permute-start | bytes 368648 | tf_op jit(solution)/shard_map/ppermute | solution.py:688
  52.1 1.0 collective-permute-done.9.sib
  53.8 5.1 %collective-permute-done.10.near = f32[384,128]{1,0:T(8,128)S(1)} collective-permute-done((f32[384,128]{1,0:T(8,128)S(1)}, f32[384,128]{1,0:T(8,128)S(1)}, u32[]{:S(2)}, u32[]{:S(2)}) %collective-permute-start.10) | collective-permute-done | bytes 196640 | tf_op jit(solution)/shard_map/ppermute | solution.py:693
  58.8 3.7 %collective-permute-start.11 = (f32[384,128]{1,0:T(8,128)S(1)}, f32[384,128]{1,0:T(8,128)S(1)}, u32[]{:S(2)}, u32[]{:S(2)}) collective-permute-start(f32[384,128]{1,0:T(8,128)S(1)} %collective-permute-done.10.near), channel_id=1, source_target_pairs={{0,4},{4,0},{8,12},{12,8},{16,20},{20,16},{24,28},{28,24},{32,36},... | collective-permute-start | bytes 589832 | tf_op jit(solution)/shard_map/ppermute | solution.py:688
  63.6 0.9 shard_map.53
  65.3 14.9 %all_to_all.5.mine = f32[32,2,8,128]{3,2,1,0:T(8,128)S(1)} all-to-all(f32[32,2,8,128]{3,2,1,0:T(8,128)S(1)} %shard_map.55), channel_id=1, replica_groups={{0,8,16,24,32,40,48,56,64,72,80,88,96,104,112,120,128,136,144,152,160,1..., dimensions={0} | all-to-all | bytes 524288 | tf_op jit(solution)/shard_map/all_to_all | solution.py:743
  80.2 3.0 %collective-permute-start.12 = (f32[32,2,8,128]{3,2,1,0:T(8,128)S(1)}, f32[32,2,8,128]{3,2,1,0:T(8,128)S(1)}, u32[]{:S(2)}, u32[]{:S(2)}) collective-permute-start(f32[32,2,8,128]{3,2,1,0:T(8,128)S(1)} %all_to_all.5.mine), channel_id=1, source_target_pairs={{0,4},{4,0},{8,12},{12,8},{16,20},{20,16},{24,28},{28,24},{32,36},... | collective-permute-start | bytes 786440 | tf_op jit(solution)/shard_map/ppermute | solution.py:688
  83.2 1.5 %collective-permute-start.13 = (f32[32,128]{1,0:T(8,128)S(1)}, f32[32,128]{1,0:T(8,128)S(1)}, u32[]{:S(2)}, u32[]{:S(2)}) collective-permute-start(f32[32,128]{1,0:T(8,128)S(1)} %get-tuple-element.51), channel_id=1, source_target_pairs={{0,252},{4,8},{8,4},{12,16},{16,12},{20,24},{24,20},{28,32},{32,28... | collective-permute-start | bytes 49160 | tf_op jit(solution)/shard_map/ppermute | solution.py:693
  84.8 3.3 %shard_map.56.e2 = f32[192,128]{1,0:T(8,128)S(1)} custom-call(s32[2]{0:T(128)S(1)} %pad_add_fusion.place, f32[32,2,8,128]{3,2,1,0:T(8,128)S(1)} %all_to_all.5.mine, f32[32,2,8,128]{3,2,1,0:T(8,128)S(1)} %collective-permute-done.12.theirs), custom_call_target="tpu_custom_call" | custom-call | tf_op jit(solution)/shard_map/pallas_call | solution.py:136
  88.8 1.7 %collective-permute-start.14 = (f32[64,128]{1,0:T(8,128)S(1)}, f32[64,128]{1,0:T(8,128)S(1)}, u32[]{:S(2)}, u32[]{:S(2)}) collective-permute-start(f32[64,128]{1,0:T(8,128)S(1)} %shard_map.57.e2), channel_id=1, source_target_pairs={{0,4},{4,0},{8,12},{12,8},{16,20},{20,16},{24,28},{28,24},{32,36},... | collective-permute-start | bytes 98312 | tf_op jit(solution)/shard_map/ppermute | solution.py:688
  91.4 0.9 collective-permute-start.16
  92.3 1.6 %collective-permute-done.15.near0 = f32[64,128]{1,0:T(8,128)S(1)} collective-permute-done((f32[64,128]{1,0:T(8,128)S(1)}, f32[64,128]{1,0:T(8,128)S(1)}, u32[]{:S(2)}, u32[]{:S(2)}) %collective-permute-start.15) | collective-permute-done | bytes 32800 | tf_op jit(solution)/shard_map/ppermute | solution.py:693
  93.9 0.9 collective-permute-done.16.near1
  94.7 1.2 %shard_map.58 = (f32[2,40,128]{2,1,0:T(8,128)S(1)}, f32[40,128]{1,0:T(8,128)S(1)}, f32[40,128]{1,0:T(8,128)S(1)}) custom-call(s32[2]{0:T(128)S(1)} %pad_add_fusion.place, f32[64,128]{1,0:T(8,128)S(1)} %shard_map.57.e2, f32[64,128]{1,0:T(8,128)S(1)} %collective-permute-done.14.e2sib, f32[64,128]{1,0:T(8,128)S(1)} %collective-permute-done.15.near0, ...), custom_call_target="tpu_custom_call" | custom-call | tf_op jit(solution)/shard_map/pallas_call | solution.py:136
  95.9 4.8 %collective-permute-start.17 = (f32[40,128]{1,0:T(8,128)S(1)}, f32[40,128]{1,0:T(8,128)S(1)}, u32[]{:S(2)}, u32[]{:S(2)}) collective-permute-start(f32[40,128]{1,0:T(8,128)S(1)} %get-tuple-element.56), channel_id=1, source_target_pairs={{0,4},{4,0},{8,12},{12,8},{16,20},{20,16},{24,28},{28,24},{32,36},... | collective-permute-start | bytes 61448 | tf_op jit(solution)/shard_map/ppermute | solution.py:688
  101.6 2.8 %shard_map.59 = f32[4,64,256]{2,1,0:T(8,128)} custom-call(s32[2]{0:T(128)S(1)} %pad_add_fusion.place, f32[2,40,128]{2,1,0:T(8,128)S(1)} %get-tuple-element.54.e1, f32[40,128]{1,0:T(8,128)S(1)} %get-tuple-element.55.edge, f32[40,128]{1,0:T(8,128)S(1)} %collective-permute-done.17.other, f32[8,40,128]{2,1,0:T(8,128)S(1)} %collective-permute-done.4.low, ...), custom_call_target="tpu_custom_call" | custom-call | tf_op jit(solution)/shard_map/pallas_call | solution.py:136
  (25 shorter events, 8.6 us)
Async XLA Ops:
  1.6 6.2 %collective-permute-start = (f32[16,8,256]{2,1,0:T(8,128)}, f32[16,8,256]{2,1,0:T(8,128)S(1)}, u32[]{:S(2)}, u32[]{:S(2)}) collective-permute-start(f32[16,8,256]{2,1,0:T(8,128)} %get-tuple-element.34), channel_id=1, source_target_pairs={{0,1},{1,2},{2,3},{3,0},{4,5},{5,6},{6,7},{7,4},{8,9},{9,10},{10,1... | collective-permute-start | bytes 393224 | tf_op jit(solution)/shard_map/ppermute | solution.py:684
  3.8 4.0 %collective-permute-start.1 = (f32[16,8,256]{2,1,0:T(8,128)}, f32[16,8,256]{2,1,0:T(8,128)S(1)}, u32[]{:S(2)}, u32[]{:S(2)}) collective-permute-start(f32[16,8,256]{2,1,0:T(8,128)} %get-tuple-element.35), channel_id=1, source_target_pairs={{0,3},{1,0},{2,1},{3,2},{4,7},{5,4},{6,5},{7,6},{8,11},{9,8},{10,9... | collective-permute-start | bytes 393224 | tf_op jit(solution)/shard_map/ppermute | solution.py:684
  8.4 11.5 %collective-permute-start.3 = (f32[600,256]{1,0:T(8,128)S(1)}, f32[600,256]{1,0:T(8,128)S(1)}, u32[]{:S(2)}, u32[]{:S(2)}) collective-permute-start(f32[600,256]{1,0:T(8,128)S(1)} %get-tuple-element.39), channel_id=1, source_target_pairs={{0,252},{4,0},{8,4},{12,8},{16,12},{20,16},{24,20},{28,24},{32,28}... | collective-permute-start | bytes 1843208 | tf_op jit(solution)/shard_map/ppermute | solution.py:684
  11.9 6.7 %collective-permute-start.2 = (f32[520,256]{1,0:T(8,128)S(1)}, f32[520,256]{1,0:T(8,128)S(1)}, u32[]{:S(2)}, u32[]{:S(2)}) collective-permute-start(f32[520,256]{1,0:T(8,128)S(1)} %get-tuple-element.38), channel_id=1, source_target_pairs={{0,4},{4,8},{8,12},{12,16},{16,20},{20,24},{24,28},{28,32},{32,36}... | collective-permute-start | bytes 1597448 | tf_op jit(solution)/shard_map/ppermute | solution.py:684
  23.0 0.8 copy-start
  23.8 10.4 %collective-permute-start.4 = (f32[8,40,128]{2,1,0:T(8,128)}, f32[8,40,128]{2,1,0:T(8,128)S(1)}, u32[]{:S(2)}, u32[]{:S(2)}) collective-permute-start(f32[8,40,128]{2,1,0:T(8,128)} %get-tuple-element.40.own), channel_id=1, source_target_pairs={{0,4},{4,8},{8,12},{12,16},{16,20},{20,24},{24,28},{28,32},{32,36}... | collective-permute-start | bytes 491528 | tf_op jit(solution)/shard_map/ppermute | solution.py:684
  24.8 9.6 %collective-permute-start.5 = (f32[8,40,128]{2,1,0:T(8,128)}, f32[8,40,128]{2,1,0:T(8,128)S(1)}, u32[]{:S(2)}, u32[]{:S(2)}) collective-permute-start(f32[8,40,128]{2,1,0:T(8,128)} %get-tuple-element.41), channel_id=1, source_target_pairs={{0,252},{4,0},{8,4},{12,8},{16,12},{20,16},{24,20},{28,24},{32,28}... | collective-permute-start | bytes 491528 | tf_op jit(solution)/shard_map/ppermute | solution.py:684
  35.6 6.9 %collective-permute-start.6 = (f32[56,128]{1,0:T(8,128)S(1)}, f32[56,128]{1,0:T(8,128)S(1)}, u32[]{:S(2)}, u32[]{:S(2)}) collective-permute-start(f32[56,128]{1,0:T(8,128)S(1)} %get-tuple-element.44), channel_id=1, source_target_pairs={{0,1},{1,2},{2,3},{3,0},{4,5},{5,6},{6,7},{7,4},{8,9},{9,10},{10,1... | collective-permute-start | bytes 86024 | tf_op jit(solution)/shard_map/ppermute | solution.py:684
  36.7 5.8 %collective-permute-start.7 = (f32[56,128]{1,0:T(8,128)S(1)}, f32[56,128]{1,0:T(8,128)S(1)}, u32[]{:S(2)}, u32[]{:S(2)}) collective-permute-start(f32[56,128]{1,0:T(8,128)S(1)} %get-tuple-element.45), channel_id=1, source_target_pairs={{0,3},{1,0},{2,1},{3,2},{4,7},{5,4},{6,5},{7,6},{8,11},{9,8},{10,9... | collective-permute-start | bytes 86024 | tf_op jit(solution)/shard_map/ppermute | solution.py:684
  38.4 4.1 %collective-permute-start.8 = (f32[40,128]{1,0:T(8,128)S(1)}, f32[40,128]{1,0:T(8,128)S(1)}, u32[]{:S(2)}, u32[]{:S(2)}) collective-permute-start(f32[40,128]{1,0:T(8,128)S(1)} %get-tuple-element.43.f2), channel_id=1, source_target_pairs={{0,2},{1,3},{2,0},{3,1},{4,6},{5,7},{6,4},{7,5},{8,10},{9,11},{10,... | collective-permute-start | bytes 61448 | tf_op jit(solution)/shard_map/ppermute | solution.py:684
  43.3 9.8 %collective-permute-start.9 = (f32[240,128]{1,0:T(8,128)S(1)}, f32[240,128]{1,0:T(8,128)S(1)}, u32[]{:S(2)}, u32[]{:S(2)}) collective-permute-start(f32[240,128]{1,0:T(8,128)S(1)} %get-tuple-element.48.msg), channel_id=1, source_target_pairs={{0,4},{4,0},{8,12},{12,8},{16,20},{20,16},{24,28},{28,24},{32,36},... | collective-permute-start | bytes 368648 | tf_op jit(solution)/shard_map/ppermute | solution.py:688
  53.7 5.2 %collective-permute-start.10 = (f32[384,128]{1,0:T(8,128)S(1)}, f32[384,128]{1,0:T(8,128)S(1)}, u32[]{:S(2)}, u32[]{:S(2)}) collective-permute-start(f32[384,128]{1,0:T(8,128)S(1)} %shard_map.52), channel_id=1, source_target_pairs={{0,252},{4,8},{8,4},{12,16},{16,12},{20,24},{24,20},{28,32},{32,28... | collective-permute-start | bytes 589832 | tf_op jit(solution)/shard_map/ppermute | solution.py:693
  58.8 4.8 %collective-permute-start.11 = (f32[384,128]{1,0:T(8,128)S(1)}, f32[384,128]{1,0:T(8,128)S(1)}, u32[]{:S(2)}, u32[]{:S(2)}) collective-permute-start(f32[384,128]{1,0:T(8,128)S(1)} %collective-permute-done.10.near), channel_id=1, source_target_pairs={{0,4},{4,0},{8,12},{12,8},{16,20},{20,16},{24,28},{28,24},{32,36},... | collective-permute-start | bytes 589832 | tf_op jit(solution)/shard_map/ppermute | solution.py:688
  80.2 4.5 %collective-permute-start.12 = (f32[32,2,8,128]{3,2,1,0:T(8,128)S(1)}, f32[32,2,8,128]{3,2,1,0:T(8,128)S(1)}, u32[]{:S(2)}, u32[]{:S(2)}) collective-permute-start(f32[32,2,8,128]{3,2,1,0:T(8,128)S(1)} %all_to_all.5.mine), channel_id=1, source_target_pairs={{0,4},{4,0},{8,12},{12,8},{16,20},{20,16},{24,28},{28,24},{32,36},... | collective-permute-start | bytes 786440 | tf_op jit(solution)/shard_map/ppermute | solution.py:688
  83.2 18.3 %copy-start.1 = (f32[6,80,256]{2,1,0:T(8,128)S(1)}, f32[6,80,256]{2,1,0:T(8,128)}, u32[]{:S(2)}) copy-start(f32[6,80,256]{2,1,0:T(8,128)} %copy-done) | copy-start | bytes 1474564
  83.2 4.9 %collective-permute-start.13 = (f32[32,128]{1,0:T(8,128)S(1)}, f32[32,128]{1,0:T(8,128)S(1)}, u32[]{:S(2)}, u32[]{:S(2)}) collective-permute-start(f32[32,128]{1,0:T(8,128)S(1)} %get-tuple-element.51), channel_id=1, source_target_pairs={{0,252},{4,8},{8,4},{12,16},{16,12},{20,24},{24,20},{28,32},{32,28... | collective-permute-start | bytes 49160 | tf_op jit(solution)/shard_map/ppermute | solution.py:693
  88.8 2.6 %collective-permute-start.14 = (f32[64,128]{1,0:T(8,128)S(1)}, f32[64,128]{1,0:T(8,128)S(1)}, u32[]{:S(2)}, u32[]{:S(2)}) collective-permute-start(f32[64,128]{1,0:T(8,128)S(1)} %shard_map.57.e2), channel_id=1, source_target_pairs={{0,4},{4,0},{8,12},{12,8},{16,20},{20,16},{24,28},{28,24},{32,36},... | collective-permute-start | bytes 98312 | tf_op jit(solution)/shard_map/ppermute | solution.py:688
  90.5 3.3 %collective-permute-start.15 = (f32[64,128]{1,0:T(8,128)S(1)}, f32[64,128]{1,0:T(8,128)S(1)}, u32[]{:S(2)}, u32[]{:S(2)}) collective-permute-start(f32[64,128]{1,0:T(8,128)S(1)} %shard_map.57.e2), channel_id=1, source_target_pairs={{0,252},{4,8},{8,4},{12,16},{16,12},{20,24},{24,20},{28,32},{32,28... | collective-permute-start | bytes 98312 | tf_op jit(solution)/shard_map/ppermute | solution.py:693
  91.4 3.3 %collective-permute-start.16 = (f32[64,128]{1,0:T(8,128)S(1)}, f32[64,128]{1,0:T(8,128)S(1)}, u32[]{:S(2)}, u32[]{:S(2)}) collective-permute-start(f32[64,128]{1,0:T(8,128)S(1)} %collective-permute-done.14.e2sib), channel_id=1, source_target_pairs={{0,252},{4,8},{8,4},{12,16},{16,12},{20,24},{24,20},{28,32},{32,28... | collective-permute-start | bytes 98312 | tf_op jit(solution)/shard_map/ppermute | solution.py:693
  95.9 5.6 %collective-permute-start.17 = (f32[40,128]{1,0:T(8,128)S(1)}, f32[40,128]{1,0:T(8,128)S(1)}, u32[]{:S(2)}, u32[]{:S(2)}) collective-permute-start(f32[40,128]{1,0:T(8,128)S(1)} %get-tuple-element.56), channel_id=1, source_target_pairs={{0,4},{4,0},{8,12},{12,8},{16,20},{20,16},{24,28},{28,24},{32,36},... | collective-permute-start | bytes 61448 | tf_op jit(solution)/shard_map/ppermute | solution.py:688

commit v5 on v4

--- a/solution.py
+++ b/solution.py
@@ -143,9 +143,6 @@
         )(*args)
 
     return run
-
-
-SCALARS = {0: pltpu.SMEM}
 
 
 def two_blocks(x):
@@ -339,8 +336,8 @@
     return jnp.concatenate([spread_block(x, 0, 64), spread_block(x, 1, 64)], axis=0)
 
 
-def coarse_start_kernel(place, f2, low, high, far, u2fine, own, msg):
-    n = place[1]
+def coarse_start_kernel(f2, low, high, far, u2fine, own, msg):
+    n = lax.axis_index("narrow")
     for piece, by in ((f2, 0), (high, 1), (far, 2), (low, 3)):
         at = pl.multiple_of(16 * lax.rem(n + by, 4), 16)
         for k in range(5):
@@ -355,8 +352,8 @@
         msg[at + 36 : at + 40] = high[40 + 8 * p : 44 + 8 * p]
 
 
-def coarse_tiles_kernel(place, msg, sib, tiles, scr):
-    odd = lax.rem(place[0], 2) == 1
+def coarse_tiles_kernel(msg, sib, tiles, scr):
+    odd = lax.rem(lax.axis_index("wide"), 2) == 1
     for a in range(3):
         here = slice(64 + 32 * a, 96 + 32 * a)
         x = jnp.where(odd, sib[here], msg[here]) if a == 0 else msg[here] + sib[here]
@@ -375,18 +372,18 @@
     return packed
 
 
-def coarse_swap_kernel(place, own, msg, sib, w1, out):
+def coarse_swap_kernel(own, msg, sib, w1, out):
     out[0:160] = msg[0:160]
     out[160:192] = sib[0:32] * sib[32:64] * (1.0 / THETA)
     out[192:224] = two_blocks(own[2])
     out[224:304] = msg[160:240]
-    par = lax.rem(place[0], 2)
+    par = lax.rem(lax.axis_index("wide"), 2)
     out[304:344] = sib[pl.ds(pl.multiple_of(160 + 40 * par, 8), 40), :]
     out[344:384] = w1[4]
 
 
-def coarse_pre_kernel(place, own, sib, near, other, w, u2, late, u1):
-    odd = lax.rem(place[0], 2) == 1
+def coarse_pre_kernel(own, sib, near, other, w, u2, late, u1):
+    odd = lax.rem(lax.axis_index("wide"), 2) == 1
 
     def below(k):
         here = slice(32 * k, 32 * k + 32)
@@ -412,8 +409,8 @@
     late[...] = two_blocks(jnp.where(odd, u2[1], u2[2]))
 
 
-def coarse_send_kernel(place, w, u2, tiles, send, scr):
-    odd = lax.rem(place[0], 2) == 1
+def coarse_send_kernel(w, u2, tiles, send, scr):
+    odd = lax.rem(lax.axis_index("wide"), 2) == 1
     total = 0.0
     for k in (1, 2):
         args = (w[8 + k], w[9 + k], w[13 + k], w[17 + k])
@@ -481,7 +478,7 @@
 THREE, FOUR = (32, 4), (16, 2)
 
 
-def bottom_kernel(place, mine, theirs, e2,
+def bottom_kernel(mine, theirs, e2,
                   f3, c1, c2, c3, d3, g3, u1, u2, res, f4, d1, d2, e3, g4, ua, ub, st, scr):
     n3, n4 = f3.shape[0], f4.shape[0]
 
@@ -492,7 +489,7 @@
 
         lax.fori_loop(0, n3 // STEP, step, 0)
 
-    odd = lax.rem(place[0], 2) == 1
+    odd = lax.rem(lax.axis_index("wide"), 2) == 1
 
     def load(j):
         here = pl.ds(j, STEP)
@@ -564,7 +561,7 @@
         wrap(dst, n4)
         src, dst = dst, src
 
-    j0 = around(place[0] // 2 - 1, n3)
+    j0 = around(lax.axis_index("wide") // 2 - 1, n3)
     k, j = iota((128, 128), 0), iota((128, 128), 1)
     unfold = (k == 16 * (j // 64) + j % 32 // 2).astype(F32)
     coarse = jnp.concatenate([src[1 + around(around(j0 - 2, n3) // 2 + m, n4)] for m in range(4)], axis=0)
@@ -592,8 +589,8 @@
         e2[pl.ds(2 * q + 1, 24, stride=8), :] = fine
 
 
-def coarse_post_kernel(place, e2, win, u2, late, out):
-    par = lax.rem(place[0], 2)
+def coarse_post_kernel(e2, win, u2, late, out):
+    par = lax.rem(lax.axis_index("wide"), 2)
     odd = par == 1
     late = both_halves(late[...])
     v = [jnp.where(odd, u2[0], late), u2[par], u2[1 + par], u2[2 + par], jnp.where(odd, late, u2[3])]
@@ -607,13 +604,18 @@
     out[...] = second_post(w[1], v[2], w[0], w[2], *args(1))
 
 
-def middle_post_kernel(place, e2, e2sib, near0, near1, msg, sib, near, f, g, w1, own, edge, send, fine, c1, v, w):
-    n, par = place[1], lax.rem(place[0], 2)
+def pair_kernel(a, b, out):
+    out[0] = a[...]
+    out[1] = b[...]
+
+
+def middle_post_kernel(e2, e2sib, far, msg, sib, near, f, g, w1, own, edge, send, fine, c1, v, w):
+    n, par = lax.axis_index("narrow"), lax.rem(lax.axis_index("wide"), 2)
     odd = par == 1
     row, col = iota((40, 64), 0), iota((40, 64), 1)
     pick = (col == lax.rem(16 * n + (row + 4) // 2 + 60, 64)).astype(F32)
     lanes = copies_of_lanes(128, 128)
-    e2, e2sib, near0, near1 = e2[...], e2sib[...], near0[...], near1[...]
+    e2, e2sib, near0, near1 = e2[...], e2sib[...], far[0], far[1]
     for k, (upper, lower) in enumerate(((e2sib, near1), (e2, near0), (near0, e2), (near1, e2sib))):
         fine[k] = mul(mul_left(pick, jnp.where(odd, upper, lower)), lanes)
     c1[0:6] = w1[0:6]
@@ -639,8 +641,8 @@
     send[...] = jnp.where(odd, out[0], out[2])
 
 
-def fine_post_kernel(place, e1, edge, other, low, high, f, c1, c2, c3, g, u2, out, v, w, scr):
-    odd = lax.rem(place[0], 2) == 1
+def fine_post_kernel(e1, edge, other, low, high, f, c1, c2, c3, g, u2, out, v, w, scr):
+    odd = lax.rem(lax.axis_index("wide"), 2) == 1
     below, above = jnp.where(odd, other[...], edge[...]), jnp.where(odd, edge[...], other[...])
     x = jnp.concatenate([below, e1[0], e1[1], above], axis=0)
     for half in range(2):
@@ -696,7 +698,6 @@
 def body(source, coef_first, coef_second, coef_third):
     wide = lax.axis_size("wide")
     n3, n4 = wide // 2, wide // 4
-    place = jnp.stack([lax.axis_index("wide"), lax.axis_index("narrow")]).astype(jnp.int32)
     big = (80, 256)
     inputs = (source, coef_first, coef_second, coef_third)
 
@@ -729,16 +730,17 @@
     )(up, low1, high1, w1, coefs)
     low, high, far = shift(up, "narrow", 1), shift(down, "narrow", -1), shift(f2, "narrow", 2)
 
-    own2, msg = call(coarse_start_kernel, [(6, 64, 128), (240, 128)], (), SCALARS)(place, f2, low, high, far, u2m)
+    own2, msg = call(coarse_start_kernel, [(6, 64, 128), (240, 128)])(f2, low, high, far, u2m)
     sib = sibling(msg)
-    (swap,) = call(coarse_swap_kernel, [(384, 128)], (), SCALARS)(place, own2, msg, sib, w1)
+    (swap,) = call(coarse_swap_kernel, [(384, 128)])(own2, msg, sib, w1)
     near = across(swap)
-    (tiles,) = call(coarse_tiles_kernel, [(3, 8, 128)], [(64, 128)], SCALARS)(place, msg, sib)
+    (tiles,) = call(coarse_tiles_kernel, [(3, 8, 128)], [(64, 128)])(msg, sib)
+    near, tiles = lax.optimization_barrier((near, tiles))
     other = sibling(near)
     w2, u2w, late = call(
-        coarse_pre_kernel, [(21, 64, 128), (4, 64, 128), (32, 128)], [(6, 64, 128)], SCALARS
-    )(place, own2, sib, near, other)
-    (send,) = call(coarse_send_kernel, [(n3, 2, 8, 128)], [(64, 128)], SCALARS)(place, w2, u2w, tiles)
+        coarse_pre_kernel, [(21, 64, 128), (4, 64, 128), (32, 128)], [(6, 64, 128)]
+    )(own2, sib, near, other)
+    (send,) = call(coarse_send_kernel, [(n3, 2, 8, 128)], [(64, 128)])(w2, u2w, tiles)
     cores = [[k for k in range(wide) if k % 2 == c] for c in range(2)]
     parts = lax.all_to_all(send, "wide", split_axis=0, concat_axis=0, tiled=True, axis_index_groups=cores)
     theirs, late = sibling(parts), across(late)
@@ -749,23 +751,22 @@
         [(192, 128)],
         [three, (n3 + 1, 8, 128), three, three, three, three, (n3 + 2, 8, 128), (n3 + 2, 8, 128), four, four]
         + [(n4 + 1, 8, 128), four, four, four, (n4 + 2, 8, 128), (n4 + 2, 8, 128), four, (32, 128)],
-        SCALARS,
-    )(place, parts, theirs)
-    (e2,) = call(coarse_post_kernel, [(64, 128)], (), SCALARS)(place, fine2, w2, u2w, late)
-    near0, e2sib = across(e2), sibling(e2)
-    near1 = across(e2sib)
+    )(parts, theirs)
+    (e2,) = call(coarse_post_kernel, [(64, 128)])(fine2, w2, u2w, late)
+    e2sib = sibling(e2)
+    (both,) = call(pair_kernel, [(2, 64, 128)])(e2, e2sib)
+    far = across(both)
 
     e1, edge, send = call(
         middle_post_kernel,
         [(2, 40, 128), (40, 128), (40, 128)],
         [(4, 40, 128), (7, 40, 128), (7, 40, 128), (7, 40, 128)],
-        SCALARS,
-    )(place, e2, e2sib, near0, near1, msg, sib, near, f1w, g1w, w1)
+    )(e2, e2sib, far, msg, sib, near, f1w, g1w, w1)
     other1 = sibling(send)
 
     (out,) = call(
-        fine_post_kernel, [(4, 64, 256)], [(8,) + big, (8,) + big, (320, 128)], SCALARS
-    )(place, e1, edge, other1, low1, high1, f, c1, c2, c3, g, u2)
+        fine_post_kernel, [(4, 64, 256)], [(8,) + big, (8,) + big, (320, 128)]
+    )(e1, edge, other1, low1, high1, f, c1, c2, c3, g, u2)
     return out
 
 

time: 105 us -> 97.1 us (0.925)
  Pallas kernels: 18.6 us -> 12.8 us
  waiting for transfers between devices: 23.3 us -> 26.3 us
  starting transfers between devices: 45.3 us -> 43.2 us
  blocking collectives: 14.9 us -> 13.2 us
    pallas_call x14 -> x15, Pallas kernels: 18.6 us -> 12.8 us  [run(): pl.pallas_call(kernel, out_shape=[jax.ShapeDtypeStruct(s, F32) for s in o...]
    all_to_all x1, blocking collectives: 14.9 us -> 13.2 us  [body(): lax.all_to_all(send, 'wide', split_axis=0, concat_axis=0, tiled=True, axi...]
    ppermute x5, starting transfers between devices: 22 us -> 20.8 us  [sibling(): lax.ppermute(x, 'wide', [(i, i ^ 1) for i in range(lax.axis_size('wide'))])]
    ppermute x9, waiting for transfers between devices: 12.9 us -> 14 us  [shift(): return lax.ppermute(x, axis, [(i, (i + by) % count) for i in range(count)])]
    ppermute x4 -> x3, waiting for transfers between devices: 7.53 us -> 8.48 us  [across(): lax.ppermute(x, 'wide', [(i, (i + 1 if i % 2 else i - 1) % count) for i i...]
    ppermute x4 -> x3, starting transfers between devices: 2.56 us -> 1.74 us  [across(): lax.ppermute(x, 'wide', [(i, (i + 1 if i % 2 else i - 1) % count) for i i...]
  transfers between devices with their start and end apart: 18 -> 17, of which waited for: 13 -> 12; matrix products, arithmetic and copies ran while one was open for 1% -> 1% of each run, Pallas kernels for 4% -> 3%
where the time goes in v5:
time: 97.1 us; the launch traced here: 96.9 us
  starting transfers between devices  43.2 us (44%)
  waiting for transfers between devices  26.3 us (27%)
  blocking collectives  13.2 us (14%)
  Pallas kernels  12.8 us (13%)
  other arithmetic  1.26 us (1%)
    ppermute x5, starting transfers between devices, sibling(): lax.ppermute(x, 'wide', [(i, i ^ 1) for i in range(lax.axis_size('wide'))])  20.8 us
    ppermute x9, starting transfers between devices, shift(): return lax.ppermute(x, axis, [(i, (i + by) % count) for i in range(count)])  20.7 us
    ppermute x9, waiting for transfers between devices, shift(): return lax.ppermute(x, axis, [(i, (i + by) % count) for i in range(count)])  14 us
    all_to_all x1, blocking collectives, body(): lax.all_to_all(send, 'wide', split_axis=0, concat_axis=0, tiled=True, axi...  13.2 us
    pallas_call x15, Pallas kernels, run(): pl.pallas_call(kernel, out_shape=[jax.ShapeDtypeStruct(s, F32) for s in o...  12.8 us
    ppermute x3, waiting for transfers between devices, across(): lax.ppermute(x, 'wide', [(i, (i + 1 if i % 2 else i - 1) % count) for i i...  8.48 us
    ppermute x5, waiting for transfers between devices, sibling(): lax.ppermute(x, 'wide', [(i, i ^ 1) for i in range(lax.axis_size('wide'))])  3.75 us
  transfers between devices with their start and end apart: 17, of which 12 were waited for; matrix products, arithmetic and copies ran while one was open for 1% of the time, Pallas kernels for 3%

profile of v5, /device:TPU:1, one launch (start us, length us, event | category | flops | bytes accessed | tf_op | source)
XLA Modules:
  0.0 96.9 jit_solution(4435947056213956510)
XLA Ops:
  0.0 1.6 %shard_map.46 = (f32[16,8,256]{2,1,0:T(8,128)}, f32[16,8,256]{2,1,0:T(8,128)}) custom-call(f32[4,64,256]{2,1,0:T(8,128)} %f.1, f32[4,64,256]{2,1,0:T(8,128)} %c1.1, f32[4,64,256]{2,1,0:T(8,128)} %c2.1, f32[4,64,256]{2,1,0:T(8,128)} %c3.1), custom_call_target="tpu_custom_call" | custom-call | tf_op jit(solution)/shard_map/pallas_call | solution.py:136
  1.6 2.2 %collective-permute-start = (f32[16,8,256]{2,1,0:T(8,128)}, f32[16,8,256]{2,1,0:T(8,128)S(1)}, u32[]{:S(2)}, u32[]{:S(2)}) collective-permute-start(f32[16,8,256]{2,1,0:T(8,128)} %get-tuple-element.36), channel_id=1, source_target_pairs={{0,1},{1,2},{2,3},{3,0},{4,5},{5,6},{6,7},{7,4},{8,9},{9,10},{10,1... | collective-permute-start | bytes 393224 | tf_op jit(solution)/shard_map/ppermute | solution.py:686
  3.8 1.5 %collective-permute-start.1 = (f32[16,8,256]{2,1,0:T(8,128)}, f32[16,8,256]{2,1,0:T(8,128)S(1)}, u32[]{:S(2)}, u32[]{:S(2)}) collective-permute-start(f32[16,8,256]{2,1,0:T(8,128)} %get-tuple-element.37), channel_id=1, source_target_pairs={{0,3},{1,0},{2,1},{3,2},{4,7},{5,4},{6,5},{7,6},{8,11},{9,8},{10,9... | collective-permute-start | bytes 393224 | tf_op jit(solution)/shard_map/ppermute | solution.py:686
  5.4 1.3 %pad_maximum_fusion.inner = f32[16,64,256]{2,1,0:T(8,128)S(1)} fusion(f32[4,64,256]{2,1,0:T(8,128)} %c3.1, f32[4,64,256]{2,1,0:T(8,128)} %c2.1, f32[4,64,256]{2,1,0:T(8,128)} %c1.1, f32[4,64,256]{2,1,0:T(8,128)} %f.1), kind=kLoop, calls=%fused_computation | loop fusion | flops 786432 | bytes 2097152 | tf_op jit(solution)/shard_map/concatenate | solution.py:715
  6.6 1.2 %collective-permute-done.low = f32[16,8,256]{2,1,0:T(8,128)S(1)} collective-permute-done((f32[16,8,256]{2,1,0:T(8,128)}, f32[16,8,256]{2,1,0:T(8,128)S(1)}, u32[]{:S(2)}, u32[]{:S(2)}) %collective-permute-start) | collective-permute-done | bytes 131104 | tf_op jit(solution)/shard_map/ppermute | solution.py:686
  8.4 3.6 %collective-permute-start.3 = (f32[600,256]{1,0:T(8,128)S(1)}, f32[600,256]{1,0:T(8,128)S(1)}, u32[]{:S(2)}, u32[]{:S(2)}) collective-permute-start(f32[600,256]{1,0:T(8,128)S(1)} %get-tuple-element.41), channel_id=1, source_target_pairs={{0,252},{4,0},{8,4},{12,8},{16,12},{20,16},{24,20},{28,24},{32,28}... | collective-permute-start | bytes 1843208 | tf_op jit(solution)/shard_map/ppermute | solution.py:686
  12.1 6.5 %collective-permute-done.2.low = f32[520,256]{1,0:T(8,128)S(1)} collective-permute-done((f32[520,256]{1,0:T(8,128)S(1)}, f32[520,256]{1,0:T(8,128)S(1)}, u32[]{:S(2)}, u32[]{:S(2)}) %collective-permute-start.2) | collective-permute-done | bytes 532512 | tf_op jit(solution)/shard_map/ppermute | solution.py:686
  18.6 1.3 %collective-permute-done.3.high = f32[600,256]{1,0:T(8,128)S(1)} collective-permute-done((f32[600,256]{1,0:T(8,128)S(1)}, f32[600,256]{1,0:T(8,128)S(1)}, u32[]{:S(2)}, u32[]{:S(2)}) %collective-permute-start.3) | collective-permute-done | bytes 614432 | tf_op jit(solution)/shard_map/ppermute | solution.py:686
  19.9 3.1 %shard_map.48 = (f32[6,80,256]{2,1,0:T(8,128)S(1)}, f32[7,80,256]{2,1,0:T(8,128)S(1)}, f32[6,80,256]{2,1,0:T(8,128)S(1)}, f32[6,80,256]{2,1,0:T(8,128)S(1)}, f32...) custom-call(f32[16,80,256]{2,1,0:T(8,128)S(1)} %get-tuple-element.38, ...), custom_call_target="tpu_custom_call" | custom-call | tf_op jit(solution)/shard_map/pallas_call | solution.py:136
  23.0 9.3 %collective-permute-start.5 = (f32[8,40,128]{2,1,0:T(8,128)S(1)}, f32[8,40,128]{2,1,0:T(8,128)S(1)}, u32[]{:S(2)}, u32[]{:S(2)}) collective-permute-start(f32[8,40,128]{2,1,0:T(8,128)S(1)} %get-tuple-element.43), channel_id=1, source_target_pairs={{0,252},{4,0},{8,4},{12,8},{16,12},{20,16},{24,20},{28,24},{32,28}... | collective-permute-start | bytes 491528 | tf_op jit(solution)/shard_map/ppermute | solution.py:686
  32.6 0.8 collective-permute-done.5.high
  33.3 1.2 %collective-permute-done.4.low = f32[8,40,128]{2,1,0:T(8,128)S(1)} collective-permute-done((f32[8,40,128]{2,1,0:T(8,128)S(1)}, f32[8,40,128]{2,1,0:T(8,128)S(1)}, u32[]{:S(2)}, u32[]{:S(2)}) %collective-permute-start.4) | collective-permute-done | bytes 163872 | tf_op jit(solution)/shard_map/ppermute | solution.py:686
  34.9 1.1 %collective-permute-start.6 = (f32[56,128]{1,0:T(8,128)S(1)}, f32[56,128]{1,0:T(8,128)S(1)}, u32[]{:S(2)}, u32[]{:S(2)}) collective-permute-start(f32[56,128]{1,0:T(8,128)S(1)} %get-tuple-element.46), channel_id=1, source_target_pairs={{0,1},{1,2},{2,3},{3,0},{4,5},{5,6},{6,7},{7,4},{8,9},{9,10},{10,1... | collective-permute-start | bytes 86024 | tf_op jit(solution)/shard_map/ppermute | solution.py:686
  36.0 1.7 %collective-permute-start.7 = (f32[56,128]{1,0:T(8,128)S(1)}, f32[56,128]{1,0:T(8,128)S(1)}, u32[]{:S(2)}, u32[]{:S(2)}) collective-permute-start(f32[56,128]{1,0:T(8,128)S(1)} %get-tuple-element.47), channel_id=1, source_target_pairs={{0,3},{1,0},{2,1},{3,2},{4,7},{5,4},{6,5},{7,6},{8,11},{9,8},{10,9... | collective-permute-start | bytes 86024 | tf_op jit(solution)/shard_map/ppermute | solution.py:686
  37.7 1.1 %collective-permute-start.8 = (f32[40,128]{1,0:T(8,128)S(1)}, f32[40,128]{1,0:T(8,128)S(1)}, u32[]{:S(2)}, u32[]{:S(2)}) collective-permute-start(f32[40,128]{1,0:T(8,128)S(1)} %get-tuple-element.45.f2), channel_id=1, source_target_pairs={{0,2},{1,3},{2,0},{3,1},{4,6},{5,7},{6,4},{7,5},{8,10},{9,11},{10,... | collective-permute-start | bytes 61448 | tf_op jit(solution)/shard_map/ppermute | solution.py:686
  38.8 3.0 %collective-permute-done.8.far = f32[40,128]{1,0:T(8,128)S(1)} collective-permute-done((f32[40,128]{1,0:T(8,128)S(1)}, f32[40,128]{1,0:T(8,128)S(1)}, u32[]{:S(2)}, u32[]{:S(2)}) %collective-permute-start.8) | collective-permute-done | bytes 20512 | tf_op jit(solution)/shard_map/ppermute | solution.py:686
  42.0 8.5 %collective-permute-start.9 = (f32[240,128]{1,0:T(8,128)S(1)}, f32[240,128]{1,0:T(8,128)S(1)}, u32[]{:S(2)}, u32[]{:S(2)}) collective-permute-start(f32[240,128]{1,0:T(8,128)S(1)} %get-tuple-element.50.msg), channel_id=1, source_target_pairs={{0,4},{4,0},{8,12},{12,8},{16,20},{20,16},{24,28},{28,24},{32,36},... | collective-permute-start | bytes 368648 | tf_op jit(solution)/shard_map/ppermute | solution.py:690
  50.5 1.0 %collective-permute-done.9.sib = f32[240,128]{1,0:T(8,128)S(1)} collective-permute-done((f32[240,128]{1,0:T(8,128)S(1)}, f32[240,128]{1,0:T(8,128)S(1)}, u32[]{:S(2)}, u32[]{:S(2)}) %collective-permute-start.9) | collective-permute-done | bytes 122912 | tf_op jit(solution)/shard_map/ppermute | solution.py:690
  51.9 4.8 %collective-permute-done.10.near = f32[384,128]{1,0:T(8,128)S(1)} collective-permute-done((f32[384,128]{1,0:T(8,128)S(1)}, f32[384,128]{1,0:T(8,128)S(1)}, u32[]{:S(2)}, u32[]{:S(2)}) %collective-permute-start.10) | collective-permute-done | bytes 196640 | tf_op jit(solution)/shard_map/ppermute | solution.py:695
  56.7 3.7 %collective-permute-start.11 = (f32[384,128]{1,0:T(8,128)S(1)}, f32[384,128]{1,0:T(8,128)S(1)}, u32[]{:S(2)}, u32[]{:S(2)}) collective-permute-start(f32[384,128]{1,0:T(8,128)S(1)} %collective-permute-done.10.near), channel_id=1, source_target_pairs={{0,4},{4,0},{8,12},{12,8},{16,20},{20,16},{24,28},{28,24},{32,36},... | collective-permute-start | bytes 589832 | tf_op jit(solution)/shard_map/ppermute | solution.py:690
  60.4 1.1 %collective-permute-done.11.other = f32[384,128]{1,0:T(8,128)S(1)} collective-permute-done((f32[384,128]{1,0:T(8,128)S(1)}, f32[384,128]{1,0:T(8,128)S(1)}, u32[]{:S(2)}, u32[]{:S(2)}) %collective-permute-start.11) | collective-permute-done | bytes 196640 | tf_op jit(solution)/shard_map/ppermute | solution.py:690
  62.1 13.2 %all_to_all.5.mine = f32[32,2,8,128]{3,2,1,0:T(8,128)S(1)} all-to-all(f32[32,2,8,128]{3,2,1,0:T(8,128)S(1)} %shard_map.55), channel_id=1, replica_groups={{0,8,16,24,32,40,48,56,64,72,80,88,96,104,112,120,128,136,144,152,160,1..., dimensions={0} | all-to-all | bytes 524288 | tf_op jit(solution)/shard_map/all_to_all | solution.py:745
  75.3 2.8 %collective-permute-start.12 = (f32[32,2,8,128]{3,2,1,0:T(8,128)S(1)}, f32[32,2,8,128]{3,2,1,0:T(8,128)S(1)}, u32[]{:S(2)}, u32[]{:S(2)}) collective-permute-start(f32[32,2,8,128]{3,2,1,0:T(8,128)S(1)} %all_to_all.5.mine), channel_id=1, source_target_pairs={{0,4},{4,0},{8,12},{12,8},{16,20},{20,16},{24,28},{28,24},{32,36},... | collective-permute-start | bytes 786440 | tf_op jit(solution)/shard_map/ppermute | solution.py:690
  78.0 1.6 %collective-permute-start.13 = (f32[32,128]{1,0:T(8,128)S(1)}, f32[32,128]{1,0:T(8,128)S(1)}, u32[]{:S(2)}, u32[]{:S(2)}) collective-permute-start(f32[32,128]{1,0:T(8,128)S(1)} %get-tuple-element.55), channel_id=1, source_target_pairs={{0,252},{4,8},{8,4},{12,16},{16,12},{20,24},{24,20},{28,32},{32,28... | collective-permute-start | bytes 49160 | tf_op jit(solution)/shard_map/ppermute | solution.py:695
  79.7 2.8 %shard_map.56.e2 = f32[192,128]{1,0:T(8,128)S(1)} custom-call(f32[32,2,8,128]{3,2,1,0:T(8,128)S(1)} %all_to_all.5.mine, f32[32,2,8,128]{3,2,1,0:T(8,128)S(1)} %collective-permute-done.12.theirs), custom_call_target="tpu_custom_call" | custom-call | tf_op jit(solution)/shard_map/pallas_call | solution.py:136
  82.7 2.1 %collective-permute-start.14 = (f32[64,128]{1,0:T(8,128)S(1)}, f32[64,128]{1,0:T(8,128)S(1)}, u32[]{:S(2)}, u32[]{:S(2)}) collective-permute-start(f32[64,128]{1,0:T(8,128)S(1)} %shard_map.57.a.e2), channel_id=1, source_target_pairs={{0,4},{4,0},{8,12},{12,8},{16,20},{20,16},{24,28},{28,24},{32,36},... | collective-permute-start | bytes 98312 | tf_op jit(solution)/shard_map/ppermute | solution.py:690
  84.8 0.9 collective-permute-done.14.b.e2sib
  85.7 3.7 %collective-permute-done.15.far = f32[2,64,128]{2,1,0:T(8,128)S(1)} collective-permute-done((f32[2,64,128]{2,1,0:T(8,128)S(1)}, f32[2,64,128]{2,1,0:T(8,128)S(1)}, u32[]{:S(2)}, u32[]{:S(2)}) %collective-permute-start.15) | collective-permute-done | bytes 65568 | tf_op jit(solution)/shard_map/ppermute | solution.py:695
  89.4 0.7 shard_map.59
  90.0 3.8 %collective-permute-start.16 = (f32[40,128]{1,0:T(8,128)S(1)}, f32[40,128]{1,0:T(8,128)S(1)}, u32[]{:S(2)}, u32[]{:S(2)}) collective-permute-start(f32[40,128]{1,0:T(8,128)S(1)} %get-tuple-element.60), channel_id=1, source_target_pairs={{0,4},{4,0},{8,12},{12,8},{16,20},{20,16},{24,28},{28,24},{32,36},... | collective-permute-start | bytes 61448 | tf_op jit(solution)/shard_map/ppermute | solution.py:690
  93.8 0.8 collective-permute-done.16.other
  94.6 2.2 %shard_map.60 = f32[4,64,256]{2,1,0:T(8,128)} custom-call(f32[2,40,128]{2,1,0:T(8,128)S(1)} %get-tuple-element.58.e1, f32[40,128]{1,0:T(8,128)S(1)} %get-tuple-element.59.edge, f32[40,128]{1,0:T(8,128)S(1)} %collective-permute-done.16.other, f32[8,40,128]{2,1,0:T(8,128)S(1)} %collective-permute-done.4.low, f32[8,40,128]{2,1,0:T(8,128)S(1)} %collective-permute-done.5.high, ...), custom_call_target="tpu_custom_call" | custom-call | tf_op jit(solution)/shard_map/pallas_call | solution.py:136
  (19 shorter events, 2.8 us)
Async XLA Ops:
  1.6 6.2 %collective-permute-start = (f32[16,8,256]{2,1,0:T(8,128)}, f32[16,8,256]{2,1,0:T(8,128)S(1)}, u32[]{:S(2)}, u32[]{:S(2)}) collective-permute-start(f32[16,8,256]{2,1,0:T(8,128)} %get-tuple-element.36), channel_id=1, source_target_pairs={{0,1},{1,2},{2,3},{3,0},{4,5},{5,6},{6,7},{7,4},{8,9},{9,10},{10,1... | collective-permute-start | bytes 393224 | tf_op jit(solution)/shard_map/ppermute | solution.py:686
  3.8 4.0 %collective-permute-start.1 = (f32[16,8,256]{2,1,0:T(8,128)}, f32[16,8,256]{2,1,0:T(8,128)S(1)}, u32[]{:S(2)}, u32[]{:S(2)}) collective-permute-start(f32[16,8,256]{2,1,0:T(8,128)} %get-tuple-element.37), channel_id=1, source_target_pairs={{0,3},{1,0},{2,1},{3,2},{4,7},{5,4},{6,5},{7,6},{8,11},{9,8},{10,9... | collective-permute-start | bytes 393224 | tf_op jit(solution)/shard_map/ppermute | solution.py:686
  8.4 11.5 %collective-permute-start.3 = (f32[600,256]{1,0:T(8,128)S(1)}, f32[600,256]{1,0:T(8,128)S(1)}, u32[]{:S(2)}, u32[]{:S(2)}) collective-permute-start(f32[600,256]{1,0:T(8,128)S(1)} %get-tuple-element.41), channel_id=1, source_target_pairs={{0,252},{4,0},{8,4},{12,8},{16,12},{20,16},{24,20},{28,24},{32,28}... | collective-permute-start | bytes 1843208 | tf_op jit(solution)/shard_map/ppermute | solution.py:686
  11.9 6.7 %collective-permute-start.2 = (f32[520,256]{1,0:T(8,128)S(1)}, f32[520,256]{1,0:T(8,128)S(1)}, u32[]{:S(2)}, u32[]{:S(2)}) collective-permute-start(f32[520,256]{1,0:T(8,128)S(1)} %get-tuple-element.40), channel_id=1, source_target_pairs={{0,4},{4,8},{8,12},{12,16},{16,20},{20,24},{24,28},{28,32},{32,36}... | collective-permute-start | bytes 1597448 | tf_op jit(solution)/shard_map/ppermute | solution.py:686
  23.0 10.4 %collective-permute-start.5 = (f32[8,40,128]{2,1,0:T(8,128)S(1)}, f32[8,40,128]{2,1,0:T(8,128)S(1)}, u32[]{:S(2)}, u32[]{:S(2)}) collective-permute-start(f32[8,40,128]{2,1,0:T(8,128)S(1)} %get-tuple-element.43), channel_id=1, source_target_pairs={{0,252},{4,0},{8,4},{12,8},{16,12},{20,16},{24,20},{28,24},{32,28}... | collective-permute-start | bytes 491528 | tf_op jit(solution)/shard_map/ppermute | solution.py:686
  32.3 2.3 %collective-permute-start.4 = (f32[8,40,128]{2,1,0:T(8,128)S(1)}, f32[8,40,128]{2,1,0:T(8,128)S(1)}, u32[]{:S(2)}, u32[]{:S(2)}) collective-permute-start(f32[8,40,128]{2,1,0:T(8,128)S(1)} %get-tuple-element.42.own), channel_id=1, source_target_pairs={{0,4},{4,8},{8,12},{12,16},{16,20},{20,24},{24,28},{28,32},{32,36}... | collective-permute-start | bytes 491528 | tf_op jit(solution)/shard_map/ppermute | solution.py:686
  34.9 6.9 %collective-permute-start.6 = (f32[56,128]{1,0:T(8,128)S(1)}, f32[56,128]{1,0:T(8,128)S(1)}, u32[]{:S(2)}, u32[]{:S(2)}) collective-permute-start(f32[56,128]{1,0:T(8,128)S(1)} %get-tuple-element.46), channel_id=1, source_target_pairs={{0,1},{1,2},{2,3},{3,0},{4,5},{5,6},{6,7},{7,4},{8,9},{9,10},{10,1... | collective-permute-start | bytes 86024 | tf_op jit(solution)/shard_map/ppermute | solution.py:686
  36.0 5.8 %collective-permute-start.7 = (f32[56,128]{1,0:T(8,128)S(1)}, f32[56,128]{1,0:T(8,128)S(1)}, u32[]{:S(2)}, u32[]{:S(2)}) collective-permute-start(f32[56,128]{1,0:T(8,128)S(1)} %get-tuple-element.47), channel_id=1, source_target_pairs={{0,3},{1,0},{2,1},{3,2},{4,7},{5,4},{6,5},{7,6},{8,11},{9,8},{10,9... | collective-permute-start | bytes 86024 | tf_op jit(solution)/shard_map/ppermute | solution.py:686
  37.7 4.1 %collective-permute-start.8 = (f32[40,128]{1,0:T(8,128)S(1)}, f32[40,128]{1,0:T(8,128)S(1)}, u32[]{:S(2)}, u32[]{:S(2)}) collective-permute-start(f32[40,128]{1,0:T(8,128)S(1)} %get-tuple-element.45.f2), channel_id=1, source_target_pairs={{0,2},{1,3},{2,0},{3,1},{4,6},{5,7},{6,4},{7,5},{8,10},{9,11},{10,... | collective-permute-start | bytes 61448 | tf_op jit(solution)/shard_map/ppermute | solution.py:686
  42.0 9.4 %collective-permute-start.9 = (f32[240,128]{1,0:T(8,128)S(1)}, f32[240,128]{1,0:T(8,128)S(1)}, u32[]{:S(2)}, u32[]{:S(2)}) collective-permute-start(f32[240,128]{1,0:T(8,128)S(1)} %get-tuple-element.50.msg), channel_id=1, source_target_pairs={{0,4},{4,0},{8,12},{12,8},{16,20},{20,16},{24,28},{28,24},{32,36},... | collective-permute-start | bytes 368648 | tf_op jit(solution)/shard_map/ppermute | solution.py:690
  51.5 5.2 %collective-permute-start.10 = (f32[384,128]{1,0:T(8,128)S(1)}, f32[384,128]{1,0:T(8,128)S(1)}, u32[]{:S(2)}, u32[]{:S(2)}) collective-permute-start(f32[384,128]{1,0:T(8,128)S(1)} %shard_map.52), channel_id=1, source_target_pairs={{0,252},{4,8},{8,4},{12,16},{16,12},{20,24},{24,20},{28,32},{32,28... | collective-permute-start | bytes 589832 | tf_op jit(solution)/shard_map/ppermute | solution.py:695
  56.7 4.8 %collective-permute-start.11 = (f32[384,128]{1,0:T(8,128)S(1)}, f32[384,128]{1,0:T(8,128)S(1)}, u32[]{:S(2)}, u32[]{:S(2)}) collective-permute-start(f32[384,128]{1,0:T(8,128)S(1)} %collective-permute-done.10.near), channel_id=1, source_target_pairs={{0,4},{4,0},{8,12},{12,8},{16,20},{20,16},{24,28},{28,24},{32,36},... | collective-permute-start | bytes 589832 | tf_op jit(solution)/shard_map/ppermute | solution.py:690
  75.3 4.4 %collective-permute-start.12 = (f32[32,2,8,128]{3,2,1,0:T(8,128)S(1)}, f32[32,2,8,128]{3,2,1,0:T(8,128)S(1)}, u32[]{:S(2)}, u32[]{:S(2)}) collective-permute-start(f32[32,2,8,128]{3,2,1,0:T(8,128)S(1)} %all_to_all.5.mine), channel_id=1, source_target_pairs={{0,4},{4,0},{8,12},{12,8},{16,20},{20,16},{24,28},{28,24},{32,36},... | collective-permute-start | bytes 786440 | tf_op jit(solution)/shard_map/ppermute | solution.py:690
  78.0 4.4 %collective-permute-start.13 = (f32[32,128]{1,0:T(8,128)S(1)}, f32[32,128]{1,0:T(8,128)S(1)}, u32[]{:S(2)}, u32[]{:S(2)}) collective-permute-start(f32[32,128]{1,0:T(8,128)S(1)} %get-tuple-element.55), channel_id=1, source_target_pairs={{0,252},{4,8},{8,4},{12,16},{16,12},{20,24},{24,20},{28,32},{32,28... | collective-permute-start | bytes 49160 | tf_op jit(solution)/shard_map/ppermute | solution.py:695
  82.7 3.0 %collective-permute-start.14 = (f32[64,128]{1,0:T(8,128)S(1)}, f32[64,128]{1,0:T(8,128)S(1)}, u32[]{:S(2)}, u32[]{:S(2)}) collective-permute-start(f32[64,128]{1,0:T(8,128)S(1)} %shard_map.57.a.e2), channel_id=1, source_target_pairs={{0,4},{4,0},{8,12},{12,8},{16,20},{20,16},{24,28},{28,24},{32,36},... | collective-permute-start | bytes 98312 | tf_op jit(solution)/shard_map/ppermute | solution.py:690
  85.7 3.7 %collective-permute-start.15 = (f32[2,64,128]{2,1,0:T(8,128)S(1)}, f32[2,64,128]{2,1,0:T(8,128)S(1)}, u32[]{:S(2)}, u32[]{:S(2)}) collective-permute-start(f32[2,64,128]{2,1,0:T(8,128)S(1)} %shard_map.58), channel_id=1, source_target_pairs={{0,252},{4,8},{8,4},{12,16},{16,12},{20,24},{24,20},{28,32},{32,28... | collective-permute-start | bytes 196616 | tf_op jit(solution)/shard_map/ppermute | solution.py:695
  90.0 4.6 %collective-permute-start.16 = (f32[40,128]{1,0:T(8,128)S(1)}, f32[40,128]{1,0:T(8,128)S(1)}, u32[]{:S(2)}, u32[]{:S(2)}) collective-permute-start(f32[40,128]{1,0:T(8,128)S(1)} %get-tuple-element.60), channel_id=1, source_target_pairs={{0,4},{4,0},{8,12},{12,8},{16,20},{20,16},{24,28},{28,24},{32,36},... | collective-permute-start | bytes 61448 | tf_op jit(solution)/shard_map/ppermute | solution.py:690

commit v6 on v5

--- a/solution.py
+++ b/solution.py
@@ -161,18 +161,20 @@
         copy.wait()
 
 
-def pad_kernel(inner, low, high, own, coef1, up, down, scr):
+def pad_kernel(inner, low, high, own, coef1, out_far, out_sib, first, scr):
     for a in range(16):
         own[a, 0:8] = low[a]
         own[a, 8:72] = inner[a]
         own[a, 72:80] = high[a]
-    for p, out, slot in ((1, down, 5), (2, up, 4)):
-        diag = diagonal(SIG[0], own[4 + p], own[5 + p], own[8 + p], own[12 + p])
-        out[80 * slot : 80 * slot + 80] = own[p] / diag / THETA
-    for a in range(4):
-        up[80 * a : 80 * a + 80] = own[4 * a + 3]
-        down[80 * a : 80 * a + 80] = own[4 * a]
-    down[320:400] = own[5]
+    par = lax.rem(lax.axis_index("wide"), 2)
+    for k in range(2):
+        diag = diagonal(SIG[0], own[5 + k], own[6 + k], own[9 + k], own[13 + k])
+        first[k] = own[1 + k] / diag / THETA
+    for out, up in ((out_far, par), (out_sib, 1 - par)):
+        for a in range(4):
+            out[80 * a : 80 * a + 80] = own[4 * a + 3 * up]
+        out[320:400] = own[5]
+        out[400:480] = first[up]
     k1 = jnp.concatenate([own[4], own[6]], axis=0)
     k2 = jnp.concatenate([own[8] + own[9], own[10] + own[11]], axis=0)
     k3 = jnp.concatenate([own[12] + own[13], own[14] + own[15]], axis=0)
@@ -180,15 +182,27 @@
     for a in range(3):
         for p in range(2):
             coef1[2 * a + p] = coarse[a][40 * p : 40 * p + 40]
-    for out, at in ((up, 400), (down, 480)):
+    for out in (out_far, out_sib):
         for k in range(6):
-            row, lane = at + 40 * (k // 2), 128 * (k % 2)
+            row, lane = 480 + 40 * (k // 2), 128 * (k % 2)
             out[row : row + 40, lane : lane + 128] = coef1[k]
 
 
-def unpack(ref, at, index):
-    row, lane = at + 40 * (index // 2), 128 * (index % 2)
-    return ref[row : row + 40, lane : lane + 128]
+def block(index):
+    row, lane = 480 + 40 * (index // 2), 128 * (index % 2)
+    return slice(row, row + 40), slice(lane, lane + 128)
+
+
+def sides(far, sib):
+    odd = lax.rem(lax.axis_index("wide"), 2) == 1
+
+    def below(*at):
+        return jnp.where(odd, sib[at], far[at])
+
+    def above(*at):
+        return jnp.where(odd, far[at], sib[at])
+
+    return below, above
 
 
 CHUNK = 16
@@ -228,14 +242,16 @@
     return SIG[0] + c1[q, here, :] + c1[q + 1, here, :] + k2 + h2 + k3 + roll(k3, -1, 1)
 
 
-def fine_pre_kernel(own, coef1, low, high, f, c1, c2, c3, g, u2, w1, msg_up, msg_down, f1, u1, res, scr):
+def fine_pre_kernel(own, coef1, far, sib, f, c1, c2, c3, g, u2, w1, out_far, out_sib, f1, u1, res, scr):
+    below, above = sides(far, sib)
     for a, ref in enumerate((f, c1, c2, c3)):
-        ref[0] = low[80 * a : 80 * a + 80]
+        here = slice(80 * a, 80 * a + 80)
+        ref[0] = below(here)
         ref[1:5] = own[4 * a : 4 * a + 4]
-        ref[5] = high[80 * a : 80 * a + 80]
-    c1[6] = high[320:400]
-    u1[0] = low[320:400]
-    u1[7] = high[400:480]
+        ref[5] = above(here)
+    c1[6] = above(slice(320, 400))
+    u1[0] = below(slice(400, 480))
+    u1[7] = above(slice(400, 480))
 
     def smooth_first(q, carry):
         def rows(r0, n):
@@ -280,16 +296,17 @@
     f1[1] = coarse[40:]
     for a in range(3):
         for p in range(2):
-            w1[6 * a + p] = unpack(low, 400, 2 * a + p)
+            w1[6 * a + p] = below(*block(2 * a + p))
             w1[6 * a + 2 + p] = coef1[2 * a + p]
-            w1[6 * a + 4 + p] = unpack(high, 480, 2 * a + p)
+            w1[6 * a + 4 + p] = above(*block(2 * a + p))
     for p in range(2):
         k = p + 2
         inverse = 1.0 / diagonal(SIG[1], w1[k], w1[k + 1], w1[6 + k], w1[12 + k])
-        for out in (msg_up, msg_down):
+        for out in (out_far, out_sib):
             out[p] = f1[p]
             out[2 + p] = inverse
-    for out, plane in ((msg_up, 4), (msg_down, 3)):
+    par = lax.rem(lax.axis_index("wide"), 2)
+    for out, plane in ((out_far, 3 + par), (out_sib, 4 - par)):
         out[4] = u2[plane, 0:40, 0:128]
         out[5] = u2[plane, 0:40, 128:256]
         out[6] = u2[plane, 40:80, 0:128]
@@ -307,10 +324,12 @@
         out[8 * k : 8 * k + 8] = two_blocks(x)
 
 
-def middle_pre_kernel(own, low, high, w1, coefs, f, g, u2, f2, up, down, u1, scr):
-    for k, ref in enumerate((low, own, high)):
-        f[2 * k : 2 * k + 2] = ref[0:2]
-        g[2 * k : 2 * k + 2] = ref[2:4]
+def middle_pre_kernel(own, far, sib, w1, coefs, f, g, u2, f2, up, down, u1, scr):
+    below, above = sides(far, sib)
+    for k, read in enumerate((below, own.__getitem__, above)):
+        for p in range(2):
+            f[2 * k + p] = read(p)
+            g[2 * k + p] = read(2 + p)
     for p in range(6):
         u1[p] = f[p] * g[p] * (1.0 / THETA)
     u2[0] = u1[0]
@@ -589,35 +608,28 @@
         e2[pl.ds(2 * q + 1, 24, stride=8), :] = fine
 
 
-def coarse_post_kernel(e2, win, u2, late, out):
-    par = lax.rem(lax.axis_index("wide"), 2)
-    odd = par == 1
-    late = both_halves(late[...])
-    v = [jnp.where(odd, u2[0], late), u2[par], u2[1 + par], u2[2 + par], jnp.where(odd, late, u2[3])]
-    v = [v[m] + e2[pl.ds(pl.multiple_of(64 * ((m + par) // 2), 64), 64), :] for m in range(5)]
-
-    def args(m):
-        k = m + par
+def coarse_post_kernel(e2, win, u2, late, late_sib, out):
+    below, above = sides(late, late_sib)
+    v = [both_halves(below(...)), u2[0], u2[1], u2[2], u2[3], both_halves(above(...))]
+    v = [v[m] + e2[64 * (m // 2) : 64 * (m // 2) + 64, :] for m in range(6)]
+
+    def args(k):
         return win[k], win[4 + k], win[8 + k], win[9 + k], win[13 + k], win[17 + k]
 
-    w = [first_post(v[m + 1], v[m], v[m + 2], *args(m)) for m in range(3)]
-    out[...] = second_post(w[1], v[2], w[0], w[2], *args(1))
-
-
-def pair_kernel(a, b, out):
-    out[0] = a[...]
-    out[1] = b[...]
-
-
-def middle_post_kernel(e2, e2sib, far, msg, sib, near, f, g, w1, own, edge, send, fine, c1, v, w):
+    w = [first_post(v[m + 1], v[m], v[m + 2], *args(m)) for m in range(4)]
+    for p in range(2):
+        out[p] = second_post(w[p + 1], v[p + 2], w[p], w[p + 2], *args(p + 1))
+
+
+def middle_post_kernel(e2, far, msg, sib, near, f, g, w1, own, edge, send, fine, c1, v, w):
     n, par = lax.axis_index("narrow"), lax.rem(lax.axis_index("wide"), 2)
     odd = par == 1
     row, col = iota((40, 64), 0), iota((40, 64), 1)
     pick = (col == lax.rem(16 * n + (row + 4) // 2 + 60, 64)).astype(F32)
     lanes = copies_of_lanes(128, 128)
-    e2, e2sib, near0, near1 = e2[...], e2sib[...], far[0], far[1]
-    for k, (upper, lower) in enumerate(((e2sib, near1), (e2, near0), (near0, e2), (near1, e2sib))):
-        fine[k] = mul(mul_left(pick, jnp.where(odd, upper, lower)), lanes)
+    planes = (e2[0], e2[1], far[0], far[1])
+    for k in range(4):
+        fine[k] = mul(mul_left(pick, jnp.where(odd, planes[k], planes[(k + 2) % 4])), lanes)
     c1[0:6] = w1[0:6]
     c1[6] = near[344:384]
     ours = [msg[160 + 40 * p : 200 + 40 * p] for p in range(2)]
@@ -641,20 +653,20 @@
     send[...] = jnp.where(odd, out[0], out[2])
 
 
-def fine_post_kernel(e1, edge, other, low, high, f, c1, c2, c3, g, u2, out, v, w, scr):
-    odd = lax.rem(lax.axis_index("wide"), 2) == 1
-    below, above = jnp.where(odd, other[...], edge[...]), jnp.where(odd, edge[...], other[...])
-    x = jnp.concatenate([below, e1[0], e1[1], above], axis=0)
+def fine_post_kernel(e1, edge, other, far, sib, f, c1, c2, c3, g, u2, out, v, w, scr):
+    below, above = sides(edge, other)
+    x = jnp.concatenate([below(...), e1[0], e1[1], above(...)], axis=0)
+    below, above = sides(far, sib)
     for half in range(2):
         here = slice(128 * half, 128 * half + 128)
         row, col = iota((128, 128), 0), iota((128, 128), 1)
         fine = mul(x, (row == 64 * half + col // 2).astype(F32))
         scr[pl.ds(0, 160, stride=2), :] = fine
         scr[pl.ds(1, 160, stride=2), :] = fine
-        for k, ref in ((0, low), (7, high)):
+        for k, read in ((0, below), (7, above)):
             at = 80 * (k // 2)
-            v[k, 0:40, here] = ref[4 + half] + scr[at : at + 40, :]
-            v[k, 40:80, here] = ref[6 + half] + scr[at + 40 : at + 80, :]
+            v[k, 0:40, here] = read(4 + half) + scr[at : at + 40, :]
+            v[k, 40:80, here] = read(6 + half) + scr[at + 40 : at + 80, :]
         for k in range(1, 7):
             at = 80 * (k // 2)
             v[k, :, here] = u2[k, :, here] + scr[at : at + 80, :]
@@ -710,24 +722,24 @@
     )(*inputs)
     low, high = shift(up, "narrow", 1), shift(down, "narrow", -1)
 
-    own, coef1, up, down = call(
-        pad_kernel, [(16,) + big, (6, 40, 128), (520, 256), (600, 256)], [(160, 128)]
+    own, coef1, far, sib = call(
+        pad_kernel, [(16,) + big, (6, 40, 128), (600, 256), (600, 256)], [(2,) + big, (160, 128)]
     )(jnp.concatenate(inputs, axis=0), low, high)
-    low, high = shift(up, "wide", 1), shift(down, "wide", -1)
-
-    f, c1, c2, c3, g, u2, w1, up, down, f1 = call(
+    far, sib = across(far), sibling(sib)
+
+    f, c1, c2, c3, g, u2, w1, out_far, out_sib, _ = call(
         fine_pre_kernel,
         [(6,) + big, (7,) + big, (6,) + big, (6,) + big, (6,) + big, (8,) + big]
         + [(18, 40, 128), (8, 40, 128), (8, 40, 128), (2, 40, 128)],
         [(8,) + big, (4,) + big, (160, 128)],
-    )(own, coef1, low, high)
-    low1, high1 = shift(up, "wide", 1), shift(down, "wide", -1)
+    )(own, coef1, far, sib)
+    far1, sib1 = across(out_far), sibling(out_sib)
     (coefs,) = call(coarse_coef_kernel, [(32, 128)], [(80, 128)])(w1)
 
     six = (6, 40, 128)
     f1w, g1w, u2m, f2, up, down = call(
         middle_pre_kernel, [six, six, six, (40, 128), (56, 128), (56, 128)], [six, (40, 128)]
-    )(up, low1, high1, w1, coefs)
+    )(out_far, far1, sib1, w1, coefs)
     low, high, far = shift(up, "narrow", 1), shift(down, "narrow", -1), shift(f2, "narrow", 2)
 
     own2, msg = call(coarse_start_kernel, [(6, 64, 128), (240, 128)])(f2, low, high, far, u2m)
@@ -741,9 +753,11 @@
         coarse_pre_kernel, [(21, 64, 128), (4, 64, 128), (32, 128)], [(6, 64, 128)]
     )(own2, sib, near, other)
     (send,) = call(coarse_send_kernel, [(n3, 2, 8, 128)], [(64, 128)])(w2, u2w, tiles)
+    late = across(late)
     cores = [[k for k in range(wide) if k % 2 == c] for c in range(2)]
     parts = lax.all_to_all(send, "wide", split_axis=0, concat_axis=0, tiled=True, axis_index_groups=cores)
-    theirs, late = sibling(parts), across(late)
+    parts, late = lax.optimization_barrier((parts, late))
+    theirs, late_sib = sibling(parts), sibling(late)
 
     three, four = (n3, 8, 128), (n4, 8, 128)
     (fine2,) = call(
@@ -752,21 +766,19 @@
         [three, (n3 + 1, 8, 128), three, three, three, three, (n3 + 2, 8, 128), (n3 + 2, 8, 128), four, four]
         + [(n4 + 1, 8, 128), four, four, four, (n4 + 2, 8, 128), (n4 + 2, 8, 128), four, (32, 128)],
     )(parts, theirs)
-    (e2,) = call(coarse_post_kernel, [(64, 128)])(fine2, w2, u2w, late)
-    e2sib = sibling(e2)
-    (both,) = call(pair_kernel, [(2, 64, 128)])(e2, e2sib)
-    far = across(both)
+    (e2,) = call(coarse_post_kernel, [(2, 64, 128)])(fine2, w2, u2w, late, late_sib)
+    far = across(e2)
 
     e1, edge, send = call(
         middle_post_kernel,
         [(2, 40, 128), (40, 128), (40, 128)],
         [(4, 40, 128), (7, 40, 128), (7, 40, 128), (7, 40, 128)],
-    )(e2, e2sib, far, msg, sib, near, f1w, g1w, w1)
+    )(e2, far, msg, sib, near, f1w, g1w, w1)
     other1 = sibling(send)
 
     (out,) = call(
         fine_post_kernel, [(4, 64, 256)], [(8,) + big, (8,) + big, (320, 128)]
-    )(e1, edge, other1, low1, high1, f, c1, c2, c3, g, u2)
+    )(e1, edge, other1, far1, sib1, f, c1, c2, c3, g, u2)
     return out
 
 

time: 97.1 us -> 96.1 us (0.990)
  blocking collectives: 13.2 us -> 0 us
  waiting for transfers between devices: 26.3 us -> 30.4 us
  local copies, waits for them, and re-layouts: 0 us -> 4.06 us
  starting transfers between devices: 43.2 us -> 46.2 us
    all_to_all x1 -> x0, blocking collectives: 13.2 us -> none  [body(): lax.all_to_all(send, 'wide', split_axis=0, concat_axis=0, tiled=True, axi...]
    ppermute x9 -> x5, starting transfers between devices: 20.7 us -> 7.64 us  [shift(): return lax.ppermute(x, axis, [(i, (i + by) % count) for i in range(count)])]
    ppermute x3 -> x5, waiting for transfers between devices: 8.48 us -> 19.9 us  [across(): lax.ppermute(x, 'wide', [(i, (i + 1 if i % 2 else i - 1) % count) for i i...]
    ppermute x9 -> x5, waiting for transfers between devices: 14 us -> 4.2 us  [shift(): return lax.ppermute(x, axis, [(i, (i + by) % count) for i in range(count)])]
    ppermute x3 -> x5, starting transfers between devices: 1.74 us -> 7.48 us  [across(): lax.ppermute(x, 'wide', [(i, (i + 1 if i % 2 else i - 1) % count) for i i...]
    ppermute x5 -> x7, starting transfers between devices: 20.8 us -> 26.1 us  [sibling(): lax.ppermute(x, 'wide', [(i, i ^ 1) for i in range(lax.axis_size('wide'))])]
    all_to_all x0 -> x1, starting transfers between devices: none -> 4.99 us  [body(): lax.all_to_all(send, 'wide', split_axis=0, concat_axis=0, tiled=True, axi...]
    unnamed x0 -> x24, local copies, waits for them, and re-layouts: none -> 4.06 us
  transfers between devices with their start and end apart: 17 -> 18, of which waited for: 12 -> 13; matrix products, arithmetic and copies ran while one was open for 1% -> 1% of each run, Pallas kernels for 3% -> 3%
where the time goes in v6:
time: 96.1 us; the launch traced here: 95.8 us
  starting transfers between devices  46.2 us (48%)
  waiting for transfers between devices  30.4 us (32%)
  Pallas kernels  13.7 us (14%)
  local copies, waits for them, and re-layouts  4.06 us (4%)
  other arithmetic  1.26 us (1%)
    ppermute x7, starting transfers between devices, sibling(): lax.ppermute(x, 'wide', [(i, i ^ 1) for i in range(lax.axis_size('wide'))])  26.1 us
    ppermute x5, waiting for transfers between devices, across(): lax.ppermute(x, 'wide', [(i, (i + 1 if i % 2 else i - 1) % count) for i i...  19.9 us
    pallas_call x14, Pallas kernels, run(): pl.pallas_call(kernel, out_shape=[jax.ShapeDtypeStruct(s, F32) for s in o...  13.7 us
    ppermute x5, starting transfers between devices, shift(): return lax.ppermute(x, axis, [(i, (i + by) % count) for i in range(count)])  7.64 us
    ppermute x5, starting transfers between devices, across(): lax.ppermute(x, 'wide', [(i, (i + 1 if i % 2 else i - 1) % count) for i i...  7.48 us
    all_to_all x1, starting transfers between devices, body(): lax.all_to_all(send, 'wide', split_axis=0, concat_axis=0, tiled=True, axi...  4.99 us
    ppermute x7, waiting for transfers between devices, sibling(): lax.ppermute(x, 'wide', [(i, i ^ 1) for i in range(lax.axis_size('wide'))])  4.55 us
    ppermute x5, waiting for transfers between devices, shift(): return lax.ppermute(x, axis, [(i, (i + by) % count) for i in range(count)])  4.2 us
  transfers between devices with their start and end apart: 18, of which 13 were waited for; matrix products, arithmetic and copies ran while one was open for 1% of the time, Pallas kernels for 3%

profile of v6, /device:TPU:1, one launch (start us, length us, event | category | flops | bytes accessed | tf_op | source)
XLA Modules:
  0.0 95.8 jit_solution(16568972608912923896)
XLA Ops:
  0.0 1.6 %shard_map.46 = (f32[16,8,256]{2,1,0:T(8,128)}, f32[16,8,256]{2,1,0:T(8,128)}) custom-call(f32[4,64,256]{2,1,0:T(8,128)} %f.1, f32[4,64,256]{2,1,0:T(8,128)} %c1.1, f32[4,64,256]{2,1,0:T(8,128)} %c2.1, f32[4,64,256]{2,1,0:T(8,128)} %c3.1), custom_call_target="tpu_custom_call" | custom-call | tf_op jit(solution)/shard_map/pallas_call | solution.py:136
  1.6 2.2 %collective-permute-start = (f32[16,8,256]{2,1,0:T(8,128)}, f32[16,8,256]{2,1,0:T(8,128)S(1)}, u32[]{:S(2)}, u32[]{:S(2)}) collective-permute-start(f32[16,8,256]{2,1,0:T(8,128)} %get-tuple-element.38), channel_id=1, source_target_pairs={{0,1},{1,2},{2,3},{3,0},{4,5},{5,6},{6,7},{7,4},{8,9},{9,10},{10,1... | collective-permute-start | bytes 393224 | tf_op jit(solution)/shard_map/ppermute | solution.py:698
  3.8 1.5 %collective-permute-start.1 = (f32[16,8,256]{2,1,0:T(8,128)}, f32[16,8,256]{2,1,0:T(8,128)S(1)}, u32[]{:S(2)}, u32[]{:S(2)}) collective-permute-start(f32[16,8,256]{2,1,0:T(8,128)} %get-tuple-element.39), channel_id=1, source_target_pairs={{0,3},{1,0},{2,1},{3,2},{4,7},{5,4},{6,5},{7,6},{8,11},{9,8},{10,9... | collective-permute-start | bytes 393224 | tf_op jit(solution)/shard_map/ppermute | solution.py:698
  5.4 1.3 %pad_maximum_fusion.inner = f32[16,64,256]{2,1,0:T(8,128)S(1)} fusion(f32[4,64,256]{2,1,0:T(8,128)} %c3.1, f32[4,64,256]{2,1,0:T(8,128)} %c2.1, f32[4,64,256]{2,1,0:T(8,128)} %c1.1, f32[4,64,256]{2,1,0:T(8,128)} %f.1), kind=kLoop, calls=%fused_computation | loop fusion | flops 786432 | bytes 2097152 | tf_op jit(solution)/shard_map/concatenate | solution.py:727
  6.6 1.2 %collective-permute-done.low = f32[16,8,256]{2,1,0:T(8,128)S(1)} collective-permute-done((f32[16,8,256]{2,1,0:T(8,128)}, f32[16,8,256]{2,1,0:T(8,128)S(1)}, u32[]{:S(2)}, u32[]{:S(2)}) %collective-permute-start) | collective-permute-done | bytes 131104 | tf_op jit(solution)/shard_map/ppermute | solution.py:698
  8.4 3.7 %collective-permute-start.2 = (f32[600,256]{1,0:T(8,128)S(1)}, f32[600,256]{1,0:T(8,128)S(1)}, u32[]{:S(2)}, u32[]{:S(2)}) collective-permute-start(f32[600,256]{1,0:T(8,128)S(1)} %get-tuple-element.42), channel_id=1, source_target_pairs={{0,252},{4,8},{8,4},{12,16},{16,12},{20,24},{24,20},{28,32},{32,28... | collective-permute-start | bytes 1843208 | tf_op jit(solution)/shard_map/ppermute | solution.py:707
  12.1 5.1 %collective-permute-start.3 = (f32[600,256]{1,0:T(8,128)S(1)}, f32[600,256]{1,0:T(8,128)S(1)}, u32[]{:S(2)}, u32[]{:S(2)}) collective-permute-start(f32[600,256]{1,0:T(8,128)S(1)} %get-tuple-element.43), channel_id=1, source_target_pairs={{0,4},{4,0},{8,12},{12,8},{16,20},{20,16},{24,28},{28,24},{32,36},... | collective-permute-start | bytes 1843208 | tf_op jit(solution)/shard_map/ppermute | solution.py:702
  17.3 3.0 %collective-permute-done.2.far = f32[600,256]{1,0:T(8,128)S(1)} collective-permute-done((f32[600,256]{1,0:T(8,128)S(1)}, f32[600,256]{1,0:T(8,128)S(1)}, u32[]{:S(2)}, u32[]{:S(2)}) %collective-permute-start.2) | collective-permute-done | bytes 614432 | tf_op jit(solution)/shard_map/ppermute | solution.py:707
  20.3 3.1 %shard_map.48 = (f32[6,80,256]{2,1,0:T(8,128)S(1)}, f32[7,80,256]{2,1,0:T(8,128)S(1)}, f32[6,80,256]{2,1,0:T(8,128)S(1)}, f32[6,80,256]{2,1,0:T(8,128)S(1)}, f32...) custom-call(f32[16,80,256]{2,1,0:T(8,128)S(1)} %get-tuple-element.40, ...), custom_call_target="tpu_custom_call" | custom-call | tf_op jit(solution)/shard_map/pallas_call | solution.py:136
  24.9 4.8 %collective-permute-start.5 = (f32[8,40,128]{2,1,0:T(8,128)S(1)}, f32[8,40,128]{2,1,0:T(8,128)S(1)}, u32[]{:S(2)}, u32[]{:S(2)}) collective-permute-start(f32[8,40,128]{2,1,0:T(8,128)S(1)} %get-tuple-element.45), channel_id=1, source_target_pairs={{0,4},{4,0},{8,12},{12,8},{16,20},{20,16},{24,28},{28,24},{32,36},... | collective-permute-start | bytes 491528 | tf_op jit(solution)/shard_map/ppermute | solution.py:702
  30.8 3.7 %collective-permute-done.4.far = f32[8,40,128]{2,1,0:T(8,128)S(1)} collective-permute-done((f32[8,40,128]{2,1,0:T(8,128)S(1)}, f32[8,40,128]{2,1,0:T(8,128)S(1)}, u32[]{:S(2)}, u32[]{:S(2)}) %collective-permute-start.4) | collective-permute-done | bytes 163872 | tf_op jit(solution)/shard_map/ppermute | solution.py:707
  35.5 1.0 %collective-permute-start.6 = (f32[56,128]{1,0:T(8,128)S(1)}, f32[56,128]{1,0:T(8,128)S(1)}, u32[]{:S(2)}, u32[]{:S(2)}) collective-permute-start(f32[56,128]{1,0:T(8,128)S(1)} %get-tuple-element.48), channel_id=1, source_target_pairs={{0,1},{1,2},{2,3},{3,0},{4,5},{5,6},{6,7},{7,4},{8,9},{9,10},{10,1... | collective-permute-start | bytes 86024 | tf_op jit(solution)/shard_map/ppermute | solution.py:698
  36.5 1.7 %collective-permute-start.7 = (f32[56,128]{1,0:T(8,128)S(1)}, f32[56,128]{1,0:T(8,128)S(1)}, u32[]{:S(2)}, u32[]{:S(2)}) collective-permute-start(f32[56,128]{1,0:T(8,128)S(1)} %get-tuple-element.49), channel_id=1, source_target_pairs={{0,3},{1,0},{2,1},{3,2},{4,7},{5,4},{6,5},{7,6},{8,11},{9,8},{10,9... | collective-permute-start | bytes 86024 | tf_op jit(solution)/shard_map/ppermute | solution.py:698
  38.2 1.2 %collective-permute-start.8 = (f32[40,128]{1,0:T(8,128)S(1)}, f32[40,128]{1,0:T(8,128)S(1)}, u32[]{:S(2)}, u32[]{:S(2)}) collective-permute-start(f32[40,128]{1,0:T(8,128)S(1)} %get-tuple-element.47.f2), channel_id=1, source_target_pairs={{0,2},{1,3},{2,0},{3,1},{4,6},{5,7},{6,4},{7,5},{8,10},{9,11},{10,... | collective-permute-start | bytes 61448 | tf_op jit(solution)/shard_map/ppermute | solution.py:698
  39.4 3.0 %collective-permute-done.8.far = f32[40,128]{1,0:T(8,128)S(1)} collective-permute-done((f32[40,128]{1,0:T(8,128)S(1)}, f32[40,128]{1,0:T(8,128)S(1)}, u32[]{:S(2)}, u32[]{:S(2)}) %collective-permute-start.8) | collective-permute-done | bytes 20512 | tf_op jit(solution)/shard_map/ppermute | solution.py:698
  42.6 5.1 %collective-permute-start.9 = (f32[240,128]{1,0:T(8,128)S(1)}, f32[240,128]{1,0:T(8,128)S(1)}, u32[]{:S(2)}, u32[]{:S(2)}) collective-permute-start(f32[240,128]{1,0:T(8,128)S(1)} %get-tuple-element.52.msg), channel_id=1, source_target_pairs={{0,4},{4,0},{8,12},{12,8},{16,20},{20,16},{24,28},{28,24},{32,36},... | collective-permute-start | bytes 368648 | tf_op jit(solution)/shard_map/ppermute | solution.py:702
  47.7 1.0 %collective-permute-done.9.sib = f32[240,128]{1,0:T(8,128)S(1)} collective-permute-done((f32[240,128]{1,0:T(8,128)S(1)}, f32[240,128]{1,0:T(8,128)S(1)}, u32[]{:S(2)}, u32[]{:S(2)}) %collective-permute-start.9) | collective-permute-done | bytes 122912 | tf_op jit(solution)/shard_map/ppermute | solution.py:702
  49.1 4.8 %collective-permute-done.10.near = f32[384,128]{1,0:T(8,128)S(1)} collective-permute-done((f32[384,128]{1,0:T(8,128)S(1)}, f32[384,128]{1,0:T(8,128)S(1)}, u32[]{:S(2)}, u32[]{:S(2)}) %collective-permute-start.10) | collective-permute-done | bytes 196640 | tf_op jit(solution)/shard_map/ppermute | solution.py:707
  53.9 3.7 %collective-permute-start.11 = (f32[384,128]{1,0:T(8,128)S(1)}, f32[384,128]{1,0:T(8,128)S(1)}, u32[]{:S(2)}, u32[]{:S(2)}) collective-permute-start(f32[384,128]{1,0:T(8,128)S(1)} %collective-permute-done.10.near), channel_id=1, source_target_pairs={{0,4},{4,0},{8,12},{12,8},{16,20},{20,16},{24,28},{28,24},{32,36},... | collective-permute-start | bytes 589832 | tf_op jit(solution)/shard_map/ppermute | solution.py:702
  57.5 1.1 %collective-permute-done.11.other = f32[384,128]{1,0:T(8,128)S(1)} collective-permute-done((f32[384,128]{1,0:T(8,128)S(1)}, f32[384,128]{1,0:T(8,128)S(1)}, u32[]{:S(2)}, u32[]{:S(2)}) %collective-permute-start.11) | collective-permute-done | bytes 196640 | tf_op jit(solution)/shard_map/ppermute | solution.py:702
  59.0 1.0 %shard_map.55 = f32[32,2,8,128]{3,2,1,0:T(8,128)} custom-call(f32[21,64,128]{2,1,0:T(8,128)S(1)} %get-tuple-element.54.w.win, f32[4,64,128]{2,1,0:T(8,128)S(1)} %get-tuple-element.55.u2, f32[3,8,128]{2,1,0:T(8,128)S(1)} %shard_map.53.tiles), custom_call_target="tpu_custom_call" | custom-call | tf_op jit(solution)/shard_map/pallas_call | solution.py:136
  60.0 5.0 %all-to-all-start = ((f32[32,2,8,128]{3,2,1,0:T(8,128)}), f32[32,2,8,128]{3,2,1,0:T(8,128)S(1)}, u32[]{:S(2)}, u32[]{:S(2)}) async-start(f32[32,2,8,128]{3,2,1,0:T(8,128)} %shard_map.55), calls=%async_computation | async-start | bytes 524288 | tf_op jit(solution)/shard_map/all_to_all | solution.py:758
  65.0 1.9 %collective-permute-start.12 = (f32[32,128]{1,0:T(8,128)S(1)}, f32[32,128]{1,0:T(8,128)S(1)}, u32[]{:S(2)}, u32[]{:S(2)}) collective-permute-start(f32[32,128]{1,0:T(8,128)S(1)} %get-tuple-element.57), channel_id=1, source_target_pairs={{0,252},{4,8},{8,4},{12,16},{16,12},{20,24},{24,20},{28,32},{32,28... | collective-permute-start | bytes 49160 | tf_op jit(solution)/shard_map/ppermute | solution.py:707
  66.9 6.4 %collective-permute-done.12.late = f32[32,128]{1,0:T(8,128)S(1)} collective-permute-done((f32[32,128]{1,0:T(8,128)S(1)}, f32[32,128]{1,0:T(8,128)S(1)}, u32[]{:S(2)}, u32[]{:S(2)}) %collective-permute-start.12) | collective-permute-done | bytes 16416 | tf_op jit(solution)/shard_map/ppermute | solution.py:707
  73.3 1.7 %all-to-all-done.mine = f32[32,2,8,128]{3,2,1,0:T(8,128)S(1)} async-done(((f32[32,2,8,128]{3,2,1,0:T(8,128)}), f32[32,2,8,128]{3,2,1,0:T(8,128)S(1)}, u32[]{:S(2)}, u32[]{:S(2)}) %all-to-all-start) | async-done | bytes 262176 | tf_op jit(solution)/shard_map/all_to_all | solution.py:758
  75.1 3.3 %collective-permute-start.13 = (f32[32,2,8,128]{3,2,1,0:T(8,128)S(1)}, f32[32,2,8,128]{3,2,1,0:T(8,128)S(1)}, u32[]{:S(2)}, u32[]{:S(2)}) collective-permute-start(f32[32,2,8,128]{3,2,1,0:T(8,128)S(1)} %all-to-all-done.mine), channel_id=1, source_target_pairs={{0,4},{4,0},{8,12},{12,8},{16,20},{20,16},{24,28},{28,24},{32,36},... | collective-permute-start | bytes 786440 | tf_op jit(solution)/shard_map/ppermute | solution.py:702
  79.5 2.8 %shard_map.56.e2 = f32[192,128]{1,0:T(8,128)S(1)} custom-call(f32[32,2,8,128]{3,2,1,0:T(8,128)S(1)} %all-to-all-done.mine, f32[32,2,8,128]{3,2,1,0:T(8,128)S(1)} %collective-permute-done.13.theirs), custom_call_target="tpu_custom_call" | custom-call | tf_op jit(solution)/shard_map/pallas_call | solution.py:136
  82.6 1.8 %collective-permute-start.15 = (f32[2,64,128]{2,1,0:T(8,128)S(1)}, f32[2,64,128]{2,1,0:T(8,128)S(1)}, u32[]{:S(2)}, u32[]{:S(2)}) collective-permute-start(f32[2,64,128]{2,1,0:T(8,128)S(1)} %shard_map.57.e2), channel_id=1, source_target_pairs={{0,252},{4,8},{8,4},{12,16},{16,12},{20,24},{24,20},{28,32},{32,28... | collective-permute-start | bytes 196616 | tf_op jit(solution)/shard_map/ppermute | solution.py:707
  84.4 2.0 %collective-permute-done.15.far = f32[2,64,128]{2,1,0:T(8,128)S(1)} collective-permute-done((f32[2,64,128]{2,1,0:T(8,128)S(1)}, f32[2,64,128]{2,1,0:T(8,128)S(1)}, u32[]{:S(2)}, u32[]{:S(2)}) %collective-permute-start.15) | collective-permute-done | bytes 65568 | tf_op jit(solution)/shard_map/ppermute | solution.py:707
  86.4 0.9 copy-done.9
  88.9 3.8 %collective-permute-start.16 = (f32[40,128]{1,0:T(8,128)S(1)}, f32[40,128]{1,0:T(8,128)S(1)}, u32[]{:S(2)}, u32[]{:S(2)}) collective-permute-start(f32[40,128]{1,0:T(8,128)S(1)} %get-tuple-element.64), channel_id=1, source_target_pairs={{0,4},{4,0},{8,12},{12,8},{16,20},{20,16},{24,28},{28,24},{32,36},... | collective-permute-start | bytes 61448 | tf_op jit(solution)/shard_map/ppermute | solution.py:702
  93.5 2.3 %shard_map.59 = f32[4,64,256]{2,1,0:T(8,128)} custom-call(f32[2,40,128]{2,1,0:T(8,128)S(1)} %get-tuple-element.62.e1, f32[40,128]{1,0:T(8,128)S(1)} %get-tuple-element.63.edge, f32[40,128]{1,0:T(8,128)S(1)} %collective-permute-done.16.other, f32[8,40,128]{2,1,0:T(8,128)S(1)} %collective-permute-done.4.far, f32[8,40,128]{2,1,0:T(8,128)S(1)} %collective-permute-done.5.sib, ...), custom_call_target="tpu_custom_call" | custom-call | tf_op jit(solution)/shard_map/pallas_call | solution.py:136
  (43 shorter events, 9.0 us)
Async XLA Ops:
  1.6 6.2 %collective-permute-start = (f32[16,8,256]{2,1,0:T(8,128)}, f32[16,8,256]{2,1,0:T(8,128)S(1)}, u32[]{:S(2)}, u32[]{:S(2)}) collective-permute-start(f32[16,8,256]{2,1,0:T(8,128)} %get-tuple-element.38), channel_id=1, source_target_pairs={{0,1},{1,2},{2,3},{3,0},{4,5},{5,6},{6,7},{7,4},{8,9},{9,10},{10,1... | collective-permute-start | bytes 393224 | tf_op jit(solution)/shard_map/ppermute | solution.py:698
  3.8 4.0 %collective-permute-start.1 = (f32[16,8,256]{2,1,0:T(8,128)}, f32[16,8,256]{2,1,0:T(8,128)S(1)}, u32[]{:S(2)}, u32[]{:S(2)}) collective-permute-start(f32[16,8,256]{2,1,0:T(8,128)} %get-tuple-element.39), channel_id=1, source_target_pairs={{0,3},{1,0},{2,1},{3,2},{4,7},{5,4},{6,5},{7,6},{8,11},{9,8},{10,9... | collective-permute-start | bytes 393224 | tf_op jit(solution)/shard_map/ppermute | solution.py:698
  8.4 11.8 %collective-permute-start.2 = (f32[600,256]{1,0:T(8,128)S(1)}, f32[600,256]{1,0:T(8,128)S(1)}, u32[]{:S(2)}, u32[]{:S(2)}) collective-permute-start(f32[600,256]{1,0:T(8,128)S(1)} %get-tuple-element.42), channel_id=1, source_target_pairs={{0,252},{4,8},{8,4},{12,16},{16,12},{20,24},{24,20},{28,32},{32,28... | collective-permute-start | bytes 1843208 | tf_op jit(solution)/shard_map/ppermute | solution.py:707
  12.1 8.1 %collective-permute-start.3 = (f32[600,256]{1,0:T(8,128)S(1)}, f32[600,256]{1,0:T(8,128)S(1)}, u32[]{:S(2)}, u32[]{:S(2)}) collective-permute-start(f32[600,256]{1,0:T(8,128)S(1)} %get-tuple-element.43), channel_id=1, source_target_pairs={{0,4},{4,0},{8,12},{12,8},{16,20},{20,16},{24,28},{28,24},{32,36},... | collective-permute-start | bytes 1843208 | tf_op jit(solution)/shard_map/ppermute | solution.py:702
  23.3 0.8 copy-start
  24.1 0.8 copy-start.2
  24.9 17.5 %copy-start.6 = (f32[6,80,256]{2,1,0:T(8,128)}, f32[6,80,256]{2,1,0:T(8,128)S(1)}, u32[]{:S(2)}) copy-start(f32[6,80,256]{2,1,0:T(8,128)S(1)} %get-tuple-element.69.g) | copy-start | bytes 1474564
  24.9 24.1 %copy-start.4 = (f32[6,80,256]{2,1,0:T(8,128)}, f32[6,80,256]{2,1,0:T(8,128)S(1)}, u32[]{:S(2)}) copy-start(f32[6,80,256]{2,1,0:T(8,128)S(1)} %get-tuple-element.68.c3) | copy-start | bytes 1474564
  24.9 5.9 %collective-permute-start.5 = (f32[8,40,128]{2,1,0:T(8,128)S(1)}, f32[8,40,128]{2,1,0:T(8,128)S(1)}, u32[]{:S(2)}, u32[]{:S(2)}) collective-permute-start(f32[8,40,128]{2,1,0:T(8,128)S(1)} %get-tuple-element.45), channel_id=1, source_target_pairs={{0,4},{4,0},{8,12},{12,8},{16,20},{20,16},{24,28},{28,24},{32,36},... | collective-permute-start | bytes 491528 | tf_op jit(solution)/shard_map/ppermute | solution.py:702
  29.8 4.7 %collective-permute-start.4 = (f32[8,40,128]{2,1,0:T(8,128)S(1)}, f32[8,40,128]{2,1,0:T(8,128)S(1)}, u32[]{:S(2)}, u32[]{:S(2)}) collective-permute-start(f32[8,40,128]{2,1,0:T(8,128)S(1)} %get-tuple-element.44.own), channel_id=1, source_target_pairs={{0,252},{4,8},{8,4},{12,16},{16,12},{20,24},{24,20},{28,32},{32,28... | collective-permute-start | bytes 491528 | tf_op jit(solution)/shard_map/ppermute | solution.py:707
  34.9 0.6 copy-start.10
  35.5 23.5 %copy-start.8 = (f32[6,40,128]{2,1,0:T(8,128)}, f32[6,40,128]{2,1,0:T(8,128)S(1)}, u32[]{:S(2)}) copy-start(f32[6,40,128]{2,1,0:T(8,128)S(1)} %get-tuple-element.60.f) | copy-start | bytes 368644
  35.5 6.9 %collective-permute-start.6 = (f32[56,128]{1,0:T(8,128)S(1)}, f32[56,128]{1,0:T(8,128)S(1)}, u32[]{:S(2)}, u32[]{:S(2)}) collective-permute-start(f32[56,128]{1,0:T(8,128)S(1)} %get-tuple-element.48), channel_id=1, source_target_pairs={{0,1},{1,2},{2,3},{3,0},{4,5},{5,6},{6,7},{7,4},{8,9},{9,10},{10,1... | collective-permute-start | bytes 86024 | tf_op jit(solution)/shard_map/ppermute | solution.py:698
  36.5 5.9 %collective-permute-start.7 = (f32[56,128]{1,0:T(8,128)S(1)}, f32[56,128]{1,0:T(8,128)S(1)}, u32[]{:S(2)}, u32[]{:S(2)}) collective-permute-start(f32[56,128]{1,0:T(8,128)S(1)} %get-tuple-element.49), channel_id=1, source_target_pairs={{0,3},{1,0},{2,1},{3,2},{4,7},{5,4},{6,5},{7,6},{8,11},{9,8},{10,9... | collective-permute-start | bytes 86024 | tf_op jit(solution)/shard_map/ppermute | solution.py:698
  38.2 4.1 %collective-permute-start.8 = (f32[40,128]{1,0:T(8,128)S(1)}, f32[40,128]{1,0:T(8,128)S(1)}, u32[]{:S(2)}, u32[]{:S(2)}) collective-permute-start(f32[40,128]{1,0:T(8,128)S(1)} %get-tuple-element.47.f2), channel_id=1, source_target_pairs={{0,2},{1,3},{2,0},{3,1},{4,6},{5,7},{6,4},{7,5},{8,10},{9,11},{10,... | collective-permute-start | bytes 61448 | tf_op jit(solution)/shard_map/ppermute | solution.py:698
  42.6 6.0 %collective-permute-start.9 = (f32[240,128]{1,0:T(8,128)S(1)}, f32[240,128]{1,0:T(8,128)S(1)}, u32[]{:S(2)}, u32[]{:S(2)}) collective-permute-start(f32[240,128]{1,0:T(8,128)S(1)} %get-tuple-element.52.msg), channel_id=1, source_target_pairs={{0,4},{4,0},{8,12},{12,8},{16,20},{20,16},{24,28},{28,24},{32,36},... | collective-permute-start | bytes 368648 | tf_op jit(solution)/shard_map/ppermute | solution.py:702
  48.7 5.2 %collective-permute-start.10 = (f32[384,128]{1,0:T(8,128)S(1)}, f32[384,128]{1,0:T(8,128)S(1)}, u32[]{:S(2)}, u32[]{:S(2)}) collective-permute-start(f32[384,128]{1,0:T(8,128)S(1)} %shard_map.52), channel_id=1, source_target_pairs={{0,252},{4,8},{8,4},{12,16},{16,12},{20,24},{24,20},{28,32},{32,28... | collective-permute-start | bytes 589832 | tf_op jit(solution)/shard_map/ppermute | solution.py:707
  53.9 4.8 %collective-permute-start.11 = (f32[384,128]{1,0:T(8,128)S(1)}, f32[384,128]{1,0:T(8,128)S(1)}, u32[]{:S(2)}, u32[]{:S(2)}) collective-permute-start(f32[384,128]{1,0:T(8,128)S(1)} %collective-permute-done.10.near), channel_id=1, source_target_pairs={{0,4},{4,0},{8,12},{12,8},{16,20},{20,16},{24,28},{28,24},{32,36},... | collective-permute-start | bytes 589832 | tf_op jit(solution)/shard_map/ppermute | solution.py:702
  60.0 15.1 %all-to-all-start = ((f32[32,2,8,128]{3,2,1,0:T(8,128)}), f32[32,2,8,128]{3,2,1,0:T(8,128)S(1)}, u32[]{:S(2)}, u32[]{:S(2)}) async-start(f32[32,2,8,128]{3,2,1,0:T(8,128)} %shard_map.55), calls=%async_computation | async-start | bytes 524288 | tf_op jit(solution)/shard_map/all_to_all | solution.py:758
  65.0 8.4 %collective-permute-start.12 = (f32[32,128]{1,0:T(8,128)S(1)}, f32[32,128]{1,0:T(8,128)S(1)}, u32[]{:S(2)}, u32[]{:S(2)}) collective-permute-start(f32[32,128]{1,0:T(8,128)S(1)} %get-tuple-element.57), channel_id=1, source_target_pairs={{0,252},{4,8},{8,4},{12,16},{16,12},{20,24},{24,20},{28,32},{32,28... | collective-permute-start | bytes 49160 | tf_op jit(solution)/shard_map/ppermute | solution.py:707
  75.1 18.5 %copy-start.1 = (f32[6,80,256]{2,1,0:T(8,128)S(1)}, f32[6,80,256]{2,1,0:T(8,128)}, u32[]{:S(2)}) copy-start(f32[6,80,256]{2,1,0:T(8,128)} %copy-done) | copy-start | bytes 1474564
  75.1 18.5 %copy-start.3 = (f32[6,80,256]{2,1,0:T(8,128)S(1)}, f32[6,80,256]{2,1,0:T(8,128)}, u32[]{:S(2)}) copy-start(f32[6,80,256]{2,1,0:T(8,128)} %copy-done.2) | copy-start | bytes 1474564
  75.1 18.5 %copy-start.5 = (f32[6,80,256]{2,1,0:T(8,128)S(1)}, f32[6,80,256]{2,1,0:T(8,128)}, u32[]{:S(2)}) copy-start(f32[6,80,256]{2,1,0:T(8,128)} %copy-done.4) | copy-start | bytes 1474564
  75.1 18.5 %copy-start.7 = (f32[6,80,256]{2,1,0:T(8,128)S(1)}, f32[6,80,256]{2,1,0:T(8,128)}, u32[]{:S(2)}) copy-start(f32[6,80,256]{2,1,0:T(8,128)} %copy-done.6) | copy-start | bytes 1474564
  75.1 4.5 %collective-permute-start.13 = (f32[32,2,8,128]{3,2,1,0:T(8,128)S(1)}, f32[32,2,8,128]{3,2,1,0:T(8,128)S(1)}, u32[]{:S(2)}, u32[]{:S(2)}) collective-permute-start(f32[32,2,8,128]{3,2,1,0:T(8,128)S(1)} %all-to-all-done.mine), channel_id=1, source_target_pairs={{0,4},{4,0},{8,12},{12,8},{16,20},{20,16},{24,28},{28,24},{32,36},... | collective-permute-start | bytes 786440 | tf_op jit(solution)/shard_map/ppermute | solution.py:702
  78.4 4.0 %collective-permute-start.14 = (f32[32,128]{1,0:T(8,128)S(1)}, f32[32,128]{1,0:T(8,128)S(1)}, u32[]{:S(2)}, u32[]{:S(2)}) collective-permute-start(f32[32,128]{1,0:T(8,128)S(1)} %collective-permute-done.12.late), channel_id=1, source_target_pairs={{0,4},{4,0},{8,12},{12,8},{16,20},{20,16},{24,28},{28,24},{32,36},... | collective-permute-start | bytes 49160 | tf_op jit(solution)/shard_map/ppermute | solution.py:702
  82.6 3.8 %collective-permute-start.15 = (f32[2,64,128]{2,1,0:T(8,128)S(1)}, f32[2,64,128]{2,1,0:T(8,128)S(1)}, u32[]{:S(2)}, u32[]{:S(2)}) collective-permute-start(f32[2,64,128]{2,1,0:T(8,128)S(1)} %shard_map.57.e2), channel_id=1, source_target_pairs={{0,252},{4,8},{8,4},{12,16},{16,12},{20,24},{24,20},{28,32},{32,28... | collective-permute-start | bytes 196616 | tf_op jit(solution)/shard_map/ppermute | solution.py:707
  86.4 0.9 copy-start.9
  87.3 0.9 copy-start.11
  88.9 4.6 %collective-permute-start.16 = (f32[40,128]{1,0:T(8,128)S(1)}, f32[40,128]{1,0:T(8,128)S(1)}, u32[]{:S(2)}, u32[]{:S(2)}) collective-permute-start(f32[40,128]{1,0:T(8,128)S(1)} %get-tuple-element.64), channel_id=1, source_target_pairs={{0,4},{4,0},{8,12},{12,8},{16,20},{20,16},{24,28},{28,24},{32,36},... | collective-permute-start | bytes 61448 | tf_op jit(solution)/shard_map/ppermute | solution.py:702

commit v7 on v6

--- a/solution.py
+++ b/solution.py
@@ -756,7 +756,6 @@
     late = across(late)
     cores = [[k for k in range(wide) if k % 2 == c] for c in range(2)]
     parts = lax.all_to_all(send, "wide", split_axis=0, concat_axis=0, tiled=True, axis_index_groups=cores)
-    parts, late = lax.optimization_barrier((parts, late))
     theirs, late_sib = sibling(parts), sibling(late)
 
     three, four = (n3, 8, 128), (n4, 8, 128)

time: 96.1 us -> 95.7 us (level)
  blocking collectives: 0 us -> 14.9 us
  waiting for transfers between devices: 30.4 us -> 24.8 us
  starting transfers between devices: 46.2 us -> 41.5 us
  local copies, waits for them, and re-layouts: 4.06 us -> 0 us
    all_to_all x0 -> x1, blocking collectives: none -> 14.9 us  [body(): lax.all_to_all(send, 'wide', split_axis=0, concat_axis=0, tiled=True, axi...]
    all_to_all x1 -> x0, starting transfers between devices: 4.99 us -> none  [body(): lax.all_to_all(send, 'wide', split_axis=0, concat_axis=0, tiled=True, axi...]
    unnamed x24 -> x0, local copies, waits for them, and re-layouts: 4.06 us -> none
    ppermute x5, waiting for transfers between devices: 19.9 us -> 16.8 us  [across(): lax.ppermute(x, 'wide', [(i, (i + 1 if i % 2 else i - 1) % count) for i i...]
    ppermute x7, starting transfers between devices: 26.1 us -> 28.4 us  [sibling(): lax.ppermute(x, 'wide', [(i, i ^ 1) for i in range(lax.axis_size('wide'))])]
    ppermute x5, starting transfers between devices: 7.48 us -> 5.42 us  [across(): lax.ppermute(x, 'wide', [(i, (i + 1 if i % 2 else i - 1) % count) for i i...]
    all_to_all x1 -> x0, waiting for transfers between devices: 1.74 us -> none  [body(): lax.all_to_all(send, 'wide', split_axis=0, concat_axis=0, tiled=True, axi...]
  transfers between devices with their start and end apart: 18 -> 17, of which waited for: 13 -> 11; matrix products, arithmetic and copies ran while one was open for 1% -> 1% of each run, Pallas kernels for 3% -> 3%
where the time goes in v7:
time: 95.7 us; the launch traced here: 95.5 us
  starting transfers between devices  41.5 us (43%)
  waiting for transfers between devices  24.8 us (26%)
  blocking collectives  14.9 us (16%)
  Pallas kernels  12.9 us (13%)
  other arithmetic  1.26 us (1%)
    ppermute x7, starting transfers between devices, sibling(): lax.ppermute(x, 'wide', [(i, i ^ 1) for i in range(lax.axis_size('wide'))])  28.4 us
    ppermute x5, waiting for transfers between devices, across(): lax.ppermute(x, 'wide', [(i, (i + 1 if i % 2 else i - 1) % count) for i i...  16.8 us
    all_to_all x1, blocking collectives, body(): lax.all_to_all(send, 'wide', split_axis=0, concat_axis=0, tiled=True, axi...  14.9 us
    pallas_call x14, Pallas kernels, run(): pl.pallas_call(kernel, out_shape=[jax.ShapeDtypeStruct(s, F32) for s in o...  12.9 us
    ppermute x5, starting transfers between devices, shift(): return lax.ppermute(x, axis, [(i, (i + by) % count) for i in range(count)])  7.72 us
    ppermute x5, starting transfers between devices, across(): lax.ppermute(x, 'wide', [(i, (i + 1 if i % 2 else i - 1) % count) for i i...  5.42 us
    ppermute x5, waiting for transfers between devices, shift(): return lax.ppermute(x, axis, [(i, (i + by) % count) for i in range(count)])  4.28 us
    ppermute x7, waiting for transfers between devices, sibling(): lax.ppermute(x, 'wide', [(i, i ^ 1) for i in range(lax.axis_size('wide'))])  3.67 us
  transfers between devices with their start and end apart: 17, of which 11 were waited for; matrix products, arithmetic and copies ran while one was open for 1% of the time, Pallas kernels for 3%

profile of v7, /device:TPU:1, one launch (start us, length us, event | category | flops | bytes accessed | tf_op | source)
XLA Modules:
  0.0 95.5 jit_solution(3872673398871432610)
XLA Ops:
  0.0 1.6 %shard_map.46 = (f32[16,8,256]{2,1,0:T(8,128)}, f32[16,8,256]{2,1,0:T(8,128)}) custom-call(f32[4,64,256]{2,1,0:T(8,128)} %f.1, f32[4,64,256]{2,1,0:T(8,128)} %c1.1, f32[4,64,256]{2,1,0:T(8,128)} %c2.1, f32[4,64,256]{2,1,0:T(8,128)} %c3.1), custom_call_target="tpu_custom_call" | custom-call | tf_op jit(solution)/shard_map/pallas_call | solution.py:136
  1.6 2.2 %collective-permute-start = (f32[16,8,256]{2,1,0:T(8,128)}, f32[16,8,256]{2,1,0:T(8,128)S(1)}, u32[]{:S(2)}, u32[]{:S(2)}) collective-permute-start(f32[16,8,256]{2,1,0:T(8,128)} %get-tuple-element.36), channel_id=1, source_target_pairs={{0,1},{1,2},{2,3},{3,0},{4,5},{5,6},{6,7},{7,4},{8,9},{9,10},{10,1... | collective-permute-start | bytes 393224 | tf_op jit(solution)/shard_map/ppermute | solution.py:698
  3.8 1.5 %collective-permute-start.1 = (f32[16,8,256]{2,1,0:T(8,128)}, f32[16,8,256]{2,1,0:T(8,128)S(1)}, u32[]{:S(2)}, u32[]{:S(2)}) collective-permute-start(f32[16,8,256]{2,1,0:T(8,128)} %get-tuple-element.37), channel_id=1, source_target_pairs={{0,3},{1,0},{2,1},{3,2},{4,7},{5,4},{6,5},{7,6},{8,11},{9,8},{10,9... | collective-permute-start | bytes 393224 | tf_op jit(solution)/shard_map/ppermute | solution.py:698
  5.4 1.3 %pad_maximum_fusion.inner = f32[16,64,256]{2,1,0:T(8,128)S(1)} fusion(f32[4,64,256]{2,1,0:T(8,128)} %c3.1, f32[4,64,256]{2,1,0:T(8,128)} %c2.1, f32[4,64,256]{2,1,0:T(8,128)} %c1.1, f32[4,64,256]{2,1,0:T(8,128)} %f.1), kind=kLoop, calls=%fused_computation | loop fusion | flops 786432 | bytes 2097152 | tf_op jit(solution)/shard_map/concatenate | solution.py:727
  6.6 1.2 %collective-permute-done.low = f32[16,8,256]{2,1,0:T(8,128)S(1)} collective-permute-done((f32[16,8,256]{2,1,0:T(8,128)}, f32[16,8,256]{2,1,0:T(8,128)S(1)}, u32[]{:S(2)}, u32[]{:S(2)}) %collective-permute-start) | collective-permute-done | bytes 131104 | tf_op jit(solution)/shard_map/ppermute | solution.py:698
  8.4 3.7 %collective-permute-start.2 = (f32[600,256]{1,0:T(8,128)S(1)}, f32[600,256]{1,0:T(8,128)S(1)}, u32[]{:S(2)}, u32[]{:S(2)}) collective-permute-start(f32[600,256]{1,0:T(8,128)S(1)} %get-tuple-element.40), channel_id=1, source_target_pairs={{0,252},{4,8},{8,4},{12,16},{16,12},{20,24},{24,20},{28,32},{32,28... | collective-permute-start | bytes 1843208 | tf_op jit(solution)/shard_map/ppermute | solution.py:707
  12.1 5.1 %collective-permute-start.3 = (f32[600,256]{1,0:T(8,128)S(1)}, f32[600,256]{1,0:T(8,128)S(1)}, u32[]{:S(2)}, u32[]{:S(2)}) collective-permute-start(f32[600,256]{1,0:T(8,128)S(1)} %get-tuple-element.41), channel_id=1, source_target_pairs={{0,4},{4,0},{8,12},{12,8},{16,20},{20,16},{24,28},{28,24},{32,36},... | collective-permute-start | bytes 1843208 | tf_op jit(solution)/shard_map/ppermute | solution.py:702
  17.3 3.0 %collective-permute-done.2.far = f32[600,256]{1,0:T(8,128)S(1)} collective-permute-done((f32[600,256]{1,0:T(8,128)S(1)}, f32[600,256]{1,0:T(8,128)S(1)}, u32[]{:S(2)}, u32[]{:S(2)}) %collective-permute-start.2) | collective-permute-done | bytes 614432 | tf_op jit(solution)/shard_map/ppermute | solution.py:707
  20.3 3.1 %shard_map.48 = (f32[6,80,256]{2,1,0:T(8,128)S(1)}, f32[7,80,256]{2,1,0:T(8,128)S(1)}, f32[6,80,256]{2,1,0:T(8,128)S(1)}, f32[6,80,256]{2,1,0:T(8,128)S(1)}, f32...) custom-call(f32[16,80,256]{2,1,0:T(8,128)S(1)} %get-tuple-element.38, ...), custom_call_target="tpu_custom_call" | custom-call | tf_op jit(solution)/shard_map/pallas_call | solution.py:136
  23.3 4.8 %collective-permute-start.5 = (f32[8,40,128]{2,1,0:T(8,128)S(1)}, f32[8,40,128]{2,1,0:T(8,128)S(1)}, u32[]{:S(2)}, u32[]{:S(2)}) collective-permute-start(f32[8,40,128]{2,1,0:T(8,128)S(1)} %get-tuple-element.43), channel_id=1, source_target_pairs={{0,4},{4,0},{8,12},{12,8},{16,20},{20,16},{24,28},{28,24},{32,36},... | collective-permute-start | bytes 491528 | tf_op jit(solution)/shard_map/ppermute | solution.py:702
  28.4 0.8 collective-permute-done.5.sib
  29.2 3.7 %collective-permute-done.4.far = f32[8,40,128]{2,1,0:T(8,128)S(1)} collective-permute-done((f32[8,40,128]{2,1,0:T(8,128)S(1)}, f32[8,40,128]{2,1,0:T(8,128)S(1)}, u32[]{:S(2)}, u32[]{:S(2)}) %collective-permute-start.4) | collective-permute-done | bytes 163872 | tf_op jit(solution)/shard_map/ppermute | solution.py:707
  33.2 1.1 %collective-permute-start.6 = (f32[56,128]{1,0:T(8,128)S(1)}, f32[56,128]{1,0:T(8,128)S(1)}, u32[]{:S(2)}, u32[]{:S(2)}) collective-permute-start(f32[56,128]{1,0:T(8,128)S(1)} %get-tuple-element.46), channel_id=1, source_target_pairs={{0,1},{1,2},{2,3},{3,0},{4,5},{5,6},{6,7},{7,4},{8,9},{9,10},{10,1... | collective-permute-start | bytes 86024 | tf_op jit(solution)/shard_map/ppermute | solution.py:698
  34.3 1.8 %collective-permute-start.7 = (f32[56,128]{1,0:T(8,128)S(1)}, f32[56,128]{1,0:T(8,128)S(1)}, u32[]{:S(2)}, u32[]{:S(2)}) collective-permute-start(f32[56,128]{1,0:T(8,128)S(1)} %get-tuple-element.47), channel_id=1, source_target_pairs={{0,3},{1,0},{2,1},{3,2},{4,7},{5,4},{6,5},{7,6},{8,11},{9,8},{10,9... | collective-permute-start | bytes 86024 | tf_op jit(solution)/shard_map/ppermute | solution.py:698
  36.1 1.1 %collective-permute-start.8 = (f32[40,128]{1,0:T(8,128)S(1)}, f32[40,128]{1,0:T(8,128)S(1)}, u32[]{:S(2)}, u32[]{:S(2)}) collective-permute-start(f32[40,128]{1,0:T(8,128)S(1)} %get-tuple-element.45.f2), channel_id=1, source_target_pairs={{0,2},{1,3},{2,0},{3,1},{4,6},{5,7},{6,4},{7,5},{8,10},{9,11},{10,... | collective-permute-start | bytes 61448 | tf_op jit(solution)/shard_map/ppermute | solution.py:698
  37.2 3.0 %collective-permute-done.8.far = f32[40,128]{1,0:T(8,128)S(1)} collective-permute-done((f32[40,128]{1,0:T(8,128)S(1)}, f32[40,128]{1,0:T(8,128)S(1)}, u32[]{:S(2)}, u32[]{:S(2)}) %collective-permute-start.8) | collective-permute-done | bytes 20512 | tf_op jit(solution)/shard_map/ppermute | solution.py:698
  40.5 5.0 %collective-permute-start.9 = (f32[240,128]{1,0:T(8,128)S(1)}, f32[240,128]{1,0:T(8,128)S(1)}, u32[]{:S(2)}, u32[]{:S(2)}) collective-permute-start(f32[240,128]{1,0:T(8,128)S(1)} %get-tuple-element.50.msg), channel_id=1, source_target_pairs={{0,4},{4,0},{8,12},{12,8},{16,20},{20,16},{24,28},{28,24},{32,36},... | collective-permute-start | bytes 368648 | tf_op jit(solution)/shard_map/ppermute | solution.py:702
  45.5 1.0 %collective-permute-done.9.sib = f32[240,128]{1,0:T(8,128)S(1)} collective-permute-done((f32[240,128]{1,0:T(8,128)S(1)}, f32[240,128]{1,0:T(8,128)S(1)}, u32[]{:S(2)}, u32[]{:S(2)}) %collective-permute-start.9) | collective-permute-done | bytes 122912 | tf_op jit(solution)/shard_map/ppermute | solution.py:702
  46.9 4.8 %collective-permute-done.10.near = f32[384,128]{1,0:T(8,128)S(1)} collective-permute-done((f32[384,128]{1,0:T(8,128)S(1)}, f32[384,128]{1,0:T(8,128)S(1)}, u32[]{:S(2)}, u32[]{:S(2)}) %collective-permute-start.10) | collective-permute-done | bytes 196640 | tf_op jit(solution)/shard_map/ppermute | solution.py:707
  51.7 3.7 %collective-permute-start.11 = (f32[384,128]{1,0:T(8,128)S(1)}, f32[384,128]{1,0:T(8,128)S(1)}, u32[]{:S(2)}, u32[]{:S(2)}) collective-permute-start(f32[384,128]{1,0:T(8,128)S(1)} %collective-permute-done.10.near), channel_id=1, source_target_pairs={{0,4},{4,0},{8,12},{12,8},{16,20},{20,16},{24,28},{28,24},{32,36},... | collective-permute-start | bytes 589832 | tf_op jit(solution)/shard_map/ppermute | solution.py:702
  55.3 1.1 %collective-permute-done.11.other = f32[384,128]{1,0:T(8,128)S(1)} collective-permute-done((f32[384,128]{1,0:T(8,128)S(1)}, f32[384,128]{1,0:T(8,128)S(1)}, u32[]{:S(2)}, u32[]{:S(2)}) %collective-permute-start.11) | collective-permute-done | bytes 196640 | tf_op jit(solution)/shard_map/ppermute | solution.py:702
  57.0 14.9 %all_to_all.5.mine = f32[32,2,8,128]{3,2,1,0:T(8,128)S(1)} all-to-all(f32[32,2,8,128]{3,2,1,0:T(8,128)S(1)} %shard_map.55), channel_id=1, replica_groups={{0,8,16,24,32,40,48,56,64,72,80,88,96,104,112,120,128,136,144,152,160,1..., dimensions={0} | all-to-all | bytes 524288 | tf_op jit(solution)/shard_map/all_to_all | solution.py:758
  71.9 3.0 %collective-permute-start.12 = (f32[32,2,8,128]{3,2,1,0:T(8,128)S(1)}, f32[32,2,8,128]{3,2,1,0:T(8,128)S(1)}, u32[]{:S(2)}, u32[]{:S(2)}) collective-permute-start(f32[32,2,8,128]{3,2,1,0:T(8,128)S(1)} %all_to_all.5.mine), channel_id=1, source_target_pairs={{0,4},{4,0},{8,12},{12,8},{16,20},{20,16},{24,28},{28,24},{32,36},... | collective-permute-start | bytes 786440 | tf_op jit(solution)/shard_map/ppermute | solution.py:702
  75.0 1.5 %collective-permute-start.13 = (f32[32,128]{1,0:T(8,128)S(1)}, f32[32,128]{1,0:T(8,128)S(1)}, u32[]{:S(2)}, u32[]{:S(2)}) collective-permute-start(f32[32,128]{1,0:T(8,128)S(1)} %get-tuple-element.55), channel_id=1, source_target_pairs={{0,252},{4,8},{8,4},{12,16},{16,12},{20,24},{24,20},{28,32},{32,28... | collective-permute-start | bytes 49160 | tf_op jit(solution)/shard_map/ppermute | solution.py:707
  76.5 1.6 %collective-permute-done.13.late = f32[32,128]{1,0:T(8,128)S(1)} collective-permute-done((f32[32,128]{1,0:T(8,128)S(1)}, f32[32,128]{1,0:T(8,128)S(1)}, u32[]{:S(2)}, u32[]{:S(2)}) %collective-permute-start.13) | collective-permute-done | bytes 16416 | tf_op jit(solution)/shard_map/ppermute | solution.py:707
  78.1 3.3 %collective-permute-start.14 = (f32[32,128]{1,0:T(8,128)S(1)}, f32[32,128]{1,0:T(8,128)S(1)}, u32[]{:S(2)}, u32[]{:S(2)}) collective-permute-start(f32[32,128]{1,0:T(8,128)S(1)} %collective-permute-done.13.late), channel_id=1, source_target_pairs={{0,4},{4,0},{8,12},{12,8},{16,20},{20,16},{24,28},{28,24},{32,36},... | collective-permute-start | bytes 49160 | tf_op jit(solution)/shard_map/ppermute | solution.py:702
  81.5 2.8 %shard_map.56.e2 = f32[192,128]{1,0:T(8,128)S(1)} custom-call(f32[32,2,8,128]{3,2,1,0:T(8,128)S(1)} %all_to_all.5.mine, f32[32,2,8,128]{3,2,1,0:T(8,128)S(1)} %collective-permute-done.12.theirs), custom_call_target="tpu_custom_call" | custom-call | tf_op jit(solution)/shard_map/pallas_call | solution.py:136
  84.6 3.7 %collective-permute-done.15.far = f32[2,64,128]{2,1,0:T(8,128)S(1)} collective-permute-done((f32[2,64,128]{2,1,0:T(8,128)S(1)}, f32[2,64,128]{2,1,0:T(8,128)S(1)}, u32[]{:S(2)}, u32[]{:S(2)}) %collective-permute-start.15) | collective-permute-done | bytes 65568 | tf_op jit(solution)/shard_map/ppermute | solution.py:707
  88.3 0.7 shard_map.58
  89.0 3.4 %collective-permute-start.16 = (f32[40,128]{1,0:T(8,128)S(1)}, f32[40,128]{1,0:T(8,128)S(1)}, u32[]{:S(2)}, u32[]{:S(2)}) collective-permute-start(f32[40,128]{1,0:T(8,128)S(1)} %get-tuple-element.60), channel_id=1, source_target_pairs={{0,4},{4,0},{8,12},{12,8},{16,20},{20,16},{24,28},{28,24},{32,36},... | collective-permute-start | bytes 61448 | tf_op jit(solution)/shard_map/ppermute | solution.py:702
  92.4 0.8 collective-permute-done.16.other
  93.2 2.2 %shard_map.59 = f32[4,64,256]{2,1,0:T(8,128)} custom-call(f32[2,40,128]{2,1,0:T(8,128)S(1)} %get-tuple-element.58.e1, f32[40,128]{1,0:T(8,128)S(1)} %get-tuple-element.59.edge, f32[40,128]{1,0:T(8,128)S(1)} %collective-permute-done.16.other, f32[8,40,128]{2,1,0:T(8,128)S(1)} %collective-permute-done.4.far, f32[8,40,128]{2,1,0:T(8,128)S(1)} %collective-permute-done.5.sib, ...), custom_call_target="tpu_custom_call" | custom-call | tf_op jit(solution)/shard_map/pallas_call | solution.py:136
  (18 shorter events, 2.8 us)
Async XLA Ops:
  1.6 6.2 %collective-permute-start = (f32[16,8,256]{2,1,0:T(8,128)}, f32[16,8,256]{2,1,0:T(8,128)S(1)}, u32[]{:S(2)}, u32[]{:S(2)}) collective-permute-start(f32[16,8,256]{2,1,0:T(8,128)} %get-tuple-element.36), channel_id=1, source_target_pairs={{0,1},{1,2},{2,3},{3,0},{4,5},{5,6},{6,7},{7,4},{8,9},{9,10},{10,1... | collective-permute-start | bytes 393224 | tf_op jit(solution)/shard_map/ppermute | solution.py:698
  3.8 4.0 %collective-permute-start.1 = (f32[16,8,256]{2,1,0:T(8,128)}, f32[16,8,256]{2,1,0:T(8,128)S(1)}, u32[]{:S(2)}, u32[]{:S(2)}) collective-permute-start(f32[16,8,256]{2,1,0:T(8,128)} %get-tuple-element.37), channel_id=1, source_target_pairs={{0,3},{1,0},{2,1},{3,2},{4,7},{5,4},{6,5},{7,6},{8,11},{9,8},{10,9... | collective-permute-start | bytes 393224 | tf_op jit(solution)/shard_map/ppermute | solution.py:698
  8.4 11.8 %collective-permute-start.2 = (f32[600,256]{1,0:T(8,128)S(1)}, f32[600,256]{1,0:T(8,128)S(1)}, u32[]{:S(2)}, u32[]{:S(2)}) collective-permute-start(f32[600,256]{1,0:T(8,128)S(1)} %get-tuple-element.40), channel_id=1, source_target_pairs={{0,252},{4,8},{8,4},{12,16},{16,12},{20,24},{24,20},{28,32},{32,28... | collective-permute-start | bytes 1843208 | tf_op jit(solution)/shard_map/ppermute | solution.py:707
  12.1 8.1 %collective-permute-start.3 = (f32[600,256]{1,0:T(8,128)S(1)}, f32[600,256]{1,0:T(8,128)S(1)}, u32[]{:S(2)}, u32[]{:S(2)}) collective-permute-start(f32[600,256]{1,0:T(8,128)S(1)} %get-tuple-element.41), channel_id=1, source_target_pairs={{0,4},{4,0},{8,12},{12,8},{16,20},{20,16},{24,28},{28,24},{32,36},... | collective-permute-start | bytes 1843208 | tf_op jit(solution)/shard_map/ppermute | solution.py:702
  23.3 5.9 %collective-permute-start.5 = (f32[8,40,128]{2,1,0:T(8,128)S(1)}, f32[8,40,128]{2,1,0:T(8,128)S(1)}, u32[]{:S(2)}, u32[]{:S(2)}) collective-permute-start(f32[8,40,128]{2,1,0:T(8,128)S(1)} %get-tuple-element.43), channel_id=1, source_target_pairs={{0,4},{4,0},{8,12},{12,8},{16,20},{20,16},{24,28},{28,24},{32,36},... | collective-permute-start | bytes 491528 | tf_op jit(solution)/shard_map/ppermute | solution.py:702
  28.2 4.7 %collective-permute-start.4 = (f32[8,40,128]{2,1,0:T(8,128)S(1)}, f32[8,40,128]{2,1,0:T(8,128)S(1)}, u32[]{:S(2)}, u32[]{:S(2)}) collective-permute-start(f32[8,40,128]{2,1,0:T(8,128)S(1)} %get-tuple-element.42.own), channel_id=1, source_target_pairs={{0,252},{4,8},{8,4},{12,16},{16,12},{20,24},{24,20},{28,32},{32,28... | collective-permute-start | bytes 491528 | tf_op jit(solution)/shard_map/ppermute | solution.py:707
  33.2 7.0 %collective-permute-start.6 = (f32[56,128]{1,0:T(8,128)S(1)}, f32[56,128]{1,0:T(8,128)S(1)}, u32[]{:S(2)}, u32[]{:S(2)}) collective-permute-start(f32[56,128]{1,0:T(8,128)S(1)} %get-tuple-element.46), channel_id=1, source_target_pairs={{0,1},{1,2},{2,3},{3,0},{4,5},{5,6},{6,7},{7,4},{8,9},{9,10},{10,1... | collective-permute-start | bytes 86024 | tf_op jit(solution)/shard_map/ppermute | solution.py:698
  34.3 6.0 %collective-permute-start.7 = (f32[56,128]{1,0:T(8,128)S(1)}, f32[56,128]{1,0:T(8,128)S(1)}, u32[]{:S(2)}, u32[]{:S(2)}) collective-permute-start(f32[56,128]{1,0:T(8,128)S(1)} %get-tuple-element.47), channel_id=1, source_target_pairs={{0,3},{1,0},{2,1},{3,2},{4,7},{5,4},{6,5},{7,6},{8,11},{9,8},{10,9... | collective-permute-start | bytes 86024 | tf_op jit(solution)/shard_map/ppermute | solution.py:698
  36.1 4.1 %collective-permute-start.8 = (f32[40,128]{1,0:T(8,128)S(1)}, f32[40,128]{1,0:T(8,128)S(1)}, u32[]{:S(2)}, u32[]{:S(2)}) collective-permute-start(f32[40,128]{1,0:T(8,128)S(1)} %get-tuple-element.45.f2), channel_id=1, source_target_pairs={{0,2},{1,3},{2,0},{3,1},{4,6},{5,7},{6,4},{7,5},{8,10},{9,11},{10,... | collective-permute-start | bytes 61448 | tf_op jit(solution)/shard_map/ppermute | solution.py:698
  40.5 6.0 %collective-permute-start.9 = (f32[240,128]{1,0:T(8,128)S(1)}, f32[240,128]{1,0:T(8,128)S(1)}, u32[]{:S(2)}, u32[]{:S(2)}) collective-permute-start(f32[240,128]{1,0:T(8,128)S(1)} %get-tuple-element.50.msg), channel_id=1, source_target_pairs={{0,4},{4,0},{8,12},{12,8},{16,20},{20,16},{24,28},{28,24},{32,36},... | collective-permute-start | bytes 368648 | tf_op jit(solution)/shard_map/ppermute | solution.py:702
  46.5 5.2 %collective-permute-start.10 = (f32[384,128]{1,0:T(8,128)S(1)}, f32[384,128]{1,0:T(8,128)S(1)}, u32[]{:S(2)}, u32[]{:S(2)}) collective-permute-start(f32[384,128]{1,0:T(8,128)S(1)} %shard_map.52), channel_id=1, source_target_pairs={{0,252},{4,8},{8,4},{12,16},{16,12},{20,24},{24,20},{28,32},{32,28... | collective-permute-start | bytes 589832 | tf_op jit(solution)/shard_map/ppermute | solution.py:707
  51.7 4.8 %collective-permute-start.11 = (f32[384,128]{1,0:T(8,128)S(1)}, f32[384,128]{1,0:T(8,128)S(1)}, u32[]{:S(2)}, u32[]{:S(2)}) collective-permute-start(f32[384,128]{1,0:T(8,128)S(1)} %collective-permute-done.10.near), channel_id=1, source_target_pairs={{0,4},{4,0},{8,12},{12,8},{16,20},{20,16},{24,28},{28,24},{32,36},... | collective-permute-start | bytes 589832 | tf_op jit(solution)/shard_map/ppermute | solution.py:702
  71.9 9.5 %collective-permute-start.12 = (f32[32,2,8,128]{3,2,1,0:T(8,128)S(1)}, f32[32,2,8,128]{3,2,1,0:T(8,128)S(1)}, u32[]{:S(2)}, u32[]{:S(2)}) collective-permute-start(f32[32,2,8,128]{3,2,1,0:T(8,128)S(1)} %all_to_all.5.mine), channel_id=1, source_target_pairs={{0,4},{4,0},{8,12},{12,8},{16,20},{20,16},{24,28},{28,24},{32,36},... | collective-permute-start | bytes 786440 | tf_op jit(solution)/shard_map/ppermute | solution.py:702
  75.0 3.2 %collective-permute-start.13 = (f32[32,128]{1,0:T(8,128)S(1)}, f32[32,128]{1,0:T(8,128)S(1)}, u32[]{:S(2)}, u32[]{:S(2)}) collective-permute-start(f32[32,128]{1,0:T(8,128)S(1)} %get-tuple-element.55), channel_id=1, source_target_pairs={{0,252},{4,8},{8,4},{12,16},{16,12},{20,24},{24,20},{28,32},{32,28... | collective-permute-start | bytes 49160 | tf_op jit(solution)/shard_map/ppermute | solution.py:707
  78.1 6.1 %collective-permute-start.14 = (f32[32,128]{1,0:T(8,128)S(1)}, f32[32,128]{1,0:T(8,128)S(1)}, u32[]{:S(2)}, u32[]{:S(2)}) collective-permute-start(f32[32,128]{1,0:T(8,128)S(1)} %collective-permute-done.13.late), channel_id=1, source_target_pairs={{0,4},{4,0},{8,12},{12,8},{16,20},{20,16},{24,28},{28,24},{32,36},... | collective-permute-start | bytes 49160 | tf_op jit(solution)/shard_map/ppermute | solution.py:702
  84.5 3.8 %collective-permute-start.15 = (f32[2,64,128]{2,1,0:T(8,128)S(1)}, f32[2,64,128]{2,1,0:T(8,128)S(1)}, u32[]{:S(2)}, u32[]{:S(2)}) collective-permute-start(f32[2,64,128]{2,1,0:T(8,128)S(1)} %shard_map.57.e2), channel_id=1, source_target_pairs={{0,252},{4,8},{8,4},{12,16},{16,12},{20,24},{24,20},{28,32},{32,28... | collective-permute-start | bytes 196616 | tf_op jit(solution)/shard_map/ppermute | solution.py:707
  89.0 4.2 %collective-permute-start.16 = (f32[40,128]{1,0:T(8,128)S(1)}, f32[40,128]{1,0:T(8,128)S(1)}, u32[]{:S(2)}, u32[]{:S(2)}) collective-permute-start(f32[40,128]{1,0:T(8,128)S(1)} %get-tuple-element.60), channel_id=1, source_target_pairs={{0,4},{4,0},{8,12},{12,8},{16,20},{20,16},{24,28},{28,24},{32,36},... | collective-permute-start | bytes 61448 | tf_op jit(solution)/shard_map/ppermute | solution.py:702

commit v8 on v7

--- a/solution.py
+++ b/solution.py
@@ -608,28 +608,35 @@
         e2[pl.ds(2 * q + 1, 24, stride=8), :] = fine
 
 
-def coarse_post_kernel(e2, win, u2, late, late_sib, out):
-    below, above = sides(late, late_sib)
-    v = [both_halves(below(...)), u2[0], u2[1], u2[2], u2[3], both_halves(above(...))]
-    v = [v[m] + e2[64 * (m // 2) : 64 * (m // 2) + 64, :] for m in range(6)]
-
-    def args(k):
+def coarse_post_kernel(e2, win, u2, late, out):
+    par = lax.rem(lax.axis_index("wide"), 2)
+    odd = par == 1
+    late = both_halves(late[...])
+    v = [jnp.where(odd, u2[0], late), u2[par], u2[1 + par], u2[2 + par], jnp.where(odd, late, u2[3])]
+    v = [v[m] + e2[pl.ds(pl.multiple_of(64 * ((m + par) // 2), 64), 64), :] for m in range(5)]
+
+    def args(m):
+        k = m + par
         return win[k], win[4 + k], win[8 + k], win[9 + k], win[13 + k], win[17 + k]
 
-    w = [first_post(v[m + 1], v[m], v[m + 2], *args(m)) for m in range(4)]
-    for p in range(2):
-        out[p] = second_post(w[p + 1], v[p + 2], w[p], w[p + 2], *args(p + 1))
-
-
-def middle_post_kernel(e2, far, msg, sib, near, f, g, w1, own, edge, send, fine, c1, v, w):
+    w = [first_post(v[m + 1], v[m], v[m + 2], *args(m)) for m in range(3)]
+    out[...] = second_post(w[1], v[2], w[0], w[2], *args(1))
+
+
+def pair_kernel(a, b, out):
+    out[0] = a[...]
+    out[1] = b[...]
+
+
+def middle_post_kernel(e2, e2sib, far, msg, sib, near, f, g, w1, own, edge, send, fine, c1, v, w):
     n, par = lax.axis_index("narrow"), lax.rem(lax.axis_index("wide"), 2)
     odd = par == 1
     row, col = iota((40, 64), 0), iota((40, 64), 1)
     pick = (col == lax.rem(16 * n + (row + 4) // 2 + 60, 64)).astype(F32)
     lanes = copies_of_lanes(128, 128)
-    planes = (e2[0], e2[1], far[0], far[1])
-    for k in range(4):
-        fine[k] = mul(mul_left(pick, jnp.where(odd, planes[k], planes[(k + 2) % 4])), lanes)
+    e2, e2sib, near0, near1 = e2[...], e2sib[...], far[0], far[1]
+    for k, (upper, lower) in enumerate(((e2sib, near1), (e2, near0), (near0, e2), (near1, e2sib))):
+        fine[k] = mul(mul_left(pick, jnp.where(odd, upper, lower)), lanes)
     c1[0:6] = w1[0:6]
     c1[6] = near[344:384]
     ours = [msg[160 + 40 * p : 200 + 40 * p] for p in range(2)]
@@ -753,10 +760,9 @@
         coarse_pre_kernel, [(21, 64, 128), (4, 64, 128), (32, 128)], [(6, 64, 128)]
     )(own2, sib, near, other)
     (send,) = call(coarse_send_kernel, [(n3, 2, 8, 128)], [(64, 128)])(w2, u2w, tiles)
-    late = across(late)
     cores = [[k for k in range(wide) if k % 2 == c] for c in range(2)]
     parts = lax.all_to_all(send, "wide", split_axis=0, concat_axis=0, tiled=True, axis_index_groups=cores)
-    theirs, late_sib = sibling(parts), sibling(late)
+    theirs, late = sibling(parts), across(late)
 
     three, four = (n3, 8, 128), (n4, 8, 128)
     (fine2,) = call(
@@ -765,14 +771,16 @@
         [three, (n3 + 1, 8, 128), three, three, three, three, (n3 + 2, 8, 128), (n3 + 2, 8, 128), four, four]
         + [(n4 + 1, 8, 128), four, four, four, (n4 + 2, 8, 128), (n4 + 2, 8, 128), four, (32, 128)],
     )(parts, theirs)
-    (e2,) = call(coarse_post_kernel, [(2, 64, 128)])(fine2, w2, u2w, late, late_sib)
-    far = across(e2)
+    (e2,) = call(coarse_post_kernel, [(64, 128)])(fine2, w2, u2w, late)
+    e2sib = sibling(e2)
+    (both,) = call(pair_kernel, [(2, 64, 128)])(e2, e2sib)
+    far = across(both)
 
     e1, edge, send = call(
         middle_post_kernel,
         [(2, 40, 128), (40, 128), (40, 128)],
         [(4, 40, 128), (7, 40, 128), (7, 40, 128), (7, 40, 128)],
-    )(e2, far, msg, sib, near, f1w, g1w, w1)
+    )(e2, e2sib, far, msg, sib, near, f1w, g1w, w1)
     other1 = sibling(send)
 
     (out,) = call(

time: 95.7 us -> 94 us (0.982)
    ppermute x5, waiting for transfers between devices: 16.8 us -> 15.2 us  [across(): lax.ppermute(x, 'wide', [(i, (i + 1 if i % 2 else i - 1) % count) for i i...]
    pallas_call x14 -> x15, Pallas kernels: 12.9 us -> 12.8 us  [run(): pl.pallas_call(kernel, out_shape=[jax.ShapeDtypeStruct(s, F32) for s in o...]
  transfers between devices with their start and end apart: 17 -> 17, of which waited for: 11 -> 11; matrix products, arithmetic and copies ran while one was open for 1% -> 1% of each run, Pallas kernels for 3% -> 4%
where the time goes in v8:
time: 94 us; the launch traced here: 93.8 us
  starting transfers between devices  40.7 us (43%)
  waiting for transfers between devices  24 us (26%)
  blocking collectives  14.9 us (16%)
  Pallas kernels  12.8 us (14%)
  other arithmetic  1.26 us (1%)
    ppermute x7, starting transfers between devices, sibling(): lax.ppermute(x, 'wide', [(i, i ^ 1) for i in range(lax.axis_size('wide'))])  27.6 us
    ppermute x5, waiting for transfers between devices, across(): lax.ppermute(x, 'wide', [(i, (i + 1 if i % 2 else i - 1) % count) for i i...  15.2 us
    all_to_all x1, blocking collectives, body(): lax.all_to_all(send, 'wide', split_axis=0, concat_axis=0, tiled=True, axi...  14.9 us
    pallas_call x15, Pallas kernels, run(): pl.pallas_call(kernel, out_shape=[jax.ShapeDtypeStruct(s, F32) for s in o...  12.8 us
    ppermute x5, starting transfers between devices, shift(): return lax.ppermute(x, axis, [(i, (i + by) % count) for i in range(count)])  7.72 us
    ppermute x5, starting transfers between devices, across(): lax.ppermute(x, 'wide', [(i, (i + 1 if i % 2 else i - 1) % count) for i i...  5.33 us
    ppermute x7, waiting for transfers between devices, sibling(): lax.ppermute(x, 'wide', [(i, i ^ 1) for i in range(lax.axis_size('wide'))])  4.53 us
    ppermute x5, waiting for transfers between devices, shift(): return lax.ppermute(x, axis, [(i, (i + by) % count) for i in range(count)])  4.28 us
  transfers between devices with their start and end apart: 17, of which 11 were waited for; matrix products, arithmetic and copies ran while one was open for 1% of the time, Pallas kernels for 4%

profile of v8, /device:TPU:1, one launch (start us, length us, event | category | flops | bytes accessed | tf_op | source)
XLA Modules:
  0.0 93.8 jit_solution(8241103190056253750)
XLA Ops:
  0.0 1.6 %shard_map.46 = (f32[16,8,256]{2,1,0:T(8,128)}, f32[16,8,256]{2,1,0:T(8,128)}) custom-call(f32[4,64,256]{2,1,0:T(8,128)} %f.1, f32[4,64,256]{2,1,0:T(8,128)} %c1.1, f32[4,64,256]{2,1,0:T(8,128)} %c2.1, f32[4,64,256]{2,1,0:T(8,128)} %c3.1), custom_call_target="tpu_custom_call" | custom-call | tf_op jit(solution)/shard_map/pallas_call | solution.py:136
  1.6 2.2 %collective-permute-start = (f32[16,8,256]{2,1,0:T(8,128)}, f32[16,8,256]{2,1,0:T(8,128)S(1)}, u32[]{:S(2)}, u32[]{:S(2)}) collective-permute-start(f32[16,8,256]{2,1,0:T(8,128)} %get-tuple-element.36), channel_id=1, source_target_pairs={{0,1},{1,2},{2,3},{3,0},{4,5},{5,6},{6,7},{7,4},{8,9},{9,10},{10,1... | collective-permute-start | bytes 393224 | tf_op jit(solution)/shard_map/ppermute | solution.py:705
  3.8 1.5 %collective-permute-start.1 = (f32[16,8,256]{2,1,0:T(8,128)}, f32[16,8,256]{2,1,0:T(8,128)S(1)}, u32[]{:S(2)}, u32[]{:S(2)}) collective-permute-start(f32[16,8,256]{2,1,0:T(8,128)} %get-tuple-element.37), channel_id=1, source_target_pairs={{0,3},{1,0},{2,1},{3,2},{4,7},{5,4},{6,5},{7,6},{8,11},{9,8},{10,9... | collective-permute-start | bytes 393224 | tf_op jit(solution)/shard_map/ppermute | solution.py:705
  5.4 1.3 %pad_maximum_fusion.inner = f32[16,64,256]{2,1,0:T(8,128)S(1)} fusion(f32[4,64,256]{2,1,0:T(8,128)} %c3.1, f32[4,64,256]{2,1,0:T(8,128)} %c2.1, f32[4,64,256]{2,1,0:T(8,128)} %c1.1, f32[4,64,256]{2,1,0:T(8,128)} %f.1), kind=kLoop, calls=%fused_computation | loop fusion | flops 786432 | bytes 2097152 | tf_op jit(solution)/shard_map/concatenate | solution.py:734
  6.6 1.2 %collective-permute-done.low = f32[16,8,256]{2,1,0:T(8,128)S(1)} collective-permute-done((f32[16,8,256]{2,1,0:T(8,128)}, f32[16,8,256]{2,1,0:T(8,128)S(1)}, u32[]{:S(2)}, u32[]{:S(2)}) %collective-permute-start) | collective-permute-done | bytes 131104 | tf_op jit(solution)/shard_map/ppermute | solution.py:705
  8.4 3.7 %collective-permute-start.2 = (f32[600,256]{1,0:T(8,128)S(1)}, f32[600,256]{1,0:T(8,128)S(1)}, u32[]{:S(2)}, u32[]{:S(2)}) collective-permute-start(f32[600,256]{1,0:T(8,128)S(1)} %get-tuple-element.40), channel_id=1, source_target_pairs={{0,252},{4,8},{8,4},{12,16},{16,12},{20,24},{24,20},{28,32},{32,28... | collective-permute-start | bytes 1843208 | tf_op jit(solution)/shard_map/ppermute | solution.py:714
  12.1 5.1 %collective-permute-start.3 = (f32[600,256]{1,0:T(8,128)S(1)}, f32[600,256]{1,0:T(8,128)S(1)}, u32[]{:S(2)}, u32[]{:S(2)}) collective-permute-start(f32[600,256]{1,0:T(8,128)S(1)} %get-tuple-element.41), channel_id=1, source_target_pairs={{0,4},{4,0},{8,12},{12,8},{16,20},{20,16},{24,28},{28,24},{32,36},... | collective-permute-start | bytes 1843208 | tf_op jit(solution)/shard_map/ppermute | solution.py:709
  17.3 3.0 %collective-permute-done.2.far = f32[600,256]{1,0:T(8,128)S(1)} collective-permute-done((f32[600,256]{1,0:T(8,128)S(1)}, f32[600,256]{1,0:T(8,128)S(1)}, u32[]{:S(2)}, u32[]{:S(2)}) %collective-permute-start.2) | collective-permute-done | bytes 614432 | tf_op jit(solution)/shard_map/ppermute | solution.py:714
  20.3 3.1 %shard_map.48 = (f32[6,80,256]{2,1,0:T(8,128)S(1)}, f32[7,80,256]{2,1,0:T(8,128)S(1)}, f32[6,80,256]{2,1,0:T(8,128)S(1)}, f32[6,80,256]{2,1,0:T(8,128)S(1)}, f32...) custom-call(f32[16,80,256]{2,1,0:T(8,128)S(1)} %get-tuple-element.38, ...), custom_call_target="tpu_custom_call" | custom-call | tf_op jit(solution)/shard_map/pallas_call | solution.py:136
  23.3 4.8 %collective-permute-start.5 = (f32[8,40,128]{2,1,0:T(8,128)S(1)}, f32[8,40,128]{2,1,0:T(8,128)S(1)}, u32[]{:S(2)}, u32[]{:S(2)}) collective-permute-start(f32[8,40,128]{2,1,0:T(8,128)S(1)} %get-tuple-element.43), channel_id=1, source_target_pairs={{0,4},{4,0},{8,12},{12,8},{16,20},{20,16},{24,28},{28,24},{32,36},... | collective-permute-start | bytes 491528 | tf_op jit(solution)/shard_map/ppermute | solution.py:709
  28.4 0.8 collective-permute-done.5.sib
  29.2 3.7 %collective-permute-done.4.far = f32[8,40,128]{2,1,0:T(8,128)S(1)} collective-permute-done((f32[8,40,128]{2,1,0:T(8,128)S(1)}, f32[8,40,128]{2,1,0:T(8,128)S(1)}, u32[]{:S(2)}, u32[]{:S(2)}) %collective-permute-start.4) | collective-permute-done | bytes 163872 | tf_op jit(solution)/shard_map/ppermute | solution.py:714
  33.2 1.1 %collective-permute-start.6 = (f32[56,128]{1,0:T(8,128)S(1)}, f32[56,128]{1,0:T(8,128)S(1)}, u32[]{:S(2)}, u32[]{:S(2)}) collective-permute-start(f32[56,128]{1,0:T(8,128)S(1)} %get-tuple-element.46), channel_id=1, source_target_pairs={{0,1},{1,2},{2,3},{3,0},{4,5},{5,6},{6,7},{7,4},{8,9},{9,10},{10,1... | collective-permute-start | bytes 86024 | tf_op jit(solution)/shard_map/ppermute | solution.py:705
  34.3 1.8 %collective-permute-start.7 = (f32[56,128]{1,0:T(8,128)S(1)}, f32[56,128]{1,0:T(8,128)S(1)}, u32[]{:S(2)}, u32[]{:S(2)}) collective-permute-start(f32[56,128]{1,0:T(8,128)S(1)} %get-tuple-element.47), channel_id=1, source_target_pairs={{0,3},{1,0},{2,1},{3,2},{4,7},{5,4},{6,5},{7,6},{8,11},{9,8},{10,9... | collective-permute-start | bytes 86024 | tf_op jit(solution)/shard_map/ppermute | solution.py:705
  36.1 1.1 %collective-permute-start.8 = (f32[40,128]{1,0:T(8,128)S(1)}, f32[40,128]{1,0:T(8,128)S(1)}, u32[]{:S(2)}, u32[]{:S(2)}) collective-permute-start(f32[40,128]{1,0:T(8,128)S(1)} %get-tuple-element.45.f2), channel_id=1, source_target_pairs={{0,2},{1,3},{2,0},{3,1},{4,6},{5,7},{6,4},{7,5},{8,10},{9,11},{10,... | collective-permute-start | bytes 61448 | tf_op jit(solution)/shard_map/ppermute | solution.py:705
  37.2 3.0 %collective-permute-done.8.far = f32[40,128]{1,0:T(8,128)S(1)} collective-permute-done((f32[40,128]{1,0:T(8,128)S(1)}, f32[40,128]{1,0:T(8,128)S(1)}, u32[]{:S(2)}, u32[]{:S(2)}) %collective-permute-start.8) | collective-permute-done | bytes 20512 | tf_op jit(solution)/shard_map/ppermute | solution.py:705
  40.5 5.0 %collective-permute-start.9 = (f32[240,128]{1,0:T(8,128)S(1)}, f32[240,128]{1,0:T(8,128)S(1)}, u32[]{:S(2)}, u32[]{:S(2)}) collective-permute-start(f32[240,128]{1,0:T(8,128)S(1)} %get-tuple-element.50.msg), channel_id=1, source_target_pairs={{0,4},{4,0},{8,12},{12,8},{16,20},{20,16},{24,28},{28,24},{32,36},... | collective-permute-start | bytes 368648 | tf_op jit(solution)/shard_map/ppermute | solution.py:709
  45.5 1.0 %collective-permute-done.9.sib = f32[240,128]{1,0:T(8,128)S(1)} collective-permute-done((f32[240,128]{1,0:T(8,128)S(1)}, f32[240,128]{1,0:T(8,128)S(1)}, u32[]{:S(2)}, u32[]{:S(2)}) %collective-permute-start.9) | collective-permute-done | bytes 122912 | tf_op jit(solution)/shard_map/ppermute | solution.py:709
  46.9 4.8 %collective-permute-done.10.near = f32[384,128]{1,0:T(8,128)S(1)} collective-permute-done((f32[384,128]{1,0:T(8,128)S(1)}, f32[384,128]{1,0:T(8,128)S(1)}, u32[]{:S(2)}, u32[]{:S(2)}) %collective-permute-start.10) | collective-permute-done | bytes 196640 | tf_op jit(solution)/shard_map/ppermute | solution.py:714
  51.7 3.7 %collective-permute-start.11 = (f32[384,128]{1,0:T(8,128)S(1)}, f32[384,128]{1,0:T(8,128)S(1)}, u32[]{:S(2)}, u32[]{:S(2)}) collective-permute-start(f32[384,128]{1,0:T(8,128)S(1)} %collective-permute-done.10.near), channel_id=1, source_target_pairs={{0,4},{4,0},{8,12},{12,8},{16,20},{20,16},{24,28},{28,24},{32,36},... | collective-permute-start | bytes 589832 | tf_op jit(solution)/shard_map/ppermute | solution.py:709
  55.3 1.1 %collective-permute-done.11.other = f32[384,128]{1,0:T(8,128)S(1)} collective-permute-done((f32[384,128]{1,0:T(8,128)S(1)}, f32[384,128]{1,0:T(8,128)S(1)}, u32[]{:S(2)}, u32[]{:S(2)}) %collective-permute-start.11) | collective-permute-done | bytes 196640 | tf_op jit(solution)/shard_map/ppermute | solution.py:709
  57.0 14.9 %all_to_all.5.mine = f32[32,2,8,128]{3,2,1,0:T(8,128)S(1)} all-to-all(f32[32,2,8,128]{3,2,1,0:T(8,128)S(1)} %shard_map.55), channel_id=1, replica_groups={{0,8,16,24,32,40,48,56,64,72,80,88,96,104,112,120,128,136,144,152,160,1..., dimensions={0} | all-to-all | bytes 524288 | tf_op jit(solution)/shard_map/all_to_all | solution.py:764
  71.9 3.0 %collective-permute-start.12 = (f32[32,2,8,128]{3,2,1,0:T(8,128)S(1)}, f32[32,2,8,128]{3,2,1,0:T(8,128)S(1)}, u32[]{:S(2)}, u32[]{:S(2)}) collective-permute-start(f32[32,2,8,128]{3,2,1,0:T(8,128)S(1)} %all_to_all.5.mine), channel_id=1, source_target_pairs={{0,4},{4,0},{8,12},{12,8},{16,20},{20,16},{24,28},{28,24},{32,36},... | collective-permute-start | bytes 786440 | tf_op jit(solution)/shard_map/ppermute | solution.py:709
  75.0 1.5 %collective-permute-start.13 = (f32[32,128]{1,0:T(8,128)S(1)}, f32[32,128]{1,0:T(8,128)S(1)}, u32[]{:S(2)}, u32[]{:S(2)}) collective-permute-start(f32[32,128]{1,0:T(8,128)S(1)} %get-tuple-element.55), channel_id=1, source_target_pairs={{0,252},{4,8},{8,4},{12,16},{16,12},{20,24},{24,20},{28,32},{32,28... | collective-permute-start | bytes 49160 | tf_op jit(solution)/shard_map/ppermute | solution.py:714
  76.5 2.8 %shard_map.56.e2 = f32[192,128]{1,0:T(8,128)S(1)} custom-call(f32[32,2,8,128]{3,2,1,0:T(8,128)S(1)} %all_to_all.5.mine, f32[32,2,8,128]{3,2,1,0:T(8,128)S(1)} %collective-permute-done.12.theirs), custom_call_target="tpu_custom_call" | custom-call | tf_op jit(solution)/shard_map/pallas_call | solution.py:136
  79.5 2.2 %collective-permute-start.14 = (f32[64,128]{1,0:T(8,128)S(1)}, f32[64,128]{1,0:T(8,128)S(1)}, u32[]{:S(2)}, u32[]{:S(2)}) collective-permute-start(f32[64,128]{1,0:T(8,128)S(1)} %shard_map.57.a.e2), channel_id=1, source_target_pairs={{0,4},{4,0},{8,12},{12,8},{16,20},{20,16},{24,28},{28,24},{32,36},... | collective-permute-start | bytes 98312 | tf_op jit(solution)/shard_map/ppermute | solution.py:709
  81.7 0.9 collective-permute-done.14.b.e2sib
  82.6 3.7 %collective-permute-done.15.far = f32[2,64,128]{2,1,0:T(8,128)S(1)} collective-permute-done((f32[2,64,128]{2,1,0:T(8,128)S(1)}, f32[2,64,128]{2,1,0:T(8,128)S(1)}, u32[]{:S(2)}, u32[]{:S(2)}) %collective-permute-start.15) | collective-permute-done | bytes 65568 | tf_op jit(solution)/shard_map/ppermute | solution.py:714
  86.3 0.7 shard_map.59
  87.0 3.7 %collective-permute-start.16 = (f32[40,128]{1,0:T(8,128)S(1)}, f32[40,128]{1,0:T(8,128)S(1)}, u32[]{:S(2)}, u32[]{:S(2)}) collective-permute-start(f32[40,128]{1,0:T(8,128)S(1)} %get-tuple-element.60), channel_id=1, source_target_pairs={{0,4},{4,0},{8,12},{12,8},{16,20},{20,16},{24,28},{28,24},{32,36},... | collective-permute-start | bytes 61448 | tf_op jit(solution)/shard_map/ppermute | solution.py:709
  90.7 0.8 collective-permute-done.16.other
  91.6 2.2 %shard_map.60 = f32[4,64,256]{2,1,0:T(8,128)} custom-call(f32[2,40,128]{2,1,0:T(8,128)S(1)} %get-tuple-element.58.e1, f32[40,128]{1,0:T(8,128)S(1)} %get-tuple-element.59.edge, f32[40,128]{1,0:T(8,128)S(1)} %collective-permute-done.16.other, f32[8,40,128]{2,1,0:T(8,128)S(1)} %collective-permute-done.4.far, f32[8,40,128]{2,1,0:T(8,128)S(1)} %collective-permute-done.5.sib, ...), custom_call_target="tpu_custom_call" | custom-call | tf_op jit(solution)/shard_map/pallas_call | solution.py:136
  (19 shorter events, 2.6 us)
Async XLA Ops:
  1.6 6.2 %collective-permute-start = (f32[16,8,256]{2,1,0:T(8,128)}, f32[16,8,256]{2,1,0:T(8,128)S(1)}, u32[]{:S(2)}, u32[]{:S(2)}) collective-permute-start(f32[16,8,256]{2,1,0:T(8,128)} %get-tuple-element.36), channel_id=1, source_target_pairs={{0,1},{1,2},{2,3},{3,0},{4,5},{5,6},{6,7},{7,4},{8,9},{9,10},{10,1... | collective-permute-start | bytes 393224 | tf_op jit(solution)/shard_map/ppermute | solution.py:705
  3.8 4.0 %collective-permute-start.1 = (f32[16,8,256]{2,1,0:T(8,128)}, f32[16,8,256]{2,1,0:T(8,128)S(1)}, u32[]{:S(2)}, u32[]{:S(2)}) collective-permute-start(f32[16,8,256]{2,1,0:T(8,128)} %get-tuple-element.37), channel_id=1, source_target_pairs={{0,3},{1,0},{2,1},{3,2},{4,7},{5,4},{6,5},{7,6},{8,11},{9,8},{10,9... | collective-permute-start | bytes 393224 | tf_op jit(solution)/shard_map/ppermute | solution.py:705
  8.4 11.8 %collective-permute-start.2 = (f32[600,256]{1,0:T(8,128)S(1)}, f32[600,256]{1,0:T(8,128)S(1)}, u32[]{:S(2)}, u32[]{:S(2)}) collective-permute-start(f32[600,256]{1,0:T(8,128)S(1)} %get-tuple-element.40), channel_id=1, source_target_pairs={{0,252},{4,8},{8,4},{12,16},{16,12},{20,24},{24,20},{28,32},{32,28... | collective-permute-start | bytes 1843208 | tf_op jit(solution)/shard_map/ppermute | solution.py:714
  12.1 8.1 %collective-permute-start.3 = (f32[600,256]{1,0:T(8,128)S(1)}, f32[600,256]{1,0:T(8,128)S(1)}, u32[]{:S(2)}, u32[]{:S(2)}) collective-permute-start(f32[600,256]{1,0:T(8,128)S(1)} %get-tuple-element.41), channel_id=1, source_target_pairs={{0,4},{4,0},{8,12},{12,8},{16,20},{20,16},{24,28},{28,24},{32,36},... | collective-permute-start | bytes 1843208 | tf_op jit(solution)/shard_map/ppermute | solution.py:709
  23.3 5.9 %collective-permute-start.5 = (f32[8,40,128]{2,1,0:T(8,128)S(1)}, f32[8,40,128]{2,1,0:T(8,128)S(1)}, u32[]{:S(2)}, u32[]{:S(2)}) collective-permute-start(f32[8,40,128]{2,1,0:T(8,128)S(1)} %get-tuple-element.43), channel_id=1, source_target_pairs={{0,4},{4,0},{8,12},{12,8},{16,20},{20,16},{24,28},{28,24},{32,36},... | collective-permute-start | bytes 491528 | tf_op jit(solution)/shard_map/ppermute | solution.py:709
  28.2 4.7 %collective-permute-start.4 = (f32[8,40,128]{2,1,0:T(8,128)S(1)}, f32[8,40,128]{2,1,0:T(8,128)S(1)}, u32[]{:S(2)}, u32[]{:S(2)}) collective-permute-start(f32[8,40,128]{2,1,0:T(8,128)S(1)} %get-tuple-element.42.own), channel_id=1, source_target_pairs={{0,252},{4,8},{8,4},{12,16},{16,12},{20,24},{24,20},{28,32},{32,28... | collective-permute-start | bytes 491528 | tf_op jit(solution)/shard_map/ppermute | solution.py:714
  33.2 7.0 %collective-permute-start.6 = (f32[56,128]{1,0:T(8,128)S(1)}, f32[56,128]{1,0:T(8,128)S(1)}, u32[]{:S(2)}, u32[]{:S(2)}) collective-permute-start(f32[56,128]{1,0:T(8,128)S(1)} %get-tuple-element.46), channel_id=1, source_target_pairs={{0,1},{1,2},{2,3},{3,0},{4,5},{5,6},{6,7},{7,4},{8,9},{9,10},{10,1... | collective-permute-start | bytes 86024 | tf_op jit(solution)/shard_map/ppermute | solution.py:705
  34.3 6.0 %collective-permute-start.7 = (f32[56,128]{1,0:T(8,128)S(1)}, f32[56,128]{1,0:T(8,128)S(1)}, u32[]{:S(2)}, u32[]{:S(2)}) collective-permute-start(f32[56,128]{1,0:T(8,128)S(1)} %get-tuple-element.47), channel_id=1, source_target_pairs={{0,3},{1,0},{2,1},{3,2},{4,7},{5,4},{6,5},{7,6},{8,11},{9,8},{10,9... | collective-permute-start | bytes 86024 | tf_op jit(solution)/shard_map/ppermute | solution.py:705
  36.1 4.1 %collective-permute-start.8 = (f32[40,128]{1,0:T(8,128)S(1)}, f32[40,128]{1,0:T(8,128)S(1)}, u32[]{:S(2)}, u32[]{:S(2)}) collective-permute-start(f32[40,128]{1,0:T(8,128)S(1)} %get-tuple-element.45.f2), channel_id=1, source_target_pairs={{0,2},{1,3},{2,0},{3,1},{4,6},{5,7},{6,4},{7,5},{8,10},{9,11},{10,... | collective-permute-start | bytes 61448 | tf_op jit(solution)/shard_map/ppermute | solution.py:705
  40.5 6.0 %collective-permute-start.9 = (f32[240,128]{1,0:T(8,128)S(1)}, f32[240,128]{1,0:T(8,128)S(1)}, u32[]{:S(2)}, u32[]{:S(2)}) collective-permute-start(f32[240,128]{1,0:T(8,128)S(1)} %get-tuple-element.50.msg), channel_id=1, source_target_pairs={{0,4},{4,0},{8,12},{12,8},{16,20},{20,16},{24,28},{28,24},{32,36},... | collective-permute-start | bytes 368648 | tf_op jit(solution)/shard_map/ppermute | solution.py:709
  46.5 5.2 %collective-permute-start.10 = (f32[384,128]{1,0:T(8,128)S(1)}, f32[384,128]{1,0:T(8,128)S(1)}, u32[]{:S(2)}, u32[]{:S(2)}) collective-permute-start(f32[384,128]{1,0:T(8,128)S(1)} %shard_map.52), channel_id=1, source_target_pairs={{0,252},{4,8},{8,4},{12,16},{16,12},{20,24},{24,20},{28,32},{32,28... | collective-permute-start | bytes 589832 | tf_op jit(solution)/shard_map/ppermute | solution.py:714
  51.7 4.8 %collective-permute-start.11 = (f32[384,128]{1,0:T(8,128)S(1)}, f32[384,128]{1,0:T(8,128)S(1)}, u32[]{:S(2)}, u32[]{:S(2)}) collective-permute-start(f32[384,128]{1,0:T(8,128)S(1)} %collective-permute-done.10.near), channel_id=1, source_target_pairs={{0,4},{4,0},{8,12},{12,8},{16,20},{20,16},{24,28},{28,24},{32,36},... | collective-permute-start | bytes 589832 | tf_op jit(solution)/shard_map/ppermute | solution.py:709
  71.9 4.5 %collective-permute-start.12 = (f32[32,2,8,128]{3,2,1,0:T(8,128)S(1)}, f32[32,2,8,128]{3,2,1,0:T(8,128)S(1)}, u32[]{:S(2)}, u32[]{:S(2)}) collective-permute-start(f32[32,2,8,128]{3,2,1,0:T(8,128)S(1)} %all_to_all.5.mine), channel_id=1, source_target_pairs={{0,4},{4,0},{8,12},{12,8},{16,20},{20,16},{24,28},{28,24},{32,36},... | collective-permute-start | bytes 786440 | tf_op jit(solution)/shard_map/ppermute | solution.py:709
  75.0 4.3 %collective-permute-start.13 = (f32[32,128]{1,0:T(8,128)S(1)}, f32[32,128]{1,0:T(8,128)S(1)}, u32[]{:S(2)}, u32[]{:S(2)}) collective-permute-start(f32[32,128]{1,0:T(8,128)S(1)} %get-tuple-element.55), channel_id=1, source_target_pairs={{0,252},{4,8},{8,4},{12,16},{16,12},{20,24},{24,20},{28,32},{32,28... | collective-permute-start | bytes 49160 | tf_op jit(solution)/shard_map/ppermute | solution.py:714
  79.5 3.1 %collective-permute-start.14 = (f32[64,128]{1,0:T(8,128)S(1)}, f32[64,128]{1,0:T(8,128)S(1)}, u32[]{:S(2)}, u32[]{:S(2)}) collective-permute-start(f32[64,128]{1,0:T(8,128)S(1)} %shard_map.57.a.e2), channel_id=1, source_target_pairs={{0,4},{4,0},{8,12},{12,8},{16,20},{20,16},{24,28},{28,24},{32,36},... | collective-permute-start | bytes 98312 | tf_op jit(solution)/shard_map/ppermute | solution.py:709
  82.6 3.7 %collective-permute-start.15 = (f32[2,64,128]{2,1,0:T(8,128)S(1)}, f32[2,64,128]{2,1,0:T(8,128)S(1)}, u32[]{:S(2)}, u32[]{:S(2)}) collective-permute-start(f32[2,64,128]{2,1,0:T(8,128)S(1)} %shard_map.58), channel_id=1, source_target_pairs={{0,252},{4,8},{8,4},{12,16},{16,12},{20,24},{24,20},{28,32},{32,28... | collective-permute-start | bytes 196616 | tf_op jit(solution)/shard_map/ppermute | solution.py:714
  87.0 4.6 %collective-permute-start.16 = (f32[40,128]{1,0:T(8,128)S(1)}, f32[40,128]{1,0:T(8,128)S(1)}, u32[]{:S(2)}, u32[]{:S(2)}) collective-permute-start(f32[40,128]{1,0:T(8,128)S(1)} %get-tuple-element.60), channel_id=1, source_target_pairs={{0,4},{4,0},{8,12},{12,8},{16,20},{20,16},{24,28},{28,24},{32,36},... | collective-permute-start | bytes 61448 | tf_op jit(solution)/shard_map/ppermute | solution.py:709

commit v9 on v8

--- a/solution.py
+++ b/solution.py
@@ -493,7 +493,7 @@
     return lax.rem(j + n, n)
 
 
-STEP = 8
+STEP = 32
 THREE, FOUR = (32, 4), (16, 2)
 
 
@@ -734,11 +734,11 @@
     )(jnp.concatenate(inputs, axis=0), low, high)
     far, sib = across(far), sibling(sib)
 
-    f, c1, c2, c3, g, u2, w1, out_far, out_sib, _ = call(
+    f, c1, c2, c3, g, u2, w1, out_far, out_sib = call(
         fine_pre_kernel,
         [(6,) + big, (7,) + big, (6,) + big, (6,) + big, (6,) + big, (8,) + big]
-        + [(18, 40, 128), (8, 40, 128), (8, 40, 128), (2, 40, 128)],
-        [(8,) + big, (4,) + big, (160, 128)],
+        + [(18, 40, 128), (8, 40, 128), (8, 40, 128)],
+        [(2, 40, 128), (8,) + big, (4,) + big, (160, 128)],
     )(own, coef1, far, sib)
     far1, sib1 = across(out_far), sibling(out_sib)
     (coefs,) = call(coarse_coef_kernel, [(32, 128)], [(80, 128)])(w1)

time: 94 us -> 93.4 us (level)
  Pallas kernels: 12.8 us -> 11.3 us
    pallas_call x15, Pallas kernels: 12.8 us -> 11.3 us  [run(): pl.pallas_call(kernel, out_shape=[jax.ShapeDtypeStruct(s, F32) for s in o...]
    ppermute x7, starting transfers between devices: 27.6 us -> 28.6 us  [sibling(): lax.ppermute(x, 'wide', [(i, i ^ 1) for i in range(lax.axis_size('wide'))])]
  transfers between devices with their start and end apart: 17 -> 17, of which waited for: 11 -> 11; matrix products, arithmetic and copies ran while one was open for 1% -> 1% of each run, Pallas kernels for 4% -> 3%
where the time goes in v9:
time: 93.4 us; the launch traced here: 93.2 us
  starting transfers between devices  41.6 us (45%)
  waiting for transfers between devices  24 us (26%)
  blocking collectives  14.9 us (16%)
  Pallas kernels  11.3 us (12%)
  other arithmetic  1.26 us (1%)
    ppermute x7, starting transfers between devices, sibling(): lax.ppermute(x, 'wide', [(i, i ^ 1) for i in range(lax.axis_size('wide'))])  28.6 us
    ppermute x5, waiting for transfers between devices, across(): lax.ppermute(x, 'wide', [(i, (i + 1 if i % 2 else i - 1) % count) for i i...  15.2 us
    all_to_all x1, blocking collectives, body(): lax.all_to_all(send, 'wide', split_axis=0, concat_axis=0, tiled=True, axi...  14.9 us
    pallas_call x15, Pallas kernels, run(): pl.pallas_call(kernel, out_shape=[jax.ShapeDtypeStruct(s, F32) for s in o...  11.3 us
    ppermute x5, starting transfers between devices, shift(): return lax.ppermute(x, axis, [(i, (i + by) % count) for i in range(count)])  7.72 us
    ppermute x5, starting transfers between devices, across(): lax.ppermute(x, 'wide', [(i, (i + 1 if i % 2 else i - 1) % count) for i i...  5.33 us
    ppermute x7, waiting for transfers between devices, sibling(): lax.ppermute(x, 'wide', [(i, i ^ 1) for i in range(lax.axis_size('wide'))])  4.53 us
    ppermute x5, waiting for transfers between devices, shift(): return lax.ppermute(x, axis, [(i, (i + by) % count) for i in range(count)])  4.28 us
  transfers between devices with their start and end apart: 17, of which 11 were waited for; matrix products, arithmetic and copies ran while one was open for 1% of the time, Pallas kernels for 3%

profile of v9, /device:TPU:1, one launch (start us, length us, event | category | flops | bytes accessed | tf_op | source)
XLA Modules:
  0.0 93.2 jit_solution(7081249442057900266)
XLA Ops:
  0.0 1.6 %shard_map.46 = (f32[16,8,256]{2,1,0:T(8,128)}, f32[16,8,256]{2,1,0:T(8,128)}) custom-call(f32[4,64,256]{2,1,0:T(8,128)} %f.1, f32[4,64,256]{2,1,0:T(8,128)} %c1.1, f32[4,64,256]{2,1,0:T(8,128)} %c2.1, f32[4,64,256]{2,1,0:T(8,128)} %c3.1), custom_call_target="tpu_custom_call" | custom-call | tf_op jit(solution)/shard_map/pallas_call | solution.py:136
  1.6 2.2 %collective-permute-start = (f32[16,8,256]{2,1,0:T(8,128)}, f32[16,8,256]{2,1,0:T(8,128)S(1)}, u32[]{:S(2)}, u32[]{:S(2)}) collective-permute-start(f32[16,8,256]{2,1,0:T(8,128)} %get-tuple-element.36), channel_id=1, source_target_pairs={{0,1},{1,2},{2,3},{3,0},{4,5},{5,6},{6,7},{7,4},{8,9},{9,10},{10,1... | collective-permute-start | bytes 393224 | tf_op jit(solution)/shard_map/ppermute | solution.py:705
  3.8 1.5 %collective-permute-start.1 = (f32[16,8,256]{2,1,0:T(8,128)}, f32[16,8,256]{2,1,0:T(8,128)S(1)}, u32[]{:S(2)}, u32[]{:S(2)}) collective-permute-start(f32[16,8,256]{2,1,0:T(8,128)} %get-tuple-element.37), channel_id=1, source_target_pairs={{0,3},{1,0},{2,1},{3,2},{4,7},{5,4},{6,5},{7,6},{8,11},{9,8},{10,9... | collective-permute-start | bytes 393224 | tf_op jit(solution)/shard_map/ppermute | solution.py:705
  5.4 1.3 %pad_maximum_fusion.inner = f32[16,64,256]{2,1,0:T(8,128)S(1)} fusion(f32[4,64,256]{2,1,0:T(8,128)} %c3.1, f32[4,64,256]{2,1,0:T(8,128)} %c2.1, f32[4,64,256]{2,1,0:T(8,128)} %c1.1, f32[4,64,256]{2,1,0:T(8,128)} %f.1), kind=kLoop, calls=%fused_computation | loop fusion | flops 786432 | bytes 2097152 | tf_op jit(solution)/shard_map/concatenate | solution.py:734
  6.6 1.2 %collective-permute-done.low = f32[16,8,256]{2,1,0:T(8,128)S(1)} collective-permute-done((f32[16,8,256]{2,1,0:T(8,128)}, f32[16,8,256]{2,1,0:T(8,128)S(1)}, u32[]{:S(2)}, u32[]{:S(2)}) %collective-permute-start) | collective-permute-done | bytes 131104 | tf_op jit(solution)/shard_map/ppermute | solution.py:705
  8.4 3.7 %collective-permute-start.2 = (f32[600,256]{1,0:T(8,128)S(1)}, f32[600,256]{1,0:T(8,128)S(1)}, u32[]{:S(2)}, u32[]{:S(2)}) collective-permute-start(f32[600,256]{1,0:T(8,128)S(1)} %get-tuple-element.40), channel_id=1, source_target_pairs={{0,252},{4,8},{8,4},{12,16},{16,12},{20,24},{24,20},{28,32},{32,28... | collective-permute-start | bytes 1843208 | tf_op jit(solution)/shard_map/ppermute | solution.py:714
  12.1 5.1 %collective-permute-start.3 = (f32[600,256]{1,0:T(8,128)S(1)}, f32[600,256]{1,0:T(8,128)S(1)}, u32[]{:S(2)}, u32[]{:S(2)}) collective-permute-start(f32[600,256]{1,0:T(8,128)S(1)} %get-tuple-element.41), channel_id=1, source_target_pairs={{0,4},{4,0},{8,12},{12,8},{16,20},{20,16},{24,28},{28,24},{32,36},... | collective-permute-start | bytes 1843208 | tf_op jit(solution)/shard_map/ppermute | solution.py:709
  17.3 3.0 %collective-permute-done.2.far = f32[600,256]{1,0:T(8,128)S(1)} collective-permute-done((f32[600,256]{1,0:T(8,128)S(1)}, f32[600,256]{1,0:T(8,128)S(1)}, u32[]{:S(2)}, u32[]{:S(2)}) %collective-permute-start.2) | collective-permute-done | bytes 614432 | tf_op jit(solution)/shard_map/ppermute | solution.py:714
  20.2 2.3 %shard_map.48 = (f32[6,80,256]{2,1,0:T(8,128)S(1)}, f32[7,80,256]{2,1,0:T(8,128)S(1)}, f32[6,80,256]{2,1,0:T(8,128)S(1)}, f32[6,80,256]{2,1,0:T(8,128)S(1)}, f32...) custom-call(f32[16,80,256]{2,1,0:T(8,128)S(1)} %get-tuple-element.38, ...), custom_call_target="tpu_custom_call" | custom-call | tf_op jit(solution)/shard_map/pallas_call | solution.py:136
  22.6 4.9 %collective-permute-start.5 = (f32[8,40,128]{2,1,0:T(8,128)S(1)}, f32[8,40,128]{2,1,0:T(8,128)S(1)}, u32[]{:S(2)}, u32[]{:S(2)}) collective-permute-start(f32[8,40,128]{2,1,0:T(8,128)S(1)} %get-tuple-element.43), channel_id=1, source_target_pairs={{0,4},{4,0},{8,12},{12,8},{16,20},{20,16},{24,28},{28,24},{32,36},... | collective-permute-start | bytes 491528 | tf_op jit(solution)/shard_map/ppermute | solution.py:709
  27.8 0.8 collective-permute-done.5.sib
  28.5 3.7 %collective-permute-done.4.far = f32[8,40,128]{2,1,0:T(8,128)S(1)} collective-permute-done((f32[8,40,128]{2,1,0:T(8,128)S(1)}, f32[8,40,128]{2,1,0:T(8,128)S(1)}, u32[]{:S(2)}, u32[]{:S(2)}) %collective-permute-start.4) | collective-permute-done | bytes 163872 | tf_op jit(solution)/shard_map/ppermute | solution.py:714
  32.6 1.1 %collective-permute-start.6 = (f32[56,128]{1,0:T(8,128)S(1)}, f32[56,128]{1,0:T(8,128)S(1)}, u32[]{:S(2)}, u32[]{:S(2)}) collective-permute-start(f32[56,128]{1,0:T(8,128)S(1)} %get-tuple-element.46), channel_id=1, source_target_pairs={{0,1},{1,2},{2,3},{3,0},{4,5},{5,6},{6,7},{7,4},{8,9},{9,10},{10,1... | collective-permute-start | bytes 86024 | tf_op jit(solution)/shard_map/ppermute | solution.py:705
  33.7 1.8 %collective-permute-start.7 = (f32[56,128]{1,0:T(8,128)S(1)}, f32[56,128]{1,0:T(8,128)S(1)}, u32[]{:S(2)}, u32[]{:S(2)}) collective-permute-start(f32[56,128]{1,0:T(8,128)S(1)} %get-tuple-element.47), channel_id=1, source_target_pairs={{0,3},{1,0},{2,1},{3,2},{4,7},{5,4},{6,5},{7,6},{8,11},{9,8},{10,9... | collective-permute-start | bytes 86024 | tf_op jit(solution)/shard_map/ppermute | solution.py:705
  35.5 1.1 %collective-permute-start.8 = (f32[40,128]{1,0:T(8,128)S(1)}, f32[40,128]{1,0:T(8,128)S(1)}, u32[]{:S(2)}, u32[]{:S(2)}) collective-permute-start(f32[40,128]{1,0:T(8,128)S(1)} %get-tuple-element.45.f2), channel_id=1, source_target_pairs={{0,2},{1,3},{2,0},{3,1},{4,6},{5,7},{6,4},{7,5},{8,10},{9,11},{10,... | collective-permute-start | bytes 61448 | tf_op jit(solution)/shard_map/ppermute | solution.py:705
  36.6 3.0 %collective-permute-done.8.far = f32[40,128]{1,0:T(8,128)S(1)} collective-permute-done((f32[40,128]{1,0:T(8,128)S(1)}, f32[40,128]{1,0:T(8,128)S(1)}, u32[]{:S(2)}, u32[]{:S(2)}) %collective-permute-start.8) | collective-permute-done | bytes 20512 | tf_op jit(solution)/shard_map/ppermute | solution.py:705
  39.9 5.1 %collective-permute-start.9 = (f32[240,128]{1,0:T(8,128)S(1)}, f32[240,128]{1,0:T(8,128)S(1)}, u32[]{:S(2)}, u32[]{:S(2)}) collective-permute-start(f32[240,128]{1,0:T(8,128)S(1)} %get-tuple-element.50.msg), channel_id=1, source_target_pairs={{0,4},{4,0},{8,12},{12,8},{16,20},{20,16},{24,28},{28,24},{32,36},... | collective-permute-start | bytes 368648 | tf_op jit(solution)/shard_map/ppermute | solution.py:709
  44.9 1.0 %collective-permute-done.9.sib = f32[240,128]{1,0:T(8,128)S(1)} collective-permute-done((f32[240,128]{1,0:T(8,128)S(1)}, f32[240,128]{1,0:T(8,128)S(1)}, u32[]{:S(2)}, u32[]{:S(2)}) %collective-permute-start.9) | collective-permute-done | bytes 122912 | tf_op jit(solution)/shard_map/ppermute | solution.py:709
  46.3 4.8 %collective-permute-done.10.near = f32[384,128]{1,0:T(8,128)S(1)} collective-permute-done((f32[384,128]{1,0:T(8,128)S(1)}, f32[384,128]{1,0:T(8,128)S(1)}, u32[]{:S(2)}, u32[]{:S(2)}) %collective-permute-start.10) | collective-permute-done | bytes 196640 | tf_op jit(solution)/shard_map/ppermute | solution.py:714
  51.1 3.7 %collective-permute-start.11 = (f32[384,128]{1,0:T(8,128)S(1)}, f32[384,128]{1,0:T(8,128)S(1)}, u32[]{:S(2)}, u32[]{:S(2)}) collective-permute-start(f32[384,128]{1,0:T(8,128)S(1)} %collective-permute-done.10.near), channel_id=1, source_target_pairs={{0,4},{4,0},{8,12},{12,8},{16,20},{20,16},{24,28},{28,24},{32,36},... | collective-permute-start | bytes 589832 | tf_op jit(solution)/shard_map/ppermute | solution.py:709
  54.8 1.1 %collective-permute-done.11.other = f32[384,128]{1,0:T(8,128)S(1)} collective-permute-done((f32[384,128]{1,0:T(8,128)S(1)}, f32[384,128]{1,0:T(8,128)S(1)}, u32[]{:S(2)}, u32[]{:S(2)}) %collective-permute-start.11) | collective-permute-done | bytes 196640 | tf_op jit(solution)/shard_map/ppermute | solution.py:709
  56.5 14.9 %all_to_all.5.mine = f32[32,2,8,128]{3,2,1,0:T(8,128)S(1)} all-to-all(f32[32,2,8,128]{3,2,1,0:T(8,128)S(1)} %shard_map.55), channel_id=1, replica_groups={{0,8,16,24,32,40,48,56,64,72,80,88,96,104,112,120,128,136,144,152,160,1..., dimensions={0} | all-to-all | bytes 524288 | tf_op jit(solution)/shard_map/all_to_all | solution.py:764
  71.4 3.0 %collective-permute-start.12 = (f32[32,2,8,128]{3,2,1,0:T(8,128)S(1)}, f32[32,2,8,128]{3,2,1,0:T(8,128)S(1)}, u32[]{:S(2)}, u32[]{:S(2)}) collective-permute-start(f32[32,2,8,128]{3,2,1,0:T(8,128)S(1)} %all_to_all.5.mine), channel_id=1, source_target_pairs={{0,4},{4,0},{8,12},{12,8},{16,20},{20,16},{24,28},{28,24},{32,36},... | collective-permute-start | bytes 786440 | tf_op jit(solution)/shard_map/ppermute | solution.py:709
  74.4 1.5 %collective-permute-start.13 = (f32[32,128]{1,0:T(8,128)S(1)}, f32[32,128]{1,0:T(8,128)S(1)}, u32[]{:S(2)}, u32[]{:S(2)}) collective-permute-start(f32[32,128]{1,0:T(8,128)S(1)} %get-tuple-element.55), channel_id=1, source_target_pairs={{0,252},{4,8},{8,4},{12,16},{16,12},{20,24},{24,20},{28,32},{32,28... | collective-permute-start | bytes 49160 | tf_op jit(solution)/shard_map/ppermute | solution.py:714
  75.9 2.0 %shard_map.56.e2 = f32[192,128]{1,0:T(8,128)S(1)} custom-call(f32[32,2,8,128]{3,2,1,0:T(8,128)S(1)} %all_to_all.5.mine, f32[32,2,8,128]{3,2,1,0:T(8,128)S(1)} %collective-permute-done.12.theirs), custom_call_target="tpu_custom_call" | custom-call | tf_op jit(solution)/shard_map/pallas_call | solution.py:136
  78.2 3.0 %collective-permute-start.14 = (f32[64,128]{1,0:T(8,128)S(1)}, f32[64,128]{1,0:T(8,128)S(1)}, u32[]{:S(2)}, u32[]{:S(2)}) collective-permute-start(f32[64,128]{1,0:T(8,128)S(1)} %shard_map.57.a.e2), channel_id=1, source_target_pairs={{0,4},{4,0},{8,12},{12,8},{16,20},{20,16},{24,28},{28,24},{32,36},... | collective-permute-start | bytes 98312 | tf_op jit(solution)/shard_map/ppermute | solution.py:709
  81.2 0.9 collective-permute-done.14.b.e2sib
  82.1 3.7 %collective-permute-done.15.far = f32[2,64,128]{2,1,0:T(8,128)S(1)} collective-permute-done((f32[2,64,128]{2,1,0:T(8,128)S(1)}, f32[2,64,128]{2,1,0:T(8,128)S(1)}, u32[]{:S(2)}, u32[]{:S(2)}) %collective-permute-start.15) | collective-permute-done | bytes 65568 | tf_op jit(solution)/shard_map/ppermute | solution.py:714
  85.8 0.7 shard_map.59
  86.4 3.7 %collective-permute-start.16 = (f32[40,128]{1,0:T(8,128)S(1)}, f32[40,128]{1,0:T(8,128)S(1)}, u32[]{:S(2)}, u32[]{:S(2)}) collective-permute-start(f32[40,128]{1,0:T(8,128)S(1)} %get-tuple-element.60), channel_id=1, source_target_pairs={{0,4},{4,0},{8,12},{12,8},{16,20},{20,16},{24,28},{28,24},{32,36},... | collective-permute-start | bytes 61448 | tf_op jit(solution)/shard_map/ppermute | solution.py:709
  90.2 0.8 collective-permute-done.16.other
  91.0 2.2 %shard_map.60 = f32[4,64,256]{2,1,0:T(8,128)} custom-call(f32[2,40,128]{2,1,0:T(8,128)S(1)} %get-tuple-element.58.e1, f32[40,128]{1,0:T(8,128)S(1)} %get-tuple-element.59.edge, f32[40,128]{1,0:T(8,128)S(1)} %collective-permute-done.16.other, f32[8,40,128]{2,1,0:T(8,128)S(1)} %collective-permute-done.4.far, f32[8,40,128]{2,1,0:T(8,128)S(1)} %collective-permute-done.5.sib, ...), custom_call_target="tpu_custom_call" | custom-call | tf_op jit(solution)/shard_map/pallas_call | solution.py:136
  (19 shorter events, 2.6 us)
Async XLA Ops:
  1.6 6.2 %collective-permute-start = (f32[16,8,256]{2,1,0:T(8,128)}, f32[16,8,256]{2,1,0:T(8,128)S(1)}, u32[]{:S(2)}, u32[]{:S(2)}) collective-permute-start(f32[16,8,256]{2,1,0:T(8,128)} %get-tuple-element.36), channel_id=1, source_target_pairs={{0,1},{1,2},{2,3},{3,0},{4,5},{5,6},{6,7},{7,4},{8,9},{9,10},{10,1... | collective-permute-start | bytes 393224 | tf_op jit(solution)/shard_map/ppermute | solution.py:705
  3.8 4.0 %collective-permute-start.1 = (f32[16,8,256]{2,1,0:T(8,128)}, f32[16,8,256]{2,1,0:T(8,128)S(1)}, u32[]{:S(2)}, u32[]{:S(2)}) collective-permute-start(f32[16,8,256]{2,1,0:T(8,128)} %get-tuple-element.37), channel_id=1, source_target_pairs={{0,3},{1,0},{2,1},{3,2},{4,7},{5,4},{6,5},{7,6},{8,11},{9,8},{10,9... | collective-permute-start | bytes 393224 | tf_op jit(solution)/shard_map/ppermute | solution.py:705
  8.4 11.8 %collective-permute-start.2 = (f32[600,256]{1,0:T(8,128)S(1)}, f32[600,256]{1,0:T(8,128)S(1)}, u32[]{:S(2)}, u32[]{:S(2)}) collective-permute-start(f32[600,256]{1,0:T(8,128)S(1)} %get-tuple-element.40), channel_id=1, source_target_pairs={{0,252},{4,8},{8,4},{12,16},{16,12},{20,24},{24,20},{28,32},{32,28... | collective-permute-start | bytes 1843208 | tf_op jit(solution)/shard_map/ppermute | solution.py:714
  12.1 8.1 %collective-permute-start.3 = (f32[600,256]{1,0:T(8,128)S(1)}, f32[600,256]{1,0:T(8,128)S(1)}, u32[]{:S(2)}, u32[]{:S(2)}) collective-permute-start(f32[600,256]{1,0:T(8,128)S(1)} %get-tuple-element.41), channel_id=1, source_target_pairs={{0,4},{4,0},{8,12},{12,8},{16,20},{20,16},{24,28},{28,24},{32,36},... | collective-permute-start | bytes 1843208 | tf_op jit(solution)/shard_map/ppermute | solution.py:709
  22.6 6.0 %collective-permute-start.5 = (f32[8,40,128]{2,1,0:T(8,128)S(1)}, f32[8,40,128]{2,1,0:T(8,128)S(1)}, u32[]{:S(2)}, u32[]{:S(2)}) collective-permute-start(f32[8,40,128]{2,1,0:T(8,128)S(1)} %get-tuple-element.43), channel_id=1, source_target_pairs={{0,4},{4,0},{8,12},{12,8},{16,20},{20,16},{24,28},{28,24},{32,36},... | collective-permute-start | bytes 491528 | tf_op jit(solution)/shard_map/ppermute | solution.py:709
  27.5 4.7 %collective-permute-start.4 = (f32[8,40,128]{2,1,0:T(8,128)S(1)}, f32[8,40,128]{2,1,0:T(8,128)S(1)}, u32[]{:S(2)}, u32[]{:S(2)}) collective-permute-start(f32[8,40,128]{2,1,0:T(8,128)S(1)} %get-tuple-element.42.own), channel_id=1, source_target_pairs={{0,252},{4,8},{8,4},{12,16},{16,12},{20,24},{24,20},{28,32},{32,28... | collective-permute-start | bytes 491528 | tf_op jit(solution)/shard_map/ppermute | solution.py:714
  32.6 7.0 %collective-permute-start.6 = (f32[56,128]{1,0:T(8,128)S(1)}, f32[56,128]{1,0:T(8,128)S(1)}, u32[]{:S(2)}, u32[]{:S(2)}) collective-permute-start(f32[56,128]{1,0:T(8,128)S(1)} %get-tuple-element.46), channel_id=1, source_target_pairs={{0,1},{1,2},{2,3},{3,0},{4,5},{5,6},{6,7},{7,4},{8,9},{9,10},{10,1... | collective-permute-start | bytes 86024 | tf_op jit(solution)/shard_map/ppermute | solution.py:705
  33.7 6.0 %collective-permute-start.7 = (f32[56,128]{1,0:T(8,128)S(1)}, f32[56,128]{1,0:T(8,128)S(1)}, u32[]{:S(2)}, u32[]{:S(2)}) collective-permute-start(f32[56,128]{1,0:T(8,128)S(1)} %get-tuple-element.47), channel_id=1, source_target_pairs={{0,3},{1,0},{2,1},{3,2},{4,7},{5,4},{6,5},{7,6},{8,11},{9,8},{10,9... | collective-permute-start | bytes 86024 | tf_op jit(solution)/shard_map/ppermute | solution.py:705
  35.5 4.1 %collective-permute-start.8 = (f32[40,128]{1,0:T(8,128)S(1)}, f32[40,128]{1,0:T(8,128)S(1)}, u32[]{:S(2)}, u32[]{:S(2)}) collective-permute-start(f32[40,128]{1,0:T(8,128)S(1)} %get-tuple-element.45.f2), channel_id=1, source_target_pairs={{0,2},{1,3},{2,0},{3,1},{4,6},{5,7},{6,4},{7,5},{8,10},{9,11},{10,... | collective-permute-start | bytes 61448 | tf_op jit(solution)/shard_map/ppermute | solution.py:705
  39.9 6.1 %collective-permute-start.9 = (f32[240,128]{1,0:T(8,128)S(1)}, f32[240,128]{1,0:T(8,128)S(1)}, u32[]{:S(2)}, u32[]{:S(2)}) collective-permute-start(f32[240,128]{1,0:T(8,128)S(1)} %get-tuple-element.50.msg), channel_id=1, source_target_pairs={{0,4},{4,0},{8,12},{12,8},{16,20},{20,16},{24,28},{28,24},{32,36},... | collective-permute-start | bytes 368648 | tf_op jit(solution)/shard_map/ppermute | solution.py:709
  45.9 5.2 %collective-permute-start.10 = (f32[384,128]{1,0:T(8,128)S(1)}, f32[384,128]{1,0:T(8,128)S(1)}, u32[]{:S(2)}, u32[]{:S(2)}) collective-permute-start(f32[384,128]{1,0:T(8,128)S(1)} %shard_map.52), channel_id=1, source_target_pairs={{0,252},{4,8},{8,4},{12,16},{16,12},{20,24},{24,20},{28,32},{32,28... | collective-permute-start | bytes 589832 | tf_op jit(solution)/shard_map/ppermute | solution.py:714
  51.1 4.8 %collective-permute-start.11 = (f32[384,128]{1,0:T(8,128)S(1)}, f32[384,128]{1,0:T(8,128)S(1)}, u32[]{:S(2)}, u32[]{:S(2)}) collective-permute-start(f32[384,128]{1,0:T(8,128)S(1)} %collective-permute-done.10.near), channel_id=1, source_target_pairs={{0,4},{4,0},{8,12},{12,8},{16,20},{20,16},{24,28},{28,24},{32,36},... | collective-permute-start | bytes 589832 | tf_op jit(solution)/shard_map/ppermute | solution.py:709
  71.4 4.5 %collective-permute-start.12 = (f32[32,2,8,128]{3,2,1,0:T(8,128)S(1)}, f32[32,2,8,128]{3,2,1,0:T(8,128)S(1)}, u32[]{:S(2)}, u32[]{:S(2)}) collective-permute-start(f32[32,2,8,128]{3,2,1,0:T(8,128)S(1)} %all_to_all.5.mine), channel_id=1, source_target_pairs={{0,4},{4,0},{8,12},{12,8},{16,20},{20,16},{24,28},{28,24},{32,36},... | collective-permute-start | bytes 786440 | tf_op jit(solution)/shard_map/ppermute | solution.py:709
  74.4 3.6 %collective-permute-start.13 = (f32[32,128]{1,0:T(8,128)S(1)}, f32[32,128]{1,0:T(8,128)S(1)}, u32[]{:S(2)}, u32[]{:S(2)}) collective-permute-start(f32[32,128]{1,0:T(8,128)S(1)} %get-tuple-element.55), channel_id=1, source_target_pairs={{0,252},{4,8},{8,4},{12,16},{16,12},{20,24},{24,20},{28,32},{32,28... | collective-permute-start | bytes 49160 | tf_op jit(solution)/shard_map/ppermute | solution.py:714
  78.2 3.9 %collective-permute-start.14 = (f32[64,128]{1,0:T(8,128)S(1)}, f32[64,128]{1,0:T(8,128)S(1)}, u32[]{:S(2)}, u32[]{:S(2)}) collective-permute-start(f32[64,128]{1,0:T(8,128)S(1)} %shard_map.57.a.e2), channel_id=1, source_target_pairs={{0,4},{4,0},{8,12},{12,8},{16,20},{20,16},{24,28},{28,24},{32,36},... | collective-permute-start | bytes 98312 | tf_op jit(solution)/shard_map/ppermute | solution.py:709
  82.1 3.7 %collective-permute-start.15 = (f32[2,64,128]{2,1,0:T(8,128)S(1)}, f32[2,64,128]{2,1,0:T(8,128)S(1)}, u32[]{:S(2)}, u32[]{:S(2)}) collective-permute-start(f32[2,64,128]{2,1,0:T(8,128)S(1)} %shard_map.58), channel_id=1, source_target_pairs={{0,252},{4,8},{8,4},{12,16},{16,12},{20,24},{24,20},{28,32},{32,28... | collective-permute-start | bytes 196616 | tf_op jit(solution)/shard_map/ppermute | solution.py:714
  86.4 4.6 %collective-permute-start.16 = (f32[40,128]{1,0:T(8,128)S(1)}, f32[40,128]{1,0:T(8,128)S(1)}, u32[]{:S(2)}, u32[]{:S(2)}) collective-permute-start(f32[40,128]{1,0:T(8,128)S(1)} %get-tuple-element.60), channel_id=1, source_target_pairs={{0,4},{4,0},{8,12},{12,8},{16,20},{20,16},{24,28},{28,24},{32,36},... | collective-permute-start | bytes 61448 | tf_op jit(solution)/shard_map/ppermute | solution.py:709

commit v10 on v6

--- a/solution.py
+++ b/solution.py
@@ -242,14 +242,19 @@
     return SIG[0] + c1[q, here, :] + c1[q + 1, here, :] + k2 + h2 + k3 + roll(k3, -1, 1)
 
 
-def fine_pre_kernel(own, coef1, far, sib, f, c1, c2, c3, g, u2, w1, out_far, out_sib, f1, u1, res, scr):
+def fine_pre_kernel(own, coef1, far, sib, f_out, c1_out, c2_out, c3_out, g, u2, w1, out_far, out_sib,
+                    f, c1, c2, c3, f1, u1, res, scr, sems):
     below, above = sides(far, sib)
+    copies = []
     for a, ref in enumerate((f, c1, c2, c3)):
         here = slice(80 * a, 80 * a + 80)
         ref[0] = below(here)
         ref[1:5] = own[4 * a : 4 * a + 4]
         ref[5] = above(here)
-    c1[6] = above(slice(320, 400))
+        if a == 1:
+            ref[6] = above(slice(320, 400))
+        copies.append(pltpu.make_async_copy(ref, (f_out, c1_out, c2_out, c3_out)[a], sems.at[a]))
+        copies[a].start()
     u1[0] = below(slice(400, 480))
     u1[7] = above(slice(400, 480))
 
@@ -311,6 +316,8 @@
         out[5] = u2[plane, 0:40, 128:256]
         out[6] = u2[plane, 40:80, 0:128]
         out[7] = u2[plane, 40:80, 128:256]
+    for copy in copies:
+        copy.wait()
 
 
 def coarse_coef_kernel(w1, out, scr):
@@ -493,7 +500,7 @@
     return lax.rem(j + n, n)
 
 
-STEP = 8
+STEP = 32
 THREE, FOUR = (32, 4), (16, 2)
 
 
@@ -727,11 +734,14 @@
     )(jnp.concatenate(inputs, axis=0), low, high)
     far, sib = across(far), sibling(sib)
 
-    f, c1, c2, c3, g, u2, w1, out_far, out_sib, _ = call(
+    f, c1, c2, c3, g, u2, w1, out_far, out_sib = call(
         fine_pre_kernel,
         [(6,) + big, (7,) + big, (6,) + big, (6,) + big, (6,) + big, (8,) + big]
-        + [(18, 40, 128), (8, 40, 128), (8, 40, 128), (2, 40, 128)],
-        [(8,) + big, (4,) + big, (160, 128)],
+        + [(18, 40, 128), (8, 40, 128), (8, 40, 128)],
+        [(6,) + big, (7,) + big, (6,) + big, (6,) + big]
+        + [(2, 40, 128), (8,) + big, (4,) + big, (160, 128), pltpu.SemaphoreType.DMA((4,))],
+        out_places={k: pltpu.HBM for k in range(4)},
+        limit=6,
     )(own, coef1, far, sib)
     far1, sib1 = across(out_far), sibling(out_sib)
     (coefs,) = call(coarse_coef_kernel, [(32, 128)], [(80, 128)])(w1)

time: 96.1 us -> 95 us (0.989)
  no operation moved by 1% of the time
where the time goes in v10:
time: 95 us; the launch traced here: 94.7 us
  starting transfers between devices  46.3 us (49%)
  waiting for transfers between devices  30.4 us (32%)
  Pallas kernels  13.3 us (14%)
  local copies, waits for them, and re-layouts  3.24 us (3%)
  other arithmetic  1.26 us (1%)
    ppermute x7, starting transfers between devices, sibling(): lax.ppermute(x, 'wide', [(i, i ^ 1) for i in range(lax.axis_size('wide'))])  26.2 us
    ppermute x5, waiting for transfers between devices, across(): lax.ppermute(x, 'wide', [(i, (i + 1 if i % 2 else i - 1) % count) for i i...  19.9 us
    pallas_call x14, Pallas kernels, run(): pl.pallas_call(kernel, out_shape=[jax.ShapeDtypeStruct(s, F32) for s in o...  13.3 us
    ppermute x5, starting transfers between devices, shift(): return lax.ppermute(x, axis, [(i, (i + by) % count) for i in range(count)])  7.64 us
    ppermute x5, starting transfers between devices, across(): lax.ppermute(x, 'wide', [(i, (i + 1 if i % 2 else i - 1) % count) for i i...  7.48 us
    all_to_all x1, starting transfers between devices, body(): lax.all_to_all(send, 'wide', split_axis=0, concat_axis=0, tiled=True, axi...  4.99 us
    ppermute x7, waiting for transfers between devices, sibling(): lax.ppermute(x, 'wide', [(i, i ^ 1) for i in range(lax.axis_size('wide'))])  4.55 us
    ppermute x5, waiting for transfers between devices, shift(): return lax.ppermute(x, axis, [(i, (i + by) % count) for i in range(count)])  4.2 us
  transfers between devices with their start and end apart: 18, of which 13 were waited for; matrix products, arithmetic and copies ran while one was open for 1% of the time, Pallas kernels for 3%

profile of v10, /device:TPU:1, one launch (start us, length us, event | category | flops | bytes accessed | tf_op | source)
XLA Modules:
  0.0 94.7 jit_solution(1905075555012626569)
XLA Ops:
  0.0 1.6 %shard_map.46 = (f32[16,8,256]{2,1,0:T(8,128)}, f32[16,8,256]{2,1,0:T(8,128)}) custom-call(f32[4,64,256]{2,1,0:T(8,128)} %f.1, f32[4,64,256]{2,1,0:T(8,128)} %c1.1, f32[4,64,256]{2,1,0:T(8,128)} %c2.1, f32[4,64,256]{2,1,0:T(8,128)} %c3.1), custom_call_target="tpu_custom_call" | custom-call | tf_op jit(solution)/shard_map/pallas_call | solution.py:136
  1.6 2.2 %collective-permute-start = (f32[16,8,256]{2,1,0:T(8,128)}, f32[16,8,256]{2,1,0:T(8,128)S(1)}, u32[]{:S(2)}, u32[]{:S(2)}) collective-permute-start(f32[16,8,256]{2,1,0:T(8,128)} %get-tuple-element.38), channel_id=1, source_target_pairs={{0,1},{1,2},{2,3},{3,0},{4,5},{5,6},{6,7},{7,4},{8,9},{9,10},{10,1... | collective-permute-start | bytes 393224 | tf_op jit(solution)/shard_map/ppermute | solution.py:705
  3.8 1.5 %collective-permute-start.1 = (f32[16,8,256]{2,1,0:T(8,128)}, f32[16,8,256]{2,1,0:T(8,128)S(1)}, u32[]{:S(2)}, u32[]{:S(2)}) collective-permute-start(f32[16,8,256]{2,1,0:T(8,128)} %get-tuple-element.39), channel_id=1, source_target_pairs={{0,3},{1,0},{2,1},{3,2},{4,7},{5,4},{6,5},{7,6},{8,11},{9,8},{10,9... | collective-permute-start | bytes 393224 | tf_op jit(solution)/shard_map/ppermute | solution.py:705
  5.4 1.3 %pad_maximum_fusion.inner = f32[16,64,256]{2,1,0:T(8,128)S(1)} fusion(f32[4,64,256]{2,1,0:T(8,128)} %c3.1, f32[4,64,256]{2,1,0:T(8,128)} %c2.1, f32[4,64,256]{2,1,0:T(8,128)} %c1.1, f32[4,64,256]{2,1,0:T(8,128)} %f.1), kind=kLoop, calls=%fused_computation | loop fusion | flops 786432 | bytes 2097152 | tf_op jit(solution)/shard_map/concatenate | solution.py:734
  6.6 1.2 %collective-permute-done.low = f32[16,8,256]{2,1,0:T(8,128)S(1)} collective-permute-done((f32[16,8,256]{2,1,0:T(8,128)}, f32[16,8,256]{2,1,0:T(8,128)S(1)}, u32[]{:S(2)}, u32[]{:S(2)}) %collective-permute-start) | collective-permute-done | bytes 131104 | tf_op jit(solution)/shard_map/ppermute | solution.py:705
  8.4 3.7 %collective-permute-start.2 = (f32[600,256]{1,0:T(8,128)S(1)}, f32[600,256]{1,0:T(8,128)S(1)}, u32[]{:S(2)}, u32[]{:S(2)}) collective-permute-start(f32[600,256]{1,0:T(8,128)S(1)} %get-tuple-element.42), channel_id=1, source_target_pairs={{0,252},{4,8},{8,4},{12,16},{16,12},{20,24},{24,20},{28,32},{32,28... | collective-permute-start | bytes 1843208 | tf_op jit(solution)/shard_map/ppermute | solution.py:714
  12.1 5.1 %collective-permute-start.3 = (f32[600,256]{1,0:T(8,128)S(1)}, f32[600,256]{1,0:T(8,128)S(1)}, u32[]{:S(2)}, u32[]{:S(2)}) collective-permute-start(f32[600,256]{1,0:T(8,128)S(1)} %get-tuple-element.43), channel_id=1, source_target_pairs={{0,4},{4,0},{8,12},{12,8},{16,20},{20,16},{24,28},{28,24},{32,36},... | collective-permute-start | bytes 1843208 | tf_op jit(solution)/shard_map/ppermute | solution.py:709
  17.3 3.0 %collective-permute-done.2.far = f32[600,256]{1,0:T(8,128)S(1)} collective-permute-done((f32[600,256]{1,0:T(8,128)S(1)}, f32[600,256]{1,0:T(8,128)S(1)}, u32[]{:S(2)}, u32[]{:S(2)}) %collective-permute-start.2) | collective-permute-done | bytes 614432 | tf_op jit(solution)/shard_map/ppermute | solution.py:714
  20.2 3.5 %shard_map.48 = (f32[6,80,256]{2,1,0:T(8,128)S(1)}, f32[7,80,256]{2,1,0:T(8,128)S(1)}, f32[6,80,256]{2,1,0:T(8,128)S(1)}, f32[6,80,256]{2,1,0:T(8,128)S(1)}, f32...) custom-call(f32[16,80,256]{2,1,0:T(8,128)S(1)} %get-tuple-element.40, ...), custom_call_target="tpu_custom_call" | custom-call | tf_op jit(solution)/shard_map/pallas_call | solution.py:136
  24.5 4.8 %collective-permute-start.5 = (f32[8,40,128]{2,1,0:T(8,128)S(1)}, f32[8,40,128]{2,1,0:T(8,128)S(1)}, u32[]{:S(2)}, u32[]{:S(2)}) collective-permute-start(f32[8,40,128]{2,1,0:T(8,128)S(1)} %get-tuple-element.45), channel_id=1, source_target_pairs={{0,4},{4,0},{8,12},{12,8},{16,20},{20,16},{24,28},{28,24},{32,36},... | collective-permute-start | bytes 491528 | tf_op jit(solution)/shard_map/ppermute | solution.py:709
  30.4 3.7 %collective-permute-done.4.far = f32[8,40,128]{2,1,0:T(8,128)S(1)} collective-permute-done((f32[8,40,128]{2,1,0:T(8,128)S(1)}, f32[8,40,128]{2,1,0:T(8,128)S(1)}, u32[]{:S(2)}, u32[]{:S(2)}) %collective-permute-start.4) | collective-permute-done | bytes 163872 | tf_op jit(solution)/shard_map/ppermute | solution.py:714
  35.1 1.0 %collective-permute-start.6 = (f32[56,128]{1,0:T(8,128)S(1)}, f32[56,128]{1,0:T(8,128)S(1)}, u32[]{:S(2)}, u32[]{:S(2)}) collective-permute-start(f32[56,128]{1,0:T(8,128)S(1)} %get-tuple-element.48), channel_id=1, source_target_pairs={{0,1},{1,2},{2,3},{3,0},{4,5},{5,6},{6,7},{7,4},{8,9},{9,10},{10,1... | collective-permute-start | bytes 86024 | tf_op jit(solution)/shard_map/ppermute | solution.py:705
  36.1 1.7 %collective-permute-start.7 = (f32[56,128]{1,0:T(8,128)S(1)}, f32[56,128]{1,0:T(8,128)S(1)}, u32[]{:S(2)}, u32[]{:S(2)}) collective-permute-start(f32[56,128]{1,0:T(8,128)S(1)} %get-tuple-element.49), channel_id=1, source_target_pairs={{0,3},{1,0},{2,1},{3,2},{4,7},{5,4},{6,5},{7,6},{8,11},{9,8},{10,9... | collective-permute-start | bytes 86024 | tf_op jit(solution)/shard_map/ppermute | solution.py:705
  37.8 1.2 %collective-permute-start.8 = (f32[40,128]{1,0:T(8,128)S(1)}, f32[40,128]{1,0:T(8,128)S(1)}, u32[]{:S(2)}, u32[]{:S(2)}) collective-permute-start(f32[40,128]{1,0:T(8,128)S(1)} %get-tuple-element.47.f2), channel_id=1, source_target_pairs={{0,2},{1,3},{2,0},{3,1},{4,6},{5,7},{6,4},{7,5},{8,10},{9,11},{10,... | collective-permute-start | bytes 61448 | tf_op jit(solution)/shard_map/ppermute | solution.py:705
  39.0 3.0 %collective-permute-done.8.far = f32[40,128]{1,0:T(8,128)S(1)} collective-permute-done((f32[40,128]{1,0:T(8,128)S(1)}, f32[40,128]{1,0:T(8,128)S(1)}, u32[]{:S(2)}, u32[]{:S(2)}) %collective-permute-start.8) | collective-permute-done | bytes 20512 | tf_op jit(solution)/shard_map/ppermute | solution.py:705
  42.2 5.2 %collective-permute-start.9 = (f32[240,128]{1,0:T(8,128)S(1)}, f32[240,128]{1,0:T(8,128)S(1)}, u32[]{:S(2)}, u32[]{:S(2)}) collective-permute-start(f32[240,128]{1,0:T(8,128)S(1)} %get-tuple-element.52.msg), channel_id=1, source_target_pairs={{0,4},{4,0},{8,12},{12,8},{16,20},{20,16},{24,28},{28,24},{32,36},... | collective-permute-start | bytes 368648 | tf_op jit(solution)/shard_map/ppermute | solution.py:709
  47.3 1.0 %collective-permute-done.9.sib = f32[240,128]{1,0:T(8,128)S(1)} collective-permute-done((f32[240,128]{1,0:T(8,128)S(1)}, f32[240,128]{1,0:T(8,128)S(1)}, u32[]{:S(2)}, u32[]{:S(2)}) %collective-permute-start.9) | collective-permute-done | bytes 122912 | tf_op jit(solution)/shard_map/ppermute | solution.py:709
  48.8 4.8 %collective-permute-done.10.near = f32[384,128]{1,0:T(8,128)S(1)} collective-permute-done((f32[384,128]{1,0:T(8,128)S(1)}, f32[384,128]{1,0:T(8,128)S(1)}, u32[]{:S(2)}, u32[]{:S(2)}) %collective-permute-start.10) | collective-permute-done | bytes 196640 | tf_op jit(solution)/shard_map/ppermute | solution.py:714
  53.5 3.7 %collective-permute-start.11 = (f32[384,128]{1,0:T(8,128)S(1)}, f32[384,128]{1,0:T(8,128)S(1)}, u32[]{:S(2)}, u32[]{:S(2)}) collective-permute-start(f32[384,128]{1,0:T(8,128)S(1)} %collective-permute-done.10.near), channel_id=1, source_target_pairs={{0,4},{4,0},{8,12},{12,8},{16,20},{20,16},{24,28},{28,24},{32,36},... | collective-permute-start | bytes 589832 | tf_op jit(solution)/shard_map/ppermute | solution.py:709
  57.2 1.1 %collective-permute-done.11.other = f32[384,128]{1,0:T(8,128)S(1)} collective-permute-done((f32[384,128]{1,0:T(8,128)S(1)}, f32[384,128]{1,0:T(8,128)S(1)}, u32[]{:S(2)}, u32[]{:S(2)}) %collective-permute-start.11) | collective-permute-done | bytes 196640 | tf_op jit(solution)/shard_map/ppermute | solution.py:709
  58.6 1.0 %shard_map.55 = f32[32,2,8,128]{3,2,1,0:T(8,128)} custom-call(f32[21,64,128]{2,1,0:T(8,128)S(1)} %get-tuple-element.54.w.win, f32[4,64,128]{2,1,0:T(8,128)S(1)} %get-tuple-element.55.u2, f32[3,8,128]{2,1,0:T(8,128)S(1)} %shard_map.53.tiles), custom_call_target="tpu_custom_call" | custom-call | tf_op jit(solution)/shard_map/pallas_call | solution.py:136
  59.6 5.0 %all-to-all-start = ((f32[32,2,8,128]{3,2,1,0:T(8,128)}), f32[32,2,8,128]{3,2,1,0:T(8,128)S(1)}, u32[]{:S(2)}, u32[]{:S(2)}) async-start(f32[32,2,8,128]{3,2,1,0:T(8,128)} %shard_map.55), calls=%async_computation | async-start | bytes 524288 | tf_op jit(solution)/shard_map/all_to_all | solution.py:768
  64.6 1.9 %collective-permute-start.12 = (f32[32,128]{1,0:T(8,128)S(1)}, f32[32,128]{1,0:T(8,128)S(1)}, u32[]{:S(2)}, u32[]{:S(2)}) collective-permute-start(f32[32,128]{1,0:T(8,128)S(1)} %get-tuple-element.57), channel_id=1, source_target_pairs={{0,252},{4,8},{8,4},{12,16},{16,12},{20,24},{24,20},{28,32},{32,28... | collective-permute-start | bytes 49160 | tf_op jit(solution)/shard_map/ppermute | solution.py:714
  66.5 6.4 %collective-permute-done.12.late = f32[32,128]{1,0:T(8,128)S(1)} collective-permute-done((f32[32,128]{1,0:T(8,128)S(1)}, f32[32,128]{1,0:T(8,128)S(1)}, u32[]{:S(2)}, u32[]{:S(2)}) %collective-permute-start.12) | collective-permute-done | bytes 16416 | tf_op jit(solution)/shard_map/ppermute | solution.py:714
  73.0 1.7 %all-to-all-done.mine = f32[32,2,8,128]{3,2,1,0:T(8,128)S(1)} async-done(((f32[32,2,8,128]{3,2,1,0:T(8,128)}), f32[32,2,8,128]{3,2,1,0:T(8,128)S(1)}, u32[]{:S(2)}, u32[]{:S(2)}) %all-to-all-start) | async-done | bytes 262176 | tf_op jit(solution)/shard_map/all_to_all | solution.py:768
  74.7 3.3 %collective-permute-start.13 = (f32[32,2,8,128]{3,2,1,0:T(8,128)S(1)}, f32[32,2,8,128]{3,2,1,0:T(8,128)S(1)}, u32[]{:S(2)}, u32[]{:S(2)}) collective-permute-start(f32[32,2,8,128]{3,2,1,0:T(8,128)S(1)} %all-to-all-done.mine), channel_id=1, source_target_pairs={{0,4},{4,0},{8,12},{12,8},{16,20},{20,16},{24,28},{28,24},{32,36},... | collective-permute-start | bytes 786440 | tf_op jit(solution)/shard_map/ppermute | solution.py:709
  79.2 2.0 %shard_map.56.e2 = f32[192,128]{1,0:T(8,128)S(1)} custom-call(f32[32,2,8,128]{3,2,1,0:T(8,128)S(1)} %all-to-all-done.mine, f32[32,2,8,128]{3,2,1,0:T(8,128)S(1)} %collective-permute-done.13.theirs), custom_call_target="tpu_custom_call" | custom-call | tf_op jit(solution)/shard_map/pallas_call | solution.py:136
  81.5 1.8 %collective-permute-start.15 = (f32[2,64,128]{2,1,0:T(8,128)S(1)}, f32[2,64,128]{2,1,0:T(8,128)S(1)}, u32[]{:S(2)}, u32[]{:S(2)}) collective-permute-start(f32[2,64,128]{2,1,0:T(8,128)S(1)} %shard_map.57.e2), channel_id=1, source_target_pairs={{0,252},{4,8},{8,4},{12,16},{16,12},{20,24},{24,20},{28,32},{32,28... | collective-permute-start | bytes 196616 | tf_op jit(solution)/shard_map/ppermute | solution.py:714
  83.3 2.0 %collective-permute-done.15.far = f32[2,64,128]{2,1,0:T(8,128)S(1)} collective-permute-done((f32[2,64,128]{2,1,0:T(8,128)S(1)}, f32[2,64,128]{2,1,0:T(8,128)S(1)}, u32[]{:S(2)}, u32[]{:S(2)}) %collective-permute-start.15) | collective-permute-done | bytes 65568 | tf_op jit(solution)/shard_map/ppermute | solution.py:714
  85.3 0.9 copy-done.9
  87.8 3.8 %collective-permute-start.16 = (f32[40,128]{1,0:T(8,128)S(1)}, f32[40,128]{1,0:T(8,128)S(1)}, u32[]{:S(2)}, u32[]{:S(2)}) collective-permute-start(f32[40,128]{1,0:T(8,128)S(1)} %get-tuple-element.64), channel_id=1, source_target_pairs={{0,4},{4,0},{8,12},{12,8},{16,20},{20,16},{24,28},{28,24},{32,36},... | collective-permute-start | bytes 61448 | tf_op jit(solution)/shard_map/ppermute | solution.py:709
  92.4 2.3 %shard_map.59 = f32[4,64,256]{2,1,0:T(8,128)} custom-call(f32[2,40,128]{2,1,0:T(8,128)S(1)} %get-tuple-element.62.e1, f32[40,128]{1,0:T(8,128)S(1)} %get-tuple-element.63.edge, f32[40,128]{1,0:T(8,128)S(1)} %collective-permute-done.16.other, f32[8,40,128]{2,1,0:T(8,128)S(1)} %collective-permute-done.4.far, f32[8,40,128]{2,1,0:T(8,128)S(1)} %collective-permute-done.5.sib, ...), custom_call_target="tpu_custom_call" | custom-call | tf_op jit(solution)/shard_map/pallas_call | solution.py:136
  (43 shorter events, 8.2 us)
Async XLA Ops:
  1.6 6.2 %collective-permute-start = (f32[16,8,256]{2,1,0:T(8,128)}, f32[16,8,256]{2,1,0:T(8,128)S(1)}, u32[]{:S(2)}, u32[]{:S(2)}) collective-permute-start(f32[16,8,256]{2,1,0:T(8,128)} %get-tuple-element.38), channel_id=1, source_target_pairs={{0,1},{1,2},{2,3},{3,0},{4,5},{5,6},{6,7},{7,4},{8,9},{9,10},{10,1... | collective-permute-start | bytes 393224 | tf_op jit(solution)/shard_map/ppermute | solution.py:705
  3.8 4.0 %collective-permute-start.1 = (f32[16,8,256]{2,1,0:T(8,128)}, f32[16,8,256]{2,1,0:T(8,128)S(1)}, u32[]{:S(2)}, u32[]{:S(2)}) collective-permute-start(f32[16,8,256]{2,1,0:T(8,128)} %get-tuple-element.39), channel_id=1, source_target_pairs={{0,3},{1,0},{2,1},{3,2},{4,7},{5,4},{6,5},{7,6},{8,11},{9,8},{10,9... | collective-permute-start | bytes 393224 | tf_op jit(solution)/shard_map/ppermute | solution.py:705
  8.4 11.8 %collective-permute-start.2 = (f32[600,256]{1,0:T(8,128)S(1)}, f32[600,256]{1,0:T(8,128)S(1)}, u32[]{:S(2)}, u32[]{:S(2)}) collective-permute-start(f32[600,256]{1,0:T(8,128)S(1)} %get-tuple-element.42), channel_id=1, source_target_pairs={{0,252},{4,8},{8,4},{12,16},{16,12},{20,24},{24,20},{28,32},{32,28... | collective-permute-start | bytes 1843208 | tf_op jit(solution)/shard_map/ppermute | solution.py:714
  12.1 8.1 %collective-permute-start.3 = (f32[600,256]{1,0:T(8,128)S(1)}, f32[600,256]{1,0:T(8,128)S(1)}, u32[]{:S(2)}, u32[]{:S(2)}) collective-permute-start(f32[600,256]{1,0:T(8,128)S(1)} %get-tuple-element.43), channel_id=1, source_target_pairs={{0,4},{4,0},{8,12},{12,8},{16,20},{20,16},{24,28},{28,24},{32,36},... | collective-permute-start | bytes 1843208 | tf_op jit(solution)/shard_map/ppermute | solution.py:709
  23.7 0.8 copy-start.6
  24.5 24.2 %copy-start = (f32[6,80,256]{2,1,0:T(8,128)}, f32[6,80,256]{2,1,0:T(8,128)S(1)}, u32[]{:S(2)}) copy-start(f32[6,80,256]{2,1,0:T(8,128)S(1)} %get-tuple-element.65.f) | copy-start | bytes 1474564
  24.5 24.2 %copy-start.2 = (f32[6,80,256]{2,1,0:T(8,128)}, f32[6,80,256]{2,1,0:T(8,128)S(1)}, u32[]{:S(2)}) copy-start(f32[6,80,256]{2,1,0:T(8,128)S(1)} %get-tuple-element.67.c2) | copy-start | bytes 1474564
  24.5 24.3 %copy-start.4 = (f32[6,80,256]{2,1,0:T(8,128)}, f32[6,80,256]{2,1,0:T(8,128)S(1)}, u32[]{:S(2)}) copy-start(f32[6,80,256]{2,1,0:T(8,128)S(1)} %get-tuple-element.68.c3) | copy-start | bytes 1474564
  24.5 5.9 %collective-permute-start.5 = (f32[8,40,128]{2,1,0:T(8,128)S(1)}, f32[8,40,128]{2,1,0:T(8,128)S(1)}, u32[]{:S(2)}, u32[]{:S(2)}) collective-permute-start(f32[8,40,128]{2,1,0:T(8,128)S(1)} %get-tuple-element.45), channel_id=1, source_target_pairs={{0,4},{4,0},{8,12},{12,8},{16,20},{20,16},{24,28},{28,24},{32,36},... | collective-permute-start | bytes 491528 | tf_op jit(solution)/shard_map/ppermute | solution.py:709
  29.3 4.7 %collective-permute-start.4 = (f32[8,40,128]{2,1,0:T(8,128)S(1)}, f32[8,40,128]{2,1,0:T(8,128)S(1)}, u32[]{:S(2)}, u32[]{:S(2)}) collective-permute-start(f32[8,40,128]{2,1,0:T(8,128)S(1)} %get-tuple-element.44.own), channel_id=1, source_target_pairs={{0,252},{4,8},{8,4},{12,16},{16,12},{20,24},{24,20},{28,32},{32,28... | collective-permute-start | bytes 491528 | tf_op jit(solution)/shard_map/ppermute | solution.py:714
  34.4 0.6 copy-start.10
  35.1 23.5 %copy-start.8 = (f32[6,40,128]{2,1,0:T(8,128)}, f32[6,40,128]{2,1,0:T(8,128)S(1)}, u32[]{:S(2)}) copy-start(f32[6,40,128]{2,1,0:T(8,128)S(1)} %get-tuple-element.60.f) | copy-start | bytes 368644
  35.1 6.9 %collective-permute-start.6 = (f32[56,128]{1,0:T(8,128)S(1)}, f32[56,128]{1,0:T(8,128)S(1)}, u32[]{:S(2)}, u32[]{:S(2)}) collective-permute-start(f32[56,128]{1,0:T(8,128)S(1)} %get-tuple-element.48), channel_id=1, source_target_pairs={{0,1},{1,2},{2,3},{3,0},{4,5},{5,6},{6,7},{7,4},{8,9},{9,10},{10,1... | collective-permute-start | bytes 86024 | tf_op jit(solution)/shard_map/ppermute | solution.py:705
  36.1 5.9 %collective-permute-start.7 = (f32[56,128]{1,0:T(8,128)S(1)}, f32[56,128]{1,0:T(8,128)S(1)}, u32[]{:S(2)}, u32[]{:S(2)}) collective-permute-start(f32[56,128]{1,0:T(8,128)S(1)} %get-tuple-element.49), channel_id=1, source_target_pairs={{0,3},{1,0},{2,1},{3,2},{4,7},{5,4},{6,5},{7,6},{8,11},{9,8},{10,9... | collective-permute-start | bytes 86024 | tf_op jit(solution)/shard_map/ppermute | solution.py:705
  37.8 4.1 %collective-permute-start.8 = (f32[40,128]{1,0:T(8,128)S(1)}, f32[40,128]{1,0:T(8,128)S(1)}, u32[]{:S(2)}, u32[]{:S(2)}) collective-permute-start(f32[40,128]{1,0:T(8,128)S(1)} %get-tuple-element.47.f2), channel_id=1, source_target_pairs={{0,2},{1,3},{2,0},{3,1},{4,6},{5,7},{6,4},{7,5},{8,10},{9,11},{10,... | collective-permute-start | bytes 61448 | tf_op jit(solution)/shard_map/ppermute | solution.py:705
  42.2 6.1 %collective-permute-start.9 = (f32[240,128]{1,0:T(8,128)S(1)}, f32[240,128]{1,0:T(8,128)S(1)}, u32[]{:S(2)}, u32[]{:S(2)}) collective-permute-start(f32[240,128]{1,0:T(8,128)S(1)} %get-tuple-element.52.msg), channel_id=1, source_target_pairs={{0,4},{4,0},{8,12},{12,8},{16,20},{20,16},{24,28},{28,24},{32,36},... | collective-permute-start | bytes 368648 | tf_op jit(solution)/shard_map/ppermute | solution.py:709
  48.3 5.2 %collective-permute-start.10 = (f32[384,128]{1,0:T(8,128)S(1)}, f32[384,128]{1,0:T(8,128)S(1)}, u32[]{:S(2)}, u32[]{:S(2)}) collective-permute-start(f32[384,128]{1,0:T(8,128)S(1)} %shard_map.52), channel_id=1, source_target_pairs={{0,252},{4,8},{8,4},{12,16},{16,12},{20,24},{24,20},{28,32},{32,28... | collective-permute-start | bytes 589832 | tf_op jit(solution)/shard_map/ppermute | solution.py:714
  53.5 4.8 %collective-permute-start.11 = (f32[384,128]{1,0:T(8,128)S(1)}, f32[384,128]{1,0:T(8,128)S(1)}, u32[]{:S(2)}, u32[]{:S(2)}) collective-permute-start(f32[384,128]{1,0:T(8,128)S(1)} %collective-permute-done.10.near), channel_id=1, source_target_pairs={{0,4},{4,0},{8,12},{12,8},{16,20},{20,16},{24,28},{28,24},{32,36},... | collective-permute-start | bytes 589832 | tf_op jit(solution)/shard_map/ppermute | solution.py:709
  59.6 15.1 %all-to-all-start = ((f32[32,2,8,128]{3,2,1,0:T(8,128)}), f32[32,2,8,128]{3,2,1,0:T(8,128)S(1)}, u32[]{:S(2)}, u32[]{:S(2)}) async-start(f32[32,2,8,128]{3,2,1,0:T(8,128)} %shard_map.55), calls=%async_computation | async-start | bytes 524288 | tf_op jit(solution)/shard_map/all_to_all | solution.py:768
  64.6 8.4 %collective-permute-start.12 = (f32[32,128]{1,0:T(8,128)S(1)}, f32[32,128]{1,0:T(8,128)S(1)}, u32[]{:S(2)}, u32[]{:S(2)}) collective-permute-start(f32[32,128]{1,0:T(8,128)S(1)} %get-tuple-element.57), channel_id=1, source_target_pairs={{0,252},{4,8},{8,4},{12,16},{16,12},{20,24},{24,20},{28,32},{32,28... | collective-permute-start | bytes 49160 | tf_op jit(solution)/shard_map/ppermute | solution.py:714
  74.7 17.7 %copy-start.1 = (f32[6,80,256]{2,1,0:T(8,128)S(1)}, f32[6,80,256]{2,1,0:T(8,128)}, u32[]{:S(2)}) copy-start(f32[6,80,256]{2,1,0:T(8,128)} %copy-done) | copy-start | bytes 1474564
  74.7 17.7 %copy-start.3 = (f32[6,80,256]{2,1,0:T(8,128)S(1)}, f32[6,80,256]{2,1,0:T(8,128)}, u32[]{:S(2)}) copy-start(f32[6,80,256]{2,1,0:T(8,128)} %copy-done.2) | copy-start | bytes 1474564
  74.7 17.7 %copy-start.5 = (f32[6,80,256]{2,1,0:T(8,128)S(1)}, f32[6,80,256]{2,1,0:T(8,128)}, u32[]{:S(2)}) copy-start(f32[6,80,256]{2,1,0:T(8,128)} %copy-done.4) | copy-start | bytes 1474564
  74.7 17.7 %copy-start.7 = (f32[6,80,256]{2,1,0:T(8,128)S(1)}, f32[6,80,256]{2,1,0:T(8,128)}, u32[]{:S(2)}) copy-start(f32[6,80,256]{2,1,0:T(8,128)} %copy-done.6) | copy-start | bytes 1474564
  74.7 4.5 %collective-permute-start.13 = (f32[32,2,8,128]{3,2,1,0:T(8,128)S(1)}, f32[32,2,8,128]{3,2,1,0:T(8,128)S(1)}, u32[]{:S(2)}, u32[]{:S(2)}) collective-permute-start(f32[32,2,8,128]{3,2,1,0:T(8,128)S(1)} %all-to-all-done.mine), channel_id=1, source_target_pairs={{0,4},{4,0},{8,12},{12,8},{16,20},{20,16},{24,28},{28,24},{32,36},... | collective-permute-start | bytes 786440 | tf_op jit(solution)/shard_map/ppermute | solution.py:709
  78.0 3.2 %collective-permute-start.14 = (f32[32,128]{1,0:T(8,128)S(1)}, f32[32,128]{1,0:T(8,128)S(1)}, u32[]{:S(2)}, u32[]{:S(2)}) collective-permute-start(f32[32,128]{1,0:T(8,128)S(1)} %collective-permute-done.12.late), channel_id=1, source_target_pairs={{0,4},{4,0},{8,12},{12,8},{16,20},{20,16},{24,28},{28,24},{32,36},... | collective-permute-start | bytes 49160 | tf_op jit(solution)/shard_map/ppermute | solution.py:709
  81.5 3.8 %collective-permute-start.15 = (f32[2,64,128]{2,1,0:T(8,128)S(1)}, f32[2,64,128]{2,1,0:T(8,128)S(1)}, u32[]{:S(2)}, u32[]{:S(2)}) collective-permute-start(f32[2,64,128]{2,1,0:T(8,128)S(1)} %shard_map.57.e2), channel_id=1, source_target_pairs={{0,252},{4,8},{8,4},{12,16},{16,12},{20,24},{24,20},{28,32},{32,28... | collective-permute-start | bytes 196616 | tf_op jit(solution)/shard_map/ppermute | solution.py:714
  85.3 0.9 copy-start.9
  86.2 0.9 copy-start.11
  87.8 4.6 %collective-permute-start.16 = (f32[40,128]{1,0:T(8,128)S(1)}, f32[40,128]{1,0:T(8,128)S(1)}, u32[]{:S(2)}, u32[]{:S(2)}) collective-permute-start(f32[40,128]{1,0:T(8,128)S(1)} %get-tuple-element.64), channel_id=1, source_target_pairs={{0,4},{4,0},{8,12},{12,8},{16,20},{20,16},{24,28},{28,24},{32,36},... | collective-permute-start | bytes 61448 | tf_op jit(solution)/shard_map/ppermute | solution.py:709

commit v11 on v6

--- a/solution.py
+++ b/solution.py
@@ -242,7 +242,7 @@
     return SIG[0] + c1[q, here, :] + c1[q + 1, here, :] + k2 + h2 + k3 + roll(k3, -1, 1)
 
 
-def fine_pre_kernel(own, coef1, far, sib, f, c1, c2, c3, g, u2, w1, out_far, out_sib, f1, u1, res, scr):
+def fine_pre_kernel(own, coef1, far, sib, f, c1, c2, c3, u2, w1, out_far, out_sib, g, f1, u1, res, scr):
     below, above = sides(far, sib)
     for a, ref in enumerate((f, c1, c2, c3)):
         here = slice(80 * a, 80 * a + 80)
@@ -269,19 +269,17 @@
         def rows(r0, n):
             here = pl.ds(r0, CHUNK)
             x, near = near_chunk(u1, q + 1, c1, c2, c3, q, r0, n)
-            u2[q + 1, here, :] = (1.0 + KEEP) * x + GAIN * (g[q, here, :] * (f[q, here, :] + near) - x)
+            u2[q, here, :] = (1.0 + KEEP) * x + GAIN * (g[q, here, :] * (f[q, here, :] + near) - x)
 
         chunked(80, rows)
         return carry
 
-    u2[0] = u1[0]
-    u2[7] = u1[7]
     lax.fori_loop(0, 6, smooth_second, 0)
 
     def residual(q, carry):
         def rows(r0, n):
             here = pl.ds(r0, CHUNK)
-            x, near = near_chunk(u2, q + 1, c1, c2, c3, q, r0, n)
+            x, near = near_chunk(u2, q, c1, c2, c3, q, r0, n)
             res[q - 1, here, :] = f[q, here, :] + near - diag_chunk(c1, c2, c3, q, r0, n) * x
 
         chunked(80, rows)
@@ -306,7 +304,7 @@
             out[p] = f1[p]
             out[2 + p] = inverse
     par = lax.rem(lax.axis_index("wide"), 2)
-    for out, plane in ((out_far, 3 + par), (out_sib, 4 - par)):
+    for out, plane in ((out_far, 2 + par), (out_sib, 3 - par)):
         out[4] = u2[plane, 0:40, 0:128]
         out[5] = u2[plane, 0:40, 128:256]
         out[6] = u2[plane, 40:80, 0:128]
@@ -324,12 +322,17 @@
         out[8 * k : 8 * k + 8] = two_blocks(x)
 
 
-def middle_pre_kernel(own, far, sib, w1, coefs, f, g, u2, f2, up, down, u1, scr):
+def middle_pre_kernel(own, far, sib, w1, coefs, f, g, u2, f2, up, down, outer, u1, scr):
     below, above = sides(far, sib)
     for k, read in enumerate((below, own.__getitem__, above)):
         for p in range(2):
             f[2 * k + p] = read(p)
             g[2 * k + p] = read(2 + p)
+    for k, read in enumerate((below, above)):
+        outer[k, 0:40, 0:128] = read(4)
+        outer[k, 0:40, 128:256] = read(5)
+        outer[k, 40:80, 0:128] = read(6)
+        outer[k, 40:80, 128:256] = read(7)
     for p in range(6):
         u1[p] = f[p] * g[p] * (1.0 / THETA)
     u2[0] = u1[0]
@@ -493,7 +496,7 @@
     return lax.rem(j + n, n)
 
 
-STEP = 8
+STEP = 32
 THREE, FOUR = (32, 4), (16, 2)
 
 
@@ -653,29 +656,27 @@
     send[...] = jnp.where(odd, out[0], out[2])
 
 
-def fine_post_kernel(e1, edge, other, far, sib, f, c1, c2, c3, g, u2, out, v, w, scr):
+def fine_post_kernel(e1, edge, other, outer, f, c1, c2, c3, u2, out, g, v, w, scr):
     below, above = sides(edge, other)
     x = jnp.concatenate([below(...), e1[0], e1[1], above(...)], axis=0)
-    below, above = sides(far, sib)
     for half in range(2):
         here = slice(128 * half, 128 * half + 128)
         row, col = iota((128, 128), 0), iota((128, 128), 1)
         fine = mul(x, (row == 64 * half + col // 2).astype(F32))
         scr[pl.ds(0, 160, stride=2), :] = fine
         scr[pl.ds(1, 160, stride=2), :] = fine
-        for k, read in ((0, below), (7, above)):
+        for k in range(8):
             at = 80 * (k // 2)
-            v[k, 0:40, here] = read(4 + half) + scr[at : at + 40, :]
-            v[k, 40:80, here] = read(6 + half) + scr[at + 40 : at + 80, :]
-        for k in range(1, 7):
-            at = 80 * (k // 2)
-            v[k, :, here] = u2[k, :, here] + scr[at : at + 80, :]
+            base = u2[k - 1, :, here] if 0 < k < 7 else outer[k // 7, :, here]
+            v[k, :, here] = base + scr[at : at + 80, :]
 
     def post1(q, carry):
         def chunk(r0, n):
             here = pl.ds(r0, CHUNK)
             x, near = near_chunk(v, q + 1, c1, c2, c3, q, r0, n)
-            w[q + 1, here, :] = x + (1.0 / THETA) * (g[q, here, :] * (f[q, here, :] + near) - x)
+            inverse = 1.0 / diag_chunk(c1, c2, c3, q, r0, n)
+            g[q, here, :] = inverse
+            w[q + 1, here, :] = x + (1.0 / THETA) * (inverse * (f[q, here, :] + near) - x)
 
         chunked(80, chunk)
         return carry
@@ -727,18 +728,18 @@
     )(jnp.concatenate(inputs, axis=0), low, high)
     far, sib = across(far), sibling(sib)
 
-    f, c1, c2, c3, g, u2, w1, out_far, out_sib, _ = call(
+    f, c1, c2, c3, u2, w1, out_far, out_sib = call(
         fine_pre_kernel,
-        [(6,) + big, (7,) + big, (6,) + big, (6,) + big, (6,) + big, (8,) + big]
-        + [(18, 40, 128), (8, 40, 128), (8, 40, 128), (2, 40, 128)],
-        [(8,) + big, (4,) + big, (160, 128)],
+        [(6,) + big, (7,) + big, (6,) + big, (6,) + big, (6,) + big]
+        + [(18, 40, 128), (8, 40, 128), (8, 40, 128)],
+        [(6,) + big, (2, 40, 128), (8,) + big, (4,) + big, (160, 128)],
     )(own, coef1, far, sib)
     far1, sib1 = across(out_far), sibling(out_sib)
     (coefs,) = call(coarse_coef_kernel, [(32, 128)], [(80, 128)])(w1)
 
     six = (6, 40, 128)
-    f1w, g1w, u2m, f2, up, down = call(
-        middle_pre_kernel, [six, six, six, (40, 128), (56, 128), (56, 128)], [six, (40, 128)]
+    f1w, g1w, u2m, f2, up, down, outer = call(
+        middle_pre_kernel, [six, six, six, (40, 128), (56, 128), (56, 128), (2,) + big], [six, (40, 128)]
     )(out_far, far1, sib1, w1, coefs)
     low, high, far = shift(up, "narrow", 1), shift(down, "narrow", -1), shift(f2, "narrow", 2)
 
@@ -777,8 +778,8 @@
     other1 = sibling(send)
 
     (out,) = call(
-        fine_post_kernel, [(4, 64, 256)], [(8,) + big, (8,) + big, (320, 128)]
-    )(e1, edge, other1, far1, sib1, f, c1, c2, c3, g, u2)
+        fine_post_kernel, [(4, 64, 256)], [(6,) + big, (8,) + big, (8,) + big, (320, 128)]
+    )(e1, edge, other1, outer, f, c1, c2, c3, u2)
     return out
 
 

time: 96.1 us -> 92.1 us (0.958)
  local copies, waits for them, and re-layouts: 4.06 us -> 1.46 us
  Pallas kernels: 13.7 us -> 12.3 us
    unnamed x24 -> x20, local copies, waits for them, and re-layouts: 4.06 us -> 1.46 us
    pallas_call x14, Pallas kernels: 13.7 us -> 12.3 us  [run(): pl.pallas_call(kernel, out_shape=[jax.ShapeDtypeStruct(s, F32) for s in o...]
where the time goes in v11:
time: 92.1 us; the launch traced here: 91.9 us
  starting transfers between devices  46.2 us (50%)
  waiting for transfers between devices  30.4 us (33%)
  Pallas kernels  12.3 us (13%)
  local copies, waits for them, and re-layouts  1.46 us (2%)
  other arithmetic  1.26 us (1%)
    ppermute x7, starting transfers between devices, sibling(): lax.ppermute(x, 'wide', [(i, i ^ 1) for i in range(lax.axis_size('wide'))])  26.1 us
    ppermute x5, waiting for transfers between devices, across(): lax.ppermute(x, 'wide', [(i, (i + 1 if i % 2 else i - 1) % count) for i i...  20 us
    pallas_call x14, Pallas kernels, run(): pl.pallas_call(kernel, out_shape=[jax.ShapeDtypeStruct(s, F32) for s in o...  12.3 us
    ppermute x5, starting transfers between devices, shift(): return lax.ppermute(x, axis, [(i, (i + by) % count) for i in range(count)])  7.65 us
    ppermute x5, starting transfers between devices, across(): lax.ppermute(x, 'wide', [(i, (i + 1 if i % 2 else i - 1) % count) for i i...  7.49 us
    all_to_all x1, starting transfers between devices, body(): lax.all_to_all(send, 'wide', split_axis=0, concat_axis=0, tiled=True, axi...  4.99 us
    ppermute x7, waiting for transfers between devices, sibling(): lax.ppermute(x, 'wide', [(i, i ^ 1) for i in range(lax.axis_size('wide'))])  4.55 us
    ppermute x5, waiting for transfers between devices, shift(): return lax.ppermute(x, axis, [(i, (i + by) % count) for i in range(count)])  4.2 us
  transfers between devices with their start and end apart: 18, of which 13 were waited for; matrix products, arithmetic and copies ran while one was open for 1% of the time, Pallas kernels for 3%

profile of v11, /device:TPU:1, one launch (start us, length us, event | category | flops | bytes accessed | tf_op | source)
XLA Modules:
  0.0 91.9 jit_solution(14776125265991984344)
XLA Ops:
  0.0 1.6 %shard_map.46 = (f32[16,8,256]{2,1,0:T(8,128)}, f32[16,8,256]{2,1,0:T(8,128)}) custom-call(f32[4,64,256]{2,1,0:T(8,128)} %f.1, f32[4,64,256]{2,1,0:T(8,128)} %c1.1, f32[4,64,256]{2,1,0:T(8,128)} %c2.1, f32[4,64,256]{2,1,0:T(8,128)} %c3.1), custom_call_target="tpu_custom_call" | custom-call | tf_op jit(solution)/shard_map/pallas_call | solution.py:136
  1.6 2.2 %collective-permute-start = (f32[16,8,256]{2,1,0:T(8,128)}, f32[16,8,256]{2,1,0:T(8,128)S(1)}, u32[]{:S(2)}, u32[]{:S(2)}) collective-permute-start(f32[16,8,256]{2,1,0:T(8,128)} %get-tuple-element.38), channel_id=1, source_target_pairs={{0,1},{1,2},{2,3},{3,0},{4,5},{5,6},{6,7},{7,4},{8,9},{9,10},{10,1... | collective-permute-start | bytes 393224 | tf_op jit(solution)/shard_map/ppermute | solution.py:699
  3.8 1.5 %collective-permute-start.1 = (f32[16,8,256]{2,1,0:T(8,128)}, f32[16,8,256]{2,1,0:T(8,128)S(1)}, u32[]{:S(2)}, u32[]{:S(2)}) collective-permute-start(f32[16,8,256]{2,1,0:T(8,128)} %get-tuple-element.39), channel_id=1, source_target_pairs={{0,3},{1,0},{2,1},{3,2},{4,7},{5,4},{6,5},{7,6},{8,11},{9,8},{10,9... | collective-permute-start | bytes 393224 | tf_op jit(solution)/shard_map/ppermute | solution.py:699
  5.4 1.3 %pad_maximum_fusion.inner = f32[16,64,256]{2,1,0:T(8,128)S(1)} fusion(f32[4,64,256]{2,1,0:T(8,128)} %c3.1, f32[4,64,256]{2,1,0:T(8,128)} %c2.1, f32[4,64,256]{2,1,0:T(8,128)} %c1.1, f32[4,64,256]{2,1,0:T(8,128)} %f.1), kind=kLoop, calls=%fused_computation | loop fusion | flops 786432 | bytes 2097152 | tf_op jit(solution)/shard_map/concatenate | solution.py:728
  6.6 1.2 %collective-permute-done.low = f32[16,8,256]{2,1,0:T(8,128)S(1)} collective-permute-done((f32[16,8,256]{2,1,0:T(8,128)}, f32[16,8,256]{2,1,0:T(8,128)S(1)}, u32[]{:S(2)}, u32[]{:S(2)}) %collective-permute-start) | collective-permute-done | bytes 131104 | tf_op jit(solution)/shard_map/ppermute | solution.py:699
  8.4 3.7 %collective-permute-start.2 = (f32[600,256]{1,0:T(8,128)S(1)}, f32[600,256]{1,0:T(8,128)S(1)}, u32[]{:S(2)}, u32[]{:S(2)}) collective-permute-start(f32[600,256]{1,0:T(8,128)S(1)} %get-tuple-element.42), channel_id=1, source_target_pairs={{0,252},{4,8},{8,4},{12,16},{16,12},{20,24},{24,20},{28,32},{32,28... | collective-permute-start | bytes 1843208 | tf_op jit(solution)/shard_map/ppermute | solution.py:708
  12.1 5.1 %collective-permute-start.3 = (f32[600,256]{1,0:T(8,128)S(1)}, f32[600,256]{1,0:T(8,128)S(1)}, u32[]{:S(2)}, u32[]{:S(2)}) collective-permute-start(f32[600,256]{1,0:T(8,128)S(1)} %get-tuple-element.43), channel_id=1, source_target_pairs={{0,4},{4,0},{8,12},{12,8},{16,20},{20,16},{24,28},{28,24},{32,36},... | collective-permute-start | bytes 1843208 | tf_op jit(solution)/shard_map/ppermute | solution.py:703
  17.2 3.0 %collective-permute-done.2.far = f32[600,256]{1,0:T(8,128)S(1)} collective-permute-done((f32[600,256]{1,0:T(8,128)S(1)}, f32[600,256]{1,0:T(8,128)S(1)}, u32[]{:S(2)}, u32[]{:S(2)}) %collective-permute-start.2) | collective-permute-done | bytes 614432 | tf_op jit(solution)/shard_map/ppermute | solution.py:708
  20.2 2.4 %shard_map.48 = (f32[6,80,256]{2,1,0:T(8,128)S(1)}, f32[7,80,256]{2,1,0:T(8,128)S(1)}, f32[6,80,256]{2,1,0:T(8,128)S(1)}, f32[6,80,256]{2,1,0:T(8,128)S(1)}, f32...) custom-call(f32[16,80,256]{2,1,0:T(8,128)S(1)} %get-tuple-element.40, ...), custom_call_target="tpu_custom_call" | custom-call | tf_op jit(solution)/shard_map/pallas_call | solution.py:136
  23.4 4.8 %collective-permute-start.5 = (f32[8,40,128]{2,1,0:T(8,128)S(1)}, f32[8,40,128]{2,1,0:T(8,128)S(1)}, u32[]{:S(2)}, u32[]{:S(2)}) collective-permute-start(f32[8,40,128]{2,1,0:T(8,128)S(1)} %get-tuple-element.45), channel_id=1, source_target_pairs={{0,4},{4,0},{8,12},{12,8},{16,20},{20,16},{24,28},{28,24},{32,36},... | collective-permute-start | bytes 491528 | tf_op jit(solution)/shard_map/ppermute | solution.py:703
  29.3 3.7 %collective-permute-done.4.far = f32[8,40,128]{2,1,0:T(8,128)S(1)} collective-permute-done((f32[8,40,128]{2,1,0:T(8,128)S(1)}, f32[8,40,128]{2,1,0:T(8,128)S(1)}, u32[]{:S(2)}, u32[]{:S(2)}) %collective-permute-start.4) | collective-permute-done | bytes 163872 | tf_op jit(solution)/shard_map/ppermute | solution.py:708
  34.0 1.0 %collective-permute-start.6 = (f32[56,128]{1,0:T(8,128)S(1)}, f32[56,128]{1,0:T(8,128)S(1)}, u32[]{:S(2)}, u32[]{:S(2)}) collective-permute-start(f32[56,128]{1,0:T(8,128)S(1)} %get-tuple-element.48), channel_id=1, source_target_pairs={{0,1},{1,2},{2,3},{3,0},{4,5},{5,6},{6,7},{7,4},{8,9},{9,10},{10,1... | collective-permute-start | bytes 86024 | tf_op jit(solution)/shard_map/ppermute | solution.py:699
  35.0 1.7 %collective-permute-start.7 = (f32[56,128]{1,0:T(8,128)S(1)}, f32[56,128]{1,0:T(8,128)S(1)}, u32[]{:S(2)}, u32[]{:S(2)}) collective-permute-start(f32[56,128]{1,0:T(8,128)S(1)} %get-tuple-element.49), channel_id=1, source_target_pairs={{0,3},{1,0},{2,1},{3,2},{4,7},{5,4},{6,5},{7,6},{8,11},{9,8},{10,9... | collective-permute-start | bytes 86024 | tf_op jit(solution)/shard_map/ppermute | solution.py:699
  36.8 1.2 %collective-permute-start.8 = (f32[40,128]{1,0:T(8,128)S(1)}, f32[40,128]{1,0:T(8,128)S(1)}, u32[]{:S(2)}, u32[]{:S(2)}) collective-permute-start(f32[40,128]{1,0:T(8,128)S(1)} %get-tuple-element.47.f2), channel_id=1, source_target_pairs={{0,2},{1,3},{2,0},{3,1},{4,6},{5,7},{6,4},{7,5},{8,10},{9,11},{10,... | collective-permute-start | bytes 61448 | tf_op jit(solution)/shard_map/ppermute | solution.py:699
  37.9 3.0 %collective-permute-done.8.far = f32[40,128]{1,0:T(8,128)S(1)} collective-permute-done((f32[40,128]{1,0:T(8,128)S(1)}, f32[40,128]{1,0:T(8,128)S(1)}, u32[]{:S(2)}, u32[]{:S(2)}) %collective-permute-start.8) | collective-permute-done | bytes 20512 | tf_op jit(solution)/shard_map/ppermute | solution.py:699
  41.1 5.1 %collective-permute-start.9 = (f32[240,128]{1,0:T(8,128)S(1)}, f32[240,128]{1,0:T(8,128)S(1)}, u32[]{:S(2)}, u32[]{:S(2)}) collective-permute-start(f32[240,128]{1,0:T(8,128)S(1)} %get-tuple-element.52.msg), channel_id=1, source_target_pairs={{0,4},{4,0},{8,12},{12,8},{16,20},{20,16},{24,28},{28,24},{32,36},... | collective-permute-start | bytes 368648 | tf_op jit(solution)/shard_map/ppermute | solution.py:703
  46.2 1.0 %collective-permute-done.9.sib = f32[240,128]{1,0:T(8,128)S(1)} collective-permute-done((f32[240,128]{1,0:T(8,128)S(1)}, f32[240,128]{1,0:T(8,128)S(1)}, u32[]{:S(2)}, u32[]{:S(2)}) %collective-permute-start.9) | collective-permute-done | bytes 122912 | tf_op jit(solution)/shard_map/ppermute | solution.py:703
  47.6 4.8 %collective-permute-done.10.near = f32[384,128]{1,0:T(8,128)S(1)} collective-permute-done((f32[384,128]{1,0:T(8,128)S(1)}, f32[384,128]{1,0:T(8,128)S(1)}, u32[]{:S(2)}, u32[]{:S(2)}) %collective-permute-start.10) | collective-permute-done | bytes 196640 | tf_op jit(solution)/shard_map/ppermute | solution.py:708
  52.4 3.7 %collective-permute-start.11 = (f32[384,128]{1,0:T(8,128)S(1)}, f32[384,128]{1,0:T(8,128)S(1)}, u32[]{:S(2)}, u32[]{:S(2)}) collective-permute-start(f32[384,128]{1,0:T(8,128)S(1)} %collective-permute-done.10.near), channel_id=1, source_target_pairs={{0,4},{4,0},{8,12},{12,8},{16,20},{20,16},{24,28},{28,24},{32,36},... | collective-permute-start | bytes 589832 | tf_op jit(solution)/shard_map/ppermute | solution.py:703
  56.0 1.1 %collective-permute-done.11.other = f32[384,128]{1,0:T(8,128)S(1)} collective-permute-done((f32[384,128]{1,0:T(8,128)S(1)}, f32[384,128]{1,0:T(8,128)S(1)}, u32[]{:S(2)}, u32[]{:S(2)}) %collective-permute-start.11) | collective-permute-done | bytes 196640 | tf_op jit(solution)/shard_map/ppermute | solution.py:703
  57.5 1.0 %shard_map.55 = f32[32,2,8,128]{3,2,1,0:T(8,128)} custom-call(f32[21,64,128]{2,1,0:T(8,128)S(1)} %get-tuple-element.54.w.win, f32[4,64,128]{2,1,0:T(8,128)S(1)} %get-tuple-element.55.u2, f32[3,8,128]{2,1,0:T(8,128)S(1)} %shard_map.53.tiles), custom_call_target="tpu_custom_call" | custom-call | tf_op jit(solution)/shard_map/pallas_call | solution.py:136
  58.5 5.0 %all-to-all-start = ((f32[32,2,8,128]{3,2,1,0:T(8,128)}), f32[32,2,8,128]{3,2,1,0:T(8,128)S(1)}, u32[]{:S(2)}, u32[]{:S(2)}) async-start(f32[32,2,8,128]{3,2,1,0:T(8,128)} %shard_map.55), calls=%async_computation | async-start | bytes 524288 | tf_op jit(solution)/shard_map/all_to_all | solution.py:759
  63.5 1.9 %collective-permute-start.12 = (f32[32,128]{1,0:T(8,128)S(1)}, f32[32,128]{1,0:T(8,128)S(1)}, u32[]{:S(2)}, u32[]{:S(2)}) collective-permute-start(f32[32,128]{1,0:T(8,128)S(1)} %get-tuple-element.57), channel_id=1, source_target_pairs={{0,252},{4,8},{8,4},{12,16},{16,12},{20,24},{24,20},{28,32},{32,28... | collective-permute-start | bytes 49160 | tf_op jit(solution)/shard_map/ppermute | solution.py:708
  65.4 6.4 %collective-permute-done.12.late = f32[32,128]{1,0:T(8,128)S(1)} collective-permute-done((f32[32,128]{1,0:T(8,128)S(1)}, f32[32,128]{1,0:T(8,128)S(1)}, u32[]{:S(2)}, u32[]{:S(2)}) %collective-permute-start.12) | collective-permute-done | bytes 16416 | tf_op jit(solution)/shard_map/ppermute | solution.py:708
  71.8 1.7 %all-to-all-done.mine = f32[32,2,8,128]{3,2,1,0:T(8,128)S(1)} async-done(((f32[32,2,8,128]{3,2,1,0:T(8,128)}), f32[32,2,8,128]{3,2,1,0:T(8,128)S(1)}, u32[]{:S(2)}, u32[]{:S(2)}) %all-to-all-start) | async-done | bytes 262176 | tf_op jit(solution)/shard_map/all_to_all | solution.py:759
  73.6 3.3 %collective-permute-start.13 = (f32[32,2,8,128]{3,2,1,0:T(8,128)S(1)}, f32[32,2,8,128]{3,2,1,0:T(8,128)S(1)}, u32[]{:S(2)}, u32[]{:S(2)}) collective-permute-start(f32[32,2,8,128]{3,2,1,0:T(8,128)S(1)} %all-to-all-done.mine), channel_id=1, source_target_pairs={{0,4},{4,0},{8,12},{12,8},{16,20},{20,16},{24,28},{28,24},{32,36},... | collective-permute-start | bytes 786440 | tf_op jit(solution)/shard_map/ppermute | solution.py:703
  77.2 0.9 collective-permute-done.13.theirs
  78.1 2.0 %shard_map.56.e2 = f32[192,128]{1,0:T(8,128)S(1)} custom-call(f32[32,2,8,128]{3,2,1,0:T(8,128)S(1)} %all-to-all-done.mine, f32[32,2,8,128]{3,2,1,0:T(8,128)S(1)} %collective-permute-done.13.theirs), custom_call_target="tpu_custom_call" | custom-call | tf_op jit(solution)/shard_map/pallas_call | solution.py:136
  80.4 1.8 %collective-permute-start.15 = (f32[2,64,128]{2,1,0:T(8,128)S(1)}, f32[2,64,128]{2,1,0:T(8,128)S(1)}, u32[]{:S(2)}, u32[]{:S(2)}) collective-permute-start(f32[2,64,128]{2,1,0:T(8,128)S(1)} %shard_map.57.e2), channel_id=1, source_target_pairs={{0,252},{4,8},{8,4},{12,16},{16,12},{20,24},{24,20},{28,32},{32,28... | collective-permute-start | bytes 196616 | tf_op jit(solution)/shard_map/ppermute | solution.py:708
  82.2 2.0 %collective-permute-done.15.far = f32[2,64,128]{2,1,0:T(8,128)S(1)} collective-permute-done((f32[2,64,128]{2,1,0:T(8,128)S(1)}, f32[2,64,128]{2,1,0:T(8,128)S(1)}, u32[]{:S(2)}, u32[]{:S(2)}) %collective-permute-start.15) | collective-permute-done | bytes 65568 | tf_op jit(solution)/shard_map/ppermute | solution.py:708
  84.9 3.8 %collective-permute-start.16 = (f32[40,128]{1,0:T(8,128)S(1)}, f32[40,128]{1,0:T(8,128)S(1)}, u32[]{:S(2)}, u32[]{:S(2)}) collective-permute-start(f32[40,128]{1,0:T(8,128)S(1)} %get-tuple-element.64), channel_id=1, source_target_pairs={{0,4},{4,0},{8,12},{12,8},{16,20},{20,16},{24,28},{28,24},{32,36},... | collective-permute-start | bytes 61448 | tf_op jit(solution)/shard_map/ppermute | solution.py:703
  89.5 2.4 %shard_map.59 = f32[4,64,256]{2,1,0:T(8,128)} custom-call(f32[2,40,128]{2,1,0:T(8,128)S(1)} %get-tuple-element.62.e1, f32[40,128]{1,0:T(8,128)S(1)} %get-tuple-element.63.edge, f32[40,128]{1,0:T(8,128)S(1)} %collective-permute-done.16.other, f32[2,80,256]{2,1,0:T(8,128)S(1)} %copy-done.5, f32[6,80,256]{2,1,0:T(8,128)S(1)} %get-tuple-element.66.f, ...), custom_call_target="tpu_custom_call" | custom-call | tf_op jit(solution)/shard_map/pallas_call | solution.py:136
  (39 shorter events, 6.4 us)
Async XLA Ops:
  1.6 6.2 %collective-permute-start = (f32[16,8,256]{2,1,0:T(8,128)}, f32[16,8,256]{2,1,0:T(8,128)S(1)}, u32[]{:S(2)}, u32[]{:S(2)}) collective-permute-start(f32[16,8,256]{2,1,0:T(8,128)} %get-tuple-element.38), channel_id=1, source_target_pairs={{0,1},{1,2},{2,3},{3,0},{4,5},{5,6},{6,7},{7,4},{8,9},{9,10},{10,1... | collective-permute-start | bytes 393224 | tf_op jit(solution)/shard_map/ppermute | solution.py:699
  3.8 4.0 %collective-permute-start.1 = (f32[16,8,256]{2,1,0:T(8,128)}, f32[16,8,256]{2,1,0:T(8,128)S(1)}, u32[]{:S(2)}, u32[]{:S(2)}) collective-permute-start(f32[16,8,256]{2,1,0:T(8,128)} %get-tuple-element.39), channel_id=1, source_target_pairs={{0,3},{1,0},{2,1},{3,2},{4,7},{5,4},{6,5},{7,6},{8,11},{9,8},{10,9... | collective-permute-start | bytes 393224 | tf_op jit(solution)/shard_map/ppermute | solution.py:699
  8.4 11.8 %collective-permute-start.2 = (f32[600,256]{1,0:T(8,128)S(1)}, f32[600,256]{1,0:T(8,128)S(1)}, u32[]{:S(2)}, u32[]{:S(2)}) collective-permute-start(f32[600,256]{1,0:T(8,128)S(1)} %get-tuple-element.42), channel_id=1, source_target_pairs={{0,252},{4,8},{8,4},{12,16},{16,12},{20,24},{24,20},{28,32},{32,28... | collective-permute-start | bytes 1843208 | tf_op jit(solution)/shard_map/ppermute | solution.py:708
  12.1 8.1 %collective-permute-start.3 = (f32[600,256]{1,0:T(8,128)S(1)}, f32[600,256]{1,0:T(8,128)S(1)}, u32[]{:S(2)}, u32[]{:S(2)}) collective-permute-start(f32[600,256]{1,0:T(8,128)S(1)} %get-tuple-element.43), channel_id=1, source_target_pairs={{0,4},{4,0},{8,12},{12,8},{16,20},{20,16},{24,28},{28,24},{32,36},... | collective-permute-start | bytes 1843208 | tf_op jit(solution)/shard_map/ppermute | solution.py:703
  22.6 0.8 copy-start
  23.4 24.2 %copy-start.2 = (f32[6,80,256]{2,1,0:T(8,128)}, f32[6,80,256]{2,1,0:T(8,128)S(1)}, u32[]{:S(2)}) copy-start(f32[6,80,256]{2,1,0:T(8,128)S(1)} %get-tuple-element.70.u2) | copy-start | bytes 1474564
  23.4 5.9 %collective-permute-start.5 = (f32[8,40,128]{2,1,0:T(8,128)S(1)}, f32[8,40,128]{2,1,0:T(8,128)S(1)}, u32[]{:S(2)}, u32[]{:S(2)}) collective-permute-start(f32[8,40,128]{2,1,0:T(8,128)S(1)} %get-tuple-element.45), channel_id=1, source_target_pairs={{0,4},{4,0},{8,12},{12,8},{16,20},{20,16},{24,28},{28,24},{32,36},... | collective-permute-start | bytes 491528 | tf_op jit(solution)/shard_map/ppermute | solution.py:703
  28.3 4.7 %collective-permute-start.4 = (f32[8,40,128]{2,1,0:T(8,128)S(1)}, f32[8,40,128]{2,1,0:T(8,128)S(1)}, u32[]{:S(2)}, u32[]{:S(2)}) collective-permute-start(f32[8,40,128]{2,1,0:T(8,128)S(1)} %get-tuple-element.44.own), channel_id=1, source_target_pairs={{0,252},{4,8},{8,4},{12,16},{16,12},{20,24},{24,20},{28,32},{32,28... | collective-permute-start | bytes 491528 | tf_op jit(solution)/shard_map/ppermute | solution.py:708
  33.4 0.7 copy-start.4
  34.0 23.5 %copy-start.6 = (f32[6,40,128]{2,1,0:T(8,128)}, f32[6,40,128]{2,1,0:T(8,128)S(1)}, u32[]{:S(2)}) copy-start(f32[6,40,128]{2,1,0:T(8,128)S(1)} %get-tuple-element.60.f) | copy-start | bytes 368644
  34.0 23.5 %copy-start.8 = (f32[6,40,128]{2,1,0:T(8,128)}, f32[6,40,128]{2,1,0:T(8,128)S(1)}, u32[]{:S(2)}) copy-start(f32[6,40,128]{2,1,0:T(8,128)S(1)} %get-tuple-element.61.g) | copy-start | bytes 368644
  34.0 6.9 %collective-permute-start.6 = (f32[56,128]{1,0:T(8,128)S(1)}, f32[56,128]{1,0:T(8,128)S(1)}, u32[]{:S(2)}, u32[]{:S(2)}) collective-permute-start(f32[56,128]{1,0:T(8,128)S(1)} %get-tuple-element.48), channel_id=1, source_target_pairs={{0,1},{1,2},{2,3},{3,0},{4,5},{5,6},{6,7},{7,4},{8,9},{9,10},{10,1... | collective-permute-start | bytes 86024 | tf_op jit(solution)/shard_map/ppermute | solution.py:699
  35.0 5.9 %collective-permute-start.7 = (f32[56,128]{1,0:T(8,128)S(1)}, f32[56,128]{1,0:T(8,128)S(1)}, u32[]{:S(2)}, u32[]{:S(2)}) collective-permute-start(f32[56,128]{1,0:T(8,128)S(1)} %get-tuple-element.49), channel_id=1, source_target_pairs={{0,3},{1,0},{2,1},{3,2},{4,7},{5,4},{6,5},{7,6},{8,11},{9,8},{10,9... | collective-permute-start | bytes 86024 | tf_op jit(solution)/shard_map/ppermute | solution.py:699
  36.8 4.1 %collective-permute-start.8 = (f32[40,128]{1,0:T(8,128)S(1)}, f32[40,128]{1,0:T(8,128)S(1)}, u32[]{:S(2)}, u32[]{:S(2)}) collective-permute-start(f32[40,128]{1,0:T(8,128)S(1)} %get-tuple-element.47.f2), channel_id=1, source_target_pairs={{0,2},{1,3},{2,0},{3,1},{4,6},{5,7},{6,4},{7,5},{8,10},{9,11},{10,... | collective-permute-start | bytes 61448 | tf_op jit(solution)/shard_map/ppermute | solution.py:699
  41.1 6.0 %collective-permute-start.9 = (f32[240,128]{1,0:T(8,128)S(1)}, f32[240,128]{1,0:T(8,128)S(1)}, u32[]{:S(2)}, u32[]{:S(2)}) collective-permute-start(f32[240,128]{1,0:T(8,128)S(1)} %get-tuple-element.52.msg), channel_id=1, source_target_pairs={{0,4},{4,0},{8,12},{12,8},{16,20},{20,16},{24,28},{28,24},{32,36},... | collective-permute-start | bytes 368648 | tf_op jit(solution)/shard_map/ppermute | solution.py:703
  47.2 5.2 %collective-permute-start.10 = (f32[384,128]{1,0:T(8,128)S(1)}, f32[384,128]{1,0:T(8,128)S(1)}, u32[]{:S(2)}, u32[]{:S(2)}) collective-permute-start(f32[384,128]{1,0:T(8,128)S(1)} %shard_map.52), channel_id=1, source_target_pairs={{0,252},{4,8},{8,4},{12,16},{16,12},{20,24},{24,20},{28,32},{32,28... | collective-permute-start | bytes 589832 | tf_op jit(solution)/shard_map/ppermute | solution.py:708
  52.4 4.8 %collective-permute-start.11 = (f32[384,128]{1,0:T(8,128)S(1)}, f32[384,128]{1,0:T(8,128)S(1)}, u32[]{:S(2)}, u32[]{:S(2)}) collective-permute-start(f32[384,128]{1,0:T(8,128)S(1)} %collective-permute-done.10.near), channel_id=1, source_target_pairs={{0,4},{4,0},{8,12},{12,8},{16,20},{20,16},{24,28},{28,24},{32,36},... | collective-permute-start | bytes 589832 | tf_op jit(solution)/shard_map/ppermute | solution.py:703
  58.5 15.1 %all-to-all-start = ((f32[32,2,8,128]{3,2,1,0:T(8,128)}), f32[32,2,8,128]{3,2,1,0:T(8,128)S(1)}, u32[]{:S(2)}, u32[]{:S(2)}) async-start(f32[32,2,8,128]{3,2,1,0:T(8,128)} %shard_map.55), calls=%async_computation | async-start | bytes 524288 | tf_op jit(solution)/shard_map/all_to_all | solution.py:759
  63.5 8.4 %collective-permute-start.12 = (f32[32,128]{1,0:T(8,128)S(1)}, f32[32,128]{1,0:T(8,128)S(1)}, u32[]{:S(2)}, u32[]{:S(2)}) collective-permute-start(f32[32,128]{1,0:T(8,128)S(1)} %get-tuple-element.57), channel_id=1, source_target_pairs={{0,252},{4,8},{8,4},{12,16},{16,12},{20,24},{24,20},{28,32},{32,28... | collective-permute-start | bytes 49160 | tf_op jit(solution)/shard_map/ppermute | solution.py:708
  73.6 10.6 %copy-start.7 = (f32[6,40,128]{2,1,0:T(8,128)S(1)}, f32[6,40,128]{2,1,0:T(8,128)}, u32[]{:S(2)}) copy-start(f32[6,40,128]{2,1,0:T(8,128)} %copy-done.6) | copy-start | bytes 368644
  73.6 10.6 %copy-start.9 = (f32[6,40,128]{2,1,0:T(8,128)S(1)}, f32[6,40,128]{2,1,0:T(8,128)}, u32[]{:S(2)}) copy-start(f32[6,40,128]{2,1,0:T(8,128)} %copy-done.8) | copy-start | bytes 368644
  73.6 15.9 %copy-start.1 = (f32[6,80,256]{2,1,0:T(8,128)S(1)}, f32[6,80,256]{2,1,0:T(8,128)}, u32[]{:S(2)}) copy-start(f32[6,80,256]{2,1,0:T(8,128)} %copy-done) | copy-start | bytes 1474564
  73.6 15.9 %copy-start.3 = (f32[6,80,256]{2,1,0:T(8,128)S(1)}, f32[6,80,256]{2,1,0:T(8,128)}, u32[]{:S(2)}) copy-start(f32[6,80,256]{2,1,0:T(8,128)} %copy-done.2) | copy-start | bytes 1474564
  73.6 15.9 %copy-start.5 = (f32[2,80,256]{2,1,0:T(8,128)S(1)}, f32[2,80,256]{2,1,0:T(8,128)}, u32[]{:S(2)}) copy-start(f32[2,80,256]{2,1,0:T(8,128)} %copy-done.4) | copy-start | bytes 491524
  73.6 4.5 %collective-permute-start.13 = (f32[32,2,8,128]{3,2,1,0:T(8,128)S(1)}, f32[32,2,8,128]{3,2,1,0:T(8,128)S(1)}, u32[]{:S(2)}, u32[]{:S(2)}) collective-permute-start(f32[32,2,8,128]{3,2,1,0:T(8,128)S(1)} %all-to-all-done.mine), channel_id=1, source_target_pairs={{0,4},{4,0},{8,12},{12,8},{16,20},{20,16},{24,28},{28,24},{32,36},... | collective-permute-start | bytes 786440 | tf_op jit(solution)/shard_map/ppermute | solution.py:703
  76.9 3.2 %collective-permute-start.14 = (f32[32,128]{1,0:T(8,128)S(1)}, f32[32,128]{1,0:T(8,128)S(1)}, u32[]{:S(2)}, u32[]{:S(2)}) collective-permute-start(f32[32,128]{1,0:T(8,128)S(1)} %collective-permute-done.12.late), channel_id=1, source_target_pairs={{0,4},{4,0},{8,12},{12,8},{16,20},{20,16},{24,28},{28,24},{32,36},... | collective-permute-start | bytes 49160 | tf_op jit(solution)/shard_map/ppermute | solution.py:703
  80.4 3.8 %collective-permute-start.15 = (f32[2,64,128]{2,1,0:T(8,128)S(1)}, f32[2,64,128]{2,1,0:T(8,128)S(1)}, u32[]{:S(2)}, u32[]{:S(2)}) collective-permute-start(f32[2,64,128]{2,1,0:T(8,128)S(1)} %shard_map.57.e2), channel_id=1, source_target_pairs={{0,252},{4,8},{8,4},{12,16},{16,12},{20,24},{24,20},{28,32},{32,28... | collective-permute-start | bytes 196616 | tf_op jit(solution)/shard_map/ppermute | solution.py:708
  84.9 4.6 %collective-permute-start.16 = (f32[40,128]{1,0:T(8,128)S(1)}, f32[40,128]{1,0:T(8,128)S(1)}, u32[]{:S(2)}, u32[]{:S(2)}) collective-permute-start(f32[40,128]{1,0:T(8,128)S(1)} %get-tuple-element.64), channel_id=1, source_target_pairs={{0,4},{4,0},{8,12},{12,8},{16,20},{20,16},{24,28},{28,24},{32,36},... | collective-permute-start | bytes 61448 | tf_op jit(solution)/shard_map/ppermute | solution.py:703

commit v12 on v11

--- a/solution.py
+++ b/solution.py
@@ -150,14 +150,24 @@
     return jnp.where(iota((half, 128), 1) < 64, x[:half], x[half:])
 
 
-def start_kernel(f, c1, c2, c3, up, down, sems):
-    copies = []
-    for a, ref in enumerate((f, c1, c2, c3)):
-        for k, (out, row) in enumerate(((up, 56), (down, 0))):
-            copy = pltpu.make_async_copy(ref.at[:, pl.ds(row, 8), :], out.at[pl.ds(4 * a, 4)], sems.at[2 * a + k])
-            copy.start()
-            copies.append(copy)
-    for copy in copies:
+def start_kernel(f, c1, c2, c3, up, down, out_far, out_sib, rows, planes, sems):
+    par = lax.rem(lax.axis_index("wide"), 2)
+    moves = []
+    for k, (out, row) in enumerate(((up, 56), (down, 0))):
+        for a, ref in enumerate((f, c1, c2, c3)):
+            moves.append((ref.at[:, pl.ds(row, 8), :], rows.at[k, pl.ds(4 * a, 4)], out.at[pl.ds(4 * a, 4)]))
+    for k, (out, upward) in enumerate(((out_far, par), (out_sib, 1 - par))):
+        for a, ref in enumerate((f, c1, c2, c3, c1)):
+            plane = 3 * upward if a < 4 else 1
+            moves.append((ref.at[pl.ds(plane, 1)], planes.at[k, pl.ds(a, 1)], out.at[pl.ds(a, 1)]))
+    first = [pltpu.make_async_copy(src, mid, sems.at[0, k]) for k, (src, mid, _) in enumerate(moves)]
+    second = [pltpu.make_async_copy(mid, dst, sems.at[1, k]) for k, (_, mid, dst) in enumerate(moves)]
+    for copy in first:
+        copy.start()
+    for one, two in zip(first, second):
+        one.wait()
+        two.start()
+    for copy in second:
         copy.wait()
 
 
@@ -171,10 +181,11 @@
         diag = diagonal(SIG[0], own[5 + k], own[6 + k], own[9 + k], own[13 + k])
         first[k] = own[1 + k] / diag / THETA
     for out, up in ((out_far, par), (out_sib, 1 - par)):
-        for a in range(4):
-            out[80 * a : 80 * a + 80] = own[4 * a + 3 * up]
-        out[320:400] = own[5]
-        out[400:480] = first[up]
+        for a in range(5):
+            plane = 4 * a + 3 * up if a < 4 else 5
+            out[16 * a : 16 * a + 8] = own[plane, 0:8]
+            out[16 * a + 8 : 16 * a + 16] = own[plane, 72:80]
+        out[80:160] = first[up]
     k1 = jnp.concatenate([own[4], own[6]], axis=0)
     k2 = jnp.concatenate([own[8] + own[9], own[10] + own[11]], axis=0)
     k3 = jnp.concatenate([own[12] + own[13], own[14] + own[15]], axis=0)
@@ -184,12 +195,12 @@
             coef1[2 * a + p] = coarse[a][40 * p : 40 * p + 40]
     for out in (out_far, out_sib):
         for k in range(6):
-            row, lane = 480 + 40 * (k // 2), 128 * (k % 2)
+            row, lane = 160 + 40 * (k // 2), 128 * (k % 2)
             out[row : row + 40, lane : lane + 128] = coef1[k]
 
 
 def block(index):
-    row, lane = 480 + 40 * (index // 2), 128 * (index % 2)
+    row, lane = 160 + 40 * (index // 2), 128 * (index % 2)
     return slice(row, row + 40), slice(lane, lane + 128)
 
 
@@ -242,16 +253,21 @@
     return SIG[0] + c1[q, here, :] + c1[q + 1, here, :] + k2 + h2 + k3 + roll(k3, -1, 1)
 
 
-def fine_pre_kernel(own, coef1, far, sib, f, c1, c2, c3, u2, w1, out_far, out_sib, g, f1, u1, res, scr):
+def fine_pre_kernel(own, coef1, far_raw, sib_raw, far, sib, f, c1, c2, c3, u2, w1, out_far, out_sib, g, f1, u1, res, scr):
     below, above = sides(far, sib)
+    below_raw, above_raw = sides(far_raw, sib_raw)
     for a, ref in enumerate((f, c1, c2, c3)):
-        here = slice(80 * a, 80 * a + 80)
-        ref[0] = below(here)
         ref[1:5] = own[4 * a : 4 * a + 4]
-        ref[5] = above(here)
-    c1[6] = above(slice(320, 400))
-    u1[0] = below(slice(400, 480))
-    u1[7] = above(slice(400, 480))
+    for a, ref, q, raw, rest in (
+        [(a, ref, 0, below_raw, below) for a, ref in enumerate((f, c1, c2, c3))]
+        + [(a, ref, 5, above_raw, above) for a, ref in enumerate((f, c1, c2, c3))]
+        + [(4, c1, 6, above_raw, above)]
+    ):
+        ref[q, 0:8] = rest(slice(16 * a, 16 * a + 8))
+        ref[q, 8:72] = raw(a)
+        ref[q, 72:80] = rest(slice(16 * a + 8, 16 * a + 16))
+    u1[0] = below(slice(80, 160))
+    u1[7] = above(slice(80, 160))
 
     def smooth_first(q, carry):
         def rows(r0, n):
@@ -714,17 +730,19 @@
     big = (80, 256)
     inputs = (source, coef_first, coef_second, coef_third)
 
-    up, down = call(
+    up, down, far_raw, sib_raw = call(
         start_kernel,
-        [(16, 8, 256), (16, 8, 256)],
-        [pltpu.SemaphoreType.DMA((8,))],
+        [(16, 8, 256), (16, 8, 256), (5, 64, 256), (5, 64, 256)],
+        [(2, 16, 8, 256), (2, 5, 64, 256), pltpu.SemaphoreType.DMA((2, 18))],
+        {k: pltpu.HBM for k in range(4)},
         {k: pltpu.HBM for k in range(4)},
         limit=60,
     )(*inputs)
+    far_raw, sib_raw = across(far_raw), sibling(sib_raw)
     low, high = shift(up, "narrow", 1), shift(down, "narrow", -1)
 
     own, coef1, far, sib = call(
-        pad_kernel, [(16,) + big, (6, 40, 128), (600, 256), (600, 256)], [(2,) + big, (160, 128)]
+        pad_kernel, [(16,) + big, (6, 40, 128), (280, 256), (280, 256)], [(2,) + big, (160, 128)]
     )(jnp.concatenate(inputs, axis=0), low, high)
     far, sib = across(far), sibling(sib)
 
@@ -733,7 +751,7 @@
         [(6,) + big, (7,) + big, (6,) + big, (6,) + big, (6,) + big]
         + [(18, 40, 128), (8, 40, 128), (8, 40, 128)],
         [(6,) + big, (2, 40, 128), (8,) + big, (4,) + big, (160, 128)],
-    )(own, coef1, far, sib)
+    )(own, coef1, far_raw, sib_raw, far, sib)
     far1, sib1 = across(out_far), sibling(out_sib)
     (coefs,) = call(coarse_coef_kernel, [(32, 128)], [(80, 128)])(w1)
 

time: 92.1 us -> 92 us (level)
  starting transfers between devices: 46.2 us -> 43.2 us
  waiting for transfers between devices: 30.4 us -> 32 us
    ppermute x5 -> x6, waiting for transfers between devices: 20 us -> 21.5 us  [across(): lax.ppermute(x, 'wide', [(i, (i + 1 if i % 2 else i - 1) % count) for i i...]
    all_to_all x1, starting transfers between devices: 4.99 us -> 3.87 us  [body(): lax.all_to_all(send, 'wide', split_axis=0, concat_axis=0, tiled=True, axi...]
    ppermute x5 -> x6, starting transfers between devices: 7.49 us -> 6.47 us  [across(): lax.ppermute(x, 'wide', [(i, (i + 1 if i % 2 else i - 1) % count) for i i...]
    ppermute x7 -> x8, waiting for transfers between devices: 4.55 us -> 4.74 us  [sibling(): lax.ppermute(x, 'wide', [(i, i ^ 1) for i in range(lax.axis_size('wide'))])]
    ppermute x7 -> x8, starting transfers between devices: 26.1 us -> 26.2 us  [sibling(): lax.ppermute(x, 'wide', [(i, i ^ 1) for i in range(lax.axis_size('wide'))])]
  transfers between devices with their start and end apart: 18 -> 20, of which waited for: 13 -> 12; matrix products, arithmetic and copies ran while one was open for 1% -> 1% of each run, Pallas kernels for 3% -> 3%
where the time goes in v12:
time: 92 us; the launch traced here: 91.8 us
  starting transfers between devices  43.2 us (47%)
  waiting for transfers between devices  32 us (35%)
  Pallas kernels  12.8 us (14%)
  local copies, waits for them, and re-layouts  2.25 us (2%)
  other arithmetic  1.26 us (1%)
    ppermute x8, starting transfers between devices, sibling(): lax.ppermute(x, 'wide', [(i, i ^ 1) for i in range(lax.axis_size('wide'))])  26.2 us
    ppermute x6, waiting for transfers between devices, across(): lax.ppermute(x, 'wide', [(i, (i + 1 if i % 2 else i - 1) % count) for i i...  21.5 us
    pallas_call x14, Pallas kernels, run(): pl.pallas_call(kernel, out_shape=[jax.ShapeDtypeStruct(s, F32) for s in o...  12.8 us
    ppermute x5, starting transfers between devices, shift(): return lax.ppermute(x, axis, [(i, (i + by) % count) for i in range(count)])  6.75 us
    ppermute x6, starting transfers between devices, across(): lax.ppermute(x, 'wide', [(i, (i + 1 if i % 2 else i - 1) % count) for i i...  6.47 us
    ppermute x8, waiting for transfers between devices, sibling(): lax.ppermute(x, 'wide', [(i, i ^ 1) for i in range(lax.axis_size('wide'))])  4.74 us
    all_to_all x1, starting transfers between devices, body(): lax.all_to_all(send, 'wide', split_axis=0, concat_axis=0, tiled=True, axi...  3.87 us
    ppermute x5, waiting for transfers between devices, shift(): return lax.ppermute(x, axis, [(i, (i + by) % count) for i in range(count)])  3.8 us
  transfers between devices with their start and end apart: 20, of which 12 were waited for; matrix products, arithmetic and copies ran while one was open for 1% of the time, Pallas kernels for 3%

profile of v12, /device:TPU:1, one launch (start us, length us, event | category | flops | bytes accessed | tf_op | source)
XLA Modules:
  0.0 91.8 jit_solution(11872398418765017533)
XLA Ops:
  0.0 2.2 %shard_map.46 = (f32[16,8,256]{2,1,0:T(8,128)}, f32[16,8,256]{2,1,0:T(8,128)}, f32[5,64,256]{2,1,0:T(8,128)}, f32[5,64,256]{2,1,0:T(8,128)}) custom-call(f32[4,64,256]{2,1,0:T(8,128)} %f.1, f32[4,64,256]{2,1,0:T(8,128)} %c1.1, f32[4,64,256]{2,1,0:T(8,128)} %c2.1, f32[4,64,256]{2,1,0:T(8,128)} %c3.1), custom_call_target="tpu_custom_call" | custom-call | tf_op jit(solution)/shard_map/pallas_call | solution.py:136
  2.2 2.2 %collective-permute-start = (f32[16,8,256]{2,1,0:T(8,128)}, f32[16,8,256]{2,1,0:T(8,128)S(1)}, u32[]{:S(2)}, u32[]{:S(2)}) collective-permute-start(f32[16,8,256]{2,1,0:T(8,128)} %get-tuple-element.40), channel_id=1, source_target_pairs={{0,1},{1,2},{2,3},{3,0},{4,5},{5,6},{6,7},{7,4},{8,9},{9,10},{10,1... | collective-permute-start | bytes 393224 | tf_op jit(solution)/shard_map/ppermute | solution.py:715
  4.4 1.5 %collective-permute-start.1 = (f32[16,8,256]{2,1,0:T(8,128)}, f32[16,8,256]{2,1,0:T(8,128)S(1)}, u32[]{:S(2)}, u32[]{:S(2)}) collective-permute-start(f32[16,8,256]{2,1,0:T(8,128)} %get-tuple-element.41), channel_id=1, source_target_pairs={{0,3},{1,0},{2,1},{3,2},{4,7},{5,4},{6,5},{7,6},{8,11},{9,8},{10,9... | collective-permute-start | bytes 393224 | tf_op jit(solution)/shard_map/ppermute | solution.py:715
  5.9 2.6 %collective-permute-start.2 = (f32[5,64,256]{2,1,0:T(8,128)}, f32[5,64,256]{2,1,0:T(8,128)S(1)}, u32[]{:S(2)}, u32[]{:S(2)}) collective-permute-start(f32[5,64,256]{2,1,0:T(8,128)} %get-tuple-element.44), channel_id=1, source_target_pairs={{0,252},{4,8},{8,4},{12,16},{16,12},{20,24},{24,20},{28,32},{32,28... | collective-permute-start | bytes 983048 | tf_op jit(solution)/shard_map/ppermute | solution.py:724
  8.5 5.6 %collective-permute-start.3 = (f32[5,64,256]{2,1,0:T(8,128)}, f32[5,64,256]{2,1,0:T(8,128)S(1)}, u32[]{:S(2)}, u32[]{:S(2)}) collective-permute-start(f32[5,64,256]{2,1,0:T(8,128)} %get-tuple-element.45), channel_id=1, source_target_pairs={{0,4},{4,0},{8,12},{12,8},{16,20},{20,16},{24,28},{28,24},{32,36},... | collective-permute-start | bytes 983048 | tf_op jit(solution)/shard_map/ppermute | solution.py:719
  14.1 1.3 %pad_maximum_fusion.inner = f32[16,64,256]{2,1,0:T(8,128)S(1)} fusion(f32[4,64,256]{2,1,0:T(8,128)} %c3.1, f32[4,64,256]{2,1,0:T(8,128)} %c2.1, f32[4,64,256]{2,1,0:T(8,128)} %c1.1, f32[4,64,256]{2,1,0:T(8,128)} %f.1), kind=kLoop, calls=%fused_computation | loop fusion | flops 786432 | bytes 2097152 | tf_op jit(solution)/shard_map/concatenate | solution.py:746
  15.9 1.8 %collective-permute-start.5 = (f32[280,256]{1,0:T(8,128)S(1)}, f32[280,256]{1,0:T(8,128)S(1)}, u32[]{:S(2)}, u32[]{:S(2)}) collective-permute-start(f32[280,256]{1,0:T(8,128)S(1)} %get-tuple-element.47), channel_id=1, source_target_pairs={{0,4},{4,0},{8,12},{12,8},{16,20},{20,16},{24,28},{28,24},{32,36},... | collective-permute-start | bytes 860168 | tf_op jit(solution)/shard_map/ppermute | solution.py:719
  17.7 4.5 %collective-permute-done.4.far = f32[280,256]{1,0:T(8,128)S(1)} collective-permute-done((f32[280,256]{1,0:T(8,128)S(1)}, f32[280,256]{1,0:T(8,128)S(1)}, u32[]{:S(2)}, u32[]{:S(2)}) %collective-permute-start.4) | collective-permute-done | bytes 286752 | tf_op jit(solution)/shard_map/ppermute | solution.py:724
  22.2 2.4 %shard_map.48 = (f32[6,80,256]{2,1,0:T(8,128)S(1)}, f32[7,80,256]{2,1,0:T(8,128)S(1)}, f32[6,80,256]{2,1,0:T(8,128)S(1)}, f32[6,80,256]{2,1,0:T(8,128)S(1)}, f32...) custom-call(f32[16,80,256]{2,1,0:T(8,128)S(1)} %get-tuple-element.42, ...), custom_call_target="tpu_custom_call" | custom-call | tf_op jit(solution)/shard_map/pallas_call | solution.py:136
  25.5 0.8 copy-done.2
  26.2 3.0 %collective-permute-start.7 = (f32[8,40,128]{2,1,0:T(8,128)S(1)}, f32[8,40,128]{2,1,0:T(8,128)S(1)}, u32[]{:S(2)}, u32[]{:S(2)}) collective-permute-start(f32[8,40,128]{2,1,0:T(8,128)S(1)} %get-tuple-element.49), channel_id=1, source_target_pairs={{0,4},{4,0},{8,12},{12,8},{16,20},{20,16},{24,28},{28,24},{32,36},... | collective-permute-start | bytes 491528 | tf_op jit(solution)/shard_map/ppermute | solution.py:719
  30.3 3.7 %collective-permute-done.6.far = f32[8,40,128]{2,1,0:T(8,128)S(1)} collective-permute-done((f32[8,40,128]{2,1,0:T(8,128)S(1)}, f32[8,40,128]{2,1,0:T(8,128)S(1)}, u32[]{:S(2)}, u32[]{:S(2)}) %collective-permute-start.6) | collective-permute-done | bytes 163872 | tf_op jit(solution)/shard_map/ppermute | solution.py:724
  35.0 2.7 %collective-permute-start.9 = (f32[56,128]{1,0:T(8,128)S(1)}, f32[56,128]{1,0:T(8,128)S(1)}, u32[]{:S(2)}, u32[]{:S(2)}) collective-permute-start(f32[56,128]{1,0:T(8,128)S(1)} %get-tuple-element.53), channel_id=1, source_target_pairs={{0,3},{1,0},{2,1},{3,2},{4,7},{5,4},{6,5},{7,6},{8,11},{9,8},{10,9... | collective-permute-start | bytes 86024 | tf_op jit(solution)/shard_map/ppermute | solution.py:715
  38.1 3.8 %collective-permute-done.10.far = f32[40,128]{1,0:T(8,128)S(1)} collective-permute-done((f32[40,128]{1,0:T(8,128)S(1)}, f32[40,128]{1,0:T(8,128)S(1)}, u32[]{:S(2)}, u32[]{:S(2)}) %collective-permute-start.10) | collective-permute-done | bytes 20512 | tf_op jit(solution)/shard_map/ppermute | solution.py:715
  42.1 5.1 %collective-permute-start.11 = (f32[240,128]{1,0:T(8,128)S(1)}, f32[240,128]{1,0:T(8,128)S(1)}, u32[]{:S(2)}, u32[]{:S(2)}) collective-permute-start(f32[240,128]{1,0:T(8,128)S(1)} %get-tuple-element.56.msg), channel_id=1, source_target_pairs={{0,4},{4,0},{8,12},{12,8},{16,20},{20,16},{24,28},{28,24},{32,36},... | collective-permute-start | bytes 368648 | tf_op jit(solution)/shard_map/ppermute | solution.py:719
  47.2 1.0 %collective-permute-done.11.sib = f32[240,128]{1,0:T(8,128)S(1)} collective-permute-done((f32[240,128]{1,0:T(8,128)S(1)}, f32[240,128]{1,0:T(8,128)S(1)}, u32[]{:S(2)}, u32[]{:S(2)}) %collective-permute-start.11) | collective-permute-done | bytes 122912 | tf_op jit(solution)/shard_map/ppermute | solution.py:719
  48.6 4.8 %collective-permute-done.12.near = f32[384,128]{1,0:T(8,128)S(1)} collective-permute-done((f32[384,128]{1,0:T(8,128)S(1)}, f32[384,128]{1,0:T(8,128)S(1)}, u32[]{:S(2)}, u32[]{:S(2)}) %collective-permute-start.12) | collective-permute-done | bytes 196640 | tf_op jit(solution)/shard_map/ppermute | solution.py:724
  53.4 3.7 %collective-permute-start.13 = (f32[384,128]{1,0:T(8,128)S(1)}, f32[384,128]{1,0:T(8,128)S(1)}, u32[]{:S(2)}, u32[]{:S(2)}) collective-permute-start(f32[384,128]{1,0:T(8,128)S(1)} %collective-permute-done.12.near), channel_id=1, source_target_pairs={{0,4},{4,0},{8,12},{12,8},{16,20},{20,16},{24,28},{28,24},{32,36},... | collective-permute-start | bytes 589832 | tf_op jit(solution)/shard_map/ppermute | solution.py:719
  57.1 1.1 %collective-permute-done.13.other = f32[384,128]{1,0:T(8,128)S(1)} collective-permute-done((f32[384,128]{1,0:T(8,128)S(1)}, f32[384,128]{1,0:T(8,128)S(1)}, u32[]{:S(2)}, u32[]{:S(2)}) %collective-permute-start.13) | collective-permute-done | bytes 196640 | tf_op jit(solution)/shard_map/ppermute | solution.py:719
  58.5 1.0 %shard_map.55 = f32[32,2,8,128]{3,2,1,0:T(8,128)} custom-call(f32[21,64,128]{2,1,0:T(8,128)S(1)} %get-tuple-element.58.w.win, f32[4,64,128]{2,1,0:T(8,128)S(1)} %get-tuple-element.59.u2, f32[3,8,128]{2,1,0:T(8,128)S(1)} %shard_map.53.tiles), custom_call_target="tpu_custom_call" | custom-call | tf_op jit(solution)/shard_map/pallas_call | solution.py:136
  59.5 3.9 %all-to-all-start = ((f32[32,2,8,128]{3,2,1,0:T(8,128)}), f32[32,2,8,128]{3,2,1,0:T(8,128)S(1)}, u32[]{:S(2)}, u32[]{:S(2)}) async-start(f32[32,2,8,128]{3,2,1,0:T(8,128)} %shard_map.55), calls=%async_computation | async-start | bytes 524288 | tf_op jit(solution)/shard_map/all_to_all | solution.py:777
  63.4 1.7 %collective-permute-start.14 = (f32[32,128]{1,0:T(8,128)S(1)}, f32[32,128]{1,0:T(8,128)S(1)}, u32[]{:S(2)}, u32[]{:S(2)}) collective-permute-start(f32[32,128]{1,0:T(8,128)S(1)} %get-tuple-element.61), channel_id=1, source_target_pairs={{0,252},{4,8},{8,4},{12,16},{16,12},{20,24},{24,20},{28,32},{32,28... | collective-permute-start | bytes 49160 | tf_op jit(solution)/shard_map/ppermute | solution.py:724
  65.1 6.5 %collective-permute-done.14.late = f32[32,128]{1,0:T(8,128)S(1)} collective-permute-done((f32[32,128]{1,0:T(8,128)S(1)}, f32[32,128]{1,0:T(8,128)S(1)}, u32[]{:S(2)}, u32[]{:S(2)}) %collective-permute-start.14) | collective-permute-done | bytes 16416 | tf_op jit(solution)/shard_map/ppermute | solution.py:724
  71.6 2.0 %all-to-all-done.mine = f32[32,2,8,128]{3,2,1,0:T(8,128)S(1)} async-done(((f32[32,2,8,128]{3,2,1,0:T(8,128)}), f32[32,2,8,128]{3,2,1,0:T(8,128)S(1)}, u32[]{:S(2)}, u32[]{:S(2)}) %all-to-all-start) | async-done | bytes 262176 | tf_op jit(solution)/shard_map/all_to_all | solution.py:777
  73.6 3.2 %collective-permute-start.15 = (f32[32,2,8,128]{3,2,1,0:T(8,128)S(1)}, f32[32,2,8,128]{3,2,1,0:T(8,128)S(1)}, u32[]{:S(2)}, u32[]{:S(2)}) collective-permute-start(f32[32,2,8,128]{3,2,1,0:T(8,128)S(1)} %all-to-all-done.mine), channel_id=1, source_target_pairs={{0,4},{4,0},{8,12},{12,8},{16,20},{20,16},{24,28},{28,24},{32,36},... | collective-permute-start | bytes 786440 | tf_op jit(solution)/shard_map/ppermute | solution.py:719
  76.9 1.1 %collective-permute-done.15.theirs = f32[32,2,8,128]{3,2,1,0:T(8,128)S(1)} collective-permute-done((f32[32,2,8,128]{3,2,1,0:T(8,128)S(1)}, f32[32,2,8,128]{3,2,1,0:T(8,128)S(1)}, u32[]{:S(2)}, u32[]{:S(2)}) %collective-permute-start.15) | collective-permute-done | bytes 262176 | tf_op jit(solution)/shard_map/ppermute | solution.py:719
  78.0 2.0 %shard_map.56.e2 = f32[192,128]{1,0:T(8,128)S(1)} custom-call(f32[32,2,8,128]{3,2,1,0:T(8,128)S(1)} %all-to-all-done.mine, f32[32,2,8,128]{3,2,1,0:T(8,128)S(1)} %collective-permute-done.15.theirs), custom_call_target="tpu_custom_call" | custom-call | tf_op jit(solution)/shard_map/pallas_call | solution.py:136
  80.3 1.9 %collective-permute-start.17 = (f32[2,64,128]{2,1,0:T(8,128)S(1)}, f32[2,64,128]{2,1,0:T(8,128)S(1)}, u32[]{:S(2)}, u32[]{:S(2)}) collective-permute-start(f32[2,64,128]{2,1,0:T(8,128)S(1)} %shard_map.57.e2), channel_id=1, source_target_pairs={{0,252},{4,8},{8,4},{12,16},{16,12},{20,24},{24,20},{28,32},{32,28... | collective-permute-start | bytes 196616 | tf_op jit(solution)/shard_map/ppermute | solution.py:724
  82.2 2.0 %collective-permute-done.17.far = f32[2,64,128]{2,1,0:T(8,128)S(1)} collective-permute-done((f32[2,64,128]{2,1,0:T(8,128)S(1)}, f32[2,64,128]{2,1,0:T(8,128)S(1)}, u32[]{:S(2)}, u32[]{:S(2)}) %collective-permute-start.17) | collective-permute-done | bytes 65568 | tf_op jit(solution)/shard_map/ppermute | solution.py:724
  84.9 3.7 %collective-permute-start.18 = (f32[40,128]{1,0:T(8,128)S(1)}, f32[40,128]{1,0:T(8,128)S(1)}, u32[]{:S(2)}, u32[]{:S(2)}) collective-permute-start(f32[40,128]{1,0:T(8,128)S(1)} %get-tuple-element.68), channel_id=1, source_target_pairs={{0,4},{4,0},{8,12},{12,8},{16,20},{20,16},{24,28},{28,24},{32,36},... | collective-permute-start | bytes 61448 | tf_op jit(solution)/shard_map/ppermute | solution.py:719
  88.5 0.8 collective-permute-done.18.other
  89.4 2.4 %shard_map.59 = f32[4,64,256]{2,1,0:T(8,128)} custom-call(f32[2,40,128]{2,1,0:T(8,128)S(1)} %get-tuple-element.66.e1, f32[40,128]{1,0:T(8,128)S(1)} %get-tuple-element.67.edge, f32[40,128]{1,0:T(8,128)S(1)} %collective-permute-done.18.other, f32[2,80,256]{2,1,0:T(8,128)S(1)} %copy-done.5, f32[6,80,256]{2,1,0:T(8,128)S(1)} %get-tuple-element.70.f, ...), custom_call_target="tpu_custom_call" | custom-call | tf_op jit(solution)/shard_map/pallas_call | solution.py:136
  (43 shorter events, 5.7 us)
Async XLA Ops:
  2.2 13.2 %collective-permute-start = (f32[16,8,256]{2,1,0:T(8,128)}, f32[16,8,256]{2,1,0:T(8,128)S(1)}, u32[]{:S(2)}, u32[]{:S(2)}) collective-permute-start(f32[16,8,256]{2,1,0:T(8,128)} %get-tuple-element.40), channel_id=1, source_target_pairs={{0,1},{1,2},{2,3},{3,0},{4,5},{5,6},{6,7},{7,4},{8,9},{9,10},{10,1... | collective-permute-start | bytes 393224 | tf_op jit(solution)/shard_map/ppermute | solution.py:715
  4.4 11.0 %collective-permute-start.1 = (f32[16,8,256]{2,1,0:T(8,128)}, f32[16,8,256]{2,1,0:T(8,128)S(1)}, u32[]{:S(2)}, u32[]{:S(2)}) collective-permute-start(f32[16,8,256]{2,1,0:T(8,128)} %get-tuple-element.41), channel_id=1, source_target_pairs={{0,3},{1,0},{2,1},{3,2},{4,7},{5,4},{6,5},{7,6},{8,11},{9,8},{10,9... | collective-permute-start | bytes 393224 | tf_op jit(solution)/shard_map/ppermute | solution.py:715
  5.9 11.8 %collective-permute-start.2 = (f32[5,64,256]{2,1,0:T(8,128)}, f32[5,64,256]{2,1,0:T(8,128)S(1)}, u32[]{:S(2)}, u32[]{:S(2)}) collective-permute-start(f32[5,64,256]{2,1,0:T(8,128)} %get-tuple-element.44), channel_id=1, source_target_pairs={{0,252},{4,8},{8,4},{12,16},{16,12},{20,24},{24,20},{28,32},{32,28... | collective-permute-start | bytes 983048 | tf_op jit(solution)/shard_map/ppermute | solution.py:724
  8.5 9.2 %collective-permute-start.3 = (f32[5,64,256]{2,1,0:T(8,128)}, f32[5,64,256]{2,1,0:T(8,128)S(1)}, u32[]{:S(2)}, u32[]{:S(2)}) collective-permute-start(f32[5,64,256]{2,1,0:T(8,128)} %get-tuple-element.45), channel_id=1, source_target_pairs={{0,4},{4,0},{8,12},{12,8},{16,20},{20,16},{24,28},{28,24},{32,36},... | collective-permute-start | bytes 983048 | tf_op jit(solution)/shard_map/ppermute | solution.py:719
  15.8 6.4 %collective-permute-start.4 = (f32[280,256]{1,0:T(8,128)S(1)}, f32[280,256]{1,0:T(8,128)S(1)}, u32[]{:S(2)}, u32[]{:S(2)}) collective-permute-start(f32[280,256]{1,0:T(8,128)S(1)} %get-tuple-element.46), channel_id=1, source_target_pairs={{0,252},{4,8},{8,4},{12,16},{16,12},{20,24},{24,20},{28,32},{32,28... | collective-permute-start | bytes 860168 | tf_op jit(solution)/shard_map/ppermute | solution.py:724
  15.9 6.3 %collective-permute-start.5 = (f32[280,256]{1,0:T(8,128)S(1)}, f32[280,256]{1,0:T(8,128)S(1)}, u32[]{:S(2)}, u32[]{:S(2)}) collective-permute-start(f32[280,256]{1,0:T(8,128)S(1)} %get-tuple-element.47), channel_id=1, source_target_pairs={{0,4},{4,0},{8,12},{12,8},{16,20},{20,16},{24,28},{28,24},{32,36},... | collective-permute-start | bytes 860168 | tf_op jit(solution)/shard_map/ppermute | solution.py:719
  24.7 0.8 copy-start
  25.5 0.8 copy-start.2
  26.2 4.1 %collective-permute-start.7 = (f32[8,40,128]{2,1,0:T(8,128)S(1)}, f32[8,40,128]{2,1,0:T(8,128)S(1)}, u32[]{:S(2)}, u32[]{:S(2)}) collective-permute-start(f32[8,40,128]{2,1,0:T(8,128)S(1)} %get-tuple-element.49), channel_id=1, source_target_pairs={{0,4},{4,0},{8,12},{12,8},{16,20},{20,16},{24,28},{28,24},{32,36},... | collective-permute-start | bytes 491528 | tf_op jit(solution)/shard_map/ppermute | solution.py:719
  29.3 4.7 %collective-permute-start.6 = (f32[8,40,128]{2,1,0:T(8,128)S(1)}, f32[8,40,128]{2,1,0:T(8,128)S(1)}, u32[]{:S(2)}, u32[]{:S(2)}) collective-permute-start(f32[8,40,128]{2,1,0:T(8,128)S(1)} %get-tuple-element.48.own), channel_id=1, source_target_pairs={{0,252},{4,8},{8,4},{12,16},{16,12},{20,24},{24,20},{28,32},{32,28... | collective-permute-start | bytes 491528 | tf_op jit(solution)/shard_map/ppermute | solution.py:724
  34.4 0.7 copy-start.4
  35.0 23.5 %copy-start.6 = (f32[6,40,128]{2,1,0:T(8,128)}, f32[6,40,128]{2,1,0:T(8,128)S(1)}, u32[]{:S(2)}) copy-start(f32[6,40,128]{2,1,0:T(8,128)S(1)} %get-tuple-element.64.f) | copy-start | bytes 368644
  35.0 23.5 %copy-start.8 = (f32[6,40,128]{2,1,0:T(8,128)}, f32[6,40,128]{2,1,0:T(8,128)S(1)}, u32[]{:S(2)}) copy-start(f32[6,40,128]{2,1,0:T(8,128)S(1)} %get-tuple-element.65.g) | copy-start | bytes 368644
  35.0 6.8 %collective-permute-start.8 = (f32[56,128]{1,0:T(8,128)S(1)}, f32[56,128]{1,0:T(8,128)S(1)}, u32[]{:S(2)}, u32[]{:S(2)}) collective-permute-start(f32[56,128]{1,0:T(8,128)S(1)} %get-tuple-element.52), channel_id=1, source_target_pairs={{0,1},{1,2},{2,3},{3,0},{4,5},{5,6},{6,7},{7,4},{8,9},{9,10},{10,1... | collective-permute-start | bytes 86024 | tf_op jit(solution)/shard_map/ppermute | solution.py:715
  35.0 6.8 %collective-permute-start.9 = (f32[56,128]{1,0:T(8,128)S(1)}, f32[56,128]{1,0:T(8,128)S(1)}, u32[]{:S(2)}, u32[]{:S(2)}) collective-permute-start(f32[56,128]{1,0:T(8,128)S(1)} %get-tuple-element.53), channel_id=1, source_target_pairs={{0,3},{1,0},{2,1},{3,2},{4,7},{5,4},{6,5},{7,6},{8,11},{9,8},{10,9... | collective-permute-start | bytes 86024 | tf_op jit(solution)/shard_map/ppermute | solution.py:715
  37.7 4.1 %collective-permute-start.10 = (f32[40,128]{1,0:T(8,128)S(1)}, f32[40,128]{1,0:T(8,128)S(1)}, u32[]{:S(2)}, u32[]{:S(2)}) collective-permute-start(f32[40,128]{1,0:T(8,128)S(1)} %get-tuple-element.51.f2), channel_id=1, source_target_pairs={{0,2},{1,3},{2,0},{3,1},{4,6},{5,7},{6,4},{7,5},{8,10},{9,11},{10,... | collective-permute-start | bytes 61448 | tf_op jit(solution)/shard_map/ppermute | solution.py:715
  42.1 6.1 %collective-permute-start.11 = (f32[240,128]{1,0:T(8,128)S(1)}, f32[240,128]{1,0:T(8,128)S(1)}, u32[]{:S(2)}, u32[]{:S(2)}) collective-permute-start(f32[240,128]{1,0:T(8,128)S(1)} %get-tuple-element.56.msg), channel_id=1, source_target_pairs={{0,4},{4,0},{8,12},{12,8},{16,20},{20,16},{24,28},{28,24},{32,36},... | collective-permute-start | bytes 368648 | tf_op jit(solution)/shard_map/ppermute | solution.py:719
  48.2 5.2 %collective-permute-start.12 = (f32[384,128]{1,0:T(8,128)S(1)}, f32[384,128]{1,0:T(8,128)S(1)}, u32[]{:S(2)}, u32[]{:S(2)}) collective-permute-start(f32[384,128]{1,0:T(8,128)S(1)} %shard_map.52), channel_id=1, source_target_pairs={{0,252},{4,8},{8,4},{12,16},{16,12},{20,24},{24,20},{28,32},{32,28... | collective-permute-start | bytes 589832 | tf_op jit(solution)/shard_map/ppermute | solution.py:724
  53.4 4.8 %collective-permute-start.13 = (f32[384,128]{1,0:T(8,128)S(1)}, f32[384,128]{1,0:T(8,128)S(1)}, u32[]{:S(2)}, u32[]{:S(2)}) collective-permute-start(f32[384,128]{1,0:T(8,128)S(1)} %collective-permute-done.12.near), channel_id=1, source_target_pairs={{0,4},{4,0},{8,12},{12,8},{16,20},{20,16},{24,28},{28,24},{32,36},... | collective-permute-start | bytes 589832 | tf_op jit(solution)/shard_map/ppermute | solution.py:719
  59.5 14.1 %all-to-all-start = ((f32[32,2,8,128]{3,2,1,0:T(8,128)}), f32[32,2,8,128]{3,2,1,0:T(8,128)S(1)}, u32[]{:S(2)}, u32[]{:S(2)}) async-start(f32[32,2,8,128]{3,2,1,0:T(8,128)} %shard_map.55), calls=%async_computation | async-start | bytes 524288 | tf_op jit(solution)/shard_map/all_to_all | solution.py:777
  63.4 8.2 %collective-permute-start.14 = (f32[32,128]{1,0:T(8,128)S(1)}, f32[32,128]{1,0:T(8,128)S(1)}, u32[]{:S(2)}, u32[]{:S(2)}) collective-permute-start(f32[32,128]{1,0:T(8,128)S(1)} %get-tuple-element.61), channel_id=1, source_target_pairs={{0,252},{4,8},{8,4},{12,16},{16,12},{20,24},{24,20},{28,32},{32,28... | collective-permute-start | bytes 49160 | tf_op jit(solution)/shard_map/ppermute | solution.py:724
  73.6 10.6 %copy-start.7 = (f32[6,40,128]{2,1,0:T(8,128)S(1)}, f32[6,40,128]{2,1,0:T(8,128)}, u32[]{:S(2)}) copy-start(f32[6,40,128]{2,1,0:T(8,128)} %copy-done.6) | copy-start | bytes 368644
  73.6 10.6 %copy-start.9 = (f32[6,40,128]{2,1,0:T(8,128)S(1)}, f32[6,40,128]{2,1,0:T(8,128)}, u32[]{:S(2)}) copy-start(f32[6,40,128]{2,1,0:T(8,128)} %copy-done.8) | copy-start | bytes 368644
  73.6 15.8 %copy-start.1 = (f32[6,80,256]{2,1,0:T(8,128)S(1)}, f32[6,80,256]{2,1,0:T(8,128)}, u32[]{:S(2)}) copy-start(f32[6,80,256]{2,1,0:T(8,128)} %copy-done) | copy-start | bytes 1474564
  73.6 15.8 %copy-start.3 = (f32[6,80,256]{2,1,0:T(8,128)S(1)}, f32[6,80,256]{2,1,0:T(8,128)}, u32[]{:S(2)}) copy-start(f32[6,80,256]{2,1,0:T(8,128)} %copy-done.2) | copy-start | bytes 1474564
  73.6 15.8 %copy-start.5 = (f32[2,80,256]{2,1,0:T(8,128)S(1)}, f32[2,80,256]{2,1,0:T(8,128)}, u32[]{:S(2)}) copy-start(f32[2,80,256]{2,1,0:T(8,128)} %copy-done.4) | copy-start | bytes 491524
  73.6 4.4 %collective-permute-start.15 = (f32[32,2,8,128]{3,2,1,0:T(8,128)S(1)}, f32[32,2,8,128]{3,2,1,0:T(8,128)S(1)}, u32[]{:S(2)}, u32[]{:S(2)}) collective-permute-start(f32[32,2,8,128]{3,2,1,0:T(8,128)S(1)} %all-to-all-done.mine), channel_id=1, source_target_pairs={{0,4},{4,0},{8,12},{12,8},{16,20},{20,16},{24,28},{28,24},{32,36},... | collective-permute-start | bytes 786440 | tf_op jit(solution)/shard_map/ppermute | solution.py:719
  76.8 3.2 %collective-permute-start.16 = (f32[32,128]{1,0:T(8,128)S(1)}, f32[32,128]{1,0:T(8,128)S(1)}, u32[]{:S(2)}, u32[]{:S(2)}) collective-permute-start(f32[32,128]{1,0:T(8,128)S(1)} %collective-permute-done.14.late), channel_id=1, source_target_pairs={{0,4},{4,0},{8,12},{12,8},{16,20},{20,16},{24,28},{28,24},{32,36},... | collective-permute-start | bytes 49160 | tf_op jit(solution)/shard_map/ppermute | solution.py:719
  80.3 3.9 %collective-permute-start.17 = (f32[2,64,128]{2,1,0:T(8,128)S(1)}, f32[2,64,128]{2,1,0:T(8,128)S(1)}, u32[]{:S(2)}, u32[]{:S(2)}) collective-permute-start(f32[2,64,128]{2,1,0:T(8,128)S(1)} %shard_map.57.e2), channel_id=1, source_target_pairs={{0,252},{4,8},{8,4},{12,16},{16,12},{20,24},{24,20},{28,32},{32,28... | collective-permute-start | bytes 196616 | tf_op jit(solution)/shard_map/ppermute | solution.py:724
  84.9 4.5 %collective-permute-start.18 = (f32[40,128]{1,0:T(8,128)S(1)}, f32[40,128]{1,0:T(8,128)S(1)}, u32[]{:S(2)}, u32[]{:S(2)}) collective-permute-start(f32[40,128]{1,0:T(8,128)S(1)} %get-tuple-element.68), channel_id=1, source_target_pairs={{0,4},{4,0},{8,12},{12,8},{16,20},{20,16},{24,28},{28,24},{32,36},... | collective-permute-start | bytes 61448 | tf_op jit(solution)/shard_map/ppermute | solution.py:719

commit v13 on v12

--- a/solution.py
+++ b/solution.py
@@ -253,7 +253,7 @@
     return SIG[0] + c1[q, here, :] + c1[q + 1, here, :] + k2 + h2 + k3 + roll(k3, -1, 1)
 
 
-def fine_pre_kernel(own, coef1, far_raw, sib_raw, far, sib, f, c1, c2, c3, u2, w1, out_far, out_sib, g, f1, u1, res, scr):
+def fine_pre_kernel(own, coef1, far_raw, sib_raw, far, sib, halo, u2, w1, out_far, out_sib, f, c1, c2, c3, g, f1, u1, res, scr):
     below, above = sides(far, sib)
     below_raw, above_raw = sides(far_raw, sib_raw)
     for a, ref in enumerate((f, c1, c2, c3)):
@@ -266,6 +266,10 @@
         ref[q, 0:8] = rest(slice(16 * a, 16 * a + 8))
         ref[q, 8:72] = raw(a)
         ref[q, 72:80] = rest(slice(16 * a + 8, 16 * a + 16))
+    for a, ref in enumerate((f, c1, c2, c3)):
+        halo[a] = ref[0]
+        halo[4 + a] = ref[5]
+    halo[8] = c1[6]
     u1[0] = below(slice(80, 160))
     u1[7] = above(slice(80, 160))
 
@@ -420,7 +424,12 @@
     out[344:384] = w1[4]
 
 
-def coarse_pre_kernel(own, sib, near, other, w, u2, late, u1):
+def coarse_pre_kernel(own, msg, sib, near, other, w, u2, late, fine, u1):
+    for p in range(2):
+        fine[p] = sib[160 + 40 * p : 200 + 40 * p]
+        fine[2 + p] = msg[160 + 40 * p : 200 + 40 * p]
+    for p in range(4):
+        fine[4 + p] = near[224 + 40 * p : 264 + 40 * p]
     odd = lax.rem(lax.axis_index("wide"), 2) == 1
 
     def below(k):
@@ -640,7 +649,7 @@
         out[p] = second_post(w[p + 1], v[p + 2], w[p], w[p + 2], *args(p + 1))
 
 
-def middle_post_kernel(e2, far, msg, sib, near, f, g, w1, own, edge, send, fine, c1, v, w):
+def middle_post_kernel(e2, far, u2, f, g, w1, own, edge, send, fine, c1, v, w):
     n, par = lax.axis_index("narrow"), lax.rem(lax.axis_index("wide"), 2)
     odd = par == 1
     row, col = iota((40, 64), 0), iota((40, 64), 1)
@@ -650,10 +659,8 @@
     for k in range(4):
         fine[k] = mul(mul_left(pick, jnp.where(odd, planes[k], planes[(k + 2) % 4])), lanes)
     c1[0:6] = w1[0:6]
-    c1[6] = near[344:384]
-    ours = [msg[160 + 40 * p : 200 + 40 * p] for p in range(2)]
-    sibs = [sib[160 + 40 * p : 200 + 40 * p] for p in range(2)]
-    next_chip = [near[224 + 40 * p : 264 + 40 * p] for p in range(3)]
+    c1[6] = u2[7]
+    sibs, ours, next_chip = ([u2[k] for k in some] for some in ((0, 1), (2, 3), (4, 5, 6)))
     upper = sibs + ours + next_chip
     lower = [next_chip[2]] + next_chip[:2] + ours + sibs
     for i in range(7):
@@ -672,7 +679,15 @@
     send[...] = jnp.where(odd, out[0], out[2])
 
 
-def fine_post_kernel(e1, edge, other, outer, f, c1, c2, c3, u2, out, g, v, w, scr):
+def fine_post_kernel(e1, edge, other, outer, inner, low, high, halo, u2, out, f, c1, c2, c3, g, v, w, scr):
+    for a, ref in enumerate((f, c1, c2, c3)):
+        ref[0] = halo[a]
+        ref[5] = halo[4 + a]
+        for p in range(4):
+            ref[p + 1, 0:8] = low[4 * a + p]
+            ref[p + 1, 8:72] = inner[4 * a + p]
+            ref[p + 1, 72:80] = high[4 * a + p]
+    c1[6] = halo[8]
     below, above = sides(edge, other)
     x = jnp.concatenate([below(...), e1[0], e1[1], above(...)], axis=0)
     for half in range(2):
@@ -739,18 +754,19 @@
         limit=60,
     )(*inputs)
     far_raw, sib_raw = across(far_raw), sibling(sib_raw)
-    low, high = shift(up, "narrow", 1), shift(down, "narrow", -1)
+    low0, high0 = shift(up, "narrow", 1), shift(down, "narrow", -1)
 
     own, coef1, far, sib = call(
         pad_kernel, [(16,) + big, (6, 40, 128), (280, 256), (280, 256)], [(2,) + big, (160, 128)]
-    )(jnp.concatenate(inputs, axis=0), low, high)
+    )(jnp.concatenate(inputs, axis=0), low0, high0)
     far, sib = across(far), sibling(sib)
 
-    f, c1, c2, c3, u2, w1, out_far, out_sib = call(
+    windows = [(6,) + big, (7,) + big, (6,) + big, (6,) + big]
+    halo, u2, w1, out_far, out_sib = call(
         fine_pre_kernel,
-        [(6,) + big, (7,) + big, (6,) + big, (6,) + big, (6,) + big]
-        + [(18, 40, 128), (8, 40, 128), (8, 40, 128)],
-        [(6,) + big, (2, 40, 128), (8,) + big, (4,) + big, (160, 128)],
+        [(9,) + big, (6,) + big, (18, 40, 128), (8, 40, 128), (8, 40, 128)],
+        windows + [(6,) + big, (2, 40, 128), (8,) + big, (4,) + big, (160, 128)],
+        limit=6,
     )(own, coef1, far_raw, sib_raw, far, sib)
     far1, sib1 = across(out_far), sibling(out_sib)
     (coefs,) = call(coarse_coef_kernel, [(32, 128)], [(80, 128)])(w1)
@@ -768,9 +784,9 @@
     (tiles,) = call(coarse_tiles_kernel, [(3, 8, 128)], [(64, 128)])(msg, sib)
     near, tiles = lax.optimization_barrier((near, tiles))
     other = sibling(near)
-    w2, u2w, late = call(
-        coarse_pre_kernel, [(21, 64, 128), (4, 64, 128), (32, 128)], [(6, 64, 128)]
-    )(own2, sib, near, other)
+    w2, u2w, late, fine1 = call(
+        coarse_pre_kernel, [(21, 64, 128), (4, 64, 128), (32, 128), (8, 40, 128)], [(6, 64, 128)]
+    )(own2, msg, sib, near, other)
     (send,) = call(coarse_send_kernel, [(n3, 2, 8, 128)], [(64, 128)])(w2, u2w, tiles)
     late = across(late)
     cores = [[k for k in range(wide) if k % 2 == c] for c in range(2)]
@@ -786,18 +802,22 @@
         + [(n4 + 1, 8, 128), four, four, four, (n4 + 2, 8, 128), (n4 + 2, 8, 128), four, (32, 128)],
     )(parts, theirs)
     (e2,) = call(coarse_post_kernel, [(2, 64, 128)])(fine2, w2, u2w, late, late_sib)
+    e2, *again = lax.optimization_barrier((e2,) + inputs)
     far = across(e2)
 
     e1, edge, send = call(
         middle_post_kernel,
         [(2, 40, 128), (40, 128), (40, 128)],
         [(4, 40, 128), (7, 40, 128), (7, 40, 128), (7, 40, 128)],
-    )(e2, far, msg, sib, near, f1w, g1w, w1)
+    )(e2, far, fine1, f1w, g1w, w1)
     other1 = sibling(send)
 
     (out,) = call(
-        fine_post_kernel, [(4, 64, 256)], [(6,) + big, (8,) + big, (8,) + big, (320, 128)]
-    )(e1, edge, other1, outer, f, c1, c2, c3, u2)
+        fine_post_kernel,
+        [(4, 64, 256)],
+        windows + [(6,) + big, (8,) + big, (8,) + big, (320, 128)],
+        limit=6,
+    )(e1, edge, other1, outer, jnp.concatenate(again, axis=0), low0, high0, halo, u2)
     return out
 
 

time: 92 us -> 90 us (0.978)
  local copies, waits for them, and re-layouts: 2.25 us -> 0.01 us
    unnamed x20 -> x8, local copies, waits for them, and re-layouts: 2.25 us -> 0.01 us
  transfers between devices with their start and end apart: 20 -> 20, of which waited for: 12 -> 12; matrix products, arithmetic and copies ran while one was open for 1% -> 2% of each run, Pallas kernels for 3% -> 3%
where the time goes in v13:
time: 90 us; the launch traced here: 89.7 us
  starting transfers between devices  43.5 us (48%)
  waiting for transfers between devices  31.9 us (35%)
  Pallas kernels  12.8 us (14%)
  other arithmetic  1.35 us (2%)
    ppermute x8, starting transfers between devices, sibling(): lax.ppermute(x, 'wide', [(i, i ^ 1) for i in range(lax.axis_size('wide'))])  26.3 us
    ppermute x6, waiting for transfers between devices, across(): lax.ppermute(x, 'wide', [(i, (i + 1 if i % 2 else i - 1) % count) for i i...  21.5 us
    pallas_call x14, Pallas kernels, run(): pl.pallas_call(kernel, out_shape=[jax.ShapeDtypeStruct(s, F32) for s in o...  12.8 us
    ppermute x5, starting transfers between devices, shift(): return lax.ppermute(x, axis, [(i, (i + by) % count) for i in range(count)])  6.82 us
    ppermute x6, starting transfers between devices, across(): lax.ppermute(x, 'wide', [(i, (i + 1 if i % 2 else i - 1) % count) for i i...  6.47 us
    ppermute x8, waiting for transfers between devices, sibling(): lax.ppermute(x, 'wide', [(i, i ^ 1) for i in range(lax.axis_size('wide'))])  4.62 us
    all_to_all x1, starting transfers between devices, body(): lax.all_to_all(send, 'wide', split_axis=0, concat_axis=0, tiled=True, axi...  3.87 us
    ppermute x5, waiting for transfers between devices, shift(): return lax.ppermute(x, axis, [(i, (i + by) % count) for i in range(count)])  3.8 us
  transfers between devices with their start and end apart: 20, of which 12 were waited for; matrix products, arithmetic and copies ran while one was open for 2% of the time, Pallas kernels for 3%

profile of v13, /device:TPU:1, one launch (start us, length us, event | category | flops | bytes accessed | tf_op | source)
XLA Modules:
  0.0 89.7 jit_solution(14911548347325890003)
XLA Ops:
  0.0 2.1 %shard_map.46 = (f32[16,8,256]{2,1,0:T(8,128)}, f32[16,8,256]{2,1,0:T(8,128)}, f32[5,64,256]{2,1,0:T(8,128)}, f32[5,64,256]{2,1,0:T(8,128)}) custom-call(f32[4,64,256]{2,1,0:T(8,128)} %f.1, f32[4,64,256]{2,1,0:T(8,128)} %c1.1, f32[4,64,256]{2,1,0:T(8,128)} %c2.1, f32[4,64,256]{2,1,0:T(8,128)} %c3.1), custom_call_target="tpu_custom_call" | custom-call | tf_op jit(solution)/shard_map/pallas_call | solution.py:136
  2.2 2.2 %collective-permute-start = (f32[16,8,256]{2,1,0:T(8,128)}, f32[16,8,256]{2,1,0:T(8,128)S(1)}, u32[]{:S(2)}, u32[]{:S(2)}) collective-permute-start(f32[16,8,256]{2,1,0:T(8,128)} %get-tuple-element.43), channel_id=1, source_target_pairs={{0,1},{1,2},{2,3},{3,0},{4,5},{5,6},{6,7},{7,4},{8,9},{9,10},{10,1... | collective-permute-start | bytes 393224 | tf_op jit(solution)/shard_map/ppermute | solution.py:730
  4.4 1.5 %collective-permute-start.1 = (f32[16,8,256]{2,1,0:T(8,128)}, f32[16,8,256]{2,1,0:T(8,128)S(1)}, u32[]{:S(2)}, u32[]{:S(2)}) collective-permute-start(f32[16,8,256]{2,1,0:T(8,128)} %get-tuple-element.44), channel_id=1, source_target_pairs={{0,3},{1,0},{2,1},{3,2},{4,7},{5,4},{6,5},{7,6},{8,11},{9,8},{10,9... | collective-permute-start | bytes 393224 | tf_op jit(solution)/shard_map/ppermute | solution.py:730
  5.9 2.6 %collective-permute-start.2 = (f32[5,64,256]{2,1,0:T(8,128)}, f32[5,64,256]{2,1,0:T(8,128)S(1)}, u32[]{:S(2)}, u32[]{:S(2)}) collective-permute-start(f32[5,64,256]{2,1,0:T(8,128)} %get-tuple-element.47), channel_id=1, source_target_pairs={{0,252},{4,8},{8,4},{12,16},{16,12},{20,24},{24,20},{28,32},{32,28... | collective-permute-start | bytes 983048 | tf_op jit(solution)/shard_map/ppermute | solution.py:739
  8.5 5.6 %collective-permute-start.3 = (f32[5,64,256]{2,1,0:T(8,128)}, f32[5,64,256]{2,1,0:T(8,128)S(1)}, u32[]{:S(2)}, u32[]{:S(2)}) collective-permute-start(f32[5,64,256]{2,1,0:T(8,128)} %get-tuple-element.48), channel_id=1, source_target_pairs={{0,4},{4,0},{8,12},{12,8},{16,20},{20,16},{24,28},{28,24},{32,36},... | collective-permute-start | bytes 983048 | tf_op jit(solution)/shard_map/ppermute | solution.py:734
  14.1 1.3 %pad_maximum_fusion.inner = f32[16,64,256]{2,1,0:T(8,128)S(1)} fusion(f32[4,64,256]{2,1,0:T(8,128)} %c3.1, f32[4,64,256]{2,1,0:T(8,128)} %c2.1, f32[4,64,256]{2,1,0:T(8,128)} %c1.1, f32[4,64,256]{2,1,0:T(8,128)} %f.1), kind=kLoop, calls=%fused_computation | loop fusion | flops 786432 | bytes 2097152 | tf_op jit(solution)/shard_map/concatenate | solution.py:761
  15.9 1.8 %collective-permute-start.5 = (f32[280,256]{1,0:T(8,128)S(1)}, f32[280,256]{1,0:T(8,128)S(1)}, u32[]{:S(2)}, u32[]{:S(2)}) collective-permute-start(f32[280,256]{1,0:T(8,128)S(1)} %get-tuple-element.50), channel_id=1, source_target_pairs={{0,4},{4,0},{8,12},{12,8},{16,20},{20,16},{24,28},{28,24},{32,36},... | collective-permute-start | bytes 860168 | tf_op jit(solution)/shard_map/ppermute | solution.py:734
  17.7 4.5 %collective-permute-done.4.far = f32[280,256]{1,0:T(8,128)S(1)} collective-permute-done((f32[280,256]{1,0:T(8,128)S(1)}, f32[280,256]{1,0:T(8,128)S(1)}, u32[]{:S(2)}, u32[]{:S(2)}) %collective-permute-start.4) | collective-permute-done | bytes 286752 | tf_op jit(solution)/shard_map/ppermute | solution.py:739
  22.2 2.4 %shard_map.48 = (f32[9,80,256]{2,1,0:T(8,128)S(1)}, f32[6,80,256]{2,1,0:T(8,128)S(1)}, f32[18,40,128]{2,1,0:T(8,128)S(1)}, f32[8,40,128]{2,1,0:T(8,128)S(1)}, f32[8,40,128]{2,1,0:T(8,128)S(1)}) custom-call(f32[16,80,256]{2,1,0:T(8,128)S(1)} %get-tuple-element.45.own, f32[6,40,128]{2,1,0:T(8,128)S(1)} %get-tuple-element.46.coef1, ...), custom_call_target="tpu_custom_call" | custom-call | tf_op jit(solution)/shard_map/pallas_call | solution.py:136
  24.6 3.1 %collective-permute-start.7 = (f32[8,40,128]{2,1,0:T(8,128)S(1)}, f32[8,40,128]{2,1,0:T(8,128)S(1)}, u32[]{:S(2)}, u32[]{:S(2)}) collective-permute-start(f32[8,40,128]{2,1,0:T(8,128)S(1)} %get-tuple-element.52), channel_id=1, source_target_pairs={{0,4},{4,0},{8,12},{12,8},{16,20},{20,16},{24,28},{28,24},{32,36},... | collective-permute-start | bytes 491528 | tf_op jit(solution)/shard_map/ppermute | solution.py:734
  28.0 0.8 collective-permute-done.7.sib
  28.7 3.7 %collective-permute-done.6.far = f32[8,40,128]{2,1,0:T(8,128)S(1)} collective-permute-done((f32[8,40,128]{2,1,0:T(8,128)S(1)}, f32[8,40,128]{2,1,0:T(8,128)S(1)}, u32[]{:S(2)}, u32[]{:S(2)}) %collective-permute-start.6) | collective-permute-done | bytes 163872 | tf_op jit(solution)/shard_map/ppermute | solution.py:739
  32.9 2.7 %collective-permute-start.9 = (f32[56,128]{1,0:T(8,128)S(1)}, f32[56,128]{1,0:T(8,128)S(1)}, u32[]{:S(2)}, u32[]{:S(2)}) collective-permute-start(f32[56,128]{1,0:T(8,128)S(1)} %get-tuple-element.56), channel_id=1, source_target_pairs={{0,3},{1,0},{2,1},{3,2},{4,7},{5,4},{6,5},{7,6},{8,11},{9,8},{10,9... | collective-permute-start | bytes 86024 | tf_op jit(solution)/shard_map/ppermute | solution.py:730
  35.9 3.8 %collective-permute-done.10.far = f32[40,128]{1,0:T(8,128)S(1)} collective-permute-done((f32[40,128]{1,0:T(8,128)S(1)}, f32[40,128]{1,0:T(8,128)S(1)}, u32[]{:S(2)}, u32[]{:S(2)}) %collective-permute-start.10) | collective-permute-done | bytes 20512 | tf_op jit(solution)/shard_map/ppermute | solution.py:730
  39.9 5.2 %collective-permute-start.11 = (f32[240,128]{1,0:T(8,128)S(1)}, f32[240,128]{1,0:T(8,128)S(1)}, u32[]{:S(2)}, u32[]{:S(2)}) collective-permute-start(f32[240,128]{1,0:T(8,128)S(1)} %get-tuple-element.59.msg), channel_id=1, source_target_pairs={{0,4},{4,0},{8,12},{12,8},{16,20},{20,16},{24,28},{28,24},{32,36},... | collective-permute-start | bytes 368648 | tf_op jit(solution)/shard_map/ppermute | solution.py:734
  45.1 1.0 %collective-permute-done.11.sib = f32[240,128]{1,0:T(8,128)S(1)} collective-permute-done((f32[240,128]{1,0:T(8,128)S(1)}, f32[240,128]{1,0:T(8,128)S(1)}, u32[]{:S(2)}, u32[]{:S(2)}) %collective-permute-start.11) | collective-permute-done | bytes 122912 | tf_op jit(solution)/shard_map/ppermute | solution.py:734
  46.5 4.8 %collective-permute-done.12.near = f32[384,128]{1,0:T(8,128)S(1)} collective-permute-done((f32[384,128]{1,0:T(8,128)S(1)}, f32[384,128]{1,0:T(8,128)S(1)}, u32[]{:S(2)}, u32[]{:S(2)}) %collective-permute-start.12) | collective-permute-done | bytes 196640 | tf_op jit(solution)/shard_map/ppermute | solution.py:739
  51.3 3.7 %collective-permute-start.13 = (f32[384,128]{1,0:T(8,128)S(1)}, f32[384,128]{1,0:T(8,128)S(1)}, u32[]{:S(2)}, u32[]{:S(2)}) collective-permute-start(f32[384,128]{1,0:T(8,128)S(1)} %collective-permute-done.12.near), channel_id=1, source_target_pairs={{0,4},{4,0},{8,12},{12,8},{16,20},{20,16},{24,28},{28,24},{32,36},... | collective-permute-start | bytes 589832 | tf_op jit(solution)/shard_map/ppermute | solution.py:734
  55.0 1.1 %collective-permute-done.13.other = f32[384,128]{1,0:T(8,128)S(1)} collective-permute-done((f32[384,128]{1,0:T(8,128)S(1)}, f32[384,128]{1,0:T(8,128)S(1)}, u32[]{:S(2)}, u32[]{:S(2)}) %collective-permute-start.13) | collective-permute-done | bytes 196640 | tf_op jit(solution)/shard_map/ppermute | solution.py:734
  56.4 1.0 %shard_map.55 = f32[32,2,8,128]{3,2,1,0:T(8,128)} custom-call(f32[21,64,128]{2,1,0:T(8,128)S(1)} %get-tuple-element.61.w.win, f32[4,64,128]{2,1,0:T(8,128)S(1)} %get-tuple-element.62.u2, f32[3,8,128]{2,1,0:T(8,128)S(1)} %shard_map.53.tiles), custom_call_target="tpu_custom_call" | custom-call | tf_op jit(solution)/shard_map/pallas_call | solution.py:136
  57.4 3.9 %all-to-all-start = ((f32[32,2,8,128]{3,2,1,0:T(8,128)}), f32[32,2,8,128]{3,2,1,0:T(8,128)S(1)}, u32[]{:S(2)}, u32[]{:S(2)}) async-start(f32[32,2,8,128]{3,2,1,0:T(8,128)} %shard_map.55), calls=%async_computation | async-start | bytes 524288 | tf_op jit(solution)/shard_map/all_to_all | solution.py:793
  61.3 1.7 %collective-permute-start.14 = (f32[32,128]{1,0:T(8,128)S(1)}, f32[32,128]{1,0:T(8,128)S(1)}, u32[]{:S(2)}, u32[]{:S(2)}) collective-permute-start(f32[32,128]{1,0:T(8,128)S(1)} %get-tuple-element.64), channel_id=1, source_target_pairs={{0,252},{4,8},{8,4},{12,16},{16,12},{20,24},{24,20},{28,32},{32,28... | collective-permute-start | bytes 49160 | tf_op jit(solution)/shard_map/ppermute | solution.py:739
  63.0 6.5 %collective-permute-done.14.late = f32[32,128]{1,0:T(8,128)S(1)} collective-permute-done((f32[32,128]{1,0:T(8,128)S(1)}, f32[32,128]{1,0:T(8,128)S(1)}, u32[]{:S(2)}, u32[]{:S(2)}) %collective-permute-start.14) | collective-permute-done | bytes 16416 | tf_op jit(solution)/shard_map/ppermute | solution.py:739
  69.5 2.0 %all-to-all-done.mine = f32[32,2,8,128]{3,2,1,0:T(8,128)S(1)} async-done(((f32[32,2,8,128]{3,2,1,0:T(8,128)}), f32[32,2,8,128]{3,2,1,0:T(8,128)S(1)}, u32[]{:S(2)}, u32[]{:S(2)}) %all-to-all-start) | async-done | bytes 262176 | tf_op jit(solution)/shard_map/all_to_all | solution.py:793
  71.5 3.2 %collective-permute-start.15 = (f32[32,2,8,128]{3,2,1,0:T(8,128)S(1)}, f32[32,2,8,128]{3,2,1,0:T(8,128)S(1)}, u32[]{:S(2)}, u32[]{:S(2)}) collective-permute-start(f32[32,2,8,128]{3,2,1,0:T(8,128)S(1)} %all-to-all-done.mine), channel_id=1, source_target_pairs={{0,4},{4,0},{8,12},{12,8},{16,20},{20,16},{24,28},{28,24},{32,36},... | collective-permute-start | bytes 786440 | tf_op jit(solution)/shard_map/ppermute | solution.py:734
  74.8 1.1 %collective-permute-done.15.theirs = f32[32,2,8,128]{3,2,1,0:T(8,128)S(1)} collective-permute-done((f32[32,2,8,128]{3,2,1,0:T(8,128)S(1)}, f32[32,2,8,128]{3,2,1,0:T(8,128)S(1)}, u32[]{:S(2)}, u32[]{:S(2)}) %collective-permute-start.15) | collective-permute-done | bytes 262176 | tf_op jit(solution)/shard_map/ppermute | solution.py:734
  75.9 2.0 %shard_map.56.e2 = f32[192,128]{1,0:T(8,128)S(1)} custom-call(f32[32,2,8,128]{3,2,1,0:T(8,128)S(1)} %all-to-all-done.mine, f32[32,2,8,128]{3,2,1,0:T(8,128)S(1)} %collective-permute-done.15.theirs), custom_call_target="tpu_custom_call" | custom-call | tf_op jit(solution)/shard_map/pallas_call | solution.py:136
  78.2 1.9 %collective-permute-start.17 = (f32[2,64,128]{2,1,0:T(8,128)S(1)}, f32[2,64,128]{2,1,0:T(8,128)S(1)}, u32[]{:S(2)}, u32[]{:S(2)}) collective-permute-start(f32[2,64,128]{2,1,0:T(8,128)S(1)} %shard_map.57.e2), channel_id=1, source_target_pairs={{0,252},{4,8},{8,4},{12,16},{16,12},{20,24},{24,20},{28,32},{32,28... | collective-permute-start | bytes 196616 | tf_op jit(solution)/shard_map/ppermute | solution.py:739
  80.1 2.0 %collective-permute-done.17.far = f32[2,64,128]{2,1,0:T(8,128)S(1)} collective-permute-done((f32[2,64,128]{2,1,0:T(8,128)S(1)}, f32[2,64,128]{2,1,0:T(8,128)S(1)}, u32[]{:S(2)}, u32[]{:S(2)}) %collective-permute-start.17) | collective-permute-done | bytes 65568 | tf_op jit(solution)/shard_map/ppermute | solution.py:739
  82.8 3.7 %collective-permute-start.18 = (f32[40,128]{1,0:T(8,128)S(1)}, f32[40,128]{1,0:T(8,128)S(1)}, u32[]{:S(2)}, u32[]{:S(2)}) collective-permute-start(f32[40,128]{1,0:T(8,128)S(1)} %get-tuple-element.73), channel_id=1, source_target_pairs={{0,4},{4,0},{8,12},{12,8},{16,20},{20,16},{24,28},{28,24},{32,36},... | collective-permute-start | bytes 61448 | tf_op jit(solution)/shard_map/ppermute | solution.py:734
  86.5 0.7 collective-permute-done.18.other
  87.3 2.4 %shard_map.59 = f32[4,64,256]{2,1,0:T(8,128)} custom-call(f32[2,40,128]{2,1,0:T(8,128)S(1)} %get-tuple-element.71.e1, f32[40,128]{1,0:T(8,128)S(1)} %get-tuple-element.72.edge, f32[40,128]{1,0:T(8,128)S(1)} %collective-permute-done.18.other, f32[2,80,256]{2,1,0:T(8,128)S(1)} %get-tuple-element.74.outer, f32[16,64,256]{2,1,0:T(8,128)S(1)} %pad_maximum_fusion.1.inner, ...), custom_call_target="tpu_custom_call" | custom-call | tf_op jit(solution)/shard_map/pallas_call | solution.py:136
  (32 shorter events, 3.7 us)
Async XLA Ops:
  2.2 13.2 %collective-permute-start = (f32[16,8,256]{2,1,0:T(8,128)}, f32[16,8,256]{2,1,0:T(8,128)S(1)}, u32[]{:S(2)}, u32[]{:S(2)}) collective-permute-start(f32[16,8,256]{2,1,0:T(8,128)} %get-tuple-element.43), channel_id=1, source_target_pairs={{0,1},{1,2},{2,3},{3,0},{4,5},{5,6},{6,7},{7,4},{8,9},{9,10},{10,1... | collective-permute-start | bytes 393224 | tf_op jit(solution)/shard_map/ppermute | solution.py:730
  4.4 11.0 %collective-permute-start.1 = (f32[16,8,256]{2,1,0:T(8,128)}, f32[16,8,256]{2,1,0:T(8,128)S(1)}, u32[]{:S(2)}, u32[]{:S(2)}) collective-permute-start(f32[16,8,256]{2,1,0:T(8,128)} %get-tuple-element.44), channel_id=1, source_target_pairs={{0,3},{1,0},{2,1},{3,2},{4,7},{5,4},{6,5},{7,6},{8,11},{9,8},{10,9... | collective-permute-start | bytes 393224 | tf_op jit(solution)/shard_map/ppermute | solution.py:730
  5.9 11.8 %collective-permute-start.2 = (f32[5,64,256]{2,1,0:T(8,128)}, f32[5,64,256]{2,1,0:T(8,128)S(1)}, u32[]{:S(2)}, u32[]{:S(2)}) collective-permute-start(f32[5,64,256]{2,1,0:T(8,128)} %get-tuple-element.47), channel_id=1, source_target_pairs={{0,252},{4,8},{8,4},{12,16},{16,12},{20,24},{24,20},{28,32},{32,28... | collective-permute-start | bytes 983048 | tf_op jit(solution)/shard_map/ppermute | solution.py:739
  8.5 9.2 %collective-permute-start.3 = (f32[5,64,256]{2,1,0:T(8,128)}, f32[5,64,256]{2,1,0:T(8,128)S(1)}, u32[]{:S(2)}, u32[]{:S(2)}) collective-permute-start(f32[5,64,256]{2,1,0:T(8,128)} %get-tuple-element.48), channel_id=1, source_target_pairs={{0,4},{4,0},{8,12},{12,8},{16,20},{20,16},{24,28},{28,24},{32,36},... | collective-permute-start | bytes 983048 | tf_op jit(solution)/shard_map/ppermute | solution.py:734
  15.8 6.4 %collective-permute-start.4 = (f32[280,256]{1,0:T(8,128)S(1)}, f32[280,256]{1,0:T(8,128)S(1)}, u32[]{:S(2)}, u32[]{:S(2)}) collective-permute-start(f32[280,256]{1,0:T(8,128)S(1)} %get-tuple-element.49), channel_id=1, source_target_pairs={{0,252},{4,8},{8,4},{12,16},{16,12},{20,24},{24,20},{28,32},{32,28... | collective-permute-start | bytes 860168 | tf_op jit(solution)/shard_map/ppermute | solution.py:739
  15.9 6.3 %collective-permute-start.5 = (f32[280,256]{1,0:T(8,128)S(1)}, f32[280,256]{1,0:T(8,128)S(1)}, u32[]{:S(2)}, u32[]{:S(2)}) collective-permute-start(f32[280,256]{1,0:T(8,128)S(1)} %get-tuple-element.50), channel_id=1, source_target_pairs={{0,4},{4,0},{8,12},{12,8},{16,20},{20,16},{24,28},{28,24},{32,36},... | collective-permute-start | bytes 860168 | tf_op jit(solution)/shard_map/ppermute | solution.py:734
  24.6 4.1 %collective-permute-start.7 = (f32[8,40,128]{2,1,0:T(8,128)S(1)}, f32[8,40,128]{2,1,0:T(8,128)S(1)}, u32[]{:S(2)}, u32[]{:S(2)}) collective-permute-start(f32[8,40,128]{2,1,0:T(8,128)S(1)} %get-tuple-element.52), channel_id=1, source_target_pairs={{0,4},{4,0},{8,12},{12,8},{16,20},{20,16},{24,28},{28,24},{32,36},... | collective-permute-start | bytes 491528 | tf_op jit(solution)/shard_map/ppermute | solution.py:734
  27.7 4.7 %collective-permute-start.6 = (f32[8,40,128]{2,1,0:T(8,128)S(1)}, f32[8,40,128]{2,1,0:T(8,128)S(1)}, u32[]{:S(2)}, u32[]{:S(2)}) collective-permute-start(f32[8,40,128]{2,1,0:T(8,128)S(1)} %get-tuple-element.51.own), channel_id=1, source_target_pairs={{0,252},{4,8},{8,4},{12,16},{16,12},{20,24},{24,20},{28,32},{32,28... | collective-permute-start | bytes 491528 | tf_op jit(solution)/shard_map/ppermute | solution.py:739
  32.8 6.9 %collective-permute-start.8 = (f32[56,128]{1,0:T(8,128)S(1)}, f32[56,128]{1,0:T(8,128)S(1)}, u32[]{:S(2)}, u32[]{:S(2)}) collective-permute-start(f32[56,128]{1,0:T(8,128)S(1)} %get-tuple-element.55), channel_id=1, source_target_pairs={{0,1},{1,2},{2,3},{3,0},{4,5},{5,6},{6,7},{7,4},{8,9},{9,10},{10,1... | collective-permute-start | bytes 86024 | tf_op jit(solution)/shard_map/ppermute | solution.py:730
  32.9 6.8 %collective-permute-start.9 = (f32[56,128]{1,0:T(8,128)S(1)}, f32[56,128]{1,0:T(8,128)S(1)}, u32[]{:S(2)}, u32[]{:S(2)}) collective-permute-start(f32[56,128]{1,0:T(8,128)S(1)} %get-tuple-element.56), channel_id=1, source_target_pairs={{0,3},{1,0},{2,1},{3,2},{4,7},{5,4},{6,5},{7,6},{8,11},{9,8},{10,9... | collective-permute-start | bytes 86024 | tf_op jit(solution)/shard_map/ppermute | solution.py:730
  35.6 4.1 %collective-permute-start.10 = (f32[40,128]{1,0:T(8,128)S(1)}, f32[40,128]{1,0:T(8,128)S(1)}, u32[]{:S(2)}, u32[]{:S(2)}) collective-permute-start(f32[40,128]{1,0:T(8,128)S(1)} %get-tuple-element.54.f2), channel_id=1, source_target_pairs={{0,2},{1,3},{2,0},{3,1},{4,6},{5,7},{6,4},{7,5},{8,10},{9,11},{10,... | collective-permute-start | bytes 61448 | tf_op jit(solution)/shard_map/ppermute | solution.py:730
  39.9 6.2 %collective-permute-start.11 = (f32[240,128]{1,0:T(8,128)S(1)}, f32[240,128]{1,0:T(8,128)S(1)}, u32[]{:S(2)}, u32[]{:S(2)}) collective-permute-start(f32[240,128]{1,0:T(8,128)S(1)} %get-tuple-element.59.msg), channel_id=1, source_target_pairs={{0,4},{4,0},{8,12},{12,8},{16,20},{20,16},{24,28},{28,24},{32,36},... | collective-permute-start | bytes 368648 | tf_op jit(solution)/shard_map/ppermute | solution.py:734
  46.1 5.2 %collective-permute-start.12 = (f32[384,128]{1,0:T(8,128)S(1)}, f32[384,128]{1,0:T(8,128)S(1)}, u32[]{:S(2)}, u32[]{:S(2)}) collective-permute-start(f32[384,128]{1,0:T(8,128)S(1)} %shard_map.52), channel_id=1, source_target_pairs={{0,252},{4,8},{8,4},{12,16},{16,12},{20,24},{24,20},{28,32},{32,28... | collective-permute-start | bytes 589832 | tf_op jit(solution)/shard_map/ppermute | solution.py:739
  51.3 4.8 %collective-permute-start.13 = (f32[384,128]{1,0:T(8,128)S(1)}, f32[384,128]{1,0:T(8,128)S(1)}, u32[]{:S(2)}, u32[]{:S(2)}) collective-permute-start(f32[384,128]{1,0:T(8,128)S(1)} %collective-permute-done.12.near), channel_id=1, source_target_pairs={{0,4},{4,0},{8,12},{12,8},{16,20},{20,16},{24,28},{28,24},{32,36},... | collective-permute-start | bytes 589832 | tf_op jit(solution)/shard_map/ppermute | solution.py:734
  57.4 14.1 %all-to-all-start = ((f32[32,2,8,128]{3,2,1,0:T(8,128)}), f32[32,2,8,128]{3,2,1,0:T(8,128)S(1)}, u32[]{:S(2)}, u32[]{:S(2)}) async-start(f32[32,2,8,128]{3,2,1,0:T(8,128)} %shard_map.55), calls=%async_computation | async-start | bytes 524288 | tf_op jit(solution)/shard_map/all_to_all | solution.py:793
  61.3 8.2 %collective-permute-start.14 = (f32[32,128]{1,0:T(8,128)S(1)}, f32[32,128]{1,0:T(8,128)S(1)}, u32[]{:S(2)}, u32[]{:S(2)}) collective-permute-start(f32[32,128]{1,0:T(8,128)S(1)} %get-tuple-element.64), channel_id=1, source_target_pairs={{0,252},{4,8},{8,4},{12,16},{16,12},{20,24},{24,20},{28,32},{32,28... | collective-permute-start | bytes 49160 | tf_op jit(solution)/shard_map/ppermute | solution.py:739
  71.5 14.9 %copy-start = (f32[4,64,256]{2,1,0:T(8,128)S(1)}, f32[4,64,256]{2,1,0:T(8,128)}, u32[]{:S(2)}) copy-start(f32[4,64,256]{2,1,0:T(8,128)} %c3.1) | copy-start | bytes 786436
  71.5 14.9 %copy-start.1 = (f32[4,64,256]{2,1,0:T(8,128)S(1)}, f32[4,64,256]{2,1,0:T(8,128)}, u32[]{:S(2)}) copy-start(f32[4,64,256]{2,1,0:T(8,128)} %c2.1) | copy-start | bytes 786436
  71.5 14.9 %copy-start.2 = (f32[4,64,256]{2,1,0:T(8,128)S(1)}, f32[4,64,256]{2,1,0:T(8,128)}, u32[]{:S(2)}) copy-start(f32[4,64,256]{2,1,0:T(8,128)} %c1.1) | copy-start | bytes 786436
  71.5 14.9 %copy-start.3 = (f32[4,64,256]{2,1,0:T(8,128)S(1)}, f32[4,64,256]{2,1,0:T(8,128)}, u32[]{:S(2)}) copy-start(f32[4,64,256]{2,1,0:T(8,128)} %f.1) | copy-start | bytes 786436
  71.5 4.4 %collective-permute-start.15 = (f32[32,2,8,128]{3,2,1,0:T(8,128)S(1)}, f32[32,2,8,128]{3,2,1,0:T(8,128)S(1)}, u32[]{:S(2)}, u32[]{:S(2)}) collective-permute-start(f32[32,2,8,128]{3,2,1,0:T(8,128)S(1)} %all-to-all-done.mine), channel_id=1, source_target_pairs={{0,4},{4,0},{8,12},{12,8},{16,20},{20,16},{24,28},{28,24},{32,36},... | collective-permute-start | bytes 786440 | tf_op jit(solution)/shard_map/ppermute | solution.py:734
  74.7 3.2 %collective-permute-start.16 = (f32[32,128]{1,0:T(8,128)S(1)}, f32[32,128]{1,0:T(8,128)S(1)}, u32[]{:S(2)}, u32[]{:S(2)}) collective-permute-start(f32[32,128]{1,0:T(8,128)S(1)} %collective-permute-done.14.late), channel_id=1, source_target_pairs={{0,4},{4,0},{8,12},{12,8},{16,20},{20,16},{24,28},{28,24},{32,36},... | collective-permute-start | bytes 49160 | tf_op jit(solution)/shard_map/ppermute | solution.py:734
  78.2 3.9 %collective-permute-start.17 = (f32[2,64,128]{2,1,0:T(8,128)S(1)}, f32[2,64,128]{2,1,0:T(8,128)S(1)}, u32[]{:S(2)}, u32[]{:S(2)}) collective-permute-start(f32[2,64,128]{2,1,0:T(8,128)S(1)} %shard_map.57.e2), channel_id=1, source_target_pairs={{0,252},{4,8},{8,4},{12,16},{16,12},{20,24},{24,20},{28,32},{32,28... | collective-permute-start | bytes 196616 | tf_op jit(solution)/shard_map/ppermute | solution.py:739
  82.8 4.5 %collective-permute-start.18 = (f32[40,128]{1,0:T(8,128)S(1)}, f32[40,128]{1,0:T(8,128)S(1)}, u32[]{:S(2)}, u32[]{:S(2)}) collective-permute-start(f32[40,128]{1,0:T(8,128)S(1)} %get-tuple-element.73), channel_id=1, source_target_pairs={{0,4},{4,0},{8,12},{12,8},{16,20},{20,16},{24,28},{28,24},{32,36},... | collective-permute-start | bytes 61448 | tf_op jit(solution)/shard_map/ppermute | solution.py:734

commit v14 on v13

--- a/solution.py
+++ b/solution.py
@@ -414,22 +414,19 @@
     return packed
 
 
-def coarse_swap_kernel(own, msg, sib, w1, out):
+def coarse_swap_kernel(own, msg, sib, out):
     out[0:160] = msg[0:160]
     out[160:192] = sib[0:32] * sib[32:64] * (1.0 / THETA)
     out[192:224] = two_blocks(own[2])
-    out[224:304] = msg[160:240]
-    par = lax.rem(lax.axis_index("wide"), 2)
-    out[304:344] = sib[pl.ds(pl.multiple_of(160 + 40 * par, 8), 40), :]
-    out[344:384] = w1[4]
-
-
-def coarse_pre_kernel(own, msg, sib, near, other, w, u2, late, fine, u1):
+
+
+def coarse_pre_kernel(own, msg, sib, near, other, w1, w, u2, late, fine, u1):
     for p in range(2):
         fine[p] = sib[160 + 40 * p : 200 + 40 * p]
         fine[2 + p] = msg[160 + 40 * p : 200 + 40 * p]
-    for p in range(4):
-        fine[4 + p] = near[224 + 40 * p : 264 + 40 * p]
+    late[32:112] = msg[160:240]
+    late[112:152] = fine[lax.rem(lax.axis_index("wide"), 2)]
+    late[152:192] = w1[4]
     odd = lax.rem(lax.axis_index("wide"), 2) == 1
 
     def below(k):
@@ -453,7 +450,7 @@
         u1[k + 1] = w[k] * w[4 + k] * (1.0 / THETA)
     for k in range(4):
         u2[k] = smooth_two(u1[k + 1], u1[k], u1[k + 2], w[k], w[4 + k], w[8 + k], w[9 + k], w[13 + k], w[17 + k])
-    late[...] = two_blocks(jnp.where(odd, u2[1], u2[2]))
+    late[0:32] = two_blocks(jnp.where(odd, u2[1], u2[2]))
 
 
 def coarse_send_kernel(w, u2, tiles, send, scr):
@@ -638,7 +635,8 @@
 
 def coarse_post_kernel(e2, win, u2, late, late_sib, out):
     below, above = sides(late, late_sib)
-    v = [both_halves(below(...)), u2[0], u2[1], u2[2], u2[3], both_halves(above(...))]
+    half = slice(0, 32)
+    v = [both_halves(below(half)), u2[0], u2[1], u2[2], u2[3], both_halves(above(half))]
     v = [v[m] + e2[64 * (m // 2) : 64 * (m // 2) + 64, :] for m in range(6)]
 
     def args(k):
@@ -646,21 +644,23 @@
 
     w = [first_post(v[m + 1], v[m], v[m + 2], *args(m)) for m in range(4)]
     for p in range(2):
-        out[p] = second_post(w[p + 1], v[p + 2], w[p], w[p + 2], *args(p + 1))
-
-
-def middle_post_kernel(e2, far, u2, f, g, w1, own, edge, send, fine, c1, v, w):
-    n, par = lax.axis_index("narrow"), lax.rem(lax.axis_index("wide"), 2)
+        x = second_post(w[p + 1], v[p + 2], w[p], w[p + 2], *args(p + 1))
+        out[p] = pltpu.roll(x, lax.rem(72 - 16 * lax.axis_index("narrow"), 64), 0)[0:32]
+
+
+def middle_post_kernel(e2, far, u2, late, f, g, w1, own, edge, send, fine, c1, v, w):
+    par = lax.rem(lax.axis_index("wide"), 2)
     odd = par == 1
-    row, col = iota((40, 64), 0), iota((40, 64), 1)
-    pick = (col == lax.rem(16 * n + (row + 4) // 2 + 60, 64)).astype(F32)
+    row, col = iota((40, 32), 0), iota((40, 32), 1)
+    pick = (col == (row + 4) // 2 + 4).astype(F32)
     lanes = copies_of_lanes(128, 128)
     planes = (e2[0], e2[1], far[0], far[1])
     for k in range(4):
         fine[k] = mul(mul_left(pick, jnp.where(odd, planes[k], planes[(k + 2) % 4])), lanes)
     c1[0:6] = w1[0:6]
-    c1[6] = u2[7]
-    sibs, ours, next_chip = ([u2[k] for k in some] for some in ((0, 1), (2, 3), (4, 5, 6)))
+    c1[6] = late[152:192]
+    sibs, ours = [u2[0], u2[1]], [u2[2], u2[3]]
+    next_chip = [late[32 + 40 * p : 72 + 40 * p] for p in range(3)]
     upper = sibs + ours + next_chip
     lower = [next_chip[2]] + next_chip[:2] + ours + sibs
     for i in range(7):
@@ -779,14 +779,14 @@
 
     own2, msg = call(coarse_start_kernel, [(6, 64, 128), (240, 128)])(f2, low, high, far, u2m)
     sib = sibling(msg)
-    (swap,) = call(coarse_swap_kernel, [(384, 128)])(own2, msg, sib, w1)
+    (swap,) = call(coarse_swap_kernel, [(224, 128)])(own2, msg, sib)
     near = across(swap)
     (tiles,) = call(coarse_tiles_kernel, [(3, 8, 128)], [(64, 128)])(msg, sib)
     near, tiles = lax.optimization_barrier((near, tiles))
     other = sibling(near)
     w2, u2w, late, fine1 = call(
-        coarse_pre_kernel, [(21, 64, 128), (4, 64, 128), (32, 128), (8, 40, 128)], [(6, 64, 128)]
-    )(own2, msg, sib, near, other)
+        coarse_pre_kernel, [(21, 64, 128), (4, 64, 128), (192, 128), (4, 40, 128)], [(6, 64, 128)]
+    )(own2, msg, sib, near, other, w1)
     (send,) = call(coarse_send_kernel, [(n3, 2, 8, 128)], [(64, 128)])(w2, u2w, tiles)
     late = across(late)
     cores = [[k for k in range(wide) if k % 2 == c] for c in range(2)]
@@ -801,7 +801,7 @@
         [three, (n3 + 1, 8, 128), three, three, three, three, (n3 + 2, 8, 128), (n3 + 2, 8, 128), four, four]
         + [(n4 + 1, 8, 128), four, four, four, (n4 + 2, 8, 128), (n4 + 2, 8, 128), four, (32, 128)],
     )(parts, theirs)
-    (e2,) = call(coarse_post_kernel, [(2, 64, 128)])(fine2, w2, u2w, late, late_sib)
+    (e2,) = call(coarse_post_kernel, [(2, 32, 128)])(fine2, w2, u2w, late, late_sib)
     e2, *again = lax.optimization_barrier((e2,) + inputs)
     far = across(e2)
 
@@ -809,7 +809,7 @@
         middle_post_kernel,
         [(2, 40, 128), (40, 128), (40, 128)],
         [(4, 40, 128), (7, 40, 128), (7, 40, 128), (7, 40, 128)],
-    )(e2, far, fine1, f1w, g1w, w1)
+    )(e2, far, fine1, late, f1w, g1w, w1)
     other1 = sibling(send)
 
     (out,) = call(

time: 90 us -> 90.4 us (level)
    ppermute x8, starting transfers between devices: 26.3 us -> 27.4 us  [sibling(): lax.ppermute(x, 'wide', [(i, i ^ 1) for i in range(lax.axis_size('wide'))])]
    ppermute x6, starting transfers between devices: 6.47 us -> 5.46 us  [across(): lax.ppermute(x, 'wide', [(i, (i + 1 if i % 2 else i - 1) % count) for i i...]
  transfers between devices with their start and end apart: 20 -> 20, of which waited for: 12 -> 12; matrix products, arithmetic and copies ran while one was open for 2% -> 1% of each run, Pallas kernels for 3% -> 3%
where the time goes in v14:
time: 90.4 us; the launch traced here: 90.1 us
  starting transfers between devices  43.6 us (48%)
  waiting for transfers between devices  31.5 us (35%)
  Pallas kernels  12.9 us (14%)
  other arithmetic  1.35 us (1%)
    ppermute x8, starting transfers between devices, sibling(): lax.ppermute(x, 'wide', [(i, i ^ 1) for i in range(lax.axis_size('wide'))])  27.4 us
    ppermute x6, waiting for transfers between devices, across(): lax.ppermute(x, 'wide', [(i, (i + 1 if i % 2 else i - 1) % count) for i i...  22.1 us
    pallas_call x14, Pallas kernels, run(): pl.pallas_call(kernel, out_shape=[jax.ShapeDtypeStruct(s, F32) for s in o...  12.9 us
    ppermute x5, starting transfers between devices, shift(): return lax.ppermute(x, axis, [(i, (i + by) % count) for i in range(count)])  6.82 us
    ppermute x6, starting transfers between devices, across(): lax.ppermute(x, 'wide', [(i, (i + 1 if i % 2 else i - 1) % count) for i i...  5.46 us
    ppermute x8, waiting for transfers between devices, sibling(): lax.ppermute(x, 'wide', [(i, i ^ 1) for i in range(lax.axis_size('wide'))])  4.52 us
    all_to_all x1, starting transfers between devices, body(): lax.all_to_all(send, 'wide', split_axis=0, concat_axis=0, tiled=True, axi...  3.87 us
    ppermute x5, waiting for transfers between devices, shift(): return lax.ppermute(x, axis, [(i, (i + by) % count) for i in range(count)])  3.8 us
  transfers between devices with their start and end apart: 20, of which 12 were waited for; matrix products, arithmetic and copies ran while one was open for 1% of the time, Pallas kernels for 3%

profile of v14, /device:TPU:1, one launch (start us, length us, event | category | flops | bytes accessed | tf_op | source)
XLA Modules:
  0.0 90.1 jit_solution(4108484133131433595)
XLA Ops:
  0.0 2.2 %shard_map.46 = (f32[16,8,256]{2,1,0:T(8,128)}, f32[16,8,256]{2,1,0:T(8,128)}, f32[5,64,256]{2,1,0:T(8,128)}, f32[5,64,256]{2,1,0:T(8,128)}) custom-call(f32[4,64,256]{2,1,0:T(8,128)} %f.1, f32[4,64,256]{2,1,0:T(8,128)} %c1.1, f32[4,64,256]{2,1,0:T(8,128)} %c2.1, f32[4,64,256]{2,1,0:T(8,128)} %c3.1), custom_call_target="tpu_custom_call" | custom-call | tf_op jit(solution)/shard_map/pallas_call | solution.py:136
  2.2 2.2 %collective-permute-start = (f32[16,8,256]{2,1,0:T(8,128)}, f32[16,8,256]{2,1,0:T(8,128)S(1)}, u32[]{:S(2)}, u32[]{:S(2)}) collective-permute-start(f32[16,8,256]{2,1,0:T(8,128)} %get-tuple-element.43), channel_id=1, source_target_pairs={{0,1},{1,2},{2,3},{3,0},{4,5},{5,6},{6,7},{7,4},{8,9},{9,10},{10,1... | collective-permute-start | bytes 393224 | tf_op jit(solution)/shard_map/ppermute | solution.py:730
  4.4 1.5 %collective-permute-start.1 = (f32[16,8,256]{2,1,0:T(8,128)}, f32[16,8,256]{2,1,0:T(8,128)S(1)}, u32[]{:S(2)}, u32[]{:S(2)}) collective-permute-start(f32[16,8,256]{2,1,0:T(8,128)} %get-tuple-element.44), channel_id=1, source_target_pairs={{0,3},{1,0},{2,1},{3,2},{4,7},{5,4},{6,5},{7,6},{8,11},{9,8},{10,9... | collective-permute-start | bytes 393224 | tf_op jit(solution)/shard_map/ppermute | solution.py:730
  5.9 2.6 %collective-permute-start.2 = (f32[5,64,256]{2,1,0:T(8,128)}, f32[5,64,256]{2,1,0:T(8,128)S(1)}, u32[]{:S(2)}, u32[]{:S(2)}) collective-permute-start(f32[5,64,256]{2,1,0:T(8,128)} %get-tuple-element.47), channel_id=1, source_target_pairs={{0,252},{4,8},{8,4},{12,16},{16,12},{20,24},{24,20},{28,32},{32,28... | collective-permute-start | bytes 983048 | tf_op jit(solution)/shard_map/ppermute | solution.py:739
  8.5 5.6 %collective-permute-start.3 = (f32[5,64,256]{2,1,0:T(8,128)}, f32[5,64,256]{2,1,0:T(8,128)S(1)}, u32[]{:S(2)}, u32[]{:S(2)}) collective-permute-start(f32[5,64,256]{2,1,0:T(8,128)} %get-tuple-element.48), channel_id=1, source_target_pairs={{0,4},{4,0},{8,12},{12,8},{16,20},{20,16},{24,28},{28,24},{32,36},... | collective-permute-start | bytes 983048 | tf_op jit(solution)/shard_map/ppermute | solution.py:734
  14.1 1.3 %pad_maximum_fusion.inner = f32[16,64,256]{2,1,0:T(8,128)S(1)} fusion(f32[4,64,256]{2,1,0:T(8,128)} %c3.1, f32[4,64,256]{2,1,0:T(8,128)} %c2.1, f32[4,64,256]{2,1,0:T(8,128)} %c1.1, f32[4,64,256]{2,1,0:T(8,128)} %f.1), kind=kLoop, calls=%fused_computation | loop fusion | flops 786432 | bytes 2097152 | tf_op jit(solution)/shard_map/concatenate | solution.py:761
  15.9 1.8 %collective-permute-start.5 = (f32[280,256]{1,0:T(8,128)S(1)}, f32[280,256]{1,0:T(8,128)S(1)}, u32[]{:S(2)}, u32[]{:S(2)}) collective-permute-start(f32[280,256]{1,0:T(8,128)S(1)} %get-tuple-element.50), channel_id=1, source_target_pairs={{0,4},{4,0},{8,12},{12,8},{16,20},{20,16},{24,28},{28,24},{32,36},... | collective-permute-start | bytes 860168 | tf_op jit(solution)/shard_map/ppermute | solution.py:734
  17.7 4.5 %collective-permute-done.4.far = f32[280,256]{1,0:T(8,128)S(1)} collective-permute-done((f32[280,256]{1,0:T(8,128)S(1)}, f32[280,256]{1,0:T(8,128)S(1)}, u32[]{:S(2)}, u32[]{:S(2)}) %collective-permute-start.4) | collective-permute-done | bytes 286752 | tf_op jit(solution)/shard_map/ppermute | solution.py:739
  22.3 2.4 %shard_map.48 = (f32[9,80,256]{2,1,0:T(8,128)S(1)}, f32[6,80,256]{2,1,0:T(8,128)S(1)}, f32[18,40,128]{2,1,0:T(8,128)S(1)}, f32[8,40,128]{2,1,0:T(8,128)S(1)}, f32[8,40,128]{2,1,0:T(8,128)S(1)}) custom-call(f32[16,80,256]{2,1,0:T(8,128)S(1)} %get-tuple-element.45.own, f32[6,40,128]{2,1,0:T(8,128)S(1)} %get-tuple-element.46.coef1, ...), custom_call_target="tpu_custom_call" | custom-call | tf_op jit(solution)/shard_map/pallas_call | solution.py:136
  24.7 3.1 %collective-permute-start.7 = (f32[8,40,128]{2,1,0:T(8,128)S(1)}, f32[8,40,128]{2,1,0:T(8,128)S(1)}, u32[]{:S(2)}, u32[]{:S(2)}) collective-permute-start(f32[8,40,128]{2,1,0:T(8,128)S(1)} %get-tuple-element.52), channel_id=1, source_target_pairs={{0,4},{4,0},{8,12},{12,8},{16,20},{20,16},{24,28},{28,24},{32,36},... | collective-permute-start | bytes 491528 | tf_op jit(solution)/shard_map/ppermute | solution.py:734
  28.1 0.8 collective-permute-done.7.sib
  28.8 3.7 %collective-permute-done.6.far = f32[8,40,128]{2,1,0:T(8,128)S(1)} collective-permute-done((f32[8,40,128]{2,1,0:T(8,128)S(1)}, f32[8,40,128]{2,1,0:T(8,128)S(1)}, u32[]{:S(2)}, u32[]{:S(2)}) %collective-permute-start.6) | collective-permute-done | bytes 163872 | tf_op jit(solution)/shard_map/ppermute | solution.py:739
  33.0 2.7 %collective-permute-start.9 = (f32[56,128]{1,0:T(8,128)S(1)}, f32[56,128]{1,0:T(8,128)S(1)}, u32[]{:S(2)}, u32[]{:S(2)}) collective-permute-start(f32[56,128]{1,0:T(8,128)S(1)} %get-tuple-element.56), channel_id=1, source_target_pairs={{0,3},{1,0},{2,1},{3,2},{4,7},{5,4},{6,5},{7,6},{8,11},{9,8},{10,9... | collective-permute-start | bytes 86024 | tf_op jit(solution)/shard_map/ppermute | solution.py:730
  36.0 3.8 %collective-permute-done.10.far = f32[40,128]{1,0:T(8,128)S(1)} collective-permute-done((f32[40,128]{1,0:T(8,128)S(1)}, f32[40,128]{1,0:T(8,128)S(1)}, u32[]{:S(2)}, u32[]{:S(2)}) %collective-permute-start.10) | collective-permute-done | bytes 20512 | tf_op jit(solution)/shard_map/ppermute | solution.py:730
  40.0 5.2 %collective-permute-start.11 = (f32[240,128]{1,0:T(8,128)S(1)}, f32[240,128]{1,0:T(8,128)S(1)}, u32[]{:S(2)}, u32[]{:S(2)}) collective-permute-start(f32[240,128]{1,0:T(8,128)S(1)} %get-tuple-element.59.msg), channel_id=1, source_target_pairs={{0,4},{4,0},{8,12},{12,8},{16,20},{20,16},{24,28},{28,24},{32,36},... | collective-permute-start | bytes 368648 | tf_op jit(solution)/shard_map/ppermute | solution.py:734
  45.2 1.0 %collective-permute-done.11.sib = f32[240,128]{1,0:T(8,128)S(1)} collective-permute-done((f32[240,128]{1,0:T(8,128)S(1)}, f32[240,128]{1,0:T(8,128)S(1)}, u32[]{:S(2)}, u32[]{:S(2)}) %collective-permute-start.11) | collective-permute-done | bytes 122912 | tf_op jit(solution)/shard_map/ppermute | solution.py:734
  46.6 3.9 %collective-permute-done.12.near = f32[224,128]{1,0:T(8,128)S(1)} collective-permute-done((f32[224,128]{1,0:T(8,128)S(1)}, f32[224,128]{1,0:T(8,128)S(1)}, u32[]{:S(2)}, u32[]{:S(2)}) %collective-permute-start.12) | collective-permute-done | bytes 114720 | tf_op jit(solution)/shard_map/ppermute | solution.py:739
  50.5 3.7 %collective-permute-start.13 = (f32[224,128]{1,0:T(8,128)S(1)}, f32[224,128]{1,0:T(8,128)S(1)}, u32[]{:S(2)}, u32[]{:S(2)}) collective-permute-start(f32[224,128]{1,0:T(8,128)S(1)} %collective-permute-done.12.near), channel_id=1, source_target_pairs={{0,4},{4,0},{8,12},{12,8},{16,20},{20,16},{24,28},{28,24},{32,36},... | collective-permute-start | bytes 344072 | tf_op jit(solution)/shard_map/ppermute | solution.py:734
  54.2 1.0 %collective-permute-done.13.other = f32[224,128]{1,0:T(8,128)S(1)} collective-permute-done((f32[224,128]{1,0:T(8,128)S(1)}, f32[224,128]{1,0:T(8,128)S(1)}, u32[]{:S(2)}, u32[]{:S(2)}) %collective-permute-start.13) | collective-permute-done | bytes 114720 | tf_op jit(solution)/shard_map/ppermute | solution.py:734
  56.2 1.0 %shard_map.55 = f32[32,2,8,128]{3,2,1,0:T(8,128)} custom-call(f32[21,64,128]{2,1,0:T(8,128)S(1)} %get-tuple-element.61.w.win, f32[4,64,128]{2,1,0:T(8,128)S(1)} %get-tuple-element.62.u2, f32[3,8,128]{2,1,0:T(8,128)S(1)} %shard_map.53.tiles), custom_call_target="tpu_custom_call" | custom-call | tf_op jit(solution)/shard_map/pallas_call | solution.py:136
  57.1 3.9 %all-to-all-start = ((f32[32,2,8,128]{3,2,1,0:T(8,128)}), f32[32,2,8,128]{3,2,1,0:T(8,128)S(1)}, u32[]{:S(2)}, u32[]{:S(2)}) async-start(f32[32,2,8,128]{3,2,1,0:T(8,128)} %shard_map.55), calls=%async_computation | async-start | bytes 524288 | tf_op jit(solution)/shard_map/all_to_all | solution.py:793
  61.0 1.7 %collective-permute-start.14 = (f32[192,128]{1,0:T(8,128)}, f32[192,128]{1,0:T(8,128)S(1)}, u32[]{:S(2)}, u32[]{:S(2)}) collective-permute-start(f32[192,128]{1,0:T(8,128)} %copy-done), channel_id=1, source_target_pairs={{0,252},{4,8},{8,4},{12,16},{16,12},{20,24},{24,20},{28,32},{32,28... | collective-permute-start | bytes 294920 | tf_op jit(solution)/shard_map/ppermute | solution.py:739
  62.7 7.4 %collective-permute-done.14.late = f32[192,128]{1,0:T(8,128)S(1)} collective-permute-done((f32[192,128]{1,0:T(8,128)}, f32[192,128]{1,0:T(8,128)S(1)}, u32[]{:S(2)}, u32[]{:S(2)}) %collective-permute-start.14) | collective-permute-done | bytes 98336 | tf_op jit(solution)/shard_map/ppermute | solution.py:739
  70.1 1.1 %all-to-all-done.mine = f32[32,2,8,128]{3,2,1,0:T(8,128)S(1)} async-done(((f32[32,2,8,128]{3,2,1,0:T(8,128)}), f32[32,2,8,128]{3,2,1,0:T(8,128)S(1)}, u32[]{:S(2)}, u32[]{:S(2)}) %all-to-all-start) | async-done | bytes 262176 | tf_op jit(solution)/shard_map/all_to_all | solution.py:793
  71.3 4.2 %collective-permute-start.15 = (f32[32,2,8,128]{3,2,1,0:T(8,128)S(1)}, f32[32,2,8,128]{3,2,1,0:T(8,128)S(1)}, u32[]{:S(2)}, u32[]{:S(2)}) collective-permute-start(f32[32,2,8,128]{3,2,1,0:T(8,128)S(1)} %all-to-all-done.mine), channel_id=1, source_target_pairs={{0,4},{4,0},{8,12},{12,8},{16,20},{20,16},{24,28},{28,24},{32,36},... | collective-permute-start | bytes 786440 | tf_op jit(solution)/shard_map/ppermute | solution.py:734
  75.5 1.1 %collective-permute-done.15.theirs = f32[32,2,8,128]{3,2,1,0:T(8,128)S(1)} collective-permute-done((f32[32,2,8,128]{3,2,1,0:T(8,128)S(1)}, f32[32,2,8,128]{3,2,1,0:T(8,128)S(1)}, u32[]{:S(2)}, u32[]{:S(2)}) %collective-permute-start.15) | collective-permute-done | bytes 262176 | tf_op jit(solution)/shard_map/ppermute | solution.py:734
  76.6 2.0 %shard_map.56.e2 = f32[192,128]{1,0:T(8,128)S(1)} custom-call(f32[32,2,8,128]{3,2,1,0:T(8,128)S(1)} %all-to-all-done.mine, f32[32,2,8,128]{3,2,1,0:T(8,128)S(1)} %collective-permute-done.15.theirs), custom_call_target="tpu_custom_call" | custom-call | tf_op jit(solution)/shard_map/pallas_call | solution.py:136
  78.9 0.9 %collective-permute-start.17 = (f32[2,32,128]{2,1,0:T(8,128)S(1)}, f32[2,32,128]{2,1,0:T(8,128)S(1)}, u32[]{:S(2)}, u32[]{:S(2)}) collective-permute-start(f32[2,32,128]{2,1,0:T(8,128)S(1)} %shard_map.57.e2), channel_id=1, source_target_pairs={{0,252},{4,8},{8,4},{12,16},{16,12},{20,24},{24,20},{28,32},{32,28... | collective-permute-start | bytes 98312 | tf_op jit(solution)/shard_map/ppermute | solution.py:739
  79.9 2.5 %collective-permute-done.17.far = f32[2,32,128]{2,1,0:T(8,128)S(1)} collective-permute-done((f32[2,32,128]{2,1,0:T(8,128)S(1)}, f32[2,32,128]{2,1,0:T(8,128)S(1)}, u32[]{:S(2)}, u32[]{:S(2)}) %collective-permute-start.17) | collective-permute-done | bytes 32800 | tf_op jit(solution)/shard_map/ppermute | solution.py:739
  83.0 3.8 %collective-permute-start.18 = (f32[40,128]{1,0:T(8,128)S(1)}, f32[40,128]{1,0:T(8,128)S(1)}, u32[]{:S(2)}, u32[]{:S(2)}) collective-permute-start(f32[40,128]{1,0:T(8,128)S(1)} %get-tuple-element.73), channel_id=1, source_target_pairs={{0,4},{4,0},{8,12},{12,8},{16,20},{20,16},{24,28},{28,24},{32,36},... | collective-permute-start | bytes 61448 | tf_op jit(solution)/shard_map/ppermute | solution.py:734
  86.9 0.7 collective-permute-done.18.other
  87.6 2.5 %shard_map.59 = f32[4,64,256]{2,1,0:T(8,128)} custom-call(f32[2,40,128]{2,1,0:T(8,128)S(1)} %get-tuple-element.71.e1, f32[40,128]{1,0:T(8,128)S(1)} %get-tuple-element.72.edge, f32[40,128]{1,0:T(8,128)S(1)} %collective-permute-done.18.other, f32[2,80,256]{2,1,0:T(8,128)S(1)} %get-tuple-element.74.outer, f32[16,64,256]{2,1,0:T(8,128)S(1)} %pad_maximum_fusion.1.inner, ...), custom_call_target="tpu_custom_call" | custom-call | tf_op jit(solution)/shard_map/pallas_call | solution.py:136
  (34 shorter events, 4.3 us)
Async XLA Ops:
  2.2 13.2 %collective-permute-start = (f32[16,8,256]{2,1,0:T(8,128)}, f32[16,8,256]{2,1,0:T(8,128)S(1)}, u32[]{:S(2)}, u32[]{:S(2)}) collective-permute-start(f32[16,8,256]{2,1,0:T(8,128)} %get-tuple-element.43), channel_id=1, source_target_pairs={{0,1},{1,2},{2,3},{3,0},{4,5},{5,6},{6,7},{7,4},{8,9},{9,10},{10,1... | collective-permute-start | bytes 393224 | tf_op jit(solution)/shard_map/ppermute | solution.py:730
  4.4 11.0 %collective-permute-start.1 = (f32[16,8,256]{2,1,0:T(8,128)}, f32[16,8,256]{2,1,0:T(8,128)S(1)}, u32[]{:S(2)}, u32[]{:S(2)}) collective-permute-start(f32[16,8,256]{2,1,0:T(8,128)} %get-tuple-element.44), channel_id=1, source_target_pairs={{0,3},{1,0},{2,1},{3,2},{4,7},{5,4},{6,5},{7,6},{8,11},{9,8},{10,9... | collective-permute-start | bytes 393224 | tf_op jit(solution)/shard_map/ppermute | solution.py:730
  5.9 11.8 %collective-permute-start.2 = (f32[5,64,256]{2,1,0:T(8,128)}, f32[5,64,256]{2,1,0:T(8,128)S(1)}, u32[]{:S(2)}, u32[]{:S(2)}) collective-permute-start(f32[5,64,256]{2,1,0:T(8,128)} %get-tuple-element.47), channel_id=1, source_target_pairs={{0,252},{4,8},{8,4},{12,16},{16,12},{20,24},{24,20},{28,32},{32,28... | collective-permute-start | bytes 983048 | tf_op jit(solution)/shard_map/ppermute | solution.py:739
  8.5 9.2 %collective-permute-start.3 = (f32[5,64,256]{2,1,0:T(8,128)}, f32[5,64,256]{2,1,0:T(8,128)S(1)}, u32[]{:S(2)}, u32[]{:S(2)}) collective-permute-start(f32[5,64,256]{2,1,0:T(8,128)} %get-tuple-element.48), channel_id=1, source_target_pairs={{0,4},{4,0},{8,12},{12,8},{16,20},{20,16},{24,28},{28,24},{32,36},... | collective-permute-start | bytes 983048 | tf_op jit(solution)/shard_map/ppermute | solution.py:734
  15.8 6.4 %collective-permute-start.4 = (f32[280,256]{1,0:T(8,128)S(1)}, f32[280,256]{1,0:T(8,128)S(1)}, u32[]{:S(2)}, u32[]{:S(2)}) collective-permute-start(f32[280,256]{1,0:T(8,128)S(1)} %get-tuple-element.49), channel_id=1, source_target_pairs={{0,252},{4,8},{8,4},{12,16},{16,12},{20,24},{24,20},{28,32},{32,28... | collective-permute-start | bytes 860168 | tf_op jit(solution)/shard_map/ppermute | solution.py:739
  15.9 6.3 %collective-permute-start.5 = (f32[280,256]{1,0:T(8,128)S(1)}, f32[280,256]{1,0:T(8,128)S(1)}, u32[]{:S(2)}, u32[]{:S(2)}) collective-permute-start(f32[280,256]{1,0:T(8,128)S(1)} %get-tuple-element.50), channel_id=1, source_target_pairs={{0,4},{4,0},{8,12},{12,8},{16,20},{20,16},{24,28},{28,24},{32,36},... | collective-permute-start | bytes 860168 | tf_op jit(solution)/shard_map/ppermute | solution.py:734
  24.7 4.1 %collective-permute-start.7 = (f32[8,40,128]{2,1,0:T(8,128)S(1)}, f32[8,40,128]{2,1,0:T(8,128)S(1)}, u32[]{:S(2)}, u32[]{:S(2)}) collective-permute-start(f32[8,40,128]{2,1,0:T(8,128)S(1)} %get-tuple-element.52), channel_id=1, source_target_pairs={{0,4},{4,0},{8,12},{12,8},{16,20},{20,16},{24,28},{28,24},{32,36},... | collective-permute-start | bytes 491528 | tf_op jit(solution)/shard_map/ppermute | solution.py:734
  27.8 4.7 %collective-permute-start.6 = (f32[8,40,128]{2,1,0:T(8,128)S(1)}, f32[8,40,128]{2,1,0:T(8,128)S(1)}, u32[]{:S(2)}, u32[]{:S(2)}) collective-permute-start(f32[8,40,128]{2,1,0:T(8,128)S(1)} %get-tuple-element.51.own), channel_id=1, source_target_pairs={{0,252},{4,8},{8,4},{12,16},{16,12},{20,24},{24,20},{28,32},{32,28... | collective-permute-start | bytes 491528 | tf_op jit(solution)/shard_map/ppermute | solution.py:739
  32.9 6.9 %collective-permute-start.8 = (f32[56,128]{1,0:T(8,128)S(1)}, f32[56,128]{1,0:T(8,128)S(1)}, u32[]{:S(2)}, u32[]{:S(2)}) collective-permute-start(f32[56,128]{1,0:T(8,128)S(1)} %get-tuple-element.55), channel_id=1, source_target_pairs={{0,1},{1,2},{2,3},{3,0},{4,5},{5,6},{6,7},{7,4},{8,9},{9,10},{10,1... | collective-permute-start | bytes 86024 | tf_op jit(solution)/shard_map/ppermute | solution.py:730
  33.0 6.8 %collective-permute-start.9 = (f32[56,128]{1,0:T(8,128)S(1)}, f32[56,128]{1,0:T(8,128)S(1)}, u32[]{:S(2)}, u32[]{:S(2)}) collective-permute-start(f32[56,128]{1,0:T(8,128)S(1)} %get-tuple-element.56), channel_id=1, source_target_pairs={{0,3},{1,0},{2,1},{3,2},{4,7},{5,4},{6,5},{7,6},{8,11},{9,8},{10,9... | collective-permute-start | bytes 86024 | tf_op jit(solution)/shard_map/ppermute | solution.py:730
  35.6 4.1 %collective-permute-start.10 = (f32[40,128]{1,0:T(8,128)S(1)}, f32[40,128]{1,0:T(8,128)S(1)}, u32[]{:S(2)}, u32[]{:S(2)}) collective-permute-start(f32[40,128]{1,0:T(8,128)S(1)} %get-tuple-element.54.f2), channel_id=1, source_target_pairs={{0,2},{1,3},{2,0},{3,1},{4,6},{5,7},{6,4},{7,5},{8,10},{9,11},{10,... | collective-permute-start | bytes 61448 | tf_op jit(solution)/shard_map/ppermute | solution.py:730
  40.0 6.2 %collective-permute-start.11 = (f32[240,128]{1,0:T(8,128)S(1)}, f32[240,128]{1,0:T(8,128)S(1)}, u32[]{:S(2)}, u32[]{:S(2)}) collective-permute-start(f32[240,128]{1,0:T(8,128)S(1)} %get-tuple-element.59.msg), channel_id=1, source_target_pairs={{0,4},{4,0},{8,12},{12,8},{16,20},{20,16},{24,28},{28,24},{32,36},... | collective-permute-start | bytes 368648 | tf_op jit(solution)/shard_map/ppermute | solution.py:734
  46.2 4.3 %collective-permute-start.12 = (f32[224,128]{1,0:T(8,128)S(1)}, f32[224,128]{1,0:T(8,128)S(1)}, u32[]{:S(2)}, u32[]{:S(2)}) collective-permute-start(f32[224,128]{1,0:T(8,128)S(1)} %shard_map.52), channel_id=1, source_target_pairs={{0,252},{4,8},{8,4},{12,16},{16,12},{20,24},{24,20},{28,32},{32,28... | collective-permute-start | bytes 344072 | tf_op jit(solution)/shard_map/ppermute | solution.py:739
  50.5 4.6 %collective-permute-start.13 = (f32[224,128]{1,0:T(8,128)S(1)}, f32[224,128]{1,0:T(8,128)S(1)}, u32[]{:S(2)}, u32[]{:S(2)}) collective-permute-start(f32[224,128]{1,0:T(8,128)S(1)} %collective-permute-done.12.near), channel_id=1, source_target_pairs={{0,4},{4,0},{8,12},{12,8},{16,20},{20,16},{24,28},{28,24},{32,36},... | collective-permute-start | bytes 344072 | tf_op jit(solution)/shard_map/ppermute | solution.py:734
  55.5 0.6 copy-start
  57.1 14.1 %all-to-all-start = ((f32[32,2,8,128]{3,2,1,0:T(8,128)}), f32[32,2,8,128]{3,2,1,0:T(8,128)S(1)}, u32[]{:S(2)}, u32[]{:S(2)}) async-start(f32[32,2,8,128]{3,2,1,0:T(8,128)} %shard_map.55), calls=%async_computation | async-start | bytes 524288 | tf_op jit(solution)/shard_map/all_to_all | solution.py:793
  61.0 9.1 %collective-permute-start.14 = (f32[192,128]{1,0:T(8,128)}, f32[192,128]{1,0:T(8,128)S(1)}, u32[]{:S(2)}, u32[]{:S(2)}) collective-permute-start(f32[192,128]{1,0:T(8,128)} %copy-done), channel_id=1, source_target_pairs={{0,252},{4,8},{8,4},{12,16},{16,12},{20,24},{24,20},{28,32},{32,28... | collective-permute-start | bytes 294920 | tf_op jit(solution)/shard_map/ppermute | solution.py:739
  71.3 15.5 %copy-start.1 = (f32[4,64,256]{2,1,0:T(8,128)S(1)}, f32[4,64,256]{2,1,0:T(8,128)}, u32[]{:S(2)}) copy-start(f32[4,64,256]{2,1,0:T(8,128)} %c3.1) | copy-start | bytes 786436
  71.3 15.5 %copy-start.2 = (f32[4,64,256]{2,1,0:T(8,128)S(1)}, f32[4,64,256]{2,1,0:T(8,128)}, u32[]{:S(2)}) copy-start(f32[4,64,256]{2,1,0:T(8,128)} %c2.1) | copy-start | bytes 786436
  71.3 15.5 %copy-start.3 = (f32[4,64,256]{2,1,0:T(8,128)S(1)}, f32[4,64,256]{2,1,0:T(8,128)}, u32[]{:S(2)}) copy-start(f32[4,64,256]{2,1,0:T(8,128)} %c1.1) | copy-start | bytes 786436
  71.3 15.5 %copy-start.4 = (f32[4,64,256]{2,1,0:T(8,128)S(1)}, f32[4,64,256]{2,1,0:T(8,128)}, u32[]{:S(2)}) copy-start(f32[4,64,256]{2,1,0:T(8,128)} %f.1) | copy-start | bytes 786436
  71.3 5.3 %collective-permute-start.15 = (f32[32,2,8,128]{3,2,1,0:T(8,128)S(1)}, f32[32,2,8,128]{3,2,1,0:T(8,128)S(1)}, u32[]{:S(2)}, u32[]{:S(2)}) collective-permute-start(f32[32,2,8,128]{3,2,1,0:T(8,128)S(1)} %all-to-all-done.mine), channel_id=1, source_target_pairs={{0,4},{4,0},{8,12},{12,8},{16,20},{20,16},{24,28},{28,24},{32,36},... | collective-permute-start | bytes 786440 | tf_op jit(solution)/shard_map/ppermute | solution.py:734
  75.4 3.2 %collective-permute-start.16 = (f32[192,128]{1,0:T(8,128)S(1)}, f32[192,128]{1,0:T(8,128)S(1)}, u32[]{:S(2)}, u32[]{:S(2)}) collective-permute-start(f32[192,128]{1,0:T(8,128)S(1)} %collective-permute-done.14.late), channel_id=1, source_target_pairs={{0,4},{4,0},{8,12},{12,8},{16,20},{20,16},{24,28},{28,24},{32,36},... | collective-permute-start | bytes 294920 | tf_op jit(solution)/shard_map/ppermute | solution.py:734
  78.9 3.4 %collective-permute-start.17 = (f32[2,32,128]{2,1,0:T(8,128)S(1)}, f32[2,32,128]{2,1,0:T(8,128)S(1)}, u32[]{:S(2)}, u32[]{:S(2)}) collective-permute-start(f32[2,32,128]{2,1,0:T(8,128)S(1)} %shard_map.57.e2), channel_id=1, source_target_pairs={{0,252},{4,8},{8,4},{12,16},{16,12},{20,24},{24,20},{28,32},{32,28... | collective-permute-start | bytes 98312 | tf_op jit(solution)/shard_map/ppermute | solution.py:739
  83.0 4.6 %collective-permute-start.18 = (f32[40,128]{1,0:T(8,128)S(1)}, f32[40,128]{1,0:T(8,128)S(1)}, u32[]{:S(2)}, u32[]{:S(2)}) collective-permute-start(f32[40,128]{1,0:T(8,128)S(1)} %get-tuple-element.73), channel_id=1, source_target_pairs={{0,4},{4,0},{8,12},{12,8},{16,20},{20,16},{24,28},{28,24},{32,36},... | collective-permute-start | bytes 61448 | tf_op jit(solution)/shard_map/ppermute | solution.py:734

commit v15 on v13

--- a/solution.py
+++ b/solution.py
@@ -646,14 +646,15 @@
 
     w = [first_post(v[m + 1], v[m], v[m + 2], *args(m)) for m in range(4)]
     for p in range(2):
-        out[p] = second_post(w[p + 1], v[p + 2], w[p], w[p + 2], *args(p + 1))
+        x = second_post(w[p + 1], v[p + 2], w[p], w[p + 2], *args(p + 1))
+        out[p] = pltpu.roll(x, lax.rem(72 - 16 * lax.axis_index("narrow"), 64), 0)[0:32]
 
 
 def middle_post_kernel(e2, far, u2, f, g, w1, own, edge, send, fine, c1, v, w):
-    n, par = lax.axis_index("narrow"), lax.rem(lax.axis_index("wide"), 2)
+    par = lax.rem(lax.axis_index("wide"), 2)
     odd = par == 1
-    row, col = iota((40, 64), 0), iota((40, 64), 1)
-    pick = (col == lax.rem(16 * n + (row + 4) // 2 + 60, 64)).astype(F32)
+    row, col = iota((40, 32), 0), iota((40, 32), 1)
+    pick = (col == (row + 4) // 2 + 4).astype(F32)
     lanes = copies_of_lanes(128, 128)
     planes = (e2[0], e2[1], far[0], far[1])
     for k in range(4):
@@ -679,7 +680,7 @@
     send[...] = jnp.where(odd, out[0], out[2])
 
 
-def fine_post_kernel(e1, edge, other, outer, inner, low, high, halo, u2, out, f, c1, c2, c3, g, v, w, scr):
+def fine_post_kernel(e1, edge, other, outer, inner, low, high, halo, u2, result, f, c1, c2, c3, g, v, w, scr, out, sems):
     for a, ref in enumerate((f, c1, c2, c3)):
         ref[0] = halo[a]
         ref[5] = halo[4 + a]
@@ -722,7 +723,13 @@
             out[q - 1, pl.ds(r0 - 8, CHUNK), :] = x + step
         return carry
 
-    lax.fori_loop(1, 5, post2, 0)
+    copies = []
+    for p in range(4):
+        post2(p + 1, 0)
+        copies.append(pltpu.make_async_copy(out.at[pl.ds(p, 1)], result.at[pl.ds(p, 1)], sems.at[p]))
+        copies[p].start()
+    for copy in copies:
+        copy.wait()
 
 
 def shift(x, axis, by):
@@ -801,7 +808,7 @@
         [three, (n3 + 1, 8, 128), three, three, three, three, (n3 + 2, 8, 128), (n3 + 2, 8, 128), four, four]
         + [(n4 + 1, 8, 128), four, four, four, (n4 + 2, 8, 128), (n4 + 2, 8, 128), four, (32, 128)],
     )(parts, theirs)
-    (e2,) = call(coarse_post_kernel, [(2, 64, 128)])(fine2, w2, u2w, late, late_sib)
+    (e2,) = call(coarse_post_kernel, [(2, 32, 128)])(fine2, w2, u2w, late, late_sib)
     e2, *again = lax.optimization_barrier((e2,) + inputs)
     far = across(e2)
 
@@ -815,7 +822,8 @@
     (out,) = call(
         fine_post_kernel,
         [(4, 64, 256)],
-        windows + [(6,) + big, (8,) + big, (8,) + big, (320, 128)],
+        windows + [(6,) + big, (8,) + big, (8,) + big, (320, 128), (4, 64, 256), pltpu.SemaphoreType.DMA((4,))],
+        out_places={0: pltpu.HBM},
         limit=6,
     )(e1, edge, other1, outer, jnp.concatenate(again, axis=0), low0, high0, halo, u2)
     return out

time: 90 us -> 89.5 us (level)
  no operation moved by 1% of the time
where the time goes in v15:
time: 89.5 us; the launch traced here: 89.3 us
  starting transfers between devices  43.5 us (49%)
  waiting for transfers between devices  31.5 us (35%)
  Pallas kernels  12.6 us (14%)
  other arithmetic  1.35 us (2%)
    ppermute x8, starting transfers between devices, sibling(): lax.ppermute(x, 'wide', [(i, i ^ 1) for i in range(lax.axis_size('wide'))])  26.3 us
    ppermute x6, waiting for transfers between devices, across(): lax.ppermute(x, 'wide', [(i, (i + 1 if i % 2 else i - 1) % count) for i i...  21.1 us
    pallas_call x14, Pallas kernels, run(): pl.pallas_call(kernel, out_shape=[jax.ShapeDtypeStruct(s, F32) for s in o...  12.6 us
    ppermute x5, starting transfers between devices, shift(): return lax.ppermute(x, axis, [(i, (i + by) % count) for i in range(count)])  6.82 us
    ppermute x6, starting transfers between devices, across(): lax.ppermute(x, 'wide', [(i, (i + 1 if i % 2 else i - 1) % count) for i i...  6.47 us
    ppermute x8, waiting for transfers between devices, sibling(): lax.ppermute(x, 'wide', [(i, i ^ 1) for i in range(lax.axis_size('wide'))])  4.62 us
    all_to_all x1, starting transfers between devices, body(): lax.all_to_all(send, 'wide', split_axis=0, concat_axis=0, tiled=True, axi...  3.87 us
    ppermute x5, waiting for transfers between devices, shift(): return lax.ppermute(x, axis, [(i, (i + by) % count) for i in range(count)])  3.8 us
  transfers between devices with their start and end apart: 20, of which 12 were waited for; matrix products, arithmetic and copies ran while one was open for 2% of the time, Pallas kernels for 3%

profile of v15, /device:TPU:1, one launch (start us, length us, event | category | flops | bytes accessed | tf_op | source)
XLA Modules:
  0.0 89.3 jit_solution(17784564751098898964)
XLA Ops:
  0.0 2.1 %shard_map.46 = (f32[16,8,256]{2,1,0:T(8,128)}, f32[16,8,256]{2,1,0:T(8,128)}, f32[5,64,256]{2,1,0:T(8,128)}, f32[5,64,256]{2,1,0:T(8,128)}) custom-call(f32[4,64,256]{2,1,0:T(8,128)} %f.1, f32[4,64,256]{2,1,0:T(8,128)} %c1.1, f32[4,64,256]{2,1,0:T(8,128)} %c2.1, f32[4,64,256]{2,1,0:T(8,128)} %c3.1), custom_call_target="tpu_custom_call" | custom-call | tf_op jit(solution)/shard_map/pallas_call | solution.py:136
  2.2 2.2 %collective-permute-start = (f32[16,8,256]{2,1,0:T(8,128)}, f32[16,8,256]{2,1,0:T(8,128)S(1)}, u32[]{:S(2)}, u32[]{:S(2)}) collective-permute-start(f32[16,8,256]{2,1,0:T(8,128)} %get-tuple-element.43), channel_id=1, source_target_pairs={{0,1},{1,2},{2,3},{3,0},{4,5},{5,6},{6,7},{7,4},{8,9},{9,10},{10,1... | collective-permute-start | bytes 393224 | tf_op jit(solution)/shard_map/ppermute | solution.py:737
  4.4 1.5 %collective-permute-start.1 = (f32[16,8,256]{2,1,0:T(8,128)}, f32[16,8,256]{2,1,0:T(8,128)S(1)}, u32[]{:S(2)}, u32[]{:S(2)}) collective-permute-start(f32[16,8,256]{2,1,0:T(8,128)} %get-tuple-element.44), channel_id=1, source_target_pairs={{0,3},{1,0},{2,1},{3,2},{4,7},{5,4},{6,5},{7,6},{8,11},{9,8},{10,9... | collective-permute-start | bytes 393224 | tf_op jit(solution)/shard_map/ppermute | solution.py:737
  5.9 2.6 %collective-permute-start.2 = (f32[5,64,256]{2,1,0:T(8,128)}, f32[5,64,256]{2,1,0:T(8,128)S(1)}, u32[]{:S(2)}, u32[]{:S(2)}) collective-permute-start(f32[5,64,256]{2,1,0:T(8,128)} %get-tuple-element.47), channel_id=1, source_target_pairs={{0,252},{4,8},{8,4},{12,16},{16,12},{20,24},{24,20},{28,32},{32,28... | collective-permute-start | bytes 983048 | tf_op jit(solution)/shard_map/ppermute | solution.py:746
  8.5 5.6 %collective-permute-start.3 = (f32[5,64,256]{2,1,0:T(8,128)}, f32[5,64,256]{2,1,0:T(8,128)S(1)}, u32[]{:S(2)}, u32[]{:S(2)}) collective-permute-start(f32[5,64,256]{2,1,0:T(8,128)} %get-tuple-element.48), channel_id=1, source_target_pairs={{0,4},{4,0},{8,12},{12,8},{16,20},{20,16},{24,28},{28,24},{32,36},... | collective-permute-start | bytes 983048 | tf_op jit(solution)/shard_map/ppermute | solution.py:741
  14.1 1.3 %pad_maximum_fusion.inner = f32[16,64,256]{2,1,0:T(8,128)S(1)} fusion(f32[4,64,256]{2,1,0:T(8,128)} %c3.1, f32[4,64,256]{2,1,0:T(8,128)} %c2.1, f32[4,64,256]{2,1,0:T(8,128)} %c1.1, f32[4,64,256]{2,1,0:T(8,128)} %f.1), kind=kLoop, calls=%fused_computation | loop fusion | flops 786432 | bytes 2097152 | tf_op jit(solution)/shard_map/concatenate | solution.py:768
  15.9 1.8 %collective-permute-start.5 = (f32[280,256]{1,0:T(8,128)S(1)}, f32[280,256]{1,0:T(8,128)S(1)}, u32[]{:S(2)}, u32[]{:S(2)}) collective-permute-start(f32[280,256]{1,0:T(8,128)S(1)} %get-tuple-element.50), channel_id=1, source_target_pairs={{0,4},{4,0},{8,12},{12,8},{16,20},{20,16},{24,28},{28,24},{32,36},... | collective-permute-start | bytes 860168 | tf_op jit(solution)/shard_map/ppermute | solution.py:741
  17.7 4.5 %collective-permute-done.4.far = f32[280,256]{1,0:T(8,128)S(1)} collective-permute-done((f32[280,256]{1,0:T(8,128)S(1)}, f32[280,256]{1,0:T(8,128)S(1)}, u32[]{:S(2)}, u32[]{:S(2)}) %collective-permute-start.4) | collective-permute-done | bytes 286752 | tf_op jit(solution)/shard_map/ppermute | solution.py:746
  22.2 2.4 %shard_map.48 = (f32[9,80,256]{2,1,0:T(8,128)S(1)}, f32[6,80,256]{2,1,0:T(8,128)S(1)}, f32[18,40,128]{2,1,0:T(8,128)S(1)}, f32[8,40,128]{2,1,0:T(8,128)S(1)}, f32[8,40,128]{2,1,0:T(8,128)S(1)}) custom-call(f32[16,80,256]{2,1,0:T(8,128)S(1)} %get-tuple-element.45.own, f32[6,40,128]{2,1,0:T(8,128)S(1)} %get-tuple-element.46.coef1, ...), custom_call_target="tpu_custom_call" | custom-call | tf_op jit(solution)/shard_map/pallas_call | solution.py:136
  24.6 3.1 %collective-permute-start.7 = (f32[8,40,128]{2,1,0:T(8,128)S(1)}, f32[8,40,128]{2,1,0:T(8,128)S(1)}, u32[]{:S(2)}, u32[]{:S(2)}) collective-permute-start(f32[8,40,128]{2,1,0:T(8,128)S(1)} %get-tuple-element.52), channel_id=1, source_target_pairs={{0,4},{4,0},{8,12},{12,8},{16,20},{20,16},{24,28},{28,24},{32,36},... | collective-permute-start | bytes 491528 | tf_op jit(solution)/shard_map/ppermute | solution.py:741
  28.0 0.8 collective-permute-done.7.sib
  28.7 3.7 %collective-permute-done.6.far = f32[8,40,128]{2,1,0:T(8,128)S(1)} collective-permute-done((f32[8,40,128]{2,1,0:T(8,128)S(1)}, f32[8,40,128]{2,1,0:T(8,128)S(1)}, u32[]{:S(2)}, u32[]{:S(2)}) %collective-permute-start.6) | collective-permute-done | bytes 163872 | tf_op jit(solution)/shard_map/ppermute | solution.py:746
  32.9 2.7 %collective-permute-start.9 = (f32[56,128]{1,0:T(8,128)S(1)}, f32[56,128]{1,0:T(8,128)S(1)}, u32[]{:S(2)}, u32[]{:S(2)}) collective-permute-start(f32[56,128]{1,0:T(8,128)S(1)} %get-tuple-element.56), channel_id=1, source_target_pairs={{0,3},{1,0},{2,1},{3,2},{4,7},{5,4},{6,5},{7,6},{8,11},{9,8},{10,9... | collective-permute-start | bytes 86024 | tf_op jit(solution)/shard_map/ppermute | solution.py:737
  35.9 3.8 %collective-permute-done.10.far = f32[40,128]{1,0:T(8,128)S(1)} collective-permute-done((f32[40,128]{1,0:T(8,128)S(1)}, f32[40,128]{1,0:T(8,128)S(1)}, u32[]{:S(2)}, u32[]{:S(2)}) %collective-permute-start.10) | collective-permute-done | bytes 20512 | tf_op jit(solution)/shard_map/ppermute | solution.py:737
  39.9 5.2 %collective-permute-start.11 = (f32[240,128]{1,0:T(8,128)S(1)}, f32[240,128]{1,0:T(8,128)S(1)}, u32[]{:S(2)}, u32[]{:S(2)}) collective-permute-start(f32[240,128]{1,0:T(8,128)S(1)} %get-tuple-element.59.msg), channel_id=1, source_target_pairs={{0,4},{4,0},{8,12},{12,8},{16,20},{20,16},{24,28},{28,24},{32,36},... | collective-permute-start | bytes 368648 | tf_op jit(solution)/shard_map/ppermute | solution.py:741
  45.1 1.0 %collective-permute-done.11.sib = f32[240,128]{1,0:T(8,128)S(1)} collective-permute-done((f32[240,128]{1,0:T(8,128)S(1)}, f32[240,128]{1,0:T(8,128)S(1)}, u32[]{:S(2)}, u32[]{:S(2)}) %collective-permute-start.11) | collective-permute-done | bytes 122912 | tf_op jit(solution)/shard_map/ppermute | solution.py:741
  46.5 4.8 %collective-permute-done.12.near = f32[384,128]{1,0:T(8,128)S(1)} collective-permute-done((f32[384,128]{1,0:T(8,128)S(1)}, f32[384,128]{1,0:T(8,128)S(1)}, u32[]{:S(2)}, u32[]{:S(2)}) %collective-permute-start.12) | collective-permute-done | bytes 196640 | tf_op jit(solution)/shard_map/ppermute | solution.py:746
  51.3 3.7 %collective-permute-start.13 = (f32[384,128]{1,0:T(8,128)S(1)}, f32[384,128]{1,0:T(8,128)S(1)}, u32[]{:S(2)}, u32[]{:S(2)}) collective-permute-start(f32[384,128]{1,0:T(8,128)S(1)} %collective-permute-done.12.near), channel_id=1, source_target_pairs={{0,4},{4,0},{8,12},{12,8},{16,20},{20,16},{24,28},{28,24},{32,36},... | collective-permute-start | bytes 589832 | tf_op jit(solution)/shard_map/ppermute | solution.py:741
  55.0 1.1 %collective-permute-done.13.other = f32[384,128]{1,0:T(8,128)S(1)} collective-permute-done((f32[384,128]{1,0:T(8,128)S(1)}, f32[384,128]{1,0:T(8,128)S(1)}, u32[]{:S(2)}, u32[]{:S(2)}) %collective-permute-start.13) | collective-permute-done | bytes 196640 | tf_op jit(solution)/shard_map/ppermute | solution.py:741
  56.4 1.0 %shard_map.55 = f32[32,2,8,128]{3,2,1,0:T(8,128)} custom-call(f32[21,64,128]{2,1,0:T(8,128)S(1)} %get-tuple-element.61.w.win, f32[4,64,128]{2,1,0:T(8,128)S(1)} %get-tuple-element.62.u2, f32[3,8,128]{2,1,0:T(8,128)S(1)} %shard_map.53.tiles), custom_call_target="tpu_custom_call" | custom-call | tf_op jit(solution)/shard_map/pallas_call | solution.py:136
  57.4 3.9 %all-to-all-start = ((f32[32,2,8,128]{3,2,1,0:T(8,128)}), f32[32,2,8,128]{3,2,1,0:T(8,128)S(1)}, u32[]{:S(2)}, u32[]{:S(2)}) async-start(f32[32,2,8,128]{3,2,1,0:T(8,128)} %shard_map.55), calls=%async_computation | async-start | bytes 524288 | tf_op jit(solution)/shard_map/all_to_all | solution.py:800
  61.3 1.7 %collective-permute-start.14 = (f32[32,128]{1,0:T(8,128)S(1)}, f32[32,128]{1,0:T(8,128)S(1)}, u32[]{:S(2)}, u32[]{:S(2)}) collective-permute-start(f32[32,128]{1,0:T(8,128)S(1)} %get-tuple-element.64), channel_id=1, source_target_pairs={{0,252},{4,8},{8,4},{12,16},{16,12},{20,24},{24,20},{28,32},{32,28... | collective-permute-start | bytes 49160 | tf_op jit(solution)/shard_map/ppermute | solution.py:746
  63.0 6.5 %collective-permute-done.14.late = f32[32,128]{1,0:T(8,128)S(1)} collective-permute-done((f32[32,128]{1,0:T(8,128)S(1)}, f32[32,128]{1,0:T(8,128)S(1)}, u32[]{:S(2)}, u32[]{:S(2)}) %collective-permute-start.14) | collective-permute-done | bytes 16416 | tf_op jit(solution)/shard_map/ppermute | solution.py:746
  69.5 2.0 %all-to-all-done.mine = f32[32,2,8,128]{3,2,1,0:T(8,128)S(1)} async-done(((f32[32,2,8,128]{3,2,1,0:T(8,128)}), f32[32,2,8,128]{3,2,1,0:T(8,128)S(1)}, u32[]{:S(2)}, u32[]{:S(2)}) %all-to-all-start) | async-done | bytes 262176 | tf_op jit(solution)/shard_map/all_to_all | solution.py:800
  71.5 3.2 %collective-permute-start.15 = (f32[32,2,8,128]{3,2,1,0:T(8,128)S(1)}, f32[32,2,8,128]{3,2,1,0:T(8,128)S(1)}, u32[]{:S(2)}, u32[]{:S(2)}) collective-permute-start(f32[32,2,8,128]{3,2,1,0:T(8,128)S(1)} %all-to-all-done.mine), channel_id=1, source_target_pairs={{0,4},{4,0},{8,12},{12,8},{16,20},{20,16},{24,28},{28,24},{32,36},... | collective-permute-start | bytes 786440 | tf_op jit(solution)/shard_map/ppermute | solution.py:741
  74.8 1.1 %collective-permute-done.15.theirs = f32[32,2,8,128]{3,2,1,0:T(8,128)S(1)} collective-permute-done((f32[32,2,8,128]{3,2,1,0:T(8,128)S(1)}, f32[32,2,8,128]{3,2,1,0:T(8,128)S(1)}, u32[]{:S(2)}, u32[]{:S(2)}) %collective-permute-start.15) | collective-permute-done | bytes 262176 | tf_op jit(solution)/shard_map/ppermute | solution.py:741
  75.9 2.0 %shard_map.56.e2 = f32[192,128]{1,0:T(8,128)S(1)} custom-call(f32[32,2,8,128]{3,2,1,0:T(8,128)S(1)} %all-to-all-done.mine, f32[32,2,8,128]{3,2,1,0:T(8,128)S(1)} %collective-permute-done.15.theirs), custom_call_target="tpu_custom_call" | custom-call | tf_op jit(solution)/shard_map/pallas_call | solution.py:136
  78.2 1.9 %collective-permute-start.17 = (f32[2,32,128]{2,1,0:T(8,128)S(1)}, f32[2,32,128]{2,1,0:T(8,128)S(1)}, u32[]{:S(2)}, u32[]{:S(2)}) collective-permute-start(f32[2,32,128]{2,1,0:T(8,128)S(1)} %shard_map.57.e2), channel_id=1, source_target_pairs={{0,252},{4,8},{8,4},{12,16},{16,12},{20,24},{24,20},{28,32},{32,28... | collective-permute-start | bytes 98312 | tf_op jit(solution)/shard_map/ppermute | solution.py:746
  80.1 1.6 %collective-permute-done.17.far = f32[2,32,128]{2,1,0:T(8,128)S(1)} collective-permute-done((f32[2,32,128]{2,1,0:T(8,128)S(1)}, f32[2,32,128]{2,1,0:T(8,128)S(1)}, u32[]{:S(2)}, u32[]{:S(2)}) %collective-permute-start.17) | collective-permute-done | bytes 32800 | tf_op jit(solution)/shard_map/ppermute | solution.py:746
  82.4 3.7 %collective-permute-start.18 = (f32[40,128]{1,0:T(8,128)S(1)}, f32[40,128]{1,0:T(8,128)S(1)}, u32[]{:S(2)}, u32[]{:S(2)}) collective-permute-start(f32[40,128]{1,0:T(8,128)S(1)} %get-tuple-element.73), channel_id=1, source_target_pairs={{0,4},{4,0},{8,12},{12,8},{16,20},{20,16},{24,28},{28,24},{32,36},... | collective-permute-start | bytes 61448 | tf_op jit(solution)/shard_map/ppermute | solution.py:741
  86.2 0.7 collective-permute-done.18.other
  86.9 2.2 %shard_map.59 = f32[4,64,256]{2,1,0:T(8,128)} custom-call(f32[2,40,128]{2,1,0:T(8,128)S(1)} %get-tuple-element.71.e1, f32[40,128]{1,0:T(8,128)S(1)} %get-tuple-element.72.edge, f32[40,128]{1,0:T(8,128)S(1)} %collective-permute-done.18.other, f32[2,80,256]{2,1,0:T(8,128)S(1)} %get-tuple-element.74.outer, f32[16,64,256]{2,1,0:T(8,128)S(1)} %pad_maximum_fusion.1.inner, ...), custom_call_target="tpu_custom_call" | custom-call | tf_op jit(solution)/shard_map/pallas_call | solution.py:136
  (32 shorter events, 3.7 us)
Async XLA Ops:
  2.2 13.2 %collective-permute-start = (f32[16,8,256]{2,1,0:T(8,128)}, f32[16,8,256]{2,1,0:T(8,128)S(1)}, u32[]{:S(2)}, u32[]{:S(2)}) collective-permute-start(f32[16,8,256]{2,1,0:T(8,128)} %get-tuple-element.43), channel_id=1, source_target_pairs={{0,1},{1,2},{2,3},{3,0},{4,5},{5,6},{6,7},{7,4},{8,9},{9,10},{10,1... | collective-permute-start | bytes 393224 | tf_op jit(solution)/shard_map/ppermute | solution.py:737
  4.4 11.0 %collective-permute-start.1 = (f32[16,8,256]{2,1,0:T(8,128)}, f32[16,8,256]{2,1,0:T(8,128)S(1)}, u32[]{:S(2)}, u32[]{:S(2)}) collective-permute-start(f32[16,8,256]{2,1,0:T(8,128)} %get-tuple-element.44), channel_id=1, source_target_pairs={{0,3},{1,0},{2,1},{3,2},{4,7},{5,4},{6,5},{7,6},{8,11},{9,8},{10,9... | collective-permute-start | bytes 393224 | tf_op jit(solution)/shard_map/ppermute | solution.py:737
  5.9 11.8 %collective-permute-start.2 = (f32[5,64,256]{2,1,0:T(8,128)}, f32[5,64,256]{2,1,0:T(8,128)S(1)}, u32[]{:S(2)}, u32[]{:S(2)}) collective-permute-start(f32[5,64,256]{2,1,0:T(8,128)} %get-tuple-element.47), channel_id=1, source_target_pairs={{0,252},{4,8},{8,4},{12,16},{16,12},{20,24},{24,20},{28,32},{32,28... | collective-permute-start | bytes 983048 | tf_op jit(solution)/shard_map/ppermute | solution.py:746
  8.5 9.2 %collective-permute-start.3 = (f32[5,64,256]{2,1,0:T(8,128)}, f32[5,64,256]{2,1,0:T(8,128)S(1)}, u32[]{:S(2)}, u32[]{:S(2)}) collective-permute-start(f32[5,64,256]{2,1,0:T(8,128)} %get-tuple-element.48), channel_id=1, source_target_pairs={{0,4},{4,0},{8,12},{12,8},{16,20},{20,16},{24,28},{28,24},{32,36},... | collective-permute-start | bytes 983048 | tf_op jit(solution)/shard_map/ppermute | solution.py:741
  15.8 6.4 %collective-permute-start.4 = (f32[280,256]{1,0:T(8,128)S(1)}, f32[280,256]{1,0:T(8,128)S(1)}, u32[]{:S(2)}, u32[]{:S(2)}) collective-permute-start(f32[280,256]{1,0:T(8,128)S(1)} %get-tuple-element.49), channel_id=1, source_target_pairs={{0,252},{4,8},{8,4},{12,16},{16,12},{20,24},{24,20},{28,32},{32,28... | collective-permute-start | bytes 860168 | tf_op jit(solution)/shard_map/ppermute | solution.py:746
  15.9 6.3 %collective-permute-start.5 = (f32[280,256]{1,0:T(8,128)S(1)}, f32[280,256]{1,0:T(8,128)S(1)}, u32[]{:S(2)}, u32[]{:S(2)}) collective-permute-start(f32[280,256]{1,0:T(8,128)S(1)} %get-tuple-element.50), channel_id=1, source_target_pairs={{0,4},{4,0},{8,12},{12,8},{16,20},{20,16},{24,28},{28,24},{32,36},... | collective-permute-start | bytes 860168 | tf_op jit(solution)/shard_map/ppermute | solution.py:741
  24.6 4.1 %collective-permute-start.7 = (f32[8,40,128]{2,1,0:T(8,128)S(1)}, f32[8,40,128]{2,1,0:T(8,128)S(1)}, u32[]{:S(2)}, u32[]{:S(2)}) collective-permute-start(f32[8,40,128]{2,1,0:T(8,128)S(1)} %get-tuple-element.52), channel_id=1, source_target_pairs={{0,4},{4,0},{8,12},{12,8},{16,20},{20,16},{24,28},{28,24},{32,36},... | collective-permute-start | bytes 491528 | tf_op jit(solution)/shard_map/ppermute | solution.py:741
  27.7 4.7 %collective-permute-start.6 = (f32[8,40,128]{2,1,0:T(8,128)S(1)}, f32[8,40,128]{2,1,0:T(8,128)S(1)}, u32[]{:S(2)}, u32[]{:S(2)}) collective-permute-start(f32[8,40,128]{2,1,0:T(8,128)S(1)} %get-tuple-element.51.own), channel_id=1, source_target_pairs={{0,252},{4,8},{8,4},{12,16},{16,12},{20,24},{24,20},{28,32},{32,28... | collective-permute-start | bytes 491528 | tf_op jit(solution)/shard_map/ppermute | solution.py:746
  32.8 6.9 %collective-permute-start.8 = (f32[56,128]{1,0:T(8,128)S(1)}, f32[56,128]{1,0:T(8,128)S(1)}, u32[]{:S(2)}, u32[]{:S(2)}) collective-permute-start(f32[56,128]{1,0:T(8,128)S(1)} %get-tuple-element.55), channel_id=1, source_target_pairs={{0,1},{1,2},{2,3},{3,0},{4,5},{5,6},{6,7},{7,4},{8,9},{9,10},{10,1... | collective-permute-start | bytes 86024 | tf_op jit(solution)/shard_map/ppermute | solution.py:737
  32.9 6.8 %collective-permute-start.9 = (f32[56,128]{1,0:T(8,128)S(1)}, f32[56,128]{1,0:T(8,128)S(1)}, u32[]{:S(2)}, u32[]{:S(2)}) collective-permute-start(f32[56,128]{1,0:T(8,128)S(1)} %get-tuple-element.56), channel_id=1, source_target_pairs={{0,3},{1,0},{2,1},{3,2},{4,7},{5,4},{6,5},{7,6},{8,11},{9,8},{10,9... | collective-permute-start | bytes 86024 | tf_op jit(solution)/shard_map/ppermute | solution.py:737
  35.6 4.1 %collective-permute-start.10 = (f32[40,128]{1,0:T(8,128)S(1)}, f32[40,128]{1,0:T(8,128)S(1)}, u32[]{:S(2)}, u32[]{:S(2)}) collective-permute-start(f32[40,128]{1,0:T(8,128)S(1)} %get-tuple-element.54.f2), channel_id=1, source_target_pairs={{0,2},{1,3},{2,0},{3,1},{4,6},{5,7},{6,4},{7,5},{8,10},{9,11},{10,... | collective-permute-start | bytes 61448 | tf_op jit(solution)/shard_map/ppermute | solution.py:737
  39.9 6.2 %collective-permute-start.11 = (f32[240,128]{1,0:T(8,128)S(1)}, f32[240,128]{1,0:T(8,128)S(1)}, u32[]{:S(2)}, u32[]{:S(2)}) collective-permute-start(f32[240,128]{1,0:T(8,128)S(1)} %get-tuple-element.59.msg), channel_id=1, source_target_pairs={{0,4},{4,0},{8,12},{12,8},{16,20},{20,16},{24,28},{28,24},{32,36},... | collective-permute-start | bytes 368648 | tf_op jit(solution)/shard_map/ppermute | solution.py:741
  46.1 5.2 %collective-permute-start.12 = (f32[384,128]{1,0:T(8,128)S(1)}, f32[384,128]{1,0:T(8,128)S(1)}, u32[]{:S(2)}, u32[]{:S(2)}) collective-permute-start(f32[384,128]{1,0:T(8,128)S(1)} %shard_map.52), channel_id=1, source_target_pairs={{0,252},{4,8},{8,4},{12,16},{16,12},{20,24},{24,20},{28,32},{32,28... | collective-permute-start | bytes 589832 | tf_op jit(solution)/shard_map/ppermute | solution.py:746
  51.3 4.8 %collective-permute-start.13 = (f32[384,128]{1,0:T(8,128)S(1)}, f32[384,128]{1,0:T(8,128)S(1)}, u32[]{:S(2)}, u32[]{:S(2)}) collective-permute-start(f32[384,128]{1,0:T(8,128)S(1)} %collective-permute-done.12.near), channel_id=1, source_target_pairs={{0,4},{4,0},{8,12},{12,8},{16,20},{20,16},{24,28},{28,24},{32,36},... | collective-permute-start | bytes 589832 | tf_op jit(solution)/shard_map/ppermute | solution.py:741
  57.4 14.1 %all-to-all-start = ((f32[32,2,8,128]{3,2,1,0:T(8,128)}), f32[32,2,8,128]{3,2,1,0:T(8,128)S(1)}, u32[]{:S(2)}, u32[]{:S(2)}) async-start(f32[32,2,8,128]{3,2,1,0:T(8,128)} %shard_map.55), calls=%async_computation | async-start | bytes 524288 | tf_op jit(solution)/shard_map/all_to_all | solution.py:800
  61.3 8.2 %collective-permute-start.14 = (f32[32,128]{1,0:T(8,128)S(1)}, f32[32,128]{1,0:T(8,128)S(1)}, u32[]{:S(2)}, u32[]{:S(2)}) collective-permute-start(f32[32,128]{1,0:T(8,128)S(1)} %get-tuple-element.64), channel_id=1, source_target_pairs={{0,252},{4,8},{8,4},{12,16},{16,12},{20,24},{24,20},{28,32},{32,28... | collective-permute-start | bytes 49160 | tf_op jit(solution)/shard_map/ppermute | solution.py:746
  71.5 14.6 %copy-start = (f32[4,64,256]{2,1,0:T(8,128)S(1)}, f32[4,64,256]{2,1,0:T(8,128)}, u32[]{:S(2)}) copy-start(f32[4,64,256]{2,1,0:T(8,128)} %c3.1) | copy-start | bytes 786436
  71.5 14.6 %copy-start.1 = (f32[4,64,256]{2,1,0:T(8,128)S(1)}, f32[4,64,256]{2,1,0:T(8,128)}, u32[]{:S(2)}) copy-start(f32[4,64,256]{2,1,0:T(8,128)} %c2.1) | copy-start | bytes 786436
  71.5 14.6 %copy-start.2 = (f32[4,64,256]{2,1,0:T(8,128)S(1)}, f32[4,64,256]{2,1,0:T(8,128)}, u32[]{:S(2)}) copy-start(f32[4,64,256]{2,1,0:T(8,128)} %c1.1) | copy-start | bytes 786436
  71.5 14.6 %copy-start.3 = (f32[4,64,256]{2,1,0:T(8,128)S(1)}, f32[4,64,256]{2,1,0:T(8,128)}, u32[]{:S(2)}) copy-start(f32[4,64,256]{2,1,0:T(8,128)} %f.1) | copy-start | bytes 786436
  71.5 4.4 %collective-permute-start.15 = (f32[32,2,8,128]{3,2,1,0:T(8,128)S(1)}, f32[32,2,8,128]{3,2,1,0:T(8,128)S(1)}, u32[]{:S(2)}, u32[]{:S(2)}) collective-permute-start(f32[32,2,8,128]{3,2,1,0:T(8,128)S(1)} %all-to-all-done.mine), channel_id=1, source_target_pairs={{0,4},{4,0},{8,12},{12,8},{16,20},{20,16},{24,28},{28,24},{32,36},... | collective-permute-start | bytes 786440 | tf_op jit(solution)/shard_map/ppermute | solution.py:741
  74.7 3.2 %collective-permute-start.16 = (f32[32,128]{1,0:T(8,128)S(1)}, f32[32,128]{1,0:T(8,128)S(1)}, u32[]{:S(2)}, u32[]{:S(2)}) collective-permute-start(f32[32,128]{1,0:T(8,128)S(1)} %collective-permute-done.14.late), channel_id=1, source_target_pairs={{0,4},{4,0},{8,12},{12,8},{16,20},{20,16},{24,28},{28,24},{32,36},... | collective-permute-start | bytes 49160 | tf_op jit(solution)/shard_map/ppermute | solution.py:741
  78.2 3.5 %collective-permute-start.17 = (f32[2,32,128]{2,1,0:T(8,128)S(1)}, f32[2,32,128]{2,1,0:T(8,128)S(1)}, u32[]{:S(2)}, u32[]{:S(2)}) collective-permute-start(f32[2,32,128]{2,1,0:T(8,128)S(1)} %shard_map.57.e2), channel_id=1, source_target_pairs={{0,252},{4,8},{8,4},{12,16},{16,12},{20,24},{24,20},{28,32},{32,28... | collective-permute-start | bytes 98312 | tf_op jit(solution)/shard_map/ppermute | solution.py:746
  82.4 4.5 %collective-permute-start.18 = (f32[40,128]{1,0:T(8,128)S(1)}, f32[40,128]{1,0:T(8,128)S(1)}, u32[]{:S(2)}, u32[]{:S(2)}) collective-permute-start(f32[40,128]{1,0:T(8,128)S(1)} %get-tuple-element.73), channel_id=1, source_target_pairs={{0,4},{4,0},{8,12},{12,8},{16,20},{20,16},{24,28},{28,24},{32,36},... | collective-permute-start | bytes 61448 | tf_op jit(solution)/shard_map/ppermute | solution.py:741

commit v16 on v15

--- a/solution.py
+++ b/solution.py
@@ -253,7 +253,7 @@
     return SIG[0] + c1[q, here, :] + c1[q + 1, here, :] + k2 + h2 + k3 + roll(k3, -1, 1)
 
 
-def fine_pre_kernel(own, coef1, far_raw, sib_raw, far, sib, halo, u2, w1, out_far, out_sib, f, c1, c2, c3, g, f1, u1, res, scr):
+def fine_pre_kernel(own, coef1, far_raw, sib_raw, far, sib, u2, out_far, out_sib, f, c1, c2, c3, g, f1, u1, res, scr):
     below, above = sides(far, sib)
     below_raw, above_raw = sides(far_raw, sib_raw)
     for a, ref in enumerate((f, c1, c2, c3)):
@@ -263,13 +263,7 @@
         + [(a, ref, 5, above_raw, above) for a, ref in enumerate((f, c1, c2, c3))]
         + [(4, c1, 6, above_raw, above)]
     ):
-        ref[q, 0:8] = rest(slice(16 * a, 16 * a + 8))
-        ref[q, 8:72] = raw(a)
-        ref[q, 72:80] = rest(slice(16 * a + 8, 16 * a + 16))
-    for a, ref in enumerate((f, c1, c2, c3)):
-        halo[a] = ref[0]
-        halo[4 + a] = ref[5]
-    halo[8] = c1[6]
+        halo_plane(ref, q, a, raw, rest)
     u1[0] = below(slice(80, 160))
     u1[7] = above(slice(80, 160))
 
@@ -312,14 +306,9 @@
     coarse = 0.5 * pair_rows(mul(sums, both), scr)
     f1[0] = coarse[:40]
     f1[1] = coarse[40:]
-    for a in range(3):
-        for p in range(2):
-            w1[6 * a + p] = below(*block(2 * a + p))
-            w1[6 * a + 2 + p] = coef1[2 * a + p]
-            w1[6 * a + 4 + p] = above(*block(2 * a + p))
     for p in range(2):
-        k = p + 2
-        inverse = 1.0 / diagonal(SIG[1], w1[k], w1[k + 1], w1[6 + k], w1[12 + k])
+        face = coef1[1] if p == 0 else above(*block(0))
+        inverse = 1.0 / diagonal(SIG[1], coef1[p], face, coef1[2 + p], coef1[4 + p])
         for out in (out_far, out_sib):
             out[p] = f1[p]
             out[2 + p] = inverse
@@ -331,7 +320,24 @@
         out[7] = u2[plane, 40:80, 128:256]
 
 
-def coarse_coef_kernel(w1, out, scr):
+def halo_plane(out, k, a, raw, rest):
+    out[k, 0:8] = rest(slice(16 * a, 16 * a + 8))
+    out[k, 8:72] = raw(a)
+    out[k, 72:80] = rest(slice(16 * a + 8, 16 * a + 16))
+
+
+def coarse_coef_kernel(coef1, far_raw, sib_raw, far, sib, w1, halo, out, scr):
+    below, above = sides(far, sib)
+    below_raw, above_raw = sides(far_raw, sib_raw)
+    for a in range(4):
+        halo_plane(halo, a, a, below_raw, below)
+        halo_plane(halo, 4 + a, a, above_raw, above)
+    halo_plane(halo, 8, 4, above_raw, above)
+    for a in range(3):
+        for p in range(2):
+            w1[6 * a + p] = below(*block(2 * a + p))
+            w1[6 * a + 2 + p] = coef1[2 * a + p]
+            w1[6 * a + 4 + p] = above(*block(2 * a + p))
     k1 = jnp.concatenate([w1[2], w1[4]], axis=0)
     k2, k3 = w1[8] + w1[9], w1[14] + w1[15]
     both, alone = pairs_of_lanes(128, 64), pairs_of_lanes(128, 64, even=True)
@@ -415,13 +421,14 @@
 
 
 def coarse_swap_kernel(own, msg, sib, w1, out):
-    out[0:160] = msg[0:160]
-    out[160:192] = sib[0:32] * sib[32:64] * (1.0 / THETA)
-    out[192:224] = two_blocks(own[2])
-    out[224:304] = msg[160:240]
+    out[0:32] = msg[0:32]
+    out[32:128] = msg[64:160]
+    out[128:160] = sib[0:32] * sib[32:64] * (1.0 / THETA)
+    out[160:192] = two_blocks(own[2])
+    out[192:272] = msg[160:240]
     par = lax.rem(lax.axis_index("wide"), 2)
-    out[304:344] = sib[pl.ds(pl.multiple_of(160 + 40 * par, 8), 40), :]
-    out[344:384] = w1[4]
+    out[272:312] = sib[pl.ds(pl.multiple_of(160 + 40 * par, 8), 40), :]
+    out[312:352] = w1[4]
 
 
 def coarse_pre_kernel(own, msg, sib, near, other, w, u2, late, fine, u1):
@@ -429,7 +436,7 @@
         fine[p] = sib[160 + 40 * p : 200 + 40 * p]
         fine[2 + p] = msg[160 + 40 * p : 200 + 40 * p]
     for p in range(4):
-        fine[4 + p] = near[224 + 40 * p : 264 + 40 * p]
+        fine[4 + p] = near[192 + 40 * p : 232 + 40 * p]
     odd = lax.rem(lax.axis_index("wide"), 2) == 1
 
     def below(k):
@@ -440,15 +447,18 @@
         here = slice(32 * k, 32 * k + 32)
         return both_halves(jnp.where(odd, near[here], other[here]))
 
-    for a, (base, plane) in enumerate(((0, 0), (4, 5), (8, 1), (13, 3), (17, 4))):
+    for a, (base, plane, slot) in enumerate(((0, 0, 0), (4, 5, None), (8, 1, 1), (13, 3, 2), (17, 4, 3))):
         mine, theirs = own[plane], both_halves(sib[32 * a : 32 * a + 32])
-        w[base] = below(a)
         w[base + 1] = jnp.where(odd, theirs, mine)
         w[base + 2] = jnp.where(odd, mine, theirs)
-        w[base + 3] = above(a)
-    w[12] = above(6)
-    u1[0] = below(5)
-    u1[5] = above(5)
+        if slot is not None:
+            w[base] = below(slot)
+            w[base + 3] = above(slot)
+    w[12] = above(5)
+    u1[0] = below(4)
+    u1[5] = above(4)
+    for k in (0, 3):
+        w[4 + k] = 1.0 / diagonal(SIG[2], w[8 + k], w[9 + k], w[13 + k], w[17 + k])
     for k in range(4):
         u1[k + 1] = w[k] * w[4 + k] * (1.0 / THETA)
     for k in range(4):
@@ -456,7 +466,7 @@
     late[...] = two_blocks(jnp.where(odd, u2[1], u2[2]))
 
 
-def coarse_send_kernel(w, u2, tiles, send, scr):
+def coarse_send_kernel(w, u2, tiles, send, scr, stack, sems):
     odd = lax.rem(lax.axis_index("wide"), 2) == 1
     total = 0.0
     for k in (1, 2):
@@ -466,9 +476,16 @@
     scr[...] = 0.5 * mul(total, pairs_of_lanes(128, 32))
     first = jnp.where(odd, tiles[1], tile_of(scr))
     second = jnp.where(odd, tiles[2], tiles[0])
-    for k in range(send.shape[0]):
-        send[k, 0] = first
-        send[k, 1] = second
+    share = stack.shape[0]
+    for k in range(share):
+        stack[k, 0] = first
+        stack[k, 1] = second
+    copies = []
+    for k in range(4):
+        copies.append(pltpu.make_async_copy(stack, send.at[pl.ds(share * k, share)], sems.at[k]))
+        copies[k].start()
+    for copy in copies:
+        copy.wait()
 
 
 def packed_sum(below, x, above, c1, h1, c2, c3, width, blocks):
@@ -769,14 +786,16 @@
     far, sib = across(far), sibling(sib)
 
     windows = [(6,) + big, (7,) + big, (6,) + big, (6,) + big]
-    halo, u2, w1, out_far, out_sib = call(
+    u2, out_far, out_sib = call(
         fine_pre_kernel,
-        [(9,) + big, (6,) + big, (18, 40, 128), (8, 40, 128), (8, 40, 128)],
+        [(6,) + big, (8, 40, 128), (8, 40, 128)],
         windows + [(6,) + big, (2, 40, 128), (8,) + big, (4,) + big, (160, 128)],
         limit=6,
     )(own, coef1, far_raw, sib_raw, far, sib)
     far1, sib1 = across(out_far), sibling(out_sib)
-    (coefs,) = call(coarse_coef_kernel, [(32, 128)], [(80, 128)])(w1)
+    w1, halo, coefs = call(
+        coarse_coef_kernel, [(18, 40, 128), (9,) + big, (32, 128)], [(80, 128)]
+    )(coef1, far_raw, sib_raw, far, sib)
 
     six = (6, 40, 128)
     f1w, g1w, u2m, f2, up, down, outer = call(
@@ -786,7 +805,7 @@
 
     own2, msg = call(coarse_start_kernel, [(6, 64, 128), (240, 128)])(f2, low, high, far, u2m)
     sib = sibling(msg)
-    (swap,) = call(coarse_swap_kernel, [(384, 128)])(own2, msg, sib, w1)
+    (swap,) = call(coarse_swap_kernel, [(352, 128)])(own2, msg, sib, w1)
     near = across(swap)
     (tiles,) = call(coarse_tiles_kernel, [(3, 8, 128)], [(64, 128)])(msg, sib)
     near, tiles = lax.optimization_barrier((near, tiles))
@@ -794,7 +813,12 @@
     w2, u2w, late, fine1 = call(
         coarse_pre_kernel, [(21, 64, 128), (4, 64, 128), (32, 128), (8, 40, 128)], [(6, 64, 128)]
     )(own2, msg, sib, near, other)
-    (send,) = call(coarse_send_kernel, [(n3, 2, 8, 128)], [(64, 128)])(w2, u2w, tiles)
+    (send,) = call(
+        coarse_send_kernel,
+        [(n3, 2, 8, 128)],
+        [(64, 128), (n3 // 4, 2, 8, 128), pltpu.SemaphoreType.DMA((4,))],
+        out_places={0: pltpu.HBM},
+    )(w2, u2w, tiles)
     late = across(late)
     cores = [[k for k in range(wide) if k % 2 == c] for c in range(2)]
     parts = lax.all_to_all(send, "wide", split_axis=0, concat_axis=0, tiled=True, axis_index_groups=cores)

time: 89.5 us -> 89.2 us (level)
  no operation moved by 1% of the time
where the time goes in v16:
time: 89.2 us; the launch traced here: 89 us
  starting transfers between devices  43.5 us (49%)
  waiting for transfers between devices  31.1 us (35%)
  Pallas kernels  12.7 us (14%)
  other arithmetic  1.35 us (2%)
    ppermute x8, starting transfers between devices, sibling(): lax.ppermute(x, 'wide', [(i, i ^ 1) for i in range(lax.axis_size('wide'))])  26.2 us
    ppermute x6, waiting for transfers between devices, across(): lax.ppermute(x, 'wide', [(i, (i + 1 if i % 2 else i - 1) % count) for i i...  20.8 us
    pallas_call x14, Pallas kernels, run(): pl.pallas_call(kernel, out_shape=[jax.ShapeDtypeStruct(s, F32) for s in o...  12.7 us
    ppermute x5, starting transfers between devices, shift(): return lax.ppermute(x, axis, [(i, (i + by) % count) for i in range(count)])  6.83 us
    ppermute x6, starting transfers between devices, across(): lax.ppermute(x, 'wide', [(i, (i + 1 if i % 2 else i - 1) % count) for i i...  6.65 us
    ppermute x8, waiting for transfers between devices, sibling(): lax.ppermute(x, 'wide', [(i, i ^ 1) for i in range(lax.axis_size('wide'))])  4.53 us
    all_to_all x1, starting transfers between devices, body(): lax.all_to_all(send, 'wide', split_axis=0, concat_axis=0, tiled=True, axi...  3.88 us
    ppermute x5, waiting for transfers between devices, shift(): return lax.ppermute(x, axis, [(i, (i + by) % count) for i in range(count)])  3.8 us
  transfers between devices with their start and end apart: 20, of which 12 were waited for; matrix products, arithmetic and copies ran while one was open for 2% of the time, Pallas kernels for 3%

profile of v16, /device:TPU:1, one launch (start us, length us, event | category | flops | bytes accessed | tf_op | source)
XLA Modules:
  0.0 89.0 jit_solution(1827032748878579931)
XLA Ops:
  0.0 2.2 %shard_map.46 = (f32[16,8,256]{2,1,0:T(8,128)}, f32[16,8,256]{2,1,0:T(8,128)}, f32[5,64,256]{2,1,0:T(8,128)}, f32[5,64,256]{2,1,0:T(8,128)}) custom-call(f32[4,64,256]{2,1,0:T(8,128)} %f.1, f32[4,64,256]{2,1,0:T(8,128)} %c1.1, f32[4,64,256]{2,1,0:T(8,128)} %c2.1, f32[4,64,256]{2,1,0:T(8,128)} %c3.1), custom_call_target="tpu_custom_call" | custom-call | tf_op jit(solution)/shard_map/pallas_call | solution.py:136
  2.2 2.2 %collective-permute-start = (f32[16,8,256]{2,1,0:T(8,128)}, f32[16,8,256]{2,1,0:T(8,128)S(1)}, u32[]{:S(2)}, u32[]{:S(2)}) collective-permute-start(f32[16,8,256]{2,1,0:T(8,128)} %get-tuple-element.44), channel_id=1, source_target_pairs={{0,1},{1,2},{2,3},{3,0},{4,5},{5,6},{6,7},{7,4},{8,9},{9,10},{10,1... | collective-permute-start | bytes 393224 | tf_op jit(solution)/shard_map/ppermute | solution.py:754
  4.4 1.5 %collective-permute-start.1 = (f32[16,8,256]{2,1,0:T(8,128)}, f32[16,8,256]{2,1,0:T(8,128)S(1)}, u32[]{:S(2)}, u32[]{:S(2)}) collective-permute-start(f32[16,8,256]{2,1,0:T(8,128)} %get-tuple-element.45), channel_id=1, source_target_pairs={{0,3},{1,0},{2,1},{3,2},{4,7},{5,4},{6,5},{7,6},{8,11},{9,8},{10,9... | collective-permute-start | bytes 393224 | tf_op jit(solution)/shard_map/ppermute | solution.py:754
  5.9 2.6 %collective-permute-start.2 = (f32[5,64,256]{2,1,0:T(8,128)}, f32[5,64,256]{2,1,0:T(8,128)S(1)}, u32[]{:S(2)}, u32[]{:S(2)}) collective-permute-start(f32[5,64,256]{2,1,0:T(8,128)} %get-tuple-element.48), channel_id=1, source_target_pairs={{0,252},{4,8},{8,4},{12,16},{16,12},{20,24},{24,20},{28,32},{32,28... | collective-permute-start | bytes 983048 | tf_op jit(solution)/shard_map/ppermute | solution.py:763
  8.5 5.6 %collective-permute-start.3 = (f32[5,64,256]{2,1,0:T(8,128)}, f32[5,64,256]{2,1,0:T(8,128)S(1)}, u32[]{:S(2)}, u32[]{:S(2)}) collective-permute-start(f32[5,64,256]{2,1,0:T(8,128)} %get-tuple-element.49), channel_id=1, source_target_pairs={{0,4},{4,0},{8,12},{12,8},{16,20},{20,16},{24,28},{28,24},{32,36},... | collective-permute-start | bytes 983048 | tf_op jit(solution)/shard_map/ppermute | solution.py:758
  14.1 1.3 %pad_maximum_fusion.inner = f32[16,64,256]{2,1,0:T(8,128)S(1)} fusion(f32[4,64,256]{2,1,0:T(8,128)} %c3.1, f32[4,64,256]{2,1,0:T(8,128)} %c2.1, f32[4,64,256]{2,1,0:T(8,128)} %c1.1, f32[4,64,256]{2,1,0:T(8,128)} %f.1), kind=kLoop, calls=%fused_computation | loop fusion | flops 786432 | bytes 2097152 | tf_op jit(solution)/shard_map/concatenate | solution.py:785
  15.9 1.8 %collective-permute-start.5 = (f32[280,256]{1,0:T(8,128)S(1)}, f32[280,256]{1,0:T(8,128)S(1)}, u32[]{:S(2)}, u32[]{:S(2)}) collective-permute-start(f32[280,256]{1,0:T(8,128)S(1)} %get-tuple-element.51), channel_id=1, source_target_pairs={{0,4},{4,0},{8,12},{12,8},{16,20},{20,16},{24,28},{28,24},{32,36},... | collective-permute-start | bytes 860168 | tf_op jit(solution)/shard_map/ppermute | solution.py:758
  17.7 4.5 %collective-permute-done.4.far = f32[280,256]{1,0:T(8,128)S(1)} collective-permute-done((f32[280,256]{1,0:T(8,128)S(1)}, f32[280,256]{1,0:T(8,128)S(1)}, u32[]{:S(2)}, u32[]{:S(2)}) %collective-permute-start.4) | collective-permute-done | bytes 286752 | tf_op jit(solution)/shard_map/ppermute | solution.py:763
  22.3 2.3 %shard_map.48 = (f32[6,80,256]{2,1,0:T(8,128)S(1)}, f32[8,40,128]{2,1,0:T(8,128)S(1)}, f32[8,40,128]{2,1,0:T(8,128)S(1)}) custom-call(f32[16,80,256]{2,1,0:T(8,128)S(1)} %get-tuple-element.46.own, f32[6,40,128]{2,1,0:T(8,128)S(1)} %get-tuple-element.47.coef1, f32[5,64,256]{2,1,0:T(8,128)S(1)} %collective-permute-done.2.far_raw, ...), custom_call_target="tpu_custom_call" | custom-call | tf_op jit(solution)/shard_map/pallas_call | solution.py:136
  24.6 3.1 %collective-permute-start.7 = (f32[8,40,128]{2,1,0:T(8,128)S(1)}, f32[8,40,128]{2,1,0:T(8,128)S(1)}, u32[]{:S(2)}, u32[]{:S(2)}) collective-permute-start(f32[8,40,128]{2,1,0:T(8,128)S(1)} %get-tuple-element.53), channel_id=1, source_target_pairs={{0,4},{4,0},{8,12},{12,8},{16,20},{20,16},{24,28},{28,24},{32,36},... | collective-permute-start | bytes 491528 | tf_op jit(solution)/shard_map/ppermute | solution.py:758
  28.0 0.7 collective-permute-done.7.sib
  28.7 3.7 %collective-permute-done.6.far = f32[8,40,128]{2,1,0:T(8,128)S(1)} collective-permute-done((f32[8,40,128]{2,1,0:T(8,128)S(1)}, f32[8,40,128]{2,1,0:T(8,128)S(1)}, u32[]{:S(2)}, u32[]{:S(2)}) %collective-permute-start.6) | collective-permute-done | bytes 163872 | tf_op jit(solution)/shard_map/ppermute | solution.py:763
  32.9 2.7 %collective-permute-start.9 = (f32[56,128]{1,0:T(8,128)S(1)}, f32[56,128]{1,0:T(8,128)S(1)}, u32[]{:S(2)}, u32[]{:S(2)}) collective-permute-start(f32[56,128]{1,0:T(8,128)S(1)} %get-tuple-element.58), channel_id=1, source_target_pairs={{0,3},{1,0},{2,1},{3,2},{4,7},{5,4},{6,5},{7,6},{8,11},{9,8},{10,9... | collective-permute-start | bytes 86024 | tf_op jit(solution)/shard_map/ppermute | solution.py:754
  35.9 3.8 %collective-permute-done.10.far = f32[40,128]{1,0:T(8,128)S(1)} collective-permute-done((f32[40,128]{1,0:T(8,128)S(1)}, f32[40,128]{1,0:T(8,128)S(1)}, u32[]{:S(2)}, u32[]{:S(2)}) %collective-permute-start.10) | collective-permute-done | bytes 20512 | tf_op jit(solution)/shard_map/ppermute | solution.py:754
  39.9 5.2 %collective-permute-start.11 = (f32[240,128]{1,0:T(8,128)S(1)}, f32[240,128]{1,0:T(8,128)S(1)}, u32[]{:S(2)}, u32[]{:S(2)}) collective-permute-start(f32[240,128]{1,0:T(8,128)S(1)} %get-tuple-element.61.msg), channel_id=1, source_target_pairs={{0,4},{4,0},{8,12},{12,8},{16,20},{20,16},{24,28},{28,24},{32,36},... | collective-permute-start | bytes 368648 | tf_op jit(solution)/shard_map/ppermute | solution.py:758
  45.1 1.0 %collective-permute-done.11.sib = f32[240,128]{1,0:T(8,128)S(1)} collective-permute-done((f32[240,128]{1,0:T(8,128)S(1)}, f32[240,128]{1,0:T(8,128)S(1)}, u32[]{:S(2)}, u32[]{:S(2)}) %collective-permute-start.11) | collective-permute-done | bytes 122912 | tf_op jit(solution)/shard_map/ppermute | solution.py:758
  46.5 4.6 %collective-permute-done.12.near = f32[352,128]{1,0:T(8,128)S(1)} collective-permute-done((f32[352,128]{1,0:T(8,128)S(1)}, f32[352,128]{1,0:T(8,128)S(1)}, u32[]{:S(2)}, u32[]{:S(2)}) %collective-permute-start.12) | collective-permute-done | bytes 180256 | tf_op jit(solution)/shard_map/ppermute | solution.py:763
  51.1 3.7 %collective-permute-start.13 = (f32[352,128]{1,0:T(8,128)S(1)}, f32[352,128]{1,0:T(8,128)S(1)}, u32[]{:S(2)}, u32[]{:S(2)}) collective-permute-start(f32[352,128]{1,0:T(8,128)S(1)} %collective-permute-done.12.near), channel_id=1, source_target_pairs={{0,4},{4,0},{8,12},{12,8},{16,20},{20,16},{24,28},{28,24},{32,36},... | collective-permute-start | bytes 540680 | tf_op jit(solution)/shard_map/ppermute | solution.py:758
  54.8 1.0 %collective-permute-done.13.other = f32[352,128]{1,0:T(8,128)S(1)} collective-permute-done((f32[352,128]{1,0:T(8,128)S(1)}, f32[352,128]{1,0:T(8,128)S(1)}, u32[]{:S(2)}, u32[]{:S(2)}) %collective-permute-start.13) | collective-permute-done | bytes 180256 | tf_op jit(solution)/shard_map/ppermute | solution.py:758
  56.3 1.0 %shard_map.55 = f32[32,2,8,128]{3,2,1,0:T(8,128)} custom-call(f32[21,64,128]{2,1,0:T(8,128)S(1)} %get-tuple-element.63.w.win, f32[4,64,128]{2,1,0:T(8,128)S(1)} %get-tuple-element.64.u2, f32[3,8,128]{2,1,0:T(8,128)S(1)} %shard_map.53.tiles), custom_call_target="tpu_custom_call" | custom-call | tf_op jit(solution)/shard_map/pallas_call | solution.py:136
  57.3 3.9 %all-to-all-start = ((f32[32,2,8,128]{3,2,1,0:T(8,128)}), f32[32,2,8,128]{3,2,1,0:T(8,128)S(1)}, u32[]{:S(2)}, u32[]{:S(2)}) async-start(f32[32,2,8,128]{3,2,1,0:T(8,128)} %shard_map.55), calls=%async_computation | async-start | bytes 524288 | tf_op jit(solution)/shard_map/all_to_all | solution.py:824
  61.2 1.9 %collective-permute-start.14 = (f32[32,128]{1,0:T(8,128)S(1)}, f32[32,128]{1,0:T(8,128)S(1)}, u32[]{:S(2)}, u32[]{:S(2)}) collective-permute-start(f32[32,128]{1,0:T(8,128)S(1)} %get-tuple-element.66), channel_id=1, source_target_pairs={{0,252},{4,8},{8,4},{12,16},{16,12},{20,24},{24,20},{28,32},{32,28... | collective-permute-start | bytes 49160 | tf_op jit(solution)/shard_map/ppermute | solution.py:763
  63.1 6.3 %collective-permute-done.14.late = f32[32,128]{1,0:T(8,128)S(1)} collective-permute-done((f32[32,128]{1,0:T(8,128)S(1)}, f32[32,128]{1,0:T(8,128)S(1)}, u32[]{:S(2)}, u32[]{:S(2)}) %collective-permute-start.14) | collective-permute-done | bytes 16416 | tf_op jit(solution)/shard_map/ppermute | solution.py:763
  69.4 2.0 %all-to-all-done.mine = f32[32,2,8,128]{3,2,1,0:T(8,128)S(1)} async-done(((f32[32,2,8,128]{3,2,1,0:T(8,128)}), f32[32,2,8,128]{3,2,1,0:T(8,128)S(1)}, u32[]{:S(2)}, u32[]{:S(2)}) %all-to-all-start) | async-done | bytes 262176 | tf_op jit(solution)/shard_map/all_to_all | solution.py:824
  71.4 3.0 %collective-permute-start.15 = (f32[32,2,8,128]{3,2,1,0:T(8,128)S(1)}, f32[32,2,8,128]{3,2,1,0:T(8,128)S(1)}, u32[]{:S(2)}, u32[]{:S(2)}) collective-permute-start(f32[32,2,8,128]{3,2,1,0:T(8,128)S(1)} %all-to-all-done.mine), channel_id=1, source_target_pairs={{0,4},{4,0},{8,12},{12,8},{16,20},{20,16},{24,28},{28,24},{32,36},... | collective-permute-start | bytes 786440 | tf_op jit(solution)/shard_map/ppermute | solution.py:758
  74.5 1.1 %collective-permute-done.15.theirs = f32[32,2,8,128]{3,2,1,0:T(8,128)S(1)} collective-permute-done((f32[32,2,8,128]{3,2,1,0:T(8,128)S(1)}, f32[32,2,8,128]{3,2,1,0:T(8,128)S(1)}, u32[]{:S(2)}, u32[]{:S(2)}) %collective-permute-start.15) | collective-permute-done | bytes 262176 | tf_op jit(solution)/shard_map/ppermute | solution.py:758
  75.6 2.0 %shard_map.56.e2 = f32[192,128]{1,0:T(8,128)S(1)} custom-call(f32[32,2,8,128]{3,2,1,0:T(8,128)S(1)} %all-to-all-done.mine, f32[32,2,8,128]{3,2,1,0:T(8,128)S(1)} %collective-permute-done.15.theirs), custom_call_target="tpu_custom_call" | custom-call | tf_op jit(solution)/shard_map/pallas_call | solution.py:136
  77.9 1.9 %collective-permute-start.17 = (f32[2,32,128]{2,1,0:T(8,128)S(1)}, f32[2,32,128]{2,1,0:T(8,128)S(1)}, u32[]{:S(2)}, u32[]{:S(2)}) collective-permute-start(f32[2,32,128]{2,1,0:T(8,128)S(1)} %shard_map.57.e2), channel_id=1, source_target_pairs={{0,252},{4,8},{8,4},{12,16},{16,12},{20,24},{24,20},{28,32},{32,28... | collective-permute-start | bytes 98312 | tf_op jit(solution)/shard_map/ppermute | solution.py:763
  79.8 1.6 %collective-permute-done.17.far = f32[2,32,128]{2,1,0:T(8,128)S(1)} collective-permute-done((f32[2,32,128]{2,1,0:T(8,128)S(1)}, f32[2,32,128]{2,1,0:T(8,128)S(1)}, u32[]{:S(2)}, u32[]{:S(2)}) %collective-permute-start.17) | collective-permute-done | bytes 32800 | tf_op jit(solution)/shard_map/ppermute | solution.py:763
  82.1 3.7 %collective-permute-start.18 = (f32[40,128]{1,0:T(8,128)S(1)}, f32[40,128]{1,0:T(8,128)S(1)}, u32[]{:S(2)}, u32[]{:S(2)}) collective-permute-start(f32[40,128]{1,0:T(8,128)S(1)} %get-tuple-element.75), channel_id=1, source_target_pairs={{0,4},{4,0},{8,12},{12,8},{16,20},{20,16},{24,28},{28,24},{32,36},... | collective-permute-start | bytes 61448 | tf_op jit(solution)/shard_map/ppermute | solution.py:758
  85.9 0.7 collective-permute-done.18.other
  86.6 2.2 %shard_map.59 = f32[4,64,256]{2,1,0:T(8,128)} custom-call(f32[2,40,128]{2,1,0:T(8,128)S(1)} %get-tuple-element.73.e1, f32[40,128]{1,0:T(8,128)S(1)} %get-tuple-element.74.edge, f32[40,128]{1,0:T(8,128)S(1)} %collective-permute-done.18.other, f32[2,80,256]{2,1,0:T(8,128)S(1)} %get-tuple-element.76.outer, f32[16,64,256]{2,1,0:T(8,128)S(1)} %pad_maximum_fusion.1.inner, ...), custom_call_target="tpu_custom_call" | custom-call | tf_op jit(solution)/shard_map/pallas_call | solution.py:136
  (32 shorter events, 3.8 us)
Async XLA Ops:
  2.2 13.2 %collective-permute-start = (f32[16,8,256]{2,1,0:T(8,128)}, f32[16,8,256]{2,1,0:T(8,128)S(1)}, u32[]{:S(2)}, u32[]{:S(2)}) collective-permute-start(f32[16,8,256]{2,1,0:T(8,128)} %get-tuple-element.44), channel_id=1, source_target_pairs={{0,1},{1,2},{2,3},{3,0},{4,5},{5,6},{6,7},{7,4},{8,9},{9,10},{10,1... | collective-permute-start | bytes 393224 | tf_op jit(solution)/shard_map/ppermute | solution.py:754
  4.4 11.0 %collective-permute-start.1 = (f32[16,8,256]{2,1,0:T(8,128)}, f32[16,8,256]{2,1,0:T(8,128)S(1)}, u32[]{:S(2)}, u32[]{:S(2)}) collective-permute-start(f32[16,8,256]{2,1,0:T(8,128)} %get-tuple-element.45), channel_id=1, source_target_pairs={{0,3},{1,0},{2,1},{3,2},{4,7},{5,4},{6,5},{7,6},{8,11},{9,8},{10,9... | collective-permute-start | bytes 393224 | tf_op jit(solution)/shard_map/ppermute | solution.py:754
  5.9 11.8 %collective-permute-start.2 = (f32[5,64,256]{2,1,0:T(8,128)}, f32[5,64,256]{2,1,0:T(8,128)S(1)}, u32[]{:S(2)}, u32[]{:S(2)}) collective-permute-start(f32[5,64,256]{2,1,0:T(8,128)} %get-tuple-element.48), channel_id=1, source_target_pairs={{0,252},{4,8},{8,4},{12,16},{16,12},{20,24},{24,20},{28,32},{32,28... | collective-permute-start | bytes 983048 | tf_op jit(solution)/shard_map/ppermute | solution.py:763
  8.5 9.2 %collective-permute-start.3 = (f32[5,64,256]{2,1,0:T(8,128)}, f32[5,64,256]{2,1,0:T(8,128)S(1)}, u32[]{:S(2)}, u32[]{:S(2)}) collective-permute-start(f32[5,64,256]{2,1,0:T(8,128)} %get-tuple-element.49), channel_id=1, source_target_pairs={{0,4},{4,0},{8,12},{12,8},{16,20},{20,16},{24,28},{28,24},{32,36},... | collective-permute-start | bytes 983048 | tf_op jit(solution)/shard_map/ppermute | solution.py:758
  15.8 6.4 %collective-permute-start.4 = (f32[280,256]{1,0:T(8,128)S(1)}, f32[280,256]{1,0:T(8,128)S(1)}, u32[]{:S(2)}, u32[]{:S(2)}) collective-permute-start(f32[280,256]{1,0:T(8,128)S(1)} %get-tuple-element.50), channel_id=1, source_target_pairs={{0,252},{4,8},{8,4},{12,16},{16,12},{20,24},{24,20},{28,32},{32,28... | collective-permute-start | bytes 860168 | tf_op jit(solution)/shard_map/ppermute | solution.py:763
  15.9 6.3 %collective-permute-start.5 = (f32[280,256]{1,0:T(8,128)S(1)}, f32[280,256]{1,0:T(8,128)S(1)}, u32[]{:S(2)}, u32[]{:S(2)}) collective-permute-start(f32[280,256]{1,0:T(8,128)S(1)} %get-tuple-element.51), channel_id=1, source_target_pairs={{0,4},{4,0},{8,12},{12,8},{16,20},{20,16},{24,28},{28,24},{32,36},... | collective-permute-start | bytes 860168 | tf_op jit(solution)/shard_map/ppermute | solution.py:758
  24.6 4.1 %collective-permute-start.7 = (f32[8,40,128]{2,1,0:T(8,128)S(1)}, f32[8,40,128]{2,1,0:T(8,128)S(1)}, u32[]{:S(2)}, u32[]{:S(2)}) collective-permute-start(f32[8,40,128]{2,1,0:T(8,128)S(1)} %get-tuple-element.53), channel_id=1, source_target_pairs={{0,4},{4,0},{8,12},{12,8},{16,20},{20,16},{24,28},{28,24},{32,36},... | collective-permute-start | bytes 491528 | tf_op jit(solution)/shard_map/ppermute | solution.py:758
  27.7 4.7 %collective-permute-start.6 = (f32[8,40,128]{2,1,0:T(8,128)S(1)}, f32[8,40,128]{2,1,0:T(8,128)S(1)}, u32[]{:S(2)}, u32[]{:S(2)}) collective-permute-start(f32[8,40,128]{2,1,0:T(8,128)S(1)} %get-tuple-element.52.own), channel_id=1, source_target_pairs={{0,252},{4,8},{8,4},{12,16},{16,12},{20,24},{24,20},{28,32},{32,28... | collective-permute-start | bytes 491528 | tf_op jit(solution)/shard_map/ppermute | solution.py:763
  32.8 6.9 %collective-permute-start.8 = (f32[56,128]{1,0:T(8,128)S(1)}, f32[56,128]{1,0:T(8,128)S(1)}, u32[]{:S(2)}, u32[]{:S(2)}) collective-permute-start(f32[56,128]{1,0:T(8,128)S(1)} %get-tuple-element.57), channel_id=1, source_target_pairs={{0,1},{1,2},{2,3},{3,0},{4,5},{5,6},{6,7},{7,4},{8,9},{9,10},{10,1... | collective-permute-start | bytes 86024 | tf_op jit(solution)/shard_map/ppermute | solution.py:754
  32.9 6.8 %collective-permute-start.9 = (f32[56,128]{1,0:T(8,128)S(1)}, f32[56,128]{1,0:T(8,128)S(1)}, u32[]{:S(2)}, u32[]{:S(2)}) collective-permute-start(f32[56,128]{1,0:T(8,128)S(1)} %get-tuple-element.58), channel_id=1, source_target_pairs={{0,3},{1,0},{2,1},{3,2},{4,7},{5,4},{6,5},{7,6},{8,11},{9,8},{10,9... | collective-permute-start | bytes 86024 | tf_op jit(solution)/shard_map/ppermute | solution.py:754
  35.5 4.1 %collective-permute-start.10 = (f32[40,128]{1,0:T(8,128)S(1)}, f32[40,128]{1,0:T(8,128)S(1)}, u32[]{:S(2)}, u32[]{:S(2)}) collective-permute-start(f32[40,128]{1,0:T(8,128)S(1)} %get-tuple-element.56.f2), channel_id=1, source_target_pairs={{0,2},{1,3},{2,0},{3,1},{4,6},{5,7},{6,4},{7,5},{8,10},{9,11},{10,... | collective-permute-start | bytes 61448 | tf_op jit(solution)/shard_map/ppermute | solution.py:754
  39.9 6.2 %collective-permute-start.11 = (f32[240,128]{1,0:T(8,128)S(1)}, f32[240,128]{1,0:T(8,128)S(1)}, u32[]{:S(2)}, u32[]{:S(2)}) collective-permute-start(f32[240,128]{1,0:T(8,128)S(1)} %get-tuple-element.61.msg), channel_id=1, source_target_pairs={{0,4},{4,0},{8,12},{12,8},{16,20},{20,16},{24,28},{28,24},{32,36},... | collective-permute-start | bytes 368648 | tf_op jit(solution)/shard_map/ppermute | solution.py:758
  46.1 5.0 %collective-permute-start.12 = (f32[352,128]{1,0:T(8,128)S(1)}, f32[352,128]{1,0:T(8,128)S(1)}, u32[]{:S(2)}, u32[]{:S(2)}) collective-permute-start(f32[352,128]{1,0:T(8,128)S(1)} %shard_map.52), channel_id=1, source_target_pairs={{0,252},{4,8},{8,4},{12,16},{16,12},{20,24},{24,20},{28,32},{32,28... | collective-permute-start | bytes 540680 | tf_op jit(solution)/shard_map/ppermute | solution.py:763
  51.1 4.7 %collective-permute-start.13 = (f32[352,128]{1,0:T(8,128)S(1)}, f32[352,128]{1,0:T(8,128)S(1)}, u32[]{:S(2)}, u32[]{:S(2)}) collective-permute-start(f32[352,128]{1,0:T(8,128)S(1)} %collective-permute-done.12.near), channel_id=1, source_target_pairs={{0,4},{4,0},{8,12},{12,8},{16,20},{20,16},{24,28},{28,24},{32,36},... | collective-permute-start | bytes 540680 | tf_op jit(solution)/shard_map/ppermute | solution.py:758
  57.3 14.1 %all-to-all-start = ((f32[32,2,8,128]{3,2,1,0:T(8,128)}), f32[32,2,8,128]{3,2,1,0:T(8,128)S(1)}, u32[]{:S(2)}, u32[]{:S(2)}) async-start(f32[32,2,8,128]{3,2,1,0:T(8,128)} %shard_map.55), calls=%async_computation | async-start | bytes 524288 | tf_op jit(solution)/shard_map/all_to_all | solution.py:824
  61.2 8.2 %collective-permute-start.14 = (f32[32,128]{1,0:T(8,128)S(1)}, f32[32,128]{1,0:T(8,128)S(1)}, u32[]{:S(2)}, u32[]{:S(2)}) collective-permute-start(f32[32,128]{1,0:T(8,128)S(1)} %get-tuple-element.66), channel_id=1, source_target_pairs={{0,252},{4,8},{8,4},{12,16},{16,12},{20,24},{24,20},{28,32},{32,28... | collective-permute-start | bytes 49160 | tf_op jit(solution)/shard_map/ppermute | solution.py:763
  71.4 14.4 %copy-start = (f32[4,64,256]{2,1,0:T(8,128)S(1)}, f32[4,64,256]{2,1,0:T(8,128)}, u32[]{:S(2)}) copy-start(f32[4,64,256]{2,1,0:T(8,128)} %c3.1) | copy-start | bytes 786436
  71.4 14.4 %copy-start.1 = (f32[4,64,256]{2,1,0:T(8,128)S(1)}, f32[4,64,256]{2,1,0:T(8,128)}, u32[]{:S(2)}) copy-start(f32[4,64,256]{2,1,0:T(8,128)} %c2.1) | copy-start | bytes 786436
  71.4 14.4 %copy-start.2 = (f32[4,64,256]{2,1,0:T(8,128)S(1)}, f32[4,64,256]{2,1,0:T(8,128)}, u32[]{:S(2)}) copy-start(f32[4,64,256]{2,1,0:T(8,128)} %c1.1) | copy-start | bytes 786436
  71.4 14.4 %copy-start.3 = (f32[4,64,256]{2,1,0:T(8,128)S(1)}, f32[4,64,256]{2,1,0:T(8,128)}, u32[]{:S(2)}) copy-start(f32[4,64,256]{2,1,0:T(8,128)} %f.1) | copy-start | bytes 786436
  71.4 4.2 %collective-permute-start.15 = (f32[32,2,8,128]{3,2,1,0:T(8,128)S(1)}, f32[32,2,8,128]{3,2,1,0:T(8,128)S(1)}, u32[]{:S(2)}, u32[]{:S(2)}) collective-permute-start(f32[32,2,8,128]{3,2,1,0:T(8,128)S(1)} %all-to-all-done.mine), channel_id=1, source_target_pairs={{0,4},{4,0},{8,12},{12,8},{16,20},{20,16},{24,28},{28,24},{32,36},... | collective-permute-start | bytes 786440 | tf_op jit(solution)/shard_map/ppermute | solution.py:758
  74.4 3.2 %collective-permute-start.16 = (f32[32,128]{1,0:T(8,128)S(1)}, f32[32,128]{1,0:T(8,128)S(1)}, u32[]{:S(2)}, u32[]{:S(2)}) collective-permute-start(f32[32,128]{1,0:T(8,128)S(1)} %collective-permute-done.14.late), channel_id=1, source_target_pairs={{0,4},{4,0},{8,12},{12,8},{16,20},{20,16},{24,28},{28,24},{32,36},... | collective-permute-start | bytes 49160 | tf_op jit(solution)/shard_map/ppermute | solution.py:758
  77.9 3.5 %collective-permute-start.17 = (f32[2,32,128]{2,1,0:T(8,128)S(1)}, f32[2,32,128]{2,1,0:T(8,128)S(1)}, u32[]{:S(2)}, u32[]{:S(2)}) collective-permute-start(f32[2,32,128]{2,1,0:T(8,128)S(1)} %shard_map.57.e2), channel_id=1, source_target_pairs={{0,252},{4,8},{8,4},{12,16},{16,12},{20,24},{24,20},{28,32},{32,28... | collective-permute-start | bytes 98312 | tf_op jit(solution)/shard_map/ppermute | solution.py:763
  82.1 4.5 %collective-permute-start.18 = (f32[40,128]{1,0:T(8,128)S(1)}, f32[40,128]{1,0:T(8,128)S(1)}, u32[]{:S(2)}, u32[]{:S(2)}) collective-permute-start(f32[40,128]{1,0:T(8,128)S(1)} %get-tuple-element.75), channel_id=1, source_target_pairs={{0,4},{4,0},{8,12},{12,8},{16,20},{20,16},{24,28},{28,24},{32,36},... | collective-permute-start | bytes 61448 | tf_op jit(solution)/shard_map/ppermute | solution.py:758

commit v17 on v16

--- a/solution.py
+++ b/solution.py
@@ -405,7 +405,7 @@
     for a in range(3):
         here = slice(64 + 32 * a, 96 + 32 * a)
         x = jnp.where(odd, sib[here], msg[here]) if a == 0 else msg[here] + sib[here]
-        scr[...] = 0.25 * mul(both_halves(x), pairs_of_lanes(128, 32, even=a == 2))
+        scr[0:64, :] = 0.25 * mul(both_halves(x), pairs_of_lanes(128, 32, even=a == 2))
         tiles[a] = tile_of(scr, a == 1)
 
 
@@ -466,26 +466,19 @@
     late[...] = two_blocks(jnp.where(odd, u2[1], u2[2]))
 
 
-def coarse_send_kernel(w, u2, tiles, send, scr, stack, sems):
+def coarse_send_kernel(w, u2, tiles, send, scr):
     odd = lax.rem(lax.axis_index("wide"), 2) == 1
     total = 0.0
     for k in (1, 2):
         args = (w[8 + k], w[9 + k], w[13 + k], w[17 + k])
         near = gather_sum(u2[k - 1], u2[k], u2[k + 1], *args)
         total = total + (w[k] + near - diagonal(SIG[2], *args) * u2[k])
-    scr[...] = 0.5 * mul(total, pairs_of_lanes(128, 32))
+    scr[0:64, :] = 0.5 * mul(total, pairs_of_lanes(128, 32))
     first = jnp.where(odd, tiles[1], tile_of(scr))
     second = jnp.where(odd, tiles[2], tiles[0])
-    share = stack.shape[0]
-    for k in range(share):
-        stack[k, 0] = first
-        stack[k, 1] = second
-    copies = []
-    for k in range(4):
-        copies.append(pltpu.make_async_copy(stack, send.at[pl.ds(share * k, share)], sems.at[k]))
-        copies[k].start()
-    for copy in copies:
-        copy.wait()
+    for k in range(send.shape[0]):
+        send[k, 0] = first
+        send[k, 1] = second
 
 
 def packed_sum(below, x, above, c1, h1, c2, c3, width, blocks):
@@ -547,11 +540,8 @@
     n3, n4 = f3.shape[0], f4.shape[0]
 
     def loop(body):
-        def step(c, carry):
-            body(pl.multiple_of(c * STEP, STEP))
-            return carry
-
-        lax.fori_loop(0, n3 // STEP, step, 0)
+        for j in range(0, n3, STEP):
+            body(j)
 
     odd = lax.rem(lax.axis_index("wide"), 2) == 1
 
@@ -781,7 +771,7 @@
     low0, high0 = shift(up, "narrow", 1), shift(down, "narrow", -1)
 
     own, coef1, far, sib = call(
-        pad_kernel, [(16,) + big, (6, 40, 128), (280, 256), (280, 256)], [(2,) + big, (160, 128)]
+        pad_kernel, [(16,) + big, (6, 40, 128), (280, 256), (280, 256)], [(2,) + big, (168, 128)]
     )(jnp.concatenate(inputs, axis=0), low0, high0)
     far, sib = across(far), sibling(sib)
 
@@ -789,17 +779,17 @@
     u2, out_far, out_sib = call(
         fine_pre_kernel,
         [(6,) + big, (8, 40, 128), (8, 40, 128)],
-        windows + [(6,) + big, (2, 40, 128), (8,) + big, (4,) + big, (160, 128)],
+        windows + [(6,) + big, (2, 40, 128), (8,) + big, (4,) + big, (168, 128)],
         limit=6,
     )(own, coef1, far_raw, sib_raw, far, sib)
     far1, sib1 = across(out_far), sibling(out_sib)
     w1, halo, coefs = call(
-        coarse_coef_kernel, [(18, 40, 128), (9,) + big, (32, 128)], [(80, 128)]
+        coarse_coef_kernel, [(18, 40, 128), (9,) + big, (32, 128)], [(88, 128)]
     )(coef1, far_raw, sib_raw, far, sib)
 
     six = (6, 40, 128)
     f1w, g1w, u2m, f2, up, down, outer = call(
-        middle_pre_kernel, [six, six, six, (40, 128), (56, 128), (56, 128), (2,) + big], [six, (40, 128)]
+        middle_pre_kernel, [six, six, six, (40, 128), (56, 128), (56, 128), (2,) + big], [six, (48, 128)]
     )(out_far, far1, sib1, w1, coefs)
     low, high, far = shift(up, "narrow", 1), shift(down, "narrow", -1), shift(f2, "narrow", 2)
 
@@ -807,18 +797,13 @@
     sib = sibling(msg)
     (swap,) = call(coarse_swap_kernel, [(352, 128)])(own2, msg, sib, w1)
     near = across(swap)
-    (tiles,) = call(coarse_tiles_kernel, [(3, 8, 128)], [(64, 128)])(msg, sib)
+    (tiles,) = call(coarse_tiles_kernel, [(3, 8, 128)], [(72, 128)])(msg, sib)
     near, tiles = lax.optimization_barrier((near, tiles))
     other = sibling(near)
     w2, u2w, late, fine1 = call(
         coarse_pre_kernel, [(21, 64, 128), (4, 64, 128), (32, 128), (8, 40, 128)], [(6, 64, 128)]
     )(own2, msg, sib, near, other)
-    (send,) = call(
-        coarse_send_kernel,
-        [(n3, 2, 8, 128)],
-        [(64, 128), (n3 // 4, 2, 8, 128), pltpu.SemaphoreType.DMA((4,))],
-        out_places={0: pltpu.HBM},
-    )(w2, u2w, tiles)
+    (send,) = call(coarse_send_kernel, [(n3, 2, 8, 128)], [(72, 128)])(w2, u2w, tiles)
     late = across(late)
     cores = [[k for k in range(wide) if k % 2 == c] for c in range(2)]
     parts = lax.all_to_all(send, "wide", split_axis=0, concat_axis=0, tiled=True, axis_index_groups=cores)
@@ -828,7 +813,7 @@
     three, four = (n3, 8, 128), (n4, 8, 128)
     (fine2,) = call(
         bottom_kernel,
-        [(192, 128)],
+        [(200, 128)],
         [three, (n3 + 1, 8, 128), three, three, three, three, (n3 + 2, 8, 128), (n3 + 2, 8, 128), four, four]
         + [(n4 + 1, 8, 128), four, four, four, (n4 + 2, 8, 128), (n4 + 2, 8, 128), four, (32, 128)],
     )(parts, theirs)
@@ -846,7 +831,7 @@
     (out,) = call(
         fine_post_kernel,
         [(4, 64, 256)],
-        windows + [(6,) + big, (8,) + big, (8,) + big, (320, 128), (4, 64, 256), pltpu.SemaphoreType.DMA((4,))],
+        windows + [(6,) + big, (8,) + big, (8,) + big, (328, 128), (4, 64, 256), pltpu.SemaphoreType.DMA((4,))],
         out_places={0: pltpu.HBM},
         limit=6,
     )(e1, edge, other1, outer, jnp.concatenate(again, axis=0), low0, high0, halo, u2)

time: 89.2 us -> 89.2 us (level)
  no operation moved by 1% of the time
where the time goes in v17:
time: 89.2 us; the launch traced here: 89 us
  starting transfers between devices  43.5 us (49%)
  waiting for transfers between devices  31.1 us (35%)
  Pallas kernels  12.7 us (14%)
  other arithmetic  1.35 us (2%)
    ppermute x8, starting transfers between devices, sibling(): lax.ppermute(x, 'wide', [(i, i ^ 1) for i in range(lax.axis_size('wide'))])  26.2 us
    ppermute x6, waiting for transfers between devices, across(): lax.ppermute(x, 'wide', [(i, (i + 1 if i % 2 else i - 1) % count) for i i...  20.8 us
    pallas_call x14, Pallas kernels, run(): pl.pallas_call(kernel, out_shape=[jax.ShapeDtypeStruct(s, F32) for s in o...  12.7 us
    ppermute x5, starting transfers between devices, shift(): return lax.ppermute(x, axis, [(i, (i + by) % count) for i in range(count)])  6.82 us
    ppermute x6, starting transfers between devices, across(): lax.ppermute(x, 'wide', [(i, (i + 1 if i % 2 else i - 1) % count) for i i...  6.65 us
    ppermute x8, waiting for transfers between devices, sibling(): lax.ppermute(x, 'wide', [(i, i ^ 1) for i in range(lax.axis_size('wide'))])  4.53 us
    all_to_all x1, starting transfers between devices, body(): lax.all_to_all(send, 'wide', split_axis=0, concat_axis=0, tiled=True, axi...  3.87 us
    ppermute x5, waiting for transfers between devices, shift(): return lax.ppermute(x, axis, [(i, (i + by) % count) for i in range(count)])  3.8 us
  transfers between devices with their start and end apart: 20, of which 12 were waited for; matrix products, arithmetic and copies ran while one was open for 2% of the time, Pallas kernels for 3%

profile of v17, /device:TPU:1, one launch (start us, length us, event | category | flops | bytes accessed | tf_op | source)
XLA Modules:
  0.0 89.0 jit_solution(9389590451655975560)
XLA Ops:
  0.0 2.2 %shard_map.46 = (f32[16,8,256]{2,1,0:T(8,128)}, f32[16,8,256]{2,1,0:T(8,128)}, f32[5,64,256]{2,1,0:T(8,128)}, f32[5,64,256]{2,1,0:T(8,128)}) custom-call(f32[4,64,256]{2,1,0:T(8,128)} %f.1, f32[4,64,256]{2,1,0:T(8,128)} %c1.1, f32[4,64,256]{2,1,0:T(8,128)} %c2.1, f32[4,64,256]{2,1,0:T(8,128)} %c3.1), custom_call_target="tpu_custom_call" | custom-call | tf_op jit(solution)/shard_map/pallas_call | solution.py:136
  2.2 2.2 %collective-permute-start = (f32[16,8,256]{2,1,0:T(8,128)}, f32[16,8,256]{2,1,0:T(8,128)S(1)}, u32[]{:S(2)}, u32[]{:S(2)}) collective-permute-start(f32[16,8,256]{2,1,0:T(8,128)} %get-tuple-element.44), channel_id=1, source_target_pairs={{0,1},{1,2},{2,3},{3,0},{4,5},{5,6},{6,7},{7,4},{8,9},{9,10},{10,1... | collective-permute-start | bytes 393224 | tf_op jit(solution)/shard_map/ppermute | solution.py:744
  4.4 1.5 %collective-permute-start.1 = (f32[16,8,256]{2,1,0:T(8,128)}, f32[16,8,256]{2,1,0:T(8,128)S(1)}, u32[]{:S(2)}, u32[]{:S(2)}) collective-permute-start(f32[16,8,256]{2,1,0:T(8,128)} %get-tuple-element.45), channel_id=1, source_target_pairs={{0,3},{1,0},{2,1},{3,2},{4,7},{5,4},{6,5},{7,6},{8,11},{9,8},{10,9... | collective-permute-start | bytes 393224 | tf_op jit(solution)/shard_map/ppermute | solution.py:744
  5.9 2.6 %collective-permute-start.2 = (f32[5,64,256]{2,1,0:T(8,128)}, f32[5,64,256]{2,1,0:T(8,128)S(1)}, u32[]{:S(2)}, u32[]{:S(2)}) collective-permute-start(f32[5,64,256]{2,1,0:T(8,128)} %get-tuple-element.48), channel_id=1, source_target_pairs={{0,252},{4,8},{8,4},{12,16},{16,12},{20,24},{24,20},{28,32},{32,28... | collective-permute-start | bytes 983048 | tf_op jit(solution)/shard_map/ppermute | solution.py:753
  8.5 5.6 %collective-permute-start.3 = (f32[5,64,256]{2,1,0:T(8,128)}, f32[5,64,256]{2,1,0:T(8,128)S(1)}, u32[]{:S(2)}, u32[]{:S(2)}) collective-permute-start(f32[5,64,256]{2,1,0:T(8,128)} %get-tuple-element.49), channel_id=1, source_target_pairs={{0,4},{4,0},{8,12},{12,8},{16,20},{20,16},{24,28},{28,24},{32,36},... | collective-permute-start | bytes 983048 | tf_op jit(solution)/shard_map/ppermute | solution.py:748
  14.1 1.3 %pad_maximum_fusion.inner = f32[16,64,256]{2,1,0:T(8,128)S(1)} fusion(f32[4,64,256]{2,1,0:T(8,128)} %c3.1, f32[4,64,256]{2,1,0:T(8,128)} %c2.1, f32[4,64,256]{2,1,0:T(8,128)} %c1.1, f32[4,64,256]{2,1,0:T(8,128)} %f.1), kind=kLoop, calls=%fused_computation | loop fusion | flops 786432 | bytes 2097152 | tf_op jit(solution)/shard_map/concatenate | solution.py:775
  15.9 1.8 %collective-permute-start.5 = (f32[280,256]{1,0:T(8,128)S(1)}, f32[280,256]{1,0:T(8,128)S(1)}, u32[]{:S(2)}, u32[]{:S(2)}) collective-permute-start(f32[280,256]{1,0:T(8,128)S(1)} %get-tuple-element.51), channel_id=1, source_target_pairs={{0,4},{4,0},{8,12},{12,8},{16,20},{20,16},{24,28},{28,24},{32,36},... | collective-permute-start | bytes 860168 | tf_op jit(solution)/shard_map/ppermute | solution.py:748
  17.7 4.5 %collective-permute-done.4.far = f32[280,256]{1,0:T(8,128)S(1)} collective-permute-done((f32[280,256]{1,0:T(8,128)S(1)}, f32[280,256]{1,0:T(8,128)S(1)}, u32[]{:S(2)}, u32[]{:S(2)}) %collective-permute-start.4) | collective-permute-done | bytes 286752 | tf_op jit(solution)/shard_map/ppermute | solution.py:753
  22.3 2.3 %shard_map.48 = (f32[6,80,256]{2,1,0:T(8,128)S(1)}, f32[8,40,128]{2,1,0:T(8,128)S(1)}, f32[8,40,128]{2,1,0:T(8,128)S(1)}) custom-call(f32[16,80,256]{2,1,0:T(8,128)S(1)} %get-tuple-element.46.own, f32[6,40,128]{2,1,0:T(8,128)S(1)} %get-tuple-element.47.coef1, f32[5,64,256]{2,1,0:T(8,128)S(1)} %collective-permute-done.2.far_raw, ...), custom_call_target="tpu_custom_call" | custom-call | tf_op jit(solution)/shard_map/pallas_call | solution.py:136
  24.6 3.1 %collective-permute-start.7 = (f32[8,40,128]{2,1,0:T(8,128)S(1)}, f32[8,40,128]{2,1,0:T(8,128)S(1)}, u32[]{:S(2)}, u32[]{:S(2)}) collective-permute-start(f32[8,40,128]{2,1,0:T(8,128)S(1)} %get-tuple-element.53), channel_id=1, source_target_pairs={{0,4},{4,0},{8,12},{12,8},{16,20},{20,16},{24,28},{28,24},{32,36},... | collective-permute-start | bytes 491528 | tf_op jit(solution)/shard_map/ppermute | solution.py:748
  28.0 0.7 collective-permute-done.7.sib
  28.7 3.7 %collective-permute-done.6.far = f32[8,40,128]{2,1,0:T(8,128)S(1)} collective-permute-done((f32[8,40,128]{2,1,0:T(8,128)S(1)}, f32[8,40,128]{2,1,0:T(8,128)S(1)}, u32[]{:S(2)}, u32[]{:S(2)}) %collective-permute-start.6) | collective-permute-done | bytes 163872 | tf_op jit(solution)/shard_map/ppermute | solution.py:753
  32.9 2.7 %collective-permute-start.9 = (f32[56,128]{1,0:T(8,128)S(1)}, f32[56,128]{1,0:T(8,128)S(1)}, u32[]{:S(2)}, u32[]{:S(2)}) collective-permute-start(f32[56,128]{1,0:T(8,128)S(1)} %get-tuple-element.58), channel_id=1, source_target_pairs={{0,3},{1,0},{2,1},{3,2},{4,7},{5,4},{6,5},{7,6},{8,11},{9,8},{10,9... | collective-permute-start | bytes 86024 | tf_op jit(solution)/shard_map/ppermute | solution.py:744
  35.9 3.8 %collective-permute-done.10.far = f32[40,128]{1,0:T(8,128)S(1)} collective-permute-done((f32[40,128]{1,0:T(8,128)S(1)}, f32[40,128]{1,0:T(8,128)S(1)}, u32[]{:S(2)}, u32[]{:S(2)}) %collective-permute-start.10) | collective-permute-done | bytes 20512 | tf_op jit(solution)/shard_map/ppermute | solution.py:744
  39.9 5.2 %collective-permute-start.11 = (f32[240,128]{1,0:T(8,128)S(1)}, f32[240,128]{1,0:T(8,128)S(1)}, u32[]{:S(2)}, u32[]{:S(2)}) collective-permute-start(f32[240,128]{1,0:T(8,128)S(1)} %get-tuple-element.61.msg), channel_id=1, source_target_pairs={{0,4},{4,0},{8,12},{12,8},{16,20},{20,16},{24,28},{28,24},{32,36},... | collective-permute-start | bytes 368648 | tf_op jit(solution)/shard_map/ppermute | solution.py:748
  45.1 1.0 %collective-permute-done.11.sib = f32[240,128]{1,0:T(8,128)S(1)} collective-permute-done((f32[240,128]{1,0:T(8,128)S(1)}, f32[240,128]{1,0:T(8,128)S(1)}, u32[]{:S(2)}, u32[]{:S(2)}) %collective-permute-start.11) | collective-permute-done | bytes 122912 | tf_op jit(solution)/shard_map/ppermute | solution.py:748
  46.5 4.6 %collective-permute-done.12.near = f32[352,128]{1,0:T(8,128)S(1)} collective-permute-done((f32[352,128]{1,0:T(8,128)S(1)}, f32[352,128]{1,0:T(8,128)S(1)}, u32[]{:S(2)}, u32[]{:S(2)}) %collective-permute-start.12) | collective-permute-done | bytes 180256 | tf_op jit(solution)/shard_map/ppermute | solution.py:753
  51.1 3.7 %collective-permute-start.13 = (f32[352,128]{1,0:T(8,128)S(1)}, f32[352,128]{1,0:T(8,128)S(1)}, u32[]{:S(2)}, u32[]{:S(2)}) collective-permute-start(f32[352,128]{1,0:T(8,128)S(1)} %collective-permute-done.12.near), channel_id=1, source_target_pairs={{0,4},{4,0},{8,12},{12,8},{16,20},{20,16},{24,28},{28,24},{32,36},... | collective-permute-start | bytes 540680 | tf_op jit(solution)/shard_map/ppermute | solution.py:748
  54.8 1.0 %collective-permute-done.13.other = f32[352,128]{1,0:T(8,128)S(1)} collective-permute-done((f32[352,128]{1,0:T(8,128)S(1)}, f32[352,128]{1,0:T(8,128)S(1)}, u32[]{:S(2)}, u32[]{:S(2)}) %collective-permute-start.13) | collective-permute-done | bytes 180256 | tf_op jit(solution)/shard_map/ppermute | solution.py:748
  56.3 1.0 %shard_map.55 = f32[32,2,8,128]{3,2,1,0:T(8,128)} custom-call(f32[21,64,128]{2,1,0:T(8,128)S(1)} %get-tuple-element.63.w.win, f32[4,64,128]{2,1,0:T(8,128)S(1)} %get-tuple-element.64.u2, f32[3,8,128]{2,1,0:T(8,128)S(1)} %shard_map.53.tiles), custom_call_target="tpu_custom_call" | custom-call | tf_op jit(solution)/shard_map/pallas_call | solution.py:136
  57.3 3.9 %all-to-all-start = ((f32[32,2,8,128]{3,2,1,0:T(8,128)}), f32[32,2,8,128]{3,2,1,0:T(8,128)S(1)}, u32[]{:S(2)}, u32[]{:S(2)}) async-start(f32[32,2,8,128]{3,2,1,0:T(8,128)} %shard_map.55), calls=%async_computation | async-start | bytes 524288 | tf_op jit(solution)/shard_map/all_to_all | solution.py:809
  61.1 1.9 %collective-permute-start.14 = (f32[32,128]{1,0:T(8,128)S(1)}, f32[32,128]{1,0:T(8,128)S(1)}, u32[]{:S(2)}, u32[]{:S(2)}) collective-permute-start(f32[32,128]{1,0:T(8,128)S(1)} %get-tuple-element.66), channel_id=1, source_target_pairs={{0,252},{4,8},{8,4},{12,16},{16,12},{20,24},{24,20},{28,32},{32,28... | collective-permute-start | bytes 49160 | tf_op jit(solution)/shard_map/ppermute | solution.py:753
  63.1 6.3 %collective-permute-done.14.late = f32[32,128]{1,0:T(8,128)S(1)} collective-permute-done((f32[32,128]{1,0:T(8,128)S(1)}, f32[32,128]{1,0:T(8,128)S(1)}, u32[]{:S(2)}, u32[]{:S(2)}) %collective-permute-start.14) | collective-permute-done | bytes 16416 | tf_op jit(solution)/shard_map/ppermute | solution.py:753
  69.4 2.0 %all-to-all-done.mine = f32[32,2,8,128]{3,2,1,0:T(8,128)S(1)} async-done(((f32[32,2,8,128]{3,2,1,0:T(8,128)}), f32[32,2,8,128]{3,2,1,0:T(8,128)S(1)}, u32[]{:S(2)}, u32[]{:S(2)}) %all-to-all-start) | async-done | bytes 262176 | tf_op jit(solution)/shard_map/all_to_all | solution.py:809
  71.4 3.0 %collective-permute-start.15 = (f32[32,2,8,128]{3,2,1,0:T(8,128)S(1)}, f32[32,2,8,128]{3,2,1,0:T(8,128)S(1)}, u32[]{:S(2)}, u32[]{:S(2)}) collective-permute-start(f32[32,2,8,128]{3,2,1,0:T(8,128)S(1)} %all-to-all-done.mine), channel_id=1, source_target_pairs={{0,4},{4,0},{8,12},{12,8},{16,20},{20,16},{24,28},{28,24},{32,36},... | collective-permute-start | bytes 786440 | tf_op jit(solution)/shard_map/ppermute | solution.py:748
  74.5 1.1 %collective-permute-done.15.theirs = f32[32,2,8,128]{3,2,1,0:T(8,128)S(1)} collective-permute-done((f32[32,2,8,128]{3,2,1,0:T(8,128)S(1)}, f32[32,2,8,128]{3,2,1,0:T(8,128)S(1)}, u32[]{:S(2)}, u32[]{:S(2)}) %collective-permute-start.15) | collective-permute-done | bytes 262176 | tf_op jit(solution)/shard_map/ppermute | solution.py:748
  75.5 2.0 %shard_map.56.e2 = f32[200,128]{1,0:T(8,128)S(1)} custom-call(f32[32,2,8,128]{3,2,1,0:T(8,128)S(1)} %all-to-all-done.mine, f32[32,2,8,128]{3,2,1,0:T(8,128)S(1)} %collective-permute-done.15.theirs), custom_call_target="tpu_custom_call" | custom-call | tf_op jit(solution)/shard_map/pallas_call | solution.py:136
  77.9 1.9 %collective-permute-start.17 = (f32[2,32,128]{2,1,0:T(8,128)S(1)}, f32[2,32,128]{2,1,0:T(8,128)S(1)}, u32[]{:S(2)}, u32[]{:S(2)}) collective-permute-start(f32[2,32,128]{2,1,0:T(8,128)S(1)} %shard_map.57.e2), channel_id=1, source_target_pairs={{0,252},{4,8},{8,4},{12,16},{16,12},{20,24},{24,20},{28,32},{32,28... | collective-permute-start | bytes 98312 | tf_op jit(solution)/shard_map/ppermute | solution.py:753
  79.8 1.6 %collective-permute-done.17.far = f32[2,32,128]{2,1,0:T(8,128)S(1)} collective-permute-done((f32[2,32,128]{2,1,0:T(8,128)S(1)}, f32[2,32,128]{2,1,0:T(8,128)S(1)}, u32[]{:S(2)}, u32[]{:S(2)}) %collective-permute-start.17) | collective-permute-done | bytes 32800 | tf_op jit(solution)/shard_map/ppermute | solution.py:753
  82.1 3.7 %collective-permute-start.18 = (f32[40,128]{1,0:T(8,128)S(1)}, f32[40,128]{1,0:T(8,128)S(1)}, u32[]{:S(2)}, u32[]{:S(2)}) collective-permute-start(f32[40,128]{1,0:T(8,128)S(1)} %get-tuple-element.75), channel_id=1, source_target_pairs={{0,4},{4,0},{8,12},{12,8},{16,20},{20,16},{24,28},{28,24},{32,36},... | collective-permute-start | bytes 61448 | tf_op jit(solution)/shard_map/ppermute | solution.py:748
  85.9 0.7 collective-permute-done.18.other
  86.6 2.2 %shard_map.59 = f32[4,64,256]{2,1,0:T(8,128)} custom-call(f32[2,40,128]{2,1,0:T(8,128)S(1)} %get-tuple-element.73.e1, f32[40,128]{1,0:T(8,128)S(1)} %get-tuple-element.74.edge, f32[40,128]{1,0:T(8,128)S(1)} %collective-permute-done.18.other, f32[2,80,256]{2,1,0:T(8,128)S(1)} %get-tuple-element.76.outer, f32[16,64,256]{2,1,0:T(8,128)S(1)} %pad_maximum_fusion.1.inner, ...), custom_call_target="tpu_custom_call" | custom-call | tf_op jit(solution)/shard_map/pallas_call | solution.py:136
  (32 shorter events, 3.8 us)
Async XLA Ops:
  2.2 13.2 %collective-permute-start = (f32[16,8,256]{2,1,0:T(8,128)}, f32[16,8,256]{2,1,0:T(8,128)S(1)}, u32[]{:S(2)}, u32[]{:S(2)}) collective-permute-start(f32[16,8,256]{2,1,0:T(8,128)} %get-tuple-element.44), channel_id=1, source_target_pairs={{0,1},{1,2},{2,3},{3,0},{4,5},{5,6},{6,7},{7,4},{8,9},{9,10},{10,1... | collective-permute-start | bytes 393224 | tf_op jit(solution)/shard_map/ppermute | solution.py:744
  4.4 11.0 %collective-permute-start.1 = (f32[16,8,256]{2,1,0:T(8,128)}, f32[16,8,256]{2,1,0:T(8,128)S(1)}, u32[]{:S(2)}, u32[]{:S(2)}) collective-permute-start(f32[16,8,256]{2,1,0:T(8,128)} %get-tuple-element.45), channel_id=1, source_target_pairs={{0,3},{1,0},{2,1},{3,2},{4,7},{5,4},{6,5},{7,6},{8,11},{9,8},{10,9... | collective-permute-start | bytes 393224 | tf_op jit(solution)/shard_map/ppermute | solution.py:744
  5.9 11.8 %collective-permute-start.2 = (f32[5,64,256]{2,1,0:T(8,128)}, f32[5,64,256]{2,1,0:T(8,128)S(1)}, u32[]{:S(2)}, u32[]{:S(2)}) collective-permute-start(f32[5,64,256]{2,1,0:T(8,128)} %get-tuple-element.48), channel_id=1, source_target_pairs={{0,252},{4,8},{8,4},{12,16},{16,12},{20,24},{24,20},{28,32},{32,28... | collective-permute-start | bytes 983048 | tf_op jit(solution)/shard_map/ppermute | solution.py:753
  8.5 9.2 %collective-permute-start.3 = (f32[5,64,256]{2,1,0:T(8,128)}, f32[5,64,256]{2,1,0:T(8,128)S(1)}, u32[]{:S(2)}, u32[]{:S(2)}) collective-permute-start(f32[5,64,256]{2,1,0:T(8,128)} %get-tuple-element.49), channel_id=1, source_target_pairs={{0,4},{4,0},{8,12},{12,8},{16,20},{20,16},{24,28},{28,24},{32,36},... | collective-permute-start | bytes 983048 | tf_op jit(solution)/shard_map/ppermute | solution.py:748
  15.8 6.4 %collective-permute-start.4 = (f32[280,256]{1,0:T(8,128)S(1)}, f32[280,256]{1,0:T(8,128)S(1)}, u32[]{:S(2)}, u32[]{:S(2)}) collective-permute-start(f32[280,256]{1,0:T(8,128)S(1)} %get-tuple-element.50), channel_id=1, source_target_pairs={{0,252},{4,8},{8,4},{12,16},{16,12},{20,24},{24,20},{28,32},{32,28... | collective-permute-start | bytes 860168 | tf_op jit(solution)/shard_map/ppermute | solution.py:753
  15.9 6.3 %collective-permute-start.5 = (f32[280,256]{1,0:T(8,128)S(1)}, f32[280,256]{1,0:T(8,128)S(1)}, u32[]{:S(2)}, u32[]{:S(2)}) collective-permute-start(f32[280,256]{1,0:T(8,128)S(1)} %get-tuple-element.51), channel_id=1, source_target_pairs={{0,4},{4,0},{8,12},{12,8},{16,20},{20,16},{24,28},{28,24},{32,36},... | collective-permute-start | bytes 860168 | tf_op jit(solution)/shard_map/ppermute | solution.py:748
  24.6 4.1 %collective-permute-start.7 = (f32[8,40,128]{2,1,0:T(8,128)S(1)}, f32[8,40,128]{2,1,0:T(8,128)S(1)}, u32[]{:S(2)}, u32[]{:S(2)}) collective-permute-start(f32[8,40,128]{2,1,0:T(8,128)S(1)} %get-tuple-element.53), channel_id=1, source_target_pairs={{0,4},{4,0},{8,12},{12,8},{16,20},{20,16},{24,28},{28,24},{32,36},... | collective-permute-start | bytes 491528 | tf_op jit(solution)/shard_map/ppermute | solution.py:748
  27.7 4.7 %collective-permute-start.6 = (f32[8,40,128]{2,1,0:T(8,128)S(1)}, f32[8,40,128]{2,1,0:T(8,128)S(1)}, u32[]{:S(2)}, u32[]{:S(2)}) collective-permute-start(f32[8,40,128]{2,1,0:T(8,128)S(1)} %get-tuple-element.52.own), channel_id=1, source_target_pairs={{0,252},{4,8},{8,4},{12,16},{16,12},{20,24},{24,20},{28,32},{32,28... | collective-permute-start | bytes 491528 | tf_op jit(solution)/shard_map/ppermute | solution.py:753
  32.8 6.9 %collective-permute-start.8 = (f32[56,128]{1,0:T(8,128)S(1)}, f32[56,128]{1,0:T(8,128)S(1)}, u32[]{:S(2)}, u32[]{:S(2)}) collective-permute-start(f32[56,128]{1,0:T(8,128)S(1)} %get-tuple-element.57), channel_id=1, source_target_pairs={{0,1},{1,2},{2,3},{3,0},{4,5},{5,6},{6,7},{7,4},{8,9},{9,10},{10,1... | collective-permute-start | bytes 86024 | tf_op jit(solution)/shard_map/ppermute | solution.py:744
  32.9 6.8 %collective-permute-start.9 = (f32[56,128]{1,0:T(8,128)S(1)}, f32[56,128]{1,0:T(8,128)S(1)}, u32[]{:S(2)}, u32[]{:S(2)}) collective-permute-start(f32[56,128]{1,0:T(8,128)S(1)} %get-tuple-element.58), channel_id=1, source_target_pairs={{0,3},{1,0},{2,1},{3,2},{4,7},{5,4},{6,5},{7,6},{8,11},{9,8},{10,9... | collective-permute-start | bytes 86024 | tf_op jit(solution)/shard_map/ppermute | solution.py:744
  35.5 4.1 %collective-permute-start.10 = (f32[40,128]{1,0:T(8,128)S(1)}, f32[40,128]{1,0:T(8,128)S(1)}, u32[]{:S(2)}, u32[]{:S(2)}) collective-permute-start(f32[40,128]{1,0:T(8,128)S(1)} %get-tuple-element.56.f2), channel_id=1, source_target_pairs={{0,2},{1,3},{2,0},{3,1},{4,6},{5,7},{6,4},{7,5},{8,10},{9,11},{10,... | collective-permute-start | bytes 61448 | tf_op jit(solution)/shard_map/ppermute | solution.py:744
  39.9 6.2 %collective-permute-start.11 = (f32[240,128]{1,0:T(8,128)S(1)}, f32[240,128]{1,0:T(8,128)S(1)}, u32[]{:S(2)}, u32[]{:S(2)}) collective-permute-start(f32[240,128]{1,0:T(8,128)S(1)} %get-tuple-element.61.msg), channel_id=1, source_target_pairs={{0,4},{4,0},{8,12},{12,8},{16,20},{20,16},{24,28},{28,24},{32,36},... | collective-permute-start | bytes 368648 | tf_op jit(solution)/shard_map/ppermute | solution.py:748
  46.1 5.0 %collective-permute-start.12 = (f32[352,128]{1,0:T(8,128)S(1)}, f32[352,128]{1,0:T(8,128)S(1)}, u32[]{:S(2)}, u32[]{:S(2)}) collective-permute-start(f32[352,128]{1,0:T(8,128)S(1)} %shard_map.52), channel_id=1, source_target_pairs={{0,252},{4,8},{8,4},{12,16},{16,12},{20,24},{24,20},{28,32},{32,28... | collective-permute-start | bytes 540680 | tf_op jit(solution)/shard_map/ppermute | solution.py:753
  51.1 4.7 %collective-permute-start.13 = (f32[352,128]{1,0:T(8,128)S(1)}, f32[352,128]{1,0:T(8,128)S(1)}, u32[]{:S(2)}, u32[]{:S(2)}) collective-permute-start(f32[352,128]{1,0:T(8,128)S(1)} %collective-permute-done.12.near), channel_id=1, source_target_pairs={{0,4},{4,0},{8,12},{12,8},{16,20},{20,16},{24,28},{28,24},{32,36},... | collective-permute-start | bytes 540680 | tf_op jit(solution)/shard_map/ppermute | solution.py:748
  57.3 14.1 %all-to-all-start = ((f32[32,2,8,128]{3,2,1,0:T(8,128)}), f32[32,2,8,128]{3,2,1,0:T(8,128)S(1)}, u32[]{:S(2)}, u32[]{:S(2)}) async-start(f32[32,2,8,128]{3,2,1,0:T(8,128)} %shard_map.55), calls=%async_computation | async-start | bytes 524288 | tf_op jit(solution)/shard_map/all_to_all | solution.py:809
  61.1 8.2 %collective-permute-start.14 = (f32[32,128]{1,0:T(8,128)S(1)}, f32[32,128]{1,0:T(8,128)S(1)}, u32[]{:S(2)}, u32[]{:S(2)}) collective-permute-start(f32[32,128]{1,0:T(8,128)S(1)} %get-tuple-element.66), channel_id=1, source_target_pairs={{0,252},{4,8},{8,4},{12,16},{16,12},{20,24},{24,20},{28,32},{32,28... | collective-permute-start | bytes 49160 | tf_op jit(solution)/shard_map/ppermute | solution.py:753
  71.4 14.4 %copy-start = (f32[4,64,256]{2,1,0:T(8,128)S(1)}, f32[4,64,256]{2,1,0:T(8,128)}, u32[]{:S(2)}) copy-start(f32[4,64,256]{2,1,0:T(8,128)} %c3.1) | copy-start | bytes 786436
  71.4 14.4 %copy-start.1 = (f32[4,64,256]{2,1,0:T(8,128)S(1)}, f32[4,64,256]{2,1,0:T(8,128)}, u32[]{:S(2)}) copy-start(f32[4,64,256]{2,1,0:T(8,128)} %c2.1) | copy-start | bytes 786436
  71.4 14.4 %copy-start.2 = (f32[4,64,256]{2,1,0:T(8,128)S(1)}, f32[4,64,256]{2,1,0:T(8,128)}, u32[]{:S(2)}) copy-start(f32[4,64,256]{2,1,0:T(8,128)} %c1.1) | copy-start | bytes 786436
  71.4 14.4 %copy-start.3 = (f32[4,64,256]{2,1,0:T(8,128)S(1)}, f32[4,64,256]{2,1,0:T(8,128)}, u32[]{:S(2)}) copy-start(f32[4,64,256]{2,1,0:T(8,128)} %f.1) | copy-start | bytes 786436
  71.4 4.2 %collective-permute-start.15 = (f32[32,2,8,128]{3,2,1,0:T(8,128)S(1)}, f32[32,2,8,128]{3,2,1,0:T(8,128)S(1)}, u32[]{:S(2)}, u32[]{:S(2)}) collective-permute-start(f32[32,2,8,128]{3,2,1,0:T(8,128)S(1)} %all-to-all-done.mine), channel_id=1, source_target_pairs={{0,4},{4,0},{8,12},{12,8},{16,20},{20,16},{24,28},{28,24},{32,36},... | collective-permute-start | bytes 786440 | tf_op jit(solution)/shard_map/ppermute | solution.py:748
  74.4 3.2 %collective-permute-start.16 = (f32[32,128]{1,0:T(8,128)S(1)}, f32[32,128]{1,0:T(8,128)S(1)}, u32[]{:S(2)}, u32[]{:S(2)}) collective-permute-start(f32[32,128]{1,0:T(8,128)S(1)} %collective-permute-done.14.late), channel_id=1, source_target_pairs={{0,4},{4,0},{8,12},{12,8},{16,20},{20,16},{24,28},{28,24},{32,36},... | collective-permute-start | bytes 49160 | tf_op jit(solution)/shard_map/ppermute | solution.py:748
  77.9 3.5 %collective-permute-start.17 = (f32[2,32,128]{2,1,0:T(8,128)S(1)}, f32[2,32,128]{2,1,0:T(8,128)S(1)}, u32[]{:S(2)}, u32[]{:S(2)}) collective-permute-start(f32[2,32,128]{2,1,0:T(8,128)S(1)} %shard_map.57.e2), channel_id=1, source_target_pairs={{0,252},{4,8},{8,4},{12,16},{16,12},{20,24},{24,20},{28,32},{32,28... | collective-permute-start | bytes 98312 | tf_op jit(solution)/shard_map/ppermute | solution.py:753
  82.1 4.5 %collective-permute-start.18 = (f32[40,128]{1,0:T(8,128)S(1)}, f32[40,128]{1,0:T(8,128)S(1)}, u32[]{:S(2)}, u32[]{:S(2)}) collective-permute-start(f32[40,128]{1,0:T(8,128)S(1)} %get-tuple-element.75), channel_id=1, source_target_pairs={{0,4},{4,0},{8,12},{12,8},{16,20},{20,16},{24,28},{28,24},{32,36},... | collective-permute-start | bytes 61448 | tf_op jit(solution)/shard_map/ppermute | solution.py:748

commit v18 on v17

--- a/solution.py
+++ b/solution.py
@@ -643,7 +643,7 @@
         e2[pl.ds(2 * q + 1, 24, stride=8), :] = fine
 
 
-def coarse_post_kernel(e2, win, u2, late, late_sib, out):
+def coarse_post_kernel(e2, win, u2, late, late_sib, out, msg):
     below, above = sides(late, late_sib)
     v = [both_halves(below(...)), u2[0], u2[1], u2[2], u2[3], both_halves(above(...))]
     v = [v[m] + e2[64 * (m // 2) : 64 * (m // 2) + 64, :] for m in range(6)]
@@ -655,6 +655,7 @@
     for p in range(2):
         x = second_post(w[p + 1], v[p + 2], w[p], w[p + 2], *args(p + 1))
         out[p] = pltpu.roll(x, lax.rem(72 - 16 * lax.axis_index("narrow"), 64), 0)[0:32]
+    msg[...] = jnp.where(iota((32, 128), 1) < 64, out[0], out[1])
 
 
 def middle_post_kernel(e2, far, u2, f, g, w1, own, edge, send, fine, c1, v, w):
@@ -663,7 +664,7 @@
     row, col = iota((40, 32), 0), iota((40, 32), 1)
     pick = (col == (row + 4) // 2 + 4).astype(F32)
     lanes = copies_of_lanes(128, 128)
-    planes = (e2[0], e2[1], far[0], far[1])
+    planes = (e2[0], e2[1], spread_block(far[...], 0, 64), spread_block(far[...], 1, 64))
     for k in range(4):
         fine[k] = mul(mul_left(pick, jnp.where(odd, planes[k], planes[(k + 2) % 4])), lanes)
     c1[0:6] = w1[0:6]
@@ -817,9 +818,9 @@
         [three, (n3 + 1, 8, 128), three, three, three, three, (n3 + 2, 8, 128), (n3 + 2, 8, 128), four, four]
         + [(n4 + 1, 8, 128), four, four, four, (n4 + 2, 8, 128), (n4 + 2, 8, 128), four, (32, 128)],
     )(parts, theirs)
-    (e2,) = call(coarse_post_kernel, [(2, 32, 128)])(fine2, w2, u2w, late, late_sib)
-    e2, *again = lax.optimization_barrier((e2,) + inputs)
-    far = across(e2)
+    e2, both = call(coarse_post_kernel, [(2, 32, 128), (32, 128)])(fine2, w2, u2w, late, late_sib)
+    both, *again = lax.optimization_barrier((both,) + inputs)
+    far = across(both)
 
     e1, edge, send = call(
         middle_post_kernel,

time: 89.2 us -> 89.1 us (level)
  no operation moved by 1% of the time
where the time goes in v18:
time: 89.1 us; the launch traced here: 88.8 us
  starting transfers between devices  43.5 us (49%)
  waiting for transfers between devices  30.9 us (35%)
  Pallas kernels  12.7 us (14%)
  other arithmetic  1.35 us (2%)
    ppermute x8, starting transfers between devices, sibling(): lax.ppermute(x, 'wide', [(i, i ^ 1) for i in range(lax.axis_size('wide'))])  26.1 us
    ppermute x6, waiting for transfers between devices, across(): lax.ppermute(x, 'wide', [(i, (i + 1 if i % 2 else i - 1) % count) for i i...  20.6 us
    pallas_call x14, Pallas kernels, run(): pl.pallas_call(kernel, out_shape=[jax.ShapeDtypeStruct(s, F32) for s in o...  12.7 us
    ppermute x5, starting transfers between devices, shift(): return lax.ppermute(x, axis, [(i, (i + by) % count) for i in range(count)])  6.82 us
    ppermute x6, starting transfers between devices, across(): lax.ppermute(x, 'wide', [(i, (i + 1 if i % 2 else i - 1) % count) for i i...  6.65 us
    ppermute x8, waiting for transfers between devices, sibling(): lax.ppermute(x, 'wide', [(i, i ^ 1) for i in range(lax.axis_size('wide'))])  4.53 us
    all_to_all x1, starting transfers between devices, body(): lax.all_to_all(send, 'wide', split_axis=0, concat_axis=0, tiled=True, axi...  3.87 us
    ppermute x5, waiting for transfers between devices, shift(): return lax.ppermute(x, axis, [(i, (i + by) % count) for i in range(count)])  3.8 us
  transfers between devices with their start and end apart: 20, of which 12 were waited for; matrix products, arithmetic and copies ran while one was open for 2% of the time, Pallas kernels for 3%

profile of v18, /device:TPU:1, one launch (start us, length us, event | category | flops | bytes accessed | tf_op | source)
XLA Modules:
  0.0 88.8 jit_solution(4146602139786442090)
XLA Ops:
  0.0 2.2 %shard_map.46 = (f32[16,8,256]{2,1,0:T(8,128)}, f32[16,8,256]{2,1,0:T(8,128)}, f32[5,64,256]{2,1,0:T(8,128)}, f32[5,64,256]{2,1,0:T(8,128)}) custom-call(f32[4,64,256]{2,1,0:T(8,128)} %f.1, f32[4,64,256]{2,1,0:T(8,128)} %c1.1, f32[4,64,256]{2,1,0:T(8,128)} %c2.1, f32[4,64,256]{2,1,0:T(8,128)} %c3.1), custom_call_target="tpu_custom_call" | custom-call | tf_op jit(solution)/shard_map/pallas_call | solution.py:136
  2.2 2.2 %collective-permute-start = (f32[16,8,256]{2,1,0:T(8,128)}, f32[16,8,256]{2,1,0:T(8,128)S(1)}, u32[]{:S(2)}, u32[]{:S(2)}) collective-permute-start(f32[16,8,256]{2,1,0:T(8,128)} %get-tuple-element.46), channel_id=1, source_target_pairs={{0,1},{1,2},{2,3},{3,0},{4,5},{5,6},{6,7},{7,4},{8,9},{9,10},{10,1... | collective-permute-start | bytes 393224 | tf_op jit(solution)/shard_map/ppermute | solution.py:745
  4.4 1.5 %collective-permute-start.1 = (f32[16,8,256]{2,1,0:T(8,128)}, f32[16,8,256]{2,1,0:T(8,128)S(1)}, u32[]{:S(2)}, u32[]{:S(2)}) collective-permute-start(f32[16,8,256]{2,1,0:T(8,128)} %get-tuple-element.47), channel_id=1, source_target_pairs={{0,3},{1,0},{2,1},{3,2},{4,7},{5,4},{6,5},{7,6},{8,11},{9,8},{10,9... | collective-permute-start | bytes 393224 | tf_op jit(solution)/shard_map/ppermute | solution.py:745
  5.9 2.6 %collective-permute-start.2 = (f32[5,64,256]{2,1,0:T(8,128)}, f32[5,64,256]{2,1,0:T(8,128)S(1)}, u32[]{:S(2)}, u32[]{:S(2)}) collective-permute-start(f32[5,64,256]{2,1,0:T(8,128)} %get-tuple-element.50), channel_id=1, source_target_pairs={{0,252},{4,8},{8,4},{12,16},{16,12},{20,24},{24,20},{28,32},{32,28... | collective-permute-start | bytes 983048 | tf_op jit(solution)/shard_map/ppermute | solution.py:754
  8.5 5.6 %collective-permute-start.3 = (f32[5,64,256]{2,1,0:T(8,128)}, f32[5,64,256]{2,1,0:T(8,128)S(1)}, u32[]{:S(2)}, u32[]{:S(2)}) collective-permute-start(f32[5,64,256]{2,1,0:T(8,128)} %get-tuple-element.51), channel_id=1, source_target_pairs={{0,4},{4,0},{8,12},{12,8},{16,20},{20,16},{24,28},{28,24},{32,36},... | collective-permute-start | bytes 983048 | tf_op jit(solution)/shard_map/ppermute | solution.py:749
  14.1 1.3 %pad_maximum_fusion.inner = f32[16,64,256]{2,1,0:T(8,128)S(1)} fusion(f32[4,64,256]{2,1,0:T(8,128)} %c3.1, f32[4,64,256]{2,1,0:T(8,128)} %c2.1, f32[4,64,256]{2,1,0:T(8,128)} %c1.1, f32[4,64,256]{2,1,0:T(8,128)} %f.1), kind=kLoop, calls=%fused_computation | loop fusion | flops 786432 | bytes 2097152 | tf_op jit(solution)/shard_map/concatenate | solution.py:776
  15.9 1.8 %collective-permute-start.5 = (f32[280,256]{1,0:T(8,128)S(1)}, f32[280,256]{1,0:T(8,128)S(1)}, u32[]{:S(2)}, u32[]{:S(2)}) collective-permute-start(f32[280,256]{1,0:T(8,128)S(1)} %get-tuple-element.53), channel_id=1, source_target_pairs={{0,4},{4,0},{8,12},{12,8},{16,20},{20,16},{24,28},{28,24},{32,36},... | collective-permute-start | bytes 860168 | tf_op jit(solution)/shard_map/ppermute | solution.py:749
  17.7 4.5 %collective-permute-done.4.far = f32[280,256]{1,0:T(8,128)S(1)} collective-permute-done((f32[280,256]{1,0:T(8,128)S(1)}, f32[280,256]{1,0:T(8,128)S(1)}, u32[]{:S(2)}, u32[]{:S(2)}) %collective-permute-start.4) | collective-permute-done | bytes 286752 | tf_op jit(solution)/shard_map/ppermute | solution.py:754
  22.3 2.3 %shard_map.48 = (f32[6,80,256]{2,1,0:T(8,128)S(1)}, f32[8,40,128]{2,1,0:T(8,128)S(1)}, f32[8,40,128]{2,1,0:T(8,128)S(1)}) custom-call(f32[16,80,256]{2,1,0:T(8,128)S(1)} %get-tuple-element.48.own, f32[6,40,128]{2,1,0:T(8,128)S(1)} %get-tuple-element.49.coef1, f32[5,64,256]{2,1,0:T(8,128)S(1)} %collective-permute-done.2.far_raw, ...), custom_call_target="tpu_custom_call" | custom-call | tf_op jit(solution)/shard_map/pallas_call | solution.py:136
  24.6 3.1 %collective-permute-start.7 = (f32[8,40,128]{2,1,0:T(8,128)S(1)}, f32[8,40,128]{2,1,0:T(8,128)S(1)}, u32[]{:S(2)}, u32[]{:S(2)}) collective-permute-start(f32[8,40,128]{2,1,0:T(8,128)S(1)} %get-tuple-element.55), channel_id=1, source_target_pairs={{0,4},{4,0},{8,12},{12,8},{16,20},{20,16},{24,28},{28,24},{32,36},... | collective-permute-start | bytes 491528 | tf_op jit(solution)/shard_map/ppermute | solution.py:749
  28.7 3.7 %collective-permute-done.6.far = f32[8,40,128]{2,1,0:T(8,128)S(1)} collective-permute-done((f32[8,40,128]{2,1,0:T(8,128)S(1)}, f32[8,40,128]{2,1,0:T(8,128)S(1)}, u32[]{:S(2)}, u32[]{:S(2)}) %collective-permute-start.6) | collective-permute-done | bytes 163872 | tf_op jit(solution)/shard_map/ppermute | solution.py:754
  32.9 2.7 %collective-permute-start.9 = (f32[56,128]{1,0:T(8,128)S(1)}, f32[56,128]{1,0:T(8,128)S(1)}, u32[]{:S(2)}, u32[]{:S(2)}) collective-permute-start(f32[56,128]{1,0:T(8,128)S(1)} %get-tuple-element.60), channel_id=1, source_target_pairs={{0,3},{1,0},{2,1},{3,2},{4,7},{5,4},{6,5},{7,6},{8,11},{9,8},{10,9... | collective-permute-start | bytes 86024 | tf_op jit(solution)/shard_map/ppermute | solution.py:745
  35.9 3.8 %collective-permute-done.10.far = f32[40,128]{1,0:T(8,128)S(1)} collective-permute-done((f32[40,128]{1,0:T(8,128)S(1)}, f32[40,128]{1,0:T(8,128)S(1)}, u32[]{:S(2)}, u32[]{:S(2)}) %collective-permute-start.10) | collective-permute-done | bytes 20512 | tf_op jit(solution)/shard_map/ppermute | solution.py:745
  39.9 5.2 %collective-permute-start.11 = (f32[240,128]{1,0:T(8,128)S(1)}, f32[240,128]{1,0:T(8,128)S(1)}, u32[]{:S(2)}, u32[]{:S(2)}) collective-permute-start(f32[240,128]{1,0:T(8,128)S(1)} %get-tuple-element.63.msg), channel_id=1, source_target_pairs={{0,4},{4,0},{8,12},{12,8},{16,20},{20,16},{24,28},{28,24},{32,36},... | collective-permute-start | bytes 368648 | tf_op jit(solution)/shard_map/ppermute | solution.py:749
  45.1 1.0 %collective-permute-done.11.sib = f32[240,128]{1,0:T(8,128)S(1)} collective-permute-done((f32[240,128]{1,0:T(8,128)S(1)}, f32[240,128]{1,0:T(8,128)S(1)}, u32[]{:S(2)}, u32[]{:S(2)}) %collective-permute-start.11) | collective-permute-done | bytes 122912 | tf_op jit(solution)/shard_map/ppermute | solution.py:749
  46.5 4.6 %collective-permute-done.12.near = f32[352,128]{1,0:T(8,128)S(1)} collective-permute-done((f32[352,128]{1,0:T(8,128)S(1)}, f32[352,128]{1,0:T(8,128)S(1)}, u32[]{:S(2)}, u32[]{:S(2)}) %collective-permute-start.12) | collective-permute-done | bytes 180256 | tf_op jit(solution)/shard_map/ppermute | solution.py:754
  51.1 3.7 %collective-permute-start.13 = (f32[352,128]{1,0:T(8,128)S(1)}, f32[352,128]{1,0:T(8,128)S(1)}, u32[]{:S(2)}, u32[]{:S(2)}) collective-permute-start(f32[352,128]{1,0:T(8,128)S(1)} %collective-permute-done.12.near), channel_id=1, source_target_pairs={{0,4},{4,0},{8,12},{12,8},{16,20},{20,16},{24,28},{28,24},{32,36},... | collective-permute-start | bytes 540680 | tf_op jit(solution)/shard_map/ppermute | solution.py:749
  54.8 1.0 %collective-permute-done.13.other = f32[352,128]{1,0:T(8,128)S(1)} collective-permute-done((f32[352,128]{1,0:T(8,128)S(1)}, f32[352,128]{1,0:T(8,128)S(1)}, u32[]{:S(2)}, u32[]{:S(2)}) %collective-permute-start.13) | collective-permute-done | bytes 180256 | tf_op jit(solution)/shard_map/ppermute | solution.py:749
  56.3 1.0 %shard_map.55 = f32[32,2,8,128]{3,2,1,0:T(8,128)} custom-call(f32[21,64,128]{2,1,0:T(8,128)S(1)} %get-tuple-element.65.w.win, f32[4,64,128]{2,1,0:T(8,128)S(1)} %get-tuple-element.66.u2, f32[3,8,128]{2,1,0:T(8,128)S(1)} %shard_map.53.tiles), custom_call_target="tpu_custom_call" | custom-call | tf_op jit(solution)/shard_map/pallas_call | solution.py:136
  57.3 3.9 %all-to-all-start = ((f32[32,2,8,128]{3,2,1,0:T(8,128)}), f32[32,2,8,128]{3,2,1,0:T(8,128)S(1)}, u32[]{:S(2)}, u32[]{:S(2)}) async-start(f32[32,2,8,128]{3,2,1,0:T(8,128)} %shard_map.55), calls=%async_computation | async-start | bytes 524288 | tf_op jit(solution)/shard_map/all_to_all | solution.py:810
  61.1 1.9 %collective-permute-start.14 = (f32[32,128]{1,0:T(8,128)S(1)}, f32[32,128]{1,0:T(8,128)S(1)}, u32[]{:S(2)}, u32[]{:S(2)}) collective-permute-start(f32[32,128]{1,0:T(8,128)S(1)} %get-tuple-element.68), channel_id=1, source_target_pairs={{0,252},{4,8},{8,4},{12,16},{16,12},{20,24},{24,20},{28,32},{32,28... | collective-permute-start | bytes 49160 | tf_op jit(solution)/shard_map/ppermute | solution.py:754
  63.1 6.3 %collective-permute-done.14.late = f32[32,128]{1,0:T(8,128)S(1)} collective-permute-done((f32[32,128]{1,0:T(8,128)S(1)}, f32[32,128]{1,0:T(8,128)S(1)}, u32[]{:S(2)}, u32[]{:S(2)}) %collective-permute-start.14) | collective-permute-done | bytes 16416 | tf_op jit(solution)/shard_map/ppermute | solution.py:754
  69.4 2.0 %all-to-all-done.mine = f32[32,2,8,128]{3,2,1,0:T(8,128)S(1)} async-done(((f32[32,2,8,128]{3,2,1,0:T(8,128)}), f32[32,2,8,128]{3,2,1,0:T(8,128)S(1)}, u32[]{:S(2)}, u32[]{:S(2)}) %all-to-all-start) | async-done | bytes 262176 | tf_op jit(solution)/shard_map/all_to_all | solution.py:810
  71.4 3.0 %collective-permute-start.15 = (f32[32,2,8,128]{3,2,1,0:T(8,128)S(1)}, f32[32,2,8,128]{3,2,1,0:T(8,128)S(1)}, u32[]{:S(2)}, u32[]{:S(2)}) collective-permute-start(f32[32,2,8,128]{3,2,1,0:T(8,128)S(1)} %all-to-all-done.mine), channel_id=1, source_target_pairs={{0,4},{4,0},{8,12},{12,8},{16,20},{20,16},{24,28},{28,24},{32,36},... | collective-permute-start | bytes 786440 | tf_op jit(solution)/shard_map/ppermute | solution.py:749
  74.5 1.1 %collective-permute-done.15.theirs = f32[32,2,8,128]{3,2,1,0:T(8,128)S(1)} collective-permute-done((f32[32,2,8,128]{3,2,1,0:T(8,128)S(1)}, f32[32,2,8,128]{3,2,1,0:T(8,128)S(1)}, u32[]{:S(2)}, u32[]{:S(2)}) %collective-permute-start.15) | collective-permute-done | bytes 262176 | tf_op jit(solution)/shard_map/ppermute | solution.py:749
  75.5 2.0 %shard_map.56.e2 = f32[200,128]{1,0:T(8,128)S(1)} custom-call(f32[32,2,8,128]{3,2,1,0:T(8,128)S(1)} %all-to-all-done.mine, f32[32,2,8,128]{3,2,1,0:T(8,128)S(1)} %collective-permute-done.15.theirs), custom_call_target="tpu_custom_call" | custom-call | tf_op jit(solution)/shard_map/pallas_call | solution.py:136
  77.9 1.9 %collective-permute-start.17 = (f32[32,128]{1,0:T(8,128)S(1)}, f32[32,128]{1,0:T(8,128)S(1)}, u32[]{:S(2)}, u32[]{:S(2)}) collective-permute-start(f32[32,128]{1,0:T(8,128)S(1)} %get-tuple-element.73), channel_id=1, source_target_pairs={{0,252},{4,8},{8,4},{12,16},{16,12},{20,24},{24,20},{28,32},{32,28... | collective-permute-start | bytes 49160 | tf_op jit(solution)/shard_map/ppermute | solution.py:754
  79.8 1.4 %collective-permute-done.17.far = f32[32,128]{1,0:T(8,128)S(1)} collective-permute-done((f32[32,128]{1,0:T(8,128)S(1)}, f32[32,128]{1,0:T(8,128)S(1)}, u32[]{:S(2)}, u32[]{:S(2)}) %collective-permute-start.17) | collective-permute-done | bytes 16416 | tf_op jit(solution)/shard_map/ppermute | solution.py:754
  81.2 0.7 shard_map.58
  82.0 3.7 %collective-permute-start.18 = (f32[40,128]{1,0:T(8,128)S(1)}, f32[40,128]{1,0:T(8,128)S(1)}, u32[]{:S(2)}, u32[]{:S(2)}) collective-permute-start(f32[40,128]{1,0:T(8,128)S(1)} %get-tuple-element.79), channel_id=1, source_target_pairs={{0,4},{4,0},{8,12},{12,8},{16,20},{20,16},{24,28},{28,24},{32,36},... | collective-permute-start | bytes 61448 | tf_op jit(solution)/shard_map/ppermute | solution.py:749
  85.8 0.7 collective-permute-done.18.other
  86.5 2.2 %shard_map.59 = f32[4,64,256]{2,1,0:T(8,128)} custom-call(f32[2,40,128]{2,1,0:T(8,128)S(1)} %get-tuple-element.77.e1, f32[40,128]{1,0:T(8,128)S(1)} %get-tuple-element.78.edge, f32[40,128]{1,0:T(8,128)S(1)} %collective-permute-done.18.other, f32[2,80,256]{2,1,0:T(8,128)S(1)} %get-tuple-element.80.outer, f32[16,64,256]{2,1,0:T(8,128)S(1)} %pad_maximum_fusion.1.inner, ...), custom_call_target="tpu_custom_call" | custom-call | tf_op jit(solution)/shard_map/pallas_call | solution.py:136
  (32 shorter events, 3.9 us)
Async XLA Ops:
  2.2 13.2 %collective-permute-start = (f32[16,8,256]{2,1,0:T(8,128)}, f32[16,8,256]{2,1,0:T(8,128)S(1)}, u32[]{:S(2)}, u32[]{:S(2)}) collective-permute-start(f32[16,8,256]{2,1,0:T(8,128)} %get-tuple-element.46), channel_id=1, source_target_pairs={{0,1},{1,2},{2,3},{3,0},{4,5},{5,6},{6,7},{7,4},{8,9},{9,10},{10,1... | collective-permute-start | bytes 393224 | tf_op jit(solution)/shard_map/ppermute | solution.py:745
  4.4 11.0 %collective-permute-start.1 = (f32[16,8,256]{2,1,0:T(8,128)}, f32[16,8,256]{2,1,0:T(8,128)S(1)}, u32[]{:S(2)}, u32[]{:S(2)}) collective-permute-start(f32[16,8,256]{2,1,0:T(8,128)} %get-tuple-element.47), channel_id=1, source_target_pairs={{0,3},{1,0},{2,1},{3,2},{4,7},{5,4},{6,5},{7,6},{8,11},{9,8},{10,9... | collective-permute-start | bytes 393224 | tf_op jit(solution)/shard_map/ppermute | solution.py:745
  5.9 11.8 %collective-permute-start.2 = (f32[5,64,256]{2,1,0:T(8,128)}, f32[5,64,256]{2,1,0:T(8,128)S(1)}, u32[]{:S(2)}, u32[]{:S(2)}) collective-permute-start(f32[5,64,256]{2,1,0:T(8,128)} %get-tuple-element.50), channel_id=1, source_target_pairs={{0,252},{4,8},{8,4},{12,16},{16,12},{20,24},{24,20},{28,32},{32,28... | collective-permute-start | bytes 983048 | tf_op jit(solution)/shard_map/ppermute | solution.py:754
  8.5 9.2 %collective-permute-start.3 = (f32[5,64,256]{2,1,0:T(8,128)}, f32[5,64,256]{2,1,0:T(8,128)S(1)}, u32[]{:S(2)}, u32[]{:S(2)}) collective-permute-start(f32[5,64,256]{2,1,0:T(8,128)} %get-tuple-element.51), channel_id=1, source_target_pairs={{0,4},{4,0},{8,12},{12,8},{16,20},{20,16},{24,28},{28,24},{32,36},... | collective-permute-start | bytes 983048 | tf_op jit(solution)/shard_map/ppermute | solution.py:749
  15.8 6.4 %collective-permute-start.4 = (f32[280,256]{1,0:T(8,128)S(1)}, f32[280,256]{1,0:T(8,128)S(1)}, u32[]{:S(2)}, u32[]{:S(2)}) collective-permute-start(f32[280,256]{1,0:T(8,128)S(1)} %get-tuple-element.52), channel_id=1, source_target_pairs={{0,252},{4,8},{8,4},{12,16},{16,12},{20,24},{24,20},{28,32},{32,28... | collective-permute-start | bytes 860168 | tf_op jit(solution)/shard_map/ppermute | solution.py:754
  15.9 6.3 %collective-permute-start.5 = (f32[280,256]{1,0:T(8,128)S(1)}, f32[280,256]{1,0:T(8,128)S(1)}, u32[]{:S(2)}, u32[]{:S(2)}) collective-permute-start(f32[280,256]{1,0:T(8,128)S(1)} %get-tuple-element.53), channel_id=1, source_target_pairs={{0,4},{4,0},{8,12},{12,8},{16,20},{20,16},{24,28},{28,24},{32,36},... | collective-permute-start | bytes 860168 | tf_op jit(solution)/shard_map/ppermute | solution.py:749
  24.6 4.1 %collective-permute-start.7 = (f32[8,40,128]{2,1,0:T(8,128)S(1)}, f32[8,40,128]{2,1,0:T(8,128)S(1)}, u32[]{:S(2)}, u32[]{:S(2)}) collective-permute-start(f32[8,40,128]{2,1,0:T(8,128)S(1)} %get-tuple-element.55), channel_id=1, source_target_pairs={{0,4},{4,0},{8,12},{12,8},{16,20},{20,16},{24,28},{28,24},{32,36},... | collective-permute-start | bytes 491528 | tf_op jit(solution)/shard_map/ppermute | solution.py:749
  27.7 4.7 %collective-permute-start.6 = (f32[8,40,128]{2,1,0:T(8,128)S(1)}, f32[8,40,128]{2,1,0:T(8,128)S(1)}, u32[]{:S(2)}, u32[]{:S(2)}) collective-permute-start(f32[8,40,128]{2,1,0:T(8,128)S(1)} %get-tuple-element.54.own), channel_id=1, source_target_pairs={{0,252},{4,8},{8,4},{12,16},{16,12},{20,24},{24,20},{28,32},{32,28... | collective-permute-start | bytes 491528 | tf_op jit(solution)/shard_map/ppermute | solution.py:754
  32.8 6.9 %collective-permute-start.8 = (f32[56,128]{1,0:T(8,128)S(1)}, f32[56,128]{1,0:T(8,128)S(1)}, u32[]{:S(2)}, u32[]{:S(2)}) collective-permute-start(f32[56,128]{1,0:T(8,128)S(1)} %get-tuple-element.59), channel_id=1, source_target_pairs={{0,1},{1,2},{2,3},{3,0},{4,5},{5,6},{6,7},{7,4},{8,9},{9,10},{10,1... | collective-permute-start | bytes 86024 | tf_op jit(solution)/shard_map/ppermute | solution.py:745
  32.9 6.8 %collective-permute-start.9 = (f32[56,128]{1,0:T(8,128)S(1)}, f32[56,128]{1,0:T(8,128)S(1)}, u32[]{:S(2)}, u32[]{:S(2)}) collective-permute-start(f32[56,128]{1,0:T(8,128)S(1)} %get-tuple-element.60), channel_id=1, source_target_pairs={{0,3},{1,0},{2,1},{3,2},{4,7},{5,4},{6,5},{7,6},{8,11},{9,8},{10,9... | collective-permute-start | bytes 86024 | tf_op jit(solution)/shard_map/ppermute | solution.py:745
  35.5 4.1 %collective-permute-start.10 = (f32[40,128]{1,0:T(8,128)S(1)}, f32[40,128]{1,0:T(8,128)S(1)}, u32[]{:S(2)}, u32[]{:S(2)}) collective-permute-start(f32[40,128]{1,0:T(8,128)S(1)} %get-tuple-element.58.f2), channel_id=1, source_target_pairs={{0,2},{1,3},{2,0},{3,1},{4,6},{5,7},{6,4},{7,5},{8,10},{9,11},{10,... | collective-permute-start | bytes 61448 | tf_op jit(solution)/shard_map/ppermute | solution.py:745
  39.9 6.2 %collective-permute-start.11 = (f32[240,128]{1,0:T(8,128)S(1)}, f32[240,128]{1,0:T(8,128)S(1)}, u32[]{:S(2)}, u32[]{:S(2)}) collective-permute-start(f32[240,128]{1,0:T(8,128)S(1)} %get-tuple-element.63.msg), channel_id=1, source_target_pairs={{0,4},{4,0},{8,12},{12,8},{16,20},{20,16},{24,28},{28,24},{32,36},... | collective-permute-start | bytes 368648 | tf_op jit(solution)/shard_map/ppermute | solution.py:749
  46.1 5.0 %collective-permute-start.12 = (f32[352,128]{1,0:T(8,128)S(1)}, f32[352,128]{1,0:T(8,128)S(1)}, u32[]{:S(2)}, u32[]{:S(2)}) collective-permute-start(f32[352,128]{1,0:T(8,128)S(1)} %shard_map.52), channel_id=1, source_target_pairs={{0,252},{4,8},{8,4},{12,16},{16,12},{20,24},{24,20},{28,32},{32,28... | collective-permute-start | bytes 540680 | tf_op jit(solution)/shard_map/ppermute | solution.py:754
  51.1 4.7 %collective-permute-start.13 = (f32[352,128]{1,0:T(8,128)S(1)}, f32[352,128]{1,0:T(8,128)S(1)}, u32[]{:S(2)}, u32[]{:S(2)}) collective-permute-start(f32[352,128]{1,0:T(8,128)S(1)} %collective-permute-done.12.near), channel_id=1, source_target_pairs={{0,4},{4,0},{8,12},{12,8},{16,20},{20,16},{24,28},{28,24},{32,36},... | collective-permute-start | bytes 540680 | tf_op jit(solution)/shard_map/ppermute | solution.py:749
  57.3 14.1 %all-to-all-start = ((f32[32,2,8,128]{3,2,1,0:T(8,128)}), f32[32,2,8,128]{3,2,1,0:T(8,128)S(1)}, u32[]{:S(2)}, u32[]{:S(2)}) async-start(f32[32,2,8,128]{3,2,1,0:T(8,128)} %shard_map.55), calls=%async_computation | async-start | bytes 524288 | tf_op jit(solution)/shard_map/all_to_all | solution.py:810
  61.1 8.2 %collective-permute-start.14 = (f32[32,128]{1,0:T(8,128)S(1)}, f32[32,128]{1,0:T(8,128)S(1)}, u32[]{:S(2)}, u32[]{:S(2)}) collective-permute-start(f32[32,128]{1,0:T(8,128)S(1)} %get-tuple-element.68), channel_id=1, source_target_pairs={{0,252},{4,8},{8,4},{12,16},{16,12},{20,24},{24,20},{28,32},{32,28... | collective-permute-start | bytes 49160 | tf_op jit(solution)/shard_map/ppermute | solution.py:754
  71.4 14.3 %copy-start = (f32[4,64,256]{2,1,0:T(8,128)S(1)}, f32[4,64,256]{2,1,0:T(8,128)}, u32[]{:S(2)}) copy-start(f32[4,64,256]{2,1,0:T(8,128)} %c3.1) | copy-start | bytes 786436
  71.4 14.3 %copy-start.1 = (f32[4,64,256]{2,1,0:T(8,128)S(1)}, f32[4,64,256]{2,1,0:T(8,128)}, u32[]{:S(2)}) copy-start(f32[4,64,256]{2,1,0:T(8,128)} %c2.1) | copy-start | bytes 786436
  71.4 14.3 %copy-start.2 = (f32[4,64,256]{2,1,0:T(8,128)S(1)}, f32[4,64,256]{2,1,0:T(8,128)}, u32[]{:S(2)}) copy-start(f32[4,64,256]{2,1,0:T(8,128)} %c1.1) | copy-start | bytes 786436
  71.4 14.3 %copy-start.3 = (f32[4,64,256]{2,1,0:T(8,128)S(1)}, f32[4,64,256]{2,1,0:T(8,128)}, u32[]{:S(2)}) copy-start(f32[4,64,256]{2,1,0:T(8,128)} %f.1) | copy-start | bytes 786436
  71.4 4.2 %collective-permute-start.15 = (f32[32,2,8,128]{3,2,1,0:T(8,128)S(1)}, f32[32,2,8,128]{3,2,1,0:T(8,128)S(1)}, u32[]{:S(2)}, u32[]{:S(2)}) collective-permute-start(f32[32,2,8,128]{3,2,1,0:T(8,128)S(1)} %all-to-all-done.mine), channel_id=1, source_target_pairs={{0,4},{4,0},{8,12},{12,8},{16,20},{20,16},{24,28},{28,24},{32,36},... | collective-permute-start | bytes 786440 | tf_op jit(solution)/shard_map/ppermute | solution.py:749
  74.4 3.2 %collective-permute-start.16 = (f32[32,128]{1,0:T(8,128)S(1)}, f32[32,128]{1,0:T(8,128)S(1)}, u32[]{:S(2)}, u32[]{:S(2)}) collective-permute-start(f32[32,128]{1,0:T(8,128)S(1)} %collective-permute-done.14.late), channel_id=1, source_target_pairs={{0,4},{4,0},{8,12},{12,8},{16,20},{20,16},{24,28},{28,24},{32,36},... | collective-permute-start | bytes 49160 | tf_op jit(solution)/shard_map/ppermute | solution.py:749
  77.9 3.4 %collective-permute-start.17 = (f32[32,128]{1,0:T(8,128)S(1)}, f32[32,128]{1,0:T(8,128)S(1)}, u32[]{:S(2)}, u32[]{:S(2)}) collective-permute-start(f32[32,128]{1,0:T(8,128)S(1)} %get-tuple-element.73), channel_id=1, source_target_pairs={{0,252},{4,8},{8,4},{12,16},{16,12},{20,24},{24,20},{28,32},{32,28... | collective-permute-start | bytes 49160 | tf_op jit(solution)/shard_map/ppermute | solution.py:754
  82.0 4.5 %collective-permute-start.18 = (f32[40,128]{1,0:T(8,128)S(1)}, f32[40,128]{1,0:T(8,128)S(1)}, u32[]{:S(2)}, u32[]{:S(2)}) collective-permute-start(f32[40,128]{1,0:T(8,128)S(1)} %get-tuple-element.79), channel_id=1, source_target_pairs={{0,4},{4,0},{8,12},{12,8},{16,20},{20,16},{24,28},{28,24},{32,36},... | collective-permute-start | bytes 61448 | tf_op jit(solution)/shard_map/ppermute | solution.py:749

commit v19 on v17

--- a/solution.py
+++ b/solution.py
@@ -253,7 +253,7 @@
     return SIG[0] + c1[q, here, :] + c1[q + 1, here, :] + k2 + h2 + k3 + roll(k3, -1, 1)
 
 
-def fine_pre_kernel(own, coef1, far_raw, sib_raw, far, sib, u2, out_far, out_sib, f, c1, c2, c3, g, f1, u1, res, scr):
+def fine_pre_kernel(own, coef1, far_raw, sib_raw, far, sib, u2, out_far, out_sib, f, c1, c2, c3, g, d, f1, u1, res, scr):
     below, above = sides(far, sib)
     below_raw, above_raw = sides(far_raw, sib_raw)
     for a, ref in enumerate((f, c1, c2, c3)):
@@ -270,7 +270,9 @@
     def smooth_first(q, carry):
         def rows(r0, n):
             here = pl.ds(r0, CHUNK)
-            inverse = 1.0 / diag_chunk(c1, c2, c3, q, r0, n)
+            diag = diag_chunk(c1, c2, c3, q, r0, n)
+            d[q, here, :] = diag
+            inverse = 1.0 / diag
             g[q, here, :] = inverse
             u1[q + 1, here, :] = f[q, here, :] * inverse * (1.0 / THETA)
 
@@ -294,7 +296,7 @@
         def rows(r0, n):
             here = pl.ds(r0, CHUNK)
             x, near = near_chunk(u2, q, c1, c2, c3, q, r0, n)
-            res[q - 1, here, :] = f[q, here, :] + near - diag_chunk(c1, c2, c3, q, r0, n) * x
+            res[q - 1, here, :] = f[q, here, :] + near - d[q, here, :] * x
 
         chunked(80, rows)
         return carry
@@ -779,7 +781,7 @@
     u2, out_far, out_sib = call(
         fine_pre_kernel,
         [(6,) + big, (8, 40, 128), (8, 40, 128)],
-        windows + [(6,) + big, (2, 40, 128), (8,) + big, (4,) + big, (168, 128)],
+        windows + [(6,) + big, (6,) + big, (2, 40, 128), (8,) + big, (4,) + big, (168, 128)],
         limit=6,
     )(own, coef1, far_raw, sib_raw, far, sib)
     far1, sib1 = across(out_far), sibling(out_sib)

time: 89.2 us -> 89.1 us (level)
  no operation moved by 1% of the time
where the time goes in v19:
time: 89.1 us; the launch traced here: 88.9 us
  starting transfers between devices  43.5 us (49%)
  waiting for transfers between devices  31.1 us (35%)
  Pallas kernels  12.6 us (14%)
  other arithmetic  1.35 us (2%)
    ppermute x8, starting transfers between devices, sibling(): lax.ppermute(x, 'wide', [(i, i ^ 1) for i in range(lax.axis_size('wide'))])  26.2 us
    ppermute x6, waiting for transfers between devices, across(): lax.ppermute(x, 'wide', [(i, (i + 1 if i % 2 else i - 1) % count) for i i...  20.8 us
    pallas_call x14, Pallas kernels, run(): pl.pallas_call(kernel, out_shape=[jax.ShapeDtypeStruct(s, F32) for s in o...  12.6 us
    ppermute x5, starting transfers between devices, shift(): return lax.ppermute(x, axis, [(i, (i + by) % count) for i in range(count)])  6.82 us
    ppermute x6, starting transfers between devices, across(): lax.ppermute(x, 'wide', [(i, (i + 1 if i % 2 else i - 1) % count) for i i...  6.65 us
    ppermute x8, waiting for transfers between devices, sibling(): lax.ppermute(x, 'wide', [(i, i ^ 1) for i in range(lax.axis_size('wide'))])  4.53 us
    all_to_all x1, starting transfers between devices, body(): lax.all_to_all(send, 'wide', split_axis=0, concat_axis=0, tiled=True, axi...  3.87 us
    ppermute x5, waiting for transfers between devices, shift(): return lax.ppermute(x, axis, [(i, (i + by) % count) for i in range(count)])  3.8 us
  transfers between devices with their start and end apart: 20, of which 12 were waited for; matrix products, arithmetic and copies ran while one was open for 2% of the time, Pallas kernels for 3%

profile of v19, /device:TPU:1, one launch (start us, length us, event | category | flops | bytes accessed | tf_op | source)
XLA Modules:
  0.0 88.9 jit_solution(1483274721871963128)
XLA Ops:
  0.0 2.2 %shard_map.46 = (f32[16,8,256]{2,1,0:T(8,128)}, f32[16,8,256]{2,1,0:T(8,128)}, f32[5,64,256]{2,1,0:T(8,128)}, f32[5,64,256]{2,1,0:T(8,128)}) custom-call(f32[4,64,256]{2,1,0:T(8,128)} %f.1, f32[4,64,256]{2,1,0:T(8,128)} %c1.1, f32[4,64,256]{2,1,0:T(8,128)} %c2.1, f32[4,64,256]{2,1,0:T(8,128)} %c3.1), custom_call_target="tpu_custom_call" | custom-call | tf_op jit(solution)/shard_map/pallas_call | solution.py:136
  2.2 2.2 %collective-permute-start = (f32[16,8,256]{2,1,0:T(8,128)}, f32[16,8,256]{2,1,0:T(8,128)S(1)}, u32[]{:S(2)}, u32[]{:S(2)}) collective-permute-start(f32[16,8,256]{2,1,0:T(8,128)} %get-tuple-element.44), channel_id=1, source_target_pairs={{0,1},{1,2},{2,3},{3,0},{4,5},{5,6},{6,7},{7,4},{8,9},{9,10},{10,1... | collective-permute-start | bytes 393224 | tf_op jit(solution)/shard_map/ppermute | solution.py:746
  4.4 1.5 %collective-permute-start.1 = (f32[16,8,256]{2,1,0:T(8,128)}, f32[16,8,256]{2,1,0:T(8,128)S(1)}, u32[]{:S(2)}, u32[]{:S(2)}) collective-permute-start(f32[16,8,256]{2,1,0:T(8,128)} %get-tuple-element.45), channel_id=1, source_target_pairs={{0,3},{1,0},{2,1},{3,2},{4,7},{5,4},{6,5},{7,6},{8,11},{9,8},{10,9... | collective-permute-start | bytes 393224 | tf_op jit(solution)/shard_map/ppermute | solution.py:746
  5.9 2.6 %collective-permute-start.2 = (f32[5,64,256]{2,1,0:T(8,128)}, f32[5,64,256]{2,1,0:T(8,128)S(1)}, u32[]{:S(2)}, u32[]{:S(2)}) collective-permute-start(f32[5,64,256]{2,1,0:T(8,128)} %get-tuple-element.48), channel_id=1, source_target_pairs={{0,252},{4,8},{8,4},{12,16},{16,12},{20,24},{24,20},{28,32},{32,28... | collective-permute-start | bytes 983048 | tf_op jit(solution)/shard_map/ppermute | solution.py:755
  8.5 5.6 %collective-permute-start.3 = (f32[5,64,256]{2,1,0:T(8,128)}, f32[5,64,256]{2,1,0:T(8,128)S(1)}, u32[]{:S(2)}, u32[]{:S(2)}) collective-permute-start(f32[5,64,256]{2,1,0:T(8,128)} %get-tuple-element.49), channel_id=1, source_target_pairs={{0,4},{4,0},{8,12},{12,8},{16,20},{20,16},{24,28},{28,24},{32,36},... | collective-permute-start | bytes 983048 | tf_op jit(solution)/shard_map/ppermute | solution.py:750
  14.1 1.3 %pad_maximum_fusion.inner = f32[16,64,256]{2,1,0:T(8,128)S(1)} fusion(f32[4,64,256]{2,1,0:T(8,128)} %c3.1, f32[4,64,256]{2,1,0:T(8,128)} %c2.1, f32[4,64,256]{2,1,0:T(8,128)} %c1.1, f32[4,64,256]{2,1,0:T(8,128)} %f.1), kind=kLoop, calls=%fused_computation | loop fusion | flops 786432 | bytes 2097152 | tf_op jit(solution)/shard_map/concatenate | solution.py:777
  15.9 1.8 %collective-permute-start.5 = (f32[280,256]{1,0:T(8,128)S(1)}, f32[280,256]{1,0:T(8,128)S(1)}, u32[]{:S(2)}, u32[]{:S(2)}) collective-permute-start(f32[280,256]{1,0:T(8,128)S(1)} %get-tuple-element.51), channel_id=1, source_target_pairs={{0,4},{4,0},{8,12},{12,8},{16,20},{20,16},{24,28},{28,24},{32,36},... | collective-permute-start | bytes 860168 | tf_op jit(solution)/shard_map/ppermute | solution.py:750
  17.7 4.5 %collective-permute-done.4.far = f32[280,256]{1,0:T(8,128)S(1)} collective-permute-done((f32[280,256]{1,0:T(8,128)S(1)}, f32[280,256]{1,0:T(8,128)S(1)}, u32[]{:S(2)}, u32[]{:S(2)}) %collective-permute-start.4) | collective-permute-done | bytes 286752 | tf_op jit(solution)/shard_map/ppermute | solution.py:755
  22.3 2.2 %shard_map.48 = (f32[6,80,256]{2,1,0:T(8,128)S(1)}, f32[8,40,128]{2,1,0:T(8,128)S(1)}, f32[8,40,128]{2,1,0:T(8,128)S(1)}) custom-call(f32[16,80,256]{2,1,0:T(8,128)S(1)} %get-tuple-element.46.own, f32[6,40,128]{2,1,0:T(8,128)S(1)} %get-tuple-element.47.coef1, f32[5,64,256]{2,1,0:T(8,128)S(1)} %collective-permute-done.2.far_raw, ...), custom_call_target="tpu_custom_call" | custom-call | tf_op jit(solution)/shard_map/pallas_call | solution.py:136
  24.5 3.1 %collective-permute-start.7 = (f32[8,40,128]{2,1,0:T(8,128)S(1)}, f32[8,40,128]{2,1,0:T(8,128)S(1)}, u32[]{:S(2)}, u32[]{:S(2)}) collective-permute-start(f32[8,40,128]{2,1,0:T(8,128)S(1)} %get-tuple-element.53), channel_id=1, source_target_pairs={{0,4},{4,0},{8,12},{12,8},{16,20},{20,16},{24,28},{28,24},{32,36},... | collective-permute-start | bytes 491528 | tf_op jit(solution)/shard_map/ppermute | solution.py:750
  27.9 0.7 collective-permute-done.7.sib
  28.6 3.7 %collective-permute-done.6.far = f32[8,40,128]{2,1,0:T(8,128)S(1)} collective-permute-done((f32[8,40,128]{2,1,0:T(8,128)S(1)}, f32[8,40,128]{2,1,0:T(8,128)S(1)}, u32[]{:S(2)}, u32[]{:S(2)}) %collective-permute-start.6) | collective-permute-done | bytes 163872 | tf_op jit(solution)/shard_map/ppermute | solution.py:755
  32.8 2.7 %collective-permute-start.9 = (f32[56,128]{1,0:T(8,128)S(1)}, f32[56,128]{1,0:T(8,128)S(1)}, u32[]{:S(2)}, u32[]{:S(2)}) collective-permute-start(f32[56,128]{1,0:T(8,128)S(1)} %get-tuple-element.58), channel_id=1, source_target_pairs={{0,3},{1,0},{2,1},{3,2},{4,7},{5,4},{6,5},{7,6},{8,11},{9,8},{10,9... | collective-permute-start | bytes 86024 | tf_op jit(solution)/shard_map/ppermute | solution.py:746
  35.8 3.8 %collective-permute-done.10.far = f32[40,128]{1,0:T(8,128)S(1)} collective-permute-done((f32[40,128]{1,0:T(8,128)S(1)}, f32[40,128]{1,0:T(8,128)S(1)}, u32[]{:S(2)}, u32[]{:S(2)}) %collective-permute-start.10) | collective-permute-done | bytes 20512 | tf_op jit(solution)/shard_map/ppermute | solution.py:746
  39.8 5.2 %collective-permute-start.11 = (f32[240,128]{1,0:T(8,128)S(1)}, f32[240,128]{1,0:T(8,128)S(1)}, u32[]{:S(2)}, u32[]{:S(2)}) collective-permute-start(f32[240,128]{1,0:T(8,128)S(1)} %get-tuple-element.61.msg), channel_id=1, source_target_pairs={{0,4},{4,0},{8,12},{12,8},{16,20},{20,16},{24,28},{28,24},{32,36},... | collective-permute-start | bytes 368648 | tf_op jit(solution)/shard_map/ppermute | solution.py:750
  45.0 1.0 %collective-permute-done.11.sib = f32[240,128]{1,0:T(8,128)S(1)} collective-permute-done((f32[240,128]{1,0:T(8,128)S(1)}, f32[240,128]{1,0:T(8,128)S(1)}, u32[]{:S(2)}, u32[]{:S(2)}) %collective-permute-start.11) | collective-permute-done | bytes 122912 | tf_op jit(solution)/shard_map/ppermute | solution.py:750
  46.4 4.6 %collective-permute-done.12.near = f32[352,128]{1,0:T(8,128)S(1)} collective-permute-done((f32[352,128]{1,0:T(8,128)S(1)}, f32[352,128]{1,0:T(8,128)S(1)}, u32[]{:S(2)}, u32[]{:S(2)}) %collective-permute-start.12) | collective-permute-done | bytes 180256 | tf_op jit(solution)/shard_map/ppermute | solution.py:755
  51.0 3.7 %collective-permute-start.13 = (f32[352,128]{1,0:T(8,128)S(1)}, f32[352,128]{1,0:T(8,128)S(1)}, u32[]{:S(2)}, u32[]{:S(2)}) collective-permute-start(f32[352,128]{1,0:T(8,128)S(1)} %collective-permute-done.12.near), channel_id=1, source_target_pairs={{0,4},{4,0},{8,12},{12,8},{16,20},{20,16},{24,28},{28,24},{32,36},... | collective-permute-start | bytes 540680 | tf_op jit(solution)/shard_map/ppermute | solution.py:750
  54.7 1.0 %collective-permute-done.13.other = f32[352,128]{1,0:T(8,128)S(1)} collective-permute-done((f32[352,128]{1,0:T(8,128)S(1)}, f32[352,128]{1,0:T(8,128)S(1)}, u32[]{:S(2)}, u32[]{:S(2)}) %collective-permute-start.13) | collective-permute-done | bytes 180256 | tf_op jit(solution)/shard_map/ppermute | solution.py:750
  56.2 1.0 %shard_map.55 = f32[32,2,8,128]{3,2,1,0:T(8,128)} custom-call(f32[21,64,128]{2,1,0:T(8,128)S(1)} %get-tuple-element.63.w.win, f32[4,64,128]{2,1,0:T(8,128)S(1)} %get-tuple-element.64.u2, f32[3,8,128]{2,1,0:T(8,128)S(1)} %shard_map.53.tiles), custom_call_target="tpu_custom_call" | custom-call | tf_op jit(solution)/shard_map/pallas_call | solution.py:136
  57.2 3.9 %all-to-all-start = ((f32[32,2,8,128]{3,2,1,0:T(8,128)}), f32[32,2,8,128]{3,2,1,0:T(8,128)S(1)}, u32[]{:S(2)}, u32[]{:S(2)}) async-start(f32[32,2,8,128]{3,2,1,0:T(8,128)} %shard_map.55), calls=%async_computation | async-start | bytes 524288 | tf_op jit(solution)/shard_map/all_to_all | solution.py:811
  61.0 1.9 %collective-permute-start.14 = (f32[32,128]{1,0:T(8,128)S(1)}, f32[32,128]{1,0:T(8,128)S(1)}, u32[]{:S(2)}, u32[]{:S(2)}) collective-permute-start(f32[32,128]{1,0:T(8,128)S(1)} %get-tuple-element.66), channel_id=1, source_target_pairs={{0,252},{4,8},{8,4},{12,16},{16,12},{20,24},{24,20},{28,32},{32,28... | collective-permute-start | bytes 49160 | tf_op jit(solution)/shard_map/ppermute | solution.py:755
  63.0 6.3 %collective-permute-done.14.late = f32[32,128]{1,0:T(8,128)S(1)} collective-permute-done((f32[32,128]{1,0:T(8,128)S(1)}, f32[32,128]{1,0:T(8,128)S(1)}, u32[]{:S(2)}, u32[]{:S(2)}) %collective-permute-start.14) | collective-permute-done | bytes 16416 | tf_op jit(solution)/shard_map/ppermute | solution.py:755
  69.3 2.0 %all-to-all-done.mine = f32[32,2,8,128]{3,2,1,0:T(8,128)S(1)} async-done(((f32[32,2,8,128]{3,2,1,0:T(8,128)}), f32[32,2,8,128]{3,2,1,0:T(8,128)S(1)}, u32[]{:S(2)}, u32[]{:S(2)}) %all-to-all-start) | async-done | bytes 262176 | tf_op jit(solution)/shard_map/all_to_all | solution.py:811
  71.3 3.0 %collective-permute-start.15 = (f32[32,2,8,128]{3,2,1,0:T(8,128)S(1)}, f32[32,2,8,128]{3,2,1,0:T(8,128)S(1)}, u32[]{:S(2)}, u32[]{:S(2)}) collective-permute-start(f32[32,2,8,128]{3,2,1,0:T(8,128)S(1)} %all-to-all-done.mine), channel_id=1, source_target_pairs={{0,4},{4,0},{8,12},{12,8},{16,20},{20,16},{24,28},{28,24},{32,36},... | collective-permute-start | bytes 786440 | tf_op jit(solution)/shard_map/ppermute | solution.py:750
  74.4 1.1 %collective-permute-done.15.theirs = f32[32,2,8,128]{3,2,1,0:T(8,128)S(1)} collective-permute-done((f32[32,2,8,128]{3,2,1,0:T(8,128)S(1)}, f32[32,2,8,128]{3,2,1,0:T(8,128)S(1)}, u32[]{:S(2)}, u32[]{:S(2)}) %collective-permute-start.15) | collective-permute-done | bytes 262176 | tf_op jit(solution)/shard_map/ppermute | solution.py:750
  75.5 2.0 %shard_map.56.e2 = f32[200,128]{1,0:T(8,128)S(1)} custom-call(f32[32,2,8,128]{3,2,1,0:T(8,128)S(1)} %all-to-all-done.mine, f32[32,2,8,128]{3,2,1,0:T(8,128)S(1)} %collective-permute-done.15.theirs), custom_call_target="tpu_custom_call" | custom-call | tf_op jit(solution)/shard_map/pallas_call | solution.py:136
  77.8 1.9 %collective-permute-start.17 = (f32[2,32,128]{2,1,0:T(8,128)S(1)}, f32[2,32,128]{2,1,0:T(8,128)S(1)}, u32[]{:S(2)}, u32[]{:S(2)}) collective-permute-start(f32[2,32,128]{2,1,0:T(8,128)S(1)} %shard_map.57.e2), channel_id=1, source_target_pairs={{0,252},{4,8},{8,4},{12,16},{16,12},{20,24},{24,20},{28,32},{32,28... | collective-permute-start | bytes 98312 | tf_op jit(solution)/shard_map/ppermute | solution.py:755
  79.7 1.6 %collective-permute-done.17.far = f32[2,32,128]{2,1,0:T(8,128)S(1)} collective-permute-done((f32[2,32,128]{2,1,0:T(8,128)S(1)}, f32[2,32,128]{2,1,0:T(8,128)S(1)}, u32[]{:S(2)}, u32[]{:S(2)}) %collective-permute-start.17) | collective-permute-done | bytes 32800 | tf_op jit(solution)/shard_map/ppermute | solution.py:755
  82.0 3.7 %collective-permute-start.18 = (f32[40,128]{1,0:T(8,128)S(1)}, f32[40,128]{1,0:T(8,128)S(1)}, u32[]{:S(2)}, u32[]{:S(2)}) collective-permute-start(f32[40,128]{1,0:T(8,128)S(1)} %get-tuple-element.75), channel_id=1, source_target_pairs={{0,4},{4,0},{8,12},{12,8},{16,20},{20,16},{24,28},{28,24},{32,36},... | collective-permute-start | bytes 61448 | tf_op jit(solution)/shard_map/ppermute | solution.py:750
  85.8 0.7 collective-permute-done.18.other
  86.5 2.2 %shard_map.59 = f32[4,64,256]{2,1,0:T(8,128)} custom-call(f32[2,40,128]{2,1,0:T(8,128)S(1)} %get-tuple-element.73.e1, f32[40,128]{1,0:T(8,128)S(1)} %get-tuple-element.74.edge, f32[40,128]{1,0:T(8,128)S(1)} %collective-permute-done.18.other, f32[2,80,256]{2,1,0:T(8,128)S(1)} %get-tuple-element.76.outer, f32[16,64,256]{2,1,0:T(8,128)S(1)} %pad_maximum_fusion.1.inner, ...), custom_call_target="tpu_custom_call" | custom-call | tf_op jit(solution)/shard_map/pallas_call | solution.py:136
  (32 shorter events, 3.8 us)
Async XLA Ops:
  2.2 13.2 %collective-permute-start = (f32[16,8,256]{2,1,0:T(8,128)}, f32[16,8,256]{2,1,0:T(8,128)S(1)}, u32[]{:S(2)}, u32[]{:S(2)}) collective-permute-start(f32[16,8,256]{2,1,0:T(8,128)} %get-tuple-element.44), channel_id=1, source_target_pairs={{0,1},{1,2},{2,3},{3,0},{4,5},{5,6},{6,7},{7,4},{8,9},{9,10},{10,1... | collective-permute-start | bytes 393224 | tf_op jit(solution)/shard_map/ppermute | solution.py:746
  4.4 11.0 %collective-permute-start.1 = (f32[16,8,256]{2,1,0:T(8,128)}, f32[16,8,256]{2,1,0:T(8,128)S(1)}, u32[]{:S(2)}, u32[]{:S(2)}) collective-permute-start(f32[16,8,256]{2,1,0:T(8,128)} %get-tuple-element.45), channel_id=1, source_target_pairs={{0,3},{1,0},{2,1},{3,2},{4,7},{5,4},{6,5},{7,6},{8,11},{9,8},{10,9... | collective-permute-start | bytes 393224 | tf_op jit(solution)/shard_map/ppermute | solution.py:746
  5.9 11.8 %collective-permute-start.2 = (f32[5,64,256]{2,1,0:T(8,128)}, f32[5,64,256]{2,1,0:T(8,128)S(1)}, u32[]{:S(2)}, u32[]{:S(2)}) collective-permute-start(f32[5,64,256]{2,1,0:T(8,128)} %get-tuple-element.48), channel_id=1, source_target_pairs={{0,252},{4,8},{8,4},{12,16},{16,12},{20,24},{24,20},{28,32},{32,28... | collective-permute-start | bytes 983048 | tf_op jit(solution)/shard_map/ppermute | solution.py:755
  8.5 9.2 %collective-permute-start.3 = (f32[5,64,256]{2,1,0:T(8,128)}, f32[5,64,256]{2,1,0:T(8,128)S(1)}, u32[]{:S(2)}, u32[]{:S(2)}) collective-permute-start(f32[5,64,256]{2,1,0:T(8,128)} %get-tuple-element.49), channel_id=1, source_target_pairs={{0,4},{4,0},{8,12},{12,8},{16,20},{20,16},{24,28},{28,24},{32,36},... | collective-permute-start | bytes 983048 | tf_op jit(solution)/shard_map/ppermute | solution.py:750
  15.8 6.4 %collective-permute-start.4 = (f32[280,256]{1,0:T(8,128)S(1)}, f32[280,256]{1,0:T(8,128)S(1)}, u32[]{:S(2)}, u32[]{:S(2)}) collective-permute-start(f32[280,256]{1,0:T(8,128)S(1)} %get-tuple-element.50), channel_id=1, source_target_pairs={{0,252},{4,8},{8,4},{12,16},{16,12},{20,24},{24,20},{28,32},{32,28... | collective-permute-start | bytes 860168 | tf_op jit(solution)/shard_map/ppermute | solution.py:755
  15.9 6.3 %collective-permute-start.5 = (f32[280,256]{1,0:T(8,128)S(1)}, f32[280,256]{1,0:T(8,128)S(1)}, u32[]{:S(2)}, u32[]{:S(2)}) collective-permute-start(f32[280,256]{1,0:T(8,128)S(1)} %get-tuple-element.51), channel_id=1, source_target_pairs={{0,4},{4,0},{8,12},{12,8},{16,20},{20,16},{24,28},{28,24},{32,36},... | collective-permute-start | bytes 860168 | tf_op jit(solution)/shard_map/ppermute | solution.py:750
  24.5 4.1 %collective-permute-start.7 = (f32[8,40,128]{2,1,0:T(8,128)S(1)}, f32[8,40,128]{2,1,0:T(8,128)S(1)}, u32[]{:S(2)}, u32[]{:S(2)}) collective-permute-start(f32[8,40,128]{2,1,0:T(8,128)S(1)} %get-tuple-element.53), channel_id=1, source_target_pairs={{0,4},{4,0},{8,12},{12,8},{16,20},{20,16},{24,28},{28,24},{32,36},... | collective-permute-start | bytes 491528 | tf_op jit(solution)/shard_map/ppermute | solution.py:750
  27.6 4.7 %collective-permute-start.6 = (f32[8,40,128]{2,1,0:T(8,128)S(1)}, f32[8,40,128]{2,1,0:T(8,128)S(1)}, u32[]{:S(2)}, u32[]{:S(2)}) collective-permute-start(f32[8,40,128]{2,1,0:T(8,128)S(1)} %get-tuple-element.52.own), channel_id=1, source_target_pairs={{0,252},{4,8},{8,4},{12,16},{16,12},{20,24},{24,20},{28,32},{32,28... | collective-permute-start | bytes 491528 | tf_op jit(solution)/shard_map/ppermute | solution.py:755
  32.7 6.9 %collective-permute-start.8 = (f32[56,128]{1,0:T(8,128)S(1)}, f32[56,128]{1,0:T(8,128)S(1)}, u32[]{:S(2)}, u32[]{:S(2)}) collective-permute-start(f32[56,128]{1,0:T(8,128)S(1)} %get-tuple-element.57), channel_id=1, source_target_pairs={{0,1},{1,2},{2,3},{3,0},{4,5},{5,6},{6,7},{7,4},{8,9},{9,10},{10,1... | collective-permute-start | bytes 86024 | tf_op jit(solution)/shard_map/ppermute | solution.py:746
  32.8 6.8 %collective-permute-start.9 = (f32[56,128]{1,0:T(8,128)S(1)}, f32[56,128]{1,0:T(8,128)S(1)}, u32[]{:S(2)}, u32[]{:S(2)}) collective-permute-start(f32[56,128]{1,0:T(8,128)S(1)} %get-tuple-element.58), channel_id=1, source_target_pairs={{0,3},{1,0},{2,1},{3,2},{4,7},{5,4},{6,5},{7,6},{8,11},{9,8},{10,9... | collective-permute-start | bytes 86024 | tf_op jit(solution)/shard_map/ppermute | solution.py:746
  35.5 4.1 %collective-permute-start.10 = (f32[40,128]{1,0:T(8,128)S(1)}, f32[40,128]{1,0:T(8,128)S(1)}, u32[]{:S(2)}, u32[]{:S(2)}) collective-permute-start(f32[40,128]{1,0:T(8,128)S(1)} %get-tuple-element.56.f2), channel_id=1, source_target_pairs={{0,2},{1,3},{2,0},{3,1},{4,6},{5,7},{6,4},{7,5},{8,10},{9,11},{10,... | collective-permute-start | bytes 61448 | tf_op jit(solution)/shard_map/ppermute | solution.py:746
  39.8 6.2 %collective-permute-start.11 = (f32[240,128]{1,0:T(8,128)S(1)}, f32[240,128]{1,0:T(8,128)S(1)}, u32[]{:S(2)}, u32[]{:S(2)}) collective-permute-start(f32[240,128]{1,0:T(8,128)S(1)} %get-tuple-element.61.msg), channel_id=1, source_target_pairs={{0,4},{4,0},{8,12},{12,8},{16,20},{20,16},{24,28},{28,24},{32,36},... | collective-permute-start | bytes 368648 | tf_op jit(solution)/shard_map/ppermute | solution.py:750
  46.0 5.0 %collective-permute-start.12 = (f32[352,128]{1,0:T(8,128)S(1)}, f32[352,128]{1,0:T(8,128)S(1)}, u32[]{:S(2)}, u32[]{:S(2)}) collective-permute-start(f32[352,128]{1,0:T(8,128)S(1)} %shard_map.52), channel_id=1, source_target_pairs={{0,252},{4,8},{8,4},{12,16},{16,12},{20,24},{24,20},{28,32},{32,28... | collective-permute-start | bytes 540680 | tf_op jit(solution)/shard_map/ppermute | solution.py:755
  51.0 4.7 %collective-permute-start.13 = (f32[352,128]{1,0:T(8,128)S(1)}, f32[352,128]{1,0:T(8,128)S(1)}, u32[]{:S(2)}, u32[]{:S(2)}) collective-permute-start(f32[352,128]{1,0:T(8,128)S(1)} %collective-permute-done.12.near), channel_id=1, source_target_pairs={{0,4},{4,0},{8,12},{12,8},{16,20},{20,16},{24,28},{28,24},{32,36},... | collective-permute-start | bytes 540680 | tf_op jit(solution)/shard_map/ppermute | solution.py:750
  57.2 14.1 %all-to-all-start = ((f32[32,2,8,128]{3,2,1,0:T(8,128)}), f32[32,2,8,128]{3,2,1,0:T(8,128)S(1)}, u32[]{:S(2)}, u32[]{:S(2)}) async-start(f32[32,2,8,128]{3,2,1,0:T(8,128)} %shard_map.55), calls=%async_computation | async-start | bytes 524288 | tf_op jit(solution)/shard_map/all_to_all | solution.py:811
  61.0 8.2 %collective-permute-start.14 = (f32[32,128]{1,0:T(8,128)S(1)}, f32[32,128]{1,0:T(8,128)S(1)}, u32[]{:S(2)}, u32[]{:S(2)}) collective-permute-start(f32[32,128]{1,0:T(8,128)S(1)} %get-tuple-element.66), channel_id=1, source_target_pairs={{0,252},{4,8},{8,4},{12,16},{16,12},{20,24},{24,20},{28,32},{32,28... | collective-permute-start | bytes 49160 | tf_op jit(solution)/shard_map/ppermute | solution.py:755
  71.3 14.4 %copy-start = (f32[4,64,256]{2,1,0:T(8,128)S(1)}, f32[4,64,256]{2,1,0:T(8,128)}, u32[]{:S(2)}) copy-start(f32[4,64,256]{2,1,0:T(8,128)} %c3.1) | copy-start | bytes 786436
  71.3 14.4 %copy-start.1 = (f32[4,64,256]{2,1,0:T(8,128)S(1)}, f32[4,64,256]{2,1,0:T(8,128)}, u32[]{:S(2)}) copy-start(f32[4,64,256]{2,1,0:T(8,128)} %c2.1) | copy-start | bytes 786436
  71.3 14.4 %copy-start.2 = (f32[4,64,256]{2,1,0:T(8,128)S(1)}, f32[4,64,256]{2,1,0:T(8,128)}, u32[]{:S(2)}) copy-start(f32[4,64,256]{2,1,0:T(8,128)} %c1.1) | copy-start | bytes 786436
  71.3 14.4 %copy-start.3 = (f32[4,64,256]{2,1,0:T(8,128)S(1)}, f32[4,64,256]{2,1,0:T(8,128)}, u32[]{:S(2)}) copy-start(f32[4,64,256]{2,1,0:T(8,128)} %f.1) | copy-start | bytes 786436
  71.3 4.2 %collective-permute-start.15 = (f32[32,2,8,128]{3,2,1,0:T(8,128)S(1)}, f32[32,2,8,128]{3,2,1,0:T(8,128)S(1)}, u32[]{:S(2)}, u32[]{:S(2)}) collective-permute-start(f32[32,2,8,128]{3,2,1,0:T(8,128)S(1)} %all-to-all-done.mine), channel_id=1, source_target_pairs={{0,4},{4,0},{8,12},{12,8},{16,20},{20,16},{24,28},{28,24},{32,36},... | collective-permute-start | bytes 786440 | tf_op jit(solution)/shard_map/ppermute | solution.py:750
  74.3 3.2 %collective-permute-start.16 = (f32[32,128]{1,0:T(8,128)S(1)}, f32[32,128]{1,0:T(8,128)S(1)}, u32[]{:S(2)}, u32[]{:S(2)}) collective-permute-start(f32[32,128]{1,0:T(8,128)S(1)} %collective-permute-done.14.late), channel_id=1, source_target_pairs={{0,4},{4,0},{8,12},{12,8},{16,20},{20,16},{24,28},{28,24},{32,36},... | collective-permute-start | bytes 49160 | tf_op jit(solution)/shard_map/ppermute | solution.py:750
  77.8 3.5 %collective-permute-start.17 = (f32[2,32,128]{2,1,0:T(8,128)S(1)}, f32[2,32,128]{2,1,0:T(8,128)S(1)}, u32[]{:S(2)}, u32[]{:S(2)}) collective-permute-start(f32[2,32,128]{2,1,0:T(8,128)S(1)} %shard_map.57.e2), channel_id=1, source_target_pairs={{0,252},{4,8},{8,4},{12,16},{16,12},{20,24},{24,20},{28,32},{32,28... | collective-permute-start | bytes 98312 | tf_op jit(solution)/shard_map/ppermute | solution.py:755
  82.0 4.5 %collective-permute-start.18 = (f32[40,128]{1,0:T(8,128)S(1)}, f32[40,128]{1,0:T(8,128)S(1)}, u32[]{:S(2)}, u32[]{:S(2)}) collective-permute-start(f32[40,128]{1,0:T(8,128)S(1)} %get-tuple-element.75), channel_id=1, source_target_pairs={{0,4},{4,0},{8,12},{12,8},{16,20},{20,16},{24,28},{28,24},{32,36},... | collective-permute-start | bytes 61448 | tf_op jit(solution)/shard_map/ppermute | solution.py:750
